TPU v7x, 32 devices: a whole 2x2x4 slice. The times are simulated.
32 devices in a mesh: dp: 4 (over z), ctx: 8 (over y, x, core).
Axes of the slice: x: 2, y: 2, z: 4, core: 2. Of those that a mesh axis runs over, the one named last changes fastest.
Arguments:
- query_in: bfloat16 [4, 1024, 4096], P('dp', 'ctx'), may hold values from -6 to 6
- key_in: bfloat16 [4, 1024, 4096], P('dp', 'ctx'), may hold values from -6 to 6
- value_in: bfloat16 [4, 1024, 4096], P('dp', 'ctx'), may hold values from -6 to 6
- grad_out: bfloat16 [4, 1024, 4096], P('dp', 'ctx'), may hold values from -6 to 6
- filters: float32 [4096, 1024], P('ctx'), may hold values from -0.1875 to 0.1875
- skip_gain: float32 [4096], replicated, may hold values from 0.1 to 1.9
Outputs:
- mixed_out: bfloat16 [4, 1024, 4096], P('dp', 'ctx')
- grad_query: bfloat16 [4, 1024, 4096], P('dp', 'ctx')
- grad_key: bfloat16 [4, 1024, 4096], P('dp', 'ctx')
- grad_value: bfloat16 [4, 1024, 4096], P('dp', 'ctx')
- grad_filter: float32 [4096, 1024], P('ctx', 'dp')
All inputs are finite; a program needn't handle non-finite values.
Results may differ from a plain program's by a relative error of at most 0.0085.
Values may be sent and summed in bfloat16 or wider, within the bound.
No kernel may reach another device: no remote copies, remote signals or barrier semaphores. Data moves between devices by JAX's collectives and lax.ppermute only.
A program may use at most 192 MiB of HBM per device.

v0:
```python
import math

import jax
import jax.numpy as jnp
from jax import lax
from jax.sharding import PartitionSpec as P


def angles(left_idx, right_idx, modulus):
    product = left_idx[:, None] * right_idx[None, :] % modulus
    return product.astype(jnp.float32) * (2.0 * math.pi / modulus)


def factors(length):
    chosen = 1
    for divisor in range(1, length + 1):
        if length % divisor == 0 and 2 * divisor * divisor <= length:
            chosen = divisor
    return (2 * chosen, length // chosen)


def matmul(form, table, data):
    return jnp.einsum(form, table, data, precision=lax.Precision.HIGHEST)


def forward_spectrum(signal):
    length, chan_width = signal.shape
    rows_split, cols_split = factors(length)
    full_length = 2 * length
    blocks = signal.reshape(rows_split // 2, cols_split, chan_width)
    first_angle = angles(
        jnp.arange(rows_split, dtype=jnp.int32),
        jnp.arange(rows_split // 2, dtype=jnp.int32),
        rows_split,
    )
    first_table = jnp.stack([jnp.cos(first_angle), -jnp.sin(first_angle)])
    section = matmul("pka,abc->pkbc", first_table, blocks)
    twiddle = angles(
        jnp.arange(rows_split, dtype=jnp.int32),
        jnp.arange(cols_split, dtype=jnp.int32),
        full_length,
    )
    cos_twid = jnp.cos(twiddle)[:, :, None]
    sin_twid = jnp.sin(twiddle)[:, :, None]
    turned = jnp.stack(
        [
            section[0] * cos_twid + section[1] * sin_twid,
            section[1] * cos_twid - section[0] * sin_twid,
        ]
    )
    last_angle = angles(
        jnp.arange(cols_split, dtype=jnp.int32), jnp.arange(cols_split, dtype=jnp.int32), cols_split
    )
    cos_last = jnp.cos(last_angle)
    sin_last = jnp.sin(last_angle)
    last_table = jnp.stack([jnp.stack([cos_last, sin_last]), jnp.stack([-sin_last, cos_last])])
    spec = matmul("qpjb,pkbc->qkjc", last_table, turned)
    return (spec[0], spec[1])


def inverse_signal(spec_real, spec_imag):
    rows_split, cols_split, chan_width = spec_real.shape
    full_length = rows_split * cols_split
    stacked = jnp.stack([spec_real, spec_imag])
    last_angle = angles(
        jnp.arange(cols_split, dtype=jnp.int32), jnp.arange(cols_split, dtype=jnp.int32), cols_split
    )
    cos_last = jnp.cos(last_angle)
    sin_last = jnp.sin(last_angle)
    last_table = jnp.stack([jnp.stack([cos_last, -sin_last]), jnp.stack([sin_last, cos_last])])
    inner = matmul("qpbj,pkjc->qkbc", last_table, stacked)
    twiddle = angles(
        jnp.arange(rows_split, dtype=jnp.int32),
        jnp.arange(cols_split, dtype=jnp.int32),
        full_length,
    )
    cos_twid = jnp.cos(twiddle)[:, :, None]
    sin_twid = jnp.sin(twiddle)[:, :, None]
    turned = jnp.stack(
        [inner[0] * cos_twid - inner[1] * sin_twid, inner[1] * cos_twid + inner[0] * sin_twid]
    )
    first_angle = angles(
        jnp.arange(rows_split // 2, dtype=jnp.int32),
        jnp.arange(rows_split, dtype=jnp.int32),
        rows_split,
    )
    first_table = jnp.stack([jnp.cos(first_angle), -jnp.sin(first_angle)])
    signal = matmul("pak,pkbc->abc", first_table, turned)
    return signal.reshape(rows_split // 2 * cols_split, chan_width) / full_length


def channel_work(key_value, weighted, filters):
    filt_real, filt_imag = forward_spectrum(filters.T)
    kv_real, kv_imag = forward_spectrum(key_value.astype(jnp.float32))
    wt_real, wt_imag = forward_spectrum(weighted.astype(jnp.float32))
    conv_out = inverse_signal(
        kv_real * filt_real - kv_imag * filt_imag, kv_real * filt_imag + kv_imag * filt_real
    )
    corr_back = inverse_signal(
        wt_real * filt_real + wt_imag * filt_imag, wt_imag * filt_real - wt_real * filt_imag
    )
    filter_term = inverse_signal(
        wt_real * kv_real + wt_imag * kv_imag, wt_imag * kv_real - wt_real * kv_imag
    )
    return (conv_out.astype(jnp.bfloat16), corr_back.astype(jnp.bfloat16), filter_term.T)


def products(query_rows, key_rows, value_rows, grad_rows):
    key_value = (key_rows.astype(jnp.float32) * value_rows.astype(jnp.float32)).astype(jnp.bfloat16)
    weighted = (grad_rows.astype(jnp.float32) * query_rows.astype(jnp.float32)).astype(jnp.bfloat16)
    return (key_value, weighted)


def finish(
    query_rows, key_rows, value_rows, grad_rows, key_value, weighted, conv_out, corr_back, chan_gain
):
    mixing = conv_out.astype(jnp.float32) + chan_gain * key_value.astype(jnp.float32)
    mixed_out = (query_rows.astype(jnp.float32) * mixing).astype(jnp.bfloat16)
    grad_query = (grad_rows.astype(jnp.float32) * mixing).astype(jnp.bfloat16)
    back_sum = corr_back.astype(jnp.float32) + chan_gain * weighted.astype(jnp.float32)
    grad_key = (back_sum * value_rows.astype(jnp.float32)).astype(jnp.bfloat16)
    grad_value = (back_sum * key_rows.astype(jnp.float32)).astype(jnp.bfloat16)
    return (mixed_out, grad_query, grad_key, grad_value)


def local(query_in, key_in, value_in, grad_out, filters, skip_gain):
    query_rows = query_in[0]
    key_rows = key_in[0]
    value_rows = value_in[0]
    grad_rows = grad_out[0]
    query_chan, key_chan, value_chan, grad_chan = (
        lax.all_to_all(query_rows, "ctx", split_axis=1, concat_axis=0, tiled=True),
        lax.all_to_all(key_rows, "ctx", split_axis=1, concat_axis=0, tiled=True),
        lax.all_to_all(value_rows, "ctx", split_axis=1, concat_axis=0, tiled=True),
        lax.all_to_all(grad_rows, "ctx", split_axis=1, concat_axis=0, tiled=True),
    )
    chan_width = filters.shape[0]
    chan_gain = lax.dynamic_slice_in_dim(skip_gain, lax.axis_index("ctx") * chan_width, chan_width)
    key_value, weighted = products(query_chan, key_chan, value_chan, grad_chan)
    conv_out, corr_back, filter_term = channel_work(key_value, weighted, filters)
    mixed_chan, gq_chan, gk_chan, gv_chan = finish(
        query_chan,
        key_chan,
        value_chan,
        grad_chan,
        key_value,
        weighted,
        conv_out,
        corr_back,
        chan_gain,
    )
    mixed_out, grad_query, grad_key, grad_value = (
        lax.all_to_all(mixed_chan, "ctx", split_axis=0, concat_axis=1, tiled=True),
        lax.all_to_all(gq_chan, "ctx", split_axis=0, concat_axis=1, tiled=True),
        lax.all_to_all(gk_chan, "ctx", split_axis=0, concat_axis=1, tiled=True),
        lax.all_to_all(gv_chan, "ctx", split_axis=0, concat_axis=1, tiled=True),
    )
    grad_filter = lax.psum_scatter(filter_term, "dp", scatter_dimension=1, tiled=True)
    return (mixed_out[None], grad_query[None], grad_key[None], grad_value[None], grad_filter)


def solution(mesh):
    return jax.shard_map(
        local,
        mesh=mesh,
        in_specs=(
            P("dp", "ctx", None),
            P("dp", "ctx", None),
            P("dp", "ctx", None),
            P("dp", "ctx", None),
            P("ctx", None),
            P(),
        ),
        out_specs=(
            P("dp", "ctx", None),
            P("dp", "ctx", None),
            P("dp", "ctx", None),
            P("dp", "ctx", None),
            P("ctx", "dp"),
        ),
        check_vma=False,
    )
```

profile of v0, /device:TPU:0, one launch (start us, length us, event | category | flops | bytes accessed | tf_op | source)
XLA Modules:
  0.0 384.3 jit_solution(17859643628655821891)
XLA Ops:
  9.5 5.2 %all-to-all-start.4 = ((bf16[128,8,512]{0,2,1:T(8,128)(2,1)}), bf16[128,8,512]{0,2,1:T(8,128)(2,1)S(1)}, u32[]{:S(2)}, u32[]{:S(2)}) async-start(bf16[128,8,512]{0,2,1:T(8,128)(2,1)} %bitcast.42), calls=%async_computation.4 | async-start | bytes 2097152 | tf_op jit(solution)/shard_map/all_to_all | solution.py:135
  16.0 14.1 %all-to-all-done.4 = bf16[128,8,512]{0,2,1:T(8,128)(2,1)S(1)} async-done(((bf16[128,8,512]{0,2,1:T(8,128)(2,1)}), bf16[128,8,512]{0,2,1:T(8,128)(2,1)S(1)}, u32[]{:S(2)}, u32[]{:S(2)}) %all-to-all-start.4) | async-done | bytes 1048608 | tf_op jit(solution)/shard_map/all_to_all | solution.py:135
  40.2 8.8 %all-to-all-done = bf16[128,8,512]{0,2,1:T(8,128)(2,1)S(1)} async-done(((bf16[128,8,512]{0,2,1:T(8,128)(2,1)}), bf16[128,8,512]{0,2,1:T(8,128)(2,1)S(1)}, u32[]{:S(2)}, u32[]{:S(2)}) %all-to-all-start) | async-done | bytes 1048608 | tf_op jit(solution)/shard_map/all_to_all | solution.py:132
  53.7 11.2 %fusion.55 = f32[2,32,64,512]{3,1,2,0:T(8,128)} fusion(f32[16,64,512]{2,1,0:T(8,128)} %bitcast.217, f32[1,32,16]{1,2,0:T(8,128)S(1)} %get-tuple-element.55, f32[1,32,16]{1,2,0:T(8,128)S(1)} %get-tuple-element.56), kind=kOutput, calls=%fused_computation.85 | convolution fusion | flops 402654208 | bytes 10489856 | tf_op jit(solution)/shard_map/pka,abc->pkbc/dot_general | solution.py:23
  67.9 4.3 %all-to-all-start.1 = ((bf16[128,8,512]{0,2,1:T(8,128)(2,1)}), bf16[128,8,512]{0,2,1:T(8,128)(2,1)}, u32[]{:S(2)}, u32[]{:S(2)}) async-start(bf16[128,8,512]{0,2,1:T(8,128)(2,1)} %bitcast.223), calls=%async_computation.1 | async-start | bytes 2097152 | tf_op jit(solution)/shard_map/all_to_all | solution.py:133
  77.0 5.7 %fusion.72 = f32[2,32,64,512]{3,1,2,0:T(8,128)} fusion(bf16[16,64,512]{2,1,0:T(8,128)(2,1)S(1)} %bitcast.222, f32[1,32,16]{1,2,0:T(8,128)S(1)} %get-tuple-element.55, f32[1,32,16]{1,2,0:T(8,128)S(1)} %get-tuple-element.56), kind=kOutput, calls=%fused_computation.94 | convolution fusion | flops 402654208 | bytes 9441280 | tf_op jit(solution)/shard_map/pka,abc->pkbc/dot_general | solution.py:23
  82.7 4.9 %all-to-all-done.1 = bf16[128,8,512]{0,2,1:T(8,128)(2,1)} async-done(((bf16[128,8,512]{0,2,1:T(8,128)(2,1)}), bf16[128,8,512]{0,2,1:T(8,128)(2,1)}, u32[]{:S(2)}, u32[]{:S(2)}) %all-to-all-start.1) | async-done | bytes 1048608 | tf_op jit(solution)/shard_map/all_to_all | solution.py:133
  89.7 5.8 %fusion.74 = f32[2,32,64,512]{3,1,2,0:T(8,128)} fusion(bf16[16,64,512]{2,1,0:T(8,128)(2,1)S(1)} %bitcast.221, f32[1,32,16]{1,2,0:T(8,128)S(1)} %get-tuple-element.55, f32[1,32,16]{1,2,0:T(8,128)S(1)} %get-tuple-element.56), kind=kOutput, calls=%fused_computation.96 | convolution fusion | flops 402654208 | bytes 9441280 | tf_op jit(solution)/shard_map/pka,abc->pkbc/dot_general | solution.py:23
  95.5 17.3 %multiply_add_fusion.4 = (f32[1,32,64,512]{3,1,2,0:T(8,128)}, f32[1,32,64,512]{3,1,2,0:T(8,128)}, f32[1,32,64,512]{3,1,2,0:T(8,128)S(1)}, f32[1,32,64,512]{3,1,2...) fusion(f32[2,32,64,512]{3,1,2,0:T(8,128)} %fusion.72, f32[32,64]{0,1:T(8,128)S(1)} %get-tuple-element.57, ...), kind=kLoop, calls=%fused_computation.45 | loop fusion | flops 18874368 | bytes 50348032 | tf_op jit(solution)/shard_map/add | solution.py:47
  112.8 8.7 %maximum_bitcast_fusion.4 = f32[2,32,64,512,1]{3,1,2,0,4:T(8,128)} fusion(f32[1,32,64,512]{3,1,2,0:T(8,128)} %get-tuple-element.26, f32[1,32,64,512]{3,1,2,0:T(8,128)} %get-tuple-element.25), kind=kLoop, calls=%fused_computation.10 | loop fusion | flops 2097152 | bytes 16777216 | tf_op jit(solution)/shard_map/stack | solution.py:45
  121.6 4.3 %maximum_bitcast_fusion = f32[2,32,64,512,1]{3,1,2,0,4:T(8,128)} fusion(f32[1,32,64,512]{3,1,2,0:T(8,128)S(1)} %copy-done.4, f32[1,32,64,512]{3,1,2,0:T(8,128)S(1)} %copy-done.5), kind=kLoop, calls=%fused_computation | loop fusion | flops 2097152 | bytes 16777216 | tf_op jit(solution)/shard_map/stack | solution.py:45
  125.9 16.4 %fusion.33 = f32[2,32,64,512]{3,2,0,1:T(8,128)S(1)} fusion(f32[2,32,64,512,1]{3,1,2,0,4:T(8,128)} %maximum_bitcast_fusion.4, f32[1,2,64,64]{3,2,1,0:T(8,128)S(1)} %get-tuple-element.50, f32[1,2,64,64]{3,2,1,0:T(8,128)S(1)} %get-tuple-element.53), kind=kOutput, calls=%fused_computation.56 | convolution fusion | flops 3221241856 | bytes 16842752 | tf_op jit(solution)/shard_map/qpjb,pkbc->qkjc/dot_general | solution.py:23
  142.3 13.4 %fusion.27 = f32[2,32,64,512]{3,2,0,1:T(8,128)} fusion(f32[2,32,64,512,1]{3,1,2,0,4:T(8,128)S(1)} %copy-done.1, f32[1,2,64,64]{3,2,1,0:T(8,128)S(1)} %get-tuple-element.50, f32[1,2,64,64]{3,2,1,0:T(8,128)S(1)} %get-tuple-element.53), kind=kOutput, calls=%fused_computation.54 | convolution fusion | flops 3221241856 | bytes 16842752 | tf_op jit(solution)/shard_map/qpjb,pkbc->qkjc/dot_general | solution.py:23
  155.8 4.3 %maximum_bitcast_fusion.1 = f32[2,32,64,512,1]{3,1,2,0,4:T(8,128)} fusion(f32[1,32,64,512]{3,1,2,0:T(8,128)S(1)} %get-tuple-element.45, f32[1,32,64,512]{3,1,2,0:T(8,128)S(1)} %copy-done.2), kind=kLoop, calls=%fused_computation.1 | loop fusion | flops 2097152 | bytes 16777216 | tf_op jit(solution)/shard_map/stack | solution.py:45
  160.1 15.8 %fusion.30 = f32[2,32,64,512]{3,2,0,1:T(8,128)S(1)} fusion(f32[2,32,64,512,1]{3,1,2,0,4:T(8,128)} %maximum_bitcast_fusion.1, f32[1,2,64,64]{3,2,1,0:T(8,128)S(1)} %get-tuple-element.50, f32[1,2,64,64]{3,2,1,0:T(8,128)S(1)} %get-tuple-element.53), kind=kOutput, calls=%fused_computation.55 | convolution fusion | flops 3221241856 | bytes 16842752 | tf_op jit(solution)/shard_map/qpjb,pkbc->qkjc/dot_general | solution.py:23
  179.1 4.3 %multiply_add_fusion.3 = (f32[1,32,64,512]{3,2,0,1:T(8,128)}, f32[1,32,64,512]{3,2,0,1:T(8,128)}) fusion(f32[2,32,64,512]{3,2,0,1:T(8,128)S(1)} %fusion.33, f32[2,32,64,512]{3,2,0,1:T(8,128)S(1)} %fusion.30), kind=kLoop, calls=%fused_computation.43 | loop fusion | flops 6291456 | bytes 25165824 | tf_op jit(solution)/shard_map/add | solution.py:100
  183.5 11.3 %multiply_add_fusion.1 = (f32[1,32,64,512]{3,2,0,1:T(8,128)}, f32[1,32,64,512]{3,2,0,1:T(8,128)}, f32[1,32,64,512]{3,2,0,1:T(8,128)S(1)}, f32[1,32,64,512]{3,2,0,1:T(8,128)}) fusion(f32[2,32,64,512]{3,2,0,1:T(8,128)S(1)} %fusion.33, f32[2,32,64,512]{3,2,0,1:T(8,128)} %fusion.27, f32[2,32,64,512]{3,2,0,1:T(8,128)} %copy-done), kind=kLoop, calls=%fused_computation.39 | loop fusion | flops 12582912 | bytes 41943040 | tf_op jit(solution)/shard_map/add | solution.py:103
  194.8 10.4 %fusion.36 = f32[32,512,2,64]{1,3,2,0:T(8,128)S(1)} fusion(f32[1,32,64,512]{3,2,0,1:T(8,128)} %get-tuple-element.16, f32[1,32,64,512]{3,2,0,1:T(8,128)} %get-tuple-element.15, f32[1,2,64,64]{3,2,1,0:T(8,128)S(1)} %get-tuple-element.54, f32[1,2,64,64]{3,2,1,0:T(8,128)S(1)} %get-tuple-element.49), kind=kOutput, calls=%fused_computation.57 | convolution fusion | flops 3223339008 | bytes 16842752 | tf_op jit(solution)/shard_map/qpbj,pkjc->qkbc/dot_general | solution.py:23
  205.2 8.1 %copy.116 = f32[32,512,2,64]{1,0,3,2:T(8,128)} copy(f32[32,512,2,64]{1,3,2,0:T(8,128)S(1)} %fusion.36) | data formatting | bytes 16777216 | tf_op jit(solution)/shard_map/qpbj,pkjc->qkbc/dot_general | solution.py:23
  213.3 10.2 %fusion.38 = f32[32,512,2,64]{1,3,2,0:T(8,128)S(1)} fusion(f32[1,32,64,512]{3,2,0,1:T(8,128)S(1)} %get-tuple-element.33, f32[1,32,64,512]{3,2,0,1:T(8,128)S(1)} %copy-done.3, f32[1,2,64,64]{3,2,1,0:T(8,128)S(1)} %get-tuple-element.54, f32[1,2,64,64]{3,2,1,0:T(8,128)S(1)} %get-tuple-element.49), kind=kOutput, calls=%fused_computation.59 | convolution fusion | flops 3223339008 | bytes 16842752 | tf_op jit(solution)/shard_map/qpbj,pkjc->qkbc/dot_general | solution.py:23
  223.5 8.1 %copy.118 = f32[32,512,2,64]{1,0,3,2:T(8,128)} copy(f32[32,512,2,64]{1,3,2,0:T(8,128)S(1)} %fusion.38) | data formatting | bytes 16777216 | tf_op jit(solution)/shard_map/qpbj,pkjc->qkbc/dot_general | solution.py:23
  231.6 9.9 %fusion.37 = f32[32,512,2,64]{1,3,2,0:T(8,128)S(1)} fusion(f32[1,32,64,512]{3,2,0,1:T(8,128)S(1)} %copy-done.7, f32[1,32,64,512]{3,2,0,1:T(8,128)S(1)} %copy-done.6, f32[1,2,64,64]{3,2,1,0:T(8,128)S(1)} %get-tuple-element.54, f32[1,2,64,64]{3,2,1,0:T(8,128)S(1)} %get-tuple-element.49), kind=kOutput, calls=%fused_computation.58 | convolution fusion | flops 3223339008 | bytes 16842752 | tf_op jit(solution)/shard_map/qpbj,pkjc->qkbc/dot_general | solution.py:23
  241.5 8.1 %copy.117 = f32[32,512,2,64]{1,0,3,2:T(8,128)} copy(f32[32,512,2,64]{1,3,2,0:T(8,128)S(1)} %fusion.37) | data formatting | bytes 16777216 | tf_op jit(solution)/shard_map/qpbj,pkjc->qkbc/dot_general | solution.py:23
  249.7 17.5 %multiply_subtract_fusion = (f32[1,32,64,512]{3,1,2,0:T(8,128)}, f32[1,32,64,512]{3,1,2,0:T(8,128)}, f32[1,32,64,512]{3,1,2,0:T(8,128)S(1)}, f32[1,32,64,512]{3,...) fusion(f32[2,32,64,512]{3,1,2,0:T(8,128)} %bitcast.214, f32[32,64]{0,1:T(8,128)S(1)} %get-tuple-element.57, ...), kind=kLoop, calls=%fused_computation.37 | loop fusion | flops 18874368 | bytes 50348032 | tf_op jit(solution)/shard_map/sub | solution.py:80
  267.2 6.3 %fusion.64 = f32[16,64,512]{2,0,1:T(8,128)S(1)} fusion(f32[1,32,64,512]{3,1,2,0:T(8,128)S(1)} %get-tuple-element.41, f32[1,32,64,512]{3,1,2,0:T(8,128)} %get-tuple-element.42, f32[1,16,32]{2,1,0:T(8,128)S(1)} %get-tuple-element.61, f32[1,16,32]{2,1,0:T(8,128)S(1)} %get-tuple-element.62), kind=kOutput, calls=%fused_computation.90 | convolution fusion | flops 406324224 | bytes 10489856 | tf_op jit(solution)/shard_map/pak,pkbc->abc/dot_general | solution.py:23
  276.5 6.7 %fusion.67 = f32[16,64,512]{2,0,1:T(8,128)S(1)} fusion(f32[1,32,64,512]{3,1,2,0:T(8,128)} %get-tuple-element.43, f32[1,32,64,512]{3,1,2,0:T(8,128)} %get-tuple-element.44, f32[1,16,32]{2,1,0:T(8,128)S(1)} %get-tuple-element.61, f32[1,16,32]{2,1,0:T(8,128)S(1)} %get-tuple-element.62), kind=kOutput, calls=%fused_computation.91 | convolution fusion | flops 406324224 | bytes 10489856 | tf_op jit(solution)/shard_map/pak,pkbc->abc/dot_general | solution.py:23
  286.3 7.0 %bitcast_multiply_fusion = f32[16,64,512]{2,0,1:T(8,128)S(1)} fusion(f32[1,32,64,512]{3,1,2,0:T(8,128)} %get-tuple-element.22, f32[1,32,64,512]{3,1,2,0:T(8,128)} %get-tuple-element.21, f32[1,16,32]{2,1,0:T(8,128)S(1)} %get-tuple-element.61, f32[1,16,32]{2,1,0:T(8,128)S(1)} %get-tuple-element.62), kind=kOutput, calls=%fused_computation.80 | convolution fusion | flops 405275648 | bytes 10489856 | tf_op jit(solution)/shard_map/pak,pkbc->abc/dot_general | solution.py:23
  295.9 4.9 %fusion.50 = (bf16[8,128,512]{1,2,0:T(8,128)(2,1)S(1)}, bf16[8,128,512]{1,2,0:T(8,128)(2,1)S(1)}, bf16[8,128,512]{1,2,0:T(8,128)(2,1)S(1)}, bf16[8,128,512]{1,2,0:T(8,128)(2,1)}) fusion(bf16[128,8,512]{0,2,1:T(8,128)(2,1)S(1)} %copy-done.9, f32[8,128,512]{1,2,0:T(8,128)} %copy.50, f32[512]{0:T(512)S(1)} %dynamic_slice.3, ...), kind=kLoop, calls=%fused_computation.77 | loop fusion | flops 11534336 | bytes 12584960 | tf_op jit(solution)/shard_map/convert_element_type | solution.py:119
  300.9 17.8 %all_to_all.104 = bf16[8,128,512]{1,2,0:T(8,128)(2,1)S(1)} all-to-all(bf16[8,128,512]{1,2,0:T(8,128)(2,1)S(1)} %get-tuple-element.38), channel_id=1, replica_groups=mesh['dp'=4,'ctx'=8] {'ctx'}, dimensions={0} | all-to-all | bytes 2097152 | tf_op jit(solution)/shard_map/all_to_all | solution.py:153
  318.7 17.8 %all_to_all.105 = bf16[8,128,512]{1,2,0:T(8,128)(2,1)S(1)} all-to-all(bf16[8,128,512]{1,2,0:T(8,128)(2,1)S(1)} %get-tuple-element.37), channel_id=1, replica_groups=mesh['dp'=4,'ctx'=8] {'ctx'}, dimensions={0} | all-to-all | bytes 2097152 | tf_op jit(solution)/shard_map/all_to_all | solution.py:154
  336.4 18.5 %all_to_all.106 = bf16[8,128,512]{1,2,0:T(8,128)(2,1)} all-to-all(bf16[8,128,512]{1,2,0:T(8,128)(2,1)S(1)} %get-tuple-element.39), channel_id=1, replica_groups=mesh['dp'=4,'ctx'=8] {'ctx'}, dimensions={0} | all-to-all | bytes 2097152 | tf_op jit(solution)/shard_map/all_to_all | solution.py:155
  363.3 10.5 %all-to-all-done.7 = bf16[8,128,512]{1,2,0:T(8,128)(2,1)S(1)} async-done(((bf16[8,128,512]{1,2,0:T(8,128)(2,1)}), bf16[8,128,512]{1,2,0:T(8,128)(2,1)S(1)}, u32[]{:S(2)}, u32[]{:S(2)}) %all-to-all-start.7) | async-done | bytes 1048608 | tf_op jit(solution)/shard_map/all_to_all | solution.py:156
  (65 shorter events, 52.0 us)
Async XLA Ops:
  7.2 7.5 %copy-start.14 = (bf16[1,128,4096]{2,1,0:T(8,128)(2,1)S(1)}, bf16[1,128,4096]{2,1,0:T(8,128)(2,1)}, u32[]{:S(2)}) copy-start(bf16[1,128,4096]{2,1,0:T(8,128)(2,1)} %param.6) | copy-start | bytes 3145732
  9.5 20.6 %all-to-all-start.4 = ((bf16[128,8,512]{0,2,1:T(8,128)(2,1)}), bf16[128,8,512]{0,2,1:T(8,128)(2,1)S(1)}, u32[]{:S(2)}, u32[]{:S(2)}) async-start(bf16[128,8,512]{0,2,1:T(8,128)(2,1)} %bitcast.42), calls=%async_computation.4 | async-start | bytes 2097152 | tf_op jit(solution)/shard_map/all_to_all | solution.py:135
  14.7 21.9 %copy-start.15 = (bf16[1,128,4096]{2,1,0:T(8,128)(2,1)S(1)}, bf16[1,128,4096]{2,1,0:T(8,128)(2,1)}, u32[]{:S(2)}) copy-start(bf16[1,128,4096]{2,1,0:T(8,128)(2,1)} %param.8) | copy-start | bytes 3145732
  30.1 44.1 %copy-start.8 = (bf16[128,8,512]{0,2,1:T(8,128)(2,1)}, bf16[128,8,512]{0,2,1:T(8,128)(2,1)S(1)}, u32[]{:S(2)}) copy-start(bf16[128,8,512]{0,2,1:T(8,128)(2,1)S(1)} %all-to-all-done.4) | copy-start | bytes 3145732
  30.1 18.9 %all-to-all-start = ((bf16[128,8,512]{0,2,1:T(8,128)(2,1)}), bf16[128,8,512]{0,2,1:T(8,128)(2,1)S(1)}, u32[]{:S(2)}, u32[]{:S(2)}) async-start(bf16[128,8,512]{0,2,1:T(8,128)(2,1)} %bitcast), calls=%async_computation | async-start | bytes 2097152 | tf_op jit(solution)/shard_map/all_to_all | solution.py:132
  49.0 25.2 %copy-start.10 = (bf16[128,8,512]{0,2,1:T(8,128)(2,1)}, bf16[128,8,512]{0,2,1:T(8,128)(2,1)S(1)}, u32[]{:S(2)}) copy-start(bf16[128,8,512]{0,2,1:T(8,128)(2,1)S(1)} %all-to-all-done) | copy-start | bytes 3145732
  49.0 18.9 %all-to-all-start.2 = ((bf16[128,8,512]{0,2,1:T(8,128)(2,1)}), bf16[128,8,512]{0,2,1:T(8,128)(2,1)S(1)}, u32[]{:S(2)}, u32[]{:S(2)}) async-start(bf16[128,8,512]{0,2,1:T(8,128)(2,1)} %bitcast.224), calls=%async_computation.2 | async-start | bytes 2097152 | tf_op jit(solution)/shard_map/all_to_all | solution.py:134
  67.9 19.7 %copy-start.12 = (bf16[128,8,512]{0,2,1:T(8,128)(2,1)}, bf16[128,8,512]{0,2,1:T(8,128)(2,1)S(1)}, u32[]{:S(2)}) copy-start(bf16[128,8,512]{0,2,1:T(8,128)(2,1)S(1)} %all-to-all-done.2) | copy-start | bytes 3145732
  67.9 19.7 %all-to-all-start.1 = ((bf16[128,8,512]{0,2,1:T(8,128)(2,1)}), bf16[128,8,512]{0,2,1:T(8,128)(2,1)}, u32[]{:S(2)}, u32[]{:S(2)}) async-start(bf16[128,8,512]{0,2,1:T(8,128)(2,1)} %bitcast.223), calls=%async_computation.1 | async-start | bytes 2097152 | tf_op jit(solution)/shard_map/all_to_all | solution.py:133
  72.2 302.9 %reduce-scatter.2.cloned.1.call-start = ((), (), s32[]{:S(2)}) async-start(), calls=%async_computation.9 | async-start | bytes 2621440 | tf_op jit(solution)/shard_map/reduce_scatter | solution.py:158
  112.8 8.8 %copy-start.4 = (f32[1,32,64,512]{3,1,2,0:T(8,128)S(1)}, f32[1,32,64,512]{3,1,2,0:T(8,128)}, u32[]{:S(2)}) copy-start(f32[1,32,64,512]{3,1,2,0:T(8,128)} %get-tuple-element.47) | copy-start | bytes 12582916
  112.8 8.8 %copy-start.5 = (f32[1,32,64,512]{3,1,2,0:T(8,128)S(1)}, f32[1,32,64,512]{3,1,2,0:T(8,128)}, u32[]{:S(2)}) copy-start(f32[1,32,64,512]{3,1,2,0:T(8,128)} %get-tuple-element.48) | copy-start | bytes 12582916
  125.9 16.4 %copy-start.1 = (f32[2,32,64,512,1]{3,1,2,0,4:T(8,128)S(1)}, f32[2,32,64,512,1]{3,1,2,0,4:T(8,128)}, u32[]{:S(2)}) copy-start(f32[2,32,64,512,1]{3,1,2,0,4:T(8,128)} %maximum_bitcast_fusion) | copy-start | bytes 25165828
  142.3 13.4 %copy-start.2 = (f32[1,32,64,512]{3,1,2,0:T(8,128)S(1)}, f32[1,32,64,512]{3,1,2,0:T(8,128)}, u32[]{:S(2)}) copy-start(f32[1,32,64,512]{3,1,2,0:T(8,128)} %get-tuple-element.46) | copy-start | bytes 12582916
  175.9 3.3 copy-start
  205.1 8.1 %copy-start.3 = (f32[1,32,64,512]{3,2,0,1:T(8,128)S(1)}, f32[1,32,64,512]{3,2,0,1:T(8,128)}, u32[]{:S(2)}) copy-start(f32[1,32,64,512]{3,2,0,1:T(8,128)} %get-tuple-element.34) | copy-start | bytes 12582916
  223.5 8.1 %copy-start.6 = (f32[1,32,64,512]{3,2,0,1:T(8,128)S(1)}, f32[1,32,64,512]{3,2,0,1:T(8,128)}, u32[]{:S(2)}) copy-start(f32[1,32,64,512]{3,2,0,1:T(8,128)} %get-tuple-element.17) | copy-start | bytes 12582916
  223.5 8.1 %copy-start.7 = (f32[1,32,64,512]{3,2,0,1:T(8,128)S(1)}, f32[1,32,64,512]{3,2,0,1:T(8,128)}, u32[]{:S(2)}) copy-start(f32[1,32,64,512]{3,2,0,1:T(8,128)} %get-tuple-element.18) | copy-start | bytes 12582916
  293.3 2.7 copy-start.9
  293.3 2.7 copy-start.11
  293.3 2.7 copy-start.13
  354.9 18.9 %all-to-all-start.7 = ((bf16[8,128,512]{1,2,0:T(8,128)(2,1)}), bf16[8,128,512]{1,2,0:T(8,128)(2,1)S(1)}, u32[]{:S(2)}, u32[]{:S(2)}) async-start(bf16[8,128,512]{1,2,0:T(8,128)(2,1)} %get-tuple-element.40), calls=%async_computation.7 | async-start | bytes 2097152 | tf_op jit(solution)/shard_map/all_to_all | solution.py:156
Sparse Core Ops, SparseCore 0:
  296.0 43.2 reduce-scatter.1
where the time goes:
time: 390 us; the launch traced here: 384 us
  matrix products  119 us (31%)
  other arithmetic  77.6 us (20%)
  local copies, waits for them, and re-layouts  57.6 us (15%)
  blocking collectives  54 us (14%)
  waiting for transfers between devices  41.3 us (11%)
  starting transfers between devices  20.4 us (5%)
  between operations  14.6 us (4%)
    dot_general x12, matrix products, matmul(): return jnp.einsum(form, table, data, precision=lax.Precision.HIGHEST)  119 us
    dot_general x3, local copies, waits for them, and re-layouts, matmul(): return jnp.einsum(form, table, data, precision=lax.Precision.HIGHEST)  24.4 us
    unnamed x42, local copies, waits for them, and re-layouts  21.7 us
    all_to_all x1, blocking collectives, local(): lax.all_to_all(gk_chan, 'ctx', split_axis=0, concat_axis=1, tiled=True)  18.5 us
    all_to_all x1, blocking collectives, local(): lax.all_to_all(gq_chan, 'ctx', split_axis=0, concat_axis=1, tiled=True)  17.8 us
    all_to_all x1, blocking collectives, local(): lax.all_to_all(mixed_chan, 'ctx', split_axis=0, concat_axis=1, tiled=True)  17.8 us
    sub x1, other arithmetic, inverse_signal(): inner[0] * cos_twid - inner[1] * sin_twid  17.5 us
    another operation x3, other arithmetic, forward_spectrum(): jnp.stack([section[0] * cos_twid + section[1] * sin_twid, section[1] * co...  17.4 us
  transfers between devices with their start and end apart: 6, of which 5 were waited for; matrix products, arithmetic and copies ran while one was open for 11% of the time, Pallas kernels for 0%

commit v1 on v0

v1 whole, which is shorter than its diff:
```python
import functools
import math

import jax
import jax.numpy as jnp
import ml_dtypes
import numpy as np
from jax import lax
from jax.experimental import pallas as pl
from jax.experimental.pallas import tpu as pltpu
from jax.sharding import PartitionSpec as P

F32 = jnp.float32
BF16 = jnp.bfloat16
VMEM_LIMIT = 56 * 1024 * 1024
ROWS = 16


def odd_forward(xs):
    n = len(xs)
    if n == 1:
        return [(xs[0], None)]
    even, odd = odd_forward(xs[0::2]), odd_forward(xs[1::2])
    out = [None] * n
    for k in range(n // 2):
        angle = 2 * math.pi * (2 * k + 1) / (4 * n)
        c, s = math.cos(angle), math.sin(angle)
        (er, ei), (zr, zi) = even[k], odd[k]
        if zi is None:
            tr, ti = c * zr, -s * zr
            out[k], out[n - 1 - k] = (er + tr, ti), (er - tr, ti)
        else:
            tr, ti = c * zr + s * zi, c * zi - s * zr
            out[k], out[n - 1 - k] = (er + tr, ei + ti), (er - tr, ti - ei)
    return out


def odd_back(ys):
    n = len(ys)
    if n == 1:
        return [ys[0][0]]
    even, odd = [], []
    for k in range(n // 2):
        angle = 2 * math.pi * (2 * k + 1) / (4 * n)
        c, s = math.cos(angle), math.sin(angle)
        (ar, ai), (br, bi) = ys[k], ys[n - 1 - k]
        dr, di = ar - br, ai + bi
        if n == 2:
            even.append((ar + br, None))
            odd.append((c * dr - s * di, None))
        else:
            even.append((ar + br, ai - bi))
            odd.append((c * dr - s * di, c * di + s * dr))
    even, odd = odd_back(even), odd_back(odd)
    return [x for pair in zip(even, odd) for x in pair]


def tables(n, b):
    k1 = np.arange(n)[:, None, None]
    k2 = np.arange(b)[None, :, None]
    n2 = np.arange(b)[None, None, :]
    turn = (n2 * (2 * k1 + 1 + 4 * n * k2)) % (4 * n * b)
    angle = 2 * np.pi * turn / (4 * n * b)
    c, s = np.cos(angle), np.sin(angle)
    forward = np.concatenate([np.concatenate([c, s], 2), np.concatenate([-s, c], 2)], 1)
    back = np.swapaxes(forward, 1, 2) / (n * b)

    def halves(x):
        hi = x.astype(ml_dtypes.bfloat16)
        lo = (x - hi.astype(np.float64)).astype(ml_dtypes.bfloat16)
        return hi, lo

    return halves(forward) + halves(back)


def halves(x):
    hi = x.astype(BF16)
    return hi, (x - hi.astype(F32)).astype(BF16)


def dot3(a_hi, a_lo, b_hi, b_lo, dims=((1,), (0,))):
    def one(a, b):
        return lax.dot_general(a, b, (dims, ((), ())), preferred_element_type=F32)

    return one(a_hi, b_hi) + one(a_lo, b_hi) + one(a_hi, b_lo)


def first_stage(x, hi, lo):
    n, b, width = x.shape

    def step(i, carry):
        r = pl.multiple_of(i * ROWS, ROWS)
        for c in range(0, width, 128):
            xs = [x[p, pl.ds(r, ROWS), c : c + 128].astype(F32) for p in range(n)]
            for k, parts in enumerate(odd_forward(xs)):
                for q, part in enumerate(parts):
                    h, l = halves(part)
                    hi[k, pl.ds(q * b + r, ROWS), c : c + 128] = h
                    lo[k, pl.ds(q * b + r, ROWS), c : c + 128] = l
        return carry

    lax.fori_loop(0, b // ROWS, step, 0)


def last_stage(z, store):
    n, b2, width = z.shape
    b = b2 // 2

    def step(i, carry):
        r = pl.multiple_of(i * ROWS, ROWS)
        for c in range(0, width, 128):
            ys = [
                (z[k, pl.ds(r, ROWS), c : c + 128], z[k, pl.ds(b + r, ROWS), c : c + 128])
                for k in range(n)
            ]
            for p, y in enumerate(odd_back(ys)):
                store(p, r, c, y)
        return carry

    lax.fori_loop(0, b // ROWS, step, 0)


def times(x, f, conj):
    b = x.shape[0] // 2
    xr, xi, fr, fi = x[:b], x[b:], f[:b], f[b:]
    if conj:
        return xr * fr + xi * fi, xi * fr - xr * fi
    return xr * fr - xi * fi, xr * fi + xi * fr


def back_product(y, back_hi, back_lo):
    (rh, rl), (ih, il) = halves(y[0]), halves(y[1])
    return dot3(back_hi, back_lo, jnp.concatenate([rh, ih], 0), jnp.concatenate([rl, il], 0))


def product_kernel(n, me, a, b, *outs):
    j = pl.program_id(0)
    value = (a[...].astype(F32) * b[...].astype(F32)).astype(BF16)
    for i in range(n):

        @pl.when(j == i)
        def _():
            outs[i][...] = value


def product_blocks(me, a, b, n):
    rows, total = a.shape
    width = total // n
    block = pl.BlockSpec((rows, width), lambda j, me: (0, me[0] ^ j))
    return pl.pallas_call(
        functools.partial(product_kernel, n),
        grid_spec=pltpu.PrefetchScalarGridSpec(
            num_scalar_prefetch=1,
            grid=(n,),
            in_specs=[block, block],
            out_specs=[pl.BlockSpec((rows, width), lambda j, me: (0, 0))] * n,
        ),
        out_shape=[jax.ShapeDtypeStruct((rows, width), BF16)] * n,
        compiler_params=pltpu.CompilerParams(vmem_limit_bytes=VMEM_LIMIT),
        name="products",
    )(me, a, b)


def filter_kernel(filt, fwd_hi, fwd_lo, spec, hi, lo):
    n, chans, b2 = hi.shape
    b = b2 // 2

    def step(i, carry):
        r = pl.multiple_of(i * ROWS, ROWS)
        xs = [filt[pl.ds(r, ROWS), p * b : (p + 1) * b] for p in range(n)]
        for k, parts in enumerate(odd_forward(xs)):
            for q, part in enumerate(parts):
                h, l = halves(part)
                hi[k, pl.ds(r, ROWS), q * b : (q + 1) * b] = h
                lo[k, pl.ds(r, ROWS), q * b : (q + 1) * b] = l
        return carry

    lax.fori_loop(0, chans // ROWS, step, 0)
    for k in range(n):
        spec[k] = dot3(fwd_hi[k], fwd_lo[k], hi[k], lo[k], ((1,), (1,)))


def filter_spectrum(filters, fwd_hi, fwd_lo, chunk):
    chans, length = filters.shape
    n, b2, _ = fwd_hi.shape
    table = pl.BlockSpec((n, b2, b2), lambda c: (0, 0, 0))
    return pl.pallas_call(
        filter_kernel,
        grid=(chans // chunk,),
        in_specs=[pl.BlockSpec((chunk, length), lambda c: (c, 0)), table, table],
        out_specs=pl.BlockSpec((n, b2, chunk), lambda c: (0, 0, c)),
        out_shape=jax.ShapeDtypeStruct((n, b2, chans), F32),
        scratch_shapes=[pltpu.VMEM((n, chunk, b2), BF16)] * 2,
        compiler_params=pltpu.CompilerParams(vmem_limit_bytes=VMEM_LIMIT),
        name="filter_spectrum",
    )(filters, fwd_hi, fwd_lo)


def conv_kernel(n, me, *refs):
    blocks, (filt, fwd_hi, fwd_lo, back_hi, back_lo, spec), refs = refs[:n], refs[n : n + 6], refs[n + 6 :]
    outs, (x, hi, lo, z, y) = refs[:n], refs[n:]
    for j in range(n):
        x[me[0] ^ j] = blocks[j][...]
    first_stage(x, hi, lo)
    for k in range(n):
        s = dot3(fwd_hi[k], fwd_lo[k], hi[k], lo[k])
        spec[k] = s
        z[k] = back_product(times(s, filt[k], False), back_hi[k], back_lo[k])

    def store(p, r, c, value):
        y[p, pl.ds(r, ROWS), c : c + 128] = value.astype(BF16)

    last_stage(z, store)
    for j in range(n):
        outs[j][...] = y[me[0] ^ j]


def back_kernel(n, d, me, *refs):
    blocks, refs = refs[:n], refs[n:]
    (filt, spec, fwd_hi, fwd_lo, back_hi, back_lo), refs = refs[:6], refs[6:]
    outs, grads, (x, hi, lo, z, zg, y, g) = refs[:n], refs[n : n + d], refs[n + d :]
    b = x.shape[1]
    for j in range(n):
        x[me[0] ^ j] = blocks[j][...]
    first_stage(x, hi, lo)
    for k in range(n):
        s = dot3(fwd_hi[k], fwd_lo[k], hi[k], lo[k])
        z[k] = back_product(times(s, filt[k], True), back_hi[k], back_lo[k])
        zg[k] = back_product(times(s, spec[k], True), back_hi[k], back_lo[k])

    def store(p, r, c, value):
        y[p, pl.ds(r, ROWS), c : c + 128] = value.astype(BF16)

    last_stage(z, store)
    for j in range(n):
        outs[j][...] = y[me[0] ^ j]

    def store_grad(p, r, c, value):
        g[p, pl.ds(r, ROWS), c : c + 128] = value

    last_stage(zg, store_grad)
    per = n // d
    for j in range(d):
        for i in range(per):
            part = g[(me[1] ^ j) * per + i]
            grads[j][i * b : (i + 1) * b] = part.astype(grads[j].dtype)


def conv(me, blocks, filt, fwd, back, chunk):
    n = len(blocks)
    b, chans = blocks[0].shape
    table = pl.BlockSpec((n, 2 * b, 2 * b), lambda c, me: (0, 0, 0))
    block = pl.BlockSpec((b, chunk), lambda c, me: (0, c))
    wide = pl.BlockSpec((n, 2 * b, chunk), lambda c, me: (0, 0, c))
    out = pl.pallas_call(
        functools.partial(conv_kernel, n),
        grid_spec=pltpu.PrefetchScalarGridSpec(
            num_scalar_prefetch=1,
            grid=(chans // chunk,),
            in_specs=[block] * n + [wide] + [table] * 4,
            out_specs=[wide] + [block] * n,
            scratch_shapes=[
                pltpu.VMEM((n, b, chunk), BF16),
                pltpu.VMEM((n, 2 * b, chunk), BF16),
                pltpu.VMEM((n, 2 * b, chunk), BF16),
                pltpu.VMEM((n, 2 * b, chunk), F32),
                pltpu.VMEM((n, b, chunk), BF16),
            ],
        ),
        out_shape=[jax.ShapeDtypeStruct((n, 2 * b, chans), F32)]
        + [jax.ShapeDtypeStruct((b, chans), BF16)] * n,
        compiler_params=pltpu.CompilerParams(vmem_limit_bytes=VMEM_LIMIT),
        name="conv",
    )(me, *blocks, filt, *fwd, *back)
    return out[0], out[1:]


def backward(me, blocks, filt, spec, fwd, back, chunk, d):
    n = len(blocks)
    b, chans = blocks[0].shape
    table = pl.BlockSpec((n, 2 * b, 2 * b), lambda c, me: (0, 0, 0))
    block = pl.BlockSpec((b, chunk), lambda c, me: (0, c))
    wide = pl.BlockSpec((n, 2 * b, chunk), lambda c, me: (0, 0, c))
    grad_rows = n * b // d
    grad = pl.BlockSpec((grad_rows, chunk), lambda c, me: (0, c))
    out = pl.pallas_call(
        functools.partial(back_kernel, n, d),
        grid_spec=pltpu.PrefetchScalarGridSpec(
            num_scalar_prefetch=1,
            grid=(chans // chunk,),
            in_specs=[block] * n + [wide, wide] + [table] * 4,
            out_specs=[block] * n + [grad] * d,
            scratch_shapes=[
                pltpu.VMEM((n, b, chunk), BF16),
                pltpu.VMEM((n, 2 * b, chunk), BF16),
                pltpu.VMEM((n, 2 * b, chunk), BF16),
                pltpu.VMEM((n, 2 * b, chunk), F32),
                pltpu.VMEM((n, 2 * b, chunk), F32),
                pltpu.VMEM((n, b, chunk), BF16),
                pltpu.VMEM((n, b, chunk), F32),
            ],
        ),
        out_shape=[jax.ShapeDtypeStruct((b, chans), BF16)] * n
        + [jax.ShapeDtypeStruct((grad_rows, chans), F32 if j == 0 else BF16) for j in range(d)],
        compiler_params=pltpu.CompilerParams(vmem_limit_bytes=VMEM_LIMIT),
        name="backward",
    )(me, *blocks, filt, spec, *fwd, *back)
    return out[:n], out[n:]


def gate_kernel(n, me, gain, left, right, out_left, out_right, *refs):
    blocks, (first, second) = refs[:n], refs[n:]
    j = pl.program_id(0)
    a, b = left[...].astype(F32), right[...].astype(F32)
    direct = (out_left[...].astype(F32) * out_right[...].astype(F32)).astype(BF16).astype(F32)
    for i in range(n):

        @pl.when(j == i)
        def _():
            total = blocks[i][...].astype(F32) + gain[...] * direct
            first[...] = (a * total).astype(BF16)
            second[...] = (b * total).astype(BF16)


def gate(me, gain, left, right, pair, blocks):
    n = len(blocks)
    rows, total = left.shape
    width = total // n
    block = pl.BlockSpec((rows, width), lambda j, me: (0, me[0] ^ j))
    whole = pl.BlockSpec((rows, width), lambda j, me: (0, 0))
    return pl.pallas_call(
        functools.partial(gate_kernel, n),
        grid_spec=pltpu.PrefetchScalarGridSpec(
            num_scalar_prefetch=1,
            grid=(n,),
            in_specs=[pl.BlockSpec((1, width), lambda j, me: (0, me[0] ^ j))]
            + [block] * 4
            + [whole] * n,
            out_specs=[block, block],
        ),
        out_shape=[jax.ShapeDtypeStruct((rows, total), BF16)] * 2,
        compiler_params=pltpu.CompilerParams(vmem_limit_bytes=VMEM_LIMIT),
        name="gate",
    )(me, gain, left, right, *pair, *blocks)


def sum_kernel(d, *refs):
    parts, out = refs[:d], refs[d]
    total = parts[0][...].astype(F32)
    for part in parts[1:]:
        total = total + part[...].astype(F32)
    out[...] = total.T


def sum_grads(parts):
    rows, chans = parts[0].shape
    return pl.pallas_call(
        functools.partial(sum_kernel, len(parts)),
        out_shape=jax.ShapeDtypeStruct((chans, rows), F32),
        compiler_params=pltpu.CompilerParams(vmem_limit_bytes=VMEM_LIMIT),
        name="sum_grads",
    )(*parts)


def exchange(blocks, axis):
    n = len(blocks)
    got = [blocks[0]] + [None] * (n - 1)
    for j in range(n - 1, 0, -1):
        got[j] = lax.ppermute(blocks[j], axis, [(i, i ^ j) for i in range(n)])
    return got


def local(n, d, query_in, key_in, value_in, grad_out, filters, skip_gain):
    query, key, value, grad = query_in[0], key_in[0], value_in[0], grad_out[0]
    b = query.shape[0]
    chunk = min(256, filters.shape[0])
    me = jnp.stack([lax.axis_index("ctx"), lax.axis_index("dp")]).astype(jnp.int32)
    tabs = [jnp.asarray(t) for t in tables(n, b)]
    fwd, back = tabs[:2], tabs[2:]
    gain = skip_gain[None, :]

    kv = exchange(product_blocks(me, key, value, n), "ctx")
    wt = exchange(product_blocks(me, query, grad, n), "ctx")
    filt = filter_spectrum(filters, *fwd, chunk)
    spec, conv_blocks = conv(me, kv, filt, fwd, back, chunk)
    conv_back = exchange(conv_blocks, "ctx")
    corr_blocks, grads = backward(me, wt, filt, spec, fwd, back, chunk, d)
    corr_back = exchange(corr_blocks, "ctx")
    grads = exchange(grads, "dp")
    mixed_out, grad_query = gate(me, gain, query, grad, (key, value), conv_back)
    grad_filter = sum_grads(grads)
    grad_key, grad_value = gate(me, gain, value, key, (query, grad), corr_back)
    return mixed_out[None], grad_query[None], grad_key[None], grad_value[None], grad_filter


def solution(mesh):
    rows = P("dp", "ctx", None)
    return jax.shard_map(
        functools.partial(local, mesh.shape["ctx"], mesh.shape["dp"]),
        mesh=mesh,
        in_specs=(rows, rows, rows, rows, P("ctx", None), P()),
        out_specs=(rows, rows, rows, rows, P("ctx", "dp")),
        check_vma=False,
    )
```

time: 390 us -> 123 us (0.32); the launches traced: 384 us -> 123 us
  matrix products: 119 us -> 0 us
  other arithmetic: 77.6 us -> 0.65 us
  Pallas kernels: 0 us -> 69.7 us
  local copies, waits for them, and re-layouts: 57.6 us -> 1.61 us
  blocking collectives: 54 us -> 0 us
  waiting for transfers between devices: 41.3 us -> 14.9 us
  starting transfers between devices: 20.4 us -> 34.9 us
  between operations: 14.6 us -> 0.94 us
    dot_general x12 -> x0, matrix products: 119 us -> none  [matmul(): return jnp.einsum(form, table, data, precision=lax.Precision.HIGHEST)]
    pallas_call x0 -> x8, Pallas kernels: none -> 69.7 us  [the longest x1 19.4 us: backward(): pl.pallas_call(functools.partial(back_kernel, n, d), grid_spec=pltpu.Pref...]
    all_to_all x3 -> x0, blocking collectives: 54 us -> none  [the longest x1 18.5 us: local(): lax.all_to_all(gk_chan, 'ctx', split_axis=0, concat_axis=1, tiled=True)]
    all_to_all x5 -> x0, waiting for transfers between devices: 41.3 us -> none  [the longest x1 14.1 us: local(): lax.all_to_all(grad_rows, 'ctx', split_axis=1, concat_axis=0, tiled=True)]
    ppermute x0 -> x31, starting transfers between devices: none -> 34.9 us  [exchange(): got[j] = lax.ppermute(blocks[j], axis, [(i, i ^ j) for i in range(n)])]
    add x3 -> x0, other arithmetic: 33 us -> none  [the longest x1 17.3 us: forward_spectrum(): section[0] * cos_twid + section[1] * sin_twid]
    dot_general x3 -> x0, local copies, waits for them, and re-layouts: 24.4 us -> none  [matmul(): return jnp.einsum(form, table, data, precision=lax.Precision.HIGHEST)]
    all_to_all x5 -> x0, starting transfers between devices: 20.1 us -> none  [the longest x1 5.17 us: local(): lax.all_to_all(grad_rows, 'ctx', split_axis=1, concat_axis=0, tiled=True)]
  transfers between devices with their start and end apart: 6 -> 31, of which waited for: 5 -> 6; matrix products, arithmetic and copies ran while one was open for 11% -> 0% of each run, Pallas kernels for 0% -> 50%
where the time goes in v1:
time: 123 us
  Pallas kernels  69.7 us (57%)
  starting transfers between devices  34.9 us (28%)
  waiting for transfers between devices  14.9 us (12%)
  local copies, waits for them, and re-layouts  1.61 us (1%)
    ppermute x31, starting transfers between devices, exchange(): got[j] = lax.ppermute(blocks[j], axis, [(i, i ^ j) for i in range(n)])  34.9 us
    pallas_call x1, Pallas kernels, backward(): pl.pallas_call(functools.partial(back_kernel, n, d), grid_spec=pltpu.Pref...  19.4 us
    pallas_call x2, Pallas kernels, gate(): pl.pallas_call(functools.partial(gate_kernel, n), grid_spec=pltpu.Prefetc...  15.9 us
    ppermute x31, waiting for transfers between devices, exchange(): got[j] = lax.ppermute(blocks[j], axis, [(i, i ^ j) for i in range(n)])  14.9 us
    pallas_call x1, Pallas kernels, conv(): pl.pallas_call(functools.partial(conv_kernel, n), grid_spec=pltpu.Prefetc...  12.9 us
    pallas_call x2, Pallas kernels, product_blocks(): pl.pallas_call(functools.partial(product_kernel, n), grid_spec=pltpu.Pref...  12.2 us
    pallas_call x1, Pallas kernels, filter_spectrum(): pl.pallas_call(filter_kernel, grid=(chans // chunk,), in_specs=[pl.BlockS...  6.98 us
  transfers between devices with their start and end apart: 31, of which 6 were waited for; matrix products, arithmetic and copies ran while one was open for 0% of the time, Pallas kernels for 50%

profile of v1, /device:TPU:0, one launch (start us, length us, event | category | flops | bytes accessed | tf_op | source)
XLA Modules:
  0.0 122.7 jit_solution(8748396094691762293)
XLA Ops:
  1.3 6.1 %products.3 = (bf16[128,512]{1,0:T(8,128)(2,1)}, bf16[128,512]{1,0:T(8,128)(2,1)}, bf16[128,512]{1,0:T(8,128)(2,1)}, bf16[128,512]{1,0:T(8,128)(2,1)}, bf16[128,...) custom-call(s32[2]{0:T(128)} %pad_add_fusion.me, ...), custom_call_target="tpu_custom_call" | custom-call | tf_op jit(solution)/shard_map/products/pallas_call | solution.py:150
  7.9 2.5 %collective-permute-start.15 = (bf16[128,512]{1,0:T(8,128)(2,1)}, bf16[128,512]{1,0:T(8,128)(2,1)S(1)}, u32[]{:S(2)}, u32[]{:S(2)}) collective-permute-start(bf16[128,512]{1,0:T(8,128)(2,1)} %get-tuple-element.66), channel_id=1, source_target_pairs={{0,2},{1,3},{2,0},{3,1},{4,6},{5,7},{6,4},{7,5},{8,10},{9,11},{10,... | collective-permute-start | bytes 393224 | tf_op jit(solution)/shard_map/ppermute | solution.py:369
  10.4 6.1 %products.2 = (bf16[128,512]{1,0:T(8,128)(2,1)}, bf16[128,512]{1,0:T(8,128)(2,1)}, bf16[128,512]{1,0:T(8,128)(2,1)}, bf16[128,512]{1,0:T(8,128)(2,1)}, bf16[128,...) custom-call(s32[2]{0:T(128)} %pad_add_fusion.me, ...), custom_call_target="tpu_custom_call" | custom-call | tf_op jit(solution)/shard_map/products/pallas_call | solution.py:150
  17.0 1.4 %collective-permute-start.2 = (bf16[128,512]{1,0:T(8,128)(2,1)}, bf16[128,512]{1,0:T(8,128)(2,1)S(1)}, u32[]{:S(2)}, u32[]{:S(2)}) collective-permute-start(bf16[128,512]{1,0:T(8,128)(2,1)} %get-tuple-element.49), channel_id=1, source_target_pairs={{0,3},{1,2},{2,1},{3,0},{4,7},{5,6},{6,5},{7,4},{8,11},{9,10},{10,... | collective-permute-start | bytes 393224 | tf_op jit(solution)/shard_map/ppermute | solution.py:369
  18.4 1.5 %collective-permute-start.3 = (bf16[128,512]{1,0:T(8,128)(2,1)}, bf16[128,512]{1,0:T(8,128)(2,1)S(1)}, u32[]{:S(2)}, u32[]{:S(2)}) collective-permute-start(bf16[128,512]{1,0:T(8,128)(2,1)} %get-tuple-element.50), channel_id=1, source_target_pairs={{0,4},{1,5},{2,6},{3,7},{4,0},{5,1},{6,2},{7,3},{8,12},{9,13},{10,... | collective-permute-start | bytes 393224 | tf_op jit(solution)/shard_map/ppermute | solution.py:369
  20.2 1.5 %collective-permute-start.5 = (bf16[128,512]{1,0:T(8,128)(2,1)}, bf16[128,512]{1,0:T(8,128)(2,1)S(1)}, u32[]{:S(2)}, u32[]{:S(2)}) collective-permute-start(bf16[128,512]{1,0:T(8,128)(2,1)} %get-tuple-element.52), channel_id=1, source_target_pairs={{0,6},{1,7},{2,4},{3,5},{4,2},{5,3},{6,0},{7,1},{8,14},{9,15},{10,... | collective-permute-start | bytes 393224 | tf_op jit(solution)/shard_map/ppermute | solution.py:369
  21.7 1.5 %collective-permute-done.1.refs_2_ = bf16[128,512]{1,0:T(8,128)(2,1)S(1)} collective-permute-done((bf16[128,512]{1,0:T(8,128)(2,1)}, bf16[128,512]{1,0:T(8,128)(2,1)S(1)}, u32[]{:S(2)}, u32[]{:S(2)}) %collective-permute-start.1) | collective-permute-done | bytes 131104 | tf_op jit(solution)/shard_map/ppermute | solution.py:369
  23.3 1.6 %collective-permute-done.2.refs_3_ = bf16[128,512]{1,0:T(8,128)(2,1)S(1)} collective-permute-done((bf16[128,512]{1,0:T(8,128)(2,1)}, bf16[128,512]{1,0:T(8,128)(2,1)S(1)}, u32[]{:S(2)}, u32[]{:S(2)}) %collective-permute-start.2) | collective-permute-done | bytes 131104 | tf_op jit(solution)/shard_map/ppermute | solution.py:369
  24.9 1.2 collective-permute-start.16
  26.0 1.8 %collective-permute-start.17 = (bf16[128,512]{1,0:T(8,128)(2,1)}, bf16[128,512]{1,0:T(8,128)(2,1)S(1)}, u32[]{:S(2)}, u32[]{:S(2)}) collective-permute-start(bf16[128,512]{1,0:T(8,128)(2,1)} %get-tuple-element.68), channel_id=1, source_target_pairs={{0,4},{1,5},{2,6},{3,7},{4,0},{5,1},{6,2},{7,3},{8,12},{9,13},{10,... | collective-permute-start | bytes 393224 | tf_op jit(solution)/shard_map/ppermute | solution.py:369
  27.8 4.7 %collective-permute-done.4.refs_5_ = bf16[128,512]{1,0:T(8,128)(2,1)S(1)} collective-permute-done((bf16[128,512]{1,0:T(8,128)(2,1)}, bf16[128,512]{1,0:T(8,128)(2,1)S(1)}, u32[]{:S(2)}, u32[]{:S(2)}) %collective-permute-start.4) | collective-permute-done | bytes 131104 | tf_op jit(solution)/shard_map/ppermute | solution.py:369
  32.5 2.1 %collective-permute-start.18 = (bf16[128,512]{1,0:T(8,128)(2,1)}, bf16[128,512]{1,0:T(8,128)(2,1)S(1)}, u32[]{:S(2)}, u32[]{:S(2)}) collective-permute-start(bf16[128,512]{1,0:T(8,128)(2,1)} %get-tuple-element.69), channel_id=1, source_target_pairs={{0,5},{1,4},{2,7},{3,6},{4,1},{5,0},{6,3},{7,2},{8,13},{9,12},{10,... | collective-permute-start | bytes 393224 | tf_op jit(solution)/shard_map/ppermute | solution.py:369
  34.8 1.5 %collective-permute-start.20 = (bf16[128,512]{1,0:T(8,128)(2,1)}, bf16[128,512]{1,0:T(8,128)(2,1)S(1)}, u32[]{:S(2)}, u32[]{:S(2)}) collective-permute-start(bf16[128,512]{1,0:T(8,128)(2,1)} %get-tuple-element.71), channel_id=1, source_target_pairs={{0,7},{1,6},{2,5},{3,4},{4,3},{5,2},{6,1},{7,0},{8,15},{9,14},{10,... | collective-permute-start | bytes 393224 | tf_op jit(solution)/shard_map/ppermute | solution.py:369
  36.3 7.0 %filter_spectrum.1.refs_8_ = f32[8,256,512]{2,1,0:T(8,128)} custom-call(f32[512,1024]{1,0:T(8,128)} %filt.1, bf16[8,256,256]{2,1,0:T(8,128)(2,1)} %constant.16.clone.fwd_hi.refs_9_.refs_10_, bf16[8,256,256]{2,1,0:T(8,128)(2,1)} %constant.17.clone.fwd_lo.refs_10_.refs_11_), custom_call_target="tpu_custom_call" | custom-call | tf_op jit(solution)/shard_map/filter_spectrum/pallas_call | solution.py:187
  43.4 12.9 %conv.1 = (f32[8,256,512]{2,1,0:T(8,128)}, bf16[128,512]{1,0:T(8,128)(2,1)}, bf16[128,512]{1,0:T(8,128)(2,1)}, bf16[128,512]{1,0:T(8,128)(2,1)}, bf16[128,512]{1...) custom-call(s32[2]{0:T(128)} %pad_add_fusion.me, ...), custom_call_target="tpu_custom_call" | custom-call | tf_op jit(solution)/shard_map/conv/pallas_call | solution.py:255
  56.3 1.4 %collective-permute-start.7 = (bf16[128,512]{1,0:T(8,128)(2,1)}, bf16[128,512]{1,0:T(8,128)(2,1)S(1)}, u32[]{:S(2)}, u32[]{:S(2)}) collective-permute-start(bf16[128,512]{1,0:T(8,128)(2,1)} %get-tuple-element.55), channel_id=1, source_target_pairs={{0,1},{1,0},{2,3},{3,2},{4,5},{5,4},{6,7},{7,6},{8,9},{9,8},{10,11... | collective-permute-start | bytes 393224 | tf_op jit(solution)/shard_map/ppermute | solution.py:369
  58.2 0.9 collective-permute-start.9
  59.6 1.6 %collective-permute-start.11 = (bf16[128,512]{1,0:T(8,128)(2,1)}, bf16[128,512]{1,0:T(8,128)(2,1)S(1)}, u32[]{:S(2)}, u32[]{:S(2)}) collective-permute-start(bf16[128,512]{1,0:T(8,128)(2,1)} %get-tuple-element.59), channel_id=1, source_target_pairs={{0,5},{1,4},{2,7},{3,6},{4,1},{5,0},{6,3},{7,2},{8,13},{9,12},{10,... | collective-permute-start | bytes 393224 | tf_op jit(solution)/shard_map/ppermute | solution.py:369
  61.2 19.4 %backward.1 = (bf16[128,512]{1,0:T(8,128)(2,1)}, bf16[128,512]{1,0:T(8,128)(2,1)}, bf16[128,512]{1,0:T(8,128)(2,1)}, bf16[128,512]{1,0:T(8,128)(2,1)}, bf16[128,...) custom-call(s32[2]{0:T(128)} %pad_add_fusion.me, ...), custom_call_target="tpu_custom_call" | custom-call | tf_op jit(solution)/shard_map/backward/pallas_call | solution.py:286
  81.5 1.1 collective-permute-start.23
  83.2 1.2 collective-permute-start.25
  85.2 2.2 %collective-permute-done.22.refs_2_ = bf16[128,512]{1,0:T(8,128)(2,1)S(1)} collective-permute-done((bf16[128,512]{1,0:T(8,128)(2,1)}, bf16[128,512]{1,0:T(8,128)(2,1)S(1)}, u32[]{:S(2)}, u32[]{:S(2)}) %collective-permute-start.22) | collective-permute-done | bytes 131104 | tf_op jit(solution)/shard_map/ppermute | solution.py:369
  87.4 1.9 %collective-permute-done.23.refs_3_ = bf16[128,512]{1,0:T(8,128)(2,1)S(1)} collective-permute-done((bf16[128,512]{1,0:T(8,128)(2,1)}, bf16[128,512]{1,0:T(8,128)(2,1)S(1)}, u32[]{:S(2)}, u32[]{:S(2)}) %collective-permute-start.23) | collective-permute-done | bytes 131104 | tf_op jit(solution)/shard_map/ppermute | solution.py:369
  89.2 1.6 %collective-permute-start.28 = (bf16[256,512]{1,0:T(8,128)(2,1)}, bf16[256,512]{1,0:T(8,128)(2,1)S(1)}, u32[]{:S(2)}, u32[]{:S(2)}) collective-permute-start(bf16[256,512]{1,0:T(8,128)(2,1)} %get-tuple-element.84), channel_id=1, source_target_pairs={{0,8},{8,0},{16,24},{24,16},{1,9},{9,1},{17,25},{25,17},{2,10},{10... | collective-permute-start | bytes 786440 | tf_op jit(solution)/shard_map/ppermute | solution.py:369
  90.8 2.6 %collective-permute-start.29 = (bf16[256,512]{1,0:T(8,128)(2,1)}, bf16[256,512]{1,0:T(8,128)(2,1)S(1)}, u32[]{:S(2)}, u32[]{:S(2)}) collective-permute-start(bf16[256,512]{1,0:T(8,128)(2,1)} %get-tuple-element.85), channel_id=1, source_target_pairs={{0,16},{8,24},{16,0},{24,8},{1,17},{9,25},{17,1},{25,9},{2,18},{10... | collective-permute-start | bytes 786440 | tf_op jit(solution)/shard_map/ppermute | solution.py:369
  93.4 3.1 %collective-permute-done.25.refs_5_ = bf16[128,512]{1,0:T(8,128)(2,1)S(1)} collective-permute-done((bf16[128,512]{1,0:T(8,128)(2,1)}, bf16[128,512]{1,0:T(8,128)(2,1)S(1)}, u32[]{:S(2)}, u32[]{:S(2)}) %collective-permute-start.25) | collective-permute-done | bytes 131104 | tf_op jit(solution)/shard_map/ppermute | solution.py:369
  96.5 3.6 %collective-permute-start.30 = (bf16[256,512]{1,0:T(8,128)(2,1)}, bf16[256,512]{1,0:T(8,128)(2,1)S(1)}, u32[]{:S(2)}, u32[]{:S(2)}) collective-permute-start(bf16[256,512]{1,0:T(8,128)(2,1)} %get-tuple-element.86), channel_id=1, source_target_pairs={{0,24},{8,16},{16,8},{24,0},{1,25},{9,17},{17,9},{25,1},{2,26},{10... | collective-permute-start | bytes 786440 | tf_op jit(solution)/shard_map/ppermute | solution.py:369
  100.1 1.2 collective-permute-start.12
  101.2 1.6 %collective-permute-start.13 = (bf16[128,512]{1,0:T(8,128)(2,1)S(1)}, bf16[128,512]{1,0:T(8,128)(2,1)S(1)}, u32[]{:S(2)}, u32[]{:S(2)}) collective-permute-start(bf16[128,512]{1,0:T(8,128)(2,1)S(1)} %copy-done.31), channel_id=1, source_target_pairs={{0,7},{1,6},{2,5},{3,4},{4,3},{5,2},{6,1},{7,0},{8,15},{9,14},{10,... | collective-permute-start | bytes 393224 | tf_op jit(solution)/shard_map/ppermute | solution.py:369
  102.9 8.0 %gate.3 = (bf16[128,4096]{1,0:T(8,128)(2,1)}, bf16[128,4096]{1,0:T(8,128)(2,1)}) custom-call(s32[2]{0:T(128)} %pad_add_fusion.me, f32[1,4096]{1,0:T(1,128)} %bitcast.23, bf16[128,4096]{1,0:T(8,128)(2,1)} %bitcast.21, bf16[128,4096]{1,0:T(8,128)(2,1)} %bitcast.18, bf16[128,4096]{1,0:T(8,128)(2,1)} %bitcast.12, bf16[128,4096]{1,0:T(8,128)(2,1)} %bitcast.15, ...), custom_call_target="tpu_custom_call" | custom-call | tf_op jit(solution)/shard_map/gate/pallas_call | solution.py:331
  111.6 7.9 %gate.2 = (bf16[128,4096]{1,0:T(8,128)(2,1)}, bf16[128,4096]{1,0:T(8,128)(2,1)}) custom-call(s32[2]{0:T(128)} %pad_add_fusion.me, f32[1,4096]{1,0:T(1,128)} %bitcast.24, bf16[128,4096]{1,0:T(8,128)(2,1)} %bitcast.13, bf16[128,4096]{1,0:T(8,128)(2,1)} %bitcast.16, bf16[128,4096]{1,0:T(8,128)(2,1)} %bitcast.19, bf16[128,4096]{1,0:T(8,128)(2,1)} %bitcast.22, ...), custom_call_target="tpu_custom_call" | custom-call | tf_op jit(solution)/shard_map/gate/pallas_call | solution.py:331
  120.4 2.3 %sum_grads.1 = f32[512,256]{1,0:T(8,128)} custom-call(f32[256,512]{1,0:T(8,128)} %get-tuple-element.83.refs_0_, bf16[256,512]{1,0:T(8,128)(2,1)} %copy-done, bf16[256,512]{1,0:T(8,128)(2,1)} %copy-done.1, bf16[256,512]{1,0:T(8,128)(2,1)} %copy-done.2), custom_call_target="tpu_custom_call" | custom-call | tf_op jit(solution)/shard_map/sum_grads/pallas_call | solution.py:357
  (105 shorter events, 7.1 us)
Async XLA Ops:
  7.4 11.0 %collective-permute-start.14 = (bf16[128,512]{1,0:T(8,128)(2,1)}, bf16[128,512]{1,0:T(8,128)(2,1)S(1)}, u32[]{:S(2)}, u32[]{:S(2)}) collective-permute-start(bf16[128,512]{1,0:T(8,128)(2,1)} %get-tuple-element.65), channel_id=1, source_target_pairs={{0,1},{1,0},{2,3},{3,2},{4,5},{5,4},{6,7},{7,6},{8,9},{9,8},{10,11... | collective-permute-start | bytes 393224 | tf_op jit(solution)/shard_map/ppermute | solution.py:369
  7.9 12.0 %collective-permute-start.15 = (bf16[128,512]{1,0:T(8,128)(2,1)}, bf16[128,512]{1,0:T(8,128)(2,1)S(1)}, u32[]{:S(2)}, u32[]{:S(2)}) collective-permute-start(bf16[128,512]{1,0:T(8,128)(2,1)} %get-tuple-element.66), channel_id=1, source_target_pairs={{0,2},{1,3},{2,0},{3,1},{4,6},{5,7},{6,4},{7,5},{8,10},{9,11},{10,... | collective-permute-start | bytes 393224 | tf_op jit(solution)/shard_map/ppermute | solution.py:369
  16.5 3.7 %collective-permute-start = (bf16[128,512]{1,0:T(8,128)(2,1)}, bf16[128,512]{1,0:T(8,128)(2,1)S(1)}, u32[]{:S(2)}, u32[]{:S(2)}) collective-permute-start(bf16[128,512]{1,0:T(8,128)(2,1)} %get-tuple-element.47), channel_id=1, source_target_pairs={{0,1},{1,0},{2,3},{3,2},{4,5},{5,4},{6,7},{7,6},{8,9},{9,8},{10,11... | collective-permute-start | bytes 393224 | tf_op jit(solution)/shard_map/ppermute | solution.py:369
  16.7 6.5 %collective-permute-start.1 = (bf16[128,512]{1,0:T(8,128)(2,1)}, bf16[128,512]{1,0:T(8,128)(2,1)S(1)}, u32[]{:S(2)}, u32[]{:S(2)}) collective-permute-start(bf16[128,512]{1,0:T(8,128)(2,1)} %get-tuple-element.48), channel_id=1, source_target_pairs={{0,2},{1,3},{2,0},{3,1},{4,6},{5,7},{6,4},{7,5},{8,10},{9,11},{10,... | collective-permute-start | bytes 393224 | tf_op jit(solution)/shard_map/ppermute | solution.py:369
  17.0 7.9 %collective-permute-start.2 = (bf16[128,512]{1,0:T(8,128)(2,1)}, bf16[128,512]{1,0:T(8,128)(2,1)S(1)}, u32[]{:S(2)}, u32[]{:S(2)}) collective-permute-start(bf16[128,512]{1,0:T(8,128)(2,1)} %get-tuple-element.49), channel_id=1, source_target_pairs={{0,3},{1,2},{2,1},{3,0},{4,7},{5,6},{6,5},{7,4},{8,11},{9,10},{10,... | collective-permute-start | bytes 393224 | tf_op jit(solution)/shard_map/ppermute | solution.py:369
  18.4 7.6 %collective-permute-start.3 = (bf16[128,512]{1,0:T(8,128)(2,1)}, bf16[128,512]{1,0:T(8,128)(2,1)S(1)}, u32[]{:S(2)}, u32[]{:S(2)}) collective-permute-start(bf16[128,512]{1,0:T(8,128)(2,1)} %get-tuple-element.50), channel_id=1, source_target_pairs={{0,4},{1,5},{2,6},{3,7},{4,0},{5,1},{6,2},{7,3},{8,12},{9,13},{10,... | collective-permute-start | bytes 393224 | tf_op jit(solution)/shard_map/ppermute | solution.py:369
  19.9 12.6 %collective-permute-start.4 = (bf16[128,512]{1,0:T(8,128)(2,1)}, bf16[128,512]{1,0:T(8,128)(2,1)S(1)}, u32[]{:S(2)}, u32[]{:S(2)}) collective-permute-start(bf16[128,512]{1,0:T(8,128)(2,1)} %get-tuple-element.51), channel_id=1, source_target_pairs={{0,5},{1,4},{2,7},{3,6},{4,1},{5,0},{6,3},{7,2},{8,13},{9,12},{10,... | collective-permute-start | bytes 393224 | tf_op jit(solution)/shard_map/ppermute | solution.py:369
  20.2 14.4 %collective-permute-start.5 = (bf16[128,512]{1,0:T(8,128)(2,1)}, bf16[128,512]{1,0:T(8,128)(2,1)S(1)}, u32[]{:S(2)}, u32[]{:S(2)}) collective-permute-start(bf16[128,512]{1,0:T(8,128)(2,1)} %get-tuple-element.52), channel_id=1, source_target_pairs={{0,6},{1,7},{2,4},{3,5},{4,2},{5,3},{6,0},{7,1},{8,14},{9,15},{10,... | collective-permute-start | bytes 393224 | tf_op jit(solution)/shard_map/ppermute | solution.py:369
  23.2 11.6 %collective-permute-start.6 = (bf16[128,512]{1,0:T(8,128)(2,1)}, bf16[128,512]{1,0:T(8,128)(2,1)S(1)}, u32[]{:S(2)}, u32[]{:S(2)}) collective-permute-start(bf16[128,512]{1,0:T(8,128)(2,1)} %get-tuple-element.53), channel_id=1, source_target_pairs={{0,7},{1,6},{2,5},{3,4},{4,3},{5,2},{6,1},{7,0},{8,15},{9,14},{10,... | collective-permute-start | bytes 393224 | tf_op jit(solution)/shard_map/ppermute | solution.py:369
  24.9 31.4 %collective-permute-start.16 = (bf16[128,512]{1,0:T(8,128)(2,1)}, bf16[128,512]{1,0:T(8,128)(2,1)S(1)}, u32[]{:S(2)}, u32[]{:S(2)}) collective-permute-start(bf16[128,512]{1,0:T(8,128)(2,1)} %get-tuple-element.67), channel_id=1, source_target_pairs={{0,3},{1,2},{2,1},{3,0},{4,7},{5,6},{6,5},{7,4},{8,11},{9,10},{10,... | collective-permute-start | bytes 393224 | tf_op jit(solution)/shard_map/ppermute | solution.py:369
  26.0 31.6 %collective-permute-start.17 = (bf16[128,512]{1,0:T(8,128)(2,1)}, bf16[128,512]{1,0:T(8,128)(2,1)S(1)}, u32[]{:S(2)}, u32[]{:S(2)}) collective-permute-start(bf16[128,512]{1,0:T(8,128)(2,1)} %get-tuple-element.68), channel_id=1, source_target_pairs={{0,4},{1,5},{2,6},{3,7},{4,0},{5,1},{6,2},{7,3},{8,12},{9,13},{10,... | collective-permute-start | bytes 393224 | tf_op jit(solution)/shard_map/ppermute | solution.py:369
  32.5 25.7 %collective-permute-start.18 = (bf16[128,512]{1,0:T(8,128)(2,1)}, bf16[128,512]{1,0:T(8,128)(2,1)S(1)}, u32[]{:S(2)}, u32[]{:S(2)}) collective-permute-start(bf16[128,512]{1,0:T(8,128)(2,1)} %get-tuple-element.69), channel_id=1, source_target_pairs={{0,5},{1,4},{2,7},{3,6},{4,1},{5,0},{6,3},{7,2},{8,13},{9,12},{10,... | collective-permute-start | bytes 393224 | tf_op jit(solution)/shard_map/ppermute | solution.py:369
  34.6 24.6 %collective-permute-start.19 = (bf16[128,512]{1,0:T(8,128)(2,1)}, bf16[128,512]{1,0:T(8,128)(2,1)S(1)}, u32[]{:S(2)}, u32[]{:S(2)}) collective-permute-start(bf16[128,512]{1,0:T(8,128)(2,1)} %get-tuple-element.70), channel_id=1, source_target_pairs={{0,6},{1,7},{2,4},{3,5},{4,2},{5,3},{6,0},{7,1},{8,14},{9,15},{10,... | collective-permute-start | bytes 393224 | tf_op jit(solution)/shard_map/ppermute | solution.py:369
  34.8 24.8 %collective-permute-start.20 = (bf16[128,512]{1,0:T(8,128)(2,1)}, bf16[128,512]{1,0:T(8,128)(2,1)S(1)}, u32[]{:S(2)}, u32[]{:S(2)}) collective-permute-start(bf16[128,512]{1,0:T(8,128)(2,1)} %get-tuple-element.71), channel_id=1, source_target_pairs={{0,7},{1,6},{2,5},{3,4},{4,3},{5,2},{6,1},{7,0},{8,15},{9,14},{10,... | collective-permute-start | bytes 393224 | tf_op jit(solution)/shard_map/ppermute | solution.py:369
  56.3 24.4 %collective-permute-start.7 = (bf16[128,512]{1,0:T(8,128)(2,1)}, bf16[128,512]{1,0:T(8,128)(2,1)S(1)}, u32[]{:S(2)}, u32[]{:S(2)}) collective-permute-start(bf16[128,512]{1,0:T(8,128)(2,1)} %get-tuple-element.55), channel_id=1, source_target_pairs={{0,1},{1,0},{2,3},{3,2},{4,5},{5,4},{6,7},{7,6},{8,9},{9,8},{10,11... | collective-permute-start | bytes 393224 | tf_op jit(solution)/shard_map/ppermute | solution.py:369
  57.7 23.1 %collective-permute-start.8 = (bf16[128,512]{1,0:T(8,128)(2,1)}, bf16[128,512]{1,0:T(8,128)(2,1)S(1)}, u32[]{:S(2)}, u32[]{:S(2)}) collective-permute-start(bf16[128,512]{1,0:T(8,128)(2,1)} %get-tuple-element.56), channel_id=1, source_target_pairs={{0,2},{1,3},{2,0},{3,1},{4,6},{5,7},{6,4},{7,5},{8,10},{9,11},{10,... | collective-permute-start | bytes 393224 | tf_op jit(solution)/shard_map/ppermute | solution.py:369
  58.2 23.3 %collective-permute-start.9 = (bf16[128,512]{1,0:T(8,128)(2,1)}, bf16[128,512]{1,0:T(8,128)(2,1)S(1)}, u32[]{:S(2)}, u32[]{:S(2)}) collective-permute-start(bf16[128,512]{1,0:T(8,128)(2,1)} %get-tuple-element.57), channel_id=1, source_target_pairs={{0,3},{1,2},{2,1},{3,0},{4,7},{5,6},{6,5},{7,4},{8,11},{9,10},{10,... | collective-permute-start | bytes 393224 | tf_op jit(solution)/shard_map/ppermute | solution.py:369
  59.1 23.5 %collective-permute-start.10 = (bf16[128,512]{1,0:T(8,128)(2,1)}, bf16[128,512]{1,0:T(8,128)(2,1)S(1)}, u32[]{:S(2)}, u32[]{:S(2)}) collective-permute-start(bf16[128,512]{1,0:T(8,128)(2,1)} %get-tuple-element.58), channel_id=1, source_target_pairs={{0,4},{1,5},{2,6},{3,7},{4,0},{5,1},{6,2},{7,3},{8,12},{9,13},{10,... | collective-permute-start | bytes 393224 | tf_op jit(solution)/shard_map/ppermute | solution.py:369
  59.6 23.5 %collective-permute-start.11 = (bf16[128,512]{1,0:T(8,128)(2,1)}, bf16[128,512]{1,0:T(8,128)(2,1)S(1)}, u32[]{:S(2)}, u32[]{:S(2)}) collective-permute-start(bf16[128,512]{1,0:T(8,128)(2,1)} %get-tuple-element.59), channel_id=1, source_target_pairs={{0,5},{1,4},{2,7},{3,6},{4,1},{5,0},{6,3},{7,2},{8,13},{9,12},{10,... | collective-permute-start | bytes 393224 | tf_op jit(solution)/shard_map/ppermute | solution.py:369
  61.2 40.0 %copy-start.31 = (bf16[128,512]{1,0:T(8,128)(2,1)S(1)}, bf16[128,512]{1,0:T(8,128)(2,1)}, u32[]{:S(2)}) copy-start(bf16[128,512]{1,0:T(8,128)(2,1)} %get-tuple-element.61) | copy-start | bytes 393220
  80.7 3.7 %collective-permute-start.21 = (bf16[128,512]{1,0:T(8,128)(2,1)}, bf16[128,512]{1,0:T(8,128)(2,1)S(1)}, u32[]{:S(2)}, u32[]{:S(2)}) collective-permute-start(bf16[128,512]{1,0:T(8,128)(2,1)} %get-tuple-element.74), channel_id=1, source_target_pairs={{0,1},{1,0},{2,3},{3,2},{4,5},{5,4},{6,7},{7,6},{8,9},{9,8},{10,11... | collective-permute-start | bytes 393224 | tf_op jit(solution)/shard_map/ppermute | solution.py:369
  80.8 6.5 %collective-permute-start.22 = (bf16[128,512]{1,0:T(8,128)(2,1)}, bf16[128,512]{1,0:T(8,128)(2,1)S(1)}, u32[]{:S(2)}, u32[]{:S(2)}) collective-permute-start(bf16[128,512]{1,0:T(8,128)(2,1)} %get-tuple-element.75), channel_id=1, source_target_pairs={{0,2},{1,3},{2,0},{3,1},{4,6},{5,7},{6,4},{7,5},{8,10},{9,11},{10,... | collective-permute-start | bytes 393224 | tf_op jit(solution)/shard_map/ppermute | solution.py:369
  81.5 7.7 %collective-permute-start.23 = (bf16[128,512]{1,0:T(8,128)(2,1)}, bf16[128,512]{1,0:T(8,128)(2,1)S(1)}, u32[]{:S(2)}, u32[]{:S(2)}) collective-permute-start(bf16[128,512]{1,0:T(8,128)(2,1)} %get-tuple-element.76), channel_id=1, source_target_pairs={{0,3},{1,2},{2,1},{3,0},{4,7},{5,6},{6,5},{7,4},{8,11},{9,10},{10,... | collective-permute-start | bytes 393224 | tf_op jit(solution)/shard_map/ppermute | solution.py:369
  82.6 8.2 %collective-permute-start.24 = (bf16[128,512]{1,0:T(8,128)(2,1)}, bf16[128,512]{1,0:T(8,128)(2,1)S(1)}, u32[]{:S(2)}, u32[]{:S(2)}) collective-permute-start(bf16[128,512]{1,0:T(8,128)(2,1)} %get-tuple-element.77), channel_id=1, source_target_pairs={{0,4},{1,5},{2,6},{3,7},{4,0},{5,1},{6,2},{7,3},{8,12},{9,13},{10,... | collective-permute-start | bytes 393224 | tf_op jit(solution)/shard_map/ppermute | solution.py:369
  83.2 13.3 %collective-permute-start.25 = (bf16[128,512]{1,0:T(8,128)(2,1)}, bf16[128,512]{1,0:T(8,128)(2,1)S(1)}, u32[]{:S(2)}, u32[]{:S(2)}) collective-permute-start(bf16[128,512]{1,0:T(8,128)(2,1)} %get-tuple-element.78), channel_id=1, source_target_pairs={{0,5},{1,4},{2,7},{3,6},{4,1},{5,0},{6,3},{7,2},{8,13},{9,12},{10,... | collective-permute-start | bytes 393224 | tf_op jit(solution)/shard_map/ppermute | solution.py:369
  84.3 15.7 %collective-permute-start.26 = (bf16[128,512]{1,0:T(8,128)(2,1)}, bf16[128,512]{1,0:T(8,128)(2,1)S(1)}, u32[]{:S(2)}, u32[]{:S(2)}) collective-permute-start(bf16[128,512]{1,0:T(8,128)(2,1)} %get-tuple-element.79), channel_id=1, source_target_pairs={{0,6},{1,7},{2,4},{3,5},{4,2},{5,3},{6,0},{7,1},{8,14},{9,15},{10,... | collective-permute-start | bytes 393224 | tf_op jit(solution)/shard_map/ppermute | solution.py:369
  87.3 13.9 %collective-permute-start.27 = (bf16[128,512]{1,0:T(8,128)(2,1)}, bf16[128,512]{1,0:T(8,128)(2,1)S(1)}, u32[]{:S(2)}, u32[]{:S(2)}) collective-permute-start(bf16[128,512]{1,0:T(8,128)(2,1)} %get-tuple-element.80), channel_id=1, source_target_pairs={{0,7},{1,6},{2,5},{3,4},{4,3},{5,2},{6,1},{7,0},{8,15},{9,14},{10,... | collective-permute-start | bytes 393224 | tf_op jit(solution)/shard_map/ppermute | solution.py:369
  89.2 30.3 %collective-permute-start.28 = (bf16[256,512]{1,0:T(8,128)(2,1)}, bf16[256,512]{1,0:T(8,128)(2,1)S(1)}, u32[]{:S(2)}, u32[]{:S(2)}) collective-permute-start(bf16[256,512]{1,0:T(8,128)(2,1)} %get-tuple-element.84), channel_id=1, source_target_pairs={{0,8},{8,0},{16,24},{24,16},{1,9},{9,1},{17,25},{25,17},{2,10},{10... | collective-permute-start | bytes 786440 | tf_op jit(solution)/shard_map/ppermute | solution.py:369
  90.8 28.8 %collective-permute-start.29 = (bf16[256,512]{1,0:T(8,128)(2,1)}, bf16[256,512]{1,0:T(8,128)(2,1)S(1)}, u32[]{:S(2)}, u32[]{:S(2)}) collective-permute-start(bf16[256,512]{1,0:T(8,128)(2,1)} %get-tuple-element.85), channel_id=1, source_target_pairs={{0,16},{8,24},{16,0},{24,8},{1,17},{9,25},{17,1},{25,9},{2,18},{10... | collective-permute-start | bytes 786440 | tf_op jit(solution)/shard_map/ppermute | solution.py:369
  96.5 23.1 %collective-permute-start.30 = (bf16[256,512]{1,0:T(8,128)(2,1)}, bf16[256,512]{1,0:T(8,128)(2,1)S(1)}, u32[]{:S(2)}, u32[]{:S(2)}) collective-permute-start(bf16[256,512]{1,0:T(8,128)(2,1)} %get-tuple-element.86), channel_id=1, source_target_pairs={{0,24},{8,16},{16,8},{24,0},{1,25},{9,17},{17,9},{25,1},{2,26},{10... | collective-permute-start | bytes 786440 | tf_op jit(solution)/shard_map/ppermute | solution.py:369
  100.1 10.8 %collective-permute-start.12 = (bf16[128,512]{1,0:T(8,128)(2,1)S(1)}, bf16[128,512]{1,0:T(8,128)(2,1)S(1)}, u32[]{:S(2)}, u32[]{:S(2)}) collective-permute-start(bf16[128,512]{1,0:T(8,128)(2,1)S(1)} %copy-done.32), channel_id=1, source_target_pairs={{0,6},{1,7},{2,4},{3,5},{4,2},{5,3},{6,0},{7,1},{8,14},{9,15},{10,... | collective-permute-start | bytes 393224 | tf_op jit(solution)/shard_map/ppermute | solution.py:369
  101.2 9.7 %collective-permute-start.13 = (bf16[128,512]{1,0:T(8,128)(2,1)S(1)}, bf16[128,512]{1,0:T(8,128)(2,1)S(1)}, u32[]{:S(2)}, u32[]{:S(2)}) collective-permute-start(bf16[128,512]{1,0:T(8,128)(2,1)S(1)} %copy-done.31), channel_id=1, source_target_pairs={{0,7},{1,6},{2,5},{3,4},{4,3},{5,2},{6,1},{7,0},{8,15},{9,14},{10,... | collective-permute-start | bytes 393224 | tf_op jit(solution)/shard_map/ppermute | solution.py:369
  (32 other events, 429.8 us)

commit v2 on v0

v2 whole, which is shorter than its diff:
```python
import functools
import math

import jax
import jax.numpy as jnp
import ml_dtypes
import numpy as np
from jax import lax
from jax.experimental import pallas as pl
from jax.experimental.pallas import tpu as pltpu
from jax.sharding import PartitionSpec as P

F32 = jnp.float32
BF16 = jnp.bfloat16
VMEM_LIMIT = 56 * 1024 * 1024
CLASSES = 8
ROWS = 16
HALVES = 2
PARAMS = pltpu.CompilerParams(vmem_limit_bytes=VMEM_LIMIT)
VMEM = pl.BlockSpec(memory_space=pltpu.VMEM)
ANY = pl.BlockSpec(memory_space=pl.ANY)


def tables(length):
    m2 = length // CLASSES
    c = np.arange(CLASSES)[:, None, None]
    j = np.arange(m2)[None, :, None]
    m = np.arange(m2)[None, None, :]
    turn = ((CLASSES * m + c) * (2 * j + 1)) % (4 * length)
    angle = 2 * np.pi * turn / (4 * length)
    forward = np.concatenate([np.cos(angle), -np.sin(angle)], 1)
    back = np.swapaxes(forward, 1, 2) / length

    def parts(x):
        hi = x.astype(ml_dtypes.bfloat16)
        return hi, (x - hi.astype(np.float64)).astype(ml_dtypes.bfloat16)

    return np.concatenate(parts(forward), 2), np.concatenate(parts(back), 1)


def parts(x):
    hi = x.astype(BF16)
    return hi, (x - hi.astype(F32)).astype(BF16)


def dot(a, b):
    return jnp.dot(a, b, preferred_element_type=F32)


def dft(z, sign):
    n = len(z)
    if n == 1:
        return z
    even, odd = dft(z[0::2], sign), dft(z[1::2], sign)
    low, high = [], []
    for k in range(n // 2):
        (er, ei), (zr, zi) = even[k], odd[k]
        if k == 0:
            tr, ti = zr, zi
        elif 4 * k == n:
            tr, ti = (-zi, zr) if sign > 0 else (zi, -zr)
        else:
            c, s = math.cos(2 * math.pi * k / n), sign * math.sin(2 * math.pi * k / n)
            if 8 * k == n:
                tr, ti = (c * (zr - zi), c * (zi + zr)) if sign > 0 else (c * (zr + zi), c * (zi - zr))
            elif 8 * k == 3 * n:
                tr, ti = (c * (zr + zi), c * (zi - zr)) if sign > 0 else (c * (zr - zi), c * (zi + zr))
            else:
                tr, ti = c * zr - s * zi, c * zi + s * zr
        low.append((er + tr, ei + ti))
        high.append((er - tr, ei - ti))
    return low + high


def times(x, f, conj):
    (xr, xi), (fr, fi) = x, f
    if conj:
        return xr * fr + xi * fi, xi * fr - xr * fi
    return xr * fr - xi * fi, xr * fi + xi * fr


def column_copies(arrays, bufs, sems, half, width, into):
    blocks = arrays[0].shape[1] // (HALVES * width)
    copies = []
    for p in range(blocks):
        row = []
        for a, array in enumerate(arrays):
            cols = array.at[:, pl.ds((HALVES * p + half) * width, width)]
            ends = (cols, bufs.at[a, p]) if into else (bufs.at[a, p], cols)
            row.append(pltpu.make_async_copy(*ends, sems.at[a, p]))
        copies.append(row)
    return copies


def product_kernel(half, key, value, query, grad, out, bufs, sems):
    width = out.shape[-1]
    copies = column_copies((key, value, query, grad), bufs, sems, half, width, True)
    for row in copies:
        for copy in row:
            copy.start()
    for p, row in enumerate(copies):
        for copy in row:
            copy.wait()
        out[p, 0] = (bufs[0, p].astype(F32) * bufs[1, p].astype(F32)).astype(BF16)
        out[p, 1] = (bufs[3, p].astype(F32) * bufs[2, p].astype(F32)).astype(BF16)


def products(half, n, key, value, query, grad):
    rows, total = key.shape
    width = total // n // HALVES
    return pl.pallas_call(
        functools.partial(product_kernel, half),
        in_specs=[ANY] * 4,
        out_specs=VMEM,
        out_shape=jax.ShapeDtypeStruct((n, 2, rows, width), BF16),
        scratch_shapes=[
            pltpu.VMEM((4, n, rows, width), BF16),
            pltpu.SemaphoreType.DMA((4, n)),
        ],
        compiler_params=PARAMS,
        name="products",
    )(key, value, query, grad)


def split_rows(x, c, lanes):
    return x[pl.ds(c, x.shape[0] // CLASSES, stride=CLASSES), lanes]


def lane_groups(width):
    return [slice(i, i + 128) for i in range(0, width, 128)]


def filter_kernel(filt, fwd, spec, x, u):
    m2 = x.shape[1] // CLASSES
    width = filt.shape[0]
    for g in range(width // 128):
        x[g] = filt[g * 128 : (g + 1) * 128, :].T
    for c in range(CLASSES):
        for g in range(width // 128):
            hi, lo = parts(x[g, pl.ds(c, m2, stride=CLASSES), :])
            u[c, :, g * 128 : (g + 1) * 128] = dot(fwd[c], jnp.concatenate([hi, hi], 0)) + dot(
                fwd[c, :, :m2], lo
            )

    def step(i, carry):
        r = pl.multiple_of(i * ROWS, ROWS)
        for lanes in lane_groups(width):
            z = [(u[c, pl.ds(r, ROWS), lanes], u[c, pl.ds(m2 + r, ROWS), lanes]) for c in range(CLASSES)]
            for k, (re, im) in enumerate(dft(z, -1)):
                spec[k, pl.ds(r, ROWS), lanes] = re
                spec[k, pl.ds(m2 + r, ROWS), lanes] = im
        return carry

    lax.fori_loop(0, m2 // ROWS, step, 0)


def filter_spectrum(half, filters, fwd):
    chans, length = filters.shape
    width = chans // HALVES
    m2 = length // CLASSES
    return pl.pallas_call(
        filter_kernel,
        grid=(1,),
        in_specs=[
            pl.BlockSpec((width, length), lambda i: (half, 0)),
            pl.BlockSpec(fwd.shape, lambda i: (0, 0, 0)),
        ],
        out_specs=pl.BlockSpec((CLASSES, 2 * m2, width), lambda i: (0, 0, 0)),
        out_shape=jax.ShapeDtypeStruct((CLASSES, 2 * m2, width), F32),
        scratch_shapes=[
            pltpu.VMEM((width // 128, length, 128), F32),
            pltpu.VMEM((CLASSES, 2 * m2, width), F32),
        ],
        compiler_params=PARAMS,
        name="filter_spectrum",
    )(filters, fwd)


def conv_kernel(got, filt, fwd, back, out, grads, nat, x, u, hi, lo):
    n, _, rows, width = got.shape
    groups = width // 128
    length = n * rows
    m2 = length // CLASSES
    d, per, _ = grads.shape

    for a in range(2):
        for g in range(groups):
            lanes = slice(g * 128, (g + 1) * 128)
            for p in range(n):
                nat[g, p * rows : (p + 1) * rows] = got[p, a, :, lanes].astype(F32)
            for c in range(CLASSES):
                x[c, :, lanes] = nat[g, pl.ds(c, m2, stride=CLASSES), :].astype(BF16)
        for c in range(CLASSES):
            data = x[c]
            u[a, c] = dot(fwd[c], jnp.concatenate([data, data], 0))

    def step(i, carry):
        r = pl.multiple_of(i * ROWS, ROWS)
        re, im = pl.ds(r, ROWS), pl.ds(m2 + r, ROWS)
        for lanes in lane_groups(width):
            kv = dft([(u[0, c, re, lanes], u[0, c, im, lanes]) for c in range(CLASSES)], -1)
            wt = dft([(u[1, c, re, lanes], u[1, c, im, lanes]) for c in range(CLASSES)], -1)
            fs = [(filt[k, re, lanes], filt[k, im, lanes]) for k in range(CLASSES)]
            for o, (left, right, conj) in enumerate([(kv, fs, False), (wt, fs, True), (wt, kv, True)]):
                y = dft([times(s, t, conj) for s, t in zip(left, right)], 1)
                for c in range(CLASSES):
                    for q, rows_at in enumerate((re, im)):
                        h, l = parts(y[c][q])
                        hi[o, c, rows_at, lanes] = h
                        lo[o, c, rows_at, lanes] = l
        return carry

    lax.fori_loop(0, m2 // ROWS, step, 0)

    for o in range(3):
        for c in range(CLASSES):
            both = dot(back[c], hi[o, c])
            y = both[:m2] + both[m2:] + dot(back[c, :m2], lo[o, c])
            for g in range(groups):
                nat[g, pl.ds(c, m2, stride=CLASSES), :] = y[:, g * 128 : (g + 1) * 128]
        for g in range(groups):
            lanes = slice(g * 128, (g + 1) * 128)
            if o < 2:
                for p in range(n):
                    out[p, o, :, lanes] = nat[g, p * rows : (p + 1) * rows].astype(BF16)
            else:
                for s in range(d):
                    grads[s, :, lanes] = nat[g, s * per : (s + 1) * per].astype(BF16)


def conv(d, got, filt, fwd, back):
    n, _, rows, width = got.shape
    length = n * rows
    m2 = length // CLASSES
    return pl.pallas_call(
        conv_kernel,
        in_specs=[VMEM] * 4,
        out_specs=[VMEM] * 2,
        out_shape=[
            jax.ShapeDtypeStruct((n, 2, rows, width), BF16),
            jax.ShapeDtypeStruct((d, length // d, width), BF16),
        ],
        scratch_shapes=[
            pltpu.VMEM((width // 128, length, 128), F32),
            pltpu.VMEM((CLASSES, m2, width), BF16),
            pltpu.VMEM((2, CLASSES, 2 * m2, width), F32),
            pltpu.VMEM((3, CLASSES, 2 * m2, width), BF16),
            pltpu.VMEM((3, CLASSES, 2 * m2, width), BF16),
        ],
        compiler_params=PARAMS,
        name="conv",
    )(got, filt, fwd, back)


def gate_kernel(half, query, grad, value, key, gain, got, *refs):
    outs, (bufs, sent, sems, out_sems) = refs[-8:-4], refs[-4:]
    n, _, _, width = got.shape
    copies = column_copies((query, grad, value, key), bufs, sems, half, width, True)
    stores = column_copies(outs, sent, out_sems, half, width, False)
    for row in copies:
        for copy in row:
            copy.start()
    for p, row in enumerate(copies):
        for copy in row:
            copy.wait()
        at = (HALVES * p + half) * width
        scale = gain[:, at : at + width]
        q, g, v, k = (bufs[a, p].astype(F32) for a in range(4))
        mixing = got[p, 0].astype(F32) + scale * (k * v).astype(BF16).astype(F32)
        sent[0, p] = (q * mixing).astype(BF16)
        sent[1, p] = (g * mixing).astype(BF16)
        total = got[p, 1].astype(F32) + scale * (g * q).astype(BF16).astype(F32)
        sent[2, p] = (total * v).astype(BF16)
        sent[3, p] = (total * k).astype(BF16)
        for copy in stores[p]:
            copy.start()
    for row in stores:
        for copy in row:
            copy.wait()


def gate(half, query, grad, value, key, gain, got, outs):
    n, _, rows, width = got.shape
    shape = (4, n, rows, width)
    return pl.pallas_call(
        functools.partial(gate_kernel, half),
        in_specs=[ANY] * 4 + [VMEM, VMEM] + [ANY] * len(outs),
        out_specs=[ANY] * 4,
        out_shape=[jax.ShapeDtypeStruct(query.shape, BF16)] * 4,
        scratch_shapes=[
            pltpu.VMEM(shape, BF16),
            pltpu.VMEM(shape, BF16),
            pltpu.SemaphoreType.DMA(shape[:2]),
            pltpu.SemaphoreType.DMA(shape[:2]),
        ],
        input_output_aliases={6 + i: i for i in range(len(outs))},
        compiler_params=PARAMS,
        name="gate",
    )(query, grad, value, key, gain, got, *outs)


def turn_kernel(*refs):
    out = refs[-1]
    for half, part in enumerate(refs[:-1]):
        width = part.shape[1]
        out[half * width : (half + 1) * width] = part[...].astype(F32).T


def turn_grads(parts_):
    rows, width = parts_[0].shape
    return pl.pallas_call(
        turn_kernel,
        in_specs=[VMEM] * len(parts_),
        out_specs=VMEM,
        out_shape=jax.ShapeDtypeStruct((len(parts_) * width, rows), F32),
        compiler_params=PARAMS,
        name="turn_grads",
    )(*parts_)


def local(n, d, query_in, key_in, value_in, grad_out, filters, skip_gain):
    query, key, value, grad = query_in[0], key_in[0], value_in[0], grad_out[0]
    fwd, back = (jnp.asarray(t) for t in tables(filters.shape[1]))
    gain = skip_gain[None, :]

    def swap(x):
        return lax.all_to_all(x, "ctx", split_axis=0, concat_axis=0, tiled=True)

    got = [swap(products(h, n, key, value, query, grad)) for h in range(HALVES)]
    specs = [filter_spectrum(h, filters, fwd) for h in range(HALVES)]
    outs, grads = [], []
    for h in range(HALVES):
        mixed, part = conv(d, got[h], specs[h], fwd, back)
        back_rows = swap(mixed)
        part = lax.psum_scatter(part, "dp", scatter_dimension=0, tiled=False)
        outs = gate(h, query, grad, value, key, gain, back_rows, outs)
        grads.append(part)
    mixed_out, grad_query, grad_key, grad_value = outs
    return mixed_out[None], grad_query[None], grad_key[None], grad_value[None], turn_grads(grads)


def solution(mesh):
    rows = P("dp", "ctx", None)
    return jax.shard_map(
        functools.partial(local, mesh.shape["ctx"], mesh.shape["dp"]),
        mesh=mesh,
        in_specs=(rows, rows, rows, rows, P("ctx", None), P()),
        out_specs=(rows, rows, rows, rows, P("ctx", "dp")),
        check_vma=False,
    )
```

time: 390 us -> 104 us (0.27); the launches traced: 384 us -> 103 us
  matrix products: 119 us -> 0 us
  other arithmetic: 77.6 us -> 0 us
  local copies, waits for them, and re-layouts: 57.6 us -> 0.99 us
  blocking collectives: 54 us -> 0 us
  Pallas kernels: 0 us -> 44.1 us
  waiting for transfers between devices: 41.3 us -> 28.1 us
  starting transfers between devices: 20.4 us -> 15.9 us
    dot_general x12 -> x0, matrix products: 119 us -> none  [matmul(): return jnp.einsum(form, table, data, precision=lax.Precision.HIGHEST)]
    all_to_all x3 -> x0, blocking collectives: 54 us -> none  [the longest x1 18.5 us: local(): lax.all_to_all(gk_chan, 'ctx', split_axis=0, concat_axis=1, tiled=True)]
    pallas_call x0 -> x9, Pallas kernels: none -> 44.1 us  [the longest x2 18.7 us: conv(): pl.pallas_call(conv_kernel, in_specs=[VMEM] * 4, out_specs=[VMEM] * 2, ou...]
    add x3 -> x0, other arithmetic: 33 us -> none  [the longest x1 17.3 us: forward_spectrum(): section[0] * cos_twid + section[1] * sin_twid]
    dot_general x3 -> x0, local copies, waits for them, and re-layouts: 24.4 us -> none  [matmul(): return jnp.einsum(form, table, data, precision=lax.Precision.HIGHEST)]
    unnamed x42 -> x8, local copies, waits for them, and re-layouts: 21.7 us -> 0.99 us
    another operation x4 -> x0, other arithmetic: 18.2 us -> none  [the longest x3 17.4 us: forward_spectrum(): jnp.stack([section[0] * cos_twid + section[1] * sin_twid, section[1] * co...]
    sub x1 -> x0, other arithmetic: 17.5 us -> none  [inverse_signal(): inner[0] * cos_twid - inner[1] * sin_twid]
  transfers between devices with their start and end apart: 6 -> 6, of which waited for: 5 -> 5; matrix products, arithmetic and copies ran while one was open for 11% -> 0% of each run, Pallas kernels for 0% -> 38%
where the time goes in v2:
time: 104 us; the launch traced here: 103 us
  Pallas kernels  44.1 us (42%)
  waiting for transfers between devices  28.1 us (27%)
  starting transfers between devices  15.9 us (15%)
  between operations  14.1 us (14%)
    all_to_all x4, waiting for transfers between devices, swap(): return lax.all_to_all(x, 'ctx', split_axis=0, concat_axis=0, tiled=True)  26.2 us
    pallas_call x2, Pallas kernels, conv(): pl.pallas_call(conv_kernel, in_specs=[VMEM] * 4, out_specs=[VMEM] * 2, ou...  18.7 us
    all_to_all x4, starting transfers between devices, swap(): return lax.all_to_all(x, 'ctx', split_axis=0, concat_axis=0, tiled=True)  15.9 us
    pallas_call x2, Pallas kernels, filter_spectrum(): pl.pallas_call(filter_kernel, grid=(1,), in_specs=[pl.BlockSpec((width, l...  9.18 us
    pallas_call x2, Pallas kernels, gate(): pl.pallas_call(functools.partial(gate_kernel, half), in_specs=[ANY] * 4 +...  8.51 us
    pallas_call x2, Pallas kernels, products(): pl.pallas_call(functools.partial(product_kernel, half), in_specs=[ANY] *...  5.74 us
  transfers between devices with their start and end apart: 6, of which 5 were waited for; matrix products, arithmetic and copies ran while one was open for 0% of the time, Pallas kernels for 38%

profile of v2, /device:TPU:0, one launch (start us, length us, event | category | flops | bytes accessed | tf_op | source)
XLA Modules:
  0.0 103.2 jit_solution(4474269276051633441)
XLA Ops:
  7.2 2.9 %products.3 = bf16[8,2,128,256]{3,2,1,0:T(8,128)(2,1)} custom-call(bf16[128,4096]{1,0:T(8,128)(2,1)} %bitcast.23, bf16[128,4096]{1,0:T(8,128)(2,1)} %bitcast.19, bf16[128,4096]{1,0:T(8,128)(2,1)} %bitcast.11, bf16[128,4096]{1,0:T(8,128)(2,1)} %bitcast.15), custom_call_target="tpu_custom_call" | custom-call | tf_op jit(solution)/shard_map/products/pallas_call | solution.py:111
  10.0 5.2 %all-to-all-start.2 = ((bf16[8,2,128,256]{3,2,1,0:T(8,128)(2,1)}), bf16[8,2,128,256]{3,2,1,0:T(8,128)(2,1)S(1)}, u32[]{:S(2)}, u32[]{:S(2)}) async-start(bf16[8,2,128,256]{3,2,1,0:T(8,128)(2,1)} %products.3), calls=%async_computation.2 | async-start | bytes 2097152 | tf_op jit(solution)/shard_map/all_to_all | solution.py:327
  15.2 2.9 %products.2 = bf16[8,2,128,256]{3,2,1,0:T(8,128)(2,1)} custom-call(bf16[128,4096]{1,0:T(8,128)(2,1)} %bitcast.24, bf16[128,4096]{1,0:T(8,128)(2,1)} %bitcast.20, bf16[128,4096]{1,0:T(8,128)(2,1)} %bitcast.12, bf16[128,4096]{1,0:T(8,128)(2,1)} %bitcast.16), custom_call_target="tpu_custom_call" | custom-call | tf_op jit(solution)/shard_map/products/pallas_call | solution.py:111
  18.1 12.5 %all-to-all-done.2.got = bf16[8,2,128,256]{3,2,1,0:T(8,128)(2,1)S(1)} async-done(((bf16[8,2,128,256]{3,2,1,0:T(8,128)(2,1)}), bf16[8,2,128,256]{3,2,1,0:T(8,128)(2,1)S(1)}, u32[]{:S(2)}, u32[]{:S(2)}) %all-to-all-start.2) | async-done | bytes 1048608 | tf_op jit(solution)/shard_map/all_to_all | solution.py:327
  30.6 0.0 copy-start.2
  30.6 3.6 %all-to-all-start = ((bf16[8,2,128,256]{3,2,1,0:T(8,128)(2,1)}), bf16[8,2,128,256]{3,2,1,0:T(8,128)(2,1)S(1)}, u32[]{:S(2)}, u32[]{:S(2)}) async-start(bf16[8,2,128,256]{3,2,1,0:T(8,128)(2,1)} %products.2), calls=%async_computation | async-start | bytes 2097152 | tf_op jit(solution)/shard_map/all_to_all | solution.py:327
  34.2 0.0 reduce-scatter.3.cloned.1.call-start
  34.3 4.6 %filter_spectrum.3.filt = f32[8,256,256]{2,1,0:T(8,128)} custom-call(f32[512,1024]{1,0:T(8,128)} %filt.3, bf16[8,256,256]{2,1,0:T(8,128)(2,1)} %constant.4.clone.fwd), custom_call_target="tpu_custom_call" | custom-call | tf_op jit(solution)/shard_map/filter_spectrum/pallas_call | solution.py:161
  38.8 0.0 copy-done.2
  38.8 9.4 %conv.3 = (bf16[8,2,128,256]{3,2,1,0:T(8,128)(2,1)}, bf16[4,256,256]{2,1,0:T(8,128)(2,1)}) custom-call(bf16[8,2,128,256]{3,2,1,0:T(8,128)(2,1)} %copy-done.2, f32[8,256,256]{2,1,0:T(8,128)} %filter_spectrum.3.filt, bf16[8,256,256]{2,1,0:T(8,128)(2,1)} %constant.4.clone.fwd, bf16[8,256,256]{2,1,0:T(8,128)(2,1)} %constant.5.clone.back), custom_call_target="tpu_custom_call" | custom-call | tf_op jit(solution)/shard_map/conv/pallas_call | solution.py:235
  48.2 0.0 reduce-scatter.3.cloned.1.call-update
  48.2 1.3 %all-to-all-done.got = bf16[8,2,128,256]{3,2,1,0:T(8,128)(2,1)S(1)} async-done(((bf16[8,2,128,256]{3,2,1,0:T(8,128)(2,1)}), bf16[8,2,128,256]{3,2,1,0:T(8,128)(2,1)S(1)}, u32[]{:S(2)}, u32[]{:S(2)}) %all-to-all-start) | async-done | bytes 1048608 | tf_op jit(solution)/shard_map/all_to_all | solution.py:327
  49.5 0.0 copy-start
  49.5 3.6 %all-to-all-start.3 = ((bf16[8,2,128,256]{3,2,1,0:T(8,128)(2,1)}), bf16[8,2,128,256]{3,2,1,0:T(8,128)(2,1)S(1)}, u32[]{:S(2)}, u32[]{:S(2)}) async-start(bf16[8,2,128,256]{3,2,1,0:T(8,128)(2,1)} %get-tuple-element.18), calls=%async_computation.3 | async-start | bytes 2097152 | tf_op jit(solution)/shard_map/all_to_all | solution.py:327
  53.1 0.0 reduce-scatter.5.cloned.1.call-start
  53.2 4.6 %filter_spectrum.2.filt = f32[8,256,256]{2,1,0:T(8,128)} custom-call(f32[512,1024]{1,0:T(8,128)} %filt.3, bf16[8,256,256]{2,1,0:T(8,128)(2,1)} %constant.4.clone.fwd), custom_call_target="tpu_custom_call" | custom-call | tf_op jit(solution)/shard_map/filter_spectrum/pallas_call | solution.py:161
  57.8 0.0 copy-done
  57.8 9.4 %conv.2 = (bf16[8,2,128,256]{3,2,1,0:T(8,128)(2,1)}, bf16[4,256,256]{2,1,0:T(8,128)(2,1)}) custom-call(bf16[8,2,128,256]{3,2,1,0:T(8,128)(2,1)} %copy-done, f32[8,256,256]{2,1,0:T(8,128)} %filter_spectrum.2.filt, bf16[8,256,256]{2,1,0:T(8,128)(2,1)} %constant.4.clone.fwd, bf16[8,256,256]{2,1,0:T(8,128)(2,1)} %constant.5.clone.back), custom_call_target="tpu_custom_call" | custom-call | tf_op jit(solution)/shard_map/conv/pallas_call | solution.py:235
  67.1 0.0 reduce-scatter.5.cloned.1.call-update
  67.1 1.3 %all-to-all-done.3.got = bf16[8,2,128,256]{3,2,1,0:T(8,128)(2,1)S(1)} async-done(((bf16[8,2,128,256]{3,2,1,0:T(8,128)(2,1)}), bf16[8,2,128,256]{3,2,1,0:T(8,128)(2,1)S(1)}, u32[]{:S(2)}, u32[]{:S(2)}) %all-to-all-start.3) | async-done | bytes 1048608 | tf_op jit(solution)/shard_map/all_to_all | solution.py:327
  68.5 0.0 copy-start.1
  68.5 3.6 %all-to-all-start.1 = ((bf16[8,2,128,256]{3,2,1,0:T(8,128)(2,1)}), bf16[8,2,128,256]{3,2,1,0:T(8,128)(2,1)S(1)}, u32[]{:S(2)}, u32[]{:S(2)}) async-start(bf16[8,2,128,256]{3,2,1,0:T(8,128)(2,1)} %get-tuple-element.17), calls=%async_computation.1 | async-start | bytes 2097152 | tf_op jit(solution)/shard_map/all_to_all | solution.py:327
  72.0 0.0 copy-done.1
  72.0 4.3 %gate.2 = (bf16[128,4096]{1,0:T(8,128)(2,1)}, bf16[128,4096]{1,0:T(8,128)(2,1)}, bf16[128,4096]{1,0:T(8,128)(2,1)}, bf16[128,4096]{1,0:T(8,128)(2,1)}) custom-call(bf16[128,4096]{1,0:T(8,128)(2,1)} %bitcast.13, bf16[128,4096]{1,0:T(8,128)(2,1)} %bitcast.17, bf16[128,4096]{1,0:T(8,128)(2,1)} %bitcast.21, bf16[128,4096]{1,0:T(8,128)(2,1)} %bitcast.25, ...), custom_call_target="tpu_custom_call" | custom-call | tf_op jit(solution)/shard_map/gate/pallas_call | solution.py:285
  76.3 11.1 %all-to-all-done.1.got = bf16[8,2,128,256]{3,2,1,0:T(8,128)(2,1)S(1)} async-done(((bf16[8,2,128,256]{3,2,1,0:T(8,128)(2,1)}), bf16[8,2,128,256]{3,2,1,0:T(8,128)(2,1)S(1)}, u32[]{:S(2)}, u32[]{:S(2)}) %all-to-all-start.1) | async-done | bytes 1048608 | tf_op jit(solution)/shard_map/all_to_all | solution.py:327
  87.4 0.0 copy-start.3
  87.4 1.0 copy-done.3
  88.3 4.3 %gate.3 = (bf16[128,4096]{1,0:T(8,128)(2,1)}, bf16[128,4096]{1,0:T(8,128)(2,1)}, bf16[128,4096]{1,0:T(8,128)(2,1)}, bf16[128,4096]{1,0:T(8,128)(2,1)}) custom-call(bf16[128,4096]{1,0:T(8,128)(2,1)} %bitcast.14, bf16[128,4096]{1,0:T(8,128)(2,1)} %bitcast.18, ...), custom_call_target="tpu_custom_call", output_to_operand_aliasing={{0}: (6, {}), {1}: (7, {}), {2}: (8, {}), {3}: (9, {})} | custom-call | tf_op jit(solution)/shard_map/gate/pallas_call | solution.py:285
  92.6 0.0 reduce-scatter.3.cloned.1.call-done
  92.6 1.8 %reduce-scatter.5.cloned.1.call-done = bf16[1,256,256]{2,1,0:T(8,128)(2,1)} async-done(((bf16[4,256,256]{2,1,0:T(8,128)(2,1)}), bf16[1,256,256]{2,1,0:T(8,128)(2,1)}) %reduce-scatter.5.cloned.1.call-update) | async-done | bytes 131088 | tf_op jit(solution)/shard_map/reduce_scatter | solution.py:335
  94.5 1.9 %turn_grads.1 = f32[512,256]{1,0:T(8,128)} custom-call(bf16[256,256]{1,0:T(8,128)(2,1)} %bitcast.31, bf16[256,256]{1,0:T(8,128)(2,1)} %bitcast.32), custom_call_target="tpu_custom_call" | custom-call | tf_op jit(solution)/shard_map/turn_grads/pallas_call | solution.py:311
Async XLA Ops:
  10.0 20.6 %all-to-all-start.2 = ((bf16[8,2,128,256]{3,2,1,0:T(8,128)(2,1)}), bf16[8,2,128,256]{3,2,1,0:T(8,128)(2,1)S(1)}, u32[]{:S(2)}, u32[]{:S(2)}) async-start(bf16[8,2,128,256]{3,2,1,0:T(8,128)(2,1)} %products.3), calls=%async_computation.2 | async-start | bytes 2097152 | tf_op jit(solution)/shard_map/all_to_all | solution.py:327
  30.6 8.2 %copy-start.2 = (bf16[8,2,128,256]{3,2,1,0:T(8,128)(2,1)}, bf16[8,2,128,256]{3,2,1,0:T(8,128)(2,1)S(1)}, u32[]{:S(2)}) copy-start(bf16[8,2,128,256]{3,2,1,0:T(8,128)(2,1)S(1)} %all-to-all-done.2.got) | copy-start | bytes 3145732
  30.6 18.9 %all-to-all-start = ((bf16[8,2,128,256]{3,2,1,0:T(8,128)(2,1)}), bf16[8,2,128,256]{3,2,1,0:T(8,128)(2,1)S(1)}, u32[]{:S(2)}, u32[]{:S(2)}) async-start(bf16[8,2,128,256]{3,2,1,0:T(8,128)(2,1)} %products.2), calls=%async_computation | async-start | bytes 2097152 | tf_op jit(solution)/shard_map/all_to_all | solution.py:327
  34.2 58.4 %reduce-scatter.3.cloned.1.call-start = ((), (), s32[]{:S(2)}) async-start(), calls=%async_computation.6 | async-start | bytes 655360 | tf_op jit(solution)/shard_map/reduce_scatter | solution.py:335
  49.5 8.2 %copy-start = (bf16[8,2,128,256]{3,2,1,0:T(8,128)(2,1)}, bf16[8,2,128,256]{3,2,1,0:T(8,128)(2,1)S(1)}, u32[]{:S(2)}) copy-start(bf16[8,2,128,256]{3,2,1,0:T(8,128)(2,1)S(1)} %all-to-all-done.got) | copy-start | bytes 3145732
  49.5 18.9 %all-to-all-start.3 = ((bf16[8,2,128,256]{3,2,1,0:T(8,128)(2,1)}), bf16[8,2,128,256]{3,2,1,0:T(8,128)(2,1)S(1)}, u32[]{:S(2)}, u32[]{:S(2)}) async-start(bf16[8,2,128,256]{3,2,1,0:T(8,128)(2,1)} %get-tuple-element.18), calls=%async_computation.3 | async-start | bytes 2097152 | tf_op jit(solution)/shard_map/all_to_all | solution.py:327
  53.1 41.3 %reduce-scatter.5.cloned.1.call-start = ((), (), s32[]{:S(2)}) async-start(), calls=%async_computation.7 | async-start | bytes 655360 | tf_op jit(solution)/shard_map/reduce_scatter | solution.py:335
  68.5 3.6 %copy-start.1 = (bf16[8,2,128,256]{3,2,1,0:T(8,128)(2,1)}, bf16[8,2,128,256]{3,2,1,0:T(8,128)(2,1)S(1)}, u32[]{:S(2)}) copy-start(bf16[8,2,128,256]{3,2,1,0:T(8,128)(2,1)S(1)} %all-to-all-done.3.got) | copy-start | bytes 3145732
  68.5 18.9 %all-to-all-start.1 = ((bf16[8,2,128,256]{3,2,1,0:T(8,128)(2,1)}), bf16[8,2,128,256]{3,2,1,0:T(8,128)(2,1)S(1)}, u32[]{:S(2)}, u32[]{:S(2)}) async-start(bf16[8,2,128,256]{3,2,1,0:T(8,128)(2,1)} %get-tuple-element.17), calls=%async_computation.1 | async-start | bytes 2097152 | tf_op jit(solution)/shard_map/all_to_all | solution.py:327
  87.4 1.0 copy-start.3
Sparse Core Ops, SparseCore 0:
  48.4 23.2 reduce-scatter.2
  74.5 19.9 reduce-scatter.4

commit v3 on v2

v3 whole, which is shorter than its diff:
```python
import functools
import math

import jax
import jax.numpy as jnp
import ml_dtypes
import numpy as np
from jax import lax
from jax.experimental import pallas as pl
from jax.experimental.pallas import tpu as pltpu
from jax.sharding import PartitionSpec as P

F32 = jnp.float32
BF16 = jnp.bfloat16
VMEM_LIMIT = 20 * 1024 * 1024
CLASSES = 8
ROWS = 16
HALVES = 2
PAIRED = (False, True)
PARAMS = pltpu.CompilerParams(vmem_limit_bytes=VMEM_LIMIT)
SMEM = pl.BlockSpec(memory_space=pltpu.SMEM)
VMEM = pl.BlockSpec(memory_space=pltpu.VMEM)
ANY = pl.BlockSpec(memory_space=pl.ANY)


def tables(length):
    m2 = length // CLASSES
    c = np.arange(CLASSES)[:, None, None]
    j = np.arange(m2)[None, :, None]
    m = np.arange(m2)[None, None, :]
    turn = ((CLASSES * m + c) * (2 * j + 1)) % (4 * length)
    angle = 2 * np.pi * turn / (4 * length)
    forward = np.concatenate([np.cos(angle), -np.sin(angle)], 1)
    back = np.swapaxes(forward, 1, 2) / length

    def parts(x):
        hi = x.astype(ml_dtypes.bfloat16)
        return hi, (x - hi.astype(np.float64)).astype(ml_dtypes.bfloat16)

    return np.concatenate(parts(forward), 2), np.concatenate(parts(back), 1)


def parts(x):
    hi = x.astype(BF16)
    return hi, (x - hi.astype(F32)).astype(BF16)


def dot(a, b):
    return jnp.dot(a, b, preferred_element_type=F32)


def dft(z, sign):
    n = len(z)
    if n == 1:
        return z
    even, odd = dft(z[0::2], sign), dft(z[1::2], sign)
    low, high = [], []
    for k in range(n // 2):
        (er, ei), (zr, zi) = even[k], odd[k]
        if k == 0:
            tr, ti = zr, zi
        elif 4 * k == n:
            tr, ti = (-zi, zr) if sign > 0 else (zi, -zr)
        else:
            c, s = math.cos(2 * math.pi * k / n), sign * math.sin(2 * math.pi * k / n)
            if 8 * k == n:
                tr, ti = (c * (zr - zi), c * (zi + zr)) if sign > 0 else (c * (zr + zi), c * (zi - zr))
            elif 8 * k == 3 * n:
                tr, ti = (c * (zr + zi), c * (zi - zr)) if sign > 0 else (c * (zr - zi), c * (zi + zr))
            else:
                tr, ti = c * zr - s * zi, c * zi + s * zr
        low.append((er + tr, ei + ti))
        high.append((er - tr, ei - ti))
    return low + high


def times(x, f, conj):
    (xr, xi), (fr, fi) = x, f
    if conj:
        return xr * fr + xi * fi, xi * fr - xr * fi
    return xr * fr - xi * fi, xr * fi + xi * fr


def resident(x):
    return pltpu.with_memory_space_constraint(x, pltpu.VMEM)


def device(me, j):
    return j if me is None else me[0] ^ j


def columns(me, half, j, width):
    return pl.ds(pl.multiple_of((HALVES * device(me, j) + half) * width, 128), width)


def product_kernel(half, n, me, key, value, query, grad, *outs):
    if len(outs) == 1:
        me, outs = None, [outs[0].at[p] for p in range(n)]
    width = outs[0].shape[-1]
    for j, out in enumerate(outs):
        cols = columns(me, half, j, width)
        out[0] = (key[:, cols].astype(F32) * value[:, cols].astype(F32)).astype(BF16)
        out[1] = (grad[:, cols].astype(F32) * query[:, cols].astype(F32)).astype(BF16)


def products(half, n, paired, me, key, value, query, grad):
    rows, total = key.shape
    width = total // n // HALVES
    if paired:
        shapes = [pltpu.VMEM((2, rows, width), BF16)] * n
    else:
        shapes = [pltpu.VMEM((n, 2, rows, width), BF16)]
    out = pl.pallas_call(
        functools.partial(product_kernel, half, n),
        in_specs=[SMEM] + [VMEM] * 4,
        out_specs=[VMEM] * len(shapes),
        out_shape=shapes,
        compiler_params=PARAMS,
        name="products",
    )(me, key, value, query, grad)
    return out


def lane_groups(width):
    return [slice(i, i + 128) for i in range(0, width, 128)]


def filter_kernel(half, filt, fwd, spec, x, u):
    m2 = x.shape[1] // CLASSES
    width = spec.shape[-1]
    for g in range(width // 128):
        x[g] = filt[half * width + g * 128 : half * width + (g + 1) * 128, :].T
    for c in range(CLASSES):
        for g in range(width // 128):
            hi, lo = parts(x[g, pl.ds(c, m2, stride=CLASSES), :])
            u[c, :, g * 128 : (g + 1) * 128] = dot(fwd[c], jnp.concatenate([hi, hi], 0)) + dot(
                fwd[c, :, :m2], lo
            )

    def step(i, carry):
        r = pl.multiple_of(i * ROWS, ROWS)
        for lanes in lane_groups(width):
            z = [(u[c, pl.ds(r, ROWS), lanes], u[c, pl.ds(m2 + r, ROWS), lanes]) for c in range(CLASSES)]
            for k, (re, im) in enumerate(dft(z, -1)):
                spec[k, pl.ds(r, ROWS), lanes] = re
                spec[k, pl.ds(m2 + r, ROWS), lanes] = im
        return carry

    lax.fori_loop(0, m2 // ROWS, step, 0)


def filter_spectrum(half, filters, fwd):
    chans, length = filters.shape
    width = chans // HALVES
    m2 = length // CLASSES
    return pl.pallas_call(
        functools.partial(filter_kernel, half),
        in_specs=[VMEM, VMEM],
        out_specs=VMEM,
        out_shape=pltpu.VMEM((CLASSES, 2 * m2, width), F32),
        scratch_shapes=[
            pltpu.VMEM((width // 128, length, 128), F32),
            pltpu.VMEM((CLASSES, 2 * m2, width), F32),
        ],
        compiler_params=PARAMS,
        name="filter_spectrum",
    )(filters, fwd)


def conv_kernel(n, d, paired, me, *refs):
    count = n if paired else 1
    got, (filt, fwd, back), refs = refs[:count], refs[count : count + 3], refs[count + 3 :]
    out, grads, (nat, x, u, hi, lo) = refs[:count], refs[count : count + d], refs[count + d :]
    mine = me if paired else None
    if not paired:
        got, out = ([r[0].at[p] for p in range(n)] for r in (got, out))
    _, rows, width = got[0].shape
    groups = width // 128
    m2 = n * rows // CLASSES
    per = grads[0].shape[0]

    for a in range(2):
        for g in range(groups):
            lanes = slice(g * 128, (g + 1) * 128)
            for j in range(n):
                at = pl.multiple_of(device(mine, j) * rows, rows)
                nat[g, pl.ds(at, rows)] = got[j][a, :, lanes].astype(F32)
            for c in range(CLASSES):
                x[c, :, lanes] = nat[g, pl.ds(c, m2, stride=CLASSES), :].astype(BF16)
        for c in range(CLASSES):
            data = x[c]
            u[a, c] = dot(fwd[c], jnp.concatenate([data, data], 0))

    def step(i, carry):
        r = pl.multiple_of(i * ROWS, ROWS)
        re, im = pl.ds(r, ROWS), pl.ds(m2 + r, ROWS)
        for lanes in lane_groups(width):
            kv = dft([(u[0, c, re, lanes], u[0, c, im, lanes]) for c in range(CLASSES)], -1)
            wt = dft([(u[1, c, re, lanes], u[1, c, im, lanes]) for c in range(CLASSES)], -1)
            fs = [(filt[k, re, lanes], filt[k, im, lanes]) for k in range(CLASSES)]
            for o, (left, right, conj) in enumerate([(kv, fs, False), (wt, fs, True), (wt, kv, True)]):
                y = dft([times(s, t, conj) for s, t in zip(left, right)], 1)
                for c in range(CLASSES):
                    for q, rows_at in enumerate((re, im)):
                        h, l = parts(y[c][q])
                        hi[o, c, rows_at, lanes] = h
                        lo[o, c, rows_at, lanes] = l
        return carry

    lax.fori_loop(0, m2 // ROWS, step, 0)

    for o in range(3):
        for c in range(CLASSES):
            both = dot(back[c], hi[o, c])
            y = both[:m2] + both[m2:] + dot(back[c, :m2], lo[o, c])
            for g in range(groups):
                nat[g, pl.ds(c, m2, stride=CLASSES), :] = y[:, g * 128 : (g + 1) * 128]
        for g in range(groups):
            lanes = slice(g * 128, (g + 1) * 128)
            if o < 2:
                for j in range(n):
                    at = pl.multiple_of(device(mine, j) * rows, rows)
                    out[j][o, :, lanes] = nat[g, pl.ds(at, rows)].astype(BF16)
            else:
                for j in range(d):
                    at = pl.multiple_of((me[1] ^ j) * per, per)
                    grads[j][:, lanes] = nat[g, pl.ds(at, per)].astype(grads[j].dtype)


def conv(n, d, paired, me, got, filt, fwd, back):
    rows, width = got[0].shape[-2:]
    length = n * rows
    m2 = length // CLASSES
    shapes = [pltpu.VMEM(got[0].shape, BF16)] * len(got)
    shapes += [pltpu.VMEM((length // d, width), F32 if j == 0 else BF16) for j in range(d)]
    out = pl.pallas_call(
        functools.partial(conv_kernel, n, d, paired),
        in_specs=[SMEM] + [VMEM] * (len(got) + 3),
        out_specs=[VMEM] * len(shapes),
        out_shape=shapes,
        scratch_shapes=[
            pltpu.VMEM((width // 128, length, 128), F32),
            pltpu.VMEM((CLASSES, m2, width), BF16),
            pltpu.VMEM((2, CLASSES, 2 * m2, width), F32),
            pltpu.VMEM((3, CLASSES, 2 * m2, width), BF16),
            pltpu.VMEM((3, CLASSES, 2 * m2, width), BF16),
        ],
        compiler_params=PARAMS,
        name="conv",
    )(me, *got, filt, fwd, back)
    return out[: len(got)], out[len(got) :]


def gate_kernel(half, n, paired, me, query, grad, value, key, gain, *refs):
    count = n if paired else 1
    got, (outs, sent, sems) = refs[:count], (refs[-6:-2], *refs[-2:])
    mine = me if paired else None
    if not paired:
        got = [got[0].at[p] for p in range(n)]
    width = got[0].shape[-1]
    copies = []
    for j in range(n):
        cols = columns(mine, half, j, width)
        scale = gain[:, cols]
        q, g, v, k = (x[:, cols].astype(F32) for x in (query, grad, value, key))
        mixing = got[j][0].astype(F32) + scale * (k * v).astype(BF16).astype(F32)
        sent[0, j] = (q * mixing).astype(BF16)
        sent[1, j] = (g * mixing).astype(BF16)
        total = got[j][1].astype(F32) + scale * (g * q).astype(BF16).astype(F32)
        sent[2, j] = (total * v).astype(BF16)
        sent[3, j] = (total * k).astype(BF16)
        for a in range(4):
            copy = pltpu.make_async_copy(sent.at[a, j], outs[a].at[:, cols], sems.at[a, j])
            copy.start()
            copies.append(copy)
    for copy in copies:
        copy.wait()


def gate(half, n, paired, me, query, grad, value, key, gain, got, outs):
    rows, width = got[0].shape[-2:]
    first = 6 + len(got)
    return pl.pallas_call(
        functools.partial(gate_kernel, half, n, paired),
        in_specs=[SMEM] + [VMEM] * (5 + len(got)) + [ANY] * len(outs),
        out_specs=[ANY] * 4,
        out_shape=[jax.ShapeDtypeStruct(query.shape, BF16)] * 4,
        scratch_shapes=[
            pltpu.VMEM((4, n, rows, width), BF16),
            pltpu.SemaphoreType.DMA((4, n)),
        ],
        input_output_aliases={first + i: i for i in range(len(outs))},
        compiler_params=PARAMS,
        name="gate",
    )(me, query, grad, value, key, gain, *got, *outs)


def turn_kernel(halves, out):
    for half, refs in enumerate(halves):
        total = refs[0][...]
        for ref in refs[1:]:
            total = total + ref[...].astype(F32)
        width = total.shape[1]
        out[half * width : (half + 1) * width] = total.T


def turn_grads(halves):
    rows, width = halves[0][0].shape
    return pl.pallas_call(
        turn_kernel,
        in_specs=[[[VMEM] * len(h) for h in halves]],
        out_specs=VMEM,
        out_shape=jax.ShapeDtypeStruct((len(halves) * width, rows), F32),
        compiler_params=PARAMS,
        name="turn_grads",
    )(halves)


def exchange(blocks, axis):
    n = len(blocks)
    return [blocks[0]] + [
        resident(lax.ppermute(blocks[j], axis, [(i, i ^ j) for i in range(n)])) for j in range(1, n)
    ]


def swap(blocks, paired):
    if paired:
        return exchange(blocks, "ctx")
    (block,) = blocks
    return [resident(lax.all_to_all(block, "ctx", split_axis=0, concat_axis=0, tiled=True))]


def local(n, d, query_in, key_in, value_in, grad_out, filters, skip_gain):
    query, key, value, grad = (resident(x[0]) for x in (query_in, key_in, value_in, grad_out))
    fwd, back = (resident(jnp.asarray(t)) for t in tables(filters.shape[1]))
    filters = resident(filters)
    gain = skip_gain[None, :]
    me = jnp.stack([lax.axis_index("ctx"), lax.axis_index("dp")]).astype(jnp.int32)

    got = [swap(products(h, n, PAIRED[h], me, key, value, query, grad), PAIRED[h]) for h in range(HALVES)]
    specs = [filter_spectrum(h, filters, fwd) for h in range(HALVES)]
    outs, grads = [], []
    for h in range(HALVES):
        mixed, part = conv(n, d, PAIRED[h], me, got[h], specs[h], fwd, back)
        got[h] = swap(mixed, PAIRED[h])
        grads.append(exchange(part, "dp"))
    for h in range(HALVES):
        outs = gate(h, n, PAIRED[h], me, query, grad, value, key, gain, got[h], outs)
    mixed_out, grad_query, grad_key, grad_value = outs
    return mixed_out[None], grad_query[None], grad_key[None], grad_value[None], turn_grads(grads)


def solution(mesh):
    rows = P("dp", "ctx", None)
    return jax.shard_map(
        functools.partial(local, mesh.shape["ctx"], mesh.shape["dp"]),
        mesh=mesh,
        in_specs=(rows, rows, rows, rows, P("ctx", None), P()),
        out_specs=(rows, rows, rows, rows, P("ctx", "dp")),
        check_vma=False,
    )
```

time: 104 us -> 119 us (1.14)
  Pallas kernels: 44.1 us -> 26.9 us
  local copies, waits for them, and re-layouts: 0.99 us -> 17.4 us
  starting transfers between devices: 15.9 us -> 31.4 us
  between operations: 14.1 us -> 1.05 us
  waiting for transfers between devices: 28.1 us -> 41.1 us
    ppermute x0 -> x20, waiting for transfers between devices: none -> 28.7 us  [exchange(): lax.ppermute(blocks[j], axis, [(i, i ^ j) for i in range(n)])]
    ppermute x0 -> x20, starting transfers between devices: none -> 21.6 us  [exchange(): lax.ppermute(blocks[j], axis, [(i, i ^ j) for i in range(n)])]
    pallas_call x9, Pallas kernels: 44.1 us -> 26.9 us  [the longest x2 14.8 us: conv(): pl.pallas_call(functools.partial(conv_kernel, n, d, paired), in_specs=[SM...]
    unnamed x8 -> x66, local copies, waits for them, and re-layouts: 0.99 us -> 17.4 us
    all_to_all x4 -> x2, waiting for transfers between devices: 26.2 us -> 12.4 us  [swap(): lax.all_to_all(block, 'ctx', split_axis=0, concat_axis=0, tiled=True)]
    all_to_all x4 -> x2, starting transfers between devices: 15.9 us -> 9.87 us  [swap(): lax.all_to_all(block, 'ctx', split_axis=0, concat_axis=0, tiled=True)]
    reduce_scatter x2 -> x0, waiting for transfers between devices: 1.85 us -> none  [local(): part = lax.psum_scatter(part, 'dp', scatter_dimension=0, tiled=False)]
  transfers between devices with their start and end apart: 6 -> 22, of which waited for: 5 -> 7; matrix products, arithmetic and copies ran while one was open for 0% -> 0% of each run, Pallas kernels for 38% -> 13%
where the time goes in v3:
time: 119 us; the launch traced here: 118 us
  waiting for transfers between devices  41.1 us (35%)
  starting transfers between devices  31.4 us (26%)
  Pallas kernels  26.9 us (23%)
  local copies, waits for them, and re-layouts  17.4 us (15%)
    ppermute x20, waiting for transfers between devices, exchange(): lax.ppermute(blocks[j], axis, [(i, i ^ j) for i in range(n)])  28.7 us
    ppermute x20, starting transfers between devices, exchange(): lax.ppermute(blocks[j], axis, [(i, i ^ j) for i in range(n)])  21.6 us
    unnamed x66, local copies, waits for them, and re-layouts  17.4 us
    pallas_call x2, Pallas kernels, conv(): pl.pallas_call(functools.partial(conv_kernel, n, d, paired), in_specs=[SM...  14.8 us
    all_to_all x2, waiting for transfers between devices, swap(): lax.all_to_all(block, 'ctx', split_axis=0, concat_axis=0, tiled=True)  12.4 us
    all_to_all x2, starting transfers between devices, swap(): lax.all_to_all(block, 'ctx', split_axis=0, concat_axis=0, tiled=True)  9.87 us
    pallas_call x2, Pallas kernels, gate(): pl.pallas_call(functools.partial(gate_kernel, half, n, paired), in_specs=...  6.09 us
    pallas_call x2, Pallas kernels, filter_spectrum(): pl.pallas_call(functools.partial(filter_kernel, half), in_specs=[VMEM, VM...  3.42 us
  transfers between devices with their start and end apart: 22, of which 7 were waited for; matrix products, arithmetic and copies ran while one was open for 0% of the time, Pallas kernels for 13%

profile of v3, /device:TPU:0, one launch (start us, length us, event | category | flops | bytes accessed | tf_op | source)
XLA Modules:
  0.0 118.0 jit_solution(8511071077321828490)
XLA Ops:
  0.7 1.2 %copy-done = bf16[1,128,4096]{2,1,0:T(8,128)(2,1)S(1)} copy-done((bf16[1,128,4096]{2,1,0:T(8,128)(2,1)S(1)}, bf16[1,128,4096]{2,1,0:T(8,128)(2,1)}, u32[]{:S(2)}) %copy-start) | copy-done | bytes 1048600
  1.9 1.2 %copy-done.2 = bf16[1,128,4096]{2,1,0:T(8,128)(2,1)S(1)} copy-done((bf16[1,128,4096]{2,1,0:T(8,128)(2,1)S(1)}, bf16[1,128,4096]{2,1,0:T(8,128)(2,1)}, u32[]{:S(2)}) %copy-start.2) | copy-done | bytes 1048600
  3.2 1.2 %copy-done.4 = bf16[1,128,4096]{2,1,0:T(8,128)(2,1)S(1)} copy-done((bf16[1,128,4096]{2,1,0:T(8,128)(2,1)S(1)}, bf16[1,128,4096]{2,1,0:T(8,128)(2,1)}, u32[]{:S(2)}) %copy-start.4) | copy-done | bytes 1048600
  4.4 1.2 %copy-done.6 = bf16[1,128,4096]{2,1,0:T(8,128)(2,1)S(1)} copy-done((bf16[1,128,4096]{2,1,0:T(8,128)(2,1)S(1)}, bf16[1,128,4096]{2,1,0:T(8,128)(2,1)}, u32[]{:S(2)}) %copy-start.6) | copy-done | bytes 1048600
  7.4 5.3 %all-to-all-start = ((bf16[8,2,128,256]{3,2,1,0:T(8,128)(2,1)}), bf16[8,2,128,256]{3,2,1,0:T(8,128)(2,1)}, u32[]{:S(2)}, u32[]{:S(2)}) async-start(bf16[8,2,128,256]{3,2,1,0:T(8,128)(2,1)} %copy-done.15), calls=%async_computation | async-start | bytes 2097152 | tf_op jit(solution)/shard_map/all_to_all | solution.py:330
  12.7 1.7 %filter_spectrum.3.refs_1_ = f32[8,256,256]{2,1,0:T(8,128)S(1)} custom-call(f32[512,1024]{1,0:T(8,128)S(1)} %copy-done.11, bf16[8,256,256]{2,1,0:T(8,128)(2,1)S(1)} %copy-done.9), custom_call_target="tpu_custom_call" | custom-call | tf_op jit(solution)/shard_map/filter_spectrum/pallas_call | solution.py:156
  14.4 1.4 %copy-done.13 = f32[8,256,256]{2,1,0:T(8,128)} copy-done((f32[8,256,256]{2,1,0:T(8,128)}, f32[8,256,256]{2,1,0:T(8,128)S(1)}, u32[]{:S(2)}) %copy-start.13) | copy-done | bytes 2097176
  15.8 12.4 %all-to-all-done.refs_0_ = bf16[8,2,128,256]{3,2,1,0:T(8,128)(2,1)} async-done(((bf16[8,2,128,256]{3,2,1,0:T(8,128)(2,1)}), bf16[8,2,128,256]{3,2,1,0:T(8,128)(2,1)}, u32[]{:S(2)}, u32[]{:S(2)}) %all-to-all-start) | async-done | bytes 1048608 | tf_op jit(solution)/shard_map/all_to_all | solution.py:330
  28.2 1.6 %copy-done.14 = f32[8,256,256]{2,1,0:T(8,128)S(1)} copy-done((f32[8,256,256]{2,1,0:T(8,128)S(1)}, f32[8,256,256]{2,1,0:T(8,128)}, u32[]{:S(2)}) %copy-start.14) | copy-done | bytes 2097176
  29.8 1.2 %copy-done.16 = bf16[8,256,256]{2,1,0:T(8,128)(2,1)S(1)} copy-done((bf16[8,256,256]{2,1,0:T(8,128)(2,1)S(1)}, bf16[8,256,256]{2,1,0:T(8,128)(2,1)}, u32[]{:S(2)}) %copy-start.16) | copy-done | bytes 1048600
  31.0 7.4 %conv.3 = (bf16[8,2,128,256]{3,2,1,0:T(8,128)(2,1)S(1)}, f32[256,256]{1,0:T(8,128)S(1)}, bf16[256,256]{1,0:T(8,128)(2,1)S(1)}, bf16[256,256]{1,0:T(8,128)(2,1)S(1)}, bf16[256,256]{1,0:T(8,128)(2,1)S(1)}) custom-call(s32[2]{0:T(128)S(1)} %pad_add_fusion.me, bf16[8,2,128,256]{3,2,1,0:T(8,128)(2,1)} %all-to-all-done.refs_0_, f32[8,256,256]{2,1,0:T(8,128)S(1)} %copy-done.14, ...), custom_call_target="tpu_custom_call" | custom-call | tf_op jit(solution)/shard_map/conv/pallas_call | solution.py:236
  41.4 4.6 %all-to-all-start.1 = ((bf16[8,2,128,256]{3,2,1,0:T(8,128)(2,1)}), bf16[8,2,128,256]{3,2,1,0:T(8,128)(2,1)}, u32[]{:S(2)}, u32[]{:S(2)}) async-start(bf16[8,2,128,256]{3,2,1,0:T(8,128)(2,1)} %copy-done.18), calls=%async_computation.1 | async-start | bytes 2097152 | tf_op jit(solution)/shard_map/all_to_all | solution.py:330
  46.0 1.2 %copy-done.7 = bf16[1,128,4096]{2,1,0:T(8,128)(2,1)S(1)} copy-done((bf16[1,128,4096]{2,1,0:T(8,128)(2,1)S(1)}, bf16[1,128,4096]{2,1,0:T(8,128)(2,1)}, u32[]{:S(2)}) %copy-start.7) | copy-done | bytes 1048600
  48.3 1.7 %collective-permute-start.1 = (bf16[2,128,256]{2,1,0:T(8,128)(2,1)S(1)}, bf16[2,128,256]{2,1,0:T(8,128)(2,1)S(1)}, u32[]{:S(2)}, u32[]{:S(2)}) collective-permute-start(bf16[2,128,256]{2,1,0:T(8,128)(2,1)S(1)} %get-tuple-element.40), channel_id=1, source_target_pairs={{0,2},{1,3},{2,0},{3,1},{4,6},{5,7},{6,4},{7,5},{8,10},{9,11},{10,... | collective-permute-start | bytes 393224 | tf_op jit(solution)/shard_map/ppermute | solution.py:322
  50.0 1.7 %collective-permute-start.3 = (bf16[2,128,256]{2,1,0:T(8,128)(2,1)S(1)}, bf16[2,128,256]{2,1,0:T(8,128)(2,1)S(1)}, u32[]{:S(2)}, u32[]{:S(2)}) collective-permute-start(bf16[2,128,256]{2,1,0:T(8,128)(2,1)S(1)} %get-tuple-element.42), channel_id=1, source_target_pairs={{0,4},{1,5},{2,6},{3,7},{4,0},{5,1},{6,2},{7,3},{8,12},{9,13},{10,... | collective-permute-start | bytes 393224 | tf_op jit(solution)/shard_map/ppermute | solution.py:322
  51.8 2.6 %collective-permute-start.5 = (bf16[2,128,256]{2,1,0:T(8,128)(2,1)S(1)}, bf16[2,128,256]{2,1,0:T(8,128)(2,1)S(1)}, u32[]{:S(2)}, u32[]{:S(2)}) collective-permute-start(bf16[2,128,256]{2,1,0:T(8,128)(2,1)S(1)} %get-tuple-element.44), channel_id=1, source_target_pairs={{0,6},{1,7},{2,4},{3,5},{4,2},{5,3},{6,0},{7,1},{8,14},{9,15},{10,... | collective-permute-start | bytes 393224 | tf_op jit(solution)/shard_map/ppermute | solution.py:322
  54.4 9.1 %collective-permute-done.1.refs_2_ = bf16[2,128,256]{2,1,0:T(8,128)(2,1)S(1)} collective-permute-done((bf16[2,128,256]{2,1,0:T(8,128)(2,1)S(1)}, bf16[2,128,256]{2,1,0:T(8,128)(2,1)S(1)}, u32[]{:S(2)}, u32[]{:S(2)}) %collective-permute-start.1) | collective-permute-done | bytes 131104 | tf_op jit(solution)/shard_map/ppermute | solution.py:322
  63.7 1.7 %filter_spectrum.2.refs_8_ = f32[8,256,256]{2,1,0:T(8,128)S(1)} custom-call(f32[512,1024]{1,0:T(8,128)S(1)} %copy-done.12, bf16[8,256,256]{2,1,0:T(8,128)(2,1)S(1)} %copy-done.10), custom_call_target="tpu_custom_call" | custom-call | tf_op jit(solution)/shard_map/filter_spectrum/pallas_call | solution.py:156
  65.5 4.5 %collective-permute-done.5.refs_6_ = bf16[2,128,256]{2,1,0:T(8,128)(2,1)S(1)} collective-permute-done((bf16[2,128,256]{2,1,0:T(8,128)(2,1)S(1)}, bf16[2,128,256]{2,1,0:T(8,128)(2,1)S(1)}, u32[]{:S(2)}, u32[]{:S(2)}) %collective-permute-start.5) | collective-permute-done | bytes 131104 | tf_op jit(solution)/shard_map/ppermute | solution.py:322
  70.0 1.9 %collective-permute-done.6.refs_7_ = bf16[2,128,256]{2,1,0:T(8,128)(2,1)S(1)} collective-permute-done((bf16[2,128,256]{2,1,0:T(8,128)(2,1)S(1)}, bf16[2,128,256]{2,1,0:T(8,128)(2,1)S(1)}, u32[]{:S(2)}, u32[]{:S(2)}) %collective-permute-start.6) | collective-permute-done | bytes 131104 | tf_op jit(solution)/shard_map/ppermute | solution.py:322
  71.9 7.4 %conv.2 = (bf16[2,128,256]{2,1,0:T(8,128)(2,1)S(1)}, bf16[2,128,256]{2,1,0:T(8,128)(2,1)S(1)}, bf16[2,128,256]{2,1,0:T(8,128)(2,1)S(1)}, bf16[2,128,256]{2,1,0:T...) custom-call(s32[2]{0:T(128)S(1)} %copy-done.25, ...), custom_call_target="tpu_custom_call" | custom-call | tf_op jit(solution)/shard_map/conv/pallas_call | solution.py:236
  80.2 2.0 %collective-permute-start.17 = (bf16[256,256]{1,0:T(8,128)(2,1)S(1)}, bf16[256,256]{1,0:T(8,128)(2,1)S(1)}, u32[]{:S(2)}, u32[]{:S(2)}) collective-permute-start(bf16[256,256]{1,0:T(8,128)(2,1)S(1)} %get-tuple-element.68), channel_id=1, source_target_pairs={{0,8},{8,0},{16,24},{24,16},{1,9},{9,1},{17,25},{25,17},{2,10},{10... | collective-permute-start | bytes 393224 | tf_op jit(solution)/shard_map/ppermute | solution.py:322
  82.2 2.6 %collective-permute-start.18 = (bf16[256,256]{1,0:T(8,128)(2,1)S(1)}, bf16[256,256]{1,0:T(8,128)(2,1)S(1)}, u32[]{:S(2)}, u32[]{:S(2)}) collective-permute-start(bf16[256,256]{1,0:T(8,128)(2,1)S(1)} %get-tuple-element.69), channel_id=1, source_target_pairs={{0,16},{8,24},{16,0},{24,8},{1,17},{9,25},{17,1},{25,9},{2,18},{10... | collective-permute-start | bytes 393224 | tf_op jit(solution)/shard_map/ppermute | solution.py:322
  87.0 3.5 %collective-permute-start.15 = (bf16[256,256]{1,0:T(8,128)(2,1)S(1)}, bf16[256,256]{1,0:T(8,128)(2,1)S(1)}, u32[]{:S(2)}, u32[]{:S(2)}) collective-permute-start(bf16[256,256]{1,0:T(8,128)(2,1)S(1)} %copy-done.30), channel_id=1, source_target_pairs={{0,16},{8,24},{16,0},{24,8},{1,17},{9,25},{17,1},{25,9},{2,18},{10... | collective-permute-start | bytes 393224 | tf_op jit(solution)/shard_map/ppermute | solution.py:322
  91.2 3.9 %collective-permute-done.18.halves_1__2_ = bf16[256,256]{1,0:T(8,128)(2,1)S(1)} collective-permute-done((bf16[256,256]{1,0:T(8,128)(2,1)S(1)}, bf16[256,256]{1,0:T(8,128)(2,1)S(1)}, u32[]{:S(2)}, u32[]{:S(2)}) %collective-permute-start.18) | collective-permute-done | bytes 131104 | tf_op jit(solution)/shard_map/ppermute | solution.py:322
  95.4 2.6 %collective-permute-start.11 = (bf16[2,128,256]{2,1,0:T(8,128)(2,1)}, bf16[2,128,256]{2,1,0:T(8,128)(2,1)}, u32[]{:S(2)}, u32[]{:S(2)}) collective-permute-start(bf16[2,128,256]{2,1,0:T(8,128)(2,1)} %get-tuple-element.51), channel_id=1, source_target_pairs={{0,5},{1,4},{2,7},{3,6},{4,1},{5,0},{6,3},{7,2},{8,13},{9,12},{10,... | collective-permute-start | bytes 393224 | tf_op jit(solution)/shard_map/ppermute | solution.py:322
  98.1 8.3 %collective-permute-done.15.halves_0__2_ = bf16[256,256]{1,0:T(8,128)(2,1)S(1)} collective-permute-done((bf16[256,256]{1,0:T(8,128)(2,1)S(1)}, bf16[256,256]{1,0:T(8,128)(2,1)S(1)}, u32[]{:S(2)}, u32[]{:S(2)}) %collective-permute-start.15) | collective-permute-done | bytes 131104 | tf_op jit(solution)/shard_map/ppermute | solution.py:322
  106.3 1.5 %collective-permute-start.12 = (bf16[2,128,256]{2,1,0:T(8,128)(2,1)}, bf16[2,128,256]{2,1,0:T(8,128)(2,1)}, u32[]{:S(2)}, u32[]{:S(2)}) collective-permute-start(bf16[2,128,256]{2,1,0:T(8,128)(2,1)} %get-tuple-element.52), channel_id=1, source_target_pairs={{0,6},{1,7},{2,4},{3,5},{4,2},{5,3},{6,0},{7,1},{8,14},{9,15},{10,... | collective-permute-start | bytes 393224 | tf_op jit(solution)/shard_map/ppermute | solution.py:322
  107.8 1.0 turn_grads.1
  108.8 1.2 %copy-done.8 = bf16[1,128,4096]{2,1,0:T(8,128)(2,1)S(1)} copy-done((bf16[1,128,4096]{2,1,0:T(8,128)(2,1)S(1)}, bf16[1,128,4096]{2,1,0:T(8,128)(2,1)}, u32[]{:S(2)}) %copy-start.8) | copy-done | bytes 1048600
  110.7 3.1 %gate.2 = (bf16[128,4096]{1,0:T(8,128)(2,1)}, bf16[128,4096]{1,0:T(8,128)(2,1)}, bf16[128,4096]{1,0:T(8,128)(2,1)}, bf16[128,4096]{1,0:T(8,128)(2,1)}) custom-call(s32[2]{0:T(128)S(1)} %copy-done.26, bf16[128,4096]{1,0:T(8,128)(2,1)S(1)} %bitcast.13, bf16[128,4096]{1,0:T(8,128)(2,1)S(1)} %bitcast.17, bf16[128,4096]{1,0:T(8,128)(2,1)S(1)} %bitcast.21, ...), custom_call_target="tpu_custom_call" | custom-call | tf_op jit(solution)/shard_map/gate/pallas_call | solution.py:283
  114.8 3.0 %gate.3 = (bf16[128,4096]{1,0:T(8,128)(2,1)}, bf16[128,4096]{1,0:T(8,128)(2,1)}, bf16[128,4096]{1,0:T(8,128)(2,1)}, bf16[128,4096]{1,0:T(8,128)(2,1)}) custom-call(s32[2]{0:T(128)S(1)} %copy-done.26, bf16[128,4096]{1,0:T(8,128)(2,1)S(1)} %bitcast.14, ...), custom_call_target="tpu_custom_call", output_to_operand_aliasing={{0}: (14, {}), {1}: (15, {}), {2}: (16, {}), {3}: (17, {})} | custom-call | tf_op jit(solution)/shard_map/gate/pallas_call | solution.py:283
  (88 shorter events, 12.0 us)
Async XLA Ops:
  0.7 45.2 %copy-start.24 = (s32[2]{0:T(128)}, s32[2]{0:T(128)S(1)}, u32[]{:S(2)}) copy-start(s32[2]{0:T(128)S(1)} %pad_add_fusion.me) | copy-start | bytes 28
  7.4 20.8 %all-to-all-start = ((bf16[8,2,128,256]{3,2,1,0:T(8,128)(2,1)}), bf16[8,2,128,256]{3,2,1,0:T(8,128)(2,1)}, u32[]{:S(2)}, u32[]{:S(2)}) async-start(bf16[8,2,128,256]{3,2,1,0:T(8,128)(2,1)} %copy-done.15), calls=%async_computation | async-start | bytes 2097152 | tf_op jit(solution)/shard_map/all_to_all | solution.py:330
  31.0 14.9 %copy-start.5 = (bf16[1,128,4096]{2,1,0:T(8,128)(2,1)S(1)}, bf16[1,128,4096]{2,1,0:T(8,128)(2,1)}, u32[]{:S(2)}) copy-start(bf16[1,128,4096]{2,1,0:T(8,128)(2,1)} %param.10) | copy-start | bytes 3145732
  41.4 67.4 %all-to-all-start.1 = ((bf16[8,2,128,256]{3,2,1,0:T(8,128)(2,1)}), bf16[8,2,128,256]{3,2,1,0:T(8,128)(2,1)}, u32[]{:S(2)}, u32[]{:S(2)}) async-start(bf16[8,2,128,256]{3,2,1,0:T(8,128)(2,1)} %copy-done.18), calls=%async_computation.1 | async-start | bytes 2097152 | tf_op jit(solution)/shard_map/all_to_all | solution.py:330
  47.2 16.5 %copy-start.10 = (bf16[8,256,256]{2,1,0:T(8,128)(2,1)S(1)}, bf16[8,256,256]{2,1,0:T(8,128)(2,1)}, u32[]{:S(2)}) copy-start(bf16[8,256,256]{2,1,0:T(8,128)(2,1)} %constant.12.clone.fwd.refs_9_.refs_2_) | copy-start | bytes 3145732
  47.2 16.5 %copy-start.12 = (f32[512,1024]{1,0:T(8,128)S(1)}, f32[512,1024]{1,0:T(8,128)}, u32[]{:S(2)}) copy-start(f32[512,1024]{1,0:T(8,128)} %filt.3) | copy-start | bytes 6291460
  48.1 3.7 %collective-permute-start = (bf16[2,128,256]{2,1,0:T(8,128)(2,1)S(1)}, bf16[2,128,256]{2,1,0:T(8,128)(2,1)S(1)}, u32[]{:S(2)}, u32[]{:S(2)}) collective-permute-start(bf16[2,128,256]{2,1,0:T(8,128)(2,1)S(1)} %get-tuple-element.39), channel_id=1, source_target_pairs={{0,1},{1,0},{2,3},{3,2},{4,5},{5,4},{6,7},{7,6},{8,9},{9,8},{10,11... | collective-permute-start | bytes 393224 | tf_op jit(solution)/shard_map/ppermute | solution.py:322
  48.3 15.2 %collective-permute-start.1 = (bf16[2,128,256]{2,1,0:T(8,128)(2,1)S(1)}, bf16[2,128,256]{2,1,0:T(8,128)(2,1)S(1)}, u32[]{:S(2)}, u32[]{:S(2)}) collective-permute-start(bf16[2,128,256]{2,1,0:T(8,128)(2,1)S(1)} %get-tuple-element.40), channel_id=1, source_target_pairs={{0,2},{1,3},{2,0},{3,1},{4,6},{5,7},{6,4},{7,5},{8,10},{9,11},{10,... | collective-permute-start | bytes 393224 | tf_op jit(solution)/shard_map/ppermute | solution.py:322
  50.0 15.5 %collective-permute-start.2 = (bf16[2,128,256]{2,1,0:T(8,128)(2,1)S(1)}, bf16[2,128,256]{2,1,0:T(8,128)(2,1)S(1)}, u32[]{:S(2)}, u32[]{:S(2)}) collective-permute-start(bf16[2,128,256]{2,1,0:T(8,128)(2,1)S(1)} %get-tuple-element.41), channel_id=1, source_target_pairs={{0,3},{1,2},{2,1},{3,0},{4,7},{5,6},{6,5},{7,4},{8,11},{9,10},{10,... | collective-permute-start | bytes 393224 | tf_op jit(solution)/shard_map/ppermute | solution.py:322
  50.0 15.5 %collective-permute-start.3 = (bf16[2,128,256]{2,1,0:T(8,128)(2,1)S(1)}, bf16[2,128,256]{2,1,0:T(8,128)(2,1)S(1)}, u32[]{:S(2)}, u32[]{:S(2)}) collective-permute-start(bf16[2,128,256]{2,1,0:T(8,128)(2,1)S(1)} %get-tuple-element.42), channel_id=1, source_target_pairs={{0,4},{1,5},{2,6},{3,7},{4,0},{5,1},{6,2},{7,3},{8,12},{9,13},{10,... | collective-permute-start | bytes 393224 | tf_op jit(solution)/shard_map/ppermute | solution.py:322
  51.7 13.8 %collective-permute-start.4 = (bf16[2,128,256]{2,1,0:T(8,128)(2,1)S(1)}, bf16[2,128,256]{2,1,0:T(8,128)(2,1)S(1)}, u32[]{:S(2)}, u32[]{:S(2)}) collective-permute-start(bf16[2,128,256]{2,1,0:T(8,128)(2,1)S(1)} %get-tuple-element.43), channel_id=1, source_target_pairs={{0,5},{1,4},{2,7},{3,6},{4,1},{5,0},{6,3},{7,2},{8,13},{9,12},{10,... | collective-permute-start | bytes 393224 | tf_op jit(solution)/shard_map/ppermute | solution.py:322
  51.8 18.2 %collective-permute-start.5 = (bf16[2,128,256]{2,1,0:T(8,128)(2,1)S(1)}, bf16[2,128,256]{2,1,0:T(8,128)(2,1)S(1)}, u32[]{:S(2)}, u32[]{:S(2)}) collective-permute-start(bf16[2,128,256]{2,1,0:T(8,128)(2,1)S(1)} %get-tuple-element.44), channel_id=1, source_target_pairs={{0,6},{1,7},{2,4},{3,5},{4,2},{5,3},{6,0},{7,1},{8,14},{9,15},{10,... | collective-permute-start | bytes 393224 | tf_op jit(solution)/shard_map/ppermute | solution.py:322
  63.5 8.4 %copy-start.17 = (bf16[8,256,256]{2,1,0:T(8,128)(2,1)S(1)}, bf16[8,256,256]{2,1,0:T(8,128)(2,1)}, u32[]{:S(2)}) copy-start(bf16[8,256,256]{2,1,0:T(8,128)(2,1)} %constant.13.clone.refs_10_.refs_3_) | copy-start | bytes 3145732
  63.5 8.4 %copy-start.25 = (s32[2]{0:T(128)S(1)}, s32[2]{0:T(128)}, u32[]{:S(2)}) copy-start(s32[2]{0:T(128)} %copy-done.24) | copy-start | bytes 28
  63.5 8.4 %collective-permute-start.6 = (bf16[2,128,256]{2,1,0:T(8,128)(2,1)S(1)}, bf16[2,128,256]{2,1,0:T(8,128)(2,1)S(1)}, u32[]{:S(2)}, u32[]{:S(2)}) collective-permute-start(bf16[2,128,256]{2,1,0:T(8,128)(2,1)S(1)} %get-tuple-element.45), channel_id=1, source_target_pairs={{0,7},{1,6},{2,5},{3,4},{4,3},{5,2},{6,1},{7,0},{8,15},{9,14},{10,... | collective-permute-start | bytes 393224 | tf_op jit(solution)/shard_map/ppermute | solution.py:322
  71.9 13.5 %copy-start.32 = (bf16[256,256]{1,0:T(8,128)(2,1)S(1)}, bf16[256,256]{1,0:T(8,128)(2,1)}, u32[]{:S(2)}) copy-start(bf16[256,256]{1,0:T(8,128)(2,1)} %copy-done.31) | copy-start | bytes 393220
  71.9 15.1 %copy-start.30 = (bf16[256,256]{1,0:T(8,128)(2,1)S(1)}, bf16[256,256]{1,0:T(8,128)(2,1)}, u32[]{:S(2)}) copy-start(bf16[256,256]{1,0:T(8,128)(2,1)} %copy-done.29) | copy-start | bytes 393220
  71.9 18.6 %copy-start.28 = (bf16[256,256]{1,0:T(8,128)(2,1)S(1)}, bf16[256,256]{1,0:T(8,128)(2,1)}, u32[]{:S(2)}) copy-start(bf16[256,256]{1,0:T(8,128)(2,1)} %copy-done.27) | copy-start | bytes 393220
  71.9 36.9 %copy-start.23 = (f32[4096]{0:T(1024)S(1)}, f32[4096]{0:T(1024)}, u32[]{:S(2)}) copy-start(f32[4096]{0:T(1024)} %param.13) | copy-start | bytes 49156
  79.3 5.4 %collective-permute-start.7 = (bf16[2,128,256]{2,1,0:T(8,128)(2,1)S(1)}, bf16[2,128,256]{2,1,0:T(8,128)(2,1)S(1)}, u32[]{:S(2)}, u32[]{:S(2)}) collective-permute-start(bf16[2,128,256]{2,1,0:T(8,128)(2,1)S(1)} %get-tuple-element.47), channel_id=1, source_target_pairs={{0,1},{1,0},{2,3},{3,2},{4,5},{5,4},{6,7},{7,6},{8,9},{9,8},{10,11... | collective-permute-start | bytes 393224 | tf_op jit(solution)/shard_map/ppermute | solution.py:322
  79.6 6.7 %collective-permute-start.8 = (bf16[2,128,256]{2,1,0:T(8,128)(2,1)S(1)}, bf16[2,128,256]{2,1,0:T(8,128)(2,1)S(1)}, u32[]{:S(2)}, u32[]{:S(2)}) collective-permute-start(bf16[2,128,256]{2,1,0:T(8,128)(2,1)S(1)} %get-tuple-element.48), channel_id=1, source_target_pairs={{0,2},{1,3},{2,0},{3,1},{4,6},{5,7},{6,4},{7,5},{8,10},{9,11},{10,... | collective-permute-start | bytes 393224 | tf_op jit(solution)/shard_map/ppermute | solution.py:322
  80.2 10.3 %collective-permute-start.17 = (bf16[256,256]{1,0:T(8,128)(2,1)S(1)}, bf16[256,256]{1,0:T(8,128)(2,1)S(1)}, u32[]{:S(2)}, u32[]{:S(2)}) collective-permute-start(bf16[256,256]{1,0:T(8,128)(2,1)S(1)} %get-tuple-element.68), channel_id=1, source_target_pairs={{0,8},{8,0},{16,24},{24,16},{1,9},{9,1},{17,25},{25,17},{2,10},{10... | collective-permute-start | bytes 393224 | tf_op jit(solution)/shard_map/ppermute | solution.py:322
  82.2 12.9 %collective-permute-start.18 = (bf16[256,256]{1,0:T(8,128)(2,1)S(1)}, bf16[256,256]{1,0:T(8,128)(2,1)S(1)}, u32[]{:S(2)}, u32[]{:S(2)}) collective-permute-start(bf16[256,256]{1,0:T(8,128)(2,1)S(1)} %get-tuple-element.69), channel_id=1, source_target_pairs={{0,16},{8,24},{16,0},{24,8},{1,17},{9,25},{17,1},{25,9},{2,18},{10... | collective-permute-start | bytes 393224 | tf_op jit(solution)/shard_map/ppermute | solution.py:322
  84.8 10.3 %collective-permute-start.19 = (bf16[256,256]{1,0:T(8,128)(2,1)S(1)}, bf16[256,256]{1,0:T(8,128)(2,1)S(1)}, u32[]{:S(2)}, u32[]{:S(2)}) collective-permute-start(bf16[256,256]{1,0:T(8,128)(2,1)S(1)} %get-tuple-element.70), channel_id=1, source_target_pairs={{0,24},{8,16},{16,8},{24,0},{1,25},{9,17},{17,9},{25,1},{2,26},{10... | collective-permute-start | bytes 393224 | tf_op jit(solution)/shard_map/ppermute | solution.py:322
  85.4 10.0 %collective-permute-start.14 = (bf16[256,256]{1,0:T(8,128)(2,1)S(1)}, bf16[256,256]{1,0:T(8,128)(2,1)S(1)}, u32[]{:S(2)}, u32[]{:S(2)}) collective-permute-start(bf16[256,256]{1,0:T(8,128)(2,1)S(1)} %copy-done.32), channel_id=1, source_target_pairs={{0,8},{8,0},{16,24},{24,16},{1,9},{9,1},{17,25},{25,17},{2,10},{10... | collective-permute-start | bytes 393224 | tf_op jit(solution)/shard_map/ppermute | solution.py:322
  87.0 19.4 %collective-permute-start.15 = (bf16[256,256]{1,0:T(8,128)(2,1)S(1)}, bf16[256,256]{1,0:T(8,128)(2,1)S(1)}, u32[]{:S(2)}, u32[]{:S(2)}) collective-permute-start(bf16[256,256]{1,0:T(8,128)(2,1)S(1)} %copy-done.30), channel_id=1, source_target_pairs={{0,16},{8,24},{16,0},{24,8},{1,17},{9,25},{17,1},{25,9},{2,18},{10... | collective-permute-start | bytes 393224 | tf_op jit(solution)/shard_map/ppermute | solution.py:322
  90.5 17.3 %collective-permute-start.16 = (bf16[256,256]{1,0:T(8,128)(2,1)S(1)}, bf16[256,256]{1,0:T(8,128)(2,1)S(1)}, u32[]{:S(2)}, u32[]{:S(2)}) collective-permute-start(bf16[256,256]{1,0:T(8,128)(2,1)S(1)} %copy-done.28), channel_id=1, source_target_pairs={{0,24},{8,16},{16,8},{24,0},{1,25},{9,17},{17,9},{25,1},{2,26},{10... | collective-permute-start | bytes 393224 | tf_op jit(solution)/shard_map/ppermute | solution.py:322
  95.1 18.7 %collective-permute-start.9 = (bf16[2,128,256]{2,1,0:T(8,128)(2,1)}, bf16[2,128,256]{2,1,0:T(8,128)(2,1)}, u32[]{:S(2)}, u32[]{:S(2)}) collective-permute-start(bf16[2,128,256]{2,1,0:T(8,128)(2,1)} %get-tuple-element.49), channel_id=1, source_target_pairs={{0,3},{1,2},{2,1},{3,0},{4,7},{5,6},{6,5},{7,4},{8,11},{9,10},{10,... | collective-permute-start | bytes 393224 | tf_op jit(solution)/shard_map/ppermute | solution.py:322
  95.1 18.7 %collective-permute-start.10 = (bf16[2,128,256]{2,1,0:T(8,128)(2,1)}, bf16[2,128,256]{2,1,0:T(8,128)(2,1)}, u32[]{:S(2)}, u32[]{:S(2)}) collective-permute-start(bf16[2,128,256]{2,1,0:T(8,128)(2,1)} %get-tuple-element.50), channel_id=1, source_target_pairs={{0,4},{1,5},{2,6},{3,7},{4,0},{5,1},{6,2},{7,3},{8,12},{9,13},{10,... | collective-permute-start | bytes 393224 | tf_op jit(solution)/shard_map/ppermute | solution.py:322
  95.4 18.4 %collective-permute-start.11 = (bf16[2,128,256]{2,1,0:T(8,128)(2,1)}, bf16[2,128,256]{2,1,0:T(8,128)(2,1)}, u32[]{:S(2)}, u32[]{:S(2)}) collective-permute-start(bf16[2,128,256]{2,1,0:T(8,128)(2,1)} %get-tuple-element.51), channel_id=1, source_target_pairs={{0,5},{1,4},{2,7},{3,6},{4,1},{5,0},{6,3},{7,2},{8,13},{9,12},{10,... | collective-permute-start | bytes 393224 | tf_op jit(solution)/shard_map/ppermute | solution.py:322
  106.3 7.5 %collective-permute-start.12 = (bf16[2,128,256]{2,1,0:T(8,128)(2,1)}, bf16[2,128,256]{2,1,0:T(8,128)(2,1)}, u32[]{:S(2)}, u32[]{:S(2)}) collective-permute-start(bf16[2,128,256]{2,1,0:T(8,128)(2,1)} %get-tuple-element.52), channel_id=1, source_target_pairs={{0,6},{1,7},{2,4},{3,5},{4,2},{5,3},{6,0},{7,1},{8,14},{9,15},{10,... | collective-permute-start | bytes 393224 | tf_op jit(solution)/shard_map/ppermute | solution.py:322
  107.8 7.0 %collective-permute-start.13 = (bf16[2,128,256]{2,1,0:T(8,128)(2,1)}, bf16[2,128,256]{2,1,0:T(8,128)(2,1)}, u32[]{:S(2)}, u32[]{:S(2)}) collective-permute-start(bf16[2,128,256]{2,1,0:T(8,128)(2,1)} %get-tuple-element.53), channel_id=1, source_target_pairs={{0,7},{1,6},{2,5},{3,4},{4,3},{5,2},{6,1},{7,0},{8,15},{9,14},{10,... | collective-permute-start | bytes 393224 | tf_op jit(solution)/shard_map/ppermute | solution.py:322
  (23 other events, 47.2 us)

commit v4 on v3

v4 whole, which is shorter than its diff:
```python
import functools
import math

import jax
import jax.numpy as jnp
import ml_dtypes
import numpy as np
from jax import lax
from jax.experimental import pallas as pl
from jax.experimental.pallas import tpu as pltpu
from jax.sharding import PartitionSpec as P

F32 = jnp.float32
BF16 = jnp.bfloat16
VMEM_LIMIT = 20 * 1024 * 1024
CLASSES = 8
ROWS = 16
HALVES = 2
PARAMS = pltpu.CompilerParams(vmem_limit_bytes=VMEM_LIMIT)
SMEM = pl.BlockSpec(memory_space=pltpu.SMEM)
VMEM = pl.BlockSpec(memory_space=pltpu.VMEM)
HBM = pl.BlockSpec(memory_space=pltpu.HBM)


def tables(length):
    m2 = length // CLASSES
    c = np.arange(CLASSES)[:, None, None]
    j = np.arange(m2)[None, :, None]
    m = np.arange(m2)[None, None, :]
    turn = ((CLASSES * m + c) * (2 * j + 1)) % (4 * length)
    angle = 2 * np.pi * turn / (4 * length)
    forward = np.concatenate([np.cos(angle), -np.sin(angle)], 1)
    back = np.swapaxes(forward, 1, 2) / length

    def parts(x):
        hi = x.astype(ml_dtypes.bfloat16)
        return hi, (x - hi.astype(np.float64)).astype(ml_dtypes.bfloat16)

    return np.concatenate(parts(forward), 2), np.concatenate(parts(back), 1)


def parts(x):
    hi = x.astype(BF16)
    return hi, (x - hi.astype(F32)).astype(BF16)


def dot(a, b):
    return jnp.dot(a, b, preferred_element_type=F32)


def dft(z, sign):
    n = len(z)
    if n == 1:
        return z
    even, odd = dft(z[0::2], sign), dft(z[1::2], sign)
    low, high = [], []
    for k in range(n // 2):
        (er, ei), (zr, zi) = even[k], odd[k]
        if k == 0:
            tr, ti = zr, zi
        elif 4 * k == n:
            tr, ti = (-zi, zr) if sign > 0 else (zi, -zr)
        else:
            c, s = math.cos(2 * math.pi * k / n), sign * math.sin(2 * math.pi * k / n)
            if 8 * k == n:
                tr, ti = (c * (zr - zi), c * (zi + zr)) if sign > 0 else (c * (zr + zi), c * (zi - zr))
            elif 8 * k == 3 * n:
                tr, ti = (c * (zr + zi), c * (zi - zr)) if sign > 0 else (c * (zr - zi), c * (zi + zr))
            else:
                tr, ti = c * zr - s * zi, c * zi + s * zr
        low.append((er + tr, ei + ti))
        high.append((er - tr, ei - ti))
    return low + high


def times(x, f, conj):
    (xr, xi), (fr, fi) = x, f
    if conj:
        return xr * fr + xi * fi, xi * fr - xr * fi
    return xr * fr - xi * fi, xr * fi + xi * fr


def resident(x):
    return pltpu.with_memory_space_constraint(x, pltpu.VMEM)


def in_hbm(x):
    return pltpu.with_memory_space_constraint(x, pltpu.HBM)


def peer_columns(me, half, j, width):
    return pl.ds(pl.multiple_of((HALVES * (me[0] ^ j) + half) * width, 128), width)


def product_kernel(n, me, key, value, query, grad, *refs):
    bufs, outs, sems = refs[:4], refs[4:-1], refs[-1]
    width = outs[0].shape[-1]
    copies = {}
    for half in range(HALVES):
        for j in range(n):
            cols = peer_columns(me, half, j, width)
            copies[half, j] = [
                pltpu.make_async_copy(src.at[:, cols], dst.at[:, cols], sems.at[a, half, j])
                for a, (src, dst) in enumerate(zip((key, value, query, grad), bufs))
            ]
            for copy in copies[half, j]:
                copy.start()
    for (half, j), row in copies.items():
        for copy in row:
            copy.wait()
        k, v, q, g = (buf[:, peer_columns(me, half, j, width)].astype(F32) for buf in bufs)
        outs[half * n + j][0] = (k * v).astype(BF16)
        outs[half * n + j][1] = (g * q).astype(BF16)


def products(n, me, key, value, query, grad):
    rows, total = key.shape
    width = total // n // HALVES
    out = pl.pallas_call(
        functools.partial(product_kernel, n),
        in_specs=[SMEM] + [HBM] * 4,
        out_specs=[VMEM] * (4 + HALVES * n),
        out_shape=[pltpu.VMEM(key.shape, BF16)] * 4
        + [pltpu.VMEM((2, rows, width), BF16)] * (HALVES * n),
        scratch_shapes=[pltpu.SemaphoreType.DMA((4, HALVES, n))],
        compiler_params=PARAMS,
        name="products",
    )(me, key, value, query, grad)
    return out[:4], [out[4 + h * n : 4 + (h + 1) * n] for h in range(HALVES)]


def lane_groups(width):
    return [slice(i, i + 128) for i in range(0, width, 128)]


def filter_kernel(half, filt, fwd, spec, x, u):
    m2 = x.shape[1] // CLASSES
    width = spec.shape[-1]
    for g in range(width // 128):
        x[g] = filt[half * width + g * 128 : half * width + (g + 1) * 128, :].T
    for c in range(CLASSES):
        for g in range(width // 128):
            hi, lo = parts(x[g, pl.ds(c, m2, stride=CLASSES), :])
            u[c, :, g * 128 : (g + 1) * 128] = dot(fwd[c], jnp.concatenate([hi, hi], 0)) + dot(
                fwd[c, :, :m2], lo
            )

    def step(i, carry):
        r = pl.multiple_of(i * ROWS, ROWS)
        for lanes in lane_groups(width):
            z = [(u[c, pl.ds(r, ROWS), lanes], u[c, pl.ds(m2 + r, ROWS), lanes]) for c in range(CLASSES)]
            for k, (re, im) in enumerate(dft(z, -1)):
                spec[k, pl.ds(r, ROWS), lanes] = re
                spec[k, pl.ds(m2 + r, ROWS), lanes] = im
        return carry

    lax.fori_loop(0, m2 // ROWS, step, 0)


def filter_spectrum(half, filters, fwd):
    chans, length = filters.shape
    width = chans // HALVES
    m2 = length // CLASSES
    return pl.pallas_call(
        functools.partial(filter_kernel, half),
        in_specs=[VMEM, VMEM],
        out_specs=VMEM,
        out_shape=pltpu.VMEM((CLASSES, 2 * m2, width), F32),
        scratch_shapes=[
            pltpu.VMEM((width // 128, length, 128), F32),
            pltpu.VMEM((CLASSES, 2 * m2, width), F32),
        ],
        compiler_params=PARAMS,
        name="filter_spectrum",
    )(filters, fwd)


def conv_kernel(n, d, half, me, *refs):
    got, (filt, fwd, back), refs = refs[:n], refs[n : n + 3], refs[n + 3 :]
    refs = refs[d * (half > 0) :]
    out, grads, (nat, x, u, y) = refs[:n], refs[n : n + d], refs[n + d :]
    _, rows, width = got[0].shape
    m2 = n * rows // CLASSES
    per = grads[0].shape[1]
    groups = lane_groups(width)

    for a in range(2):
        for g, lanes in enumerate(groups):
            for j in range(n):
                at = pl.multiple_of((me[0] ^ j) * rows, rows)
                nat[a, g, pl.ds(at, rows)] = got[j][a, :, lanes].astype(F32)
            for c in range(CLASSES):
                x[a, c, :, lanes] = nat[a, g, pl.ds(c, m2, stride=CLASSES), :].astype(BF16)
        for c in range(CLASSES):
            data = x[a, c]
            u[a, c] = dot(fwd[c], jnp.concatenate([data, data], 0))

    def step(i, carry):
        r = pl.multiple_of(i * ROWS, ROWS)
        re, im = pl.ds(r, ROWS), pl.ds(m2 + r, ROWS)
        for lanes in groups:
            kv = dft([(u[0, c, re, lanes], u[0, c, im, lanes]) for c in range(CLASSES)], -1)
            wt = dft([(u[1, c, re, lanes], u[1, c, im, lanes]) for c in range(CLASSES)], -1)
            fs = [(filt[k, re, lanes], filt[k, im, lanes]) for k in range(CLASSES)]
            for o, (left, right, conj) in enumerate([(kv, fs, False), (wt, fs, True), (wt, kv, True)]):
                z = dft([times(s, t, conj) for s, t in zip(left, right)], 1)
                for c in range(CLASSES):
                    y[o, c, re, lanes] = z[c][0].astype(BF16)
                    y[o, c, im, lanes] = z[c][1].astype(BF16)
        return carry

    lax.fori_loop(0, m2 // ROWS, step, 0)

    for o in range(3):
        for c in range(CLASSES):
            both = dot(back[c], y[o, c])
            both = both[:m2] + both[m2:]
            for g, lanes in enumerate(groups):
                nat[o, g, pl.ds(c, m2, stride=CLASSES), :] = both[:, lanes]
        for g, lanes in enumerate(groups):
            if o < 2:
                for j in range(n):
                    at = pl.multiple_of((me[0] ^ j) * rows, rows)
                    out[j][o, :, lanes] = nat[o, g, pl.ds(at, rows)].astype(BF16)
            else:
                for j in range(d):
                    at = pl.multiple_of((me[1] ^ j) * per, per)
                    grads[j][half, :, lanes] = nat[o, g, pl.ds(at, per)].astype(grads[j].dtype)


def conv(n, d, half, me, got, filt, fwd, back, grads):
    _, rows, width = got[0].shape
    length = n * rows
    m2 = length // CLASSES
    out = pl.pallas_call(
        functools.partial(conv_kernel, n, d, half),
        in_specs=[SMEM] + [VMEM] * (n + 3 + len(grads)),
        out_specs=[VMEM] * (n + d),
        out_shape=[pltpu.VMEM(got[0].shape, BF16)] * n
        + [pltpu.VMEM((HALVES, length // d, width), F32 if j == 0 else BF16) for j in range(d)],
        scratch_shapes=[
            pltpu.VMEM((3, width // 128, length, 128), F32),
            pltpu.VMEM((2, CLASSES, m2, width), BF16),
            pltpu.VMEM((2, CLASSES, 2 * m2, width), F32),
            pltpu.VMEM((3, CLASSES, 2 * m2, width), BF16),
        ],
        input_output_aliases={n + 4 + j: n + j for j in range(len(grads))},
        compiler_params=PARAMS,
        name="conv",
    )(me, *got, filt, fwd, back, *grads)
    return out[:n], out[n:]


def gate_kernel(half, n, me, query, grad, value, key, gain, *refs):
    got, outs, (sent, sems) = refs[:n], refs[-6:-2], refs[-2:]
    width = got[0].shape[-1]
    copies = []
    for j in range(n):
        cols = peer_columns(me, half, j, width)
        scale = gain[:, cols]
        q, g, v, k = (x[:, cols].astype(F32) for x in (query, grad, value, key))
        mixing = got[j][0].astype(F32) + scale * (k * v).astype(BF16).astype(F32)
        sent[0, j] = (q * mixing).astype(BF16)
        sent[1, j] = (g * mixing).astype(BF16)
        total = got[j][1].astype(F32) + scale * (g * q).astype(BF16).astype(F32)
        sent[2, j] = (total * v).astype(BF16)
        sent[3, j] = (total * k).astype(BF16)
        for a in range(4):
            copy = pltpu.make_async_copy(sent.at[a, j], outs[a].at[:, cols], sems.at[a, j])
            copy.start()
            copies.append(copy)
    for copy in copies:
        copy.wait()


def gate(half, me, query, grad, value, key, gain, got, outs):
    n = len(got)
    _, rows, width = got[0].shape
    return pl.pallas_call(
        functools.partial(gate_kernel, half, n),
        in_specs=[SMEM] + [VMEM] * (5 + n) + [HBM] * len(outs),
        out_specs=[HBM] * 4,
        out_shape=[jax.ShapeDtypeStruct(query.shape, BF16)] * 4,
        scratch_shapes=[
            pltpu.VMEM((4, n, rows, width), BF16),
            pltpu.SemaphoreType.DMA((4, n)),
        ],
        input_output_aliases={6 + n + i: i for i in range(len(outs))},
        compiler_params=PARAMS,
        name="gate",
    )(me, query, grad, value, key, gain, *got, *outs)


def turn_kernel(*refs):
    parts, out = refs[:-1], refs[-1]
    for half in range(HALVES):
        total = parts[0][half]
        for part in parts[1:]:
            total = total + part[half].astype(F32)
        width = total.shape[1]
        out[half * width : (half + 1) * width] = total.T


def turn_grads(parts):
    _, rows, width = parts[0].shape
    return pl.pallas_call(
        turn_kernel,
        in_specs=[VMEM] * len(parts),
        out_specs=VMEM,
        out_shape=jax.ShapeDtypeStruct((HALVES * width, rows), F32),
        compiler_params=PARAMS,
        name="turn_grads",
    )(*parts)


def exchange(blocks, axis):
    n = len(blocks)
    return [blocks[0]] + [
        resident(lax.ppermute(blocks[j], axis, [(i, i ^ j) for i in range(n)])) for j in range(1, n)
    ]


def local(n, d, query_in, key_in, value_in, grad_out, filters, skip_gain):
    fwd, back = (resident(jnp.asarray(t)) for t in tables(filters.shape[1]))
    filters = resident(filters)
    gain = skip_gain[None, :]
    me = jnp.stack([lax.axis_index("ctx"), lax.axis_index("dp")]).astype(jnp.int32)

    arrays = [in_hbm(x[0]) for x in (key_in, value_in, query_in, grad_out)]
    (key, value, query, grad), got = products(n, me, *arrays)
    got = [exchange(blocks, "ctx") for blocks in got]
    specs = [filter_spectrum(h, filters, fwd) for h in range(HALVES)]
    outs, grads = [], []
    for h in range(HALVES):
        mixed, grads = conv(n, d, h, me, got[h], specs[h], fwd, back, grads)
        got[h] = exchange(mixed, "ctx")
    grads = exchange(grads, "dp")
    for h in range(HALVES):
        outs = gate(h, me, query, grad, value, key, gain, got[h], outs)
    mixed_out, grad_query, grad_key, grad_value = outs
    return mixed_out[None], grad_query[None], grad_key[None], grad_value[None], turn_grads(grads)


def solution(mesh):
    rows = P("dp", "ctx", None)
    return jax.shard_map(
        functools.partial(local, mesh.shape["ctx"], mesh.shape["dp"]),
        mesh=mesh,
        in_specs=(rows, rows, rows, rows, P("ctx", None), P()),
        out_specs=(rows, rows, rows, rows, P("ctx", "dp")),
        check_vma=False,
    )
```

time: 119 us -> 85.2 us (0.72)
  waiting for transfers between devices: 41.1 us -> 21.3 us
  local copies, waits for them, and re-layouts: 17.4 us -> 0.02 us
  starting transfers between devices: 31.4 us -> 38.6 us
  Pallas kernels: 26.9 us -> 23.8 us
    unnamed x66 -> x8, local copies, waits for them, and re-layouts: 17.4 us -> 0.02 us
    ppermute x20 -> x31, starting transfers between devices: 21.6 us -> 38.6 us  [exchange(): lax.ppermute(blocks[j], axis, [(i, i ^ j) for i in range(n)])]
    all_to_all x2 -> x0, waiting for transfers between devices: 12.4 us -> none  [swap(): lax.all_to_all(block, 'ctx', split_axis=0, concat_axis=0, tiled=True)]
    all_to_all x2 -> x0, starting transfers between devices: 9.87 us -> none  [swap(): lax.all_to_all(block, 'ctx', split_axis=0, concat_axis=0, tiled=True)]
    ppermute x20 -> x31, waiting for transfers between devices: 28.7 us -> 21.3 us  [exchange(): lax.ppermute(blocks[j], axis, [(i, i ^ j) for i in range(n)])]
    pallas_call x7 -> x6, Pallas kernels: 23.5 us -> 20.2 us  [the longest x2 10.8 us: conv(): pl.pallas_call(functools.partial(conv_kernel, n, d, half), in_specs=[SMEM...]
  transfers between devices with their start and end apart: 22 -> 31, of which waited for: 7 -> 10; matrix products, arithmetic and copies ran while one was open for 0% -> 0% of each run, Pallas kernels for 13% -> 16%
where the time goes in v4:
time: 85.2 us; the launch traced here: 84.6 us
  starting transfers between devices  38.6 us (45%)
  Pallas kernels  23.8 us (28%)
  waiting for transfers between devices  21.3 us (25%)
    ppermute x31, starting transfers between devices, exchange(): lax.ppermute(blocks[j], axis, [(i, i ^ j) for i in range(n)])  38.6 us
    ppermute x31, waiting for transfers between devices, exchange(): lax.ppermute(blocks[j], axis, [(i, i ^ j) for i in range(n)])  21.3 us
    pallas_call x2, Pallas kernels, conv(): pl.pallas_call(functools.partial(conv_kernel, n, d, half), in_specs=[SMEM...  10.8 us
    pallas_call x2, Pallas kernels, gate(): pl.pallas_call(functools.partial(gate_kernel, half, n), in_specs=[SMEM] +...  4.75 us
    pallas_call x1, Pallas kernels, products(): pl.pallas_call(functools.partial(product_kernel, n), in_specs=[SMEM] + [H...  3.66 us
    pallas_call x2, Pallas kernels, filter_spectrum(): pl.pallas_call(functools.partial(filter_kernel, half), in_specs=[VMEM, VM...  3.6 us
  transfers between devices with their start and end apart: 31, of which 10 were waited for; matrix products, arithmetic and copies ran while one was open for 0% of the time, Pallas kernels for 16%

profile of v4, /device:TPU:0, one launch (start us, length us, event | category | flops | bytes accessed | tf_op | source)
XLA Modules:
  0.0 84.6 jit_solution(9550568508805674892)
XLA Ops:
  0.7 3.7 %products.1 = (bf16[128,4096]{1,0:T(8,128)(2,1)S(1)}, bf16[128,4096]{1,0:T(8,128)(2,1)S(1)}, bf16[128,4096]{1,0:T(8,128)(2,1)S(1)}, bf16[128,4096]{1,0:T(8,128)(...) custom-call(s32[2]{0:T(128)S(1)} %pad_add_fusion.me, ...), custom_call_target="tpu_custom_call" | custom-call | tf_op jit(solution)/shard_map/products/pallas_call | solution.py:119
  4.9 2.6 %collective-permute-start.1 = (bf16[2,128,256]{2,1,0:T(8,128)(2,1)S(1)}, bf16[2,128,256]{2,1,0:T(8,128)(2,1)S(1)}, u32[]{:S(2)}, u32[]{:S(2)}) collective-permute-start(bf16[2,128,256]{2,1,0:T(8,128)(2,1)S(1)} %get-tuple-element.63), channel_id=1, source_target_pairs={{0,2},{1,3},{2,0},{3,1},{4,6},{5,7},{6,4},{7,5},{8,10},{9,11},{10,... | collective-permute-start | bytes 393224 | tf_op jit(solution)/shard_map/ppermute | solution.py:319
  7.9 1.4 %collective-permute-start.9 = (bf16[2,128,256]{2,1,0:T(8,128)(2,1)S(1)}, bf16[2,128,256]{2,1,0:T(8,128)(2,1)S(1)}, u32[]{:S(2)}, u32[]{:S(2)}) collective-permute-start(bf16[2,128,256]{2,1,0:T(8,128)(2,1)S(1)} %get-tuple-element.72), channel_id=1, source_target_pairs={{0,3},{1,2},{2,1},{3,0},{4,7},{5,6},{6,5},{7,4},{8,11},{9,10},{10,... | collective-permute-start | bytes 393224 | tf_op jit(solution)/shard_map/ppermute | solution.py:319
  9.3 1.5 %collective-permute-start.10 = (bf16[2,128,256]{2,1,0:T(8,128)(2,1)S(1)}, bf16[2,128,256]{2,1,0:T(8,128)(2,1)S(1)}, u32[]{:S(2)}, u32[]{:S(2)}) collective-permute-start(bf16[2,128,256]{2,1,0:T(8,128)(2,1)S(1)} %get-tuple-element.73), channel_id=1, source_target_pairs={{0,4},{1,5},{2,6},{3,7},{4,0},{5,1},{6,2},{7,3},{8,12},{9,13},{10,... | collective-permute-start | bytes 393224 | tf_op jit(solution)/shard_map/ppermute | solution.py:319
  12.6 2.1 %collective-permute-start.12 = (bf16[2,128,256]{2,1,0:T(8,128)(2,1)S(1)}, bf16[2,128,256]{2,1,0:T(8,128)(2,1)S(1)}, u32[]{:S(2)}, u32[]{:S(2)}) collective-permute-start(bf16[2,128,256]{2,1,0:T(8,128)(2,1)S(1)} %get-tuple-element.75), channel_id=1, source_target_pairs={{0,6},{1,7},{2,4},{3,5},{4,2},{5,3},{6,0},{7,1},{8,14},{9,15},{10,... | collective-permute-start | bytes 393224 | tf_op jit(solution)/shard_map/ppermute | solution.py:319
  14.7 1.6 %collective-permute-start.13 = (bf16[2,128,256]{2,1,0:T(8,128)(2,1)S(1)}, bf16[2,128,256]{2,1,0:T(8,128)(2,1)S(1)}, u32[]{:S(2)}, u32[]{:S(2)}) collective-permute-start(bf16[2,128,256]{2,1,0:T(8,128)(2,1)S(1)} %get-tuple-element.76), channel_id=1, source_target_pairs={{0,7},{1,6},{2,5},{3,4},{4,3},{5,2},{6,1},{7,0},{8,15},{9,14},{10,... | collective-permute-start | bytes 393224 | tf_op jit(solution)/shard_map/ppermute | solution.py:319
  16.9 2.2 %collective-permute-start.2 = (bf16[2,128,256]{2,1,0:T(8,128)(2,1)S(1)}, bf16[2,128,256]{2,1,0:T(8,128)(2,1)S(1)}, u32[]{:S(2)}, u32[]{:S(2)}) collective-permute-start(bf16[2,128,256]{2,1,0:T(8,128)(2,1)S(1)} %get-tuple-element.64), channel_id=1, source_target_pairs={{0,3},{1,2},{2,1},{3,0},{4,7},{5,6},{6,5},{7,4},{8,11},{9,10},{10,... | collective-permute-start | bytes 393224 | tf_op jit(solution)/shard_map/ppermute | solution.py:319
  19.1 1.5 %collective-permute-start.3 = (bf16[2,128,256]{2,1,0:T(8,128)(2,1)S(1)}, bf16[2,128,256]{2,1,0:T(8,128)(2,1)S(1)}, u32[]{:S(2)}, u32[]{:S(2)}) collective-permute-start(bf16[2,128,256]{2,1,0:T(8,128)(2,1)S(1)} %get-tuple-element.65), channel_id=1, source_target_pairs={{0,4},{1,5},{2,6},{3,7},{4,0},{5,1},{6,2},{7,3},{8,12},{9,13},{10,... | collective-permute-start | bytes 393224 | tf_op jit(solution)/shard_map/ppermute | solution.py:319
  20.6 1.7 %collective-permute-done.11.refs_5_ = bf16[2,128,256]{2,1,0:T(8,128)(2,1)S(1)} collective-permute-done((bf16[2,128,256]{2,1,0:T(8,128)(2,1)S(1)}, bf16[2,128,256]{2,1,0:T(8,128)(2,1)S(1)}, u32[]{:S(2)}, u32[]{:S(2)}) %collective-permute-start.11) | collective-permute-done | bytes 131104 | tf_op jit(solution)/shard_map/ppermute | solution.py:319
  22.4 2.3 %collective-permute-start.4 = (bf16[2,128,256]{2,1,0:T(8,128)(2,1)S(1)}, bf16[2,128,256]{2,1,0:T(8,128)(2,1)S(1)}, u32[]{:S(2)}, u32[]{:S(2)}) collective-permute-start(bf16[2,128,256]{2,1,0:T(8,128)(2,1)S(1)} %get-tuple-element.66), channel_id=1, source_target_pairs={{0,5},{1,4},{2,7},{3,6},{4,1},{5,0},{6,3},{7,2},{8,13},{9,12},{10,... | collective-permute-start | bytes 393224 | tf_op jit(solution)/shard_map/ppermute | solution.py:319
  24.7 3.0 %collective-permute-start.6 = (bf16[2,128,256]{2,1,0:T(8,128)(2,1)S(1)}, bf16[2,128,256]{2,1,0:T(8,128)(2,1)S(1)}, u32[]{:S(2)}, u32[]{:S(2)}) collective-permute-start(bf16[2,128,256]{2,1,0:T(8,128)(2,1)S(1)} %get-tuple-element.68), channel_id=1, source_target_pairs={{0,7},{1,6},{2,5},{3,4},{4,3},{5,2},{6,1},{7,0},{8,15},{9,14},{10,... | collective-permute-start | bytes 393224 | tf_op jit(solution)/shard_map/ppermute | solution.py:319
  27.7 1.9 %filter_spectrum.3.refs_8_ = f32[8,256,256]{2,1,0:T(8,128)S(1)} custom-call(f32[512,1024]{1,0:T(8,128)S(1)} %copy-done.1, bf16[8,256,256]{2,1,0:T(8,128)(2,1)S(1)} %copy-done), custom_call_target="tpu_custom_call" | custom-call | tf_op jit(solution)/shard_map/filter_spectrum/pallas_call | solution.py:164
  29.6 1.7 %filter_spectrum.2.refs_8_ = f32[8,256,256]{2,1,0:T(8,128)S(1)} custom-call(f32[512,1024]{1,0:T(8,128)S(1)} %copy-done.1, bf16[8,256,256]{2,1,0:T(8,128)(2,1)S(1)} %copy-done), custom_call_target="tpu_custom_call" | custom-call | tf_op jit(solution)/shard_map/filter_spectrum/pallas_call | solution.py:164
  31.3 5.4 %conv.2 = (bf16[2,128,256]{2,1,0:T(8,128)(2,1)S(1)}, bf16[2,128,256]{2,1,0:T(8,128)(2,1)S(1)}, bf16[2,128,256]{2,1,0:T(8,128)(2,1)S(1)}, bf16[2,128,256]{2,1,0:T...) custom-call(s32[2]{0:T(128)S(1)} %pad_add_fusion.me, ...), custom_call_target="tpu_custom_call" | custom-call | tf_op jit(solution)/shard_map/conv/pallas_call | solution.py:235
  36.8 5.4 %conv.3 = (bf16[2,128,256]{2,1,0:T(8,128)(2,1)S(1)}, bf16[2,128,256]{2,1,0:T(8,128)(2,1)S(1)}, bf16[2,128,256]{2,1,0:T(8,128)(2,1)S(1)}, bf16[2,128,256]{2,1,0:T...) custom-call(s32[2]{0:T(128)S(1)} %pad_add_fusion.me, ...), custom_call_target="tpu_custom_call", output_to_operand_aliasing={{8}: (12, {}), {9}: (13, {}), {10}: (14, {}), {11}: (15, {})} | custom-call | tf_op jit(solution)/shard_map/conv/pallas_call | solution.py:235
  42.4 1.8 %collective-permute-start.16 = (bf16[2,128,256]{2,1,0:T(8,128)(2,1)S(1)}, bf16[2,128,256]{2,1,0:T(8,128)(2,1)S(1)}, u32[]{:S(2)}, u32[]{:S(2)}) collective-permute-start(bf16[2,128,256]{2,1,0:T(8,128)(2,1)S(1)} %get-tuple-element.84), channel_id=1, source_target_pairs={{0,3},{1,2},{2,1},{3,0},{4,7},{5,6},{6,5},{7,4},{8,11},{9,10},{10,... | collective-permute-start | bytes 393224 | tf_op jit(solution)/shard_map/ppermute | solution.py:319
  44.4 1.5 %collective-permute-start.18 = (bf16[2,128,256]{2,1,0:T(8,128)(2,1)S(1)}, bf16[2,128,256]{2,1,0:T(8,128)(2,1)S(1)}, u32[]{:S(2)}, u32[]{:S(2)}) collective-permute-start(bf16[2,128,256]{2,1,0:T(8,128)(2,1)S(1)} %get-tuple-element.86), channel_id=1, source_target_pairs={{0,5},{1,4},{2,7},{3,6},{4,1},{5,0},{6,3},{7,2},{8,13},{9,12},{10,... | collective-permute-start | bytes 393224 | tf_op jit(solution)/shard_map/ppermute | solution.py:319
  46.3 2.4 %collective-permute-done.15.refs_2_ = bf16[2,128,256]{2,1,0:T(8,128)(2,1)S(1)} collective-permute-done((bf16[2,128,256]{2,1,0:T(8,128)(2,1)S(1)}, bf16[2,128,256]{2,1,0:T(8,128)(2,1)S(1)}, u32[]{:S(2)}, u32[]{:S(2)}) %collective-permute-start.15) | collective-permute-done | bytes 131104 | tf_op jit(solution)/shard_map/ppermute | solution.py:319
  48.7 1.8 %collective-permute-done.16.refs_3_ = bf16[2,128,256]{2,1,0:T(8,128)(2,1)S(1)} collective-permute-done((bf16[2,128,256]{2,1,0:T(8,128)(2,1)S(1)}, bf16[2,128,256]{2,1,0:T(8,128)(2,1)S(1)}, u32[]{:S(2)}, u32[]{:S(2)}) %collective-permute-start.16) | collective-permute-done | bytes 131104 | tf_op jit(solution)/shard_map/ppermute | solution.py:319
  53.0 1.7 %collective-permute-start.26 = (bf16[2,128,256]{2,1,0:T(8,128)(2,1)S(1)}, bf16[2,128,256]{2,1,0:T(8,128)(2,1)S(1)}, u32[]{:S(2)}, u32[]{:S(2)}) collective-permute-start(bf16[2,128,256]{2,1,0:T(8,128)(2,1)S(1)} %get-tuple-element.95), channel_id=1, source_target_pairs={{0,6},{1,7},{2,4},{3,5},{4,2},{5,3},{6,0},{7,1},{8,14},{9,15},{10,... | collective-permute-start | bytes 393224 | tf_op jit(solution)/shard_map/ppermute | solution.py:319
  55.7 1.5 %collective-permute-start.28 = (bf16[2,256,256]{2,1,0:T(8,128)(2,1)S(1)}, bf16[2,256,256]{2,1,0:T(8,128)(2,1)S(1)}, u32[]{:S(2)}, u32[]{:S(2)}) collective-permute-start(bf16[2,256,256]{2,1,0:T(8,128)(2,1)S(1)} %get-tuple-element.106), channel_id=1, source_target_pairs={{0,8},{8,0},{16,24},{24,16},{1,9},{9,1},{17,25},{25,17},{2,10},{10... | collective-permute-start | bytes 786440 | tf_op jit(solution)/shard_map/ppermute | solution.py:319
  57.2 6.0 %collective-permute-done.24.refs_4_ = bf16[2,128,256]{2,1,0:T(8,128)(2,1)S(1)} collective-permute-done((bf16[2,128,256]{2,1,0:T(8,128)(2,1)S(1)}, bf16[2,128,256]{2,1,0:T(8,128)(2,1)S(1)}, u32[]{:S(2)}, u32[]{:S(2)}) %collective-permute-start.24) | collective-permute-done | bytes 131104 | tf_op jit(solution)/shard_map/ppermute | solution.py:319
  63.2 2.6 %collective-permute-start.29 = (bf16[2,256,256]{2,1,0:T(8,128)(2,1)S(1)}, bf16[2,256,256]{2,1,0:T(8,128)(2,1)S(1)}, u32[]{:S(2)}, u32[]{:S(2)}) collective-permute-start(bf16[2,256,256]{2,1,0:T(8,128)(2,1)S(1)} %get-tuple-element.107), channel_id=1, source_target_pairs={{0,16},{8,24},{16,0},{24,8},{1,17},{9,25},{17,1},{25,9},{2,18},{10... | collective-permute-start | bytes 786440 | tf_op jit(solution)/shard_map/ppermute | solution.py:319
  65.8 2.6 %collective-permute-start.30 = (bf16[2,256,256]{2,1,0:T(8,128)(2,1)S(1)}, bf16[2,256,256]{2,1,0:T(8,128)(2,1)S(1)}, u32[]{:S(2)}, u32[]{:S(2)}) collective-permute-start(bf16[2,256,256]{2,1,0:T(8,128)(2,1)S(1)} %get-tuple-element.108), channel_id=1, source_target_pairs={{0,24},{8,16},{16,8},{24,0},{1,25},{9,17},{17,9},{25,1},{2,26},{10... | collective-permute-start | bytes 786440 | tf_op jit(solution)/shard_map/ppermute | solution.py:319
  68.4 1.3 %collective-permute-start.19 = (bf16[2,128,256]{2,1,0:T(8,128)(2,1)S(1)}, bf16[2,128,256]{2,1,0:T(8,128)(2,1)S(1)}, u32[]{:S(2)}, u32[]{:S(2)}) collective-permute-start(bf16[2,128,256]{2,1,0:T(8,128)(2,1)S(1)} %get-tuple-element.87), channel_id=1, source_target_pairs={{0,6},{1,7},{2,4},{3,5},{4,2},{5,3},{6,0},{7,1},{8,14},{9,15},{10,... | collective-permute-start | bytes 393224 | tf_op jit(solution)/shard_map/ppermute | solution.py:319
  69.7 1.4 %collective-permute-start.20 = (bf16[2,128,256]{2,1,0:T(8,128)(2,1)S(1)}, bf16[2,128,256]{2,1,0:T(8,128)(2,1)S(1)}, u32[]{:S(2)}, u32[]{:S(2)}) collective-permute-start(bf16[2,128,256]{2,1,0:T(8,128)(2,1)S(1)} %get-tuple-element.88), channel_id=1, source_target_pairs={{0,7},{1,6},{2,5},{3,4},{4,3},{5,2},{6,1},{7,0},{8,15},{9,14},{10,... | collective-permute-start | bytes 393224 | tf_op jit(solution)/shard_map/ppermute | solution.py:319
  71.1 2.4 %gate.2 = (bf16[128,4096]{1,0:T(8,128)(2,1)}, bf16[128,4096]{1,0:T(8,128)(2,1)}, bf16[128,4096]{1,0:T(8,128)(2,1)}, bf16[128,4096]{1,0:T(8,128)(2,1)}) custom-call(s32[2]{0:T(128)S(1)} %pad_add_fusion.me, bf16[128,4096]{1,0:T(8,128)(2,1)S(1)} %get-tuple-element.57.query, bf16[128,4096]{1,0:T(8,128)(2,1)S(1)} %get-tuple-element.58.grad, ...), custom_call_target="tpu_custom_call" | custom-call | tf_op jit(solution)/shard_map/gate/pallas_call | solution.py:279
  73.5 2.1 %collective-permute-done.19.refs_6_ = bf16[2,128,256]{2,1,0:T(8,128)(2,1)S(1)} collective-permute-done((bf16[2,128,256]{2,1,0:T(8,128)(2,1)S(1)}, bf16[2,128,256]{2,1,0:T(8,128)(2,1)S(1)}, u32[]{:S(2)}, u32[]{:S(2)}) %collective-permute-start.19) | collective-permute-done | bytes 131104 | tf_op jit(solution)/shard_map/ppermute | solution.py:319
  75.6 1.9 %collective-permute-done.20.refs_7_ = bf16[2,128,256]{2,1,0:T(8,128)(2,1)S(1)} collective-permute-done((bf16[2,128,256]{2,1,0:T(8,128)(2,1)S(1)}, bf16[2,128,256]{2,1,0:T(8,128)(2,1)S(1)}, u32[]{:S(2)}, u32[]{:S(2)}) %collective-permute-start.20) | collective-permute-done | bytes 131104 | tf_op jit(solution)/shard_map/ppermute | solution.py:319
  77.5 2.4 %gate.3 = (bf16[128,4096]{1,0:T(8,128)(2,1)}, bf16[128,4096]{1,0:T(8,128)(2,1)}, bf16[128,4096]{1,0:T(8,128)(2,1)}, bf16[128,4096]{1,0:T(8,128)(2,1)}) custom-call(s32[2]{0:T(128)S(1)} %pad_add_fusion.me, bf16[128,4096]{1,0:T(8,128)(2,1)S(1)} %get-tuple-element.57.query, ...), custom_call_target="tpu_custom_call", output_to_operand_aliasing={{0}: (14, {}), {1}: (15, {}), {2}: (16, {}), {3}: (17, {})} | custom-call | tf_op jit(solution)/shard_map/gate/pallas_call | solution.py:279
  79.9 3.8 %collective-permute-done.29.refs_2_ = bf16[2,256,256]{2,1,0:T(8,128)(2,1)S(1)} collective-permute-done((bf16[2,256,256]{2,1,0:T(8,128)(2,1)S(1)}, bf16[2,256,256]{2,1,0:T(8,128)(2,1)S(1)}, u32[]{:S(2)}, u32[]{:S(2)}) %collective-permute-start.29) | collective-permute-done | bytes 262176 | tf_op jit(solution)/shard_map/ppermute | solution.py:319
  83.6 1.0 %turn_grads.1 = f32[512,256]{1,0:T(8,128)} custom-call(f32[2,256,256]{2,1,0:T(8,128)S(1)} %get-tuple-element.105.refs_0_, bf16[2,256,256]{2,1,0:T(8,128)(2,1)S(1)} %collective-permute-done.28.refs_1_, bf16[2,256,256]{2,1,0:T(8,128)(2,1)S(1)} %collective-permute-done.29.refs_2_, bf16[2,256,256]{2,1,0:T(8,128)(2,1)S(1)} %collective-permute-done.30.refs_3_), custom_call_target="tpu_custom_call" | custom-call | tf_op jit(solution)/shard_map/turn_grads/pallas_call | solution.py:306
  (47 shorter events, 7.7 us)
Async XLA Ops:
  4.4 4.9 %collective-permute-start = (bf16[2,128,256]{2,1,0:T(8,128)(2,1)S(1)}, bf16[2,128,256]{2,1,0:T(8,128)(2,1)S(1)}, u32[]{:S(2)}, u32[]{:S(2)}) collective-permute-start(bf16[2,128,256]{2,1,0:T(8,128)(2,1)S(1)} %get-tuple-element.62), channel_id=1, source_target_pairs={{0,1},{1,0},{2,3},{3,2},{4,5},{5,4},{6,7},{7,6},{8,9},{9,8},{10,11... | collective-permute-start | bytes 393224 | tf_op jit(solution)/shard_map/ppermute | solution.py:319
  4.9 6.9 %collective-permute-start.1 = (bf16[2,128,256]{2,1,0:T(8,128)(2,1)S(1)}, bf16[2,128,256]{2,1,0:T(8,128)(2,1)S(1)}, u32[]{:S(2)}, u32[]{:S(2)}) collective-permute-start(bf16[2,128,256]{2,1,0:T(8,128)(2,1)S(1)} %get-tuple-element.63), channel_id=1, source_target_pairs={{0,2},{1,3},{2,0},{3,1},{4,6},{5,7},{6,4},{7,5},{8,10},{9,11},{10,... | collective-permute-start | bytes 393224 | tf_op jit(solution)/shard_map/ppermute | solution.py:319
  7.5 5.1 %collective-permute-start.7 = (bf16[2,128,256]{2,1,0:T(8,128)(2,1)S(1)}, bf16[2,128,256]{2,1,0:T(8,128)(2,1)S(1)}, u32[]{:S(2)}, u32[]{:S(2)}) collective-permute-start(bf16[2,128,256]{2,1,0:T(8,128)(2,1)S(1)} %get-tuple-element.70), channel_id=1, source_target_pairs={{0,1},{1,0},{2,3},{3,2},{4,5},{5,4},{6,7},{7,6},{8,9},{9,8},{10,11... | collective-permute-start | bytes 393224 | tf_op jit(solution)/shard_map/ppermute | solution.py:319
  7.6 7.1 %collective-permute-start.8 = (bf16[2,128,256]{2,1,0:T(8,128)(2,1)S(1)}, bf16[2,128,256]{2,1,0:T(8,128)(2,1)S(1)}, u32[]{:S(2)}, u32[]{:S(2)}) collective-permute-start(bf16[2,128,256]{2,1,0:T(8,128)(2,1)S(1)} %get-tuple-element.71), channel_id=1, source_target_pairs={{0,2},{1,3},{2,0},{3,1},{4,6},{5,7},{6,4},{7,5},{8,10},{9,11},{10,... | collective-permute-start | bytes 393224 | tf_op jit(solution)/shard_map/ppermute | solution.py:319
  7.9 9.0 %collective-permute-start.9 = (bf16[2,128,256]{2,1,0:T(8,128)(2,1)S(1)}, bf16[2,128,256]{2,1,0:T(8,128)(2,1)S(1)}, u32[]{:S(2)}, u32[]{:S(2)}) collective-permute-start(bf16[2,128,256]{2,1,0:T(8,128)(2,1)S(1)} %get-tuple-element.72), channel_id=1, source_target_pairs={{0,3},{1,2},{2,1},{3,0},{4,7},{5,6},{6,5},{7,4},{8,11},{9,10},{10,... | collective-permute-start | bytes 393224 | tf_op jit(solution)/shard_map/ppermute | solution.py:319
  9.3 9.8 %collective-permute-start.10 = (bf16[2,128,256]{2,1,0:T(8,128)(2,1)S(1)}, bf16[2,128,256]{2,1,0:T(8,128)(2,1)S(1)}, u32[]{:S(2)}, u32[]{:S(2)}) collective-permute-start(bf16[2,128,256]{2,1,0:T(8,128)(2,1)S(1)} %get-tuple-element.73), channel_id=1, source_target_pairs={{0,4},{1,5},{2,6},{3,7},{4,0},{5,1},{6,2},{7,3},{8,12},{9,13},{10,... | collective-permute-start | bytes 393224 | tf_op jit(solution)/shard_map/ppermute | solution.py:319
  11.8 10.5 %collective-permute-start.11 = (bf16[2,128,256]{2,1,0:T(8,128)(2,1)S(1)}, bf16[2,128,256]{2,1,0:T(8,128)(2,1)S(1)}, u32[]{:S(2)}, u32[]{:S(2)}) collective-permute-start(bf16[2,128,256]{2,1,0:T(8,128)(2,1)S(1)} %get-tuple-element.74), channel_id=1, source_target_pairs={{0,5},{1,4},{2,7},{3,6},{4,1},{5,0},{6,3},{7,2},{8,13},{9,12},{10,... | collective-permute-start | bytes 393224 | tf_op jit(solution)/shard_map/ppermute | solution.py:319
  12.6 12.1 %collective-permute-start.12 = (bf16[2,128,256]{2,1,0:T(8,128)(2,1)S(1)}, bf16[2,128,256]{2,1,0:T(8,128)(2,1)S(1)}, u32[]{:S(2)}, u32[]{:S(2)}) collective-permute-start(bf16[2,128,256]{2,1,0:T(8,128)(2,1)S(1)} %get-tuple-element.75), channel_id=1, source_target_pairs={{0,6},{1,7},{2,4},{3,5},{4,2},{5,3},{6,0},{7,1},{8,14},{9,15},{10,... | collective-permute-start | bytes 393224 | tf_op jit(solution)/shard_map/ppermute | solution.py:319
  14.7 10.0 %collective-permute-start.13 = (bf16[2,128,256]{2,1,0:T(8,128)(2,1)S(1)}, bf16[2,128,256]{2,1,0:T(8,128)(2,1)S(1)}, u32[]{:S(2)}, u32[]{:S(2)}) collective-permute-start(bf16[2,128,256]{2,1,0:T(8,128)(2,1)S(1)} %get-tuple-element.76), channel_id=1, source_target_pairs={{0,7},{1,6},{2,5},{3,4},{4,3},{5,2},{6,1},{7,0},{8,15},{9,14},{10,... | collective-permute-start | bytes 393224 | tf_op jit(solution)/shard_map/ppermute | solution.py:319
  16.9 19.8 %collective-permute-start.2 = (bf16[2,128,256]{2,1,0:T(8,128)(2,1)S(1)}, bf16[2,128,256]{2,1,0:T(8,128)(2,1)S(1)}, u32[]{:S(2)}, u32[]{:S(2)}) collective-permute-start(bf16[2,128,256]{2,1,0:T(8,128)(2,1)S(1)} %get-tuple-element.64), channel_id=1, source_target_pairs={{0,3},{1,2},{2,1},{3,0},{4,7},{5,6},{6,5},{7,4},{8,11},{9,10},{10,... | collective-permute-start | bytes 393224 | tf_op jit(solution)/shard_map/ppermute | solution.py:319
  19.1 17.6 %collective-permute-start.3 = (bf16[2,128,256]{2,1,0:T(8,128)(2,1)S(1)}, bf16[2,128,256]{2,1,0:T(8,128)(2,1)S(1)}, u32[]{:S(2)}, u32[]{:S(2)}) collective-permute-start(bf16[2,128,256]{2,1,0:T(8,128)(2,1)S(1)} %get-tuple-element.65), channel_id=1, source_target_pairs={{0,4},{1,5},{2,6},{3,7},{4,0},{5,1},{6,2},{7,3},{8,12},{9,13},{10,... | collective-permute-start | bytes 393224 | tf_op jit(solution)/shard_map/ppermute | solution.py:319
  22.4 14.4 %collective-permute-start.4 = (bf16[2,128,256]{2,1,0:T(8,128)(2,1)S(1)}, bf16[2,128,256]{2,1,0:T(8,128)(2,1)S(1)}, u32[]{:S(2)}, u32[]{:S(2)}) collective-permute-start(bf16[2,128,256]{2,1,0:T(8,128)(2,1)S(1)} %get-tuple-element.66), channel_id=1, source_target_pairs={{0,5},{1,4},{2,7},{3,6},{4,1},{5,0},{6,3},{7,2},{8,13},{9,12},{10,... | collective-permute-start | bytes 393224 | tf_op jit(solution)/shard_map/ppermute | solution.py:319
  24.7 12.1 %collective-permute-start.5 = (bf16[2,128,256]{2,1,0:T(8,128)(2,1)S(1)}, bf16[2,128,256]{2,1,0:T(8,128)(2,1)S(1)}, u32[]{:S(2)}, u32[]{:S(2)}) collective-permute-start(bf16[2,128,256]{2,1,0:T(8,128)(2,1)S(1)} %get-tuple-element.67), channel_id=1, source_target_pairs={{0,6},{1,7},{2,4},{3,5},{4,2},{5,3},{6,0},{7,1},{8,14},{9,15},{10,... | collective-permute-start | bytes 393224 | tf_op jit(solution)/shard_map/ppermute | solution.py:319
  24.7 12.1 %collective-permute-start.6 = (bf16[2,128,256]{2,1,0:T(8,128)(2,1)S(1)}, bf16[2,128,256]{2,1,0:T(8,128)(2,1)S(1)}, u32[]{:S(2)}, u32[]{:S(2)}) collective-permute-start(bf16[2,128,256]{2,1,0:T(8,128)(2,1)S(1)} %get-tuple-element.68), channel_id=1, source_target_pairs={{0,7},{1,6},{2,5},{3,4},{4,3},{5,2},{6,1},{7,0},{8,15},{9,14},{10,... | collective-permute-start | bytes 393224 | tf_op jit(solution)/shard_map/ppermute | solution.py:319
  36.8 34.3 %copy-start.3 = (f32[4096]{0:T(1024)S(1)}, f32[4096]{0:T(1024)}, u32[]{:S(2)}) copy-start(f32[4096]{0:T(1024)} %param.13) | copy-start | bytes 49156
  42.2 3.6 %collective-permute-start.14 = (bf16[2,128,256]{2,1,0:T(8,128)(2,1)S(1)}, bf16[2,128,256]{2,1,0:T(8,128)(2,1)S(1)}, u32[]{:S(2)}, u32[]{:S(2)}) collective-permute-start(bf16[2,128,256]{2,1,0:T(8,128)(2,1)S(1)} %get-tuple-element.82), channel_id=1, source_target_pairs={{0,1},{1,0},{2,3},{3,2},{4,5},{5,4},{6,7},{7,6},{8,9},{9,8},{10,11... | collective-permute-start | bytes 393224 | tf_op jit(solution)/shard_map/ppermute | solution.py:319
  42.4 6.3 %collective-permute-start.15 = (bf16[2,128,256]{2,1,0:T(8,128)(2,1)S(1)}, bf16[2,128,256]{2,1,0:T(8,128)(2,1)S(1)}, u32[]{:S(2)}, u32[]{:S(2)}) collective-permute-start(bf16[2,128,256]{2,1,0:T(8,128)(2,1)S(1)} %get-tuple-element.83), channel_id=1, source_target_pairs={{0,2},{1,3},{2,0},{3,1},{4,6},{5,7},{6,4},{7,5},{8,10},{9,11},{10,... | collective-permute-start | bytes 393224 | tf_op jit(solution)/shard_map/ppermute | solution.py:319
  42.4 8.2 %collective-permute-start.16 = (bf16[2,128,256]{2,1,0:T(8,128)(2,1)S(1)}, bf16[2,128,256]{2,1,0:T(8,128)(2,1)S(1)}, u32[]{:S(2)}, u32[]{:S(2)}) collective-permute-start(bf16[2,128,256]{2,1,0:T(8,128)(2,1)S(1)} %get-tuple-element.84), channel_id=1, source_target_pairs={{0,3},{1,2},{2,1},{3,0},{4,7},{5,6},{6,5},{7,4},{8,11},{9,10},{10,... | collective-permute-start | bytes 393224 | tf_op jit(solution)/shard_map/ppermute | solution.py:319
  44.2 7.1 %collective-permute-start.17 = (bf16[2,128,256]{2,1,0:T(8,128)(2,1)S(1)}, bf16[2,128,256]{2,1,0:T(8,128)(2,1)S(1)}, u32[]{:S(2)}, u32[]{:S(2)}) collective-permute-start(bf16[2,128,256]{2,1,0:T(8,128)(2,1)S(1)} %get-tuple-element.85), channel_id=1, source_target_pairs={{0,4},{1,5},{2,6},{3,7},{4,0},{5,1},{6,2},{7,3},{8,12},{9,13},{10,... | collective-permute-start | bytes 393224 | tf_op jit(solution)/shard_map/ppermute | solution.py:319
  44.4 7.8 %collective-permute-start.18 = (bf16[2,128,256]{2,1,0:T(8,128)(2,1)S(1)}, bf16[2,128,256]{2,1,0:T(8,128)(2,1)S(1)}, u32[]{:S(2)}, u32[]{:S(2)}) collective-permute-start(bf16[2,128,256]{2,1,0:T(8,128)(2,1)S(1)} %get-tuple-element.86), channel_id=1, source_target_pairs={{0,5},{1,4},{2,7},{3,6},{4,1},{5,0},{6,3},{7,2},{8,13},{9,12},{10,... | collective-permute-start | bytes 393224 | tf_op jit(solution)/shard_map/ppermute | solution.py:319
  45.9 7.2 %collective-permute-start.21 = (bf16[2,128,256]{2,1,0:T(8,128)(2,1)S(1)}, bf16[2,128,256]{2,1,0:T(8,128)(2,1)S(1)}, u32[]{:S(2)}, u32[]{:S(2)}) collective-permute-start(bf16[2,128,256]{2,1,0:T(8,128)(2,1)S(1)} %get-tuple-element.90), channel_id=1, source_target_pairs={{0,1},{1,0},{2,3},{3,2},{4,5},{5,4},{6,7},{7,6},{8,9},{9,8},{10,11... | collective-permute-start | bytes 393224 | tf_op jit(solution)/shard_map/ppermute | solution.py:319
  48.7 6.1 %collective-permute-start.22 = (bf16[2,128,256]{2,1,0:T(8,128)(2,1)S(1)}, bf16[2,128,256]{2,1,0:T(8,128)(2,1)S(1)}, u32[]{:S(2)}, u32[]{:S(2)}) collective-permute-start(bf16[2,128,256]{2,1,0:T(8,128)(2,1)S(1)} %get-tuple-element.91), channel_id=1, source_target_pairs={{0,2},{1,3},{2,0},{3,1},{4,6},{5,7},{6,4},{7,5},{8,10},{9,11},{10,... | collective-permute-start | bytes 393224 | tf_op jit(solution)/shard_map/ppermute | solution.py:319
  50.5 5.2 %collective-permute-start.23 = (bf16[2,128,256]{2,1,0:T(8,128)(2,1)S(1)}, bf16[2,128,256]{2,1,0:T(8,128)(2,1)S(1)}, u32[]{:S(2)}, u32[]{:S(2)}) collective-permute-start(bf16[2,128,256]{2,1,0:T(8,128)(2,1)S(1)} %get-tuple-element.92), channel_id=1, source_target_pairs={{0,3},{1,2},{2,1},{3,0},{4,7},{5,6},{6,5},{7,4},{8,11},{9,10},{10,... | collective-permute-start | bytes 393224 | tf_op jit(solution)/shard_map/ppermute | solution.py:319
  51.3 11.9 %collective-permute-start.24 = (bf16[2,128,256]{2,1,0:T(8,128)(2,1)S(1)}, bf16[2,128,256]{2,1,0:T(8,128)(2,1)S(1)}, u32[]{:S(2)}, u32[]{:S(2)}) collective-permute-start(bf16[2,128,256]{2,1,0:T(8,128)(2,1)S(1)} %get-tuple-element.93), channel_id=1, source_target_pairs={{0,4},{1,5},{2,6},{3,7},{4,0},{5,1},{6,2},{7,3},{8,12},{9,13},{10,... | collective-permute-start | bytes 393224 | tf_op jit(solution)/shard_map/ppermute | solution.py:319
  52.1 13.6 %collective-permute-start.25 = (bf16[2,128,256]{2,1,0:T(8,128)(2,1)S(1)}, bf16[2,128,256]{2,1,0:T(8,128)(2,1)S(1)}, u32[]{:S(2)}, u32[]{:S(2)}) collective-permute-start(bf16[2,128,256]{2,1,0:T(8,128)(2,1)S(1)} %get-tuple-element.94), channel_id=1, source_target_pairs={{0,5},{1,4},{2,7},{3,6},{4,1},{5,0},{6,3},{7,2},{8,13},{9,12},{10,... | collective-permute-start | bytes 393224 | tf_op jit(solution)/shard_map/ppermute | solution.py:319
  53.0 15.4 %collective-permute-start.26 = (bf16[2,128,256]{2,1,0:T(8,128)(2,1)S(1)}, bf16[2,128,256]{2,1,0:T(8,128)(2,1)S(1)}, u32[]{:S(2)}, u32[]{:S(2)}) collective-permute-start(bf16[2,128,256]{2,1,0:T(8,128)(2,1)S(1)} %get-tuple-element.95), channel_id=1, source_target_pairs={{0,6},{1,7},{2,4},{3,5},{4,2},{5,3},{6,0},{7,1},{8,14},{9,15},{10,... | collective-permute-start | bytes 393224 | tf_op jit(solution)/shard_map/ppermute | solution.py:319
  54.8 14.9 %collective-permute-start.27 = (bf16[2,128,256]{2,1,0:T(8,128)(2,1)S(1)}, bf16[2,128,256]{2,1,0:T(8,128)(2,1)S(1)}, u32[]{:S(2)}, u32[]{:S(2)}) collective-permute-start(bf16[2,128,256]{2,1,0:T(8,128)(2,1)S(1)} %get-tuple-element.96), channel_id=1, source_target_pairs={{0,7},{1,6},{2,5},{3,4},{4,3},{5,2},{6,1},{7,0},{8,15},{9,14},{10,... | collective-permute-start | bytes 393224 | tf_op jit(solution)/shard_map/ppermute | solution.py:319
  55.7 24.2 %collective-permute-start.28 = (bf16[2,256,256]{2,1,0:T(8,128)(2,1)S(1)}, bf16[2,256,256]{2,1,0:T(8,128)(2,1)S(1)}, u32[]{:S(2)}, u32[]{:S(2)}) collective-permute-start(bf16[2,256,256]{2,1,0:T(8,128)(2,1)S(1)} %get-tuple-element.106), channel_id=1, source_target_pairs={{0,8},{8,0},{16,24},{24,16},{1,9},{9,1},{17,25},{25,17},{2,10},{10... | collective-permute-start | bytes 786440 | tf_op jit(solution)/shard_map/ppermute | solution.py:319
  63.2 20.4 %collective-permute-start.29 = (bf16[2,256,256]{2,1,0:T(8,128)(2,1)S(1)}, bf16[2,256,256]{2,1,0:T(8,128)(2,1)S(1)}, u32[]{:S(2)}, u32[]{:S(2)}) collective-permute-start(bf16[2,256,256]{2,1,0:T(8,128)(2,1)S(1)} %get-tuple-element.107), channel_id=1, source_target_pairs={{0,16},{8,24},{16,0},{24,8},{1,17},{9,25},{17,1},{25,9},{2,18},{10... | collective-permute-start | bytes 786440 | tf_op jit(solution)/shard_map/ppermute | solution.py:319
  65.8 17.8 %collective-permute-start.30 = (bf16[2,256,256]{2,1,0:T(8,128)(2,1)S(1)}, bf16[2,256,256]{2,1,0:T(8,128)(2,1)S(1)}, u32[]{:S(2)}, u32[]{:S(2)}) collective-permute-start(bf16[2,256,256]{2,1,0:T(8,128)(2,1)S(1)} %get-tuple-element.108), channel_id=1, source_target_pairs={{0,24},{8,16},{16,8},{24,0},{1,25},{9,17},{17,9},{25,1},{2,26},{10... | collective-permute-start | bytes 786440 | tf_op jit(solution)/shard_map/ppermute | solution.py:319
  68.4 7.2 %collective-permute-start.19 = (bf16[2,128,256]{2,1,0:T(8,128)(2,1)S(1)}, bf16[2,128,256]{2,1,0:T(8,128)(2,1)S(1)}, u32[]{:S(2)}, u32[]{:S(2)}) collective-permute-start(bf16[2,128,256]{2,1,0:T(8,128)(2,1)S(1)} %get-tuple-element.87), channel_id=1, source_target_pairs={{0,6},{1,7},{2,4},{3,5},{4,2},{5,3},{6,0},{7,1},{8,14},{9,15},{10,... | collective-permute-start | bytes 393224 | tf_op jit(solution)/shard_map/ppermute | solution.py:319
  69.7 7.8 %collective-permute-start.20 = (bf16[2,128,256]{2,1,0:T(8,128)(2,1)S(1)}, bf16[2,128,256]{2,1,0:T(8,128)(2,1)S(1)}, u32[]{:S(2)}, u32[]{:S(2)}) collective-permute-start(bf16[2,128,256]{2,1,0:T(8,128)(2,1)S(1)} %get-tuple-element.88), channel_id=1, source_target_pairs={{0,7},{1,6},{2,5},{3,4},{4,3},{5,2},{6,1},{7,0},{8,15},{9,14},{10,... | collective-permute-start | bytes 393224 | tf_op jit(solution)/shard_map/ppermute | solution.py:319
  (3 other events, 55.6 us)

commit v5 on v4

--- a/solution.py
+++ b/solution.py
@@ -133,55 +133,59 @@
     return [slice(i, i + 128) for i in range(0, width, 128)]
 
 
-def filter_kernel(half, filt, fwd, spec, x, u):
+def filter_kernel(filt, fwd, *refs):
+    specs, (x, u) = refs[-2 - HALVES : -2], refs[-2:]
     m2 = x.shape[1] // CLASSES
-    width = spec.shape[-1]
-    for g in range(width // 128):
-        x[g] = filt[half * width + g * 128 : half * width + (g + 1) * 128, :].T
-    for c in range(CLASSES):
-        for g in range(width // 128):
-            hi, lo = parts(x[g, pl.ds(c, m2, stride=CLASSES), :])
-            u[c, :, g * 128 : (g + 1) * 128] = dot(fwd[c], jnp.concatenate([hi, hi], 0)) + dot(
-                fwd[c, :, :m2], lo
-            )
-
-    def step(i, carry):
-        r = pl.multiple_of(i * ROWS, ROWS)
-        for lanes in lane_groups(width):
-            z = [(u[c, pl.ds(r, ROWS), lanes], u[c, pl.ds(m2 + r, ROWS), lanes]) for c in range(CLASSES)]
-            for k, (re, im) in enumerate(dft(z, -1)):
-                spec[k, pl.ds(r, ROWS), lanes] = re
-                spec[k, pl.ds(m2 + r, ROWS), lanes] = im
-        return carry
-
-    lax.fori_loop(0, m2 // ROWS, step, 0)
-
-
-def filter_spectrum(half, filters, fwd):
+    width = specs[0].shape[-1]
+    groups = lane_groups(width)
+    for half, spec in enumerate(specs):
+        for g, lanes in enumerate(groups):
+            x[g] = filt[half * width + lanes.start : half * width + lanes.stop, :].T
+        for c in range(CLASSES):
+            for g, lanes in enumerate(groups):
+                hi, lo = parts(x[g, pl.ds(c, m2, stride=CLASSES), :])
+                u[c, :, lanes] = dot(fwd[c], jnp.concatenate([hi, hi], 0)) + dot(fwd[c, :, :m2], lo)
+
+        def step(i, carry):
+            r = pl.multiple_of(i * ROWS, ROWS)
+            re, im = pl.ds(r, ROWS), pl.ds(m2 + r, ROWS)
+            for lanes in groups:
+                z = dft([(u[c, re, lanes], u[c, im, lanes]) for c in range(CLASSES)], -1)
+                for k in range(CLASSES):
+                    spec[k, re, lanes], spec[k, im, lanes] = z[k]
+            return carry
+
+        lax.fori_loop(0, m2 // ROWS, step, 0)
+
+
+def filter_spectra(filters, fwd, after, then):
     chans, length = filters.shape
     width = chans // HALVES
     m2 = length // CLASSES
-    return pl.pallas_call(
-        functools.partial(filter_kernel, half),
-        in_specs=[VMEM, VMEM],
-        out_specs=VMEM,
-        out_shape=pltpu.VMEM((CLASSES, 2 * m2, width), F32),
+    out = pl.pallas_call(
+        filter_kernel,
+        in_specs=[VMEM] * (2 + len(after) + len(then)),
+        out_specs=[VMEM] * (len(then) + HALVES),
+        out_shape=[pltpu.VMEM(t.shape, t.dtype) for t in then]
+        + [pltpu.VMEM((CLASSES, 2 * m2, width), F32)] * HALVES,
         scratch_shapes=[
             pltpu.VMEM((width // 128, length, 128), F32),
             pltpu.VMEM((CLASSES, 2 * m2, width), F32),
         ],
-        compiler_params=PARAMS,
-        name="filter_spectrum",
-    )(filters, fwd)
-
-
-def conv_kernel(n, d, half, me, *refs):
-    got, (filt, fwd, back), refs = refs[:n], refs[n : n + 3], refs[n + 3 :]
-    refs = refs[d * (half > 0) :]
+        input_output_aliases={2 + len(after) + i: i for i in range(len(then))},
+        compiler_params=PARAMS,
+        name="filter_spectra",
+    )(filters, fwd, *after, *then)
+    return out[len(then) :], out[: len(then)]
+
+
+def conv_kernel(n, d, me, *refs):
+    got, (filt, fwd, back) = refs[:n], refs[n : n + 3]
+    refs = refs[-(n + d + 4) :]
     out, grads, (nat, x, u, y) = refs[:n], refs[n : n + d], refs[n + d :]
     _, rows, width = got[0].shape
     m2 = n * rows // CLASSES
-    per = grads[0].shape[1]
+    per = grads[0].shape[0]
     groups = lane_groups(width)
 
     for a in range(2):
@@ -225,29 +229,28 @@
             else:
                 for j in range(d):
                     at = pl.multiple_of((me[1] ^ j) * per, per)
-                    grads[j][half, :, lanes] = nat[o, g, pl.ds(at, per)].astype(grads[j].dtype)
-
-
-def conv(n, d, half, me, got, filt, fwd, back, grads):
+                    grads[j][:, lanes] = nat[o, g, pl.ds(at, per)].astype(grads[j].dtype)
+
+
+def conv(n, d, me, got, filt, fwd, back, after):
     _, rows, width = got[0].shape
     length = n * rows
     m2 = length // CLASSES
     out = pl.pallas_call(
-        functools.partial(conv_kernel, n, d, half),
-        in_specs=[SMEM] + [VMEM] * (n + 3 + len(grads)),
+        functools.partial(conv_kernel, n, d),
+        in_specs=[SMEM] + [VMEM] * (n + 3 + len(after)),
         out_specs=[VMEM] * (n + d),
         out_shape=[pltpu.VMEM(got[0].shape, BF16)] * n
-        + [pltpu.VMEM((HALVES, length // d, width), F32 if j == 0 else BF16) for j in range(d)],
+        + [pltpu.VMEM((length // d, width), F32 if j == 0 else BF16) for j in range(d)],
         scratch_shapes=[
             pltpu.VMEM((3, width // 128, length, 128), F32),
             pltpu.VMEM((2, CLASSES, m2, width), BF16),
             pltpu.VMEM((2, CLASSES, 2 * m2, width), F32),
             pltpu.VMEM((3, CLASSES, 2 * m2, width), BF16),
         ],
-        input_output_aliases={n + 4 + j: n + j for j in range(len(grads))},
         compiler_params=PARAMS,
         name="conv",
-    )(me, *got, filt, fwd, back, *grads)
+    )(me, *got, filt, fwd, back, *after)
     return out[:n], out[n:]
 
 
@@ -291,26 +294,28 @@
     )(me, query, grad, value, key, gain, *got, *outs)
 
 
-def turn_kernel(*refs):
-    parts, out = refs[:-1], refs[-1]
+def turn_kernel(d, *refs):
+    out = refs[-1]
     for half in range(HALVES):
-        total = parts[0][half]
-        for part in parts[1:]:
-            total = total + part[half].astype(F32)
+        first, *rest = refs[half * d : (half + 1) * d]
+        total = first[...]
+        for part in rest:
+            total = total + part[...].astype(F32)
         width = total.shape[1]
         out[half * width : (half + 1) * width] = total.T
 
 
-def turn_grads(parts):
-    _, rows, width = parts[0].shape
+def turn_grads(halves):
+    d = len(halves[0])
+    rows, width = halves[0][0].shape
     return pl.pallas_call(
-        turn_kernel,
-        in_specs=[VMEM] * len(parts),
+        functools.partial(turn_kernel, d),
+        in_specs=[VMEM] * (HALVES * d),
         out_specs=VMEM,
         out_shape=jax.ShapeDtypeStruct((HALVES * width, rows), F32),
         compiler_params=PARAMS,
         name="turn_grads",
-    )(*parts)
+    )(*halves[0], *halves[1])
 
 
 def exchange(blocks, axis):
@@ -328,15 +333,17 @@
 
     arrays = [in_hbm(x[0]) for x in (key_in, value_in, query_in, grad_out)]
     (key, value, query, grad), got = products(n, me, *arrays)
-    got = [exchange(blocks, "ctx") for blocks in got]
-    specs = [filter_spectrum(h, filters, fwd) for h in range(HALVES)]
-    outs, grads = [], []
-    for h in range(HALVES):
-        mixed, grads = conv(n, d, h, me, got[h], specs[h], fwd, back, grads)
-        got[h] = exchange(mixed, "ctx")
-    grads = exchange(grads, "dp")
-    for h in range(HALVES):
-        outs = gate(h, me, query, grad, value, key, gain, got[h], outs)
+    first = exchange(got[0], "ctx")
+    specs, sent = filter_spectra(filters, fwd, first[1:5], got[1])
+    second = exchange(sent, "ctx")
+    mixed, part = conv(n, d, me, first, specs[0], fwd, back, [])
+    first = exchange(mixed, "ctx")
+    grads = [exchange(part, "dp")]
+    mixed, part = conv(n, d, me, second, specs[1], fwd, back, first[1:3])
+    grads.append(exchange(part, "dp"))
+    second = exchange(mixed, "ctx")
+    outs = gate(0, me, query, grad, value, key, gain, first, [])
+    outs = gate(1, me, query, grad, value, key, gain, second, outs)
     mixed_out, grad_query, grad_key, grad_value = outs
     return mixed_out[None], grad_query[None], grad_key[None], grad_value[None], turn_grads(grads)
 

time: 85.2 us -> 84.7 us (level)
  starting transfers between devices: 38.6 us -> 40.2 us
  waiting for transfers between devices: 21.3 us -> 19.8 us
    ppermute x31 -> x34, starting transfers between devices: 38.6 us -> 40.2 us  [exchange(): lax.ppermute(blocks[j], axis, [(i, i ^ j) for i in range(n)])]
    ppermute x31 -> x34, waiting for transfers between devices: 21.3 us -> 19.8 us  [exchange(): lax.ppermute(blocks[j], axis, [(i, i ^ j) for i in range(n)])]
    pallas_call x5 -> x4, Pallas kernels: 15.4 us -> 15.2 us  [the longest x2 10.6 us: conv(): pl.pallas_call(functools.partial(conv_kernel, n, d), in_specs=[SMEM] + [V...]
  transfers between devices with their start and end apart: 31 -> 34, of which waited for: 10 -> 12; matrix products, arithmetic and copies ran while one was open for 0% -> 0% of each run, Pallas kernels for 16% -> 21%
where the time goes in v5:
time: 84.7 us; the launch traced here: 84.6 us
  starting transfers between devices  40.2 us (47%)
  Pallas kernels  23.6 us (28%)
  waiting for transfers between devices  19.8 us (23%)
  between operations  0.91 us (1%)
    ppermute x34, starting transfers between devices, exchange(): lax.ppermute(blocks[j], axis, [(i, i ^ j) for i in range(n)])  40.2 us
    ppermute x34, waiting for transfers between devices, exchange(): lax.ppermute(blocks[j], axis, [(i, i ^ j) for i in range(n)])  19.8 us
    pallas_call x2, Pallas kernels, conv(): pl.pallas_call(functools.partial(conv_kernel, n, d), in_specs=[SMEM] + [V...  10.6 us
    pallas_call x2, Pallas kernels, gate(): pl.pallas_call(functools.partial(gate_kernel, half, n), in_specs=[SMEM] +...  4.76 us
    pallas_call x1, Pallas kernels, products(): pl.pallas_call(functools.partial(product_kernel, n), in_specs=[SMEM] + [H...  3.66 us
    pallas_call x1, Pallas kernels, filter_spectra(): pl.pallas_call(filter_kernel, in_specs=[VMEM] * (2 + len(after) + len(the...  3.6 us
  transfers between devices with their start and end apart: 34, of which 12 were waited for; matrix products, arithmetic and copies ran while one was open for 0% of the time, Pallas kernels for 21%

profile of v5, /device:TPU:0, one launch (start us, length us, event | category | flops | bytes accessed | tf_op | source)
XLA Modules:
  0.0 84.6 jit_solution(10588838928140332418)
XLA Ops:
  0.7 3.7 %products.1 = (bf16[128,4096]{1,0:T(8,128)(2,1)S(1)}, bf16[128,4096]{1,0:T(8,128)(2,1)S(1)}, bf16[128,4096]{1,0:T(8,128)(2,1)S(1)}, bf16[128,4096]{1,0:T(8,128)(...) custom-call(s32[2]{0:T(128)S(1)} %pad_add_fusion.me, ...), custom_call_target="tpu_custom_call" | custom-call | tf_op jit(solution)/shard_map/products/pallas_call | solution.py:119
  4.9 2.6 %collective-permute-start.1 = (bf16[2,128,256]{2,1,0:T(8,128)(2,1)S(1)}, bf16[2,128,256]{2,1,0:T(8,128)(2,1)S(1)}, u32[]{:S(2)}, u32[]{:S(2)}) collective-permute-start(bf16[2,128,256]{2,1,0:T(8,128)(2,1)S(1)} %get-tuple-element.72), channel_id=1, source_target_pairs={{0,2},{1,3},{2,0},{3,1},{4,6},{5,7},{6,4},{7,5},{8,10},{9,11},{10,... | collective-permute-start | bytes 393224 | tf_op jit(solution)/shard_map/ppermute | solution.py:324
  7.5 1.8 %collective-permute-start.3 = (bf16[2,128,256]{2,1,0:T(8,128)(2,1)S(1)}, bf16[2,128,256]{2,1,0:T(8,128)(2,1)S(1)}, u32[]{:S(2)}, u32[]{:S(2)}) collective-permute-start(bf16[2,128,256]{2,1,0:T(8,128)(2,1)S(1)} %get-tuple-element.74), channel_id=1, source_target_pairs={{0,4},{1,5},{2,6},{3,7},{4,0},{5,1},{6,2},{7,3},{8,12},{9,13},{10,... | collective-permute-start | bytes 393224 | tf_op jit(solution)/shard_map/ppermute | solution.py:324
  9.3 2.6 %collective-permute-start.12 = (bf16[2,128,256]{2,1,0:T(8,128)(2,1)S(1)}, bf16[2,128,256]{2,1,0:T(8,128)(2,1)S(1)}, u32[]{:S(2)}, u32[]{:S(2)}) collective-permute-start(bf16[2,128,256]{2,1,0:T(8,128)(2,1)S(1)} %get-tuple-element.94), channel_id=1, source_target_pairs={{0,6},{1,7},{2,4},{3,5},{4,2},{5,3},{6,0},{7,1},{8,14},{9,15},{10,... | collective-permute-start | bytes 393224 | tf_op jit(solution)/shard_map/ppermute | solution.py:324
  11.9 1.6 %collective-permute-start.13 = (bf16[2,128,256]{2,1,0:T(8,128)(2,1)S(1)}, bf16[2,128,256]{2,1,0:T(8,128)(2,1)S(1)}, u32[]{:S(2)}, u32[]{:S(2)}) collective-permute-start(bf16[2,128,256]{2,1,0:T(8,128)(2,1)S(1)} %get-tuple-element.95), channel_id=1, source_target_pairs={{0,7},{1,6},{2,5},{3,4},{4,3},{5,2},{6,1},{7,0},{8,15},{9,14},{10,... | collective-permute-start | bytes 393224 | tf_op jit(solution)/shard_map/ppermute | solution.py:324
  14.1 3.6 %filter_spectra.1 = (bf16[2,128,256]{2,1,0:T(8,128)(2,1)S(1)}, bf16[2,128,256]{2,1,0:T(8,128)(2,1)S(1)}, bf16[2,128,256]{2,1,0:T(8,128)(2,1)S(1)}, bf16[2,128,25...) custom-call(f32[512,1024]{1,0:T(8,128)S(1)} %copy-done.2, ...), custom_call_target="tpu_custom_call", output_to_operand_aliasing={{0}: (6, {}), {1}: (7, {}), {2}: (8, {}), {3}: (9, {}), {4}... | custom-call | tf_op jit(solution)/shard_map/filter_spectra/pallas_call | solution.py:165
  18.5 1.8 %collective-permute-start.5 = (bf16[2,128,256]{2,1,0:T(8,128)(2,1)S(1)}, bf16[2,128,256]{2,1,0:T(8,128)(2,1)S(1)}, u32[]{:S(2)}, u32[]{:S(2)}) collective-permute-start(bf16[2,128,256]{2,1,0:T(8,128)(2,1)S(1)} %get-tuple-element.85), channel_id=1, source_target_pairs={{0,2},{1,3},{2,0},{3,1},{4,6},{5,7},{6,4},{7,5},{8,10},{9,11},{10,... | collective-permute-start | bytes 393224 | tf_op jit(solution)/shard_map/ppermute | solution.py:324
  21.0 1.9 %collective-permute-start.6 = (bf16[2,128,256]{2,1,0:T(8,128)(2,1)S(1)}, bf16[2,128,256]{2,1,0:T(8,128)(2,1)S(1)}, u32[]{:S(2)}, u32[]{:S(2)}) collective-permute-start(bf16[2,128,256]{2,1,0:T(8,128)(2,1)S(1)} %get-tuple-element.86), channel_id=1, source_target_pairs={{0,3},{1,2},{2,1},{3,0},{4,7},{5,6},{6,5},{7,4},{8,11},{9,10},{10,... | collective-permute-start | bytes 393224 | tf_op jit(solution)/shard_map/ppermute | solution.py:324
  22.9 1.5 %collective-permute-start.7 = (bf16[2,128,256]{2,1,0:T(8,128)(2,1)S(1)}, bf16[2,128,256]{2,1,0:T(8,128)(2,1)S(1)}, u32[]{:S(2)}, u32[]{:S(2)}) collective-permute-start(bf16[2,128,256]{2,1,0:T(8,128)(2,1)S(1)} %get-tuple-element.87), channel_id=1, source_target_pairs={{0,4},{1,5},{2,6},{3,7},{4,0},{5,1},{6,2},{7,3},{8,12},{9,13},{10,... | collective-permute-start | bytes 393224 | tf_op jit(solution)/shard_map/ppermute | solution.py:324
  24.4 1.4 %collective-permute-start.9 = (bf16[2,128,256]{2,1,0:T(8,128)(2,1)S(1)}, bf16[2,128,256]{2,1,0:T(8,128)(2,1)S(1)}, u32[]{:S(2)}, u32[]{:S(2)}) collective-permute-start(bf16[2,128,256]{2,1,0:T(8,128)(2,1)S(1)} %get-tuple-element.89), channel_id=1, source_target_pairs={{0,6},{1,7},{2,4},{3,5},{4,2},{5,3},{6,0},{7,1},{8,14},{9,15},{10,... | collective-permute-start | bytes 393224 | tf_op jit(solution)/shard_map/ppermute | solution.py:324
  25.8 1.4 %collective-permute-start.10 = (bf16[2,128,256]{2,1,0:T(8,128)(2,1)S(1)}, bf16[2,128,256]{2,1,0:T(8,128)(2,1)S(1)}, u32[]{:S(2)}, u32[]{:S(2)}) collective-permute-start(bf16[2,128,256]{2,1,0:T(8,128)(2,1)S(1)} %get-tuple-element.90), channel_id=1, source_target_pairs={{0,7},{1,6},{2,5},{3,4},{4,3},{5,2},{6,1},{7,0},{8,15},{9,14},{10,... | collective-permute-start | bytes 393224 | tf_op jit(solution)/shard_map/ppermute | solution.py:324
  27.3 5.3 %conv.2 = (bf16[2,128,256]{2,1,0:T(8,128)(2,1)S(1)}, bf16[2,128,256]{2,1,0:T(8,128)(2,1)S(1)}, bf16[2,128,256]{2,1,0:T(8,128)(2,1)S(1)}, bf16[2,128,256]{2,1,0:T...) custom-call(s32[2]{0:T(128)S(1)} %pad_add_fusion.me, ...), custom_call_target="tpu_custom_call" | custom-call | tf_op jit(solution)/shard_map/conv/pallas_call | solution.py:239
  32.9 1.9 %collective-permute-done.7.refs_4_ = bf16[2,128,256]{2,1,0:T(8,128)(2,1)S(1)} collective-permute-done((bf16[2,128,256]{2,1,0:T(8,128)(2,1)S(1)}, bf16[2,128,256]{2,1,0:T(8,128)(2,1)S(1)}, u32[]{:S(2)}, u32[]{:S(2)}) %collective-permute-start.7) | collective-permute-done | bytes 131104 | tf_op jit(solution)/shard_map/ppermute | solution.py:324
  34.8 1.2 %collective-permute-done.8.refs_5_ = bf16[2,128,256]{2,1,0:T(8,128)(2,1)S(1)} collective-permute-done((bf16[2,128,256]{2,1,0:T(8,128)(2,1)S(1)}, bf16[2,128,256]{2,1,0:T(8,128)(2,1)S(1)}, u32[]{:S(2)}, u32[]{:S(2)}) %collective-permute-start.8) | collective-permute-done | bytes 131104 | tf_op jit(solution)/shard_map/ppermute | solution.py:324
  36.5 1.7 %collective-permute-start.24 = (bf16[2,128,256]{2,1,0:T(8,128)(2,1)S(1)}, bf16[2,128,256]{2,1,0:T(8,128)(2,1)S(1)}, u32[]{:S(2)}, u32[]{:S(2)}) collective-permute-start(bf16[2,128,256]{2,1,0:T(8,128)(2,1)S(1)} %get-tuple-element.109), channel_id=1, source_target_pairs={{0,4},{1,5},{2,6},{3,7},{4,0},{5,1},{6,2},{7,3},{8,12},{9,13},{10,... | collective-permute-start | bytes 393224 | tf_op jit(solution)/shard_map/ppermute | solution.py:324
  38.3 2.2 %collective-permute-start.26 = (bf16[2,128,256]{2,1,0:T(8,128)(2,1)S(1)}, bf16[2,128,256]{2,1,0:T(8,128)(2,1)S(1)}, u32[]{:S(2)}, u32[]{:S(2)}) collective-permute-start(bf16[2,128,256]{2,1,0:T(8,128)(2,1)S(1)} %get-tuple-element.111), channel_id=1, source_target_pairs={{0,6},{1,7},{2,4},{3,5},{4,2},{5,3},{6,0},{7,1},{8,14},{9,15},{10,... | collective-permute-start | bytes 393224 | tf_op jit(solution)/shard_map/ppermute | solution.py:324
  41.8 1.6 %collective-permute-start.28 = (bf16[256,256]{1,0:T(8,128)(2,1)S(1)}, bf16[256,256]{1,0:T(8,128)(2,1)S(1)}, u32[]{:S(2)}, u32[]{:S(2)}) collective-permute-start(bf16[256,256]{1,0:T(8,128)(2,1)S(1)} %get-tuple-element.122), channel_id=1, source_target_pairs={{0,8},{8,0},{16,24},{24,16},{1,9},{9,1},{17,25},{25,17},{2,10},{10... | collective-permute-start | bytes 393224 | tf_op jit(solution)/shard_map/ppermute | solution.py:324
  43.4 4.2 %collective-permute-done.24.refs_4_ = bf16[2,128,256]{2,1,0:T(8,128)(2,1)S(1)} collective-permute-done((bf16[2,128,256]{2,1,0:T(8,128)(2,1)S(1)}, bf16[2,128,256]{2,1,0:T(8,128)(2,1)S(1)}, u32[]{:S(2)}, u32[]{:S(2)}) %collective-permute-start.24) | collective-permute-done | bytes 131104 | tf_op jit(solution)/shard_map/ppermute | solution.py:324
  47.6 2.6 %collective-permute-start.29 = (bf16[256,256]{1,0:T(8,128)(2,1)S(1)}, bf16[256,256]{1,0:T(8,128)(2,1)S(1)}, u32[]{:S(2)}, u32[]{:S(2)}) collective-permute-start(bf16[256,256]{1,0:T(8,128)(2,1)S(1)} %get-tuple-element.123), channel_id=1, source_target_pairs={{0,16},{8,24},{16,0},{24,8},{1,17},{9,25},{17,1},{25,9},{2,18},{10... | collective-permute-start | bytes 393224 | tf_op jit(solution)/shard_map/ppermute | solution.py:324
  50.3 3.3 %collective-permute-start.30 = (bf16[256,256]{1,0:T(8,128)(2,1)S(1)}, bf16[256,256]{1,0:T(8,128)(2,1)S(1)}, u32[]{:S(2)}, u32[]{:S(2)}) collective-permute-start(bf16[256,256]{1,0:T(8,128)(2,1)S(1)} %get-tuple-element.124), channel_id=1, source_target_pairs={{0,24},{8,16},{16,8},{24,0},{1,25},{9,17},{17,9},{25,1},{2,26},{10... | collective-permute-start | bytes 393224 | tf_op jit(solution)/shard_map/ppermute | solution.py:324
  53.6 5.3 %conv.3 = (bf16[2,128,256]{2,1,0:T(8,128)(2,1)S(1)}, bf16[2,128,256]{2,1,0:T(8,128)(2,1)S(1)}, bf16[2,128,256]{2,1,0:T(8,128)(2,1)S(1)}, bf16[2,128,256]{2,1,0:T...) custom-call(s32[2]{0:T(128)S(1)} %pad_add_fusion.me, ...), custom_call_target="tpu_custom_call" | custom-call | tf_op jit(solution)/shard_map/conv/pallas_call | solution.py:239
  59.3 1.2 %collective-permute-start.17 = (bf16[2,128,256]{2,1,0:T(8,128)(2,1)S(1)}, bf16[2,128,256]{2,1,0:T(8,128)(2,1)S(1)}, u32[]{:S(2)}, u32[]{:S(2)}) collective-permute-start(bf16[2,128,256]{2,1,0:T(8,128)(2,1)S(1)} %get-tuple-element.101), channel_id=1, source_target_pairs={{0,2},{1,3},{2,0},{3,1},{4,6},{5,7},{6,4},{7,5},{8,10},{9,11},{10,... | collective-permute-start | bytes 393224 | tf_op jit(solution)/shard_map/ppermute | solution.py:324
  60.6 1.9 %collective-permute-start.32 = (bf16[256,256]{1,0:T(8,128)(2,1)S(1)}, bf16[256,256]{1,0:T(8,128)(2,1)S(1)}, u32[]{:S(2)}, u32[]{:S(2)}) collective-permute-start(bf16[256,256]{1,0:T(8,128)(2,1)S(1)} %get-tuple-element.127), channel_id=1, source_target_pairs={{0,16},{8,24},{16,0},{24,8},{1,17},{9,25},{17,1},{25,9},{2,18},{10... | collective-permute-start | bytes 393224 | tf_op jit(solution)/shard_map/ppermute | solution.py:324
  62.5 2.5 %collective-permute-start.33 = (bf16[256,256]{1,0:T(8,128)(2,1)S(1)}, bf16[256,256]{1,0:T(8,128)(2,1)S(1)}, u32[]{:S(2)}, u32[]{:S(2)}) collective-permute-start(bf16[256,256]{1,0:T(8,128)(2,1)S(1)} %get-tuple-element.128), channel_id=1, source_target_pairs={{0,24},{8,16},{16,8},{24,0},{1,25},{9,17},{17,9},{25,1},{2,26},{10... | collective-permute-start | bytes 393224 | tf_op jit(solution)/shard_map/ppermute | solution.py:324
  65.0 1.6 %collective-permute-start.19 = (bf16[2,128,256]{2,1,0:T(8,128)(2,1)S(1)}, bf16[2,128,256]{2,1,0:T(8,128)(2,1)S(1)}, u32[]{:S(2)}, u32[]{:S(2)}) collective-permute-start(bf16[2,128,256]{2,1,0:T(8,128)(2,1)S(1)} %get-tuple-element.103), channel_id=1, source_target_pairs={{0,4},{1,5},{2,6},{3,7},{4,0},{5,1},{6,2},{7,3},{8,12},{9,13},{10,... | collective-permute-start | bytes 393224 | tf_op jit(solution)/shard_map/ppermute | solution.py:324
  66.5 1.3 %collective-permute-done.31.refs_5_ = bf16[256,256]{1,0:T(8,128)(2,1)S(1)} collective-permute-done((bf16[256,256]{1,0:T(8,128)(2,1)S(1)}, bf16[256,256]{1,0:T(8,128)(2,1)S(1)}, u32[]{:S(2)}, u32[]{:S(2)}) %collective-permute-start.31) | collective-permute-done | bytes 131104 | tf_op jit(solution)/shard_map/ppermute | solution.py:324
  67.8 5.7 %collective-permute-done.32.refs_6_ = bf16[256,256]{1,0:T(8,128)(2,1)S(1)} collective-permute-done((bf16[256,256]{1,0:T(8,128)(2,1)S(1)}, bf16[256,256]{1,0:T(8,128)(2,1)S(1)}, u32[]{:S(2)}, u32[]{:S(2)}) %collective-permute-start.32) | collective-permute-done | bytes 131104 | tf_op jit(solution)/shard_map/ppermute | solution.py:324
  73.5 1.8 %collective-permute-start.21 = (bf16[2,128,256]{2,1,0:T(8,128)(2,1)S(1)}, bf16[2,128,256]{2,1,0:T(8,128)(2,1)S(1)}, u32[]{:S(2)}, u32[]{:S(2)}) collective-permute-start(bf16[2,128,256]{2,1,0:T(8,128)(2,1)S(1)} %get-tuple-element.105), channel_id=1, source_target_pairs={{0,6},{1,7},{2,4},{3,5},{4,2},{5,3},{6,0},{7,1},{8,14},{9,15},{10,... | collective-permute-start | bytes 393224 | tf_op jit(solution)/shard_map/ppermute | solution.py:324
  75.3 2.4 %gate.2 = (bf16[128,4096]{1,0:T(8,128)(2,1)}, bf16[128,4096]{1,0:T(8,128)(2,1)}, bf16[128,4096]{1,0:T(8,128)(2,1)}, bf16[128,4096]{1,0:T(8,128)(2,1)}) custom-call(s32[2]{0:T(128)S(1)} %pad_add_fusion.me, bf16[128,4096]{1,0:T(8,128)(2,1)S(1)} %get-tuple-element.67.query, bf16[128,4096]{1,0:T(8,128)(2,1)S(1)} %get-tuple-element.68.grad, ...), custom_call_target="tpu_custom_call" | custom-call | tf_op jit(solution)/shard_map/gate/pallas_call | solution.py:282
  77.7 1.0 %turn_grads.1 = f32[512,256]{1,0:T(8,128)} custom-call(f32[256,256]{1,0:T(8,128)S(1)} %get-tuple-element.121.refs_0_, bf16[256,256]{1,0:T(8,128)(2,1)S(1)} %collective-permute-done.28.refs_1_, bf16[256,256]{1,0:T(8,128)(2,1)S(1)} %collective-permute-done.29.refs_2_, bf16[256,256]{1,0:T(8,128)(2,1)S(1)} %collective-permute-done.30.refs_3_, ...), custom_call_target="tpu_custom_call" | custom-call | tf_op jit(solution)/shard_map/turn_grads/pallas_call | solution.py:311
  79.6 2.5 %collective-permute-done.22.refs_7_ = bf16[2,128,256]{2,1,0:T(8,128)(2,1)S(1)} collective-permute-done((bf16[2,128,256]{2,1,0:T(8,128)(2,1)S(1)}, bf16[2,128,256]{2,1,0:T(8,128)(2,1)S(1)}, u32[]{:S(2)}, u32[]{:S(2)}) %collective-permute-start.22) | collective-permute-done | bytes 131104 | tf_op jit(solution)/shard_map/ppermute | solution.py:324
  82.0 2.4 %gate.3 = (bf16[128,4096]{1,0:T(8,128)(2,1)}, bf16[128,4096]{1,0:T(8,128)(2,1)}, bf16[128,4096]{1,0:T(8,128)(2,1)}, bf16[128,4096]{1,0:T(8,128)(2,1)}) custom-call(s32[2]{0:T(128)S(1)} %pad_add_fusion.me, bf16[128,4096]{1,0:T(8,128)(2,1)S(1)} %get-tuple-element.67.query, ...), custom_call_target="tpu_custom_call", output_to_operand_aliasing={{0}: (14, {}), {1}: (15, {}), {2}: (16, {}), {3}: (17, {})} | custom-call | tf_op jit(solution)/shard_map/gate/pallas_call | solution.py:282
  (52 shorter events, 6.2 us)
Async XLA Ops:
  4.9 7.0 %collective-permute-start.1 = (bf16[2,128,256]{2,1,0:T(8,128)(2,1)S(1)}, bf16[2,128,256]{2,1,0:T(8,128)(2,1)S(1)}, u32[]{:S(2)}, u32[]{:S(2)}) collective-permute-start(bf16[2,128,256]{2,1,0:T(8,128)(2,1)S(1)} %get-tuple-element.72), channel_id=1, source_target_pairs={{0,2},{1,3},{2,0},{3,1},{4,6},{5,7},{6,4},{7,5},{8,10},{9,11},{10,... | collective-permute-start | bytes 393224 | tf_op jit(solution)/shard_map/ppermute | solution.py:324
  7.5 6.6 %collective-permute-start.2 = (bf16[2,128,256]{2,1,0:T(8,128)(2,1)S(1)}, bf16[2,128,256]{2,1,0:T(8,128)(2,1)S(1)}, u32[]{:S(2)}, u32[]{:S(2)}) collective-permute-start(bf16[2,128,256]{2,1,0:T(8,128)(2,1)S(1)} %get-tuple-element.73), channel_id=1, source_target_pairs={{0,3},{1,2},{2,1},{3,0},{4,7},{5,6},{6,5},{7,4},{8,11},{9,10},{10,... | collective-permute-start | bytes 393224 | tf_op jit(solution)/shard_map/ppermute | solution.py:324
  7.5 6.6 %collective-permute-start.3 = (bf16[2,128,256]{2,1,0:T(8,128)(2,1)S(1)}, bf16[2,128,256]{2,1,0:T(8,128)(2,1)S(1)}, u32[]{:S(2)}, u32[]{:S(2)}) collective-permute-start(bf16[2,128,256]{2,1,0:T(8,128)(2,1)S(1)} %get-tuple-element.74), channel_id=1, source_target_pairs={{0,4},{1,5},{2,6},{3,7},{4,0},{5,1},{6,2},{7,3},{8,12},{9,13},{10,... | collective-permute-start | bytes 393224 | tf_op jit(solution)/shard_map/ppermute | solution.py:324
  9.3 11.7 %collective-permute-start.11 = (bf16[2,128,256]{2,1,0:T(8,128)(2,1)S(1)}, bf16[2,128,256]{2,1,0:T(8,128)(2,1)S(1)}, u32[]{:S(2)}, u32[]{:S(2)}) collective-permute-start(bf16[2,128,256]{2,1,0:T(8,128)(2,1)S(1)} %get-tuple-element.93), channel_id=1, source_target_pairs={{0,5},{1,4},{2,7},{3,6},{4,1},{5,0},{6,3},{7,2},{8,13},{9,12},{10,... | collective-permute-start | bytes 393224 | tf_op jit(solution)/shard_map/ppermute | solution.py:324
  9.3 13.6 %collective-permute-start.12 = (bf16[2,128,256]{2,1,0:T(8,128)(2,1)S(1)}, bf16[2,128,256]{2,1,0:T(8,128)(2,1)S(1)}, u32[]{:S(2)}, u32[]{:S(2)}) collective-permute-start(bf16[2,128,256]{2,1,0:T(8,128)(2,1)S(1)} %get-tuple-element.94), channel_id=1, source_target_pairs={{0,6},{1,7},{2,4},{3,5},{4,2},{5,3},{6,0},{7,1},{8,14},{9,15},{10,... | collective-permute-start | bytes 393224 | tf_op jit(solution)/shard_map/ppermute | solution.py:324
  11.9 12.5 %collective-permute-start.13 = (bf16[2,128,256]{2,1,0:T(8,128)(2,1)S(1)}, bf16[2,128,256]{2,1,0:T(8,128)(2,1)S(1)}, u32[]{:S(2)}, u32[]{:S(2)}) collective-permute-start(bf16[2,128,256]{2,1,0:T(8,128)(2,1)S(1)} %get-tuple-element.95), channel_id=1, source_target_pairs={{0,7},{1,6},{2,5},{3,4},{4,3},{5,2},{6,1},{7,0},{8,15},{9,14},{10,... | collective-permute-start | bytes 393224 | tf_op jit(solution)/shard_map/ppermute | solution.py:324
  17.7 6.7 %collective-permute-start.4 = (bf16[2,128,256]{2,1,0:T(8,128)(2,1)S(1)}, bf16[2,128,256]{2,1,0:T(8,128)(2,1)S(1)}, u32[]{:S(2)}, u32[]{:S(2)}) collective-permute-start(bf16[2,128,256]{2,1,0:T(8,128)(2,1)S(1)} %get-tuple-element.84), channel_id=1, source_target_pairs={{0,1},{1,0},{2,3},{3,2},{4,5},{5,4},{6,7},{7,6},{8,9},{9,8},{10,11... | collective-permute-start | bytes 393224 | tf_op jit(solution)/shard_map/ppermute | solution.py:324
  18.5 7.3 %collective-permute-start.5 = (bf16[2,128,256]{2,1,0:T(8,128)(2,1)S(1)}, bf16[2,128,256]{2,1,0:T(8,128)(2,1)S(1)}, u32[]{:S(2)}, u32[]{:S(2)}) collective-permute-start(bf16[2,128,256]{2,1,0:T(8,128)(2,1)S(1)} %get-tuple-element.85), channel_id=1, source_target_pairs={{0,2},{1,3},{2,0},{3,1},{4,6},{5,7},{6,4},{7,5},{8,10},{9,11},{10,... | collective-permute-start | bytes 393224 | tf_op jit(solution)/shard_map/ppermute | solution.py:324
  21.0 11.6 %collective-permute-start.6 = (bf16[2,128,256]{2,1,0:T(8,128)(2,1)S(1)}, bf16[2,128,256]{2,1,0:T(8,128)(2,1)S(1)}, u32[]{:S(2)}, u32[]{:S(2)}) collective-permute-start(bf16[2,128,256]{2,1,0:T(8,128)(2,1)S(1)} %get-tuple-element.86), channel_id=1, source_target_pairs={{0,3},{1,2},{2,1},{3,0},{4,7},{5,6},{6,5},{7,4},{8,11},{9,10},{10,... | collective-permute-start | bytes 393224 | tf_op jit(solution)/shard_map/ppermute | solution.py:324
  22.9 12.0 %collective-permute-start.7 = (bf16[2,128,256]{2,1,0:T(8,128)(2,1)S(1)}, bf16[2,128,256]{2,1,0:T(8,128)(2,1)S(1)}, u32[]{:S(2)}, u32[]{:S(2)}) collective-permute-start(bf16[2,128,256]{2,1,0:T(8,128)(2,1)S(1)} %get-tuple-element.87), channel_id=1, source_target_pairs={{0,4},{1,5},{2,6},{3,7},{4,0},{5,1},{6,2},{7,3},{8,12},{9,13},{10,... | collective-permute-start | bytes 393224 | tf_op jit(solution)/shard_map/ppermute | solution.py:324
  24.4 11.6 %collective-permute-start.8 = (bf16[2,128,256]{2,1,0:T(8,128)(2,1)S(1)}, bf16[2,128,256]{2,1,0:T(8,128)(2,1)S(1)}, u32[]{:S(2)}, u32[]{:S(2)}) collective-permute-start(bf16[2,128,256]{2,1,0:T(8,128)(2,1)S(1)} %get-tuple-element.88), channel_id=1, source_target_pairs={{0,5},{1,4},{2,7},{3,6},{4,1},{5,0},{6,3},{7,2},{8,13},{9,12},{10,... | collective-permute-start | bytes 393224 | tf_op jit(solution)/shard_map/ppermute | solution.py:324
  24.4 12.1 %collective-permute-start.9 = (bf16[2,128,256]{2,1,0:T(8,128)(2,1)S(1)}, bf16[2,128,256]{2,1,0:T(8,128)(2,1)S(1)}, u32[]{:S(2)}, u32[]{:S(2)}) collective-permute-start(bf16[2,128,256]{2,1,0:T(8,128)(2,1)S(1)} %get-tuple-element.89), channel_id=1, source_target_pairs={{0,6},{1,7},{2,4},{3,5},{4,2},{5,3},{6,0},{7,1},{8,14},{9,15},{10,... | collective-permute-start | bytes 393224 | tf_op jit(solution)/shard_map/ppermute | solution.py:324
  25.8 12.5 %collective-permute-start.10 = (bf16[2,128,256]{2,1,0:T(8,128)(2,1)S(1)}, bf16[2,128,256]{2,1,0:T(8,128)(2,1)S(1)}, u32[]{:S(2)}, u32[]{:S(2)}) collective-permute-start(bf16[2,128,256]{2,1,0:T(8,128)(2,1)S(1)} %get-tuple-element.90), channel_id=1, source_target_pairs={{0,7},{1,6},{2,5},{3,4},{4,3},{5,2},{6,1},{7,0},{8,15},{9,14},{10,... | collective-permute-start | bytes 393224 | tf_op jit(solution)/shard_map/ppermute | solution.py:324
  32.6 5.7 %collective-permute-start.14 = (bf16[2,128,256]{2,1,0:T(8,128)(2,1)S(1)}, bf16[2,128,256]{2,1,0:T(8,128)(2,1)S(1)}, u32[]{:S(2)}, u32[]{:S(2)}) collective-permute-start(bf16[2,128,256]{2,1,0:T(8,128)(2,1)S(1)} %get-tuple-element.97), channel_id=1, source_target_pairs={{0,1},{1,0},{2,3},{3,2},{4,5},{5,4},{6,7},{7,6},{8,9},{9,8},{10,11... | collective-permute-start | bytes 393224 | tf_op jit(solution)/shard_map/ppermute | solution.py:324
  34.8 5.8 %collective-permute-start.15 = (bf16[2,128,256]{2,1,0:T(8,128)(2,1)S(1)}, bf16[2,128,256]{2,1,0:T(8,128)(2,1)S(1)}, u32[]{:S(2)}, u32[]{:S(2)}) collective-permute-start(bf16[2,128,256]{2,1,0:T(8,128)(2,1)S(1)} %get-tuple-element.98), channel_id=1, source_target_pairs={{0,2},{1,3},{2,0},{3,1},{4,6},{5,7},{6,4},{7,5},{8,10},{9,11},{10,... | collective-permute-start | bytes 393224 | tf_op jit(solution)/shard_map/ppermute | solution.py:324
  36.0 5.7 %collective-permute-start.23 = (bf16[2,128,256]{2,1,0:T(8,128)(2,1)S(1)}, bf16[2,128,256]{2,1,0:T(8,128)(2,1)S(1)}, u32[]{:S(2)}, u32[]{:S(2)}) collective-permute-start(bf16[2,128,256]{2,1,0:T(8,128)(2,1)S(1)} %get-tuple-element.108), channel_id=1, source_target_pairs={{0,3},{1,2},{2,1},{3,0},{4,7},{5,6},{6,5},{7,4},{8,11},{9,10},{10,... | collective-permute-start | bytes 393224 | tf_op jit(solution)/shard_map/ppermute | solution.py:324
  36.5 11.1 %collective-permute-start.24 = (bf16[2,128,256]{2,1,0:T(8,128)(2,1)S(1)}, bf16[2,128,256]{2,1,0:T(8,128)(2,1)S(1)}, u32[]{:S(2)}, u32[]{:S(2)}) collective-permute-start(bf16[2,128,256]{2,1,0:T(8,128)(2,1)S(1)} %get-tuple-element.109), channel_id=1, source_target_pairs={{0,4},{1,5},{2,6},{3,7},{4,0},{5,1},{6,2},{7,3},{8,12},{9,13},{10,... | collective-permute-start | bytes 393224 | tf_op jit(solution)/shard_map/ppermute | solution.py:324
  38.3 12.0 %collective-permute-start.25 = (bf16[2,128,256]{2,1,0:T(8,128)(2,1)S(1)}, bf16[2,128,256]{2,1,0:T(8,128)(2,1)S(1)}, u32[]{:S(2)}, u32[]{:S(2)}) collective-permute-start(bf16[2,128,256]{2,1,0:T(8,128)(2,1)S(1)} %get-tuple-element.110), channel_id=1, source_target_pairs={{0,5},{1,4},{2,7},{3,6},{4,1},{5,0},{6,3},{7,2},{8,13},{9,12},{10,... | collective-permute-start | bytes 393224 | tf_op jit(solution)/shard_map/ppermute | solution.py:324
  38.3 20.6 %collective-permute-start.26 = (bf16[2,128,256]{2,1,0:T(8,128)(2,1)S(1)}, bf16[2,128,256]{2,1,0:T(8,128)(2,1)S(1)}, u32[]{:S(2)}, u32[]{:S(2)}) collective-permute-start(bf16[2,128,256]{2,1,0:T(8,128)(2,1)S(1)} %get-tuple-element.111), channel_id=1, source_target_pairs={{0,6},{1,7},{2,4},{3,5},{4,2},{5,3},{6,0},{7,1},{8,14},{9,15},{10,... | collective-permute-start | bytes 393224 | tf_op jit(solution)/shard_map/ppermute | solution.py:324
  40.6 18.8 %collective-permute-start.27 = (bf16[2,128,256]{2,1,0:T(8,128)(2,1)S(1)}, bf16[2,128,256]{2,1,0:T(8,128)(2,1)S(1)}, u32[]{:S(2)}, u32[]{:S(2)}) collective-permute-start(bf16[2,128,256]{2,1,0:T(8,128)(2,1)S(1)} %get-tuple-element.112), channel_id=1, source_target_pairs={{0,7},{1,6},{2,5},{3,4},{4,3},{5,2},{6,1},{7,0},{8,15},{9,14},{10,... | collective-permute-start | bytes 393224 | tf_op jit(solution)/shard_map/ppermute | solution.py:324
  41.8 18.8 %collective-permute-start.28 = (bf16[256,256]{1,0:T(8,128)(2,1)S(1)}, bf16[256,256]{1,0:T(8,128)(2,1)S(1)}, u32[]{:S(2)}, u32[]{:S(2)}) collective-permute-start(bf16[256,256]{1,0:T(8,128)(2,1)S(1)} %get-tuple-element.122), channel_id=1, source_target_pairs={{0,8},{8,0},{16,24},{24,16},{1,9},{9,1},{17,25},{25,17},{2,10},{10... | collective-permute-start | bytes 393224 | tf_op jit(solution)/shard_map/ppermute | solution.py:324
  47.6 13.0 %collective-permute-start.29 = (bf16[256,256]{1,0:T(8,128)(2,1)S(1)}, bf16[256,256]{1,0:T(8,128)(2,1)S(1)}, u32[]{:S(2)}, u32[]{:S(2)}) collective-permute-start(bf16[256,256]{1,0:T(8,128)(2,1)S(1)} %get-tuple-element.123), channel_id=1, source_target_pairs={{0,16},{8,24},{16,0},{24,8},{1,17},{9,25},{17,1},{25,9},{2,18},{10... | collective-permute-start | bytes 393224 | tf_op jit(solution)/shard_map/ppermute | solution.py:324
  50.3 12.1 %collective-permute-start.30 = (bf16[256,256]{1,0:T(8,128)(2,1)S(1)}, bf16[256,256]{1,0:T(8,128)(2,1)S(1)}, u32[]{:S(2)}, u32[]{:S(2)}) collective-permute-start(bf16[256,256]{1,0:T(8,128)(2,1)S(1)} %get-tuple-element.124), channel_id=1, source_target_pairs={{0,24},{8,16},{16,8},{24,0},{1,25},{9,17},{17,9},{25,1},{2,26},{10... | collective-permute-start | bytes 393224 | tf_op jit(solution)/shard_map/ppermute | solution.py:324
  59.0 6.0 %collective-permute-start.16 = (bf16[2,128,256]{2,1,0:T(8,128)(2,1)S(1)}, bf16[2,128,256]{2,1,0:T(8,128)(2,1)S(1)}, u32[]{:S(2)}, u32[]{:S(2)}) collective-permute-start(bf16[2,128,256]{2,1,0:T(8,128)(2,1)S(1)} %get-tuple-element.100), channel_id=1, source_target_pairs={{0,1},{1,0},{2,3},{3,2},{4,5},{5,4},{6,7},{7,6},{8,9},{9,8},{10,11... | collective-permute-start | bytes 393224 | tf_op jit(solution)/shard_map/ppermute | solution.py:324
  60.6 7.3 %collective-permute-start.31 = (bf16[256,256]{1,0:T(8,128)(2,1)S(1)}, bf16[256,256]{1,0:T(8,128)(2,1)S(1)}, u32[]{:S(2)}, u32[]{:S(2)}) collective-permute-start(bf16[256,256]{1,0:T(8,128)(2,1)S(1)} %get-tuple-element.126), channel_id=1, source_target_pairs={{0,8},{8,0},{16,24},{24,16},{1,9},{9,1},{17,25},{25,17},{2,10},{10... | collective-permute-start | bytes 393224 | tf_op jit(solution)/shard_map/ppermute | solution.py:324
  60.6 13.0 %collective-permute-start.32 = (bf16[256,256]{1,0:T(8,128)(2,1)S(1)}, bf16[256,256]{1,0:T(8,128)(2,1)S(1)}, u32[]{:S(2)}, u32[]{:S(2)}) collective-permute-start(bf16[256,256]{1,0:T(8,128)(2,1)S(1)} %get-tuple-element.127), channel_id=1, source_target_pairs={{0,16},{8,24},{16,0},{24,8},{1,17},{9,25},{17,1},{25,9},{2,18},{10... | collective-permute-start | bytes 393224 | tf_op jit(solution)/shard_map/ppermute | solution.py:324
  62.5 12.8 %collective-permute-start.33 = (bf16[256,256]{1,0:T(8,128)(2,1)S(1)}, bf16[256,256]{1,0:T(8,128)(2,1)S(1)}, u32[]{:S(2)}, u32[]{:S(2)}) collective-permute-start(bf16[256,256]{1,0:T(8,128)(2,1)S(1)} %get-tuple-element.128), channel_id=1, source_target_pairs={{0,24},{8,16},{16,8},{24,0},{1,25},{9,17},{17,9},{25,1},{2,26},{10... | collective-permute-start | bytes 393224 | tf_op jit(solution)/shard_map/ppermute | solution.py:324
  65.0 13.8 %collective-permute-start.18 = (bf16[2,128,256]{2,1,0:T(8,128)(2,1)S(1)}, bf16[2,128,256]{2,1,0:T(8,128)(2,1)S(1)}, u32[]{:S(2)}, u32[]{:S(2)}) collective-permute-start(bf16[2,128,256]{2,1,0:T(8,128)(2,1)S(1)} %get-tuple-element.102), channel_id=1, source_target_pairs={{0,3},{1,2},{2,1},{3,0},{4,7},{5,6},{6,5},{7,4},{8,11},{9,10},{10,... | collective-permute-start | bytes 393224 | tf_op jit(solution)/shard_map/ppermute | solution.py:324
  65.0 13.8 %collective-permute-start.19 = (bf16[2,128,256]{2,1,0:T(8,128)(2,1)S(1)}, bf16[2,128,256]{2,1,0:T(8,128)(2,1)S(1)}, u32[]{:S(2)}, u32[]{:S(2)}) collective-permute-start(bf16[2,128,256]{2,1,0:T(8,128)(2,1)S(1)} %get-tuple-element.103), channel_id=1, source_target_pairs={{0,4},{1,5},{2,6},{3,7},{4,0},{5,1},{6,2},{7,3},{8,12},{9,13},{10,... | collective-permute-start | bytes 393224 | tf_op jit(solution)/shard_map/ppermute | solution.py:324
  67.8 10.9 %collective-permute-start.20 = (bf16[2,128,256]{2,1,0:T(8,128)(2,1)S(1)}, bf16[2,128,256]{2,1,0:T(8,128)(2,1)S(1)}, u32[]{:S(2)}, u32[]{:S(2)}) collective-permute-start(bf16[2,128,256]{2,1,0:T(8,128)(2,1)S(1)} %get-tuple-element.104), channel_id=1, source_target_pairs={{0,5},{1,4},{2,7},{3,6},{4,1},{5,0},{6,3},{7,2},{8,13},{9,12},{10,... | collective-permute-start | bytes 393224 | tf_op jit(solution)/shard_map/ppermute | solution.py:324
  73.5 6.0 %collective-permute-start.21 = (bf16[2,128,256]{2,1,0:T(8,128)(2,1)S(1)}, bf16[2,128,256]{2,1,0:T(8,128)(2,1)S(1)}, u32[]{:S(2)}, u32[]{:S(2)}) collective-permute-start(bf16[2,128,256]{2,1,0:T(8,128)(2,1)S(1)} %get-tuple-element.105), channel_id=1, source_target_pairs={{0,6},{1,7},{2,4},{3,5},{4,2},{5,3},{6,0},{7,1},{8,14},{9,15},{10,... | collective-permute-start | bytes 393224 | tf_op jit(solution)/shard_map/ppermute | solution.py:324
  75.3 6.7 %collective-permute-start.22 = (bf16[2,128,256]{2,1,0:T(8,128)(2,1)S(1)}, bf16[2,128,256]{2,1,0:T(8,128)(2,1)S(1)}, u32[]{:S(2)}, u32[]{:S(2)}) collective-permute-start(bf16[2,128,256]{2,1,0:T(8,128)(2,1)S(1)} %get-tuple-element.106), channel_id=1, source_target_pairs={{0,7},{1,6},{2,5},{3,4},{4,3},{5,2},{6,1},{7,0},{8,15},{9,14},{10,... | collective-permute-start | bytes 393224 | tf_op jit(solution)/shard_map/ppermute | solution.py:324
  (6 other events, 72.2 us)

commit v6 on v5

v6 whole, which is shorter than its diff:
```python
import functools
import math

import jax
import jax.numpy as jnp
import ml_dtypes
import numpy as np
from jax import lax
from jax.experimental import pallas as pl
from jax.experimental.pallas import tpu as pltpu
from jax.sharding import PartitionSpec as P

F32 = jnp.float32
BF16 = jnp.bfloat16
CLASSES = 8
HALVES = 2
STEPS = 4
PARAMS = pltpu.CompilerParams(vmem_limit_bytes=16 * 1024 * 1024)
CONV_PARAMS = pltpu.CompilerParams(vmem_limit_bytes=34 * 1024 * 1024)
SMEM = pl.BlockSpec(memory_space=pltpu.SMEM)
VMEM = pl.BlockSpec(memory_space=pltpu.VMEM)
HBM = pl.BlockSpec(memory_space=pltpu.HBM)


def tables(length):
    m2 = length // CLASSES
    c = np.arange(CLASSES)[:, None, None]
    j = np.arange(m2)[None, :, None]
    m = np.arange(m2)[None, None, :]
    turn = ((CLASSES * m + c) * (2 * j + 1)) % (4 * length)
    angle = 2 * np.pi * turn / (4 * length)
    forward = np.concatenate([np.cos(angle), -np.sin(angle)], 1)
    back = np.swapaxes(forward, 1, 2) / length

    def parts(x):
        hi = x.astype(ml_dtypes.bfloat16)
        return hi, (x - hi.astype(np.float64)).astype(ml_dtypes.bfloat16)

    return np.concatenate(parts(forward), 2), np.concatenate(parts(back), 1)


def parts(x):
    hi = x.astype(BF16)
    return hi, (x - hi.astype(F32)).astype(BF16)


def dot(a, b):
    return jnp.dot(a, b, preferred_element_type=F32)


def dft(z, sign):
    n = len(z)
    if n == 1:
        return z
    even, odd = dft(z[0::2], sign), dft(z[1::2], sign)
    low, high = [], []
    for k in range(n // 2):
        (er, ei), (zr, zi) = even[k], odd[k]
        if k == 0:
            tr, ti = zr, zi
        elif 4 * k == n:
            tr, ti = (-zi, zr) if sign > 0 else (zi, -zr)
        else:
            c, s = math.cos(2 * math.pi * k / n), sign * math.sin(2 * math.pi * k / n)
            if 8 * k == n:
                tr, ti = (c * (zr - zi), c * (zi + zr)) if sign > 0 else (c * (zr + zi), c * (zi - zr))
            elif 8 * k == 3 * n:
                tr, ti = (c * (zr + zi), c * (zi - zr)) if sign > 0 else (c * (zr - zi), c * (zi + zr))
            else:
                tr, ti = c * zr - s * zi, c * zi + s * zr
        low.append((er + tr, ei + ti))
        high.append((er - tr, ei - ti))
    return low + high


def times(x, f, conj):
    (xr, xi), (fr, fi) = x, f
    if conj:
        return xr * fr + xi * fi, xi * fr - xr * fi
    return xr * fr - xi * fi, xr * fi + xi * fr


def resident(x):
    return pltpu.with_memory_space_constraint(x, pltpu.VMEM)


def in_hbm(x):
    return pltpu.with_memory_space_constraint(x, pltpu.HBM)


def peer_columns(me, j, width):
    return pl.ds(pl.multiple_of((me[0] ^ j) * width, 128), width)


def product_kernel(n, me, key, value, query, grad, *refs):
    bufs, outs, sems = refs[:4], refs[4:-1], refs[-1]
    _, rows, width = outs[0].shape
    step = rows // STEPS
    copies = []
    for i in range(STEPS):
        at = pl.ds(i * step, step)
        copies.append(
            [
                pltpu.make_async_copy(src.at[at], dst.at[at], sems.at[a, i])
                for a, (src, dst) in enumerate(zip((key, value, query, grad), bufs))
            ]
        )
        for copy in copies[i]:
            copy.start()
    for i in range(STEPS):
        at = pl.ds(i * step, step)
        for a, (left, right) in enumerate((bufs[:2], bufs[2:])):
            copies[i][2 * a].wait()
            copies[i][2 * a + 1].wait()
            for j, out in enumerate(outs):
                cols = peer_columns(me, j, width)
                out[a, at] = (left[at, cols].astype(F32) * right[at, cols].astype(F32)).astype(BF16)


def products(n, me, key, value, query, grad):
    rows, total = key.shape
    out = pl.pallas_call(
        functools.partial(product_kernel, n),
        in_specs=[SMEM] + [HBM] * 4,
        out_specs=[VMEM] * (4 + n),
        out_shape=[pltpu.VMEM(key.shape, BF16)] * 4
        + [pltpu.VMEM((2, rows, total // n), BF16)] * n,
        scratch_shapes=[pltpu.SemaphoreType.DMA((4, STEPS))],
        compiler_params=PARAMS,
        name="products",
    )(me, key, value, query, grad)
    return out[:4], out[4:]


def lane_groups(width):
    return [slice(i, i + 128) for i in range(0, width, 128)]


def filter_kernel(filt, fwd, spec, x, u):
    m2, width = x.shape[1] // CLASSES, u.shape[-1]
    groups = lane_groups(width)
    rows = m2 // CLASSES
    for half in range(HALVES):
        for g, lanes in enumerate(groups):
            x[g] = filt[half * width + lanes.start : half * width + lanes.stop, :].T
        for c in range(CLASSES):
            for g, lanes in enumerate(groups):
                hi, lo = parts(x[g, pl.ds(c, m2, stride=CLASSES), :])
                u[c, :, lanes] = dot(fwd[c], jnp.concatenate([hi, hi], 0)) + dot(fwd[c, :, :m2], lo)

        def step(i, carry):
            r = pl.multiple_of(i * rows, rows)
            re, im = pl.ds(r, rows), pl.ds(m2 + r, rows)
            for lanes in groups:
                z = dft([(u[c, re, lanes], u[c, im, lanes]) for c in range(CLASSES)], -1)
                for k in range(CLASSES):
                    spec[half, k, re, lanes], spec[half, k, im, lanes] = z[k]
            return carry

        lax.fori_loop(0, CLASSES, step, 0)


def filter_spectra(filters, fwd):
    chans, length = filters.shape
    width = chans // HALVES
    m2 = length // CLASSES
    return pl.pallas_call(
        filter_kernel,
        in_specs=[VMEM, VMEM],
        out_specs=VMEM,
        out_shape=pltpu.VMEM((HALVES, CLASSES, 2 * m2, width), F32),
        scratch_shapes=[
            pltpu.VMEM((width // 128, length, 128), F32),
            pltpu.VMEM((CLASSES, 2 * m2, width), F32),
        ],
        compiler_params=PARAMS,
        name="filter_spectra",
    )(filters, fwd)


def conv_kernel(n, d, me, *refs):
    got, (filt, fwd, back), refs = refs[:n], refs[n : n + 3], refs[n + 3 :]
    out, (keep, send, nat), refs = refs[:n], refs[n : n + 3], refs[n + 3 :]
    xs, us, ys, turned = (refs[i : i + HALVES] for i in range(0, 4 * HALVES, HALVES))
    rows = got[0].shape[1]
    m2, width = xs[0].shape[2:]
    per = keep.shape[1]
    groups = lane_groups(width)
    step_rows = m2 // CLASSES

    def load(half):
        for a in range(2):
            for g, lanes in enumerate(groups):
                chans = slice(half * width + lanes.start, half * width + lanes.stop)
                for j in range(n):
                    at = pl.multiple_of((me[0] ^ j) * rows, rows)
                    nat[a, g, pl.ds(at, rows)] = got[j][a, :, chans].astype(F32)
                for c in range(CLASSES):
                    piece = nat[a, g, pl.ds(c, m2, stride=CLASSES), :]
                    xs[half][a, c, :, lanes] = piece.astype(BF16)

    def forward(half, c):
        for a in range(2):
            data = xs[half][a, c]
            us[half][a, c] = dot(fwd[c], jnp.concatenate([data, data], 0))

    def middle(half, i):
        u, y = us[half], ys[half]
        r = pl.multiple_of(i * step_rows, step_rows)
        re, im = pl.ds(r, step_rows), pl.ds(m2 + r, step_rows)
        for lanes in groups:
            kv = dft([(u[0, c, re, lanes], u[0, c, im, lanes]) for c in range(CLASSES)], -1)
            wt = dft([(u[1, c, re, lanes], u[1, c, im, lanes]) for c in range(CLASSES)], -1)
            fs = [(filt[half, k, re, lanes], filt[half, k, im, lanes]) for k in range(CLASSES)]
            for o, (left, right, conj) in enumerate([(kv, fs, False), (wt, fs, True), (wt, kv, True)]):
                z = dft([times(s, t, conj) for s, t in zip(left, right)], 1)
                for c in range(CLASSES):
                    y[o, c, re, lanes] = z[c][0].astype(BF16)
                    y[o, c, im, lanes] = z[c][1].astype(BF16)

    def inverse(half, c):
        for o in range(3):
            both = dot(back[c], ys[half][o, c])
            both = both[:m2] + both[m2:]
            for g, lanes in enumerate(groups):
                turned[half][o, g, pl.ds(c, m2, stride=CLASSES), :] = both[:, lanes]

    def store(half):
        for g, lanes in enumerate(groups):
            chans = slice(half * width + lanes.start, half * width + lanes.stop)
            for o in range(2):
                for j in range(n):
                    at = pl.multiple_of((me[0] ^ j) * rows, rows)
                    out[j][o, :, chans] = turned[half][o, g, pl.ds(at, rows)].astype(BF16)
            for j in range(d):
                at = pl.multiple_of((me[1] ^ j) * per, per)
                part = turned[half][2, g, pl.ds(at, per)]
                if j % 2:
                    send[j // 2, :, chans] = part.astype(BF16)
                else:
                    keep[j // 2, :, chans] = part

    def first(i, carry):
        middle(0, i)
        forward(1, i)
        return carry

    def second(i, carry):
        middle(1, i)
        inverse(0, i)
        return carry

    load(0)
    for c in range(CLASSES):
        forward(0, c)
    load(1)
    lax.fori_loop(0, CLASSES, first, 0)
    lax.fori_loop(0, CLASSES, second, 0)
    store(0)
    for c in range(CLASSES):
        inverse(1, c)
    store(1)


def conv(n, d, me, got, filt, fwd, back):
    _, rows, chans = got[0].shape
    width = chans // HALVES
    length = n * rows
    m2 = length // CLASSES
    natural = (width // 128, length, 128)
    out = pl.pallas_call(
        functools.partial(conv_kernel, n, d),
        in_specs=[SMEM] + [VMEM] * (n + 3),
        out_specs=[VMEM] * (n + 2),
        out_shape=[pltpu.VMEM(got[0].shape, BF16)] * n
        + [pltpu.VMEM((d // 2, length // d, chans), dtype) for dtype in (F32, BF16)],
        scratch_shapes=[pltpu.VMEM((2, *natural), F32)]
        + [pltpu.VMEM((2, CLASSES, m2, width), BF16)] * HALVES
        + [pltpu.VMEM((2, CLASSES, 2 * m2, width), F32)] * HALVES
        + [pltpu.VMEM((3, CLASSES, 2 * m2, width), BF16)] * HALVES
        + [pltpu.VMEM((3, *natural), F32)] * HALVES,
        compiler_params=CONV_PARAMS,
        name="conv",
    )(me, *got, filt, fwd, back)
    return out[:n], out[n], out[n + 1]


def gate_kernel(js, me, query, grad, value, key, gain, *refs):
    got, outs, (sent, sems) = refs[: len(js)], refs[-6:-2], refs[-2:]
    width = got[0].shape[-1]
    copies = []
    for i, j in enumerate(js):
        cols = peer_columns(me, j, width)
        scale = gain[:, cols]
        q, g, v, k = (x[:, cols].astype(F32) for x in (query, grad, value, key))
        mixing = got[i][0].astype(F32) + scale * (k * v).astype(BF16).astype(F32)
        sent[0, i] = (q * mixing).astype(BF16)
        sent[1, i] = (g * mixing).astype(BF16)
        total = got[i][1].astype(F32) + scale * (g * q).astype(BF16).astype(F32)
        sent[2, i] = (total * v).astype(BF16)
        sent[3, i] = (total * k).astype(BF16)
        for a in range(4):
            copy = pltpu.make_async_copy(sent.at[a, i], outs[a].at[:, cols], sems.at[a, i])
            copy.start()
            copies.append(copy)
    for copy in copies:
        copy.wait()


def gate(js, me, query, grad, value, key, gain, got, outs):
    _, rows, width = got[0].shape
    return pl.pallas_call(
        functools.partial(gate_kernel, js),
        in_specs=[SMEM] + [VMEM] * (5 + len(js)) + [HBM] * len(outs),
        out_specs=[HBM] * 4,
        out_shape=[jax.ShapeDtypeStruct(query.shape, BF16)] * 4,
        scratch_shapes=[
            pltpu.VMEM((4, len(js), rows, width), BF16),
            pltpu.SemaphoreType.DMA((4, len(js))),
        ],
        input_output_aliases={6 + len(js) + i: i for i in range(len(outs))},
        compiler_params=PARAMS,
        name="gate",
    )(me, query, grad, value, key, gain, *(got[j] for j in js), *outs)


def add_kernel(keep, got, new_keep, new_send):
    for i in range(new_keep.shape[0]):
        new_keep[i] = keep[2 * i] + got[2 * i].astype(F32)
        new_send[i] = (keep[2 * i + 1] + got[2 * i + 1].astype(F32)).astype(BF16)


def turn_kernel(keep, got, out):
    out[...] = (keep[0] + got[0].astype(F32)).T


def sum_grads(d, keep, send):
    _, per, chans = keep.shape
    bit = 1
    while True:
        got = resident(lax.ppermute(send, "dp", [(i, i ^ bit) for i in range(d)]))
        if keep.shape[0] == 1:
            break
        shape = (keep.shape[0] // 2, per, chans)
        keep, send = pl.pallas_call(
            add_kernel,
            in_specs=[VMEM] * 2,
            out_specs=[VMEM] * 2,
            out_shape=[pltpu.VMEM(shape, F32), pltpu.VMEM(shape, BF16)],
            compiler_params=PARAMS,
            name="add_grads",
        )(keep, got)
        bit *= 2
    return pl.pallas_call(
        turn_kernel,
        in_specs=[VMEM] * 2,
        out_specs=VMEM,
        out_shape=jax.ShapeDtypeStruct((chans, per), F32),
        compiler_params=PARAMS,
        name="turn_grads",
    )(keep, got)


def exchange(blocks, axis):
    n = len(blocks)
    return [blocks[0]] + [
        resident(lax.ppermute(blocks[j], axis, [(i, i ^ j) for i in range(n)])) for j in range(1, n)
    ]


def local(n, d, query_in, key_in, value_in, grad_out, filters, skip_gain):
    fwd, back = (resident(jnp.asarray(t)) for t in tables(filters.shape[1]))
    filters = resident(filters)
    gain = skip_gain[None, :]
    me = jnp.stack([lax.axis_index("ctx"), lax.axis_index("dp")]).astype(jnp.int32)

    arrays = [in_hbm(x[0]) for x in (key_in, value_in, query_in, grad_out)]
    (key, value, query, grad), got = products(n, me, *arrays)
    got = exchange(got, "ctx")
    spec = filter_spectra(filters, fwd)
    mixed, keep, send = conv(n, d, me, got, spec, fwd, back)
    grad_filter = sum_grads(d, keep, send)
    mixed = exchange(mixed, "ctx")
    early = 3 * n // 4
    outs = gate(range(early), me, query, grad, value, key, gain, mixed, [])
    outs = gate(range(early, n), me, query, grad, value, key, gain, mixed, outs)
    return *(x[None] for x in outs), grad_filter


def solution(mesh):
    rows = P("dp", "ctx", None)
    return jax.shard_map(
        functools.partial(local, mesh.shape["ctx"], mesh.shape["dp"]),
        mesh=mesh,
        in_specs=(rows, rows, rows, rows, P("ctx", None), P()),
        out_specs=(rows, rows, rows, rows, P("ctx", "dp")),
        check_vma=False,
    )
```

time: 84.7 us -> 76.7 us (0.906)
  starting transfers between devices: 40.2 us -> 21.9 us
  waiting for transfers between devices: 19.8 us -> 31.1 us
  Pallas kernels: 23.6 us -> 22.3 us
    ppermute x34 -> x14, starting transfers between devices: 40.2 us -> 17.2 us  [exchange(): lax.ppermute(blocks[j], axis, [(i, i ^ j) for i in range(n)])]
    ppermute x34 -> x14, waiting for transfers between devices: 19.8 us -> 30.4 us  [exchange(): lax.ppermute(blocks[j], axis, [(i, i ^ j) for i in range(n)])]
    ppermute x0 -> x2, starting transfers between devices: none -> 4.71 us  [sum_grads(): got = resident(lax.ppermute(send, 'dp', [(i, i ^ bit) for i in range(d)]))]
    pallas_call x2 -> x1, Pallas kernels: 10.6 us -> 10 us  [conv(): pl.pallas_call(functools.partial(conv_kernel, n, d), in_specs=[SMEM] + [V...]
    pallas_call x4 -> x5, Pallas kernels: 9.37 us -> 9.13 us  [the longest x2 4.63 us: gate(): pl.pallas_call(functools.partial(gate_kernel, js), in_specs=[SMEM] + [VME...]
  transfers between devices with their start and end apart: 34 -> 16, of which waited for: 12 -> 5; matrix products, arithmetic and copies ran while one was open for 0% -> 0% of each run, Pallas kernels for 21% -> 11%
where the time goes in v6:
time: 76.7 us; the launch traced here: 76.3 us
  waiting for transfers between devices  31.1 us (41%)
  Pallas kernels  22.3 us (29%)
  starting transfers between devices  21.9 us (29%)
  between operations  0.78 us (1%)
    ppermute x14, waiting for transfers between devices, exchange(): lax.ppermute(blocks[j], axis, [(i, i ^ j) for i in range(n)])  30.4 us
    ppermute x14, starting transfers between devices, exchange(): lax.ppermute(blocks[j], axis, [(i, i ^ j) for i in range(n)])  17.2 us
    pallas_call x1, Pallas kernels, conv(): pl.pallas_call(functools.partial(conv_kernel, n, d), in_specs=[SMEM] + [V...  10 us
    ppermute x2, starting transfers between devices, sum_grads(): got = resident(lax.ppermute(send, 'dp', [(i, i ^ bit) for i in range(d)]))  4.71 us
    pallas_call x2, Pallas kernels, gate(): pl.pallas_call(functools.partial(gate_kernel, js), in_specs=[SMEM] + [VME...  4.63 us
    pallas_call x1, Pallas kernels, filter_spectra(): pl.pallas_call(filter_kernel, in_specs=[VMEM, VMEM], out_specs=VMEM, out_...  3.41 us
    pallas_call x1, Pallas kernels, products(): pl.pallas_call(functools.partial(product_kernel, n), in_specs=[SMEM] + [H...  3.18 us
  transfers between devices with their start and end apart: 16, of which 5 were waited for; matrix products, arithmetic and copies ran while one was open for 0% of the time, Pallas kernels for 11%

profile of v6, /device:TPU:0, one launch (start us, length us, event | category | flops | bytes accessed | tf_op | source)
XLA Modules:
  0.0 76.3 jit_solution(6008585530922594966)
XLA Ops:
  0.6 0.0 copy-start
  0.7 0.1 pad_add_fusion.me
  0.7 3.2 %products.1 = (bf16[128,4096]{1,0:T(8,128)(2,1)S(1)}, bf16[128,4096]{1,0:T(8,128)(2,1)S(1)}, bf16[128,4096]{1,0:T(8,128)(2,1)S(1)}, bf16[128,4096]{1,0:T(8,128)(...) custom-call(s32[2]{0:T(128)S(1)} %pad_add_fusion.me, ...), custom_call_target="tpu_custom_call" | custom-call | tf_op jit(solution)/shard_map/products/pallas_call | solution.py:122
  3.9 0.0 copy-start.2
  3.9 0.5 collective-permute-start
  4.5 2.6 %collective-permute-start.1 = (bf16[2,128,512]{2,1,0:T(8,128)(2,1)S(1)}, bf16[2,128,512]{2,1,0:T(8,128)(2,1)S(1)}, u32[]{:S(2)}, u32[]{:S(2)}) collective-permute-start(bf16[2,128,512]{2,1,0:T(8,128)(2,1)S(1)} %get-tuple-element.43), channel_id=1, source_target_pairs={{0,2},{1,3},{2,0},{3,1},{4,6},{5,7},{6,4},{7,5},{8,10},{9,11},{10,... | collective-permute-start | bytes 786440 | tf_op jit(solution)/shard_map/ppermute | solution.py:367
  7.0 0.1 collective-permute-start.2
  7.1 1.8 %collective-permute-start.3 = (bf16[2,128,512]{2,1,0:T(8,128)(2,1)S(1)}, bf16[2,128,512]{2,1,0:T(8,128)(2,1)S(1)}, u32[]{:S(2)}, u32[]{:S(2)}) collective-permute-start(bf16[2,128,512]{2,1,0:T(8,128)(2,1)S(1)} %get-tuple-element.45), channel_id=1, source_target_pairs={{0,4},{1,5},{2,6},{3,7},{4,0},{5,1},{6,2},{7,3},{8,12},{9,13},{10,... | collective-permute-start | bytes 786440 | tf_op jit(solution)/shard_map/ppermute | solution.py:367
  8.9 2.6 %collective-permute-start.5 = (bf16[2,128,512]{2,1,0:T(8,128)(2,1)S(1)}, bf16[2,128,512]{2,1,0:T(8,128)(2,1)S(1)}, u32[]{:S(2)}, u32[]{:S(2)}) collective-permute-start(bf16[2,128,512]{2,1,0:T(8,128)(2,1)S(1)} %get-tuple-element.47), channel_id=1, source_target_pairs={{0,6},{1,7},{2,4},{3,5},{4,2},{5,3},{6,0},{7,1},{8,14},{9,15},{10,... | collective-permute-start | bytes 786440 | tf_op jit(solution)/shard_map/ppermute | solution.py:367
  11.5 2.7 %collective-permute-done.1.refs_2_ = bf16[2,128,512]{2,1,0:T(8,128)(2,1)S(1)} collective-permute-done((bf16[2,128,512]{2,1,0:T(8,128)(2,1)S(1)}, bf16[2,128,512]{2,1,0:T(8,128)(2,1)S(1)}, u32[]{:S(2)}, u32[]{:S(2)}) %collective-permute-start.1) | collective-permute-done | bytes 262176 | tf_op jit(solution)/shard_map/ppermute | solution.py:367
  14.2 1.7 %collective-permute-start.6 = (bf16[2,128,512]{2,1,0:T(8,128)(2,1)S(1)}, bf16[2,128,512]{2,1,0:T(8,128)(2,1)S(1)}, u32[]{:S(2)}, u32[]{:S(2)}) collective-permute-start(bf16[2,128,512]{2,1,0:T(8,128)(2,1)S(1)} %get-tuple-element.48), channel_id=1, source_target_pairs={{0,7},{1,6},{2,5},{3,4},{4,3},{5,2},{6,1},{7,0},{8,15},{9,14},{10,... | collective-permute-start | bytes 786440 | tf_op jit(solution)/shard_map/ppermute | solution.py:367
  15.9 3.4 %filter_spectra.1.refs_8_ = f32[2,8,256,256]{3,2,1,0:T(8,128)S(1)} custom-call(f32[512,1024]{1,0:T(8,128)S(1)} %copy-done.1, bf16[8,256,256]{2,1,0:T(8,128)(2,1)S(1)} %copy-done), custom_call_target="tpu_custom_call" | custom-call | tf_op jit(solution)/shard_map/filter_spectra/pallas_call | solution.py:167
  19.3 0.0 collective-permute-done.2.refs_3_
  19.3 12.4 %collective-permute-done.4.refs_5_ = bf16[2,128,512]{2,1,0:T(8,128)(2,1)S(1)} collective-permute-done((bf16[2,128,512]{2,1,0:T(8,128)(2,1)S(1)}, bf16[2,128,512]{2,1,0:T(8,128)(2,1)S(1)}, u32[]{:S(2)}, u32[]{:S(2)}) %collective-permute-start.4) | collective-permute-done | bytes 262176 | tf_op jit(solution)/shard_map/ppermute | solution.py:367
  31.8 0.0 copy-start.3
  31.8 10.0 %conv.1 = (bf16[2,128,512]{2,1,0:T(8,128)(2,1)S(1)}, bf16[2,128,512]{2,1,0:T(8,128)(2,1)S(1)}, bf16[2,128,512]{2,1,0:T(8,128)(2,1)S(1)}, bf16[2,128,512]{2,1,0:T...) custom-call(s32[2]{0:T(128)S(1)} %pad_add_fusion.me, ...), custom_call_target="tpu_custom_call" | custom-call | tf_op jit(solution)/shard_map/conv/pallas_call | solution.py:271
  41.8 2.1 %collective-permute-start.14 = (bf16[2,256,512]{2,1,0:T(8,128)(2,1)S(1)}, bf16[2,256,512]{2,1,0:T(8,128)(2,1)S(1)}, u32[]{:S(2)}, u32[]{:S(2)}) collective-permute-start(bf16[2,256,512]{2,1,0:T(8,128)(2,1)S(1)} %get-tuple-element.66), channel_id=1, source_target_pairs={{0,8},{8,0},{16,24},{24,16},{1,9},{9,1},{17,25},{25,17},{2,10},{10... | collective-permute-start | bytes 1572872 | tf_op jit(solution)/shard_map/ppermute | solution.py:341
  43.9 0.1 collective-permute-start.9
  44.0 1.5 %collective-permute-start.10 = (bf16[2,128,512]{2,1,0:T(8,128)(2,1)S(1)}, bf16[2,128,512]{2,1,0:T(8,128)(2,1)S(1)}, u32[]{:S(2)}, u32[]{:S(2)}) collective-permute-start(bf16[2,128,512]{2,1,0:T(8,128)(2,1)S(1)} %get-tuple-element.53), channel_id=1, source_target_pairs={{0,2},{1,3},{2,0},{3,1},{4,6},{5,7},{6,4},{7,5},{8,10},{9,11},{10,... | collective-permute-start | bytes 786440 | tf_op jit(solution)/shard_map/ppermute | solution.py:367
  45.5 0.3 collective-permute-start.11
  45.8 1.5 %collective-permute-start.12 = (bf16[2,128,512]{2,1,0:T(8,128)(2,1)S(1)}, bf16[2,128,512]{2,1,0:T(8,128)(2,1)S(1)}, u32[]{:S(2)}, u32[]{:S(2)}) collective-permute-start(bf16[2,128,512]{2,1,0:T(8,128)(2,1)S(1)} %get-tuple-element.55), channel_id=1, source_target_pairs={{0,4},{1,5},{2,6},{3,7},{4,0},{5,1},{6,2},{7,3},{8,12},{9,13},{10,... | collective-permute-start | bytes 786440 | tf_op jit(solution)/shard_map/ppermute | solution.py:367
  47.3 0.2 collective-permute-start.13
  47.5 5.6 %collective-permute-done.10.refs_2_ = bf16[2,128,512]{2,1,0:T(8,128)(2,1)S(1)} collective-permute-done((bf16[2,128,512]{2,1,0:T(8,128)(2,1)S(1)}, bf16[2,128,512]{2,1,0:T(8,128)(2,1)S(1)}, u32[]{:S(2)}, u32[]{:S(2)}) %collective-permute-start.10) | collective-permute-done | bytes 262176 | tf_op jit(solution)/shard_map/ppermute | solution.py:367
  53.1 2.5 %collective-permute-start.7 = (bf16[2,128,512]{2,1,0:T(8,128)(2,1)S(1)}, bf16[2,128,512]{2,1,0:T(8,128)(2,1)S(1)}, u32[]{:S(2)}, u32[]{:S(2)}) collective-permute-start(bf16[2,128,512]{2,1,0:T(8,128)(2,1)S(1)} %get-tuple-element.49), channel_id=1, source_target_pairs={{0,6},{1,7},{2,4},{3,5},{4,2},{5,3},{6,0},{7,1},{8,14},{9,15},{10,... | collective-permute-start | bytes 786440 | tf_op jit(solution)/shard_map/ppermute | solution.py:367
  55.6 0.7 collective-permute-done.14.got
  56.3 1.9 %collective-permute-start.8 = (bf16[2,128,512]{2,1,0:T(8,128)(2,1)S(1)}, bf16[2,128,512]{2,1,0:T(8,128)(2,1)S(1)}, u32[]{:S(2)}, u32[]{:S(2)}) collective-permute-start(bf16[2,128,512]{2,1,0:T(8,128)(2,1)S(1)} %get-tuple-element.50), channel_id=1, source_target_pairs={{0,7},{1,6},{2,5},{3,4},{4,3},{5,2},{6,1},{7,0},{8,15},{9,14},{10,... | collective-permute-start | bytes 786440 | tf_op jit(solution)/shard_map/ppermute | solution.py:367
  58.2 0.1 add_grads.1
  58.3 2.7 %collective-permute-start.15 = (bf16[1,256,512]{2,1,0:T(8,128)(2,1)S(1)}, bf16[1,256,512]{2,1,0:T(8,128)(2,1)S(1)}, u32[]{:S(2)}, u32[]{:S(2)}) collective-permute-start(bf16[1,256,512]{2,1,0:T(8,128)(2,1)S(1)} %get-tuple-element.68), channel_id=1, source_target_pairs={{0,16},{8,24},{16,0},{24,8},{1,17},{9,25},{17,1},{25,9},{2,18},{10... | collective-permute-start | bytes 786440 | tf_op jit(solution)/shard_map/ppermute | solution.py:341
  61.0 9.6 %collective-permute-done.13.refs_5_ = bf16[2,128,512]{2,1,0:T(8,128)(2,1)S(1)} collective-permute-done((bf16[2,128,512]{2,1,0:T(8,128)(2,1)S(1)}, bf16[2,128,512]{2,1,0:T(8,128)(2,1)S(1)}, u32[]{:S(2)}, u32[]{:S(2)}) %collective-permute-start.13) | collective-permute-done | bytes 262176 | tf_op jit(solution)/shard_map/ppermute | solution.py:367
  70.6 2.8 %gate.2 = (bf16[128,4096]{1,0:T(8,128)(2,1)}, bf16[128,4096]{1,0:T(8,128)(2,1)}, bf16[128,4096]{1,0:T(8,128)(2,1)}, bf16[128,4096]{1,0:T(8,128)(2,1)}) custom-call(s32[2]{0:T(128)S(1)} %pad_add_fusion.me, bf16[128,4096]{1,0:T(8,128)(2,1)S(1)} %get-tuple-element.37.query, bf16[128,4096]{1,0:T(8,128)(2,1)S(1)} %get-tuple-element.38.grad, ...), custom_call_target="tpu_custom_call" | custom-call | tf_op jit(solution)/shard_map/gate/pallas_call | solution.py:312
  73.4 1.8 %gate.3 = (bf16[128,4096]{1,0:T(8,128)(2,1)}, bf16[128,4096]{1,0:T(8,128)(2,1)}, bf16[128,4096]{1,0:T(8,128)(2,1)}, bf16[128,4096]{1,0:T(8,128)(2,1)}) custom-call(s32[2]{0:T(128)S(1)} %pad_add_fusion.me, bf16[128,4096]{1,0:T(8,128)(2,1)S(1)} %get-tuple-element.37.query, ...), custom_call_target="tpu_custom_call", output_to_operand_aliasing={{0}: (8, {}), {1}: (9, {}), {2}: (10, {}), {3}: (11, {})} | custom-call | tf_op jit(solution)/shard_map/gate/pallas_call | solution.py:312
  75.3 1.0 %turn_grads.1 = f32[512,256]{1,0:T(8,128)} custom-call(f32[1,256,512]{2,1,0:T(8,128)S(1)} %get-tuple-element.67.keep, bf16[1,256,512]{2,1,0:T(8,128)(2,1)S(1)} %collective-permute-done.15.got), custom_call_target="tpu_custom_call" | custom-call | tf_op jit(solution)/shard_map/turn_grads/pallas_call | solution.py:354
  (16 shorter events, 0.0 us)
Async XLA Ops:
  0.6 15.3 %copy-start = (bf16[8,256,256]{2,1,0:T(8,128)(2,1)S(1)}, bf16[8,256,256]{2,1,0:T(8,128)(2,1)}, u32[]{:S(2)}) copy-start(bf16[8,256,256]{2,1,0:T(8,128)(2,1)} %constant.12.clone.fwd.refs_9_) | copy-start | bytes 3145732
  0.6 15.3 %copy-start.1 = (f32[512,1024]{1,0:T(8,128)S(1)}, f32[512,1024]{1,0:T(8,128)}, u32[]{:S(2)}) copy-start(f32[512,1024]{1,0:T(8,128)} %filt.1) | copy-start | bytes 6291460
  3.9 27.9 %copy-start.2 = (bf16[8,256,256]{2,1,0:T(8,128)(2,1)S(1)}, bf16[8,256,256]{2,1,0:T(8,128)(2,1)}, u32[]{:S(2)}) copy-start(bf16[8,256,256]{2,1,0:T(8,128)(2,1)} %constant.13.clone.refs_10_) | copy-start | bytes 3145732
  3.9 4.9 %collective-permute-start = (bf16[2,128,512]{2,1,0:T(8,128)(2,1)S(1)}, bf16[2,128,512]{2,1,0:T(8,128)(2,1)S(1)}, u32[]{:S(2)}, u32[]{:S(2)}) collective-permute-start(bf16[2,128,512]{2,1,0:T(8,128)(2,1)S(1)} %get-tuple-element.42), channel_id=1, source_target_pairs={{0,1},{1,0},{2,3},{3,2},{4,5},{5,4},{6,7},{7,6},{8,9},{9,8},{10,11... | collective-permute-start | bytes 786440 | tf_op jit(solution)/shard_map/ppermute | solution.py:367
  4.5 9.7 %collective-permute-start.1 = (bf16[2,128,512]{2,1,0:T(8,128)(2,1)S(1)}, bf16[2,128,512]{2,1,0:T(8,128)(2,1)S(1)}, u32[]{:S(2)}, u32[]{:S(2)}) collective-permute-start(bf16[2,128,512]{2,1,0:T(8,128)(2,1)S(1)} %get-tuple-element.43), channel_id=1, source_target_pairs={{0,2},{1,3},{2,0},{3,1},{4,6},{5,7},{6,4},{7,5},{8,10},{9,11},{10,... | collective-permute-start | bytes 786440 | tf_op jit(solution)/shard_map/ppermute | solution.py:367
  7.0 12.3 %collective-permute-start.2 = (bf16[2,128,512]{2,1,0:T(8,128)(2,1)S(1)}, bf16[2,128,512]{2,1,0:T(8,128)(2,1)S(1)}, u32[]{:S(2)}, u32[]{:S(2)}) collective-permute-start(bf16[2,128,512]{2,1,0:T(8,128)(2,1)S(1)} %get-tuple-element.44), channel_id=1, source_target_pairs={{0,3},{1,2},{2,1},{3,0},{4,7},{5,6},{6,5},{7,4},{8,11},{9,10},{10,... | collective-permute-start | bytes 786440 | tf_op jit(solution)/shard_map/ppermute | solution.py:367
  7.1 12.2 %collective-permute-start.3 = (bf16[2,128,512]{2,1,0:T(8,128)(2,1)S(1)}, bf16[2,128,512]{2,1,0:T(8,128)(2,1)S(1)}, u32[]{:S(2)}, u32[]{:S(2)}) collective-permute-start(bf16[2,128,512]{2,1,0:T(8,128)(2,1)S(1)} %get-tuple-element.45), channel_id=1, source_target_pairs={{0,4},{1,5},{2,6},{3,7},{4,0},{5,1},{6,2},{7,3},{8,12},{9,13},{10,... | collective-permute-start | bytes 786440 | tf_op jit(solution)/shard_map/ppermute | solution.py:367
  8.9 22.9 %collective-permute-start.4 = (bf16[2,128,512]{2,1,0:T(8,128)(2,1)S(1)}, bf16[2,128,512]{2,1,0:T(8,128)(2,1)S(1)}, u32[]{:S(2)}, u32[]{:S(2)}) collective-permute-start(bf16[2,128,512]{2,1,0:T(8,128)(2,1)S(1)} %get-tuple-element.46), channel_id=1, source_target_pairs={{0,5},{1,4},{2,7},{3,6},{4,1},{5,0},{6,3},{7,2},{8,13},{9,12},{10,... | collective-permute-start | bytes 786440 | tf_op jit(solution)/shard_map/ppermute | solution.py:367
  8.9 22.9 %collective-permute-start.5 = (bf16[2,128,512]{2,1,0:T(8,128)(2,1)S(1)}, bf16[2,128,512]{2,1,0:T(8,128)(2,1)S(1)}, u32[]{:S(2)}, u32[]{:S(2)}) collective-permute-start(bf16[2,128,512]{2,1,0:T(8,128)(2,1)S(1)} %get-tuple-element.47), channel_id=1, source_target_pairs={{0,6},{1,7},{2,4},{3,5},{4,2},{5,3},{6,0},{7,1},{8,14},{9,15},{10,... | collective-permute-start | bytes 786440 | tf_op jit(solution)/shard_map/ppermute | solution.py:367
  14.2 17.6 %collective-permute-start.6 = (bf16[2,128,512]{2,1,0:T(8,128)(2,1)S(1)}, bf16[2,128,512]{2,1,0:T(8,128)(2,1)S(1)}, u32[]{:S(2)}, u32[]{:S(2)}) collective-permute-start(bf16[2,128,512]{2,1,0:T(8,128)(2,1)S(1)} %get-tuple-element.48), channel_id=1, source_target_pairs={{0,7},{1,6},{2,5},{3,4},{4,3},{5,2},{6,1},{7,0},{8,15},{9,14},{10,... | collective-permute-start | bytes 786440 | tf_op jit(solution)/shard_map/ppermute | solution.py:367
  31.8 38.8 %copy-start.3 = (f32[4096]{0:T(1024)S(1)}, f32[4096]{0:T(1024)}, u32[]{:S(2)}) copy-start(f32[4096]{0:T(1024)} %param.13) | copy-start | bytes 49156
  41.8 14.5 %collective-permute-start.14 = (bf16[2,256,512]{2,1,0:T(8,128)(2,1)S(1)}, bf16[2,256,512]{2,1,0:T(8,128)(2,1)S(1)}, u32[]{:S(2)}, u32[]{:S(2)}) collective-permute-start(bf16[2,256,512]{2,1,0:T(8,128)(2,1)S(1)} %get-tuple-element.66), channel_id=1, source_target_pairs={{0,8},{8,0},{16,24},{24,16},{1,9},{9,1},{17,25},{25,17},{2,10},{10... | collective-permute-start | bytes 1572872 | tf_op jit(solution)/shard_map/ppermute | solution.py:341
  43.9 3.4 %collective-permute-start.9 = (bf16[2,128,512]{2,1,0:T(8,128)(2,1)S(1)}, bf16[2,128,512]{2,1,0:T(8,128)(2,1)S(1)}, u32[]{:S(2)}, u32[]{:S(2)}) collective-permute-start(bf16[2,128,512]{2,1,0:T(8,128)(2,1)S(1)} %get-tuple-element.52), channel_id=1, source_target_pairs={{0,1},{1,0},{2,3},{3,2},{4,5},{5,4},{6,7},{7,6},{8,9},{9,8},{10,11... | collective-permute-start | bytes 786440 | tf_op jit(solution)/shard_map/ppermute | solution.py:367
  44.0 9.1 %collective-permute-start.10 = (bf16[2,128,512]{2,1,0:T(8,128)(2,1)S(1)}, bf16[2,128,512]{2,1,0:T(8,128)(2,1)S(1)}, u32[]{:S(2)}, u32[]{:S(2)}) collective-permute-start(bf16[2,128,512]{2,1,0:T(8,128)(2,1)S(1)} %get-tuple-element.53), channel_id=1, source_target_pairs={{0,2},{1,3},{2,0},{3,1},{4,6},{5,7},{6,4},{7,5},{8,10},{9,11},{10,... | collective-permute-start | bytes 786440 | tf_op jit(solution)/shard_map/ppermute | solution.py:367
  45.5 12.9 %collective-permute-start.11 = (bf16[2,128,512]{2,1,0:T(8,128)(2,1)S(1)}, bf16[2,128,512]{2,1,0:T(8,128)(2,1)S(1)}, u32[]{:S(2)}, u32[]{:S(2)}) collective-permute-start(bf16[2,128,512]{2,1,0:T(8,128)(2,1)S(1)} %get-tuple-element.54), channel_id=1, source_target_pairs={{0,3},{1,2},{2,1},{3,0},{4,7},{5,6},{6,5},{7,4},{8,11},{9,10},{10,... | collective-permute-start | bytes 786440 | tf_op jit(solution)/shard_map/ppermute | solution.py:367
  45.8 15.2 %collective-permute-start.12 = (bf16[2,128,512]{2,1,0:T(8,128)(2,1)S(1)}, bf16[2,128,512]{2,1,0:T(8,128)(2,1)S(1)}, u32[]{:S(2)}, u32[]{:S(2)}) collective-permute-start(bf16[2,128,512]{2,1,0:T(8,128)(2,1)S(1)} %get-tuple-element.55), channel_id=1, source_target_pairs={{0,4},{1,5},{2,6},{3,7},{4,0},{5,1},{6,2},{7,3},{8,12},{9,13},{10,... | collective-permute-start | bytes 786440 | tf_op jit(solution)/shard_map/ppermute | solution.py:367
  47.3 23.3 %collective-permute-start.13 = (bf16[2,128,512]{2,1,0:T(8,128)(2,1)S(1)}, bf16[2,128,512]{2,1,0:T(8,128)(2,1)S(1)}, u32[]{:S(2)}, u32[]{:S(2)}) collective-permute-start(bf16[2,128,512]{2,1,0:T(8,128)(2,1)S(1)} %get-tuple-element.56), channel_id=1, source_target_pairs={{0,5},{1,4},{2,7},{3,6},{4,1},{5,0},{6,3},{7,2},{8,13},{9,12},{10,... | collective-permute-start | bytes 786440 | tf_op jit(solution)/shard_map/ppermute | solution.py:367
  53.1 20.3 %collective-permute-start.7 = (bf16[2,128,512]{2,1,0:T(8,128)(2,1)S(1)}, bf16[2,128,512]{2,1,0:T(8,128)(2,1)S(1)}, u32[]{:S(2)}, u32[]{:S(2)}) collective-permute-start(bf16[2,128,512]{2,1,0:T(8,128)(2,1)S(1)} %get-tuple-element.49), channel_id=1, source_target_pairs={{0,6},{1,7},{2,4},{3,5},{4,2},{5,3},{6,0},{7,1},{8,14},{9,15},{10,... | collective-permute-start | bytes 786440 | tf_op jit(solution)/shard_map/ppermute | solution.py:367
  56.3 17.1 %collective-permute-start.8 = (bf16[2,128,512]{2,1,0:T(8,128)(2,1)S(1)}, bf16[2,128,512]{2,1,0:T(8,128)(2,1)S(1)}, u32[]{:S(2)}, u32[]{:S(2)}) collective-permute-start(bf16[2,128,512]{2,1,0:T(8,128)(2,1)S(1)} %get-tuple-element.50), channel_id=1, source_target_pairs={{0,7},{1,6},{2,5},{3,4},{4,3},{5,2},{6,1},{7,0},{8,15},{9,14},{10,... | collective-permute-start | bytes 786440 | tf_op jit(solution)/shard_map/ppermute | solution.py:367
  58.3 16.9 %collective-permute-start.15 = (bf16[1,256,512]{2,1,0:T(8,128)(2,1)S(1)}, bf16[1,256,512]{2,1,0:T(8,128)(2,1)S(1)}, u32[]{:S(2)}, u32[]{:S(2)}) collective-permute-start(bf16[1,256,512]{2,1,0:T(8,128)(2,1)S(1)} %get-tuple-element.68), channel_id=1, source_target_pairs={{0,16},{8,24},{16,0},{24,8},{1,17},{9,25},{17,1},{25,9},{2,18},{10... | collective-permute-start | bytes 786440 | tf_op jit(solution)/shard_map/ppermute | solution.py:341

commit v7 on v6

v7 whole, which is shorter than its diff:
```python
import functools
import math

import jax
import jax.numpy as jnp
import ml_dtypes
import numpy as np
from jax import lax
from jax.experimental import pallas as pl
from jax.experimental.pallas import tpu as pltpu
from jax.sharding import PartitionSpec as P

F32 = jnp.float32
BF16 = jnp.bfloat16
CLASSES = 8
HALVES = 2
STEPS = 4
PARAMS = pltpu.CompilerParams(vmem_limit_bytes=16 * 1024 * 1024)
CONV_PARAMS = pltpu.CompilerParams(vmem_limit_bytes=34 * 1024 * 1024)
SMEM = pl.BlockSpec(memory_space=pltpu.SMEM)
VMEM = pl.BlockSpec(memory_space=pltpu.VMEM)
HBM = pl.BlockSpec(memory_space=pltpu.HBM)


def tables(length):
    m2 = length // CLASSES
    c = np.arange(CLASSES)[:, None, None]
    j = np.arange(m2)[None, :, None]
    m = np.arange(m2)[None, None, :]
    turn = ((CLASSES * m + c) * (2 * j + 1)) % (4 * length)
    angle = 2 * np.pi * turn / (4 * length)
    forward = np.concatenate([np.cos(angle), -np.sin(angle)], 1)
    back = np.swapaxes(forward, 1, 2) / length

    def parts(x):
        hi = x.astype(ml_dtypes.bfloat16)
        return hi, (x - hi.astype(np.float64)).astype(ml_dtypes.bfloat16)

    return np.concatenate(parts(forward), 2), back.astype(ml_dtypes.bfloat16)


def parts(x):
    hi = x.astype(BF16)
    return hi, (x - hi.astype(F32)).astype(BF16)


def dot(a, b):
    return jnp.dot(a, b, preferred_element_type=F32)


def dft(z, sign):
    n = len(z)
    if n == 1:
        return z
    even, odd = dft(z[0::2], sign), dft(z[1::2], sign)
    low, high = [], []
    for k in range(n // 2):
        (er, ei), (zr, zi) = even[k], odd[k]
        if k == 0:
            tr, ti = zr, zi
        elif 4 * k == n:
            tr, ti = (-zi, zr) if sign > 0 else (zi, -zr)
        else:
            c, s = math.cos(2 * math.pi * k / n), sign * math.sin(2 * math.pi * k / n)
            if 8 * k == n:
                tr, ti = (c * (zr - zi), c * (zi + zr)) if sign > 0 else (c * (zr + zi), c * (zi - zr))
            elif 8 * k == 3 * n:
                tr, ti = (c * (zr + zi), c * (zi - zr)) if sign > 0 else (c * (zr - zi), c * (zi + zr))
            else:
                tr, ti = c * zr - s * zi, c * zi + s * zr
        low.append((er + tr, ei + ti))
        high.append((er - tr, ei - ti))
    return low + high


def times(x, f, conj):
    (xr, xi), (fr, fi) = x, f
    if conj:
        return xr * fr + xi * fi, xi * fr - xr * fi
    return xr * fr - xi * fi, xr * fi + xi * fr


def resident(x):
    return pltpu.with_memory_space_constraint(x, pltpu.VMEM)


def in_hbm(x):
    return pltpu.with_memory_space_constraint(x, pltpu.HBM)


def peer_columns(me, j, width):
    return pl.ds(pl.multiple_of((me[0] ^ j) * width, 128), width)


def product_kernel(n, me, key, value, query, grad, *refs):
    bufs, outs, sems = refs[:4], refs[4:-1], refs[-1]
    _, rows, width = outs[0].shape
    width *= HALVES
    step = rows // STEPS
    copies = []
    for i in range(STEPS):
        at = pl.ds(i * step, step)
        copies.append(
            [
                pltpu.make_async_copy(src.at[at], dst.at[at], sems.at[a, i])
                for a, (src, dst) in enumerate(zip((key, value, query, grad), bufs))
            ]
        )
        for copy in copies[i]:
            copy.start()
    for s in range(STEPS):
        at = pl.ds(s * step, step)
        for a, (left, right) in enumerate((bufs[:2], bufs[2:])):
            copies[s][2 * a].wait()
            copies[s][2 * a + 1].wait()
            for i, j in enumerate(peers(n)):
                cols = peer_columns(me, j, width)
                value = (left[at, cols].astype(F32) * right[at, cols].astype(F32)).astype(BF16)
                for half in range(HALVES):
                    outs[half * n + i][a, at] = value[:, half * width // HALVES :][:, : width // HALVES]


def products(n, me, key, value, query, grad):
    rows, total = key.shape
    width = total // n // HALVES
    out = pl.pallas_call(
        functools.partial(product_kernel, n),
        in_specs=[SMEM] + [HBM] * 4,
        out_specs=[VMEM] * (4 + HALVES * n),
        out_shape=[pltpu.VMEM(key.shape, BF16)] * 4
        + [pltpu.VMEM((2, rows, width), BF16)] * (HALVES * n),
        scratch_shapes=[pltpu.SemaphoreType.DMA((4, STEPS))],
        compiler_params=PARAMS,
        name="products",
    )(me, key, value, query, grad)
    return out[:4], [out[4 + h * n : 4 + (h + 1) * n] for h in range(HALVES)]


def lane_groups(width):
    return [slice(i, i + 128) for i in range(0, width, 128)]


def filter_kernel(filt, fwd, *refs):
    spec, x, u = refs[-3:]
    m2, width = x.shape[1] // CLASSES, u.shape[-1]
    groups = lane_groups(width)
    rows = m2 // CLASSES
    for half in range(HALVES):
        for g, lanes in enumerate(groups):
            x[g] = filt[half * width + lanes.start : half * width + lanes.stop, :].T
        for c in range(CLASSES):
            for g, lanes in enumerate(groups):
                hi, lo = parts(x[g, pl.ds(c, m2, stride=CLASSES), :])
                u[c, :, lanes] = dot(fwd[c], jnp.concatenate([hi, hi], 0)) + dot(fwd[c, :, :m2], lo)

        def step(i, carry):
            r = pl.multiple_of(i * rows, rows)
            re, im = pl.ds(r, rows), pl.ds(m2 + r, rows)
            for lanes in groups:
                z = dft([(u[c, re, lanes], u[c, im, lanes]) for c in range(CLASSES)], -1)
                for k in range(CLASSES):
                    spec[half, k, re, lanes], spec[half, k, im, lanes] = z[k]
            return carry

        lax.fori_loop(0, CLASSES, step, 0)


def filter_spectra(filters, fwd, after, then):
    chans, length = filters.shape
    width = chans // HALVES
    m2 = length // CLASSES
    out = pl.pallas_call(
        filter_kernel,
        in_specs=[VMEM] * (2 + len(after) + len(then)),
        out_specs=[VMEM] * (len(then) + 1),
        out_shape=[pltpu.VMEM(t.shape, t.dtype) for t in then]
        + [pltpu.VMEM((HALVES, CLASSES, 2 * m2, width), F32)],
        scratch_shapes=[
            pltpu.VMEM((width // 128, length, 128), F32),
            pltpu.VMEM((CLASSES, 2 * m2, width), F32),
        ],
        input_output_aliases={2 + len(after) + i: i for i in range(len(then))},
        compiler_params=PARAMS,
        name="filter_spectra",
    )(filters, fwd, *after, *then)
    return out[-1], out[:-1]


def conv_kernel(n, d, half, me, *refs):
    got, (filt, fwd, back) = refs[:n], refs[n : n + 3]
    refs = refs[-(n + 2 + 6) :]
    out, (keep, send), (nat, x, u, y, turned, grad) = refs[:n], refs[n : n + 2], refs[n + 2 :]
    _, rows, width = got[0].shape
    m2 = x.shape[2]
    per = keep.shape[1] // CLASSES
    groups = lane_groups(width)
    step_rows = m2 // CLASSES
    part_rows = rows // CLASSES
    chans = slice(half * width, (half + 1) * width)

    for a in range(2):
        for g, lanes in enumerate(groups):
            for i, j in enumerate(peers(n)):
                at = pl.multiple_of((me[0] ^ j) * rows, rows)
                nat[a, g, pl.ds(at, rows)] = got[i][a, :, lanes].astype(F32)
            for c in range(CLASSES):
                x[a, c, :, lanes] = nat[a, g, pl.ds(c, m2, stride=CLASSES), :].astype(BF16)
        for c in range(CLASSES):
            data = x[a, c]
            u[a, c] = dot(fwd[c], jnp.concatenate([data, data], 0))

    def middle(i, carry):
        r = pl.multiple_of(i * step_rows, step_rows)
        re, im = pl.ds(r, step_rows), pl.ds(m2 + r, step_rows)
        for lanes in groups:
            kv = dft([(u[0, c, re, lanes], u[0, c, im, lanes]) for c in range(CLASSES)], -1)
            wt = dft([(u[1, c, re, lanes], u[1, c, im, lanes]) for c in range(CLASSES)], -1)
            fs = [(filt[half, k, re, lanes], filt[half, k, im, lanes]) for k in range(CLASSES)]
            for o, (left, right, conj) in enumerate([(kv, fs, False), (wt, fs, True), (wt, kv, True)]):
                z = dft([times(s, t, conj) for s, t in zip(left, right)], 1)
                for c in range(CLASSES):
                    y[o, c, re, lanes] = z[c][0].astype(BF16)
                    y[o, c, im, lanes] = z[c][1].astype(BF16)
        return carry

    lax.fori_loop(0, CLASSES, middle, 0)

    for c in range(CLASSES):
        grad[c] = dot(back[c], y[2, c])
        for o in range(2):
            turned[o, c] = dot(back[c], y[o, c]).astype(BF16)
    for i, j in enumerate(peers(n)):
        at = pl.multiple_of((me[0] ^ j) * part_rows, part_rows)
        for o in range(2):
            for c in range(CLASSES):
                out[i][half, o, c * part_rows : (c + 1) * part_rows] = turned[o, c, pl.ds(at, part_rows)]
    for j in range(d):
        at = pl.multiple_of((me[1] ^ j) * per, per)
        for c in range(CLASSES):
            part = grad[c, pl.ds(at, per)]
            if j % 2:
                send[j // 2, c * per : (c + 1) * per, chans] = part.astype(BF16)
            else:
                keep[j // 2, c * per : (c + 1) * per, chans] = part


def conv(n, d, half, me, got, filt, fwd, back, before):
    _, rows, width = got[0].shape
    length = n * rows
    m2 = length // CLASSES
    out = pl.pallas_call(
        functools.partial(conv_kernel, n, d, half),
        in_specs=[SMEM] + [VMEM] * (n + 3 + len(before)),
        out_specs=[VMEM] * (n + 2),
        out_shape=[pltpu.VMEM((HALVES, 2, rows, width), BF16)] * n
        + [pltpu.VMEM((d // 2, length // d, HALVES * width), dtype) for dtype in (F32, BF16)],
        scratch_shapes=[
            pltpu.VMEM((2, width // 128, length, 128), F32),
            pltpu.VMEM((2, CLASSES, m2, width), BF16),
            pltpu.VMEM((2, CLASSES, 2 * m2, width), F32),
            pltpu.VMEM((3, CLASSES, 2 * m2, width), BF16),
            pltpu.VMEM((2, CLASSES, m2, width), BF16),
            pltpu.VMEM((CLASSES, m2, width), F32),
        ],
        input_output_aliases={n + 4 + i: i for i in range(len(before))},
        compiler_params=CONV_PARAMS,
        name="conv",
    )(me, *got, filt, fwd, back, *before)
    return out


def natural(scratch, piece):
    rows = piece.shape[0] // CLASSES
    for c in range(CLASSES):
        scratch[pl.ds(c, rows, stride=CLASSES), :] = piece[c * rows : (c + 1) * rows]
    return scratch[...]


def gate_kernel(js, me, query, grad, value, key, gain, *refs):
    got, outs, (sent, sems, nat) = refs[: len(js)], refs[-7:-3], refs[-3:]
    _, _, rows, width = got[0].shape
    copies = []
    for i, j in enumerate(js):
        block = peer_columns(me, j, HALVES * width)
        for half in range(HALVES):
            for g, lanes in enumerate(lane_groups(width)):
                at = half * width + lanes.start
                start = pl.multiple_of((me[0] ^ j) * HALVES * width + at, 128)
                cols = pl.ds(start, 128)
                to = slice(at, at + 128)
                scale = gain[:, cols]
                q, g_, v, k = (x[:, cols].astype(F32) for x in (query, grad, value, key))
                conv_out, corr_back = (
                    natural(nat.at[i, o, half, g], got[i][half, o, :, lanes].astype(F32)) for o in range(2)
                )
                mixing = conv_out + scale * (k * v).astype(BF16).astype(F32)
                sent[0, i, :, to] = (q * mixing).astype(BF16)
                sent[1, i, :, to] = (g_ * mixing).astype(BF16)
                total = corr_back + scale * (g_ * q).astype(BF16).astype(F32)
                sent[2, i, :, to] = (total * v).astype(BF16)
                sent[3, i, :, to] = (total * k).astype(BF16)
        for a in range(4):
            copy = pltpu.make_async_copy(sent.at[a, i], outs[a].at[:, block], sems.at[a, i])
            copy.start()
            copies.append(copy)
    for copy in copies:
        copy.wait()


def gate(js, me, query, grad, value, key, gain, got, outs):
    _, _, rows, width = got[0].shape
    return pl.pallas_call(
        functools.partial(gate_kernel, js),
        in_specs=[SMEM] + [VMEM] * (5 + len(js)) + [HBM] * len(outs),
        out_specs=[HBM] * 4,
        out_shape=[jax.ShapeDtypeStruct(query.shape, BF16)] * 4,
        scratch_shapes=[
            pltpu.VMEM((4, len(js), rows, HALVES * width), BF16),
            pltpu.SemaphoreType.DMA((4, len(js))),
            pltpu.VMEM((len(js), 2, HALVES, width // 128, rows, 128), F32),
        ],
        input_output_aliases={6 + len(js) + i: i for i in range(len(outs))},
        compiler_params=PARAMS,
        name="gate",
    )(me, query, grad, value, key, gain, *got, *outs)


def add_kernel(keep, got, new_keep, new_send):
    for i in range(new_keep.shape[0]):
        new_keep[i] = keep[2 * i] + got[2 * i].astype(F32)
        new_send[i] = (keep[2 * i + 1] + got[2 * i + 1].astype(F32)).astype(BF16)


def turn_kernel(keep, got, out, nat):
    for g, lanes in enumerate(lane_groups(keep.shape[2])):
        total = keep[0, :, lanes] + got[0, :, lanes].astype(F32)
        out[lanes, :] = natural(nat.at[g], total).T


def sum_grads(d, keep, send):
    _, per, chans = keep.shape
    bit = 1
    while True:
        got = resident(lax.ppermute(send, "dp", [(i, i ^ bit) for i in range(d)]))
        if keep.shape[0] == 1:
            break
        shape = (keep.shape[0] // 2, per, chans)
        keep, send = pl.pallas_call(
            add_kernel,
            in_specs=[VMEM] * 2,
            out_specs=[VMEM] * 2,
            out_shape=[pltpu.VMEM(shape, F32), pltpu.VMEM(shape, BF16)],
            compiler_params=PARAMS,
            name="add_grads",
        )(keep, got)
        bit *= 2
    return pl.pallas_call(
        turn_kernel,
        in_specs=[VMEM] * 2,
        out_specs=VMEM,
        out_shape=jax.ShapeDtypeStruct((chans, per), F32),
        scratch_shapes=[pltpu.VMEM((chans // 128, per, 128), F32)],
        compiler_params=PARAMS,
        name="turn_grads",
    )(keep, got)


def peers(n):
    return [0, *range(2, n, 2), *range(1, n, 2)]


def exchange(blocks, axis):
    n = len(blocks)
    got = [blocks[0]]
    for j, block in zip(peers(n)[1:], blocks[1:]):
        got.append(resident(lax.ppermute(block, axis, [(i, i ^ j) for i in range(n)])))
    return got


def local(n, d, query_in, key_in, value_in, grad_out, filters, skip_gain):
    fwd, back = (resident(jnp.asarray(t)) for t in tables(filters.shape[1]))
    filters = resident(filters)
    gain = skip_gain[None, :]
    me = jnp.stack([lax.axis_index("ctx"), lax.axis_index("dp")]).astype(jnp.int32)

    arrays = [in_hbm(x[0]) for x in (key_in, value_in, query_in, grad_out)]
    (key, value, query, grad), got = products(n, me, *arrays)
    first = exchange(got[0], "ctx")
    spec, second = filter_spectra(filters, fwd, [first[1]], got[1])
    second = exchange(second, "ctx")
    results = conv(n, d, 0, me, first, spec, fwd, back, [])
    *mixed, keep, send = conv(n, d, 1, me, second, spec, fwd, back, results)
    mixed = exchange(mixed, "ctx")
    grad_filter = sum_grads(d, keep, send)
    outs = []
    early = 3 * n // 4
    for at in (slice(early), slice(early, n)):
        outs = gate(peers(n)[at], me, query, grad, value, key, gain, mixed[at], outs)
    return *(x[None] for x in outs), grad_filter


def solution(mesh):
    rows = P("dp", "ctx", None)
    return jax.shard_map(
        functools.partial(local, mesh.shape["ctx"], mesh.shape["dp"]),
        mesh=mesh,
        in_specs=(rows, rows, rows, rows, P("ctx", None), P()),
        out_specs=(rows, rows, rows, rows, P("ctx", "dp")),
        check_vma=False,
    )
```

time: 76.7 us -> 72 us (0.939)
  waiting for transfers between devices: 31.1 us -> 18.8 us
  starting transfers between devices: 21.9 us -> 28.8 us
  Pallas kernels: 22.3 us -> 23.4 us
    ppermute x14 -> x21, waiting for transfers between devices: 30.4 us -> 18.8 us  [exchange(): lax.ppermute(block, axis, [(i, i ^ j) for i in range(n)])]
    ppermute x14 -> x21, starting transfers between devices: 17.2 us -> 24.4 us  [exchange(): lax.ppermute(block, axis, [(i, i ^ j) for i in range(n)])]
    pallas_call x2, Pallas kernels: 4.63 us -> 5.93 us  [gate(): pl.pallas_call(functools.partial(gate_kernel, js), in_specs=[SMEM] + [VME...]
    pallas_call x2 -> x3, Pallas kernels: 13.5 us -> 13.1 us  [the longest x2 9.54 us: conv(): pl.pallas_call(functools.partial(conv_kernel, n, d, half), in_specs=[SMEM...]
  transfers between devices with their start and end apart: 16 -> 23, of which waited for: 5 -> 8; matrix products, arithmetic and copies ran while one was open for 0% -> 0% of each run, Pallas kernels for 11% -> 20%
where the time goes in v7:
time: 72 us; the launch traced here: 71.9 us
  starting transfers between devices  28.8 us (40%)
  Pallas kernels  23.4 us (32%)
  waiting for transfers between devices  18.8 us (26%)
  between operations  0.78 us (1%)
    ppermute x21, starting transfers between devices, exchange(): lax.ppermute(block, axis, [(i, i ^ j) for i in range(n)])  24.4 us
    ppermute x21, waiting for transfers between devices, exchange(): lax.ppermute(block, axis, [(i, i ^ j) for i in range(n)])  18.8 us
    pallas_call x2, Pallas kernels, conv(): pl.pallas_call(functools.partial(conv_kernel, n, d, half), in_specs=[SMEM...  9.54 us
    pallas_call x2, Pallas kernels, gate(): pl.pallas_call(functools.partial(gate_kernel, js), in_specs=[SMEM] + [VME...  5.93 us
    ppermute x2, starting transfers between devices, sum_grads(): got = resident(lax.ppermute(send, 'dp', [(i, i ^ bit) for i in range(d)]))  4.32 us
    pallas_call x1, Pallas kernels, filter_spectra(): pl.pallas_call(filter_kernel, in_specs=[VMEM] * (2 + len(after) + len(the...  3.6 us
    pallas_call x1, Pallas kernels, products(): pl.pallas_call(functools.partial(product_kernel, n), in_specs=[SMEM] + [H...  3.19 us
  transfers between devices with their start and end apart: 23, of which 8 were waited for; matrix products, arithmetic and copies ran while one was open for 0% of the time, Pallas kernels for 20%

profile of v7, /device:TPU:0, one launch (start us, length us, event | category | flops | bytes accessed | tf_op | source)
XLA Modules:
  0.0 71.9 jit_solution(6347183474682652403)
XLA Ops:
  0.7 0.1 pad_add_fusion.me
  0.7 3.2 %products.1 = (bf16[128,4096]{1,0:T(8,128)(2,1)S(1)}, bf16[128,4096]{1,0:T(8,128)(2,1)S(1)}, bf16[128,4096]{1,0:T(8,128)(2,1)S(1)}, bf16[128,4096]{1,0:T(8,128)(...) custom-call(s32[2]{0:T(128)S(1)} %pad_add_fusion.me, ...), custom_call_target="tpu_custom_call" | custom-call | tf_op jit(solution)/shard_map/products/pallas_call | solution.py:126
  3.9 3.0 %collective-permute-start = (bf16[2,128,256]{2,1,0:T(8,128)(2,1)S(1)}, bf16[2,128,256]{2,1,0:T(8,128)(2,1)S(1)}, u32[]{:S(2)}, u32[]{:S(2)}) collective-permute-start(bf16[2,128,256]{2,1,0:T(8,128)(2,1)S(1)} %get-tuple-element.68), channel_id=1, source_target_pairs={{0,2},{1,3},{2,0},{3,1},{4,6},{5,7},{6,4},{7,5},{8,10},{9,11},{10,... | collective-permute-start | bytes 393224 | tf_op jit(solution)/shard_map/ppermute | solution.py:376
  6.9 1.5 %collective-permute-start.8 = (bf16[2,128,256]{2,1,0:T(8,128)(2,1)S(1)}, bf16[2,128,256]{2,1,0:T(8,128)(2,1)S(1)}, u32[]{:S(2)}, u32[]{:S(2)}) collective-permute-start(bf16[2,128,256]{2,1,0:T(8,128)(2,1)S(1)} %get-tuple-element.87), channel_id=1, source_target_pairs={{0,4},{1,5},{2,6},{3,7},{4,0},{5,1},{6,2},{7,3},{8,12},{9,13},{10,... | collective-permute-start | bytes 393224 | tf_op jit(solution)/shard_map/ppermute | solution.py:376
  8.5 2.1 %collective-permute-start.11 = (bf16[2,128,256]{2,1,0:T(8,128)(2,1)S(1)}, bf16[2,128,256]{2,1,0:T(8,128)(2,1)S(1)}, u32[]{:S(2)}, u32[]{:S(2)}) collective-permute-start(bf16[2,128,256]{2,1,0:T(8,128)(2,1)S(1)} %get-tuple-element.90), channel_id=1, source_target_pairs={{0,3},{1,2},{2,1},{3,0},{4,7},{5,6},{6,5},{7,4},{8,11},{9,10},{10,... | collective-permute-start | bytes 393224 | tf_op jit(solution)/shard_map/ppermute | solution.py:376
  10.5 0.3 collective-permute-done.refs_0_.refs_1_
  10.8 0.8 %collective-permute-start.12 = (bf16[2,128,256]{2,1,0:T(8,128)(2,1)S(1)}, bf16[2,128,256]{2,1,0:T(8,128)(2,1)S(1)}, u32[]{:S(2)}, u32[]{:S(2)}) collective-permute-start(bf16[2,128,256]{2,1,0:T(8,128)(2,1)S(1)} %get-tuple-element.91), channel_id=1, source_target_pairs={{0,5},{1,4},{2,7},{3,6},{4,1},{5,0},{6,3},{7,2},{8,13},{9,12},{10,... | collective-permute-start | bytes 393224 | tf_op jit(solution)/shard_map/ppermute | solution.py:376
  11.7 3.6 %filter_spectra.1 = (bf16[2,128,256]{2,1,0:T(8,128)(2,1)S(1)}, bf16[2,128,256]{2,1,0:T(8,128)(2,1)S(1)}, bf16[2,128,256]{2,1,0:T(8,128)(2,1)S(1)}, bf16[2,128,25...) custom-call(f32[512,1024]{1,0:T(8,128)S(1)} %copy-done.1, ...), custom_call_target="tpu_custom_call", output_to_operand_aliasing={{0}: (3, {}), {1}: (4, {}), {2}: (5, {}), {3}: (6, {}), {4}... | custom-call | tf_op jit(solution)/shard_map/filter_spectra/pallas_call | solution.py:172
  15.3 2.9 %collective-permute-start.13 = (bf16[2,128,256]{2,1,0:T(8,128)(2,1)S(1)}, bf16[2,128,256]{2,1,0:T(8,128)(2,1)S(1)}, u32[]{:S(2)}, u32[]{:S(2)}) collective-permute-start(bf16[2,128,256]{2,1,0:T(8,128)(2,1)S(1)} %get-tuple-element.92), channel_id=1, source_target_pairs={{0,7},{1,6},{2,5},{3,4},{4,3},{5,2},{6,1},{7,0},{8,15},{9,14},{10,... | collective-permute-start | bytes 393224 | tf_op jit(solution)/shard_map/ppermute | solution.py:376
  18.2 1.6 %collective-permute-start.2 = (bf16[2,128,256]{2,1,0:T(8,128)(2,1)S(1)}, bf16[2,128,256]{2,1,0:T(8,128)(2,1)S(1)}, u32[]{:S(2)}, u32[]{:S(2)}) collective-permute-start(bf16[2,128,256]{2,1,0:T(8,128)(2,1)S(1)} %get-tuple-element.79), channel_id=1, source_target_pairs={{0,4},{1,5},{2,6},{3,7},{4,0},{5,1},{6,2},{7,3},{8,12},{9,13},{10,... | collective-permute-start | bytes 393224 | tf_op jit(solution)/shard_map/ppermute | solution.py:376
  19.8 1.9 %collective-permute-start.3 = (bf16[2,128,256]{2,1,0:T(8,128)(2,1)S(1)}, bf16[2,128,256]{2,1,0:T(8,128)(2,1)S(1)}, u32[]{:S(2)}, u32[]{:S(2)}) collective-permute-start(bf16[2,128,256]{2,1,0:T(8,128)(2,1)S(1)} %get-tuple-element.80), channel_id=1, source_target_pairs={{0,6},{1,7},{2,4},{3,5},{4,2},{5,3},{6,0},{7,1},{8,14},{9,15},{10,... | collective-permute-start | bytes 393224 | tf_op jit(solution)/shard_map/ppermute | solution.py:376
  21.7 0.4 collective-permute-done.13.refs_7_
  22.0 3.1 %collective-permute-start.5 = (bf16[2,128,256]{2,1,0:T(8,128)(2,1)S(1)}, bf16[2,128,256]{2,1,0:T(8,128)(2,1)S(1)}, u32[]{:S(2)}, u32[]{:S(2)}) collective-permute-start(bf16[2,128,256]{2,1,0:T(8,128)(2,1)S(1)} %get-tuple-element.82), channel_id=1, source_target_pairs={{0,3},{1,2},{2,1},{3,0},{4,7},{5,6},{6,5},{7,4},{8,11},{9,10},{10,... | collective-permute-start | bytes 393224 | tf_op jit(solution)/shard_map/ppermute | solution.py:376
  25.1 1.0 %collective-permute-done.2.refs_2_ = bf16[2,128,256]{2,1,0:T(8,128)(2,1)S(1)} collective-permute-done((bf16[2,128,256]{2,1,0:T(8,128)(2,1)S(1)}, bf16[2,128,256]{2,1,0:T(8,128)(2,1)S(1)}, u32[]{:S(2)}, u32[]{:S(2)}) %collective-permute-start.2) | collective-permute-done | bytes 131104 | tf_op jit(solution)/shard_map/ppermute | solution.py:376
  26.1 2.5 %collective-permute-start.7 = (bf16[2,128,256]{2,1,0:T(8,128)(2,1)S(1)}, bf16[2,128,256]{2,1,0:T(8,128)(2,1)S(1)}, u32[]{:S(2)}, u32[]{:S(2)}) collective-permute-start(bf16[2,128,256]{2,1,0:T(8,128)(2,1)S(1)} %get-tuple-element.84), channel_id=1, source_target_pairs={{0,7},{1,6},{2,5},{3,4},{4,3},{5,2},{6,1},{7,0},{8,15},{9,14},{10,... | collective-permute-start | bytes 393224 | tf_op jit(solution)/shard_map/ppermute | solution.py:376
  28.5 4.8 %conv.2 = (bf16[2,2,128,256]{3,2,1,0:T(8,128)(2,1)S(1)}, bf16[2,2,128,256]{3,2,1,0:T(8,128)(2,1)S(1)}, bf16[2,2,128,256]{3,2,1,0:T(8,128)(2,1)S(1)}, bf16[2,2,12...) custom-call(s32[2]{0:T(128)S(1)} %pad_add_fusion.me, ...), custom_call_target="tpu_custom_call" | custom-call | tf_op jit(solution)/shard_map/conv/pallas_call | solution.py:251
  33.3 0.6 collective-permute-done.6.refs_6_
  33.9 4.8 %conv.3 = (bf16[2,2,128,256]{3,2,1,0:T(8,128)(2,1)S(1)}, bf16[2,2,128,256]{3,2,1,0:T(8,128)(2,1)S(1)}, bf16[2,2,128,256]{3,2,1,0:T(8,128)(2,1)S(1)}, bf16[2,2,12...) custom-call(s32[2]{0:T(128)S(1)} %pad_add_fusion.me, ...), custom_call_target="tpu_custom_call", output_to_operand_aliasing={{0}: (12, {}), {1}: (13, {}), {2}: (14, {}), {3}: (15, {}),... | custom-call | tf_op jit(solution)/shard_map/conv/pallas_call | solution.py:251
  38.7 1.7 %collective-permute-start.21 = (bf16[2,256,512]{2,1,0:T(8,128)(2,1)S(1)}, bf16[2,256,512]{2,1,0:T(8,128)(2,1)S(1)}, u32[]{:S(2)}, u32[]{:S(2)}) collective-permute-start(bf16[2,256,512]{2,1,0:T(8,128)(2,1)S(1)} %get-tuple-element.120), channel_id=1, source_target_pairs={{0,8},{8,0},{16,24},{24,16},{1,9},{9,1},{17,25},{25,17},{2,10},{10... | collective-permute-start | bytes 1572872 | tf_op jit(solution)/shard_map/ppermute | solution.py:344
  40.4 2.4 %collective-permute-start.16 = (bf16[2,2,128,256]{3,2,1,0:T(8,128)(2,1)S(1)}, bf16[2,2,128,256]{3,2,1,0:T(8,128)(2,1)S(1)}, u32[]{:S(2)}, u32[]{:S(2)}) collective-permute-start(bf16[2,2,128,256]{3,2,1,0:T(8,128)(2,1)S(1)} %get-tuple-element.106), channel_id=1, source_target_pairs={{0,2},{1,3},{2,0},{3,1},{4,6},{5,7},{6,4},{7,5},{8,10},{9,11},{10,... | collective-permute-start | bytes 786440 | tf_op jit(solution)/shard_map/ppermute | solution.py:376
  42.8 0.5 collective-permute-start.17
  43.3 0.9 %collective-permute-start.18 = (bf16[2,2,128,256]{3,2,1,0:T(8,128)(2,1)S(1)}, bf16[2,2,128,256]{3,2,1,0:T(8,128)(2,1)S(1)}, u32[]{:S(2)}, u32[]{:S(2)}) collective-permute-start(bf16[2,2,128,256]{3,2,1,0:T(8,128)(2,1)S(1)} %get-tuple-element.108), channel_id=1, source_target_pairs={{0,6},{1,7},{2,4},{3,5},{4,2},{5,3},{6,0},{7,1},{8,14},{9,15},{10,... | collective-permute-start | bytes 786440 | tf_op jit(solution)/shard_map/ppermute | solution.py:376
  44.2 5.7 %collective-permute-done.16.refs_1_ = bf16[2,2,128,256]{3,2,1,0:T(8,128)(2,1)S(1)} collective-permute-done((bf16[2,2,128,256]{3,2,1,0:T(8,128)(2,1)S(1)}, bf16[2,2,128,256]{3,2,1,0:T(8,128)(2,1)S(1)}, u32[]{:S(2)}, u32[]{:S(2)}) %collective-permute-start.16) | collective-permute-done | bytes 262176 | tf_op jit(solution)/shard_map/ppermute | solution.py:376
  49.9 6.2 %collective-permute-done.17.refs_2_ = bf16[2,2,128,256]{3,2,1,0:T(8,128)(2,1)S(1)} collective-permute-done((bf16[2,2,128,256]{3,2,1,0:T(8,128)(2,1)S(1)}, bf16[2,2,128,256]{3,2,1,0:T(8,128)(2,1)S(1)}, u32[]{:S(2)}, u32[]{:S(2)}) %collective-permute-start.17) | collective-permute-done | bytes 262176 | tf_op jit(solution)/shard_map/ppermute | solution.py:376
  56.2 1.2 %collective-permute-start.15 = (bf16[2,2,128,256]{3,2,1,0:T(8,128)(2,1)S(1)}, bf16[2,2,128,256]{3,2,1,0:T(8,128)(2,1)S(1)}, u32[]{:S(2)}, u32[]{:S(2)}) collective-permute-start(bf16[2,2,128,256]{3,2,1,0:T(8,128)(2,1)S(1)} %get-tuple-element.104), channel_id=1, source_target_pairs={{0,7},{1,6},{2,5},{3,4},{4,3},{5,2},{6,1},{7,0},{8,15},{9,14},{10,... | collective-permute-start | bytes 786440 | tf_op jit(solution)/shard_map/ppermute | solution.py:376
  57.4 0.1 add_grads.1
  57.5 2.7 %collective-permute-start.22 = (bf16[1,256,512]{2,1,0:T(8,128)(2,1)S(1)}, bf16[1,256,512]{2,1,0:T(8,128)(2,1)S(1)}, u32[]{:S(2)}, u32[]{:S(2)}) collective-permute-start(bf16[1,256,512]{2,1,0:T(8,128)(2,1)S(1)} %get-tuple-element.122), channel_id=1, source_target_pairs={{0,16},{8,24},{16,0},{24,8},{1,17},{9,25},{17,1},{25,9},{2,18},{10... | collective-permute-start | bytes 786440 | tf_op jit(solution)/shard_map/ppermute | solution.py:344
  60.2 0.6 collective-permute-done.20.refs_5_
  60.7 3.8 %gate.2 = (bf16[128,4096]{1,0:T(8,128)(2,1)}, bf16[128,4096]{1,0:T(8,128)(2,1)}, bf16[128,4096]{1,0:T(8,128)(2,1)}, bf16[128,4096]{1,0:T(8,128)(2,1)}) custom-call(s32[2]{0:T(128)S(1)} %pad_add_fusion.me, bf16[128,4096]{1,0:T(8,128)(2,1)S(1)} %get-tuple-element.64.query, bf16[128,4096]{1,0:T(8,128)(2,1)S(1)} %get-tuple-element.65.grad, ...), custom_call_target="tpu_custom_call" | custom-call | tf_op jit(solution)/shard_map/gate/pallas_call | solution.py:312
  64.5 4.1 %collective-permute-done.14.refs_0_ = bf16[2,2,128,256]{3,2,1,0:T(8,128)(2,1)S(1)} collective-permute-done((bf16[2,2,128,256]{3,2,1,0:T(8,128)(2,1)S(1)}, bf16[2,2,128,256]{3,2,1,0:T(8,128)(2,1)S(1)}, u32[]{:S(2)}, u32[]{:S(2)}) %collective-permute-start.14) | collective-permute-done | bytes 262176 | tf_op jit(solution)/shard_map/ppermute | solution.py:376
  68.6 2.1 %gate.3 = (bf16[128,4096]{1,0:T(8,128)(2,1)}, bf16[128,4096]{1,0:T(8,128)(2,1)}, bf16[128,4096]{1,0:T(8,128)(2,1)}, bf16[128,4096]{1,0:T(8,128)(2,1)}) custom-call(s32[2]{0:T(128)S(1)} %pad_add_fusion.me, bf16[128,4096]{1,0:T(8,128)(2,1)S(1)} %get-tuple-element.64.query, ...), custom_call_target="tpu_custom_call", output_to_operand_aliasing={{0}: (8, {}), {1}: (9, {}), {2}: (10, {}), {3}: (11, {})} | custom-call | tf_op jit(solution)/shard_map/gate/pallas_call | solution.py:312
  70.8 1.1 %turn_grads.1 = f32[512,256]{1,0:T(8,128)} custom-call(f32[1,256,512]{2,1,0:T(8,128)S(1)} %get-tuple-element.121.keep, bf16[1,256,512]{2,1,0:T(8,128)(2,1)S(1)} %collective-permute-done.22.got), custom_call_target="tpu_custom_call" | custom-call | tf_op jit(solution)/shard_map/turn_grads/pallas_call | solution.py:357
  (31 shorter events, 0.1 us)
Async XLA Ops:
  0.6 11.0 %copy-start = (bf16[8,256,256]{2,1,0:T(8,128)(2,1)S(1)}, bf16[8,256,256]{2,1,0:T(8,128)(2,1)}, u32[]{:S(2)}) copy-start(bf16[8,256,256]{2,1,0:T(8,128)(2,1)} %constant.12.clone.fwd.refs_9_) | copy-start | bytes 3145732
  0.6 11.0 %copy-start.1 = (f32[512,1024]{1,0:T(8,128)S(1)}, f32[512,1024]{1,0:T(8,128)}, u32[]{:S(2)}) copy-start(f32[512,1024]{1,0:T(8,128)} %filt.1) | copy-start | bytes 6291460
  0.7 27.8 %copy-start.2 = (bf16[8,128,256]{2,1,0:T(8,128)(2,1)S(1)}, bf16[8,128,256]{2,1,0:T(8,128)(2,1)}, u32[]{:S(2)}) copy-start(bf16[8,128,256]{2,1,0:T(8,128)(2,1)} %constant.13.clone.refs_10_) | copy-start | bytes 1572868
  3.9 6.9 %collective-permute-start = (bf16[2,128,256]{2,1,0:T(8,128)(2,1)S(1)}, bf16[2,128,256]{2,1,0:T(8,128)(2,1)S(1)}, u32[]{:S(2)}, u32[]{:S(2)}) collective-permute-start(bf16[2,128,256]{2,1,0:T(8,128)(2,1)S(1)} %get-tuple-element.68), channel_id=1, source_target_pairs={{0,2},{1,3},{2,0},{3,1},{4,6},{5,7},{6,4},{7,5},{8,10},{9,11},{10,... | collective-permute-start | bytes 393224 | tf_op jit(solution)/shard_map/ppermute | solution.py:376
  6.9 8.3 %collective-permute-start.8 = (bf16[2,128,256]{2,1,0:T(8,128)(2,1)S(1)}, bf16[2,128,256]{2,1,0:T(8,128)(2,1)S(1)}, u32[]{:S(2)}, u32[]{:S(2)}) collective-permute-start(bf16[2,128,256]{2,1,0:T(8,128)(2,1)S(1)} %get-tuple-element.87), channel_id=1, source_target_pairs={{0,4},{1,5},{2,6},{3,7},{4,0},{5,1},{6,2},{7,3},{8,12},{9,13},{10,... | collective-permute-start | bytes 393224 | tf_op jit(solution)/shard_map/ppermute | solution.py:376
  8.5 9.7 %collective-permute-start.9 = (bf16[2,128,256]{2,1,0:T(8,128)(2,1)S(1)}, bf16[2,128,256]{2,1,0:T(8,128)(2,1)S(1)}, u32[]{:S(2)}, u32[]{:S(2)}) collective-permute-start(bf16[2,128,256]{2,1,0:T(8,128)(2,1)S(1)} %get-tuple-element.88), channel_id=1, source_target_pairs={{0,6},{1,7},{2,4},{3,5},{4,2},{5,3},{6,0},{7,1},{8,14},{9,15},{10,... | collective-permute-start | bytes 393224 | tf_op jit(solution)/shard_map/ppermute | solution.py:376
  8.5 9.7 %collective-permute-start.10 = (bf16[2,128,256]{2,1,0:T(8,128)(2,1)S(1)}, bf16[2,128,256]{2,1,0:T(8,128)(2,1)S(1)}, u32[]{:S(2)}, u32[]{:S(2)}) collective-permute-start(bf16[2,128,256]{2,1,0:T(8,128)(2,1)S(1)} %get-tuple-element.89), channel_id=1, source_target_pairs={{0,1},{1,0},{2,3},{3,2},{4,5},{5,4},{6,7},{7,6},{8,9},{9,8},{10,11... | collective-permute-start | bytes 393224 | tf_op jit(solution)/shard_map/ppermute | solution.py:376
  8.5 11.3 %collective-permute-start.11 = (bf16[2,128,256]{2,1,0:T(8,128)(2,1)S(1)}, bf16[2,128,256]{2,1,0:T(8,128)(2,1)S(1)}, u32[]{:S(2)}, u32[]{:S(2)}) collective-permute-start(bf16[2,128,256]{2,1,0:T(8,128)(2,1)S(1)} %get-tuple-element.90), channel_id=1, source_target_pairs={{0,3},{1,2},{2,1},{3,0},{4,7},{5,6},{6,5},{7,4},{8,11},{9,10},{10,... | collective-permute-start | bytes 393224 | tf_op jit(solution)/shard_map/ppermute | solution.py:376
  10.8 10.9 %collective-permute-start.12 = (bf16[2,128,256]{2,1,0:T(8,128)(2,1)S(1)}, bf16[2,128,256]{2,1,0:T(8,128)(2,1)S(1)}, u32[]{:S(2)}, u32[]{:S(2)}) collective-permute-start(bf16[2,128,256]{2,1,0:T(8,128)(2,1)S(1)} %get-tuple-element.91), channel_id=1, source_target_pairs={{0,5},{1,4},{2,7},{3,6},{4,1},{5,0},{6,3},{7,2},{8,13},{9,12},{10,... | collective-permute-start | bytes 393224 | tf_op jit(solution)/shard_map/ppermute | solution.py:376
  15.3 6.8 %collective-permute-start.13 = (bf16[2,128,256]{2,1,0:T(8,128)(2,1)S(1)}, bf16[2,128,256]{2,1,0:T(8,128)(2,1)S(1)}, u32[]{:S(2)}, u32[]{:S(2)}) collective-permute-start(bf16[2,128,256]{2,1,0:T(8,128)(2,1)S(1)} %get-tuple-element.92), channel_id=1, source_target_pairs={{0,7},{1,6},{2,5},{3,4},{4,3},{5,2},{6,1},{7,0},{8,15},{9,14},{10,... | collective-permute-start | bytes 393224 | tf_op jit(solution)/shard_map/ppermute | solution.py:376
  18.2 6.9 %collective-permute-start.1 = (bf16[2,128,256]{2,1,0:T(8,128)(2,1)S(1)}, bf16[2,128,256]{2,1,0:T(8,128)(2,1)S(1)}, u32[]{:S(2)}, u32[]{:S(2)}) collective-permute-start(bf16[2,128,256]{2,1,0:T(8,128)(2,1)S(1)} %get-tuple-element.78), channel_id=1, source_target_pairs={{0,2},{1,3},{2,0},{3,1},{4,6},{5,7},{6,4},{7,5},{8,10},{9,11},{10,... | collective-permute-start | bytes 393224 | tf_op jit(solution)/shard_map/ppermute | solution.py:376
  18.2 7.9 %collective-permute-start.2 = (bf16[2,128,256]{2,1,0:T(8,128)(2,1)S(1)}, bf16[2,128,256]{2,1,0:T(8,128)(2,1)S(1)}, u32[]{:S(2)}, u32[]{:S(2)}) collective-permute-start(bf16[2,128,256]{2,1,0:T(8,128)(2,1)S(1)} %get-tuple-element.79), channel_id=1, source_target_pairs={{0,4},{1,5},{2,6},{3,7},{4,0},{5,1},{6,2},{7,3},{8,12},{9,13},{10,... | collective-permute-start | bytes 393224 | tf_op jit(solution)/shard_map/ppermute | solution.py:376
  19.8 13.5 %collective-permute-start.3 = (bf16[2,128,256]{2,1,0:T(8,128)(2,1)S(1)}, bf16[2,128,256]{2,1,0:T(8,128)(2,1)S(1)}, u32[]{:S(2)}, u32[]{:S(2)}) collective-permute-start(bf16[2,128,256]{2,1,0:T(8,128)(2,1)S(1)} %get-tuple-element.80), channel_id=1, source_target_pairs={{0,6},{1,7},{2,4},{3,5},{4,2},{5,3},{6,0},{7,1},{8,14},{9,15},{10,... | collective-permute-start | bytes 393224 | tf_op jit(solution)/shard_map/ppermute | solution.py:376
  21.7 11.6 %collective-permute-start.4 = (bf16[2,128,256]{2,1,0:T(8,128)(2,1)S(1)}, bf16[2,128,256]{2,1,0:T(8,128)(2,1)S(1)}, u32[]{:S(2)}, u32[]{:S(2)}) collective-permute-start(bf16[2,128,256]{2,1,0:T(8,128)(2,1)S(1)} %get-tuple-element.81), channel_id=1, source_target_pairs={{0,1},{1,0},{2,3},{3,2},{4,5},{5,4},{6,7},{7,6},{8,9},{9,8},{10,11... | collective-permute-start | bytes 393224 | tf_op jit(solution)/shard_map/ppermute | solution.py:376
  22.0 11.3 %collective-permute-start.5 = (bf16[2,128,256]{2,1,0:T(8,128)(2,1)S(1)}, bf16[2,128,256]{2,1,0:T(8,128)(2,1)S(1)}, u32[]{:S(2)}, u32[]{:S(2)}) collective-permute-start(bf16[2,128,256]{2,1,0:T(8,128)(2,1)S(1)} %get-tuple-element.82), channel_id=1, source_target_pairs={{0,3},{1,2},{2,1},{3,0},{4,7},{5,6},{6,5},{7,4},{8,11},{9,10},{10,... | collective-permute-start | bytes 393224 | tf_op jit(solution)/shard_map/ppermute | solution.py:376
  25.1 8.8 %collective-permute-start.6 = (bf16[2,128,256]{2,1,0:T(8,128)(2,1)S(1)}, bf16[2,128,256]{2,1,0:T(8,128)(2,1)S(1)}, u32[]{:S(2)}, u32[]{:S(2)}) collective-permute-start(bf16[2,128,256]{2,1,0:T(8,128)(2,1)S(1)} %get-tuple-element.83), channel_id=1, source_target_pairs={{0,5},{1,4},{2,7},{3,6},{4,1},{5,0},{6,3},{7,2},{8,13},{9,12},{10,... | collective-permute-start | bytes 393224 | tf_op jit(solution)/shard_map/ppermute | solution.py:376
  26.1 7.9 %collective-permute-start.7 = (bf16[2,128,256]{2,1,0:T(8,128)(2,1)S(1)}, bf16[2,128,256]{2,1,0:T(8,128)(2,1)S(1)}, u32[]{:S(2)}, u32[]{:S(2)}) collective-permute-start(bf16[2,128,256]{2,1,0:T(8,128)(2,1)S(1)} %get-tuple-element.84), channel_id=1, source_target_pairs={{0,7},{1,6},{2,5},{3,4},{4,3},{5,2},{6,1},{7,0},{8,15},{9,14},{10,... | collective-permute-start | bytes 393224 | tf_op jit(solution)/shard_map/ppermute | solution.py:376
  33.9 26.8 %copy-start.3 = (f32[4096]{0:T(1024)S(1)}, f32[4096]{0:T(1024)}, u32[]{:S(2)}) copy-start(f32[4096]{0:T(1024)} %param.13) | copy-start | bytes 49156
  38.7 17.4 %collective-permute-start.21 = (bf16[2,256,512]{2,1,0:T(8,128)(2,1)S(1)}, bf16[2,256,512]{2,1,0:T(8,128)(2,1)S(1)}, u32[]{:S(2)}, u32[]{:S(2)}) collective-permute-start(bf16[2,256,512]{2,1,0:T(8,128)(2,1)S(1)} %get-tuple-element.120), channel_id=1, source_target_pairs={{0,8},{8,0},{16,24},{24,16},{1,9},{9,1},{17,25},{25,17},{2,10},{10... | collective-permute-start | bytes 1572872 | tf_op jit(solution)/shard_map/ppermute | solution.py:344
  40.4 9.5 %collective-permute-start.16 = (bf16[2,2,128,256]{3,2,1,0:T(8,128)(2,1)S(1)}, bf16[2,2,128,256]{3,2,1,0:T(8,128)(2,1)S(1)}, u32[]{:S(2)}, u32[]{:S(2)}) collective-permute-start(bf16[2,2,128,256]{3,2,1,0:T(8,128)(2,1)S(1)} %get-tuple-element.106), channel_id=1, source_target_pairs={{0,2},{1,3},{2,0},{3,1},{4,6},{5,7},{6,4},{7,5},{8,10},{9,11},{10,... | collective-permute-start | bytes 786440 | tf_op jit(solution)/shard_map/ppermute | solution.py:376
  42.8 13.4 %collective-permute-start.17 = (bf16[2,2,128,256]{3,2,1,0:T(8,128)(2,1)S(1)}, bf16[2,2,128,256]{3,2,1,0:T(8,128)(2,1)S(1)}, u32[]{:S(2)}, u32[]{:S(2)}) collective-permute-start(bf16[2,2,128,256]{3,2,1,0:T(8,128)(2,1)S(1)} %get-tuple-element.107), channel_id=1, source_target_pairs={{0,4},{1,5},{2,6},{3,7},{4,0},{5,1},{6,2},{7,3},{8,12},{9,13},{10,... | collective-permute-start | bytes 786440 | tf_op jit(solution)/shard_map/ppermute | solution.py:376
  43.3 14.2 %collective-permute-start.18 = (bf16[2,2,128,256]{3,2,1,0:T(8,128)(2,1)S(1)}, bf16[2,2,128,256]{3,2,1,0:T(8,128)(2,1)S(1)}, u32[]{:S(2)}, u32[]{:S(2)}) collective-permute-start(bf16[2,2,128,256]{3,2,1,0:T(8,128)(2,1)S(1)} %get-tuple-element.108), channel_id=1, source_target_pairs={{0,6},{1,7},{2,4},{3,5},{4,2},{5,3},{6,0},{7,1},{8,14},{9,15},{10,... | collective-permute-start | bytes 786440 | tf_op jit(solution)/shard_map/ppermute | solution.py:376
  44.2 15.9 %collective-permute-start.19 = (bf16[2,2,128,256]{3,2,1,0:T(8,128)(2,1)S(1)}, bf16[2,2,128,256]{3,2,1,0:T(8,128)(2,1)S(1)}, u32[]{:S(2)}, u32[]{:S(2)}) collective-permute-start(bf16[2,2,128,256]{3,2,1,0:T(8,128)(2,1)S(1)} %get-tuple-element.109), channel_id=1, source_target_pairs={{0,1},{1,0},{2,3},{3,2},{4,5},{5,4},{6,7},{7,6},{8,9},{9,8},{10,11... | collective-permute-start | bytes 786440 | tf_op jit(solution)/shard_map/ppermute | solution.py:376
  49.9 10.8 %collective-permute-start.20 = (bf16[2,2,128,256]{3,2,1,0:T(8,128)(2,1)S(1)}, bf16[2,2,128,256]{3,2,1,0:T(8,128)(2,1)S(1)}, u32[]{:S(2)}, u32[]{:S(2)}) collective-permute-start(bf16[2,2,128,256]{3,2,1,0:T(8,128)(2,1)S(1)} %get-tuple-element.110), channel_id=1, source_target_pairs={{0,3},{1,2},{2,1},{3,0},{4,7},{5,6},{6,5},{7,4},{8,11},{9,10},{10,... | collective-permute-start | bytes 786440 | tf_op jit(solution)/shard_map/ppermute | solution.py:376
  56.2 12.5 %collective-permute-start.14 = (bf16[2,2,128,256]{3,2,1,0:T(8,128)(2,1)S(1)}, bf16[2,2,128,256]{3,2,1,0:T(8,128)(2,1)S(1)}, u32[]{:S(2)}, u32[]{:S(2)}) collective-permute-start(bf16[2,2,128,256]{3,2,1,0:T(8,128)(2,1)S(1)} %get-tuple-element.103), channel_id=1, source_target_pairs={{0,5},{1,4},{2,7},{3,6},{4,1},{5,0},{6,3},{7,2},{8,13},{9,12},{10,... | collective-permute-start | bytes 786440 | tf_op jit(solution)/shard_map/ppermute | solution.py:376
  56.2 12.5 %collective-permute-start.15 = (bf16[2,2,128,256]{3,2,1,0:T(8,128)(2,1)S(1)}, bf16[2,2,128,256]{3,2,1,0:T(8,128)(2,1)S(1)}, u32[]{:S(2)}, u32[]{:S(2)}) collective-permute-start(bf16[2,2,128,256]{3,2,1,0:T(8,128)(2,1)S(1)} %get-tuple-element.104), channel_id=1, source_target_pairs={{0,7},{1,6},{2,5},{3,4},{4,3},{5,2},{6,1},{7,0},{8,15},{9,14},{10,... | collective-permute-start | bytes 786440 | tf_op jit(solution)/shard_map/ppermute | solution.py:376
  57.5 13.3 %collective-permute-start.22 = (bf16[1,256,512]{2,1,0:T(8,128)(2,1)S(1)}, bf16[1,256,512]{2,1,0:T(8,128)(2,1)S(1)}, u32[]{:S(2)}, u32[]{:S(2)}) collective-permute-start(bf16[1,256,512]{2,1,0:T(8,128)(2,1)S(1)} %get-tuple-element.122), channel_id=1, source_target_pairs={{0,16},{8,24},{16,0},{24,8},{1,17},{9,25},{17,1},{25,9},{2,18},{10... | collective-permute-start | bytes 786440 | tf_op jit(solution)/shard_map/ppermute | solution.py:344

commit v8 on v7

--- a/solution.py
+++ b/solution.py
@@ -165,25 +165,22 @@
         lax.fori_loop(0, CLASSES, step, 0)
 
 
-def filter_spectra(filters, fwd, after, then):
+def filter_spectra(filters, fwd, arrived):
     chans, length = filters.shape
     width = chans // HALVES
     m2 = length // CLASSES
-    out = pl.pallas_call(
+    return pl.pallas_call(
         filter_kernel,
-        in_specs=[VMEM] * (2 + len(after) + len(then)),
-        out_specs=[VMEM] * (len(then) + 1),
-        out_shape=[pltpu.VMEM(t.shape, t.dtype) for t in then]
-        + [pltpu.VMEM((HALVES, CLASSES, 2 * m2, width), F32)],
+        in_specs=[VMEM] * (2 + len(arrived)),
+        out_specs=VMEM,
+        out_shape=pltpu.VMEM((HALVES, CLASSES, 2 * m2, width), F32),
         scratch_shapes=[
             pltpu.VMEM((width // 128, length, 128), F32),
             pltpu.VMEM((CLASSES, 2 * m2, width), F32),
         ],
-        input_output_aliases={2 + len(after) + i: i for i in range(len(then))},
         compiler_params=PARAMS,
         name="filter_spectra",
-    )(filters, fwd, *after, *then)
-    return out[-1], out[:-1]
+    )(filters, fwd, *arrived)
 
 
 def conv_kernel(n, d, half, me, *refs):
@@ -311,7 +308,7 @@
     _, _, rows, width = got[0].shape
     return pl.pallas_call(
         functools.partial(gate_kernel, js),
-        in_specs=[SMEM] + [VMEM] * (5 + len(js)) + [HBM] * len(outs),
+        in_specs=[SMEM] + [VMEM] * (5 + len(got)) + [HBM] * len(outs),
         out_specs=[HBM] * 4,
         out_shape=[jax.ShapeDtypeStruct(query.shape, BF16)] * 4,
         scratch_shapes=[
@@ -319,7 +316,7 @@
             pltpu.SemaphoreType.DMA((4, len(js))),
             pltpu.VMEM((len(js), 2, HALVES, width // 128, rows, 128), F32),
         ],
-        input_output_aliases={6 + len(js) + i: i for i in range(len(outs))},
+        input_output_aliases={6 + len(got) + i: i for i in range(len(outs))},
         compiler_params=PARAMS,
         name="gate",
     )(me, query, grad, value, key, gain, *got, *outs)
@@ -366,15 +363,31 @@
 
 
 def peers(n):
-    return [0, *range(2, n, 2), *range(1, n, 2)]
-
-
-def exchange(blocks, axis):
-    n = len(blocks)
-    got = [blocks[0]]
-    for j, block in zip(peers(n)[1:], blocks[1:]):
-        got.append(resident(lax.ppermute(block, axis, [(i, i ^ j) for i in range(n)])))
-    return got
+    return [0, 1, *range(2, n, 2), *range(3, n, 2)]
+
+
+def exchange(n, js, blocks):
+    return [
+        resident(lax.ppermute(block, "ctx", [(i, i ^ j) for i in range(n)])) if j else block
+        for j, block in zip(js, blocks)
+    ]
+
+
+def after_kernel(*refs):
+    pass
+
+
+def after(arrived, blocks):
+    count = len(arrived)
+    return pl.pallas_call(
+        after_kernel,
+        in_specs=[VMEM] * (count + len(blocks)),
+        out_specs=[VMEM] * len(blocks),
+        out_shape=[pltpu.VMEM(b.shape, b.dtype) for b in blocks],
+        input_output_aliases={count + i: i for i in range(len(blocks))},
+        compiler_params=PARAMS,
+        name="after",
+    )(*arrived, *blocks)
 
 
 def local(n, d, query_in, key_in, value_in, grad_out, filters, skip_gain):
@@ -385,15 +398,16 @@
 
     arrays = [in_hbm(x[0]) for x in (key_in, value_in, query_in, grad_out)]
     (key, value, query, grad), got = products(n, me, *arrays)
-    first = exchange(got[0], "ctx")
-    spec, second = filter_spectra(filters, fwd, [first[1]], got[1])
-    second = exchange(second, "ctx")
+    first = exchange(n, peers(n), got[0])
+    second = exchange(n, peers(n), after([first[1]], got[1]))
+    spec = filter_spectra(filters, fwd, [second[1]])
     results = conv(n, d, 0, me, first, spec, fwd, back, [])
     *mixed, keep, send = conv(n, d, 1, me, second, spec, fwd, back, results)
-    mixed = exchange(mixed, "ctx")
-    grad_filter = sum_grads(d, keep, send)
+    mixed = exchange(n, peers(n), mixed)
+    grad_filter = sum_grads(d, keep, *after([mixed[1]], [send]))
+
     outs = []
-    early = 3 * n // 4
+    early = n - 2
     for at in (slice(early), slice(early, n)):
         outs = gate(peers(n)[at], me, query, grad, value, key, gain, mixed[at], outs)
     return *(x[None] for x in outs), grad_filter

time: 72 us -> 72.1 us (level)
  starting transfers between devices: 28.8 us -> 25.2 us
  waiting for transfers between devices: 18.8 us -> 22.4 us
    ppermute x2, waiting for transfers between devices: 0.01 us -> 5.27 us  [sum_grads(): got = resident(lax.ppermute(send, 'dp', [(i, i ^ bit) for i in range(d)]))]
    ppermute x21, starting transfers between devices: 24.4 us -> 21 us  [exchange(): lax.ppermute(block, 'ctx', [(i, i ^ j) for i in range(n)])]
    ppermute x21, waiting for transfers between devices: 18.8 us -> 17.2 us  [exchange(): lax.ppermute(block, 'ctx', [(i, i ^ j) for i in range(n)])]
    pallas_call x1 -> x3, Pallas kernels: 3.6 us -> 3.59 us  [the longest x1 3.59 us: filter_spectra(): pl.pallas_call(filter_kernel, in_specs=[VMEM] * (2 + len(arrived)), out_s...]
  transfers between devices with their start and end apart: 23 -> 23, of which waited for: 8 -> 10; matrix products, arithmetic and copies ran while one was open for 0% -> 0% of each run, Pallas kernels for 20% -> 20%
where the time goes in v8:
time: 72.1 us; the launch traced here: 71.9 us
  starting transfers between devices  25.2 us (35%)
  Pallas kernels  23.5 us (33%)
  waiting for transfers between devices  22.4 us (31%)
  between operations  0.78 us (1%)
    ppermute x21, starting transfers between devices, exchange(): lax.ppermute(block, 'ctx', [(i, i ^ j) for i in range(n)])  21 us
    ppermute x21, waiting for transfers between devices, exchange(): lax.ppermute(block, 'ctx', [(i, i ^ j) for i in range(n)])  17.2 us
    pallas_call x2, Pallas kernels, conv(): pl.pallas_call(functools.partial(conv_kernel, n, d, half), in_specs=[SMEM...  9.58 us
    pallas_call x2, Pallas kernels, gate(): pl.pallas_call(functools.partial(gate_kernel, js), in_specs=[SMEM] + [VME...  5.93 us
    ppermute x2, waiting for transfers between devices, sum_grads(): got = resident(lax.ppermute(send, 'dp', [(i, i ^ bit) for i in range(d)]))  5.27 us
    ppermute x2, starting transfers between devices, sum_grads(): got = resident(lax.ppermute(send, 'dp', [(i, i ^ bit) for i in range(d)]))  4.16 us
    pallas_call x1, Pallas kernels, filter_spectra(): pl.pallas_call(filter_kernel, in_specs=[VMEM] * (2 + len(arrived)), out_s...  3.59 us
    pallas_call x1, Pallas kernels, products(): pl.pallas_call(functools.partial(product_kernel, n), in_specs=[SMEM] + [H...  3.18 us
  transfers between devices with their start and end apart: 23, of which 10 were waited for; matrix products, arithmetic and copies ran while one was open for 0% of the time, Pallas kernels for 20%

profile of v8, /device:TPU:0, one launch (start us, length us, event | category | flops | bytes accessed | tf_op | source)
XLA Modules:
  0.0 71.9 jit_solution(7296732535992117570)
XLA Ops:
  0.7 3.2 %products.1 = (bf16[128,4096]{1,0:T(8,128)(2,1)S(1)}, bf16[128,4096]{1,0:T(8,128)(2,1)S(1)}, bf16[128,4096]{1,0:T(8,128)(2,1)S(1)}, bf16[128,4096]{1,0:T(8,128)(...) custom-call(s32[2]{0:T(128)S(1)} %pad_add_fusion.me, ...), custom_call_target="tpu_custom_call" | custom-call | tf_op jit(solution)/shard_map/products/pallas_call | solution.py:126
  4.4 2.6 %collective-permute-start.8 = (bf16[2,128,256]{2,1,0:T(8,128)(2,1)S(1)}, bf16[2,128,256]{2,1,0:T(8,128)(2,1)S(1)}, u32[]{:S(2)}, u32[]{:S(2)}) collective-permute-start(bf16[2,128,256]{2,1,0:T(8,128)(2,1)S(1)} %get-tuple-element.85), channel_id=1, source_target_pairs={{0,2},{1,3},{2,0},{3,1},{4,6},{5,7},{6,4},{7,5},{8,10},{9,11},{10,... | collective-permute-start | bytes 393224 | tf_op jit(solution)/shard_map/ppermute | solution.py:371
  7.0 1.5 %collective-permute-start.9 = (bf16[2,128,256]{2,1,0:T(8,128)(2,1)S(1)}, bf16[2,128,256]{2,1,0:T(8,128)(2,1)S(1)}, u32[]{:S(2)}, u32[]{:S(2)}) collective-permute-start(bf16[2,128,256]{2,1,0:T(8,128)(2,1)S(1)} %get-tuple-element.86), channel_id=1, source_target_pairs={{0,4},{1,5},{2,6},{3,7},{4,0},{5,1},{6,2},{7,3},{8,12},{9,13},{10,... | collective-permute-start | bytes 393224 | tf_op jit(solution)/shard_map/ppermute | solution.py:371
  8.5 1.2 %collective-permute-start.11 = (bf16[2,128,256]{2,1,0:T(8,128)(2,1)S(1)}, bf16[2,128,256]{2,1,0:T(8,128)(2,1)S(1)}, u32[]{:S(2)}, u32[]{:S(2)}) collective-permute-start(bf16[2,128,256]{2,1,0:T(8,128)(2,1)S(1)} %get-tuple-element.88), channel_id=1, source_target_pairs={{0,3},{1,2},{2,1},{3,0},{4,7},{5,6},{6,5},{7,4},{8,11},{9,10},{10,... | collective-permute-start | bytes 393224 | tf_op jit(solution)/shard_map/ppermute | solution.py:371
  9.7 2.0 %collective-permute-start.12 = (bf16[2,128,256]{2,1,0:T(8,128)(2,1)S(1)}, bf16[2,128,256]{2,1,0:T(8,128)(2,1)S(1)}, u32[]{:S(2)}, u32[]{:S(2)}) collective-permute-start(bf16[2,128,256]{2,1,0:T(8,128)(2,1)S(1)} %get-tuple-element.89), channel_id=1, source_target_pairs={{0,5},{1,4},{2,7},{3,6},{4,1},{5,0},{6,3},{7,2},{8,13},{9,12},{10,... | collective-permute-start | bytes 393224 | tf_op jit(solution)/shard_map/ppermute | solution.py:371
  11.7 1.3 %collective-permute-start.13 = (bf16[2,128,256]{2,1,0:T(8,128)(2,1)S(1)}, bf16[2,128,256]{2,1,0:T(8,128)(2,1)S(1)}, u32[]{:S(2)}, u32[]{:S(2)}) collective-permute-start(bf16[2,128,256]{2,1,0:T(8,128)(2,1)S(1)} %get-tuple-element.90), channel_id=1, source_target_pairs={{0,7},{1,6},{2,5},{3,4},{4,3},{5,2},{6,1},{7,0},{8,15},{9,14},{10,... | collective-permute-start | bytes 393224 | tf_op jit(solution)/shard_map/ppermute | solution.py:371
  13.1 2.0 %collective-permute-done.9.refs_3_ = bf16[2,128,256]{2,1,0:T(8,128)(2,1)S(1)} collective-permute-done((bf16[2,128,256]{2,1,0:T(8,128)(2,1)S(1)}, bf16[2,128,256]{2,1,0:T(8,128)(2,1)S(1)}, u32[]{:S(2)}, u32[]{:S(2)}) %collective-permute-start.9) | collective-permute-done | bytes 131104 | tf_op jit(solution)/shard_map/ppermute | solution.py:371
  15.1 0.8 %collective-permute-done.10.refs_4_ = bf16[2,128,256]{2,1,0:T(8,128)(2,1)S(1)} collective-permute-done((bf16[2,128,256]{2,1,0:T(8,128)(2,1)S(1)}, bf16[2,128,256]{2,1,0:T(8,128)(2,1)S(1)}, u32[]{:S(2)}, u32[]{:S(2)}) %collective-permute-start.10) | collective-permute-done | bytes 131104 | tf_op jit(solution)/shard_map/ppermute | solution.py:371
  15.9 1.3 %collective-permute-start.2 = (bf16[2,128,256]{2,1,0:T(8,128)(2,1)S(1)}, bf16[2,128,256]{2,1,0:T(8,128)(2,1)S(1)}, u32[]{:S(2)}, u32[]{:S(2)}) collective-permute-start(bf16[2,128,256]{2,1,0:T(8,128)(2,1)S(1)} %get-tuple-element.78), channel_id=1, source_target_pairs={{0,2},{1,3},{2,0},{3,1},{4,6},{5,7},{6,4},{7,5},{8,10},{9,11},{10,... | collective-permute-start | bytes 393224 | tf_op jit(solution)/shard_map/ppermute | solution.py:371
  17.1 1.0 %collective-permute-start.3 = (bf16[2,128,256]{2,1,0:T(8,128)(2,1)S(1)}, bf16[2,128,256]{2,1,0:T(8,128)(2,1)S(1)}, u32[]{:S(2)}, u32[]{:S(2)}) collective-permute-start(bf16[2,128,256]{2,1,0:T(8,128)(2,1)S(1)} %get-tuple-element.79), channel_id=1, source_target_pairs={{0,4},{1,5},{2,6},{3,7},{4,0},{5,1},{6,2},{7,3},{8,12},{9,13},{10,... | collective-permute-start | bytes 393224 | tf_op jit(solution)/shard_map/ppermute | solution.py:371
  18.2 2.7 %collective-permute-done.12.refs_6_ = bf16[2,128,256]{2,1,0:T(8,128)(2,1)S(1)} collective-permute-done((bf16[2,128,256]{2,1,0:T(8,128)(2,1)S(1)}, bf16[2,128,256]{2,1,0:T(8,128)(2,1)S(1)}, u32[]{:S(2)}, u32[]{:S(2)}) %collective-permute-start.12) | collective-permute-done | bytes 131104 | tf_op jit(solution)/shard_map/ppermute | solution.py:371
  20.8 1.1 %collective-permute-start.4 = (bf16[2,128,256]{2,1,0:T(8,128)(2,1)S(1)}, bf16[2,128,256]{2,1,0:T(8,128)(2,1)S(1)}, u32[]{:S(2)}, u32[]{:S(2)}) collective-permute-start(bf16[2,128,256]{2,1,0:T(8,128)(2,1)S(1)} %get-tuple-element.80), channel_id=1, source_target_pairs={{0,6},{1,7},{2,4},{3,5},{4,2},{5,3},{6,0},{7,1},{8,14},{9,15},{10,... | collective-permute-start | bytes 393224 | tf_op jit(solution)/shard_map/ppermute | solution.py:371
  22.0 2.0 %collective-permute-start.5 = (bf16[2,128,256]{2,1,0:T(8,128)(2,1)S(1)}, bf16[2,128,256]{2,1,0:T(8,128)(2,1)S(1)}, u32[]{:S(2)}, u32[]{:S(2)}) collective-permute-start(bf16[2,128,256]{2,1,0:T(8,128)(2,1)S(1)} %get-tuple-element.81), channel_id=1, source_target_pairs={{0,3},{1,2},{2,1},{3,0},{4,7},{5,6},{6,5},{7,4},{8,11},{9,10},{10,... | collective-permute-start | bytes 393224 | tf_op jit(solution)/shard_map/ppermute | solution.py:371
  24.6 3.6 %filter_spectra.1.refs_8_ = f32[2,8,256,256]{3,2,1,0:T(8,128)S(1)} custom-call(f32[512,1024]{1,0:T(8,128)S(1)} %copy-done.1, bf16[8,256,256]{2,1,0:T(8,128)(2,1)S(1)} %copy-done, bf16[2,128,256]{2,1,0:T(8,128)(2,1)S(1)} %collective-permute-done.1.refs_0_.refs_1_), custom_call_target="tpu_custom_call" | custom-call | tf_op jit(solution)/shard_map/filter_spectra/pallas_call | solution.py:172
  28.2 4.8 %conv.2 = (bf16[2,2,128,256]{3,2,1,0:T(8,128)(2,1)S(1)}, bf16[2,2,128,256]{3,2,1,0:T(8,128)(2,1)S(1)}, bf16[2,2,128,256]{3,2,1,0:T(8,128)(2,1)S(1)}, bf16[2,2,12...) custom-call(s32[2]{0:T(128)S(1)} %pad_add_fusion.me, ...), custom_call_target="tpu_custom_call" | custom-call | tf_op jit(solution)/shard_map/conv/pallas_call | solution.py:248
  33.1 4.8 %conv.3 = (bf16[2,2,128,256]{3,2,1,0:T(8,128)(2,1)S(1)}, bf16[2,2,128,256]{3,2,1,0:T(8,128)(2,1)S(1)}, bf16[2,2,128,256]{3,2,1,0:T(8,128)(2,1)S(1)}, bf16[2,2,12...) custom-call(s32[2]{0:T(128)S(1)} %pad_add_fusion.me, ...), custom_call_target="tpu_custom_call", output_to_operand_aliasing={{0}: (12, {}), {1}: (13, {}), {2}: (14, {}), {3}: (15, {}),... | custom-call | tf_op jit(solution)/shard_map/conv/pallas_call | solution.py:248
  37.9 1.0 %collective-permute-start.16 = (bf16[2,2,128,256]{3,2,1,0:T(8,128)(2,1)S(1)}, bf16[2,2,128,256]{3,2,1,0:T(8,128)(2,1)S(1)}, u32[]{:S(2)}, u32[]{:S(2)}) collective-permute-start(bf16[2,2,128,256]{3,2,1,0:T(8,128)(2,1)S(1)} %get-tuple-element.104), channel_id=1, source_target_pairs={{0,1},{1,0},{2,3},{3,2},{4,5},{5,4},{6,7},{7,6},{8,9},{9,8},{10,11... | collective-permute-start | bytes 786440 | tf_op jit(solution)/shard_map/ppermute | solution.py:371
  38.9 1.2 %collective-permute-done.16.refs_1_.refs_0_ = bf16[2,2,128,256]{3,2,1,0:T(8,128)(2,1)S(1)} collective-permute-done((bf16[2,2,128,256]{3,2,1,0:T(8,128)(2,1)S(1)}, bf16[2,2,128,256]{3,2,1,0:T(8,128)(2,1)S(1)}, u32[]{:S(2)}, u32[]{:S(2)}) %collective-permute-start.16) | collective-permute-done | bytes 262176 | tf_op jit(solution)/shard_map/ppermute | solution.py:371
  40.1 1.6 %collective-permute-start.21 = (bf16[2,256,512]{2,1,0:T(8,128)(2,1)S(1)}, bf16[2,256,512]{2,1,0:T(8,128)(2,1)S(1)}, u32[]{:S(2)}, u32[]{:S(2)}) collective-permute-start(bf16[2,256,512]{2,1,0:T(8,128)(2,1)S(1)} %after.3), channel_id=1, source_target_pairs={{0,8},{8,0},{16,24},{24,16},{1,9},{9,1},{17,25},{25,17},{2,10},{10... | collective-permute-start | bytes 1572872 | tf_op jit(solution)/shard_map/ppermute | solution.py:341
  41.6 1.9 %collective-permute-start.17 = (bf16[2,2,128,256]{3,2,1,0:T(8,128)(2,1)S(1)}, bf16[2,2,128,256]{3,2,1,0:T(8,128)(2,1)S(1)}, u32[]{:S(2)}, u32[]{:S(2)}) collective-permute-start(bf16[2,2,128,256]{3,2,1,0:T(8,128)(2,1)S(1)} %get-tuple-element.105), channel_id=1, source_target_pairs={{0,2},{1,3},{2,0},{3,1},{4,6},{5,7},{6,4},{7,5},{8,10},{9,11},{10,... | collective-permute-start | bytes 786440 | tf_op jit(solution)/shard_map/ppermute | solution.py:371
  43.7 1.5 %collective-permute-start.19 = (bf16[2,2,128,256]{3,2,1,0:T(8,128)(2,1)S(1)}, bf16[2,2,128,256]{3,2,1,0:T(8,128)(2,1)S(1)}, u32[]{:S(2)}, u32[]{:S(2)}) collective-permute-start(bf16[2,2,128,256]{3,2,1,0:T(8,128)(2,1)S(1)} %get-tuple-element.107), channel_id=1, source_target_pairs={{0,6},{1,7},{2,4},{3,5},{4,2},{5,3},{6,0},{7,1},{8,14},{9,15},{10,... | collective-permute-start | bytes 786440 | tf_op jit(solution)/shard_map/ppermute | solution.py:371
  45.7 5.1 %collective-permute-done.17.refs_2_ = bf16[2,2,128,256]{3,2,1,0:T(8,128)(2,1)S(1)} collective-permute-done((bf16[2,2,128,256]{3,2,1,0:T(8,128)(2,1)S(1)}, bf16[2,2,128,256]{3,2,1,0:T(8,128)(2,1)S(1)}, u32[]{:S(2)}, u32[]{:S(2)}) %collective-permute-start.17) | collective-permute-done | bytes 262176 | tf_op jit(solution)/shard_map/ppermute | solution.py:371
  50.8 3.5 %collective-permute-done.21.got = bf16[2,256,512]{2,1,0:T(8,128)(2,1)S(1)} collective-permute-done((bf16[2,256,512]{2,1,0:T(8,128)(2,1)S(1)}, bf16[2,256,512]{2,1,0:T(8,128)(2,1)S(1)}, u32[]{:S(2)}, u32[]{:S(2)}) %collective-permute-start.21) | collective-permute-done | bytes 524320 | tf_op jit(solution)/shard_map/ppermute | solution.py:341
  54.3 0.7 collective-permute-start.15
  55.1 3.2 %collective-permute-done.18.refs_3_ = bf16[2,2,128,256]{3,2,1,0:T(8,128)(2,1)S(1)} collective-permute-done((bf16[2,2,128,256]{3,2,1,0:T(8,128)(2,1)S(1)}, bf16[2,2,128,256]{3,2,1,0:T(8,128)(2,1)S(1)}, u32[]{:S(2)}, u32[]{:S(2)}) %collective-permute-start.18) | collective-permute-done | bytes 262176 | tf_op jit(solution)/shard_map/ppermute | solution.py:371
  58.3 2.6 %collective-permute-start.22 = (bf16[1,256,512]{2,1,0:T(8,128)(2,1)S(1)}, bf16[1,256,512]{2,1,0:T(8,128)(2,1)S(1)}, u32[]{:S(2)}, u32[]{:S(2)}) collective-permute-start(bf16[1,256,512]{2,1,0:T(8,128)(2,1)S(1)} %get-tuple-element.120), channel_id=1, source_target_pairs={{0,16},{8,24},{16,0},{24,8},{1,17},{9,25},{17,1},{25,9},{2,18},{10... | collective-permute-start | bytes 786440 | tf_op jit(solution)/shard_map/ppermute | solution.py:341
  60.9 0.7 collective-permute-done.20.refs_5_
  61.5 3.8 %gate.2 = (bf16[128,4096]{1,0:T(8,128)(2,1)}, bf16[128,4096]{1,0:T(8,128)(2,1)}, bf16[128,4096]{1,0:T(8,128)(2,1)}, bf16[128,4096]{1,0:T(8,128)(2,1)}) custom-call(s32[2]{0:T(128)S(1)} %pad_add_fusion.me, bf16[128,4096]{1,0:T(8,128)(2,1)S(1)} %get-tuple-element.63.query, bf16[128,4096]{1,0:T(8,128)(2,1)S(1)} %get-tuple-element.64.grad, ...), custom_call_target="tpu_custom_call" | custom-call | tf_op jit(solution)/shard_map/gate/pallas_call | solution.py:309
  65.3 1.6 %collective-permute-done.14.refs_0_ = bf16[2,2,128,256]{3,2,1,0:T(8,128)(2,1)S(1)} collective-permute-done((bf16[2,2,128,256]{3,2,1,0:T(8,128)(2,1)S(1)}, bf16[2,2,128,256]{3,2,1,0:T(8,128)(2,1)S(1)}, u32[]{:S(2)}, u32[]{:S(2)}) %collective-permute-start.14) | collective-permute-done | bytes 262176 | tf_op jit(solution)/shard_map/ppermute | solution.py:371
  66.9 2.1 %gate.3 = (bf16[128,4096]{1,0:T(8,128)(2,1)}, bf16[128,4096]{1,0:T(8,128)(2,1)}, bf16[128,4096]{1,0:T(8,128)(2,1)}, bf16[128,4096]{1,0:T(8,128)(2,1)}) custom-call(s32[2]{0:T(128)S(1)} %pad_add_fusion.me, bf16[128,4096]{1,0:T(8,128)(2,1)S(1)} %get-tuple-element.63.query, ...), custom_call_target="tpu_custom_call", output_to_operand_aliasing={{0}: (8, {}), {1}: (9, {}), {2}: (10, {}), {3}: (11, {})} | custom-call | tf_op jit(solution)/shard_map/gate/pallas_call | solution.py:309
  69.1 1.8 %collective-permute-done.22.got = bf16[1,256,512]{2,1,0:T(8,128)(2,1)S(1)} collective-permute-done((bf16[1,256,512]{2,1,0:T(8,128)(2,1)S(1)}, bf16[1,256,512]{2,1,0:T(8,128)(2,1)S(1)}, u32[]{:S(2)}, u32[]{:S(2)}) %collective-permute-start.22) | collective-permute-done | bytes 262176 | tf_op jit(solution)/shard_map/ppermute | solution.py:341
  70.9 1.1 %turn_grads.1 = f32[512,256]{1,0:T(8,128)} custom-call(f32[1,256,512]{2,1,0:T(8,128)S(1)} %get-tuple-element.119.keep, bf16[1,256,512]{2,1,0:T(8,128)(2,1)S(1)} %collective-permute-done.22.got), custom_call_target="tpu_custom_call" | custom-call | tf_op jit(solution)/shard_map/turn_grads/pallas_call | solution.py:354
  (33 shorter events, 2.1 us)
Async XLA Ops:
  0.6 24.0 %copy-start = (bf16[8,256,256]{2,1,0:T(8,128)(2,1)S(1)}, bf16[8,256,256]{2,1,0:T(8,128)(2,1)}, u32[]{:S(2)}) copy-start(bf16[8,256,256]{2,1,0:T(8,128)(2,1)} %constant.12.clone.fwd.refs_9_) | copy-start | bytes 3145732
  0.6 24.0 %copy-start.1 = (f32[512,1024]{1,0:T(8,128)S(1)}, f32[512,1024]{1,0:T(8,128)}, u32[]{:S(2)}) copy-start(f32[512,1024]{1,0:T(8,128)} %filt.1) | copy-start | bytes 6291460
  3.9 5.8 %collective-permute-start = (bf16[2,128,256]{2,1,0:T(8,128)(2,1)S(1)}, bf16[2,128,256]{2,1,0:T(8,128)(2,1)S(1)}, u32[]{:S(2)}, u32[]{:S(2)}) collective-permute-start(bf16[2,128,256]{2,1,0:T(8,128)(2,1)S(1)} %get-tuple-element.67), channel_id=1, source_target_pairs={{0,1},{1,0},{2,3},{3,2},{4,5},{5,4},{6,7},{7,6},{8,9},{9,8},{10,11... | collective-permute-start | bytes 393224 | tf_op jit(solution)/shard_map/ppermute | solution.py:371
  4.4 7.3 %collective-permute-start.8 = (bf16[2,128,256]{2,1,0:T(8,128)(2,1)S(1)}, bf16[2,128,256]{2,1,0:T(8,128)(2,1)S(1)}, u32[]{:S(2)}, u32[]{:S(2)}) collective-permute-start(bf16[2,128,256]{2,1,0:T(8,128)(2,1)S(1)} %get-tuple-element.85), channel_id=1, source_target_pairs={{0,2},{1,3},{2,0},{3,1},{4,6},{5,7},{6,4},{7,5},{8,10},{9,11},{10,... | collective-permute-start | bytes 393224 | tf_op jit(solution)/shard_map/ppermute | solution.py:371
  7.0 8.1 %collective-permute-start.9 = (bf16[2,128,256]{2,1,0:T(8,128)(2,1)S(1)}, bf16[2,128,256]{2,1,0:T(8,128)(2,1)S(1)}, u32[]{:S(2)}, u32[]{:S(2)}) collective-permute-start(bf16[2,128,256]{2,1,0:T(8,128)(2,1)S(1)} %get-tuple-element.86), channel_id=1, source_target_pairs={{0,4},{1,5},{2,6},{3,7},{4,0},{5,1},{6,2},{7,3},{8,12},{9,13},{10,... | collective-permute-start | bytes 393224 | tf_op jit(solution)/shard_map/ppermute | solution.py:371
  8.5 7.3 %collective-permute-start.10 = (bf16[2,128,256]{2,1,0:T(8,128)(2,1)S(1)}, bf16[2,128,256]{2,1,0:T(8,128)(2,1)S(1)}, u32[]{:S(2)}, u32[]{:S(2)}) collective-permute-start(bf16[2,128,256]{2,1,0:T(8,128)(2,1)S(1)} %get-tuple-element.87), channel_id=1, source_target_pairs={{0,6},{1,7},{2,4},{3,5},{4,2},{5,3},{6,0},{7,1},{8,14},{9,15},{10,... | collective-permute-start | bytes 393224 | tf_op jit(solution)/shard_map/ppermute | solution.py:371
  8.5 8.6 %collective-permute-start.11 = (bf16[2,128,256]{2,1,0:T(8,128)(2,1)S(1)}, bf16[2,128,256]{2,1,0:T(8,128)(2,1)S(1)}, u32[]{:S(2)}, u32[]{:S(2)}) collective-permute-start(bf16[2,128,256]{2,1,0:T(8,128)(2,1)S(1)} %get-tuple-element.88), channel_id=1, source_target_pairs={{0,3},{1,2},{2,1},{3,0},{4,7},{5,6},{6,5},{7,4},{8,11},{9,10},{10,... | collective-permute-start | bytes 393224 | tf_op jit(solution)/shard_map/ppermute | solution.py:371
  9.7 11.1 %collective-permute-start.12 = (bf16[2,128,256]{2,1,0:T(8,128)(2,1)S(1)}, bf16[2,128,256]{2,1,0:T(8,128)(2,1)S(1)}, u32[]{:S(2)}, u32[]{:S(2)}) collective-permute-start(bf16[2,128,256]{2,1,0:T(8,128)(2,1)S(1)} %get-tuple-element.89), channel_id=1, source_target_pairs={{0,5},{1,4},{2,7},{3,6},{4,1},{5,0},{6,3},{7,2},{8,13},{9,12},{10,... | collective-permute-start | bytes 393224 | tf_op jit(solution)/shard_map/ppermute | solution.py:371
  11.7 16.5 %copy-start.2 = (bf16[8,128,256]{2,1,0:T(8,128)(2,1)S(1)}, bf16[8,128,256]{2,1,0:T(8,128)(2,1)}, u32[]{:S(2)}) copy-start(bf16[8,128,256]{2,1,0:T(8,128)(2,1)} %constant.13.clone.refs_10_) | copy-start | bytes 1572868
  11.7 10.2 %collective-permute-start.13 = (bf16[2,128,256]{2,1,0:T(8,128)(2,1)S(1)}, bf16[2,128,256]{2,1,0:T(8,128)(2,1)S(1)}, u32[]{:S(2)}, u32[]{:S(2)}) collective-permute-start(bf16[2,128,256]{2,1,0:T(8,128)(2,1)S(1)} %get-tuple-element.90), channel_id=1, source_target_pairs={{0,7},{1,6},{2,5},{3,4},{4,3},{5,2},{6,1},{7,0},{8,15},{9,14},{10,... | collective-permute-start | bytes 393224 | tf_op jit(solution)/shard_map/ppermute | solution.py:371
  15.1 8.8 %collective-permute-start.1 = (bf16[2,128,256]{2,1,0:T(8,128)(2,1)S(1)}, bf16[2,128,256]{2,1,0:T(8,128)(2,1)S(1)}, u32[]{:S(2)}, u32[]{:S(2)}) collective-permute-start(bf16[2,128,256]{2,1,0:T(8,128)(2,1)S(1)} %get-tuple-element.77), channel_id=1, source_target_pairs={{0,1},{1,0},{2,3},{3,2},{4,5},{5,4},{6,7},{7,6},{8,9},{9,8},{10,11... | collective-permute-start | bytes 393224 | tf_op jit(solution)/shard_map/ppermute | solution.py:371
  15.9 8.2 %collective-permute-start.2 = (bf16[2,128,256]{2,1,0:T(8,128)(2,1)S(1)}, bf16[2,128,256]{2,1,0:T(8,128)(2,1)S(1)}, u32[]{:S(2)}, u32[]{:S(2)}) collective-permute-start(bf16[2,128,256]{2,1,0:T(8,128)(2,1)S(1)} %get-tuple-element.78), channel_id=1, source_target_pairs={{0,2},{1,3},{2,0},{3,1},{4,6},{5,7},{6,4},{7,5},{8,10},{9,11},{10,... | collective-permute-start | bytes 393224 | tf_op jit(solution)/shard_map/ppermute | solution.py:371
  17.1 15.9 %collective-permute-start.3 = (bf16[2,128,256]{2,1,0:T(8,128)(2,1)S(1)}, bf16[2,128,256]{2,1,0:T(8,128)(2,1)S(1)}, u32[]{:S(2)}, u32[]{:S(2)}) collective-permute-start(bf16[2,128,256]{2,1,0:T(8,128)(2,1)S(1)} %get-tuple-element.79), channel_id=1, source_target_pairs={{0,4},{1,5},{2,6},{3,7},{4,0},{5,1},{6,2},{7,3},{8,12},{9,13},{10,... | collective-permute-start | bytes 393224 | tf_op jit(solution)/shard_map/ppermute | solution.py:371
  20.8 12.2 %collective-permute-start.4 = (bf16[2,128,256]{2,1,0:T(8,128)(2,1)S(1)}, bf16[2,128,256]{2,1,0:T(8,128)(2,1)S(1)}, u32[]{:S(2)}, u32[]{:S(2)}) collective-permute-start(bf16[2,128,256]{2,1,0:T(8,128)(2,1)S(1)} %get-tuple-element.80), channel_id=1, source_target_pairs={{0,6},{1,7},{2,4},{3,5},{4,2},{5,3},{6,0},{7,1},{8,14},{9,15},{10,... | collective-permute-start | bytes 393224 | tf_op jit(solution)/shard_map/ppermute | solution.py:371
  22.0 11.1 %collective-permute-start.5 = (bf16[2,128,256]{2,1,0:T(8,128)(2,1)S(1)}, bf16[2,128,256]{2,1,0:T(8,128)(2,1)S(1)}, u32[]{:S(2)}, u32[]{:S(2)}) collective-permute-start(bf16[2,128,256]{2,1,0:T(8,128)(2,1)S(1)} %get-tuple-element.81), channel_id=1, source_target_pairs={{0,3},{1,2},{2,1},{3,0},{4,7},{5,6},{6,5},{7,4},{8,11},{9,10},{10,... | collective-permute-start | bytes 393224 | tf_op jit(solution)/shard_map/ppermute | solution.py:371
  23.9 9.1 %collective-permute-start.6 = (bf16[2,128,256]{2,1,0:T(8,128)(2,1)S(1)}, bf16[2,128,256]{2,1,0:T(8,128)(2,1)S(1)}, u32[]{:S(2)}, u32[]{:S(2)}) collective-permute-start(bf16[2,128,256]{2,1,0:T(8,128)(2,1)S(1)} %get-tuple-element.82), channel_id=1, source_target_pairs={{0,5},{1,4},{2,7},{3,6},{4,1},{5,0},{6,3},{7,2},{8,13},{9,12},{10,... | collective-permute-start | bytes 393224 | tf_op jit(solution)/shard_map/ppermute | solution.py:371
  24.1 9.0 %collective-permute-start.7 = (bf16[2,128,256]{2,1,0:T(8,128)(2,1)S(1)}, bf16[2,128,256]{2,1,0:T(8,128)(2,1)S(1)}, u32[]{:S(2)}, u32[]{:S(2)}) collective-permute-start(bf16[2,128,256]{2,1,0:T(8,128)(2,1)S(1)} %get-tuple-element.83), channel_id=1, source_target_pairs={{0,7},{1,6},{2,5},{3,4},{4,3},{5,2},{6,1},{7,0},{8,15},{9,14},{10,... | collective-permute-start | bytes 393224 | tf_op jit(solution)/shard_map/ppermute | solution.py:371
  33.1 28.5 %copy-start.3 = (f32[4096]{0:T(1024)S(1)}, f32[4096]{0:T(1024)}, u32[]{:S(2)}) copy-start(f32[4096]{0:T(1024)} %param.13) | copy-start | bytes 49156
  37.9 2.2 %collective-permute-start.16 = (bf16[2,2,128,256]{3,2,1,0:T(8,128)(2,1)S(1)}, bf16[2,2,128,256]{3,2,1,0:T(8,128)(2,1)S(1)}, u32[]{:S(2)}, u32[]{:S(2)}) collective-permute-start(bf16[2,2,128,256]{3,2,1,0:T(8,128)(2,1)S(1)} %get-tuple-element.104), channel_id=1, source_target_pairs={{0,1},{1,0},{2,3},{3,2},{4,5},{5,4},{6,7},{7,6},{8,9},{9,8},{10,11... | collective-permute-start | bytes 786440 | tf_op jit(solution)/shard_map/ppermute | solution.py:371
  40.1 14.2 %collective-permute-start.21 = (bf16[2,256,512]{2,1,0:T(8,128)(2,1)S(1)}, bf16[2,256,512]{2,1,0:T(8,128)(2,1)S(1)}, u32[]{:S(2)}, u32[]{:S(2)}) collective-permute-start(bf16[2,256,512]{2,1,0:T(8,128)(2,1)S(1)} %after.3), channel_id=1, source_target_pairs={{0,8},{8,0},{16,24},{24,16},{1,9},{9,1},{17,25},{25,17},{2,10},{10... | collective-permute-start | bytes 1572872 | tf_op jit(solution)/shard_map/ppermute | solution.py:341
  41.6 9.2 %collective-permute-start.17 = (bf16[2,2,128,256]{3,2,1,0:T(8,128)(2,1)S(1)}, bf16[2,2,128,256]{3,2,1,0:T(8,128)(2,1)S(1)}, u32[]{:S(2)}, u32[]{:S(2)}) collective-permute-start(bf16[2,2,128,256]{3,2,1,0:T(8,128)(2,1)S(1)} %get-tuple-element.105), channel_id=1, source_target_pairs={{0,2},{1,3},{2,0},{3,1},{4,6},{5,7},{6,4},{7,5},{8,10},{9,11},{10,... | collective-permute-start | bytes 786440 | tf_op jit(solution)/shard_map/ppermute | solution.py:371
  43.6 14.7 %collective-permute-start.18 = (bf16[2,2,128,256]{3,2,1,0:T(8,128)(2,1)S(1)}, bf16[2,2,128,256]{3,2,1,0:T(8,128)(2,1)S(1)}, u32[]{:S(2)}, u32[]{:S(2)}) collective-permute-start(bf16[2,2,128,256]{3,2,1,0:T(8,128)(2,1)S(1)} %get-tuple-element.106), channel_id=1, source_target_pairs={{0,4},{1,5},{2,6},{3,7},{4,0},{5,1},{6,2},{7,3},{8,12},{9,13},{10,... | collective-permute-start | bytes 786440 | tf_op jit(solution)/shard_map/ppermute | solution.py:371
  43.7 17.2 %collective-permute-start.19 = (bf16[2,2,128,256]{3,2,1,0:T(8,128)(2,1)S(1)}, bf16[2,2,128,256]{3,2,1,0:T(8,128)(2,1)S(1)}, u32[]{:S(2)}, u32[]{:S(2)}) collective-permute-start(bf16[2,2,128,256]{3,2,1,0:T(8,128)(2,1)S(1)} %get-tuple-element.107), channel_id=1, source_target_pairs={{0,6},{1,7},{2,4},{3,5},{4,2},{5,3},{6,0},{7,1},{8,14},{9,15},{10,... | collective-permute-start | bytes 786440 | tf_op jit(solution)/shard_map/ppermute | solution.py:371
  45.1 16.4 %collective-permute-start.20 = (bf16[2,2,128,256]{3,2,1,0:T(8,128)(2,1)S(1)}, bf16[2,2,128,256]{3,2,1,0:T(8,128)(2,1)S(1)}, u32[]{:S(2)}, u32[]{:S(2)}) collective-permute-start(bf16[2,2,128,256]{3,2,1,0:T(8,128)(2,1)S(1)} %get-tuple-element.108), channel_id=1, source_target_pairs={{0,3},{1,2},{2,1},{3,0},{4,7},{5,6},{6,5},{7,4},{8,11},{9,10},{10,... | collective-permute-start | bytes 786440 | tf_op jit(solution)/shard_map/ppermute | solution.py:371
  50.8 16.1 %collective-permute-start.14 = (bf16[2,2,128,256]{3,2,1,0:T(8,128)(2,1)S(1)}, bf16[2,2,128,256]{3,2,1,0:T(8,128)(2,1)S(1)}, u32[]{:S(2)}, u32[]{:S(2)}) collective-permute-start(bf16[2,2,128,256]{3,2,1,0:T(8,128)(2,1)S(1)} %get-tuple-element.101), channel_id=1, source_target_pairs={{0,5},{1,4},{2,7},{3,6},{4,1},{5,0},{6,3},{7,2},{8,13},{9,12},{10,... | collective-permute-start | bytes 786440 | tf_op jit(solution)/shard_map/ppermute | solution.py:371
  54.3 12.6 %collective-permute-start.15 = (bf16[2,2,128,256]{3,2,1,0:T(8,128)(2,1)S(1)}, bf16[2,2,128,256]{3,2,1,0:T(8,128)(2,1)S(1)}, u32[]{:S(2)}, u32[]{:S(2)}) collective-permute-start(bf16[2,2,128,256]{3,2,1,0:T(8,128)(2,1)S(1)} %get-tuple-element.102), channel_id=1, source_target_pairs={{0,7},{1,6},{2,5},{3,4},{4,3},{5,2},{6,1},{7,0},{8,15},{9,14},{10,... | collective-permute-start | bytes 786440 | tf_op jit(solution)/shard_map/ppermute | solution.py:371
  58.3 12.6 %collective-permute-start.22 = (bf16[1,256,512]{2,1,0:T(8,128)(2,1)S(1)}, bf16[1,256,512]{2,1,0:T(8,128)(2,1)S(1)}, u32[]{:S(2)}, u32[]{:S(2)}) collective-permute-start(bf16[1,256,512]{2,1,0:T(8,128)(2,1)S(1)} %get-tuple-element.120), channel_id=1, source_target_pairs={{0,16},{8,24},{16,0},{24,8},{1,17},{9,25},{17,1},{25,9},{2,18},{10... | collective-permute-start | bytes 786440 | tf_op jit(solution)/shard_map/ppermute | solution.py:341

commit v9 on v8

--- a/solution.py
+++ b/solution.py
@@ -19,6 +19,7 @@
 CONV_PARAMS = pltpu.CompilerParams(vmem_limit_bytes=34 * 1024 * 1024)
 SMEM = pl.BlockSpec(memory_space=pltpu.SMEM)
 VMEM = pl.BlockSpec(memory_space=pltpu.VMEM)
+SMALL_COST = pl.CostEstimate(flops=0, bytes_accessed=1024, transcendentals=0)
 HBM = pl.BlockSpec(memory_space=pltpu.HBM)
 
 
@@ -88,14 +89,24 @@
     return pltpu.with_memory_space_constraint(x, pltpu.HBM)
 
 
-def peer_columns(me, j, width):
-    return pl.ds(pl.multiple_of((me[0] ^ j) * width, 128), width)
+def chips(n):
+    return range(0, n, 2)
+
+
+def sources(n, got, passed):
+    straight = [(chip, got[i].at[0]) for i, chip in enumerate(chips(n))]
+    return straight + [(chip + 1, passed.at[i]) for i, chip in enumerate(chips(n))]
+
+
+def peer_columns(me, j, half, width, lane=0, lanes=None):
+    start = (HALVES * (me[0] ^ j) + half) * width + lane
+    return pl.ds(pl.multiple_of(start, 128), lanes or width)
 
 
 def product_kernel(n, me, key, value, query, grad, *refs):
     bufs, outs, sems = refs[:4], refs[4:-1], refs[-1]
-    _, rows, width = outs[0].shape
-    width *= HALVES
+    width = outs[0].shape[-1]
+    rows = key.shape[0]
     step = rows // STEPS
     copies = []
     for i in range(STEPS):
@@ -113,27 +124,30 @@
         for a, (left, right) in enumerate((bufs[:2], bufs[2:])):
             copies[s][2 * a].wait()
             copies[s][2 * a + 1].wait()
-            for i, j in enumerate(peers(n)):
-                cols = peer_columns(me, j, width)
-                value = (left[at, cols].astype(F32) * right[at, cols].astype(F32)).astype(BF16)
-                for half in range(HALVES):
-                    outs[half * n + i][a, at] = value[:, half * width // HALVES :][:, : width // HALVES]
+            for half in range(HALVES):
+                for i, chip in enumerate(chips(n)):
+                    for core in range(2):
+                        cols = peer_columns(me, chip + core, half, width)
+                        value = left[at, cols].astype(F32) * right[at, cols].astype(F32)
+                        outs[half * (n // 2) + i][core, a, at] = value.astype(BF16)
 
 
 def products(n, me, key, value, query, grad):
     rows, total = key.shape
     width = total // n // HALVES
+    count = n // 2
     out = pl.pallas_call(
         functools.partial(product_kernel, n),
         in_specs=[SMEM] + [HBM] * 4,
-        out_specs=[VMEM] * (4 + HALVES * n),
+        out_specs=[VMEM] * (4 + HALVES * count),
         out_shape=[pltpu.VMEM(key.shape, BF16)] * 4
-        + [pltpu.VMEM((2, rows, width), BF16)] * (HALVES * n),
+        + [pltpu.VMEM((2, 2, rows, width), BF16)] * (HALVES * count),
         scratch_shapes=[pltpu.SemaphoreType.DMA((4, STEPS))],
+        cost_estimate=SMALL_COST,
         compiler_params=PARAMS,
         name="products",
     )(me, key, value, query, grad)
-    return out[:4], [out[4 + h * n : 4 + (h + 1) * n] for h in range(HALVES)]
+    return out[:4], [out[4 + h * count : 4 + (h + 1) * count] for h in range(HALVES)]
 
 
 def lane_groups(width):
@@ -178,16 +192,19 @@
             pltpu.VMEM((width // 128, length, 128), F32),
             pltpu.VMEM((CLASSES, 2 * m2, width), F32),
         ],
+        cost_estimate=SMALL_COST,
         compiler_params=PARAMS,
         name="filter_spectra",
     )(filters, fwd, *arrived)
 
 
 def conv_kernel(n, d, half, me, *refs):
-    got, (filt, fwd, back) = refs[:n], refs[n : n + 3]
-    refs = refs[-(n + 2 + 6) :]
-    out, (keep, send), (nat, x, u, y, turned, grad) = refs[:n], refs[n : n + 2], refs[n + 2 :]
-    _, rows, width = got[0].shape
+    count = n // 2
+    got, (passed, filt, fwd, back) = refs[:count], refs[count : count + 4]
+    refs = refs[-(count + 2 + 6) :]
+    out, (keep, send), (nat, x, u, y, turned, grad) = refs[:count], refs[count : count + 2], refs[count + 2 :]
+    rows, width = passed.shape[2:]
+    blocks = sources(n, got, passed)
     m2 = x.shape[2]
     per = keep.shape[1] // CLASSES
     groups = lane_groups(width)
@@ -197,9 +214,9 @@
 
     for a in range(2):
         for g, lanes in enumerate(groups):
-            for i, j in enumerate(peers(n)):
+            for j, block in blocks:
                 at = pl.multiple_of((me[0] ^ j) * rows, rows)
-                nat[a, g, pl.ds(at, rows)] = got[i][a, :, lanes].astype(F32)
+                nat[a, g, pl.ds(at, rows)] = block[a, :, lanes].astype(F32)
             for c in range(CLASSES):
                 x[a, c, :, lanes] = nat[a, g, pl.ds(c, m2, stride=CLASSES), :].astype(BF16)
         for c in range(CLASSES):
@@ -226,11 +243,11 @@
         grad[c] = dot(back[c], y[2, c])
         for o in range(2):
             turned[o, c] = dot(back[c], y[o, c]).astype(BF16)
-    for i, j in enumerate(peers(n)):
+    for j in range(n):
         at = pl.multiple_of((me[0] ^ j) * part_rows, part_rows)
         for o in range(2):
             for c in range(CLASSES):
-                out[i][half, o, c * part_rows : (c + 1) * part_rows] = turned[o, c, pl.ds(at, part_rows)]
+                out[j // 2][j % 2, o, c * part_rows : (c + 1) * part_rows] = turned[o, c, pl.ds(at, part_rows)]
     for j in range(d):
         at = pl.multiple_of((me[1] ^ j) * per, per)
         for c in range(CLASSES):
@@ -241,15 +258,16 @@
                 keep[j // 2, c * per : (c + 1) * per, chans] = part
 
 
-def conv(n, d, half, me, got, filt, fwd, back, before):
-    _, rows, width = got[0].shape
+def conv(n, d, half, me, got, passed, filt, fwd, back, before):
+    _, _, rows, width = got[0].shape
     length = n * rows
     m2 = length // CLASSES
+    count = n // 2
     out = pl.pallas_call(
         functools.partial(conv_kernel, n, d, half),
-        in_specs=[SMEM] + [VMEM] * (n + 3 + len(before)),
-        out_specs=[VMEM] * (n + 2),
-        out_shape=[pltpu.VMEM((HALVES, 2, rows, width), BF16)] * n
+        in_specs=[SMEM] + [VMEM] * (count + 4 + len(before)),
+        out_specs=[VMEM] * (count + 2),
+        out_shape=[pltpu.VMEM((2, 2, rows, width), BF16)] * count
         + [pltpu.VMEM((d // 2, length // d, HALVES * width), dtype) for dtype in (F32, BF16)],
         scratch_shapes=[
             pltpu.VMEM((2, width // 128, length, 128), F32),
@@ -259,11 +277,12 @@
             pltpu.VMEM((2, CLASSES, m2, width), BF16),
             pltpu.VMEM((CLASSES, m2, width), F32),
         ],
-        input_output_aliases={n + 4 + i: i for i in range(len(before))},
+        input_output_aliases={count + 5 + i: count + i for i in range(len(before))},
+        cost_estimate=SMALL_COST,
         compiler_params=CONV_PARAMS,
         name="conv",
-    )(me, *got, filt, fwd, back, *before)
-    return out
+    )(me, *got, passed, filt, fwd, back, *before)
+    return out[:count], out[count:]
 
 
 def natural(scratch, piece):
@@ -273,53 +292,51 @@
     return scratch[...]
 
 
-def gate_kernel(js, me, query, grad, value, key, gain, *refs):
-    got, outs, (sent, sems, nat) = refs[: len(js)], refs[-7:-3], refs[-3:]
-    _, _, rows, width = got[0].shape
+def gate_kernel(half, js, picks, me, query, grad, value, key, gain, *refs):
+    outs, (sent, sems, nat) = refs[-7:-3], refs[-3:]
+    rows, width = sent.shape[2:]
     copies = []
-    for i, j in enumerate(js):
-        block = peer_columns(me, j, HALVES * width)
-        for half in range(HALVES):
-            for g, lanes in enumerate(lane_groups(width)):
-                at = half * width + lanes.start
-                start = pl.multiple_of((me[0] ^ j) * HALVES * width + at, 128)
-                cols = pl.ds(start, 128)
-                to = slice(at, at + 128)
-                scale = gain[:, cols]
-                q, g_, v, k = (x[:, cols].astype(F32) for x in (query, grad, value, key))
-                conv_out, corr_back = (
-                    natural(nat.at[i, o, half, g], got[i][half, o, :, lanes].astype(F32)) for o in range(2)
-                )
-                mixing = conv_out + scale * (k * v).astype(BF16).astype(F32)
-                sent[0, i, :, to] = (q * mixing).astype(BF16)
-                sent[1, i, :, to] = (g_ * mixing).astype(BF16)
-                total = corr_back + scale * (g_ * q).astype(BF16).astype(F32)
-                sent[2, i, :, to] = (total * v).astype(BF16)
-                sent[3, i, :, to] = (total * k).astype(BF16)
+    for i, (j, (array, place)) in enumerate(zip(js, picks)):
+        block = refs[array].at[place]
+        for g, lanes in enumerate(lane_groups(width)):
+            cols = peer_columns(me, j, half, width, lanes.start, 128)
+            scale = gain[:, cols]
+            q, g_, v, k = (x[:, cols].astype(F32) for x in (query, grad, value, key))
+            conv_out, corr_back = (
+                natural(nat.at[i, o, g], block[o, :, lanes].astype(F32)) for o in range(2)
+            )
+            mixing = conv_out + scale * (k * v).astype(BF16).astype(F32)
+            sent[0, i, :, lanes] = (q * mixing).astype(BF16)
+            sent[1, i, :, lanes] = (g_ * mixing).astype(BF16)
+            total = corr_back + scale * (g_ * q).astype(BF16).astype(F32)
+            sent[2, i, :, lanes] = (total * v).astype(BF16)
+            sent[3, i, :, lanes] = (total * k).astype(BF16)
         for a in range(4):
-            copy = pltpu.make_async_copy(sent.at[a, i], outs[a].at[:, block], sems.at[a, i])
+            to = outs[a].at[:, peer_columns(me, j, half, width)]
+            copy = pltpu.make_async_copy(sent.at[a, i], to, sems.at[a, i])
             copy.start()
             copies.append(copy)
     for copy in copies:
         copy.wait()
 
 
-def gate(js, me, query, grad, value, key, gain, got, outs):
-    _, _, rows, width = got[0].shape
+def gate(half, js, picks, me, arrays, gain, got, outs):
+    rows, width = got[0].shape[-2:]
     return pl.pallas_call(
-        functools.partial(gate_kernel, js),
+        functools.partial(gate_kernel, half, js, picks),
         in_specs=[SMEM] + [VMEM] * (5 + len(got)) + [HBM] * len(outs),
         out_specs=[HBM] * 4,
-        out_shape=[jax.ShapeDtypeStruct(query.shape, BF16)] * 4,
+        out_shape=[jax.ShapeDtypeStruct(arrays[0].shape, BF16)] * 4,
         scratch_shapes=[
-            pltpu.VMEM((4, len(js), rows, HALVES * width), BF16),
+            pltpu.VMEM((4, len(js), rows, width), BF16),
             pltpu.SemaphoreType.DMA((4, len(js))),
-            pltpu.VMEM((len(js), 2, HALVES, width // 128, rows, 128), F32),
+            pltpu.VMEM((len(js), 2, width // 128, rows, 128), F32),
         ],
         input_output_aliases={6 + len(got) + i: i for i in range(len(outs))},
+        cost_estimate=SMALL_COST,
         compiler_params=PARAMS,
         name="gate",
-    )(me, query, grad, value, key, gain, *got, *outs)
+    )(me, *arrays, gain, *got, *outs)
 
 
 def add_kernel(keep, got, new_keep, new_send):
@@ -347,7 +364,8 @@
             in_specs=[VMEM] * 2,
             out_specs=[VMEM] * 2,
             out_shape=[pltpu.VMEM(shape, F32), pltpu.VMEM(shape, BF16)],
-            compiler_params=PARAMS,
+            cost_estimate=SMALL_COST,
+        compiler_params=PARAMS,
             name="add_grads",
         )(keep, got)
         bit *= 2
@@ -357,20 +375,35 @@
         out_specs=VMEM,
         out_shape=jax.ShapeDtypeStruct((chans, per), F32),
         scratch_shapes=[pltpu.VMEM((chans // 128, per, 128), F32)],
+        cost_estimate=SMALL_COST,
         compiler_params=PARAMS,
         name="turn_grads",
     )(keep, got)
 
 
-def peers(n):
-    return [0, 1, *range(2, n, 2), *range(3, n, 2)]
-
-
-def exchange(n, js, blocks):
-    return [
-        resident(lax.ppermute(block, "ctx", [(i, i ^ j) for i in range(n)])) if j else block
-        for j, block in zip(js, blocks)
+def across(n, blocks):
+    return [blocks[0]] + [
+        resident(lax.ppermute(block, "ctx", [(i, i ^ chip) for i in range(n)]))
+        for chip, block in zip(chips(n)[1:], blocks[1:])
     ]
+
+
+def pack_kernel(*refs):
+    for i, ref in enumerate(refs[:-1]):
+        refs[-1][i] = ref[1]
+
+
+def inside(n, got):
+    packed = pl.pallas_call(
+        pack_kernel,
+        in_specs=[VMEM] * len(got),
+        out_specs=VMEM,
+        out_shape=pltpu.VMEM((len(got), *got[0].shape[1:]), BF16),
+        cost_estimate=SMALL_COST,
+        compiler_params=PARAMS,
+        name="pack",
+    )(*got)
+    return resident(lax.ppermute(packed, "ctx", [(i, i ^ 1) for i in range(n)]))
 
 
 def after_kernel(*refs):
@@ -385,6 +418,7 @@
         out_specs=[VMEM] * len(blocks),
         out_shape=[pltpu.VMEM(b.shape, b.dtype) for b in blocks],
         input_output_aliases={count + i: i for i in range(len(blocks))},
+        cost_estimate=SMALL_COST,
         compiler_params=PARAMS,
         name="after",
     )(*arrived, *blocks)
@@ -397,19 +431,26 @@
     me = jnp.stack([lax.axis_index("ctx"), lax.axis_index("dp")]).astype(jnp.int32)
 
     arrays = [in_hbm(x[0]) for x in (key_in, value_in, query_in, grad_out)]
-    (key, value, query, grad), got = products(n, me, *arrays)
-    first = exchange(n, peers(n), got[0])
-    second = exchange(n, peers(n), after([first[1]], got[1]))
-    spec = filter_spectra(filters, fwd, [second[1]])
-    results = conv(n, d, 0, me, first, spec, fwd, back, [])
-    *mixed, keep, send = conv(n, d, 1, me, second, spec, fwd, back, results)
-    mixed = exchange(n, peers(n), mixed)
-    grad_filter = sum_grads(d, keep, *after([mixed[1]], [send]))
-
+    (key, value, query, grad), sent = products(n, me, *arrays)
+    arrays = query, grad, value, key
+    spec = filter_spectra(filters, fwd, [])
+    got = [across(n, blocks) for blocks in sent]
+    mixed, sums = [], []
+    for half in range(HALVES):
+        if mixed:
+            got[half] = after(mixed[0][:1], got[half])
+        passed = inside(n, got[half])
+        blocks, sums = conv(n, d, half, me, got[half], passed, spec, fwd, back, sums)
+        mixed.append(across(n, blocks))
+    grad_filter = sum_grads(d, *sums)
+
+    straight = [(i, 0) for i in range(n // 2)]
     outs = []
-    early = n - 2
-    for at in (slice(early), slice(early, n)):
-        outs = gate(peers(n)[at], me, query, grad, value, key, gain, mixed[at], outs)
+    for half in range(HALVES):
+        passed = inside(n, mixed[half])
+        outs = gate(half, chips(n), straight, me, arrays, gain, mixed[half], outs)
+        handed = [(0, i) for i in range(n // 2)]
+        outs = gate(half, [c + 1 for c in chips(n)], handed, me, arrays, gain, [passed], outs)
     return *(x[None] for x in outs), grad_filter
 
 

time: 72.1 us -> 81.7 us (1.13)
  waiting for transfers between devices: 22.4 us -> 33.8 us
  starting transfers between devices: 25.2 us -> 20.5 us
  Pallas kernels: 23.5 us -> 26.1 us
    ppermute x21 -> x16, waiting for transfers between devices: 17.2 us -> 27.6 us  [the longest x12 27.6 us: across(): lax.ppermute(block, 'ctx', [(i, i ^ chip) for i in range(n)])]
    ppermute x21 -> x16, starting transfers between devices: 21 us -> 16.2 us  [the longest x12 15.9 us: across(): lax.ppermute(block, 'ctx', [(i, i ^ chip) for i in range(n)])]
    pallas_call x2 -> x8, Pallas kernels: 5.93 us -> 8.66 us  [the longest x4 8.52 us: gate(): pl.pallas_call(functools.partial(gate_kernel, half, js, picks), in_specs=...]
    ppermute x2, waiting for transfers between devices: 5.27 us -> 6.2 us  [sum_grads(): got = resident(lax.ppermute(send, 'dp', [(i, i ^ bit) for i in range(d)]))]
  transfers between devices with their start and end apart: 23 -> 18, of which waited for: 10 -> 8; matrix products, arithmetic and copies ran while one was open for 0% -> 0% of each run, Pallas kernels for 20% -> 25%
where the time goes in v9:
time: 81.7 us; the launch traced here: 81.5 us
  waiting for transfers between devices  33.8 us (41%)
  Pallas kernels  26.1 us (32%)
  starting transfers between devices  20.5 us (25%)
  between operations  0.99 us (1%)
    ppermute x12, waiting for transfers between devices, across(): lax.ppermute(block, 'ctx', [(i, i ^ chip) for i in range(n)])  27.6 us
    ppermute x12, starting transfers between devices, across(): lax.ppermute(block, 'ctx', [(i, i ^ chip) for i in range(n)])  15.9 us
    pallas_call x2, Pallas kernels, conv(): pl.pallas_call(functools.partial(conv_kernel, n, d, half), in_specs=[SMEM...  9.52 us
    pallas_call x4, Pallas kernels, gate(): pl.pallas_call(functools.partial(gate_kernel, half, js, picks), in_specs=...  8.52 us
    ppermute x2, waiting for transfers between devices, sum_grads(): got = resident(lax.ppermute(send, 'dp', [(i, i ^ bit) for i in range(d)]))  6.2 us
    ppermute x2, starting transfers between devices, sum_grads(): got = resident(lax.ppermute(send, 'dp', [(i, i ^ bit) for i in range(d)]))  4.29 us
    pallas_call x1, Pallas kernels, filter_spectra(): pl.pallas_call(filter_kernel, in_specs=[VMEM] * (2 + len(arrived)), out_s...  3.59 us
    pallas_call x1, Pallas kernels, products(): pl.pallas_call(functools.partial(product_kernel, n), in_specs=[SMEM] + [H...  3.19 us
  transfers between devices with their start and end apart: 18, of which 8 were waited for; matrix products, arithmetic and copies ran while one was open for 0% of the time, Pallas kernels for 25%

profile of v9, /device:TPU:0, one launch (start us, length us, event | category | flops | bytes accessed | tf_op | source)
XLA Modules:
  0.0 81.5 jit_solution(16987682293701173983)
XLA Ops:
  0.7 0.1 pad_add_fusion.me
  0.7 3.2 %products.1 = (bf16[128,4096]{1,0:T(8,128)(2,1)S(1)}, bf16[128,4096]{1,0:T(8,128)(2,1)S(1)}, bf16[128,4096]{1,0:T(8,128)(2,1)S(1)}, bf16[128,4096]{1,0:T(8,128)(...) custom-call(s32[2]{0:T(128)S(1)} %pad_add_fusion.me, ...), custom_call_target="tpu_custom_call" | custom-call | bytes 1024 | tf_op jit(solution)/shard_map/products/pallas_call | solution.py:139
  3.9 3.0 %collective-permute-start = (bf16[2,2,128,256]{3,2,1,0:T(8,128)(2,1)S(1)}, bf16[2,2,128,256]{3,2,1,0:T(8,128)(2,1)S(1)}, u32[]{:S(2)}, u32[]{:S(2)}) collective-permute-start(bf16[2,2,128,256]{3,2,1,0:T(8,128)(2,1)S(1)} %get-tuple-element.56), channel_id=1, source_target_pairs={{0,2},{1,3},{2,0},{3,1},{4,6},{5,7},{6,4},{7,5},{8,10},{9,11},{10,... | collective-permute-start | bytes 786440 | tf_op jit(solution)/shard_map/ppermute | solution.py:386
  6.9 1.5 %collective-permute-start.1 = (bf16[2,2,128,256]{3,2,1,0:T(8,128)(2,1)S(1)}, bf16[2,2,128,256]{3,2,1,0:T(8,128)(2,1)S(1)}, u32[]{:S(2)}, u32[]{:S(2)}) collective-permute-start(bf16[2,2,128,256]{3,2,1,0:T(8,128)(2,1)S(1)} %get-tuple-element.57), channel_id=1, source_target_pairs={{0,4},{1,5},{2,6},{3,7},{4,0},{5,1},{6,2},{7,3},{8,12},{9,13},{10,... | collective-permute-start | bytes 786440 | tf_op jit(solution)/shard_map/ppermute | solution.py:386
  8.5 5.6 %collective-permute-done.refs_1_ = bf16[2,2,128,256]{3,2,1,0:T(8,128)(2,1)S(1)} collective-permute-done((bf16[2,2,128,256]{3,2,1,0:T(8,128)(2,1)S(1)}, bf16[2,2,128,256]{3,2,1,0:T(8,128)(2,1)S(1)}, u32[]{:S(2)}, u32[]{:S(2)}) %collective-permute-start) | collective-permute-done | bytes 262176 | tf_op jit(solution)/shard_map/ppermute | solution.py:386
  14.1 6.2 %collective-permute-done.1.refs_2_ = bf16[2,2,128,256]{3,2,1,0:T(8,128)(2,1)S(1)} collective-permute-done((bf16[2,2,128,256]{3,2,1,0:T(8,128)(2,1)S(1)}, bf16[2,2,128,256]{3,2,1,0:T(8,128)(2,1)S(1)}, u32[]{:S(2)}, u32[]{:S(2)}) %collective-permute-start.1) | collective-permute-done | bytes 262176 | tf_op jit(solution)/shard_map/ppermute | solution.py:386
  20.4 1.3 %collective-permute-start.4 = (bf16[2,2,128,256]{3,2,1,0:T(8,128)(2,1)S(1)}, bf16[2,2,128,256]{3,2,1,0:T(8,128)(2,1)S(1)}, u32[]{:S(2)}, u32[]{:S(2)}) collective-permute-start(bf16[2,2,128,256]{3,2,1,0:T(8,128)(2,1)S(1)} %get-tuple-element.61), channel_id=1, source_target_pairs={{0,2},{1,3},{2,0},{3,1},{4,6},{5,7},{6,4},{7,5},{8,10},{9,11},{10,... | collective-permute-start | bytes 786440 | tf_op jit(solution)/shard_map/ppermute | solution.py:386
  21.7 0.8 %collective-permute-start.5 = (bf16[2,2,128,256]{3,2,1,0:T(8,128)(2,1)S(1)}, bf16[2,2,128,256]{3,2,1,0:T(8,128)(2,1)S(1)}, u32[]{:S(2)}, u32[]{:S(2)}) collective-permute-start(bf16[2,2,128,256]{3,2,1,0:T(8,128)(2,1)S(1)} %get-tuple-element.62), channel_id=1, source_target_pairs={{0,4},{1,5},{2,6},{3,7},{4,0},{5,1},{6,2},{7,3},{8,12},{9,13},{10,... | collective-permute-start | bytes 786440 | tf_op jit(solution)/shard_map/ppermute | solution.py:386
  22.6 1.4 %collective-permute-start.6 = (bf16[2,2,128,256]{3,2,1,0:T(8,128)(2,1)S(1)}, bf16[2,2,128,256]{3,2,1,0:T(8,128)(2,1)S(1)}, u32[]{:S(2)}, u32[]{:S(2)}) collective-permute-start(bf16[2,2,128,256]{3,2,1,0:T(8,128)(2,1)S(1)} %get-tuple-element.63), channel_id=1, source_target_pairs={{0,6},{1,7},{2,4},{3,5},{4,2},{5,3},{6,0},{7,1},{8,14},{9,15},{10,... | collective-permute-start | bytes 786440 | tf_op jit(solution)/shard_map/ppermute | solution.py:386
  24.0 3.6 %filter_spectra.1.refs_5_ = f32[2,8,256,256]{3,2,1,0:T(8,128)S(1)} custom-call(f32[512,1024]{1,0:T(8,128)S(1)} %copy-done.1, bf16[8,256,256]{2,1,0:T(8,128)(2,1)S(1)} %copy-done), custom_call_target="tpu_custom_call" | custom-call | bytes 1024 | tf_op jit(solution)/shard_map/filter_spectra/pallas_call | solution.py:186
  27.6 4.8 %conv.2 = (bf16[2,2,128,256]{3,2,1,0:T(8,128)(2,1)S(1)}, bf16[2,2,128,256]{3,2,1,0:T(8,128)(2,1)S(1)}, bf16[2,2,128,256]{3,2,1,0:T(8,128)(2,1)S(1)}, bf16[2,2,12...) custom-call(s32[2]{0:T(128)S(1)} %pad_add_fusion.me, ...), custom_call_target="tpu_custom_call" | custom-call | bytes 1024 | tf_op jit(solution)/shard_map/conv/pallas_call | solution.py:266
  32.4 1.7 %collective-permute-done.5.refs_3_ = bf16[2,2,128,256]{3,2,1,0:T(8,128)(2,1)S(1)} collective-permute-done((bf16[2,2,128,256]{3,2,1,0:T(8,128)(2,1)S(1)}, bf16[2,2,128,256]{3,2,1,0:T(8,128)(2,1)S(1)}, u32[]{:S(2)}, u32[]{:S(2)}) %collective-permute-start.5) | collective-permute-done | bytes 262176 | tf_op jit(solution)/shard_map/ppermute | solution.py:386
  34.1 1.6 %collective-permute-done.6.refs_4_ = bf16[2,2,128,256]{3,2,1,0:T(8,128)(2,1)S(1)} collective-permute-done((bf16[2,2,128,256]{3,2,1,0:T(8,128)(2,1)S(1)}, bf16[2,2,128,256]{3,2,1,0:T(8,128)(2,1)S(1)}, u32[]{:S(2)}, u32[]{:S(2)}) %collective-permute-start.6) | collective-permute-done | bytes 262176 | tf_op jit(solution)/shard_map/ppermute | solution.py:386
  35.9 0.9 %collective-permute-start.12 = (bf16[2,2,128,256]{3,2,1,0:T(8,128)(2,1)S(1)}, bf16[2,2,128,256]{3,2,1,0:T(8,128)(2,1)S(1)}, u32[]{:S(2)}, u32[]{:S(2)}) collective-permute-start(bf16[2,2,128,256]{3,2,1,0:T(8,128)(2,1)S(1)} %get-tuple-element.74), channel_id=1, source_target_pairs={{0,2},{1,3},{2,0},{3,1},{4,6},{5,7},{6,4},{7,5},{8,10},{9,11},{10,... | collective-permute-start | bytes 786440 | tf_op jit(solution)/shard_map/ppermute | solution.py:386
  36.7 1.5 %collective-permute-start.13 = (bf16[2,2,128,256]{3,2,1,0:T(8,128)(2,1)S(1)}, bf16[2,2,128,256]{3,2,1,0:T(8,128)(2,1)S(1)}, u32[]{:S(2)}, u32[]{:S(2)}) collective-permute-start(bf16[2,2,128,256]{3,2,1,0:T(8,128)(2,1)S(1)} %get-tuple-element.75), channel_id=1, source_target_pairs={{0,4},{1,5},{2,6},{3,7},{4,0},{5,1},{6,2},{7,3},{8,12},{9,13},{10,... | collective-permute-start | bytes 786440 | tf_op jit(solution)/shard_map/ppermute | solution.py:386
  38.2 1.2 %collective-permute-start.14 = (bf16[2,2,128,256]{3,2,1,0:T(8,128)(2,1)S(1)}, bf16[2,2,128,256]{3,2,1,0:T(8,128)(2,1)S(1)}, u32[]{:S(2)}, u32[]{:S(2)}) collective-permute-start(bf16[2,2,128,256]{3,2,1,0:T(8,128)(2,1)S(1)} %get-tuple-element.76), channel_id=1, source_target_pairs={{0,6},{1,7},{2,4},{3,5},{4,2},{5,3},{6,0},{7,1},{8,14},{9,15},{10,... | collective-permute-start | bytes 786440 | tf_op jit(solution)/shard_map/ppermute | solution.py:386
  39.4 4.8 %conv.3 = (bf16[2,2,128,256]{3,2,1,0:T(8,128)(2,1)S(1)}, bf16[2,2,128,256]{3,2,1,0:T(8,128)(2,1)S(1)}, bf16[2,2,128,256]{3,2,1,0:T(8,128)(2,1)S(1)}, bf16[2,2,12...) custom-call(s32[2]{0:T(128)S(1)} %pad_add_fusion.me, ...), custom_call_target="tpu_custom_call", output_to_operand_aliasing={{4}: (9, {}), {5}: (10, {})} | custom-call | bytes 1024 | tf_op jit(solution)/shard_map/conv/pallas_call | solution.py:266
  44.2 1.6 %collective-permute-start.16 = (bf16[2,256,512]{2,1,0:T(8,128)(2,1)S(1)}, bf16[2,256,512]{2,1,0:T(8,128)(2,1)S(1)}, u32[]{:S(2)}, u32[]{:S(2)}) collective-permute-start(bf16[2,256,512]{2,1,0:T(8,128)(2,1)S(1)} %get-tuple-element.94), channel_id=1, source_target_pairs={{0,8},{8,0},{16,24},{24,16},{1,9},{9,1},{17,25},{25,17},{2,10},{10... | collective-permute-start | bytes 1572872 | tf_op jit(solution)/shard_map/ppermute | solution.py:358
  45.8 1.8 %collective-permute-start.10 = (bf16[2,2,128,256]{3,2,1,0:T(8,128)(2,1)S(1)}, bf16[2,2,128,256]{3,2,1,0:T(8,128)(2,1)S(1)}, u32[]{:S(2)}, u32[]{:S(2)}) collective-permute-start(bf16[2,2,128,256]{3,2,1,0:T(8,128)(2,1)S(1)} %get-tuple-element.73), channel_id=1, source_target_pairs={{0,6},{1,7},{2,4},{3,5},{4,2},{5,3},{6,0},{7,1},{8,14},{9,15},{10,... | collective-permute-start | bytes 786440 | tf_op jit(solution)/shard_map/ppermute | solution.py:386
  47.6 0.5 collective-permute-start.8
  48.1 8.1 %collective-permute-done.13.refs_2_ = bf16[2,2,128,256]{3,2,1,0:T(8,128)(2,1)S(1)} collective-permute-done((bf16[2,2,128,256]{3,2,1,0:T(8,128)(2,1)S(1)}, bf16[2,2,128,256]{3,2,1,0:T(8,128)(2,1)S(1)}, u32[]{:S(2)}, u32[]{:S(2)}) %collective-permute-start.13) | collective-permute-done | bytes 262176 | tf_op jit(solution)/shard_map/ppermute | solution.py:386
  56.3 2.0 %collective-permute-start.9 = (bf16[2,2,128,256]{3,2,1,0:T(8,128)(2,1)S(1)}, bf16[2,2,128,256]{3,2,1,0:T(8,128)(2,1)S(1)}, u32[]{:S(2)}, u32[]{:S(2)}) collective-permute-start(bf16[2,2,128,256]{3,2,1,0:T(8,128)(2,1)S(1)} %get-tuple-element.72), channel_id=1, source_target_pairs={{0,4},{1,5},{2,6},{3,7},{4,0},{5,1},{6,2},{7,3},{8,12},{9,13},{10,... | collective-permute-start | bytes 786440 | tf_op jit(solution)/shard_map/ppermute | solution.py:386
  58.4 3.1 %collective-permute-done.8.refs_1_ = bf16[2,2,128,256]{3,2,1,0:T(8,128)(2,1)S(1)} collective-permute-done((bf16[2,2,128,256]{3,2,1,0:T(8,128)(2,1)S(1)}, bf16[2,2,128,256]{3,2,1,0:T(8,128)(2,1)S(1)}, u32[]{:S(2)}, u32[]{:S(2)}) %collective-permute-start.8) | collective-permute-done | bytes 262176 | tf_op jit(solution)/shard_map/ppermute | solution.py:386
  61.5 1.2 %collective-permute-done.9.refs_2_ = bf16[2,2,128,256]{3,2,1,0:T(8,128)(2,1)S(1)} collective-permute-done((bf16[2,2,128,256]{3,2,1,0:T(8,128)(2,1)S(1)}, bf16[2,2,128,256]{3,2,1,0:T(8,128)(2,1)S(1)}, u32[]{:S(2)}, u32[]{:S(2)}) %collective-permute-start.9) | collective-permute-done | bytes 262176 | tf_op jit(solution)/shard_map/ppermute | solution.py:386
  62.8 0.1 add_grads.1
  62.9 2.7 %collective-permute-start.17 = (bf16[1,256,512]{2,1,0:T(8,128)(2,1)S(1)}, bf16[1,256,512]{2,1,0:T(8,128)(2,1)S(1)}, u32[]{:S(2)}, u32[]{:S(2)}) collective-permute-start(bf16[1,256,512]{2,1,0:T(8,128)(2,1)S(1)} %get-tuple-element.96), channel_id=1, source_target_pairs={{0,16},{8,24},{16,0},{24,8},{1,17},{9,25},{17,1},{25,9},{2,18},{10... | collective-permute-start | bytes 786440 | tf_op jit(solution)/shard_map/ppermute | solution.py:358
  65.5 2.1 %gate.4 = (bf16[128,4096]{1,0:T(8,128)(2,1)}, bf16[128,4096]{1,0:T(8,128)(2,1)}, bf16[128,4096]{1,0:T(8,128)(2,1)}, bf16[128,4096]{1,0:T(8,128)(2,1)}) custom-call(s32[2]{0:T(128)S(1)} %pad_add_fusion.me, bf16[128,4096]{1,0:T(8,128)(2,1)S(1)} %get-tuple-element.51.query, bf16[128,4096]{1,0:T(8,128)(2,1)S(1)} %get-tuple-element.52.grad, ...), custom_call_target="tpu_custom_call" | custom-call | bytes 1024 | tf_op jit(solution)/shard_map/gate/pallas_call | solution.py:325
  67.7 2.1 %gate.5 = (bf16[128,4096]{1,0:T(8,128)(2,1)}, bf16[128,4096]{1,0:T(8,128)(2,1)}, bf16[128,4096]{1,0:T(8,128)(2,1)}, bf16[128,4096]{1,0:T(8,128)(2,1)}) custom-call(s32[2]{0:T(128)S(1)} %pad_add_fusion.me, bf16[128,4096]{1,0:T(8,128)(2,1)S(1)} %get-tuple-element.51.query, ...), custom_call_target="tpu_custom_call", output_to_operand_aliasing={{0}: (7, {}), {1}: (8, {}), {2}: (9, {}), {3}: (10, {})} | custom-call | bytes 1024 | tf_op jit(solution)/shard_map/gate/pallas_call | solution.py:325
  69.8 2.1 %gate.6 = (bf16[128,4096]{1,0:T(8,128)(2,1)}, bf16[128,4096]{1,0:T(8,128)(2,1)}, bf16[128,4096]{1,0:T(8,128)(2,1)}, bf16[128,4096]{1,0:T(8,128)(2,1)}) custom-call(s32[2]{0:T(128)S(1)} %pad_add_fusion.me, bf16[128,4096]{1,0:T(8,128)(2,1)S(1)} %get-tuple-element.51.query, ...), custom_call_target="tpu_custom_call", output_to_operand_aliasing={{0}: (10, {}), {1}: (11, {}), {2}: (12, {}), {3}: (13, {})} | custom-call | bytes 1024 | tf_op jit(solution)/shard_map/gate/pallas_call | solution.py:325
  72.0 6.2 %collective-permute-done.17.got = bf16[1,256,512]{2,1,0:T(8,128)(2,1)S(1)} collective-permute-done((bf16[1,256,512]{2,1,0:T(8,128)(2,1)S(1)}, bf16[1,256,512]{2,1,0:T(8,128)(2,1)S(1)}, u32[]{:S(2)}, u32[]{:S(2)}) %collective-permute-start.17) | collective-permute-done | bytes 262176 | tf_op jit(solution)/shard_map/ppermute | solution.py:358
  78.2 1.1 %turn_grads.1 = f32[512,256]{1,0:T(8,128)} custom-call(f32[1,256,512]{2,1,0:T(8,128)S(1)} %get-tuple-element.95.keep, bf16[1,256,512]{2,1,0:T(8,128)(2,1)S(1)} %collective-permute-done.17.got), custom_call_target="tpu_custom_call" | custom-call | bytes 1024 | tf_op jit(solution)/shard_map/turn_grads/pallas_call | solution.py:372
  79.2 2.1 %gate.7 = (bf16[128,4096]{1,0:T(8,128)(2,1)}, bf16[128,4096]{1,0:T(8,128)(2,1)}, bf16[128,4096]{1,0:T(8,128)(2,1)}, bf16[128,4096]{1,0:T(8,128)(2,1)}) custom-call(s32[2]{0:T(128)S(1)} %pad_add_fusion.me, bf16[128,4096]{1,0:T(8,128)(2,1)S(1)} %get-tuple-element.51.query, ...), custom_call_target="tpu_custom_call", output_to_operand_aliasing={{0}: (7, {}), {1}: (8, {}), {2}: (9, {}), {3}: (10, {})} | custom-call | bytes 1024 | tf_op jit(solution)/shard_map/gate/pallas_call | solution.py:325
  (28 shorter events, 0.5 us)
Async XLA Ops:
  0.6 23.4 %copy-start = (bf16[8,256,256]{2,1,0:T(8,128)(2,1)S(1)}, bf16[8,256,256]{2,1,0:T(8,128)(2,1)}, u32[]{:S(2)}) copy-start(bf16[8,256,256]{2,1,0:T(8,128)(2,1)} %constant.12.clone.fwd.refs_6_) | copy-start | bytes 3145732
  0.6 23.4 %copy-start.1 = (f32[512,1024]{1,0:T(8,128)S(1)}, f32[512,1024]{1,0:T(8,128)}, u32[]{:S(2)}) copy-start(f32[512,1024]{1,0:T(8,128)} %filt.1) | copy-start | bytes 6291460
  3.9 10.1 %collective-permute-start = (bf16[2,2,128,256]{3,2,1,0:T(8,128)(2,1)S(1)}, bf16[2,2,128,256]{3,2,1,0:T(8,128)(2,1)S(1)}, u32[]{:S(2)}, u32[]{:S(2)}) collective-permute-start(bf16[2,2,128,256]{3,2,1,0:T(8,128)(2,1)S(1)} %get-tuple-element.56), channel_id=1, source_target_pairs={{0,2},{1,3},{2,0},{3,1},{4,6},{5,7},{6,4},{7,5},{8,10},{9,11},{10,... | collective-permute-start | bytes 786440 | tf_op jit(solution)/shard_map/ppermute | solution.py:386
  6.9 13.4 %collective-permute-start.1 = (bf16[2,2,128,256]{3,2,1,0:T(8,128)(2,1)S(1)}, bf16[2,2,128,256]{3,2,1,0:T(8,128)(2,1)S(1)}, u32[]{:S(2)}, u32[]{:S(2)}) collective-permute-start(bf16[2,2,128,256]{3,2,1,0:T(8,128)(2,1)S(1)} %get-tuple-element.57), channel_id=1, source_target_pairs={{0,4},{1,5},{2,6},{3,7},{4,0},{5,1},{6,2},{7,3},{8,12},{9,13},{10,... | collective-permute-start | bytes 786440 | tf_op jit(solution)/shard_map/ppermute | solution.py:386
  8.5 11.9 %collective-permute-start.2 = (bf16[2,2,128,256]{3,2,1,0:T(8,128)(2,1)S(1)}, bf16[2,2,128,256]{3,2,1,0:T(8,128)(2,1)S(1)}, u32[]{:S(2)}, u32[]{:S(2)}) collective-permute-start(bf16[2,2,128,256]{3,2,1,0:T(8,128)(2,1)S(1)} %get-tuple-element.58), channel_id=1, source_target_pairs={{0,6},{1,7},{2,4},{3,5},{4,2},{5,3},{6,0},{7,1},{8,14},{9,15},{10,... | collective-permute-start | bytes 786440 | tf_op jit(solution)/shard_map/ppermute | solution.py:386
  20.3 7.3 %copy-start.2 = (bf16[8,128,256]{2,1,0:T(8,128)(2,1)S(1)}, bf16[8,128,256]{2,1,0:T(8,128)(2,1)}, u32[]{:S(2)}) copy-start(bf16[8,128,256]{2,1,0:T(8,128)(2,1)} %constant.13.clone.refs_7_) | copy-start | bytes 1572868
  20.4 7.2 %collective-permute-start.3 = (bf16[4,2,128,256]{3,2,1,0:T(8,128)(2,1)S(1)}, bf16[4,2,128,256]{3,2,1,0:T(8,128)(2,1)S(1)}, u32[]{:S(2)}, u32[]{:S(2)}) collective-permute-start(bf16[4,2,128,256]{3,2,1,0:T(8,128)(2,1)S(1)} %pack.4), channel_id=1, source_target_pairs={{0,1},{1,0},{2,3},{3,2},{4,5},{5,4},{6,7},{7,6},{8,9},{9,8},{10,11... | collective-permute-start | bytes 1572872 | tf_op jit(solution)/shard_map/ppermute | solution.py:406
  20.4 12.0 %collective-permute-start.4 = (bf16[2,2,128,256]{3,2,1,0:T(8,128)(2,1)S(1)}, bf16[2,2,128,256]{3,2,1,0:T(8,128)(2,1)S(1)}, u32[]{:S(2)}, u32[]{:S(2)}) collective-permute-start(bf16[2,2,128,256]{3,2,1,0:T(8,128)(2,1)S(1)} %get-tuple-element.61), channel_id=1, source_target_pairs={{0,2},{1,3},{2,0},{3,1},{4,6},{5,7},{6,4},{7,5},{8,10},{9,11},{10,... | collective-permute-start | bytes 786440 | tf_op jit(solution)/shard_map/ppermute | solution.py:386
  21.7 12.4 %collective-permute-start.5 = (bf16[2,2,128,256]{3,2,1,0:T(8,128)(2,1)S(1)}, bf16[2,2,128,256]{3,2,1,0:T(8,128)(2,1)S(1)}, u32[]{:S(2)}, u32[]{:S(2)}) collective-permute-start(bf16[2,2,128,256]{3,2,1,0:T(8,128)(2,1)S(1)} %get-tuple-element.62), channel_id=1, source_target_pairs={{0,4},{1,5},{2,6},{3,7},{4,0},{5,1},{6,2},{7,3},{8,12},{9,13},{10,... | collective-permute-start | bytes 786440 | tf_op jit(solution)/shard_map/ppermute | solution.py:386
  22.6 13.2 %collective-permute-start.6 = (bf16[2,2,128,256]{3,2,1,0:T(8,128)(2,1)S(1)}, bf16[2,2,128,256]{3,2,1,0:T(8,128)(2,1)S(1)}, u32[]{:S(2)}, u32[]{:S(2)}) collective-permute-start(bf16[2,2,128,256]{3,2,1,0:T(8,128)(2,1)S(1)} %get-tuple-element.63), channel_id=1, source_target_pairs={{0,6},{1,7},{2,4},{3,5},{4,2},{5,3},{6,0},{7,1},{8,14},{9,15},{10,... | collective-permute-start | bytes 786440 | tf_op jit(solution)/shard_map/ppermute | solution.py:386
  35.8 3.6 %collective-permute-start.7 = (bf16[4,2,128,256]{3,2,1,0:T(8,128)(2,1)S(1)}, bf16[4,2,128,256]{3,2,1,0:T(8,128)(2,1)S(1)}, u32[]{:S(2)}, u32[]{:S(2)}) collective-permute-start(bf16[4,2,128,256]{3,2,1,0:T(8,128)(2,1)S(1)} %pack.5), channel_id=1, source_target_pairs={{0,1},{1,0},{2,3},{3,2},{4,5},{5,4},{6,7},{7,6},{8,9},{9,8},{10,11... | collective-permute-start | bytes 1572872 | tf_op jit(solution)/shard_map/ppermute | solution.py:406
  35.9 11.7 %collective-permute-start.12 = (bf16[2,2,128,256]{3,2,1,0:T(8,128)(2,1)S(1)}, bf16[2,2,128,256]{3,2,1,0:T(8,128)(2,1)S(1)}, u32[]{:S(2)}, u32[]{:S(2)}) collective-permute-start(bf16[2,2,128,256]{3,2,1,0:T(8,128)(2,1)S(1)} %get-tuple-element.74), channel_id=1, source_target_pairs={{0,2},{1,3},{2,0},{3,1},{4,6},{5,7},{6,4},{7,5},{8,10},{9,11},{10,... | collective-permute-start | bytes 786440 | tf_op jit(solution)/shard_map/ppermute | solution.py:386
  36.7 19.5 %collective-permute-start.13 = (bf16[2,2,128,256]{3,2,1,0:T(8,128)(2,1)S(1)}, bf16[2,2,128,256]{3,2,1,0:T(8,128)(2,1)S(1)}, u32[]{:S(2)}, u32[]{:S(2)}) collective-permute-start(bf16[2,2,128,256]{3,2,1,0:T(8,128)(2,1)S(1)} %get-tuple-element.75), channel_id=1, source_target_pairs={{0,4},{1,5},{2,6},{3,7},{4,0},{5,1},{6,2},{7,3},{8,12},{9,13},{10,... | collective-permute-start | bytes 786440 | tf_op jit(solution)/shard_map/ppermute | solution.py:386
  38.2 20.0 %collective-permute-start.14 = (bf16[2,2,128,256]{3,2,1,0:T(8,128)(2,1)S(1)}, bf16[2,2,128,256]{3,2,1,0:T(8,128)(2,1)S(1)}, u32[]{:S(2)}, u32[]{:S(2)}) collective-permute-start(bf16[2,2,128,256]{3,2,1,0:T(8,128)(2,1)S(1)} %get-tuple-element.76), channel_id=1, source_target_pairs={{0,6},{1,7},{2,4},{3,5},{4,2},{5,3},{6,0},{7,1},{8,14},{9,15},{10,... | collective-permute-start | bytes 786440 | tf_op jit(solution)/shard_map/ppermute | solution.py:386
  44.2 21.4 %copy-start.3 = (f32[4096]{0:T(1024)S(1)}, f32[4096]{0:T(1024)}, u32[]{:S(2)}) copy-start(f32[4096]{0:T(1024)} %param.13) | copy-start | bytes 49156
  44.2 18.6 %collective-permute-start.16 = (bf16[2,256,512]{2,1,0:T(8,128)(2,1)S(1)}, bf16[2,256,512]{2,1,0:T(8,128)(2,1)S(1)}, u32[]{:S(2)}, u32[]{:S(2)}) collective-permute-start(bf16[2,256,512]{2,1,0:T(8,128)(2,1)S(1)} %get-tuple-element.94), channel_id=1, source_target_pairs={{0,8},{8,0},{16,24},{24,16},{1,9},{9,1},{17,25},{25,17},{2,10},{10... | collective-permute-start | bytes 1572872 | tf_op jit(solution)/shard_map/ppermute | solution.py:358
  45.8 12.5 %collective-permute-start.10 = (bf16[2,2,128,256]{3,2,1,0:T(8,128)(2,1)S(1)}, bf16[2,2,128,256]{3,2,1,0:T(8,128)(2,1)S(1)}, u32[]{:S(2)}, u32[]{:S(2)}) collective-permute-start(bf16[2,2,128,256]{3,2,1,0:T(8,128)(2,1)S(1)} %get-tuple-element.73), channel_id=1, source_target_pairs={{0,6},{1,7},{2,4},{3,5},{4,2},{5,3},{6,0},{7,1},{8,14},{9,15},{10,... | collective-permute-start | bytes 786440 | tf_op jit(solution)/shard_map/ppermute | solution.py:386
  47.6 13.9 %collective-permute-start.8 = (bf16[2,2,128,256]{3,2,1,0:T(8,128)(2,1)S(1)}, bf16[2,2,128,256]{3,2,1,0:T(8,128)(2,1)S(1)}, u32[]{:S(2)}, u32[]{:S(2)}) collective-permute-start(bf16[2,2,128,256]{3,2,1,0:T(8,128)(2,1)S(1)} %get-tuple-element.71), channel_id=1, source_target_pairs={{0,2},{1,3},{2,0},{3,1},{4,6},{5,7},{6,4},{7,5},{8,10},{9,11},{10,... | collective-permute-start | bytes 786440 | tf_op jit(solution)/shard_map/ppermute | solution.py:386
  56.3 6.4 %collective-permute-start.9 = (bf16[2,2,128,256]{3,2,1,0:T(8,128)(2,1)S(1)}, bf16[2,2,128,256]{3,2,1,0:T(8,128)(2,1)S(1)}, u32[]{:S(2)}, u32[]{:S(2)}) collective-permute-start(bf16[2,2,128,256]{3,2,1,0:T(8,128)(2,1)S(1)} %get-tuple-element.72), channel_id=1, source_target_pairs={{0,4},{1,5},{2,6},{3,7},{4,0},{5,1},{6,2},{7,3},{8,12},{9,13},{10,... | collective-permute-start | bytes 786440 | tf_op jit(solution)/shard_map/ppermute | solution.py:386
  58.3 9.4 %collective-permute-start.15 = (bf16[4,2,128,256]{3,2,1,0:T(8,128)(2,1)S(1)}, bf16[4,2,128,256]{3,2,1,0:T(8,128)(2,1)S(1)}, u32[]{:S(2)}, u32[]{:S(2)}) collective-permute-start(bf16[4,2,128,256]{3,2,1,0:T(8,128)(2,1)S(1)} %pack.7), channel_id=1, source_target_pairs={{0,1},{1,0},{2,3},{3,2},{4,5},{5,4},{6,7},{7,6},{8,9},{9,8},{10,11... | collective-permute-start | bytes 1572872 | tf_op jit(solution)/shard_map/ppermute | solution.py:406
  62.7 16.6 %collective-permute-start.11 = (bf16[4,2,128,256]{3,2,1,0:T(8,128)(2,1)S(1)}, bf16[4,2,128,256]{3,2,1,0:T(8,128)(2,1)S(1)}, u32[]{:S(2)}, u32[]{:S(2)}) collective-permute-start(bf16[4,2,128,256]{3,2,1,0:T(8,128)(2,1)S(1)} %pack.6), channel_id=1, source_target_pairs={{0,1},{1,0},{2,3},{3,2},{4,5},{5,4},{6,7},{7,6},{8,9},{9,8},{10,11... | collective-permute-start | bytes 1572872 | tf_op jit(solution)/shard_map/ppermute | solution.py:406
  62.9 15.3 %collective-permute-start.17 = (bf16[1,256,512]{2,1,0:T(8,128)(2,1)S(1)}, bf16[1,256,512]{2,1,0:T(8,128)(2,1)S(1)}, u32[]{:S(2)}, u32[]{:S(2)}) collective-permute-start(bf16[1,256,512]{2,1,0:T(8,128)(2,1)S(1)} %get-tuple-element.96), channel_id=1, source_target_pairs={{0,16},{8,24},{16,0},{24,8},{1,17},{9,25},{17,1},{25,9},{2,18},{10... | collective-permute-start | bytes 786440 | tf_op jit(solution)/shard_map/ppermute | solution.py:358

commit v10 on v9

--- a/solution.py
+++ b/solution.py
@@ -95,7 +95,7 @@
 
 def sources(n, got, passed):
     straight = [(chip, got[i].at[0]) for i, chip in enumerate(chips(n))]
-    return straight + [(chip + 1, passed.at[i]) for i, chip in enumerate(chips(n))]
+    return straight + [(chip + 1, passed[i]) for i, chip in enumerate(chips(n))]
 
 
 def peer_columns(me, j, half, width, lane=0, lanes=None):
@@ -200,17 +200,16 @@
 
 def conv_kernel(n, d, half, me, *refs):
     count = n // 2
-    got, (passed, filt, fwd, back) = refs[:count], refs[count : count + 4]
+    got, passed, (filt, fwd, back) = refs[:count], refs[count:n], refs[n : n + 3]
     refs = refs[-(count + 2 + 6) :]
     out, (keep, send), (nat, x, u, y, turned, grad) = refs[:count], refs[count : count + 2], refs[count + 2 :]
-    rows, width = passed.shape[2:]
+    rows, width = passed[0].shape[1:]
     blocks = sources(n, got, passed)
     m2 = x.shape[2]
     per = keep.shape[1] // CLASSES
     groups = lane_groups(width)
     step_rows = m2 // CLASSES
     part_rows = rows // CLASSES
-    chans = slice(half * width, (half + 1) * width)
 
     for a in range(2):
         for g, lanes in enumerate(groups):
@@ -253,22 +252,22 @@
         for c in range(CLASSES):
             part = grad[c, pl.ds(at, per)]
             if j % 2:
-                send[j // 2, c * per : (c + 1) * per, chans] = part.astype(BF16)
+                send[j // 2, c * per : (c + 1) * per] = part.astype(BF16)
             else:
-                keep[j // 2, c * per : (c + 1) * per, chans] = part
-
-
-def conv(n, d, half, me, got, passed, filt, fwd, back, before):
+                keep[j // 2, c * per : (c + 1) * per] = part
+
+
+def conv(n, d, half, me, got, passed, filt, fwd, back):
     _, _, rows, width = got[0].shape
     length = n * rows
     m2 = length // CLASSES
     count = n // 2
     out = pl.pallas_call(
         functools.partial(conv_kernel, n, d, half),
-        in_specs=[SMEM] + [VMEM] * (count + 4 + len(before)),
+        in_specs=[SMEM] + [VMEM] * (n + 3),
         out_specs=[VMEM] * (count + 2),
         out_shape=[pltpu.VMEM((2, 2, rows, width), BF16)] * count
-        + [pltpu.VMEM((d // 2, length // d, HALVES * width), dtype) for dtype in (F32, BF16)],
+        + [pltpu.VMEM((d // 2, length // d, width), dtype) for dtype in (F32, BF16)],
         scratch_shapes=[
             pltpu.VMEM((2, width // 128, length, 128), F32),
             pltpu.VMEM((2, CLASSES, m2, width), BF16),
@@ -277,11 +276,10 @@
             pltpu.VMEM((2, CLASSES, m2, width), BF16),
             pltpu.VMEM((CLASSES, m2, width), F32),
         ],
-        input_output_aliases={count + 5 + i: count + i for i in range(len(before))},
         cost_estimate=SMALL_COST,
         compiler_params=CONV_PARAMS,
         name="conv",
-    )(me, *got, passed, filt, fwd, back, *before)
+    )(me, *got, *passed, filt, fwd, back)
     return out[:count], out[count:]
 
 
@@ -292,12 +290,12 @@
     return scratch[...]
 
 
-def gate_kernel(half, js, picks, me, query, grad, value, key, gain, *refs):
+def gate_kernel(half, js, straight, me, query, grad, value, key, gain, *refs):
     outs, (sent, sems, nat) = refs[-7:-3], refs[-3:]
     rows, width = sent.shape[2:]
     copies = []
-    for i, (j, (array, place)) in enumerate(zip(js, picks)):
-        block = refs[array].at[place]
+    for i, j in enumerate(js):
+        block = refs[i].at[0] if straight else refs[i]
         for g, lanes in enumerate(lane_groups(width)):
             cols = peer_columns(me, j, half, width, lanes.start, 128)
             scale = gain[:, cols]
@@ -320,10 +318,11 @@
         copy.wait()
 
 
-def gate(half, js, picks, me, arrays, gain, got, outs):
+def gate(half, js, me, arrays, gain, got, outs):
     rows, width = got[0].shape[-2:]
+    straight = got[0].ndim == 4
     return pl.pallas_call(
-        functools.partial(gate_kernel, half, js, picks),
+        functools.partial(gate_kernel, half, js, straight),
         in_specs=[SMEM] + [VMEM] * (5 + len(got)) + [HBM] * len(outs),
         out_specs=[HBM] * 4,
         out_shape=[jax.ShapeDtypeStruct(arrays[0].shape, BF16)] * 4,
@@ -345,40 +344,46 @@
         new_send[i] = (keep[2 * i + 1] + got[2 * i + 1].astype(F32)).astype(BF16)
 
 
-def turn_kernel(keep, got, out, nat):
-    for g, lanes in enumerate(lane_groups(keep.shape[2])):
-        total = keep[0, :, lanes] + got[0, :, lanes].astype(F32)
-        out[lanes, :] = natural(nat.at[g], total).T
-
-
-def sum_grads(d, keep, send):
-    _, per, chans = keep.shape
-    bit = 1
-    while True:
-        got = resident(lax.ppermute(send, "dp", [(i, i ^ bit) for i in range(d)]))
-        if keep.shape[0] == 1:
-            break
-        shape = (keep.shape[0] // 2, per, chans)
-        keep, send = pl.pallas_call(
-            add_kernel,
-            in_specs=[VMEM] * 2,
-            out_specs=[VMEM] * 2,
-            out_shape=[pltpu.VMEM(shape, F32), pltpu.VMEM(shape, BF16)],
-            cost_estimate=SMALL_COST,
-        compiler_params=PARAMS,
-            name="add_grads",
-        )(keep, got)
-        bit *= 2
+def trade(d, bit, send):
+    return resident(lax.ppermute(send, "dp", [(i, i ^ bit) for i in range(d)]))
+
+
+def add_grads(keep, got):
+    shape = (keep.shape[0] // 2, *keep.shape[1:])
+    return pl.pallas_call(
+        add_kernel,
+        in_specs=[VMEM] * 2,
+        out_specs=[VMEM] * 2,
+        out_shape=[pltpu.VMEM(shape, F32), pltpu.VMEM(shape, BF16)],
+        cost_estimate=SMALL_COST,
+        compiler_params=PARAMS,
+        name="add_grads",
+    )(keep, got)
+
+
+def turn_kernel(*refs):
+    out, nat = refs[-2:]
+    width = refs[0].shape[2]
+    for half in range(HALVES):
+        keep, got = refs[2 * half : 2 * half + 2]
+        for g, lanes in enumerate(lane_groups(width)):
+            total = keep[0, :, lanes] + got[0, :, lanes].astype(F32)
+            to = slice(half * width + lanes.start, half * width + lanes.stop)
+            out[to, :] = natural(nat.at[half, g], total).T
+
+
+def turn_grads(halves):
+    _, per, width = halves[0][0].shape
     return pl.pallas_call(
         turn_kernel,
-        in_specs=[VMEM] * 2,
+        in_specs=[VMEM] * (2 * HALVES),
         out_specs=VMEM,
-        out_shape=jax.ShapeDtypeStruct((chans, per), F32),
-        scratch_shapes=[pltpu.VMEM((chans // 128, per, 128), F32)],
+        out_shape=jax.ShapeDtypeStruct((HALVES * width, per), F32),
+        scratch_shapes=[pltpu.VMEM((HALVES, width // 128, per, 128), F32)],
         cost_estimate=SMALL_COST,
         compiler_params=PARAMS,
         name="turn_grads",
-    )(keep, got)
+    )(*halves[0], *halves[1])
 
 
 def across(n, blocks):
@@ -389,21 +394,22 @@
 
 
 def pack_kernel(*refs):
-    for i, ref in enumerate(refs[:-1]):
-        refs[-1][i] = ref[1]
+    count = len(refs) // 2
+    for ref, out in zip(refs[:count], refs[count:]):
+        out[...] = ref[1]
 
 
 def inside(n, got):
     packed = pl.pallas_call(
         pack_kernel,
         in_specs=[VMEM] * len(got),
-        out_specs=VMEM,
-        out_shape=pltpu.VMEM((len(got), *got[0].shape[1:]), BF16),
+        out_specs=[VMEM] * len(got),
+        out_shape=[pltpu.VMEM(got[0].shape[1:], BF16)] * len(got),
         cost_estimate=SMALL_COST,
         compiler_params=PARAMS,
         name="pack",
     )(*got)
-    return resident(lax.ppermute(packed, "ctx", [(i, i ^ 1) for i in range(n)]))
+    return [resident(lax.ppermute(x, "ctx", [(i, i ^ 1) for i in range(n)])) for x in packed]
 
 
 def after_kernel(*refs):
@@ -435,22 +441,30 @@
     arrays = query, grad, value, key
     spec = filter_spectra(filters, fwd, [])
     got = [across(n, blocks) for blocks in sent]
-    mixed, sums = [], []
-    for half in range(HALVES):
-        if mixed:
-            got[half] = after(mixed[0][:1], got[half])
-        passed = inside(n, got[half])
-        blocks, sums = conv(n, d, half, me, got[half], passed, spec, fwd, back, sums)
-        mixed.append(across(n, blocks))
-    grad_filter = sum_grads(d, *sums)
-
-    straight = [(i, 0) for i in range(n // 2)]
-    outs = []
-    for half in range(HALVES):
-        passed = inside(n, mixed[half])
-        outs = gate(half, chips(n), straight, me, arrays, gain, mixed[half], outs)
-        handed = [(0, i) for i in range(n // 2)]
-        outs = gate(half, [c + 1 for c in chips(n)], handed, me, arrays, gain, [passed], outs)
+    bits = [1 << b for b in range(d.bit_length() - 1)]
+    blocks, (keep, send) = conv(n, d, 0, me, got[0], inside(n, got[0]), spec, fwd, back)
+    first = across(n, blocks)
+    keep, send = add_grads(keep, trade(d, 1, send))
+    for bit in bits[1:-1]:
+        keep, send = add_grads(keep, trade(d, bit, send))
+    sums = [(keep, trade(d, bits[-1], send))]
+
+    got[1] = after(blocks[:1], got[1])
+    blocks, (keep, send) = conv(n, d, 1, me, got[1], inside(n, got[1]), spec, fwd, back)
+    second = across(n, after(sums[0][:1], blocks))
+    keep, send = add_grads(keep, trade(d, 1, send))
+    for bit in bits[1:-1]:
+        keep, send = add_grads(keep, trade(d, bit, send))
+    sums.append((keep, trade(d, bits[-1], send)))
+
+    odd = [c + 1 for c in chips(n)]
+    passed = inside(n, first)
+    outs = gate(0, chips(n), me, arrays, gain, after([keep, sums[0][1]], first), [])
+    outs = gate(0, odd, me, arrays, gain, passed, outs)
+    grad_filter = turn_grads(sums)
+    passed = inside(n, second)
+    outs = gate(1, chips(n), me, arrays, gain, second, outs)
+    outs = gate(1, odd, me, arrays, gain, passed, outs)
     return *(x[None] for x in outs), grad_filter
 
 

time: 81.7 us -> 79.1 us (0.968)
  waiting for transfers between devices: 33.8 us -> 23.9 us
  starting transfers between devices: 20.5 us -> 27.8 us
    ppermute x12, waiting for transfers between devices: 27.6 us -> 20.9 us  [across(): lax.ppermute(block, 'ctx', [(i, i ^ chip) for i in range(n)])]
    ppermute x6 -> x20, starting transfers between devices: 4.58 us -> 10.5 us  [the longest x4 7.33 us: trade(): return resident(lax.ppermute(send, 'dp', [(i, i ^ bit) for i in range(d)]))]
    ppermute x6 -> x20, waiting for transfers between devices: 6.21 us -> 3.06 us  [the longest x4 2.19 us: trade(): return resident(lax.ppermute(send, 'dp', [(i, i ^ bit) for i in range(d)]))]
    ppermute x12, starting transfers between devices: 15.9 us -> 17.3 us  [across(): lax.ppermute(block, 'ctx', [(i, i ^ chip) for i in range(n)])]
    pallas_call x10 -> x11, Pallas kernels: 9.85 us -> 9.82 us  [the longest x4 8.53 us: gate(): pl.pallas_call(functools.partial(gate_kernel, half, js, straight), in_spe...]
  transfers between devices with their start and end apart: 18 -> 32, of which waited for: 8 -> 9; matrix products, arithmetic and copies ran while one was open for 0% -> 0% of each run, Pallas kernels for 25% -> 26%
where the time goes in v10:
time: 79.1 us; the launch traced here: 79 us
  starting transfers between devices  27.8 us (35%)
  Pallas kernels  26.1 us (33%)
  waiting for transfers between devices  23.9 us (30%)
  between operations  1.04 us (1%)
    ppermute x12, waiting for transfers between devices, across(): lax.ppermute(block, 'ctx', [(i, i ^ chip) for i in range(n)])  20.9 us
    ppermute x12, starting transfers between devices, across(): lax.ppermute(block, 'ctx', [(i, i ^ chip) for i in range(n)])  17.3 us
    pallas_call x2, Pallas kernels, conv(): pl.pallas_call(functools.partial(conv_kernel, n, d, half), in_specs=[SMEM...  9.5 us
    pallas_call x4, Pallas kernels, gate(): pl.pallas_call(functools.partial(gate_kernel, half, js, straight), in_spe...  8.53 us
    ppermute x4, starting transfers between devices, trade(): return resident(lax.ppermute(send, 'dp', [(i, i ^ bit) for i in range(d)]))  7.33 us
    pallas_call x1, Pallas kernels, filter_spectra(): pl.pallas_call(filter_kernel, in_specs=[VMEM] * (2 + len(arrived)), out_s...  3.59 us
    pallas_call x1, Pallas kernels, products(): pl.pallas_call(functools.partial(product_kernel, n), in_specs=[SMEM] + [H...  3.19 us
    ppermute x16, starting transfers between devices, inside(): lax.ppermute(x, 'ctx', [(i, i ^ 1) for i in range(n)])  3.19 us
  transfers between devices with their start and end apart: 32, of which 9 were waited for; matrix products, arithmetic and copies ran while one was open for 0% of the time, Pallas kernels for 26%

profile of v10, /device:TPU:0, one launch (start us, length us, event | category | flops | bytes accessed | tf_op | source)
XLA Modules:
  0.0 79.0 jit_solution(7389403238474657687)
XLA Ops:
  0.7 3.2 %products.1 = (bf16[128,4096]{1,0:T(8,128)(2,1)S(1)}, bf16[128,4096]{1,0:T(8,128)(2,1)S(1)}, bf16[128,4096]{1,0:T(8,128)(2,1)S(1)}, bf16[128,4096]{1,0:T(8,128)(...) custom-call(s32[2]{0:T(128)S(1)} %pad_add_fusion.me, ...), custom_call_target="tpu_custom_call" | custom-call | bytes 1024 | tf_op jit(solution)/shard_map/products/pallas_call | solution.py:139
  3.9 3.0 %collective-permute-start = (bf16[2,2,128,256]{3,2,1,0:T(8,128)(2,1)S(1)}, bf16[2,2,128,256]{3,2,1,0:T(8,128)(2,1)S(1)}, u32[]{:S(2)}, u32[]{:S(2)}) collective-permute-start(bf16[2,2,128,256]{3,2,1,0:T(8,128)(2,1)S(1)} %get-tuple-element.82), channel_id=1, source_target_pairs={{0,2},{1,3},{2,0},{3,1},{4,6},{5,7},{6,4},{7,5},{8,10},{9,11},{10,... | collective-permute-start | bytes 786440 | tf_op jit(solution)/shard_map/ppermute | solution.py:391
  6.9 1.5 %collective-permute-start.1 = (bf16[2,2,128,256]{3,2,1,0:T(8,128)(2,1)S(1)}, bf16[2,2,128,256]{3,2,1,0:T(8,128)(2,1)S(1)}, u32[]{:S(2)}, u32[]{:S(2)}) collective-permute-start(bf16[2,2,128,256]{3,2,1,0:T(8,128)(2,1)S(1)} %get-tuple-element.83), channel_id=1, source_target_pairs={{0,4},{1,5},{2,6},{3,7},{4,0},{5,1},{6,2},{7,3},{8,12},{9,13},{10,... | collective-permute-start | bytes 786440 | tf_op jit(solution)/shard_map/ppermute | solution.py:391
  8.5 5.6 %collective-permute-done.refs_1_ = bf16[2,2,128,256]{3,2,1,0:T(8,128)(2,1)S(1)} collective-permute-done((bf16[2,2,128,256]{3,2,1,0:T(8,128)(2,1)S(1)}, bf16[2,2,128,256]{3,2,1,0:T(8,128)(2,1)S(1)}, u32[]{:S(2)}, u32[]{:S(2)}) %collective-permute-start) | collective-permute-done | bytes 262176 | tf_op jit(solution)/shard_map/ppermute | solution.py:391
  14.1 6.2 %collective-permute-done.1.refs_2_ = bf16[2,2,128,256]{3,2,1,0:T(8,128)(2,1)S(1)} collective-permute-done((bf16[2,2,128,256]{3,2,1,0:T(8,128)(2,1)S(1)}, bf16[2,2,128,256]{3,2,1,0:T(8,128)(2,1)S(1)}, u32[]{:S(2)}, u32[]{:S(2)}) %collective-permute-start.1) | collective-permute-done | bytes 262176 | tf_op jit(solution)/shard_map/ppermute | solution.py:391
  20.9 1.5 %collective-permute-start.10 = (bf16[2,2,128,256]{3,2,1,0:T(8,128)(2,1)S(1)}, bf16[2,2,128,256]{3,2,1,0:T(8,128)(2,1)S(1)}, u32[]{:S(2)}, u32[]{:S(2)}) collective-permute-start(bf16[2,2,128,256]{3,2,1,0:T(8,128)(2,1)S(1)} %get-tuple-element.96), channel_id=1, source_target_pairs={{0,6},{1,7},{2,4},{3,5},{4,2},{5,3},{6,0},{7,1},{8,14},{9,15},{10,... | collective-permute-start | bytes 786440 | tf_op jit(solution)/shard_map/ppermute | solution.py:391
  22.4 1.5 %collective-permute-start.8 = (bf16[2,2,128,256]{3,2,1,0:T(8,128)(2,1)S(1)}, bf16[2,2,128,256]{3,2,1,0:T(8,128)(2,1)S(1)}, u32[]{:S(2)}, u32[]{:S(2)}) collective-permute-start(bf16[2,2,128,256]{3,2,1,0:T(8,128)(2,1)S(1)} %get-tuple-element.94), channel_id=1, source_target_pairs={{0,2},{1,3},{2,0},{3,1},{4,6},{5,7},{6,4},{7,5},{8,10},{9,11},{10,... | collective-permute-start | bytes 786440 | tf_op jit(solution)/shard_map/ppermute | solution.py:391
  25.0 3.6 %filter_spectra.1.refs_8_ = f32[2,8,256,256]{3,2,1,0:T(8,128)S(1)} custom-call(f32[512,1024]{1,0:T(8,128)S(1)} %copy-done.1, bf16[8,256,256]{2,1,0:T(8,128)(2,1)S(1)} %copy-done), custom_call_target="tpu_custom_call" | custom-call | bytes 1024 | tf_op jit(solution)/shard_map/filter_spectra/pallas_call | solution.py:186
  28.6 4.8 %conv.2 = (bf16[2,2,128,256]{3,2,1,0:T(8,128)(2,1)S(1)}, bf16[2,2,128,256]{3,2,1,0:T(8,128)(2,1)S(1)}, bf16[2,2,128,256]{3,2,1,0:T(8,128)(2,1)S(1)}, bf16[2,2,12...) custom-call(s32[2]{0:T(128)S(1)} %pad_add_fusion.me, ...), custom_call_target="tpu_custom_call" | custom-call | bytes 1024 | tf_op jit(solution)/shard_map/conv/pallas_call | solution.py:265
  33.4 2.5 %collective-permute-done.8.refs_2_ = bf16[2,2,128,256]{3,2,1,0:T(8,128)(2,1)S(1)} collective-permute-done((bf16[2,2,128,256]{3,2,1,0:T(8,128)(2,1)S(1)}, bf16[2,2,128,256]{3,2,1,0:T(8,128)(2,1)S(1)}, u32[]{:S(2)}, u32[]{:S(2)}) %collective-permute-start.8) | collective-permute-done | bytes 262176 | tf_op jit(solution)/shard_map/ppermute | solution.py:391
  36.5 1.6 %collective-permute-start.7 = (bf16[2,256,256]{2,1,0:T(8,128)(2,1)S(1)}, bf16[2,256,256]{2,1,0:T(8,128)(2,1)S(1)}, u32[]{:S(2)}, u32[]{:S(2)}) collective-permute-start(bf16[2,256,256]{2,1,0:T(8,128)(2,1)S(1)} %get-tuple-element.90), channel_id=1, source_target_pairs={{0,8},{8,0},{16,24},{24,16},{1,9},{9,1},{17,25},{25,17},{2,10},{10... | collective-permute-start | bytes 786440 | tf_op jit(solution)/shard_map/ppermute | solution.py:348
  38.0 1.1 %collective-permute-start.22 = (bf16[2,2,128,256]{3,2,1,0:T(8,128)(2,1)S(1)}, bf16[2,2,128,256]{3,2,1,0:T(8,128)(2,1)S(1)}, u32[]{:S(2)}, u32[]{:S(2)}) collective-permute-start(bf16[2,2,128,256]{3,2,1,0:T(8,128)(2,1)S(1)} %get-tuple-element.117), channel_id=1, source_target_pairs={{0,2},{1,3},{2,0},{3,1},{4,6},{5,7},{6,4},{7,5},{8,10},{9,11},{10,... | collective-permute-start | bytes 786440 | tf_op jit(solution)/shard_map/ppermute | solution.py:391
  39.2 0.8 %collective-permute-start.23 = (bf16[2,2,128,256]{3,2,1,0:T(8,128)(2,1)S(1)}, bf16[2,2,128,256]{3,2,1,0:T(8,128)(2,1)S(1)}, u32[]{:S(2)}, u32[]{:S(2)}) collective-permute-start(bf16[2,2,128,256]{3,2,1,0:T(8,128)(2,1)S(1)} %get-tuple-element.118), channel_id=1, source_target_pairs={{0,4},{1,5},{2,6},{3,7},{4,0},{5,1},{6,2},{7,3},{8,12},{9,13},{10,... | collective-permute-start | bytes 786440 | tf_op jit(solution)/shard_map/ppermute | solution.py:391
  40.5 0.8 %collective-permute-done.13.refs_6_ = bf16[2,128,256]{2,1,0:T(8,128)(2,1)S(1)} collective-permute-done((bf16[2,128,256]{2,1,0:T(8,128)(2,1)S(1)}, bf16[2,128,256]{2,1,0:T(8,128)(2,1)S(1)}, u32[]{:S(2)}, u32[]{:S(2)}) %collective-permute-start.13) | collective-permute-done | bytes 131104 | tf_op jit(solution)/shard_map/ppermute | solution.py:412
  41.3 1.5 %collective-permute-start.24 = (bf16[2,2,128,256]{3,2,1,0:T(8,128)(2,1)S(1)}, bf16[2,2,128,256]{3,2,1,0:T(8,128)(2,1)S(1)}, u32[]{:S(2)}, u32[]{:S(2)}) collective-permute-start(bf16[2,2,128,256]{3,2,1,0:T(8,128)(2,1)S(1)} %get-tuple-element.119), channel_id=1, source_target_pairs={{0,6},{1,7},{2,4},{3,5},{4,2},{5,3},{6,0},{7,1},{8,14},{9,15},{10,... | collective-permute-start | bytes 786440 | tf_op jit(solution)/shard_map/ppermute | solution.py:391
  42.9 4.7 %conv.3 = (bf16[2,2,128,256]{3,2,1,0:T(8,128)(2,1)S(1)}, bf16[2,2,128,256]{3,2,1,0:T(8,128)(2,1)S(1)}, bf16[2,2,128,256]{3,2,1,0:T(8,128)(2,1)S(1)}, bf16[2,2,12...) custom-call(s32[2]{0:T(128)S(1)} %pad_add_fusion.me, ...), custom_call_target="tpu_custom_call" | custom-call | bytes 1024 | tf_op jit(solution)/shard_map/conv/pallas_call | solution.py:265
  47.7 0.5 collective-permute-start.29
  48.2 1.2 %collective-permute-start.15 = (bf16[2,2,128,256]{3,2,1,0:T(8,128)(2,1)S(1)}, bf16[2,2,128,256]{3,2,1,0:T(8,128)(2,1)S(1)}, u32[]{:S(2)}, u32[]{:S(2)}) collective-permute-start(bf16[2,2,128,256]{3,2,1,0:T(8,128)(2,1)S(1)} %get-tuple-element.110), channel_id=1, source_target_pairs={{0,2},{1,3},{2,0},{3,1},{4,6},{5,7},{6,4},{7,5},{8,10},{9,11},{10,... | collective-permute-start | bytes 786440 | tf_op jit(solution)/shard_map/ppermute | solution.py:391
  49.4 0.8 %collective-permute-start.16 = (bf16[2,2,128,256]{3,2,1,0:T(8,128)(2,1)S(1)}, bf16[2,2,128,256]{3,2,1,0:T(8,128)(2,1)S(1)}, u32[]{:S(2)}, u32[]{:S(2)}) collective-permute-start(bf16[2,2,128,256]{3,2,1,0:T(8,128)(2,1)S(1)} %get-tuple-element.111), channel_id=1, source_target_pairs={{0,4},{1,5},{2,6},{3,7},{4,0},{5,1},{6,2},{7,3},{8,12},{9,13},{10,... | collective-permute-start | bytes 786440 | tf_op jit(solution)/shard_map/ppermute | solution.py:391
  50.3 3.7 %collective-permute-start.17 = (bf16[2,2,128,256]{3,2,1,0:T(8,128)(2,1)S(1)}, bf16[2,2,128,256]{3,2,1,0:T(8,128)(2,1)S(1)}, u32[]{:S(2)}, u32[]{:S(2)}) collective-permute-start(bf16[2,2,128,256]{3,2,1,0:T(8,128)(2,1)S(1)} %get-tuple-element.112), channel_id=1, source_target_pairs={{0,6},{1,7},{2,4},{3,5},{4,2},{5,3},{6,0},{7,1},{8,14},{9,15},{10,... | collective-permute-start | bytes 786440 | tf_op jit(solution)/shard_map/ppermute | solution.py:391
  54.0 2.6 %collective-permute-start.30 = (bf16[1,256,256]{2,1,0:T(8,128)(2,1)S(1)}, bf16[1,256,256]{2,1,0:T(8,128)(2,1)S(1)}, u32[]{:S(2)}, u32[]{:S(2)}) collective-permute-start(bf16[1,256,256]{2,1,0:T(8,128)(2,1)S(1)} %get-tuple-element.127), channel_id=1, source_target_pairs={{0,16},{8,24},{16,0},{24,8},{1,17},{9,25},{17,1},{25,9},{2,18},{10... | collective-permute-start | bytes 393224 | tf_op jit(solution)/shard_map/ppermute | solution.py:348
  56.6 0.6 collective-permute-done.29.got
  57.2 1.3 %collective-permute-done.15.refs_1_ = bf16[2,2,128,256]{3,2,1,0:T(8,128)(2,1)S(1)} collective-permute-done((bf16[2,2,128,256]{3,2,1,0:T(8,128)(2,1)S(1)}, bf16[2,2,128,256]{3,2,1,0:T(8,128)(2,1)S(1)}, u32[]{:S(2)}, u32[]{:S(2)}) %collective-permute-start.15) | collective-permute-done | bytes 262176 | tf_op jit(solution)/shard_map/ppermute | solution.py:391
  58.5 0.7 collective-permute-done.16.refs_2_
  59.3 4.5 %collective-permute-done.17.refs_3_ = bf16[2,2,128,256]{3,2,1,0:T(8,128)(2,1)S(1)} collective-permute-done((bf16[2,2,128,256]{3,2,1,0:T(8,128)(2,1)S(1)}, bf16[2,2,128,256]{3,2,1,0:T(8,128)(2,1)S(1)}, u32[]{:S(2)}, u32[]{:S(2)}) %collective-permute-start.17) | collective-permute-done | bytes 262176 | tf_op jit(solution)/shard_map/ppermute | solution.py:391
  63.9 2.7 %collective-permute-start.31 = (bf16[1,256,256]{2,1,0:T(8,128)(2,1)S(1)}, bf16[1,256,256]{2,1,0:T(8,128)(2,1)S(1)}, u32[]{:S(2)}, u32[]{:S(2)}) collective-permute-start(bf16[1,256,256]{2,1,0:T(8,128)(2,1)S(1)} %get-tuple-element.148), channel_id=1, source_target_pairs={{0,16},{8,24},{16,0},{24,8},{1,17},{9,25},{17,1},{25,9},{2,18},{10... | collective-permute-start | bytes 393224 | tf_op jit(solution)/shard_map/ppermute | solution.py:348
  67.6 2.1 %gate.4 = (bf16[128,4096]{1,0:T(8,128)(2,1)}, bf16[128,4096]{1,0:T(8,128)(2,1)}, bf16[128,4096]{1,0:T(8,128)(2,1)}, bf16[128,4096]{1,0:T(8,128)(2,1)}) custom-call(s32[2]{0:T(128)S(1)} %pad_add_fusion.me, bf16[128,4096]{1,0:T(8,128)(2,1)S(1)} %get-tuple-element.77.query, bf16[128,4096]{1,0:T(8,128)(2,1)S(1)} %get-tuple-element.78.grad, ...), custom_call_target="tpu_custom_call" | custom-call | bytes 1024 | tf_op jit(solution)/shard_map/gate/pallas_call | solution.py:324
  69.7 2.1 %gate.5 = (bf16[128,4096]{1,0:T(8,128)(2,1)}, bf16[128,4096]{1,0:T(8,128)(2,1)}, bf16[128,4096]{1,0:T(8,128)(2,1)}, bf16[128,4096]{1,0:T(8,128)(2,1)}) custom-call(s32[2]{0:T(128)S(1)} %pad_add_fusion.me, bf16[128,4096]{1,0:T(8,128)(2,1)S(1)} %get-tuple-element.77.query, ...), custom_call_target="tpu_custom_call", output_to_operand_aliasing={{0}: (10, {}), {1}: (11, {}), {2}: (12, {}), {3}: (13, {})} | custom-call | bytes 1024 | tf_op jit(solution)/shard_map/gate/pallas_call | solution.py:324
  71.8 1.6 %collective-permute-done.31.refs_3_ = bf16[1,256,256]{2,1,0:T(8,128)(2,1)S(1)} collective-permute-done((bf16[1,256,256]{2,1,0:T(8,128)(2,1)S(1)}, bf16[1,256,256]{2,1,0:T(8,128)(2,1)S(1)}, u32[]{:S(2)}, u32[]{:S(2)}) %collective-permute-start.31) | collective-permute-done | bytes 131104 | tf_op jit(solution)/shard_map/ppermute | solution.py:348
  73.4 1.1 %turn_grads.1 = f32[512,256]{1,0:T(8,128)} custom-call(f32[1,256,256]{2,1,0:T(8,128)S(1)} %get-tuple-element.91.refs_0_, bf16[1,256,256]{2,1,0:T(8,128)(2,1)S(1)} %collective-permute-done.30.refs_1_, f32[1,256,256]{2,1,0:T(8,128)S(1)} %get-tuple-element.126.refs_0_.refs_2_, bf16[1,256,256]{2,1,0:T(8,128)(2,1)S(1)} %collective-permute-done.31.refs_3_), custom_call_target="tpu_custom_call" | custom-call | bytes 1024 | tf_op jit(solution)/shard_map/turn_grads/pallas_call | solution.py:377
  74.5 2.1 %gate.6 = (bf16[128,4096]{1,0:T(8,128)(2,1)}, bf16[128,4096]{1,0:T(8,128)(2,1)}, bf16[128,4096]{1,0:T(8,128)(2,1)}, bf16[128,4096]{1,0:T(8,128)(2,1)}) custom-call(s32[2]{0:T(128)S(1)} %pad_add_fusion.me, bf16[128,4096]{1,0:T(8,128)(2,1)S(1)} %get-tuple-element.77.query, ...), custom_call_target="tpu_custom_call", output_to_operand_aliasing={{0}: (10, {}), {1}: (11, {}), {2}: (12, {}), {3}: (13, {})} | custom-call | bytes 1024 | tf_op jit(solution)/shard_map/gate/pallas_call | solution.py:324
  76.7 2.1 %gate.7 = (bf16[128,4096]{1,0:T(8,128)(2,1)}, bf16[128,4096]{1,0:T(8,128)(2,1)}, bf16[128,4096]{1,0:T(8,128)(2,1)}, bf16[128,4096]{1,0:T(8,128)(2,1)}) custom-call(s32[2]{0:T(128)S(1)} %pad_add_fusion.me, bf16[128,4096]{1,0:T(8,128)(2,1)S(1)} %get-tuple-element.77.query, ...), custom_call_target="tpu_custom_call", output_to_operand_aliasing={{0}: (10, {}), {1}: (11, {}), {2}: (12, {}), {3}: (13, {})} | custom-call | bytes 1024 | tf_op jit(solution)/shard_map/gate/pallas_call | solution.py:324
  (59 shorter events, 4.1 us)
Async XLA Ops:
  3.9 10.1 %collective-permute-start = (bf16[2,2,128,256]{3,2,1,0:T(8,128)(2,1)S(1)}, bf16[2,2,128,256]{3,2,1,0:T(8,128)(2,1)S(1)}, u32[]{:S(2)}, u32[]{:S(2)}) collective-permute-start(bf16[2,2,128,256]{3,2,1,0:T(8,128)(2,1)S(1)} %get-tuple-element.82), channel_id=1, source_target_pairs={{0,2},{1,3},{2,0},{3,1},{4,6},{5,7},{6,4},{7,5},{8,10},{9,11},{10,... | collective-permute-start | bytes 786440 | tf_op jit(solution)/shard_map/ppermute | solution.py:391
  6.9 13.4 %collective-permute-start.1 = (bf16[2,2,128,256]{3,2,1,0:T(8,128)(2,1)S(1)}, bf16[2,2,128,256]{3,2,1,0:T(8,128)(2,1)S(1)}, u32[]{:S(2)}, u32[]{:S(2)}) collective-permute-start(bf16[2,2,128,256]{3,2,1,0:T(8,128)(2,1)S(1)} %get-tuple-element.83), channel_id=1, source_target_pairs={{0,4},{1,5},{2,6},{3,7},{4,0},{5,1},{6,2},{7,3},{8,12},{9,13},{10,... | collective-permute-start | bytes 786440 | tf_op jit(solution)/shard_map/ppermute | solution.py:391
  8.5 11.9 %collective-permute-start.2 = (bf16[2,2,128,256]{3,2,1,0:T(8,128)(2,1)S(1)}, bf16[2,2,128,256]{3,2,1,0:T(8,128)(2,1)S(1)}, u32[]{:S(2)}, u32[]{:S(2)}) collective-permute-start(bf16[2,2,128,256]{3,2,1,0:T(8,128)(2,1)S(1)} %get-tuple-element.84), channel_id=1, source_target_pairs={{0,6},{1,7},{2,4},{3,5},{4,2},{5,3},{6,0},{7,1},{8,14},{9,15},{10,... | collective-permute-start | bytes 786440 | tf_op jit(solution)/shard_map/ppermute | solution.py:391
  20.4 4.1 %collective-permute-start.3 = (bf16[2,128,256]{2,1,0:T(8,128)(2,1)S(1)}, bf16[2,128,256]{2,1,0:T(8,128)(2,1)S(1)}, u32[]{:S(2)}, u32[]{:S(2)}) collective-permute-start(bf16[2,128,256]{2,1,0:T(8,128)(2,1)S(1)} %get-tuple-element.85), channel_id=1, source_target_pairs={{0,1},{1,0},{2,3},{3,2},{4,5},{5,4},{6,7},{7,6},{8,9},{9,8},{10,11... | collective-permute-start | bytes 393224 | tf_op jit(solution)/shard_map/ppermute | solution.py:412
  20.4 4.0 %collective-permute-start.4 = (bf16[2,128,256]{2,1,0:T(8,128)(2,1)S(1)}, bf16[2,128,256]{2,1,0:T(8,128)(2,1)S(1)}, u32[]{:S(2)}, u32[]{:S(2)}) collective-permute-start(bf16[2,128,256]{2,1,0:T(8,128)(2,1)S(1)} %get-tuple-element.86), channel_id=1, source_target_pairs={{0,1},{1,0},{2,3},{3,2},{4,5},{5,4},{6,7},{7,6},{8,9},{9,8},{10,11... | collective-permute-start | bytes 393224 | tf_op jit(solution)/shard_map/ppermute | solution.py:412
  20.9 12.4 %collective-permute-start.10 = (bf16[2,2,128,256]{3,2,1,0:T(8,128)(2,1)S(1)}, bf16[2,2,128,256]{3,2,1,0:T(8,128)(2,1)S(1)}, u32[]{:S(2)}, u32[]{:S(2)}) collective-permute-start(bf16[2,2,128,256]{3,2,1,0:T(8,128)(2,1)S(1)} %get-tuple-element.96), channel_id=1, source_target_pairs={{0,6},{1,7},{2,4},{3,5},{4,2},{5,3},{6,0},{7,1},{8,14},{9,15},{10,... | collective-permute-start | bytes 786440 | tf_op jit(solution)/shard_map/ppermute | solution.py:391
  22.4 13.4 %collective-permute-start.8 = (bf16[2,2,128,256]{3,2,1,0:T(8,128)(2,1)S(1)}, bf16[2,2,128,256]{3,2,1,0:T(8,128)(2,1)S(1)}, u32[]{:S(2)}, u32[]{:S(2)}) collective-permute-start(bf16[2,2,128,256]{3,2,1,0:T(8,128)(2,1)S(1)} %get-tuple-element.94), channel_id=1, source_target_pairs={{0,2},{1,3},{2,0},{3,1},{4,6},{5,7},{6,4},{7,5},{8,10},{9,11},{10,... | collective-permute-start | bytes 786440 | tf_op jit(solution)/shard_map/ppermute | solution.py:391
  23.9 11.9 %collective-permute-start.9 = (bf16[2,2,128,256]{3,2,1,0:T(8,128)(2,1)S(1)}, bf16[2,2,128,256]{3,2,1,0:T(8,128)(2,1)S(1)}, u32[]{:S(2)}, u32[]{:S(2)}) collective-permute-start(bf16[2,2,128,256]{3,2,1,0:T(8,128)(2,1)S(1)} %get-tuple-element.95), channel_id=1, source_target_pairs={{0,4},{1,5},{2,6},{3,7},{4,0},{5,1},{6,2},{7,3},{8,12},{9,13},{10,... | collective-permute-start | bytes 786440 | tf_op jit(solution)/shard_map/ppermute | solution.py:391
  24.4 4.1 %collective-permute-start.5 = (bf16[2,128,256]{2,1,0:T(8,128)(2,1)S(1)}, bf16[2,128,256]{2,1,0:T(8,128)(2,1)S(1)}, u32[]{:S(2)}, u32[]{:S(2)}) collective-permute-start(bf16[2,128,256]{2,1,0:T(8,128)(2,1)S(1)} %get-tuple-element.87), channel_id=1, source_target_pairs={{0,1},{1,0},{2,3},{3,2},{4,5},{5,4},{6,7},{7,6},{8,9},{9,8},{10,11... | collective-permute-start | bytes 393224 | tf_op jit(solution)/shard_map/ppermute | solution.py:412
  24.4 4.1 %collective-permute-start.6 = (bf16[2,128,256]{2,1,0:T(8,128)(2,1)S(1)}, bf16[2,128,256]{2,1,0:T(8,128)(2,1)S(1)}, u32[]{:S(2)}, u32[]{:S(2)}) collective-permute-start(bf16[2,128,256]{2,1,0:T(8,128)(2,1)S(1)} %get-tuple-element.88), channel_id=1, source_target_pairs={{0,1},{1,0},{2,3},{3,2},{4,5},{5,4},{6,7},{7,6},{8,9},{9,8},{10,11... | collective-permute-start | bytes 393224 | tf_op jit(solution)/shard_map/ppermute | solution.py:412
  35.9 4.1 %collective-permute-start.11 = (bf16[2,128,256]{2,1,0:T(8,128)(2,1)S(1)}, bf16[2,128,256]{2,1,0:T(8,128)(2,1)S(1)}, u32[]{:S(2)}, u32[]{:S(2)}) collective-permute-start(bf16[2,128,256]{2,1,0:T(8,128)(2,1)S(1)} %get-tuple-element.101), channel_id=1, source_target_pairs={{0,1},{1,0},{2,3},{3,2},{4,5},{5,4},{6,7},{7,6},{8,9},{9,8},{10,11... | collective-permute-start | bytes 393224 | tf_op jit(solution)/shard_map/ppermute | solution.py:412
  36.0 4.0 %collective-permute-start.12 = (bf16[2,128,256]{2,1,0:T(8,128)(2,1)S(1)}, bf16[2,128,256]{2,1,0:T(8,128)(2,1)S(1)}, u32[]{:S(2)}, u32[]{:S(2)}) collective-permute-start(bf16[2,128,256]{2,1,0:T(8,128)(2,1)S(1)} %get-tuple-element.102), channel_id=1, source_target_pairs={{0,1},{1,0},{2,3},{3,2},{4,5},{5,4},{6,7},{7,6},{8,9},{9,8},{10,11... | collective-permute-start | bytes 393224 | tf_op jit(solution)/shard_map/ppermute | solution.py:412
  36.5 11.7 %collective-permute-start.7 = (bf16[2,256,256]{2,1,0:T(8,128)(2,1)S(1)}, bf16[2,256,256]{2,1,0:T(8,128)(2,1)S(1)}, u32[]{:S(2)}, u32[]{:S(2)}) collective-permute-start(bf16[2,256,256]{2,1,0:T(8,128)(2,1)S(1)} %get-tuple-element.90), channel_id=1, source_target_pairs={{0,8},{8,0},{16,24},{24,16},{1,9},{9,1},{17,25},{25,17},{2,10},{10... | collective-permute-start | bytes 786440 | tf_op jit(solution)/shard_map/ppermute | solution.py:348
  38.0 11.4 %collective-permute-start.22 = (bf16[2,2,128,256]{3,2,1,0:T(8,128)(2,1)S(1)}, bf16[2,2,128,256]{3,2,1,0:T(8,128)(2,1)S(1)}, u32[]{:S(2)}, u32[]{:S(2)}) collective-permute-start(bf16[2,2,128,256]{3,2,1,0:T(8,128)(2,1)S(1)} %get-tuple-element.117), channel_id=1, source_target_pairs={{0,2},{1,3},{2,0},{3,1},{4,6},{5,7},{6,4},{7,5},{8,10},{9,11},{10,... | collective-permute-start | bytes 786440 | tf_op jit(solution)/shard_map/ppermute | solution.py:391
  39.2 11.1 %collective-permute-start.23 = (bf16[2,2,128,256]{3,2,1,0:T(8,128)(2,1)S(1)}, bf16[2,2,128,256]{3,2,1,0:T(8,128)(2,1)S(1)}, u32[]{:S(2)}, u32[]{:S(2)}) collective-permute-start(bf16[2,2,128,256]{3,2,1,0:T(8,128)(2,1)S(1)} %get-tuple-element.118), channel_id=1, source_target_pairs={{0,4},{1,5},{2,6},{3,7},{4,0},{5,1},{6,2},{7,3},{8,12},{9,13},{10,... | collective-permute-start | bytes 786440 | tf_op jit(solution)/shard_map/ppermute | solution.py:391
  40.0 1.3 %collective-permute-start.13 = (bf16[2,128,256]{2,1,0:T(8,128)(2,1)S(1)}, bf16[2,128,256]{2,1,0:T(8,128)(2,1)S(1)}, u32[]{:S(2)}, u32[]{:S(2)}) collective-permute-start(bf16[2,128,256]{2,1,0:T(8,128)(2,1)S(1)} %get-tuple-element.103), channel_id=1, source_target_pairs={{0,1},{1,0},{2,3},{3,2},{4,5},{5,4},{6,7},{7,6},{8,9},{9,8},{10,11... | collective-permute-start | bytes 393224 | tf_op jit(solution)/shard_map/ppermute | solution.py:412
  40.0 2.9 %collective-permute-start.14 = (bf16[2,128,256]{2,1,0:T(8,128)(2,1)S(1)}, bf16[2,128,256]{2,1,0:T(8,128)(2,1)S(1)}, u32[]{:S(2)}, u32[]{:S(2)}) collective-permute-start(bf16[2,128,256]{2,1,0:T(8,128)(2,1)S(1)} %get-tuple-element.104), channel_id=1, source_target_pairs={{0,1},{1,0},{2,3},{3,2},{4,5},{5,4},{6,7},{7,6},{8,9},{9,8},{10,11... | collective-permute-start | bytes 393224 | tf_op jit(solution)/shard_map/ppermute | solution.py:412
  41.3 12.6 %collective-permute-start.24 = (bf16[2,2,128,256]{3,2,1,0:T(8,128)(2,1)S(1)}, bf16[2,2,128,256]{3,2,1,0:T(8,128)(2,1)S(1)}, u32[]{:S(2)}, u32[]{:S(2)}) collective-permute-start(bf16[2,2,128,256]{3,2,1,0:T(8,128)(2,1)S(1)} %get-tuple-element.119), channel_id=1, source_target_pairs={{0,6},{1,7},{2,4},{3,5},{4,2},{5,3},{6,0},{7,1},{8,14},{9,15},{10,... | collective-permute-start | bytes 786440 | tf_op jit(solution)/shard_map/ppermute | solution.py:391
  47.7 9.6 %collective-permute-start.29 = (bf16[2,256,256]{2,1,0:T(8,128)(2,1)S(1)}, bf16[2,256,256]{2,1,0:T(8,128)(2,1)S(1)}, u32[]{:S(2)}, u32[]{:S(2)}) collective-permute-start(bf16[2,256,256]{2,1,0:T(8,128)(2,1)S(1)} %get-tuple-element.125), channel_id=1, source_target_pairs={{0,8},{8,0},{16,24},{24,16},{1,9},{9,1},{17,25},{25,17},{2,10},{10... | collective-permute-start | bytes 786440 | tf_op jit(solution)/shard_map/ppermute | solution.py:348
  48.2 10.3 %collective-permute-start.15 = (bf16[2,2,128,256]{3,2,1,0:T(8,128)(2,1)S(1)}, bf16[2,2,128,256]{3,2,1,0:T(8,128)(2,1)S(1)}, u32[]{:S(2)}, u32[]{:S(2)}) collective-permute-start(bf16[2,2,128,256]{3,2,1,0:T(8,128)(2,1)S(1)} %get-tuple-element.110), channel_id=1, source_target_pairs={{0,2},{1,3},{2,0},{3,1},{4,6},{5,7},{6,4},{7,5},{8,10},{9,11},{10,... | collective-permute-start | bytes 786440 | tf_op jit(solution)/shard_map/ppermute | solution.py:391
  49.4 9.8 %collective-permute-start.16 = (bf16[2,2,128,256]{3,2,1,0:T(8,128)(2,1)S(1)}, bf16[2,2,128,256]{3,2,1,0:T(8,128)(2,1)S(1)}, u32[]{:S(2)}, u32[]{:S(2)}) collective-permute-start(bf16[2,2,128,256]{3,2,1,0:T(8,128)(2,1)S(1)} %get-tuple-element.111), channel_id=1, source_target_pairs={{0,4},{1,5},{2,6},{3,7},{4,0},{5,1},{6,2},{7,3},{8,12},{9,13},{10,... | collective-permute-start | bytes 786440 | tf_op jit(solution)/shard_map/ppermute | solution.py:391
  50.3 13.5 %collective-permute-start.17 = (bf16[2,2,128,256]{3,2,1,0:T(8,128)(2,1)S(1)}, bf16[2,2,128,256]{3,2,1,0:T(8,128)(2,1)S(1)}, u32[]{:S(2)}, u32[]{:S(2)}) collective-permute-start(bf16[2,2,128,256]{3,2,1,0:T(8,128)(2,1)S(1)} %get-tuple-element.112), channel_id=1, source_target_pairs={{0,6},{1,7},{2,4},{3,5},{4,2},{5,3},{6,0},{7,1},{8,14},{9,15},{10,... | collective-permute-start | bytes 786440 | tf_op jit(solution)/shard_map/ppermute | solution.py:391
  54.0 9.9 %collective-permute-start.30 = (bf16[1,256,256]{2,1,0:T(8,128)(2,1)S(1)}, bf16[1,256,256]{2,1,0:T(8,128)(2,1)S(1)}, u32[]{:S(2)}, u32[]{:S(2)}) collective-permute-start(bf16[1,256,256]{2,1,0:T(8,128)(2,1)S(1)} %get-tuple-element.127), channel_id=1, source_target_pairs={{0,16},{8,24},{16,0},{24,8},{1,17},{9,25},{17,1},{25,9},{2,18},{10... | collective-permute-start | bytes 393224 | tf_op jit(solution)/shard_map/ppermute | solution.py:348
  57.2 9.3 %collective-permute-start.25 = (bf16[2,128,256]{2,1,0:T(8,128)(2,1)S(1)}, bf16[2,128,256]{2,1,0:T(8,128)(2,1)S(1)}, u32[]{:S(2)}, u32[]{:S(2)}) collective-permute-start(bf16[2,128,256]{2,1,0:T(8,128)(2,1)S(1)} %get-tuple-element.120), channel_id=1, source_target_pairs={{0,1},{1,0},{2,3},{3,2},{4,5},{5,4},{6,7},{7,6},{8,9},{9,8},{10,11... | collective-permute-start | bytes 393224 | tf_op jit(solution)/shard_map/ppermute | solution.py:412
  58.5 8.2 %collective-permute-start.26 = (bf16[2,128,256]{2,1,0:T(8,128)(2,1)S(1)}, bf16[2,128,256]{2,1,0:T(8,128)(2,1)S(1)}, u32[]{:S(2)}, u32[]{:S(2)}) collective-permute-start(bf16[2,128,256]{2,1,0:T(8,128)(2,1)S(1)} %get-tuple-element.121), channel_id=1, source_target_pairs={{0,1},{1,0},{2,3},{3,2},{4,5},{5,4},{6,7},{7,6},{8,9},{9,8},{10,11... | collective-permute-start | bytes 393224 | tf_op jit(solution)/shard_map/ppermute | solution.py:412
  59.3 7.8 %collective-permute-start.27 = (bf16[2,128,256]{2,1,0:T(8,128)(2,1)S(1)}, bf16[2,128,256]{2,1,0:T(8,128)(2,1)S(1)}, u32[]{:S(2)}, u32[]{:S(2)}) collective-permute-start(bf16[2,128,256]{2,1,0:T(8,128)(2,1)S(1)} %get-tuple-element.122), channel_id=1, source_target_pairs={{0,1},{1,0},{2,3},{3,2},{4,5},{5,4},{6,7},{7,6},{8,9},{9,8},{10,11... | collective-permute-start | bytes 393224 | tf_op jit(solution)/shard_map/ppermute | solution.py:412
  63.8 3.5 %collective-permute-start.28 = (bf16[2,128,256]{2,1,0:T(8,128)(2,1)S(1)}, bf16[2,128,256]{2,1,0:T(8,128)(2,1)S(1)}, u32[]{:S(2)}, u32[]{:S(2)}) collective-permute-start(bf16[2,128,256]{2,1,0:T(8,128)(2,1)S(1)} %get-tuple-element.123), channel_id=1, source_target_pairs={{0,1},{1,0},{2,3},{3,2},{4,5},{5,4},{6,7},{7,6},{8,9},{9,8},{10,11... | collective-permute-start | bytes 393224 | tf_op jit(solution)/shard_map/ppermute | solution.py:412
  63.9 9.6 %collective-permute-start.31 = (bf16[1,256,256]{2,1,0:T(8,128)(2,1)S(1)}, bf16[1,256,256]{2,1,0:T(8,128)(2,1)S(1)}, u32[]{:S(2)}, u32[]{:S(2)}) collective-permute-start(bf16[1,256,256]{2,1,0:T(8,128)(2,1)S(1)} %get-tuple-element.148), channel_id=1, source_target_pairs={{0,16},{8,24},{16,0},{24,8},{1,17},{9,25},{17,1},{25,9},{2,18},{10... | collective-permute-start | bytes 393224 | tf_op jit(solution)/shard_map/ppermute | solution.py:348
  66.5 10.1 %collective-permute-start.18 = (bf16[2,128,256]{2,1,0:T(8,128)(2,1)S(1)}, bf16[2,128,256]{2,1,0:T(8,128)(2,1)S(1)}, u32[]{:S(2)}, u32[]{:S(2)}) collective-permute-start(bf16[2,128,256]{2,1,0:T(8,128)(2,1)S(1)} %get-tuple-element.113), channel_id=1, source_target_pairs={{0,1},{1,0},{2,3},{3,2},{4,5},{5,4},{6,7},{7,6},{8,9},{9,8},{10,11... | collective-permute-start | bytes 393224 | tf_op jit(solution)/shard_map/ppermute | solution.py:412
  66.8 9.9 %collective-permute-start.19 = (bf16[2,128,256]{2,1,0:T(8,128)(2,1)S(1)}, bf16[2,128,256]{2,1,0:T(8,128)(2,1)S(1)}, u32[]{:S(2)}, u32[]{:S(2)}) collective-permute-start(bf16[2,128,256]{2,1,0:T(8,128)(2,1)S(1)} %get-tuple-element.114), channel_id=1, source_target_pairs={{0,1},{1,0},{2,3},{3,2},{4,5},{5,4},{6,7},{7,6},{8,9},{9,8},{10,11... | collective-permute-start | bytes 393224 | tf_op jit(solution)/shard_map/ppermute | solution.py:412
  67.0 9.6 %collective-permute-start.20 = (bf16[2,128,256]{2,1,0:T(8,128)(2,1)S(1)}, bf16[2,128,256]{2,1,0:T(8,128)(2,1)S(1)}, u32[]{:S(2)}, u32[]{:S(2)}) collective-permute-start(bf16[2,128,256]{2,1,0:T(8,128)(2,1)S(1)} %get-tuple-element.115), channel_id=1, source_target_pairs={{0,1},{1,0},{2,3},{3,2},{4,5},{5,4},{6,7},{7,6},{8,9},{9,8},{10,11... | collective-permute-start | bytes 393224 | tf_op jit(solution)/shard_map/ppermute | solution.py:412
  67.3 9.4 %collective-permute-start.21 = (bf16[2,128,256]{2,1,0:T(8,128)(2,1)S(1)}, bf16[2,128,256]{2,1,0:T(8,128)(2,1)S(1)}, u32[]{:S(2)}, u32[]{:S(2)}) collective-permute-start(bf16[2,128,256]{2,1,0:T(8,128)(2,1)S(1)} %get-tuple-element.116), channel_id=1, source_target_pairs={{0,1},{1,0},{2,3},{3,2},{4,5},{5,4},{6,7},{7,6},{8,9},{9,8},{10,11... | collective-permute-start | bytes 393224 | tf_op jit(solution)/shard_map/ppermute | solution.py:412
  (4 other events, 76.8 us)

commit v11 on v8

--- a/solution.py
+++ b/solution.py
@@ -95,7 +95,6 @@
 def product_kernel(n, me, key, value, query, grad, *refs):
     bufs, outs, sems = refs[:4], refs[4:-1], refs[-1]
     _, rows, width = outs[0].shape
-    width *= HALVES
     step = rows // STEPS
     copies = []
     for i in range(STEPS):
@@ -113,11 +112,11 @@
         for a, (left, right) in enumerate((bufs[:2], bufs[2:])):
             copies[s][2 * a].wait()
             copies[s][2 * a + 1].wait()
-            for i, j in enumerate(peers(n)):
-                cols = peer_columns(me, j, width)
+            for j in range(n):
+                cols = peer_columns(me, j, HALVES * width)
                 value = (left[at, cols].astype(F32) * right[at, cols].astype(F32)).astype(BF16)
-                for half in range(HALVES):
-                    outs[half * n + i][a, at] = value[:, half * width // HALVES :][:, : width // HALVES]
+                outs[peers(n).index(j)][a, at] = value[:, :width]
+                outs[n + j // 2][j % 2, a, at] = value[:, width:]
 
 
 def products(n, me, key, value, query, grad):
@@ -126,14 +125,15 @@
     out = pl.pallas_call(
         functools.partial(product_kernel, n),
         in_specs=[SMEM] + [HBM] * 4,
-        out_specs=[VMEM] * (4 + HALVES * n),
+        out_specs=[VMEM] * (4 + n + n // 2),
         out_shape=[pltpu.VMEM(key.shape, BF16)] * 4
-        + [pltpu.VMEM((2, rows, width), BF16)] * (HALVES * n),
+        + [pltpu.VMEM((2, rows, width), BF16)] * n
+        + [pltpu.VMEM((2, 2, rows, width), BF16)] * (n // 2),
         scratch_shapes=[pltpu.SemaphoreType.DMA((4, STEPS))],
         compiler_params=PARAMS,
         name="products",
     )(me, key, value, query, grad)
-    return out[:4], [out[4 + h * n : 4 + (h + 1) * n] for h in range(HALVES)]
+    return out[:4], out[4 : 4 + n], out[4 + n :]
 
 
 def lane_groups(width):
@@ -184,10 +184,16 @@
 
 
 def conv_kernel(n, d, half, me, *refs):
-    got, (filt, fwd, back) = refs[:n], refs[n : n + 3]
-    refs = refs[-(n + 2 + 6) :]
-    out, (keep, send), (nat, x, u, y, turned, grad) = refs[:n], refs[n : n + 2], refs[n + 2 :]
-    _, rows, width = got[0].shape
+    taken = n // 2 + 1 if half else n
+    got, (filt, fwd, back) = refs[:taken], refs[taken : taken + 3]
+    refs = refs[-(n - 1 + 2 + 6) :]
+    *near, far, keep, send, nat, x, u, y, turned, grad = refs
+    rows, width = got[0].shape[-2:]
+    if half:
+        blocks = [(chip, got[chip // 2].at[0]) for chip in range(0, n, 2)]
+        blocks += [(chip + 1, got[-1].at[chip // 2]) for chip in range(0, n, 2)]
+    else:
+        blocks = list(zip(peers(n), got))
     m2 = x.shape[2]
     per = keep.shape[1] // CLASSES
     groups = lane_groups(width)
@@ -197,9 +203,9 @@
 
     for a in range(2):
         for g, lanes in enumerate(groups):
-            for i, j in enumerate(peers(n)):
+            for j, block in blocks:
                 at = pl.multiple_of((me[0] ^ j) * rows, rows)
-                nat[a, g, pl.ds(at, rows)] = got[i][a, :, lanes].astype(F32)
+                nat[a, g, pl.ds(at, rows)] = block[a, :, lanes].astype(F32)
             for c in range(CLASSES):
                 x[a, c, :, lanes] = nat[a, g, pl.ds(c, m2, stride=CLASSES), :].astype(BF16)
         for c in range(CLASSES):
@@ -226,11 +232,12 @@
         grad[c] = dot(back[c], y[2, c])
         for o in range(2):
             turned[o, c] = dot(back[c], y[o, c]).astype(BF16)
-    for i, j in enumerate(peers(n)):
+    ends = [*zip(near_peers(n), near), (n - 2, far.at[0]), (n - 1, far.at[1])]
+    for j, block in ends:
         at = pl.multiple_of((me[0] ^ j) * part_rows, part_rows)
         for o in range(2):
             for c in range(CLASSES):
-                out[i][half, o, c * part_rows : (c + 1) * part_rows] = turned[o, c, pl.ds(at, part_rows)]
+                block[half, o, c * part_rows : (c + 1) * part_rows] = turned[o, c, pl.ds(at, part_rows)]
     for j in range(d):
         at = pl.multiple_of((me[1] ^ j) * per, per)
         for c in range(CLASSES):
@@ -242,14 +249,16 @@
 
 
 def conv(n, d, half, me, got, filt, fwd, back, before):
-    _, rows, width = got[0].shape
+    rows, width = got[0].shape[-2:]
     length = n * rows
     m2 = length // CLASSES
+    first = 4 + len(got)
     out = pl.pallas_call(
         functools.partial(conv_kernel, n, d, half),
-        in_specs=[SMEM] + [VMEM] * (n + 3 + len(before)),
-        out_specs=[VMEM] * (n + 2),
-        out_shape=[pltpu.VMEM((HALVES, 2, rows, width), BF16)] * n
+        in_specs=[SMEM] + [VMEM] * (len(got) + 3 + len(before)),
+        out_specs=[VMEM] * (n - 1 + 2),
+        out_shape=[pltpu.VMEM((HALVES, 2, rows, width), BF16)] * (n - 2)
+        + [pltpu.VMEM((2, HALVES, 2, rows, width), BF16)]
         + [pltpu.VMEM((d // 2, length // d, HALVES * width), dtype) for dtype in (F32, BF16)],
         scratch_shapes=[
             pltpu.VMEM((2, width // 128, length, 128), F32),
@@ -259,7 +268,7 @@
             pltpu.VMEM((2, CLASSES, m2, width), BF16),
             pltpu.VMEM((CLASSES, m2, width), F32),
         ],
-        input_output_aliases={n + 4 + i: i for i in range(len(before))},
+        input_output_aliases={first + i: i for i in range(len(before))},
         compiler_params=CONV_PARAMS,
         name="conv",
     )(me, *got, filt, fwd, back, *before)
@@ -275,6 +284,7 @@
 
 def gate_kernel(js, me, query, grad, value, key, gain, *refs):
     got, outs, (sent, sems, nat) = refs[: len(js)], refs[-7:-3], refs[-3:]
+    got = [ref.at[0] if len(ref.shape) == 5 else ref for ref in got]
     _, _, rows, width = got[0].shape
     copies = []
     for i, j in enumerate(js):
@@ -334,13 +344,14 @@
         out[lanes, :] = natural(nat.at[g], total).T
 
 
-def sum_grads(d, keep, send):
+def sum_grads(d, keep, send, arrived):
     _, per, chans = keep.shape
     bit = 1
     while True:
         got = resident(lax.ppermute(send, "dp", [(i, i ^ bit) for i in range(d)]))
         if keep.shape[0] == 1:
             break
+        got, = after(arrived, [got])
         shape = (keep.shape[0] // 2, per, chans)
         keep, send = pl.pallas_call(
             add_kernel,
@@ -366,11 +377,29 @@
     return [0, 1, *range(2, n, 2), *range(3, n, 2)]
 
 
-def exchange(n, js, blocks):
-    return [
-        resident(lax.ppermute(block, "ctx", [(i, i ^ j) for i in range(n)])) if j else block
-        for j, block in zip(js, blocks)
-    ]
+def near_peers(n):
+    return [j for j in peers(n) if j < n - 2]
+
+
+def swap(n, j, block):
+    return resident(lax.ppermute(block, "ctx", [(i, i ^ j) for i in range(n)]))
+
+
+def pack_kernel(*refs):
+    for i, ref in enumerate(refs[:-1]):
+        refs[-1][i] = ref[1]
+
+
+def hand_over(n, got):
+    packed = pl.pallas_call(
+        pack_kernel,
+        in_specs=[VMEM] * len(got),
+        out_specs=VMEM,
+        out_shape=pltpu.VMEM((len(got), *got[0].shape[1:]), BF16),
+        compiler_params=PARAMS,
+        name="pack",
+    )(*got)
+    return swap(n, 1, packed)
 
 
 def after_kernel(*refs):
@@ -397,19 +426,21 @@
     me = jnp.stack([lax.axis_index("ctx"), lax.axis_index("dp")]).astype(jnp.int32)
 
     arrays = [in_hbm(x[0]) for x in (key_in, value_in, query_in, grad_out)]
-    (key, value, query, grad), got = products(n, me, *arrays)
-    first = exchange(n, peers(n), got[0])
-    second = exchange(n, peers(n), after([first[1]], got[1]))
-    spec = filter_spectra(filters, fwd, [second[1]])
+    (key, value, query, grad), first, second = products(n, me, *arrays)
+    first = [first[0], *(swap(n, j, x) for j, x in zip(peers(n)[1:], first[1:]))]
+    second = [second[0], *(swap(n, 2 * i, x) for i, x in enumerate(second[1:], 1))]
+    spec = filter_spectra(filters, fwd, [])
     results = conv(n, d, 0, me, first, spec, fwd, back, [])
+    second = after(results[:1], second)
+    second = [*second, hand_over(n, second)]
     *mixed, keep, send = conv(n, d, 1, me, second, spec, fwd, back, results)
-    mixed = exchange(n, peers(n), mixed)
-    grad_filter = sum_grads(d, keep, *after([mixed[1]], [send]))
-
-    outs = []
-    early = n - 2
-    for at in (slice(early), slice(early, n)):
-        outs = gate(peers(n)[at], me, query, grad, value, key, gain, mixed[at], outs)
+    near = [mixed[0], *(swap(n, j, x) for j, x in zip(near_peers(n)[1:], mixed[1:-1]))]
+    far = swap(n, n - 2, mixed[-1])
+    grad_filter = sum_grads(d, keep, send, near[2:4])
+    passed = hand_over(n, [far])
+    js = [*near_peers(n)[:-2], n - 2, n - 1]
+    outs = gate(js, me, query, grad, value, key, gain, [*near[:-2], far, passed], [])
+    outs = gate(near_peers(n)[-2:], me, query, grad, value, key, gain, near[-2:], outs)
     return *(x[None] for x in outs), grad_filter
 
 

time: 72.1 us -> 87.7 us (1.22)
  waiting for transfers between devices: 22.4 us -> 39.4 us
  starting transfers between devices: 25.2 us -> 23.6 us
    ppermute x21 -> x18, waiting for transfers between devices: 17.2 us -> 29.7 us  [swap(): return resident(lax.ppermute(block, 'ctx', [(i, i ^ j) for i in range(n)]))]
    ppermute x2, waiting for transfers between devices: 5.27 us -> 9.76 us  [sum_grads(): got = resident(lax.ppermute(send, 'dp', [(i, i ^ bit) for i in range(d)]))]
    ppermute x21 -> x18, starting transfers between devices: 21 us -> 19.7 us  [swap(): return resident(lax.ppermute(block, 'ctx', [(i, i ^ j) for i in range(n)]))]
  transfers between devices with their start and end apart: 23 -> 20, of which waited for: 10 -> 6; matrix products, arithmetic and copies ran while one was open for 0% -> 0% of each run, Pallas kernels for 20% -> 15%
where the time goes in v11:
time: 87.7 us; the launch traced here: 87.5 us
  waiting for transfers between devices  39.4 us (45%)
  starting transfers between devices  23.6 us (27%)
  Pallas kernels  23.5 us (27%)
  between operations  0.96 us (1%)
    ppermute x18, waiting for transfers between devices, swap(): return resident(lax.ppermute(block, 'ctx', [(i, i ^ j) for i in range(n)]))  29.7 us
    ppermute x18, starting transfers between devices, swap(): return resident(lax.ppermute(block, 'ctx', [(i, i ^ j) for i in range(n)]))  19.7 us
    ppermute x2, waiting for transfers between devices, sum_grads(): got = resident(lax.ppermute(send, 'dp', [(i, i ^ bit) for i in range(d)]))  9.76 us
    pallas_call x2, Pallas kernels, conv(): pl.pallas_call(functools.partial(conv_kernel, n, d, half), in_specs=[SMEM...  9.52 us
    pallas_call x2, Pallas kernels, gate(): pl.pallas_call(functools.partial(gate_kernel, js), in_specs=[SMEM] + [VME...  5.95 us
    ppermute x2, starting transfers between devices, sum_grads(): got = resident(lax.ppermute(send, 'dp', [(i, i ^ bit) for i in range(d)]))  3.85 us
    pallas_call x1, Pallas kernels, filter_spectra(): pl.pallas_call(filter_kernel, in_specs=[VMEM] * (2 + len(arrived)), out_s...  3.59 us
    pallas_call x1, Pallas kernels, products(): pl.pallas_call(functools.partial(product_kernel, n), in_specs=[SMEM] + [H...  3.18 us
  transfers between devices with their start and end apart: 20, of which 6 were waited for; matrix products, arithmetic and copies ran while one was open for 0% of the time, Pallas kernels for 15%

profile of v11, /device:TPU:0, one launch (start us, length us, event | category | flops | bytes accessed | tf_op | source)
XLA Modules:
  0.0 87.5 jit_solution(19295036910621414)
XLA Ops:
  0.7 0.1 pad_add_fusion.me
  0.7 3.2 %products.1 = (bf16[128,4096]{1,0:T(8,128)(2,1)S(1)}, bf16[128,4096]{1,0:T(8,128)(2,1)S(1)}, bf16[128,4096]{1,0:T(8,128)(2,1)S(1)}, bf16[128,4096]{1,0:T(8,128)(...) custom-call(s32[2]{0:T(128)S(1)} %pad_add_fusion.me, ...), custom_call_target="tpu_custom_call" | custom-call | tf_op jit(solution)/shard_map/products/pallas_call | solution.py:125
  3.9 0.5 collective-permute-start
  4.5 2.6 %collective-permute-start.1 = (bf16[2,128,256]{2,1,0:T(8,128)(2,1)S(1)}, bf16[2,128,256]{2,1,0:T(8,128)(2,1)S(1)}, u32[]{:S(2)}, u32[]{:S(2)}) collective-permute-start(bf16[2,128,256]{2,1,0:T(8,128)(2,1)S(1)} %get-tuple-element.59), channel_id=1, source_target_pairs={{0,2},{1,3},{2,0},{3,1},{4,6},{5,7},{6,4},{7,5},{8,10},{9,11},{10,... | collective-permute-start | bytes 393224 | tf_op jit(solution)/shard_map/ppermute | solution.py:385
  7.0 1.5 %collective-permute-start.2 = (bf16[2,128,256]{2,1,0:T(8,128)(2,1)S(1)}, bf16[2,128,256]{2,1,0:T(8,128)(2,1)S(1)}, u32[]{:S(2)}, u32[]{:S(2)}) collective-permute-start(bf16[2,128,256]{2,1,0:T(8,128)(2,1)S(1)} %get-tuple-element.60), channel_id=1, source_target_pairs={{0,4},{1,5},{2,6},{3,7},{4,0},{5,1},{6,2},{7,3},{8,12},{9,13},{10,... | collective-permute-start | bytes 393224 | tf_op jit(solution)/shard_map/ppermute | solution.py:385
  8.6 1.2 %collective-permute-start.4 = (bf16[2,128,256]{2,1,0:T(8,128)(2,1)S(1)}, bf16[2,128,256]{2,1,0:T(8,128)(2,1)S(1)}, u32[]{:S(2)}, u32[]{:S(2)}) collective-permute-start(bf16[2,128,256]{2,1,0:T(8,128)(2,1)S(1)} %get-tuple-element.62), channel_id=1, source_target_pairs={{0,3},{1,2},{2,1},{3,0},{4,7},{5,6},{6,5},{7,4},{8,11},{9,10},{10,... | collective-permute-start | bytes 393224 | tf_op jit(solution)/shard_map/ppermute | solution.py:385
  9.7 0.8 collective-permute-start.7
  10.5 0.6 collective-permute-done.1.refs_2_
  11.2 2.1 %collective-permute-start.8 = (bf16[2,2,128,256]{3,2,1,0:T(8,128)(2,1)S(1)}, bf16[2,2,128,256]{3,2,1,0:T(8,128)(2,1)S(1)}, u32[]{:S(2)}, u32[]{:S(2)}) collective-permute-start(bf16[2,2,128,256]{3,2,1,0:T(8,128)(2,1)S(1)} %get-tuple-element.68), channel_id=1, source_target_pairs={{0,4},{1,5},{2,6},{3,7},{4,0},{5,1},{6,2},{7,3},{8,12},{9,13},{10,... | collective-permute-start | bytes 786440 | tf_op jit(solution)/shard_map/ppermute | solution.py:385
  13.2 2.0 %collective-permute-done.2.refs_3_ = bf16[2,128,256]{2,1,0:T(8,128)(2,1)S(1)} collective-permute-done((bf16[2,128,256]{2,1,0:T(8,128)(2,1)S(1)}, bf16[2,128,256]{2,1,0:T(8,128)(2,1)S(1)}, u32[]{:S(2)}, u32[]{:S(2)}) %collective-permute-start.2) | collective-permute-done | bytes 131104 | tf_op jit(solution)/shard_map/ppermute | solution.py:385
  15.2 1.8 %collective-permute-start.9 = (bf16[2,2,128,256]{3,2,1,0:T(8,128)(2,1)S(1)}, bf16[2,2,128,256]{3,2,1,0:T(8,128)(2,1)S(1)}, u32[]{:S(2)}, u32[]{:S(2)}) collective-permute-start(bf16[2,2,128,256]{3,2,1,0:T(8,128)(2,1)S(1)} %get-tuple-element.69), channel_id=1, source_target_pairs={{0,6},{1,7},{2,4},{3,5},{4,2},{5,3},{6,0},{7,1},{8,14},{9,15},{10,... | collective-permute-start | bytes 786440 | tf_op jit(solution)/shard_map/ppermute | solution.py:385
  17.0 3.4 %collective-permute-start.6 = (bf16[2,128,256]{2,1,0:T(8,128)(2,1)S(1)}, bf16[2,128,256]{2,1,0:T(8,128)(2,1)S(1)}, u32[]{:S(2)}, u32[]{:S(2)}) collective-permute-start(bf16[2,128,256]{2,1,0:T(8,128)(2,1)S(1)} %get-tuple-element.64), channel_id=1, source_target_pairs={{0,7},{1,6},{2,5},{3,4},{4,3},{5,2},{6,1},{7,0},{8,15},{9,14},{10,... | collective-permute-start | bytes 393224 | tf_op jit(solution)/shard_map/ppermute | solution.py:385
  20.3 3.6 %filter_spectra.1.refs_8_.refs_5_ = f32[2,8,256,256]{3,2,1,0:T(8,128)S(1)} custom-call(f32[512,1024]{1,0:T(8,128)S(1)} %copy-done.1, bf16[8,256,256]{2,1,0:T(8,128)(2,1)S(1)} %copy-done), custom_call_target="tpu_custom_call" | custom-call | tf_op jit(solution)/shard_map/filter_spectra/pallas_call | solution.py:172
  23.9 8.2 %collective-permute-done.5.refs_6_ = bf16[2,128,256]{2,1,0:T(8,128)(2,1)S(1)} collective-permute-done((bf16[2,128,256]{2,1,0:T(8,128)(2,1)S(1)}, bf16[2,128,256]{2,1,0:T(8,128)(2,1)S(1)}, u32[]{:S(2)}, u32[]{:S(2)}) %collective-permute-start.5) | collective-permute-done | bytes 131104 | tf_op jit(solution)/shard_map/ppermute | solution.py:385
  32.2 4.8 %conv.2 = (bf16[2,2,128,256]{3,2,1,0:T(8,128)(2,1)S(1)}, bf16[2,2,128,256]{3,2,1,0:T(8,128)(2,1)S(1)}, bf16[2,2,128,256]{3,2,1,0:T(8,128)(2,1)S(1)}, bf16[2,2,12...) custom-call(s32[2]{0:T(128)S(1)} %pad_add_fusion.me, ...), custom_call_target="tpu_custom_call" | custom-call | tf_op jit(solution)/shard_map/conv/pallas_call | solution.py:256
  37.0 0.2 collective-permute-start.10
  37.2 1.8 %collective-permute-done.10.refs_4_ = bf16[4,2,128,256]{3,2,1,0:T(8,128)(2,1)S(1)} collective-permute-done((bf16[4,2,128,256]{3,2,1,0:T(8,128)(2,1)S(1)}, bf16[4,2,128,256]{3,2,1,0:T(8,128)(2,1)S(1)}, u32[]{:S(2)}, u32[]{:S(2)}) %collective-permute-start.10) | collective-permute-done | bytes 524320 | tf_op jit(solution)/shard_map/ppermute | solution.py:385
  39.0 4.8 %conv.3 = (bf16[2,2,128,256]{3,2,1,0:T(8,128)(2,1)S(1)}, bf16[2,2,128,256]{3,2,1,0:T(8,128)(2,1)S(1)}, bf16[2,2,128,256]{3,2,1,0:T(8,128)(2,1)S(1)}, bf16[2,2,12...) custom-call(s32[2]{0:T(128)S(1)} %pad_add_fusion.me, ...), custom_call_target="tpu_custom_call", output_to_operand_aliasing={{0}: (9, {}), {1}: (10, {}), {2}: (11, {}), {3}: (12, {}), ... | custom-call | tf_op jit(solution)/shard_map/conv/pallas_call | solution.py:256
  43.8 1.2 %collective-permute-start.18 = (bf16[2,256,512]{2,1,0:T(8,128)(2,1)S(1)}, bf16[2,256,512]{2,1,0:T(8,128)(2,1)S(1)}, u32[]{:S(2)}, u32[]{:S(2)}) collective-permute-start(bf16[2,256,512]{2,1,0:T(8,128)(2,1)S(1)} %get-tuple-element.98), channel_id=1, source_target_pairs={{0,8},{8,0},{16,24},{24,16},{1,9},{9,1},{17,25},{25,17},{2,10},{10... | collective-permute-start | bytes 1572872 | tf_op jit(solution)/shard_map/ppermute | solution.py:351
  45.0 1.5 %collective-permute-start.16 = (bf16[2,2,2,128,256]{4,3,2,1,0:T(8,128)(2,1)S(1)}, bf16[2,2,2,128,256]{4,3,2,1,0:T(8,128)(2,1)S(1)}, u32[]{:S(2)}, u32[]{:S(2)}) collective-permute-start(bf16[2,2,2,128,256]{4,3,2,1,0:T(8,128)(2,1)S(1)} %get-tuple-element.88), channel_id=1, source_target_pairs={{0,6},{1,7},{2,4},{3,5},{4,2},{5,3},{6,0},{7,1},{8,14},{9,15},{10,... | collective-permute-start | bytes 1572872 | tf_op jit(solution)/shard_map/ppermute | solution.py:385
  46.5 1.5 %collective-permute-start.14 = (bf16[2,2,128,256]{3,2,1,0:T(8,128)(2,1)S(1)}, bf16[2,2,128,256]{3,2,1,0:T(8,128)(2,1)S(1)}, u32[]{:S(2)}, u32[]{:S(2)}) collective-permute-start(bf16[2,2,128,256]{3,2,1,0:T(8,128)(2,1)S(1)} %get-tuple-element.86), channel_id=1, source_target_pairs={{0,2},{1,3},{2,0},{3,1},{4,6},{5,7},{6,4},{7,5},{8,10},{9,11},{10,... | collective-permute-start | bytes 786440 | tf_op jit(solution)/shard_map/ppermute | solution.py:385
  48.0 0.5 collective-permute-start.15
  48.5 17.0 %collective-permute-done.14.refs_2_.refs_0_ = bf16[2,2,128,256]{3,2,1,0:T(8,128)(2,1)S(1)} collective-permute-done((bf16[2,2,128,256]{3,2,1,0:T(8,128)(2,1)S(1)}, bf16[2,2,128,256]{3,2,1,0:T(8,128)(2,1)S(1)}, u32[]{:S(2)}, u32[]{:S(2)}) %collective-permute-start.14) | collective-permute-done | bytes 262176 | tf_op jit(solution)/shard_map/ppermute | solution.py:385
  65.5 0.1 add_grads.1
  65.6 2.7 %collective-permute-start.19 = (bf16[1,256,512]{2,1,0:T(8,128)(2,1)S(1)}, bf16[1,256,512]{2,1,0:T(8,128)(2,1)S(1)}, u32[]{:S(2)}, u32[]{:S(2)}) collective-permute-start(bf16[1,256,512]{2,1,0:T(8,128)(2,1)S(1)} %get-tuple-element.100), channel_id=1, source_target_pairs={{0,16},{8,24},{16,0},{24,8},{1,17},{9,25},{17,1},{25,9},{2,18},{10... | collective-permute-start | bytes 786440 | tf_op jit(solution)/shard_map/ppermute | solution.py:351
  68.3 0.6 collective-permute-start.17
  68.8 0.8 collective-permute-start.11
  69.7 0.9 %collective-permute-start.12 = (bf16[2,2,128,256]{3,2,1,0:T(8,128)(2,1)S(1)}, bf16[2,2,128,256]{3,2,1,0:T(8,128)(2,1)S(1)}, u32[]{:S(2)}, u32[]{:S(2)}) collective-permute-start(bf16[2,2,128,256]{3,2,1,0:T(8,128)(2,1)S(1)} %get-tuple-element.83), channel_id=1, source_target_pairs={{0,5},{1,4},{2,7},{3,6},{4,1},{5,0},{6,3},{7,2},{8,13},{9,12},{10,... | collective-permute-start | bytes 786440 | tf_op jit(solution)/shard_map/ppermute | solution.py:385
  70.5 9.8 %collective-permute-done.19.got = bf16[1,256,512]{2,1,0:T(8,128)(2,1)S(1)} collective-permute-done((bf16[1,256,512]{2,1,0:T(8,128)(2,1)S(1)}, bf16[1,256,512]{2,1,0:T(8,128)(2,1)S(1)}, u32[]{:S(2)}, u32[]{:S(2)}) %collective-permute-start.19) | collective-permute-done | bytes 262176 | tf_op jit(solution)/shard_map/ppermute | solution.py:351
  80.3 1.1 %turn_grads.1 = f32[512,256]{1,0:T(8,128)} custom-call(f32[1,256,512]{2,1,0:T(8,128)S(1)} %get-tuple-element.99.keep, bf16[1,256,512]{2,1,0:T(8,128)(2,1)S(1)} %collective-permute-done.19.got), custom_call_target="tpu_custom_call" | custom-call | tf_op jit(solution)/shard_map/turn_grads/pallas_call | solution.py:365
  81.4 3.8 %gate.2 = (bf16[128,4096]{1,0:T(8,128)(2,1)}, bf16[128,4096]{1,0:T(8,128)(2,1)}, bf16[128,4096]{1,0:T(8,128)(2,1)}, bf16[128,4096]{1,0:T(8,128)(2,1)}) custom-call(s32[2]{0:T(128)S(1)} %pad_add_fusion.me, bf16[128,4096]{1,0:T(8,128)(2,1)S(1)} %get-tuple-element.53.query, bf16[128,4096]{1,0:T(8,128)(2,1)S(1)} %get-tuple-element.54.grad, ...), custom_call_target="tpu_custom_call" | custom-call | tf_op jit(solution)/shard_map/gate/pallas_call | solution.py:319
  85.2 2.2 %gate.3 = (bf16[128,4096]{1,0:T(8,128)(2,1)}, bf16[128,4096]{1,0:T(8,128)(2,1)}, bf16[128,4096]{1,0:T(8,128)(2,1)}, bf16[128,4096]{1,0:T(8,128)(2,1)}) custom-call(s32[2]{0:T(128)S(1)} %pad_add_fusion.me, bf16[128,4096]{1,0:T(8,128)(2,1)S(1)} %get-tuple-element.53.query, ...), custom_call_target="tpu_custom_call", output_to_operand_aliasing={{0}: (8, {}), {1}: (9, {}), {2}: (10, {}), {3}: (11, {})} | custom-call | tf_op jit(solution)/shard_map/gate/pallas_call | solution.py:319
  (29 shorter events, 0.1 us)
Async XLA Ops:
  0.6 19.7 %copy-start = (bf16[8,256,256]{2,1,0:T(8,128)(2,1)S(1)}, bf16[8,256,256]{2,1,0:T(8,128)(2,1)}, u32[]{:S(2)}) copy-start(bf16[8,256,256]{2,1,0:T(8,128)(2,1)} %constant.12.clone.fwd.refs_9_.refs_6_) | copy-start | bytes 3145732
  0.6 19.7 %copy-start.1 = (f32[512,1024]{1,0:T(8,128)S(1)}, f32[512,1024]{1,0:T(8,128)}, u32[]{:S(2)}) copy-start(f32[512,1024]{1,0:T(8,128)} %filt.1) | copy-start | bytes 6291460
  3.9 28.2 %copy-start.2 = (bf16[8,128,256]{2,1,0:T(8,128)(2,1)S(1)}, bf16[8,128,256]{2,1,0:T(8,128)(2,1)}, u32[]{:S(2)}) copy-start(bf16[8,128,256]{2,1,0:T(8,128)(2,1)} %constant.13.clone.refs_10_.refs_7_) | copy-start | bytes 1572868
  3.9 5.8 %collective-permute-start = (bf16[2,128,256]{2,1,0:T(8,128)(2,1)S(1)}, bf16[2,128,256]{2,1,0:T(8,128)(2,1)S(1)}, u32[]{:S(2)}, u32[]{:S(2)}) collective-permute-start(bf16[2,128,256]{2,1,0:T(8,128)(2,1)S(1)} %get-tuple-element.58), channel_id=1, source_target_pairs={{0,1},{1,0},{2,3},{3,2},{4,5},{5,4},{6,7},{7,6},{8,9},{9,8},{10,11... | collective-permute-start | bytes 393224 | tf_op jit(solution)/shard_map/ppermute | solution.py:385
  4.5 6.7 %collective-permute-start.1 = (bf16[2,128,256]{2,1,0:T(8,128)(2,1)S(1)}, bf16[2,128,256]{2,1,0:T(8,128)(2,1)S(1)}, u32[]{:S(2)}, u32[]{:S(2)}) collective-permute-start(bf16[2,128,256]{2,1,0:T(8,128)(2,1)S(1)} %get-tuple-element.59), channel_id=1, source_target_pairs={{0,2},{1,3},{2,0},{3,1},{4,6},{5,7},{6,4},{7,5},{8,10},{9,11},{10,... | collective-permute-start | bytes 393224 | tf_op jit(solution)/shard_map/ppermute | solution.py:385
  7.0 8.2 %collective-permute-start.2 = (bf16[2,128,256]{2,1,0:T(8,128)(2,1)S(1)}, bf16[2,128,256]{2,1,0:T(8,128)(2,1)S(1)}, u32[]{:S(2)}, u32[]{:S(2)}) collective-permute-start(bf16[2,128,256]{2,1,0:T(8,128)(2,1)S(1)} %get-tuple-element.60), channel_id=1, source_target_pairs={{0,4},{1,5},{2,6},{3,7},{4,0},{5,1},{6,2},{7,3},{8,12},{9,13},{10,... | collective-permute-start | bytes 393224 | tf_op jit(solution)/shard_map/ppermute | solution.py:385
  8.5 8.4 %collective-permute-start.3 = (bf16[2,128,256]{2,1,0:T(8,128)(2,1)S(1)}, bf16[2,128,256]{2,1,0:T(8,128)(2,1)S(1)}, u32[]{:S(2)}, u32[]{:S(2)}) collective-permute-start(bf16[2,128,256]{2,1,0:T(8,128)(2,1)S(1)} %get-tuple-element.61), channel_id=1, source_target_pairs={{0,6},{1,7},{2,4},{3,5},{4,2},{5,3},{6,0},{7,1},{8,14},{9,15},{10,... | collective-permute-start | bytes 393224 | tf_op jit(solution)/shard_map/ppermute | solution.py:385
  8.6 8.4 %collective-permute-start.4 = (bf16[2,128,256]{2,1,0:T(8,128)(2,1)S(1)}, bf16[2,128,256]{2,1,0:T(8,128)(2,1)S(1)}, u32[]{:S(2)}, u32[]{:S(2)}) collective-permute-start(bf16[2,128,256]{2,1,0:T(8,128)(2,1)S(1)} %get-tuple-element.62), channel_id=1, source_target_pairs={{0,3},{1,2},{2,1},{3,0},{4,7},{5,6},{6,5},{7,4},{8,11},{9,10},{10,... | collective-permute-start | bytes 393224 | tf_op jit(solution)/shard_map/ppermute | solution.py:385
  9.7 27.2 %collective-permute-start.7 = (bf16[2,2,128,256]{3,2,1,0:T(8,128)(2,1)S(1)}, bf16[2,2,128,256]{3,2,1,0:T(8,128)(2,1)S(1)}, u32[]{:S(2)}, u32[]{:S(2)}) collective-permute-start(bf16[2,2,128,256]{3,2,1,0:T(8,128)(2,1)S(1)} %get-tuple-element.67), channel_id=1, source_target_pairs={{0,2},{1,3},{2,0},{3,1},{4,6},{5,7},{6,4},{7,5},{8,10},{9,11},{10,... | collective-permute-start | bytes 786440 | tf_op jit(solution)/shard_map/ppermute | solution.py:385
  11.2 25.8 %collective-permute-start.8 = (bf16[2,2,128,256]{3,2,1,0:T(8,128)(2,1)S(1)}, bf16[2,2,128,256]{3,2,1,0:T(8,128)(2,1)S(1)}, u32[]{:S(2)}, u32[]{:S(2)}) collective-permute-start(bf16[2,2,128,256]{3,2,1,0:T(8,128)(2,1)S(1)} %get-tuple-element.68), channel_id=1, source_target_pairs={{0,4},{1,5},{2,6},{3,7},{4,0},{5,1},{6,2},{7,3},{8,12},{9,13},{10,... | collective-permute-start | bytes 786440 | tf_op jit(solution)/shard_map/ppermute | solution.py:385
  15.2 21.7 %collective-permute-start.9 = (bf16[2,2,128,256]{3,2,1,0:T(8,128)(2,1)S(1)}, bf16[2,2,128,256]{3,2,1,0:T(8,128)(2,1)S(1)}, u32[]{:S(2)}, u32[]{:S(2)}) collective-permute-start(bf16[2,2,128,256]{3,2,1,0:T(8,128)(2,1)S(1)} %get-tuple-element.69), channel_id=1, source_target_pairs={{0,6},{1,7},{2,4},{3,5},{4,2},{5,3},{6,0},{7,1},{8,14},{9,15},{10,... | collective-permute-start | bytes 786440 | tf_op jit(solution)/shard_map/ppermute | solution.py:385
  17.0 15.2 %collective-permute-start.5 = (bf16[2,128,256]{2,1,0:T(8,128)(2,1)S(1)}, bf16[2,128,256]{2,1,0:T(8,128)(2,1)S(1)}, u32[]{:S(2)}, u32[]{:S(2)}) collective-permute-start(bf16[2,128,256]{2,1,0:T(8,128)(2,1)S(1)} %get-tuple-element.63), channel_id=1, source_target_pairs={{0,5},{1,4},{2,7},{3,6},{4,1},{5,0},{6,3},{7,2},{8,13},{9,12},{10,... | collective-permute-start | bytes 393224 | tf_op jit(solution)/shard_map/ppermute | solution.py:385
  17.0 15.2 %collective-permute-start.6 = (bf16[2,128,256]{2,1,0:T(8,128)(2,1)S(1)}, bf16[2,128,256]{2,1,0:T(8,128)(2,1)S(1)}, u32[]{:S(2)}, u32[]{:S(2)}) collective-permute-start(bf16[2,128,256]{2,1,0:T(8,128)(2,1)S(1)} %get-tuple-element.64), channel_id=1, source_target_pairs={{0,7},{1,6},{2,5},{3,4},{4,3},{5,2},{6,1},{7,0},{8,15},{9,14},{10,... | collective-permute-start | bytes 393224 | tf_op jit(solution)/shard_map/ppermute | solution.py:385
  37.0 2.0 %collective-permute-start.10 = (bf16[4,2,128,256]{3,2,1,0:T(8,128)(2,1)S(1)}, bf16[4,2,128,256]{3,2,1,0:T(8,128)(2,1)S(1)}, u32[]{:S(2)}, u32[]{:S(2)}) collective-permute-start(bf16[4,2,128,256]{3,2,1,0:T(8,128)(2,1)S(1)} %pack.2), channel_id=1, source_target_pairs={{0,1},{1,0},{2,3},{3,2},{4,5},{5,4},{6,7},{7,6},{8,9},{9,8},{10,11... | collective-permute-start | bytes 1572872 | tf_op jit(solution)/shard_map/ppermute | solution.py:385
  43.8 37.6 %copy-start.3 = (f32[4096]{0:T(1024)S(1)}, f32[4096]{0:T(1024)}, u32[]{:S(2)}) copy-start(f32[4096]{0:T(1024)} %param.13) | copy-start | bytes 49156
  43.8 21.7 %collective-permute-start.18 = (bf16[2,256,512]{2,1,0:T(8,128)(2,1)S(1)}, bf16[2,256,512]{2,1,0:T(8,128)(2,1)S(1)}, u32[]{:S(2)}, u32[]{:S(2)}) collective-permute-start(bf16[2,256,512]{2,1,0:T(8,128)(2,1)S(1)} %get-tuple-element.98), channel_id=1, source_target_pairs={{0,8},{8,0},{16,24},{24,16},{1,9},{9,1},{17,25},{25,17},{2,10},{10... | collective-permute-start | bytes 1572872 | tf_op jit(solution)/shard_map/ppermute | solution.py:351
  45.0 23.3 %collective-permute-start.16 = (bf16[2,2,2,128,256]{4,3,2,1,0:T(8,128)(2,1)S(1)}, bf16[2,2,2,128,256]{4,3,2,1,0:T(8,128)(2,1)S(1)}, u32[]{:S(2)}, u32[]{:S(2)}) collective-permute-start(bf16[2,2,2,128,256]{4,3,2,1,0:T(8,128)(2,1)S(1)} %get-tuple-element.88), channel_id=1, source_target_pairs={{0,6},{1,7},{2,4},{3,5},{4,2},{5,3},{6,0},{7,1},{8,14},{9,15},{10,... | collective-permute-start | bytes 1572872 | tf_op jit(solution)/shard_map/ppermute | solution.py:385
  46.5 19.0 %collective-permute-start.14 = (bf16[2,2,128,256]{3,2,1,0:T(8,128)(2,1)S(1)}, bf16[2,2,128,256]{3,2,1,0:T(8,128)(2,1)S(1)}, u32[]{:S(2)}, u32[]{:S(2)}) collective-permute-start(bf16[2,2,128,256]{3,2,1,0:T(8,128)(2,1)S(1)} %get-tuple-element.86), channel_id=1, source_target_pairs={{0,2},{1,3},{2,0},{3,1},{4,6},{5,7},{6,4},{7,5},{8,10},{9,11},{10,... | collective-permute-start | bytes 786440 | tf_op jit(solution)/shard_map/ppermute | solution.py:385
  48.0 17.5 %collective-permute-start.15 = (bf16[2,2,128,256]{3,2,1,0:T(8,128)(2,1)S(1)}, bf16[2,2,128,256]{3,2,1,0:T(8,128)(2,1)S(1)}, u32[]{:S(2)}, u32[]{:S(2)}) collective-permute-start(bf16[2,2,128,256]{3,2,1,0:T(8,128)(2,1)S(1)} %get-tuple-element.87), channel_id=1, source_target_pairs={{0,4},{1,5},{2,6},{3,7},{4,0},{5,1},{6,2},{7,3},{8,12},{9,13},{10,... | collective-permute-start | bytes 786440 | tf_op jit(solution)/shard_map/ppermute | solution.py:385
  65.6 14.7 %collective-permute-start.19 = (bf16[1,256,512]{2,1,0:T(8,128)(2,1)S(1)}, bf16[1,256,512]{2,1,0:T(8,128)(2,1)S(1)}, u32[]{:S(2)}, u32[]{:S(2)}) collective-permute-start(bf16[1,256,512]{2,1,0:T(8,128)(2,1)S(1)} %get-tuple-element.100), channel_id=1, source_target_pairs={{0,16},{8,24},{16,0},{24,8},{1,17},{9,25},{17,1},{25,9},{2,18},{10... | collective-permute-start | bytes 786440 | tf_op jit(solution)/shard_map/ppermute | solution.py:351
  68.2 13.1 %collective-permute-start.13 = (bf16[2,2,128,256]{3,2,1,0:T(8,128)(2,1)S(1)}, bf16[2,2,128,256]{3,2,1,0:T(8,128)(2,1)S(1)}, u32[]{:S(2)}, u32[]{:S(2)}) collective-permute-start(bf16[2,2,128,256]{3,2,1,0:T(8,128)(2,1)S(1)} %get-tuple-element.85), channel_id=1, source_target_pairs={{0,1},{1,0},{2,3},{3,2},{4,5},{5,4},{6,7},{7,6},{8,9},{9,8},{10,11... | collective-permute-start | bytes 786440 | tf_op jit(solution)/shard_map/ppermute | solution.py:385
  68.3 13.1 %collective-permute-start.17 = (bf16[1,2,2,128,256]{4,3,2,1,0:T(8,128)(2,1)S(1)}, bf16[1,2,2,128,256]{4,3,2,1,0:T(8,128)(2,1)S(1)}, u32[]{:S(2)}, u32[]{:S(2)}) collective-permute-start(bf16[1,2,2,128,256]{4,3,2,1,0:T(8,128)(2,1)S(1)} %pack.3), channel_id=1, source_target_pairs={{0,1},{1,0},{2,3},{3,2},{4,5},{5,4},{6,7},{7,6},{8,9},{9,8},{10,11... | collective-permute-start | bytes 786440 | tf_op jit(solution)/shard_map/ppermute | solution.py:385
  68.8 16.3 %collective-permute-start.11 = (bf16[2,2,128,256]{3,2,1,0:T(8,128)(2,1)S(1)}, bf16[2,2,128,256]{3,2,1,0:T(8,128)(2,1)S(1)}, u32[]{:S(2)}, u32[]{:S(2)}) collective-permute-start(bf16[2,2,128,256]{3,2,1,0:T(8,128)(2,1)S(1)} %get-tuple-element.82), channel_id=1, source_target_pairs={{0,3},{1,2},{2,1},{3,0},{4,7},{5,6},{6,5},{7,4},{8,11},{9,10},{10,... | collective-permute-start | bytes 786440 | tf_op jit(solution)/shard_map/ppermute | solution.py:385
  69.7 15.5 %collective-permute-start.12 = (bf16[2,2,128,256]{3,2,1,0:T(8,128)(2,1)S(1)}, bf16[2,2,128,256]{3,2,1,0:T(8,128)(2,1)S(1)}, u32[]{:S(2)}, u32[]{:S(2)}) collective-permute-start(bf16[2,2,128,256]{3,2,1,0:T(8,128)(2,1)S(1)} %get-tuple-element.83), channel_id=1, source_target_pairs={{0,5},{1,4},{2,7},{3,6},{4,1},{5,0},{6,3},{7,2},{8,13},{9,12},{10,... | collective-permute-start | bytes 786440 | tf_op jit(solution)/shard_map/ppermute | solution.py:385

commit v12 on v8

--- a/solution.py
+++ b/solution.py
@@ -140,46 +140,45 @@
     return [slice(i, i + 128) for i in range(0, width, 128)]
 
 
-def filter_kernel(filt, fwd, *refs):
+def filter_kernel(half, filt, fwd, *refs):
     spec, x, u = refs[-3:]
     m2, width = x.shape[1] // CLASSES, u.shape[-1]
     groups = lane_groups(width)
     rows = m2 // CLASSES
-    for half in range(HALVES):
+    for g, lanes in enumerate(groups):
+        x[g] = filt[half * width + lanes.start : half * width + lanes.stop, :].T
+    for c in range(CLASSES):
         for g, lanes in enumerate(groups):
-            x[g] = filt[half * width + lanes.start : half * width + lanes.stop, :].T
-        for c in range(CLASSES):
-            for g, lanes in enumerate(groups):
-                hi, lo = parts(x[g, pl.ds(c, m2, stride=CLASSES), :])
-                u[c, :, lanes] = dot(fwd[c], jnp.concatenate([hi, hi], 0)) + dot(fwd[c, :, :m2], lo)
-
-        def step(i, carry):
-            r = pl.multiple_of(i * rows, rows)
-            re, im = pl.ds(r, rows), pl.ds(m2 + r, rows)
-            for lanes in groups:
-                z = dft([(u[c, re, lanes], u[c, im, lanes]) for c in range(CLASSES)], -1)
-                for k in range(CLASSES):
-                    spec[half, k, re, lanes], spec[half, k, im, lanes] = z[k]
-            return carry
-
-        lax.fori_loop(0, CLASSES, step, 0)
-
-
-def filter_spectra(filters, fwd, arrived):
+            hi, lo = parts(x[g, pl.ds(c, m2, stride=CLASSES), :])
+            u[c, :, lanes] = dot(fwd[c], jnp.concatenate([hi, hi], 0)) + dot(fwd[c, :, :m2], lo)
+
+    def step(i, carry):
+        r = pl.multiple_of(i * rows, rows)
+        re, im = pl.ds(r, rows), pl.ds(m2 + r, rows)
+        for lanes in groups:
+            z = dft([(u[c, re, lanes], u[c, im, lanes]) for c in range(CLASSES)], -1)
+            for k in range(CLASSES):
+                spec[k, re, lanes], spec[k, im, lanes] = z[k]
+        return carry
+
+    lax.fori_loop(0, CLASSES, step, 0)
+
+
+def filter_spectrum(half, filters, fwd, arrived):
     chans, length = filters.shape
     width = chans // HALVES
     m2 = length // CLASSES
     return pl.pallas_call(
-        filter_kernel,
+        functools.partial(filter_kernel, half),
         in_specs=[VMEM] * (2 + len(arrived)),
         out_specs=VMEM,
-        out_shape=pltpu.VMEM((HALVES, CLASSES, 2 * m2, width), F32),
+        out_shape=pltpu.VMEM((CLASSES, 2 * m2, width), F32),
         scratch_shapes=[
             pltpu.VMEM((width // 128, length, 128), F32),
             pltpu.VMEM((CLASSES, 2 * m2, width), F32),
         ],
         compiler_params=PARAMS,
-        name="filter_spectra",
+        name="filter_spectrum",
     )(filters, fwd, *arrived)
 
 
@@ -212,7 +211,7 @@
         for lanes in groups:
             kv = dft([(u[0, c, re, lanes], u[0, c, im, lanes]) for c in range(CLASSES)], -1)
             wt = dft([(u[1, c, re, lanes], u[1, c, im, lanes]) for c in range(CLASSES)], -1)
-            fs = [(filt[half, k, re, lanes], filt[half, k, im, lanes]) for k in range(CLASSES)]
+            fs = [(filt[k, re, lanes], filt[k, im, lanes]) for k in range(CLASSES)]
             for o, (left, right, conj) in enumerate([(kv, fs, False), (wt, fs, True), (wt, kv, True)]):
                 z = dft([times(s, t, conj) for s, t in zip(left, right)], 1)
                 for c in range(CLASSES):
@@ -334,23 +333,24 @@
         out[lanes, :] = natural(nat.at[g], total).T
 
 
-def sum_grads(d, keep, send):
+def trade(d, bit, send):
+    return resident(lax.ppermute(send, "dp", [(i, i ^ bit) for i in range(d)]))
+
+
+def add_grads(keep, got):
+    shape = (keep.shape[0] // 2, *keep.shape[1:])
+    return pl.pallas_call(
+        add_kernel,
+        in_specs=[VMEM] * 2,
+        out_specs=[VMEM] * 2,
+        out_shape=[pltpu.VMEM(shape, F32), pltpu.VMEM(shape, BF16)],
+        compiler_params=PARAMS,
+        name="add_grads",
+    )(keep, got)
+
+
+def turn_grads(keep, got):
     _, per, chans = keep.shape
-    bit = 1
-    while True:
-        got = resident(lax.ppermute(send, "dp", [(i, i ^ bit) for i in range(d)]))
-        if keep.shape[0] == 1:
-            break
-        shape = (keep.shape[0] // 2, per, chans)
-        keep, send = pl.pallas_call(
-            add_kernel,
-            in_specs=[VMEM] * 2,
-            out_specs=[VMEM] * 2,
-            out_shape=[pltpu.VMEM(shape, F32), pltpu.VMEM(shape, BF16)],
-            compiler_params=PARAMS,
-            name="add_grads",
-        )(keep, got)
-        bit *= 2
     return pl.pallas_call(
         turn_kernel,
         in_specs=[VMEM] * 2,
@@ -398,13 +398,24 @@
 
     arrays = [in_hbm(x[0]) for x in (key_in, value_in, query_in, grad_out)]
     (key, value, query, grad), got = products(n, me, *arrays)
-    first = exchange(n, peers(n), got[0])
-    second = exchange(n, peers(n), after([first[1]], got[1]))
-    spec = filter_spectra(filters, fwd, [second[1]])
+    js = peers(n)
+    cut = n // 2
+    first = exchange(n, js, got[0])
+    spec = filter_spectrum(0, filters, fwd, first[1:3])
+    second = exchange(n, js[:cut], after([spec], got[1][:cut]))
+    spec_other = filter_spectrum(1, filters, fwd, [spec])
+    second += exchange(n, js[cut:], after([spec_other], got[1][cut:]))
     results = conv(n, d, 0, me, first, spec, fwd, back, [])
-    *mixed, keep, send = conv(n, d, 1, me, second, spec, fwd, back, results)
-    mixed = exchange(n, peers(n), mixed)
-    grad_filter = sum_grads(d, keep, *after([mixed[1]], [send]))
+    *mixed, keep, send = conv(n, d, 1, me, second, spec_other, fwd, back, results)
+
+    bits = [1 << b for b in range(d.bit_length() - 1)]
+    traded = trade(d, 1, send)
+    early = exchange(n, js[:-1], mixed[:-1])
+    for bit in bits[1:]:
+        keep, send = add_grads(keep, traded)
+        traded = trade(d, bit, send)
+    grad_filter = turn_grads(keep, traded)
+    mixed = early + exchange(n, js[-1:], after([keep], mixed[-1:]))
 
     outs = []
     early = n - 2

time: 72.1 us -> 70.8 us (0.982)
  waiting for transfers between devices: 22.4 us -> 20 us
  starting transfers between devices: 25.2 us -> 26.2 us
    ppermute x21, waiting for transfers between devices: 17.2 us -> 7.39 us  [exchange(): lax.ppermute(block, 'ctx', [(i, i ^ j) for i in range(n)])]
    ppermute x2, waiting for transfers between devices: 5.27 us -> 12.6 us  [trade(): return resident(lax.ppermute(send, 'dp', [(i, i ^ bit) for i in range(d)]))]
    ppermute x21, starting transfers between devices: 21 us -> 22.5 us  [exchange(): lax.ppermute(block, 'ctx', [(i, i ^ j) for i in range(n)])]
    pallas_call x3 -> x4, Pallas kernels: 4.78 us -> 4.79 us  [the longest x2 3.6 us: filter_spectrum(): pl.pallas_call(functools.partial(filter_kernel, half), in_specs=[VMEM] *...]
  transfers between devices with their start and end apart: 23 -> 23, of which waited for: 10 -> 8; matrix products, arithmetic and copies ran while one was open for 0% -> 0% of each run, Pallas kernels for 20% -> 19%
where the time goes in v12:
time: 70.8 us; the launch traced here: 70.6 us
  starting transfers between devices  26.2 us (37%)
  Pallas kernels  23.5 us (33%)
  waiting for transfers between devices  20 us (28%)
  between operations  0.94 us (1%)
    ppermute x21, starting transfers between devices, exchange(): lax.ppermute(block, 'ctx', [(i, i ^ j) for i in range(n)])  22.5 us
    ppermute x2, waiting for transfers between devices, trade(): return resident(lax.ppermute(send, 'dp', [(i, i ^ bit) for i in range(d)]))  12.6 us
    pallas_call x2, Pallas kernels, conv(): pl.pallas_call(functools.partial(conv_kernel, n, d, half), in_specs=[SMEM...  9.58 us
    ppermute x21, waiting for transfers between devices, exchange(): lax.ppermute(block, 'ctx', [(i, i ^ j) for i in range(n)])  7.39 us
    pallas_call x2, Pallas kernels, gate(): pl.pallas_call(functools.partial(gate_kernel, js), in_specs=[SMEM] + [VME...  5.93 us
    ppermute x2, starting transfers between devices, trade(): return resident(lax.ppermute(send, 'dp', [(i, i ^ bit) for i in range(d)]))  3.65 us
    pallas_call x2, Pallas kernels, filter_spectrum(): pl.pallas_call(functools.partial(filter_kernel, half), in_specs=[VMEM] *...  3.6 us
    pallas_call x1, Pallas kernels, products(): pl.pallas_call(functools.partial(product_kernel, n), in_specs=[SMEM] + [H...  3.14 us
  transfers between devices with their start and end apart: 23, of which 8 were waited for; matrix products, arithmetic and copies ran while one was open for 0% of the time, Pallas kernels for 19%

profile of v12, /device:TPU:0, one launch (start us, length us, event | category | flops | bytes accessed | tf_op | source)
XLA Modules:
  0.0 70.6 jit_solution(13758080601104899356)
XLA Ops:
  0.7 3.1 %products.1 = (bf16[128,4096]{1,0:T(8,128)(2,1)S(1)}, bf16[128,4096]{1,0:T(8,128)(2,1)S(1)}, bf16[128,4096]{1,0:T(8,128)(2,1)S(1)}, bf16[128,4096]{1,0:T(8,128)(...) custom-call(s32[2]{0:T(128)S(1)} %pad_add_fusion.me, ...), custom_call_target="tpu_custom_call" | custom-call | tf_op jit(solution)/shard_map/products/pallas_call | solution.py:126
  4.4 2.6 %collective-permute-start.1 = (bf16[2,128,256]{2,1,0:T(8,128)(2,1)S(1)}, bf16[2,128,256]{2,1,0:T(8,128)(2,1)S(1)}, u32[]{:S(2)}, u32[]{:S(2)}) collective-permute-start(bf16[2,128,256]{2,1,0:T(8,128)(2,1)S(1)} %get-tuple-element.68), channel_id=1, source_target_pairs={{0,2},{1,3},{2,0},{3,1},{4,6},{5,7},{6,4},{7,5},{8,10},{9,11},{10,... | collective-permute-start | bytes 393224 | tf_op jit(solution)/shard_map/ppermute | solution.py:371
  6.9 1.5 %collective-permute-start.9 = (bf16[2,128,256]{2,1,0:T(8,128)(2,1)S(1)}, bf16[2,128,256]{2,1,0:T(8,128)(2,1)S(1)}, u32[]{:S(2)}, u32[]{:S(2)}) collective-permute-start(bf16[2,128,256]{2,1,0:T(8,128)(2,1)S(1)} %get-tuple-element.86), channel_id=1, source_target_pairs={{0,4},{1,5},{2,6},{3,7},{4,0},{5,1},{6,2},{7,3},{8,12},{9,13},{10,... | collective-permute-start | bytes 393224 | tf_op jit(solution)/shard_map/ppermute | solution.py:371
  8.5 1.2 %collective-permute-start.11 = (bf16[2,128,256]{2,1,0:T(8,128)(2,1)S(1)}, bf16[2,128,256]{2,1,0:T(8,128)(2,1)S(1)}, u32[]{:S(2)}, u32[]{:S(2)}) collective-permute-start(bf16[2,128,256]{2,1,0:T(8,128)(2,1)S(1)} %get-tuple-element.88), channel_id=1, source_target_pairs={{0,3},{1,2},{2,1},{3,0},{4,7},{5,6},{6,5},{7,4},{8,11},{9,10},{10,... | collective-permute-start | bytes 393224 | tf_op jit(solution)/shard_map/ppermute | solution.py:371
  9.7 2.0 %collective-permute-start.12 = (bf16[2,128,256]{2,1,0:T(8,128)(2,1)S(1)}, bf16[2,128,256]{2,1,0:T(8,128)(2,1)S(1)}, u32[]{:S(2)}, u32[]{:S(2)}) collective-permute-start(bf16[2,128,256]{2,1,0:T(8,128)(2,1)S(1)} %get-tuple-element.89), channel_id=1, source_target_pairs={{0,5},{1,4},{2,7},{3,6},{4,1},{5,0},{6,3},{7,2},{8,13},{9,12},{10,... | collective-permute-start | bytes 393224 | tf_op jit(solution)/shard_map/ppermute | solution.py:371
  11.7 1.3 %collective-permute-start.13 = (bf16[2,128,256]{2,1,0:T(8,128)(2,1)S(1)}, bf16[2,128,256]{2,1,0:T(8,128)(2,1)S(1)}, u32[]{:S(2)}, u32[]{:S(2)}) collective-permute-start(bf16[2,128,256]{2,1,0:T(8,128)(2,1)S(1)} %get-tuple-element.90), channel_id=1, source_target_pairs={{0,7},{1,6},{2,5},{3,4},{4,3},{5,2},{6,1},{7,0},{8,15},{9,14},{10,... | collective-permute-start | bytes 393224 | tf_op jit(solution)/shard_map/ppermute | solution.py:371
  13.0 1.9 %filter_spectrum.2.refs_0_.refs_8_ = f32[8,256,256]{2,1,0:T(8,128)S(1)} custom-call(f32[512,1024]{1,0:T(8,128)S(1)} %copy-done.1, bf16[8,256,256]{2,1,0:T(8,128)(2,1)S(1)} %copy-done, bf16[2,128,256]{2,1,0:T(8,128)(2,1)S(1)} %collective-permute-done.refs_0_.refs_1_, bf16[2,128,256]{2,1,0:T(8,128)(2,1)S(1)} %collective-permute-done.1.refs_1_.refs_2_), custom_call_target="tpu_custom_call" | custom-call | tf_op jit(solution)/shard_map/filter_spectrum/pallas_call | solution.py:171
  15.0 1.3 %collective-permute-start.2 = (bf16[2,128,256]{2,1,0:T(8,128)(2,1)S(1)}, bf16[2,128,256]{2,1,0:T(8,128)(2,1)S(1)}, u32[]{:S(2)}, u32[]{:S(2)}) collective-permute-start(bf16[2,128,256]{2,1,0:T(8,128)(2,1)S(1)} %get-tuple-element.74), channel_id=1, source_target_pairs={{0,1},{1,0},{2,3},{3,2},{4,5},{5,4},{6,7},{7,6},{8,9},{9,8},{10,11... | collective-permute-start | bytes 393224 | tf_op jit(solution)/shard_map/ppermute | solution.py:371
  16.3 0.7 %collective-permute-start.3 = (bf16[2,128,256]{2,1,0:T(8,128)(2,1)S(1)}, bf16[2,128,256]{2,1,0:T(8,128)(2,1)S(1)}, u32[]{:S(2)}, u32[]{:S(2)}) collective-permute-start(bf16[2,128,256]{2,1,0:T(8,128)(2,1)S(1)} %get-tuple-element.75), channel_id=1, source_target_pairs={{0,2},{1,3},{2,0},{3,1},{4,6},{5,7},{6,4},{7,5},{8,10},{9,11},{10,... | collective-permute-start | bytes 393224 | tf_op jit(solution)/shard_map/ppermute | solution.py:371
  17.1 1.7 %filter_spectrum.3.refs_0_.refs_8_ = f32[8,256,256]{2,1,0:T(8,128)S(1)} custom-call(f32[512,1024]{1,0:T(8,128)S(1)} %copy-done.1, bf16[8,256,256]{2,1,0:T(8,128)(2,1)S(1)} %copy-done, f32[8,256,256]{2,1,0:T(8,128)S(1)} %filter_spectrum.2.refs_0_.refs_8_), custom_call_target="tpu_custom_call" | custom-call | tf_op jit(solution)/shard_map/filter_spectrum/pallas_call | solution.py:171
  18.8 1.0 %collective-permute-start.4 = (bf16[2,128,256]{2,1,0:T(8,128)(2,1)S(1)}, bf16[2,128,256]{2,1,0:T(8,128)(2,1)S(1)}, u32[]{:S(2)}, u32[]{:S(2)}) collective-permute-start(bf16[2,128,256]{2,1,0:T(8,128)(2,1)S(1)} %get-tuple-element.76), channel_id=1, source_target_pairs={{0,4},{1,5},{2,6},{3,7},{4,0},{5,1},{6,2},{7,3},{8,12},{9,13},{10,... | collective-permute-start | bytes 393224 | tf_op jit(solution)/shard_map/ppermute | solution.py:371
  19.8 0.9 %collective-permute-done.12.refs_6_ = bf16[2,128,256]{2,1,0:T(8,128)(2,1)S(1)} collective-permute-done((bf16[2,128,256]{2,1,0:T(8,128)(2,1)S(1)}, bf16[2,128,256]{2,1,0:T(8,128)(2,1)S(1)}, u32[]{:S(2)}, u32[]{:S(2)}) %collective-permute-start.12) | collective-permute-done | bytes 131104 | tf_op jit(solution)/shard_map/ppermute | solution.py:371
  20.8 1.1 %collective-permute-start.5 = (bf16[2,128,256]{2,1,0:T(8,128)(2,1)S(1)}, bf16[2,128,256]{2,1,0:T(8,128)(2,1)S(1)}, u32[]{:S(2)}, u32[]{:S(2)}) collective-permute-start(bf16[2,128,256]{2,1,0:T(8,128)(2,1)S(1)} %get-tuple-element.81), channel_id=1, source_target_pairs={{0,6},{1,7},{2,4},{3,5},{4,2},{5,3},{6,0},{7,1},{8,14},{9,15},{10,... | collective-permute-start | bytes 393224 | tf_op jit(solution)/shard_map/ppermute | solution.py:371
  21.9 1.5 %collective-permute-start.6 = (bf16[2,128,256]{2,1,0:T(8,128)(2,1)S(1)}, bf16[2,128,256]{2,1,0:T(8,128)(2,1)S(1)}, u32[]{:S(2)}, u32[]{:S(2)}) collective-permute-start(bf16[2,128,256]{2,1,0:T(8,128)(2,1)S(1)} %get-tuple-element.82), channel_id=1, source_target_pairs={{0,3},{1,2},{2,1},{3,0},{4,7},{5,6},{6,5},{7,4},{8,11},{9,10},{10,... | collective-permute-start | bytes 393224 | tf_op jit(solution)/shard_map/ppermute | solution.py:371
  23.4 0.6 collective-permute-start.7
  24.0 0.6 collective-permute-start.8
  24.6 4.8 %conv.2 = (bf16[2,2,128,256]{3,2,1,0:T(8,128)(2,1)S(1)}, bf16[2,2,128,256]{3,2,1,0:T(8,128)(2,1)S(1)}, bf16[2,2,128,256]{3,2,1,0:T(8,128)(2,1)S(1)}, bf16[2,2,12...) custom-call(s32[2]{0:T(128)S(1)} %pad_add_fusion.me, ...), custom_call_target="tpu_custom_call" | custom-call | tf_op jit(solution)/shard_map/conv/pallas_call | solution.py:247
  29.4 0.8 %collective-permute-done.6.refs_5_ = bf16[2,128,256]{2,1,0:T(8,128)(2,1)S(1)} collective-permute-done((bf16[2,128,256]{2,1,0:T(8,128)(2,1)S(1)}, bf16[2,128,256]{2,1,0:T(8,128)(2,1)S(1)}, u32[]{:S(2)}, u32[]{:S(2)}) %collective-permute-start.6) | collective-permute-done | bytes 131104 | tf_op jit(solution)/shard_map/ppermute | solution.py:371
  30.8 1.6 %collective-permute-done.8.refs_7_ = bf16[2,128,256]{2,1,0:T(8,128)(2,1)S(1)} collective-permute-done((bf16[2,128,256]{2,1,0:T(8,128)(2,1)S(1)}, bf16[2,128,256]{2,1,0:T(8,128)(2,1)S(1)}, u32[]{:S(2)}, u32[]{:S(2)}) %collective-permute-start.8) | collective-permute-done | bytes 131104 | tf_op jit(solution)/shard_map/ppermute | solution.py:371
  32.4 4.8 %conv.3 = (bf16[2,2,128,256]{3,2,1,0:T(8,128)(2,1)S(1)}, bf16[2,2,128,256]{3,2,1,0:T(8,128)(2,1)S(1)}, bf16[2,2,128,256]{3,2,1,0:T(8,128)(2,1)S(1)}, bf16[2,2,12...) custom-call(s32[2]{0:T(128)S(1)} %pad_add_fusion.me, ...), custom_call_target="tpu_custom_call", output_to_operand_aliasing={{0}: (12, {}), {1}: (13, {}), {2}: (14, {}), {3}: (15, {}),... | custom-call | tf_op jit(solution)/shard_map/conv/pallas_call | solution.py:247
  37.2 1.3 %collective-permute-start.15 = (bf16[2,256,512]{2,1,0:T(8,128)(2,1)S(1)}, bf16[2,256,512]{2,1,0:T(8,128)(2,1)S(1)}, u32[]{:S(2)}, u32[]{:S(2)}) collective-permute-start(bf16[2,256,512]{2,1,0:T(8,128)(2,1)S(1)} %get-tuple-element.103), channel_id=1, source_target_pairs={{0,8},{8,0},{16,24},{24,16},{1,9},{9,1},{17,25},{25,17},{2,10},{10... | collective-permute-start | bytes 1572872 | tf_op jit(solution)/shard_map/ppermute | solution.py:337
  38.6 1.5 %collective-permute-start.18 = (bf16[2,2,128,256]{3,2,1,0:T(8,128)(2,1)S(1)}, bf16[2,2,128,256]{3,2,1,0:T(8,128)(2,1)S(1)}, u32[]{:S(2)}, u32[]{:S(2)}) collective-permute-start(bf16[2,2,128,256]{3,2,1,0:T(8,128)(2,1)S(1)} %get-tuple-element.108), channel_id=1, source_target_pairs={{0,2},{1,3},{2,0},{3,1},{4,6},{5,7},{6,4},{7,5},{8,10},{9,11},{10,... | collective-permute-start | bytes 786440 | tf_op jit(solution)/shard_map/ppermute | solution.py:371
  40.1 1.4 %collective-permute-start.19 = (bf16[2,2,128,256]{3,2,1,0:T(8,128)(2,1)S(1)}, bf16[2,2,128,256]{3,2,1,0:T(8,128)(2,1)S(1)}, u32[]{:S(2)}, u32[]{:S(2)}) collective-permute-start(bf16[2,2,128,256]{3,2,1,0:T(8,128)(2,1)S(1)} %get-tuple-element.109), channel_id=1, source_target_pairs={{0,4},{1,5},{2,6},{3,7},{4,0},{5,1},{6,2},{7,3},{8,12},{9,13},{10,... | collective-permute-start | bytes 786440 | tf_op jit(solution)/shard_map/ppermute | solution.py:371
  41.5 0.7 %collective-permute-start.20 = (bf16[2,2,128,256]{3,2,1,0:T(8,128)(2,1)S(1)}, bf16[2,2,128,256]{3,2,1,0:T(8,128)(2,1)S(1)}, u32[]{:S(2)}, u32[]{:S(2)}) collective-permute-start(bf16[2,2,128,256]{3,2,1,0:T(8,128)(2,1)S(1)} %get-tuple-element.110), channel_id=1, source_target_pairs={{0,6},{1,7},{2,4},{3,5},{4,2},{5,3},{6,0},{7,1},{8,14},{9,15},{10,... | collective-permute-start | bytes 786440 | tf_op jit(solution)/shard_map/ppermute | solution.py:371
  42.3 9.2 %collective-permute-done.15.got = bf16[2,256,512]{2,1,0:T(8,128)(2,1)S(1)} collective-permute-done((bf16[2,256,512]{2,1,0:T(8,128)(2,1)S(1)}, bf16[2,256,512]{2,1,0:T(8,128)(2,1)S(1)}, u32[]{:S(2)}, u32[]{:S(2)}) %collective-permute-start.15) | collective-permute-done | bytes 524320 | tf_op jit(solution)/shard_map/ppermute | solution.py:337
  51.7 2.4 %collective-permute-start.22 = (bf16[1,256,512]{2,1,0:T(8,128)(2,1)S(1)}, bf16[1,256,512]{2,1,0:T(8,128)(2,1)S(1)}, u32[]{:S(2)}, u32[]{:S(2)}) collective-permute-start(bf16[1,256,512]{2,1,0:T(8,128)(2,1)S(1)} %get-tuple-element.120), channel_id=1, source_target_pairs={{0,16},{8,24},{16,0},{24,8},{1,17},{9,25},{17,1},{25,9},{2,18},{10... | collective-permute-start | bytes 786440 | tf_op jit(solution)/shard_map/ppermute | solution.py:337
  54.1 2.2 %collective-permute-start.14 = (bf16[2,2,128,256]{3,2,1,0:T(8,128)(2,1)S(1)}, bf16[2,2,128,256]{3,2,1,0:T(8,128)(2,1)S(1)}, u32[]{:S(2)}, u32[]{:S(2)}) collective-permute-start(bf16[2,2,128,256]{3,2,1,0:T(8,128)(2,1)S(1)} %get-tuple-element.101), channel_id=1, source_target_pairs={{0,5},{1,4},{2,7},{3,6},{4,1},{5,0},{6,3},{7,2},{8,13},{9,12},{10,... | collective-permute-start | bytes 786440 | tf_op jit(solution)/shard_map/ppermute | solution.py:371
  56.7 3.4 %collective-permute-done.21.refs_5_ = bf16[2,2,128,256]{3,2,1,0:T(8,128)(2,1)S(1)} collective-permute-done((bf16[2,2,128,256]{3,2,1,0:T(8,128)(2,1)S(1)}, bf16[2,2,128,256]{3,2,1,0:T(8,128)(2,1)S(1)}, u32[]{:S(2)}, u32[]{:S(2)}) %collective-permute-start.21) | collective-permute-done | bytes 262176 | tf_op jit(solution)/shard_map/ppermute | solution.py:371
  60.1 3.8 %gate.2 = (bf16[128,4096]{1,0:T(8,128)(2,1)}, bf16[128,4096]{1,0:T(8,128)(2,1)}, bf16[128,4096]{1,0:T(8,128)(2,1)}, bf16[128,4096]{1,0:T(8,128)(2,1)}) custom-call(s32[2]{0:T(128)S(1)} %pad_add_fusion.me, bf16[128,4096]{1,0:T(8,128)(2,1)S(1)} %get-tuple-element.63.query, bf16[128,4096]{1,0:T(8,128)(2,1)S(1)} %get-tuple-element.64.grad, ...), custom_call_target="tpu_custom_call" | custom-call | tf_op jit(solution)/shard_map/gate/pallas_call | solution.py:308
  63.9 3.3 %collective-permute-done.22.got = bf16[1,256,512]{2,1,0:T(8,128)(2,1)S(1)} collective-permute-done((bf16[1,256,512]{2,1,0:T(8,128)(2,1)S(1)}, bf16[1,256,512]{2,1,0:T(8,128)(2,1)S(1)}, u32[]{:S(2)}, u32[]{:S(2)}) %collective-permute-start.22) | collective-permute-done | bytes 262176 | tf_op jit(solution)/shard_map/ppermute | solution.py:337
  67.2 1.1 %turn_grads.1 = f32[512,256]{1,0:T(8,128)} custom-call(f32[1,256,512]{2,1,0:T(8,128)S(1)} %get-tuple-element.104.refs_0_.keep, bf16[1,256,512]{2,1,0:T(8,128)(2,1)S(1)} %collective-permute-done.22.got), custom_call_target="tpu_custom_call" | custom-call | tf_op jit(solution)/shard_map/turn_grads/pallas_call | solution.py:354
  68.3 2.1 %gate.3 = (bf16[128,4096]{1,0:T(8,128)(2,1)}, bf16[128,4096]{1,0:T(8,128)(2,1)}, bf16[128,4096]{1,0:T(8,128)(2,1)}, bf16[128,4096]{1,0:T(8,128)(2,1)}) custom-call(s32[2]{0:T(128)S(1)} %pad_add_fusion.me, bf16[128,4096]{1,0:T(8,128)(2,1)S(1)} %get-tuple-element.63.query, ...), custom_call_target="tpu_custom_call", output_to_operand_aliasing={{0}: (8, {}), {1}: (9, {}), {2}: (10, {}), {3}: (11, {})} | custom-call | tf_op jit(solution)/shard_map/gate/pallas_call | solution.py:308
  (35 shorter events, 2.2 us)
Async XLA Ops:
  0.7 12.3 %copy-start = (bf16[8,256,256]{2,1,0:T(8,128)(2,1)S(1)}, bf16[8,256,256]{2,1,0:T(8,128)(2,1)}, u32[]{:S(2)}) copy-start(bf16[8,256,256]{2,1,0:T(8,128)(2,1)} %constant.12.clone.fwd.refs_9_) | copy-start | bytes 3145732
  0.7 12.3 %copy-start.1 = (f32[512,1024]{1,0:T(8,128)S(1)}, f32[512,1024]{1,0:T(8,128)}, u32[]{:S(2)}) copy-start(f32[512,1024]{1,0:T(8,128)} %filt.3) | copy-start | bytes 6291460
  3.9 5.8 %collective-permute-start = (bf16[2,128,256]{2,1,0:T(8,128)(2,1)S(1)}, bf16[2,128,256]{2,1,0:T(8,128)(2,1)S(1)}, u32[]{:S(2)}, u32[]{:S(2)}) collective-permute-start(bf16[2,128,256]{2,1,0:T(8,128)(2,1)S(1)} %get-tuple-element.67), channel_id=1, source_target_pairs={{0,1},{1,0},{2,3},{3,2},{4,5},{5,4},{6,7},{7,6},{8,9},{9,8},{10,11... | collective-permute-start | bytes 393224 | tf_op jit(solution)/shard_map/ppermute | solution.py:371
  4.4 7.3 %collective-permute-start.1 = (bf16[2,128,256]{2,1,0:T(8,128)(2,1)S(1)}, bf16[2,128,256]{2,1,0:T(8,128)(2,1)S(1)}, u32[]{:S(2)}, u32[]{:S(2)}) collective-permute-start(bf16[2,128,256]{2,1,0:T(8,128)(2,1)S(1)} %get-tuple-element.68), channel_id=1, source_target_pairs={{0,2},{1,3},{2,0},{3,1},{4,6},{5,7},{6,4},{7,5},{8,10},{9,11},{10,... | collective-permute-start | bytes 393224 | tf_op jit(solution)/shard_map/ppermute | solution.py:371
  6.9 8.1 %collective-permute-start.9 = (bf16[2,128,256]{2,1,0:T(8,128)(2,1)S(1)}, bf16[2,128,256]{2,1,0:T(8,128)(2,1)S(1)}, u32[]{:S(2)}, u32[]{:S(2)}) collective-permute-start(bf16[2,128,256]{2,1,0:T(8,128)(2,1)S(1)} %get-tuple-element.86), channel_id=1, source_target_pairs={{0,4},{1,5},{2,6},{3,7},{4,0},{5,1},{6,2},{7,3},{8,12},{9,13},{10,... | collective-permute-start | bytes 393224 | tf_op jit(solution)/shard_map/ppermute | solution.py:371
  8.5 7.8 %collective-permute-start.10 = (bf16[2,128,256]{2,1,0:T(8,128)(2,1)S(1)}, bf16[2,128,256]{2,1,0:T(8,128)(2,1)S(1)}, u32[]{:S(2)}, u32[]{:S(2)}) collective-permute-start(bf16[2,128,256]{2,1,0:T(8,128)(2,1)S(1)} %get-tuple-element.87), channel_id=1, source_target_pairs={{0,6},{1,7},{2,4},{3,5},{4,2},{5,3},{6,0},{7,1},{8,14},{9,15},{10,... | collective-permute-start | bytes 393224 | tf_op jit(solution)/shard_map/ppermute | solution.py:371
  8.5 10.3 %collective-permute-start.11 = (bf16[2,128,256]{2,1,0:T(8,128)(2,1)S(1)}, bf16[2,128,256]{2,1,0:T(8,128)(2,1)S(1)}, u32[]{:S(2)}, u32[]{:S(2)}) collective-permute-start(bf16[2,128,256]{2,1,0:T(8,128)(2,1)S(1)} %get-tuple-element.88), channel_id=1, source_target_pairs={{0,3},{1,2},{2,1},{3,0},{4,7},{5,6},{6,5},{7,4},{8,11},{9,10},{10,... | collective-permute-start | bytes 393224 | tf_op jit(solution)/shard_map/ppermute | solution.py:371
  9.7 11.1 %collective-permute-start.12 = (bf16[2,128,256]{2,1,0:T(8,128)(2,1)S(1)}, bf16[2,128,256]{2,1,0:T(8,128)(2,1)S(1)}, u32[]{:S(2)}, u32[]{:S(2)}) collective-permute-start(bf16[2,128,256]{2,1,0:T(8,128)(2,1)S(1)} %get-tuple-element.89), channel_id=1, source_target_pairs={{0,5},{1,4},{2,7},{3,6},{4,1},{5,0},{6,3},{7,2},{8,13},{9,12},{10,... | collective-permute-start | bytes 393224 | tf_op jit(solution)/shard_map/ppermute | solution.py:371
  11.7 10.2 %collective-permute-start.13 = (bf16[2,128,256]{2,1,0:T(8,128)(2,1)S(1)}, bf16[2,128,256]{2,1,0:T(8,128)(2,1)S(1)}, u32[]{:S(2)}, u32[]{:S(2)}) collective-permute-start(bf16[2,128,256]{2,1,0:T(8,128)(2,1)S(1)} %get-tuple-element.90), channel_id=1, source_target_pairs={{0,7},{1,6},{2,5},{3,4},{4,3},{5,2},{6,1},{7,0},{8,15},{9,14},{10,... | collective-permute-start | bytes 393224 | tf_op jit(solution)/shard_map/ppermute | solution.py:371
  15.0 8.3 %collective-permute-start.2 = (bf16[2,128,256]{2,1,0:T(8,128)(2,1)S(1)}, bf16[2,128,256]{2,1,0:T(8,128)(2,1)S(1)}, u32[]{:S(2)}, u32[]{:S(2)}) collective-permute-start(bf16[2,128,256]{2,1,0:T(8,128)(2,1)S(1)} %get-tuple-element.74), channel_id=1, source_target_pairs={{0,1},{1,0},{2,3},{3,2},{4,5},{5,4},{6,7},{7,6},{8,9},{9,8},{10,11... | collective-permute-start | bytes 393224 | tf_op jit(solution)/shard_map/ppermute | solution.py:371
  16.3 7.7 %collective-permute-start.3 = (bf16[2,128,256]{2,1,0:T(8,128)(2,1)S(1)}, bf16[2,128,256]{2,1,0:T(8,128)(2,1)S(1)}, u32[]{:S(2)}, u32[]{:S(2)}) collective-permute-start(bf16[2,128,256]{2,1,0:T(8,128)(2,1)S(1)} %get-tuple-element.75), channel_id=1, source_target_pairs={{0,2},{1,3},{2,0},{3,1},{4,6},{5,7},{6,4},{7,5},{8,10},{9,11},{10,... | collective-permute-start | bytes 393224 | tf_op jit(solution)/shard_map/ppermute | solution.py:371
  18.8 5.8 %copy-start.2 = (bf16[8,128,256]{2,1,0:T(8,128)(2,1)S(1)}, bf16[8,128,256]{2,1,0:T(8,128)(2,1)}, u32[]{:S(2)}) copy-start(bf16[8,128,256]{2,1,0:T(8,128)(2,1)} %constant.13.clone.refs_10_) | copy-start | bytes 1572868
  18.8 10.6 %collective-permute-start.4 = (bf16[2,128,256]{2,1,0:T(8,128)(2,1)S(1)}, bf16[2,128,256]{2,1,0:T(8,128)(2,1)S(1)}, u32[]{:S(2)}, u32[]{:S(2)}) collective-permute-start(bf16[2,128,256]{2,1,0:T(8,128)(2,1)S(1)} %get-tuple-element.76), channel_id=1, source_target_pairs={{0,4},{1,5},{2,6},{3,7},{4,0},{5,1},{6,2},{7,3},{8,12},{9,13},{10,... | collective-permute-start | bytes 393224 | tf_op jit(solution)/shard_map/ppermute | solution.py:371
  20.8 8.6 %collective-permute-start.5 = (bf16[2,128,256]{2,1,0:T(8,128)(2,1)S(1)}, bf16[2,128,256]{2,1,0:T(8,128)(2,1)S(1)}, u32[]{:S(2)}, u32[]{:S(2)}) collective-permute-start(bf16[2,128,256]{2,1,0:T(8,128)(2,1)S(1)} %get-tuple-element.81), channel_id=1, source_target_pairs={{0,6},{1,7},{2,4},{3,5},{4,2},{5,3},{6,0},{7,1},{8,14},{9,15},{10,... | collective-permute-start | bytes 393224 | tf_op jit(solution)/shard_map/ppermute | solution.py:371
  21.9 8.3 %collective-permute-start.6 = (bf16[2,128,256]{2,1,0:T(8,128)(2,1)S(1)}, bf16[2,128,256]{2,1,0:T(8,128)(2,1)S(1)}, u32[]{:S(2)}, u32[]{:S(2)}) collective-permute-start(bf16[2,128,256]{2,1,0:T(8,128)(2,1)S(1)} %get-tuple-element.82), channel_id=1, source_target_pairs={{0,3},{1,2},{2,1},{3,0},{4,7},{5,6},{6,5},{7,4},{8,11},{9,10},{10,... | collective-permute-start | bytes 393224 | tf_op jit(solution)/shard_map/ppermute | solution.py:371
  23.4 7.4 %collective-permute-start.7 = (bf16[2,128,256]{2,1,0:T(8,128)(2,1)S(1)}, bf16[2,128,256]{2,1,0:T(8,128)(2,1)S(1)}, u32[]{:S(2)}, u32[]{:S(2)}) collective-permute-start(bf16[2,128,256]{2,1,0:T(8,128)(2,1)S(1)} %get-tuple-element.83), channel_id=1, source_target_pairs={{0,5},{1,4},{2,7},{3,6},{4,1},{5,0},{6,3},{7,2},{8,13},{9,12},{10,... | collective-permute-start | bytes 393224 | tf_op jit(solution)/shard_map/ppermute | solution.py:371
  24.0 8.4 %collective-permute-start.8 = (bf16[2,128,256]{2,1,0:T(8,128)(2,1)S(1)}, bf16[2,128,256]{2,1,0:T(8,128)(2,1)S(1)}, u32[]{:S(2)}, u32[]{:S(2)}) collective-permute-start(bf16[2,128,256]{2,1,0:T(8,128)(2,1)S(1)} %get-tuple-element.84), channel_id=1, source_target_pairs={{0,7},{1,6},{2,5},{3,4},{4,3},{5,2},{6,1},{7,0},{8,15},{9,14},{10,... | collective-permute-start | bytes 393224 | tf_op jit(solution)/shard_map/ppermute | solution.py:371
  37.2 23.0 %copy-start.3 = (f32[4096]{0:T(1024)S(1)}, f32[4096]{0:T(1024)}, u32[]{:S(2)}) copy-start(f32[4096]{0:T(1024)} %param.13) | copy-start | bytes 49156
  37.2 14.3 %collective-permute-start.15 = (bf16[2,256,512]{2,1,0:T(8,128)(2,1)S(1)}, bf16[2,256,512]{2,1,0:T(8,128)(2,1)S(1)}, u32[]{:S(2)}, u32[]{:S(2)}) collective-permute-start(bf16[2,256,512]{2,1,0:T(8,128)(2,1)S(1)} %get-tuple-element.103), channel_id=1, source_target_pairs={{0,8},{8,0},{16,24},{24,16},{1,9},{9,1},{17,25},{25,17},{2,10},{10... | collective-permute-start | bytes 1572872 | tf_op jit(solution)/shard_map/ppermute | solution.py:337
  38.4 13.3 %collective-permute-start.17 = (bf16[2,2,128,256]{3,2,1,0:T(8,128)(2,1)S(1)}, bf16[2,2,128,256]{3,2,1,0:T(8,128)(2,1)S(1)}, u32[]{:S(2)}, u32[]{:S(2)}) collective-permute-start(bf16[2,2,128,256]{3,2,1,0:T(8,128)(2,1)S(1)} %get-tuple-element.107), channel_id=1, source_target_pairs={{0,1},{1,0},{2,3},{3,2},{4,5},{5,4},{6,7},{7,6},{8,9},{9,8},{10,11... | collective-permute-start | bytes 786440 | tf_op jit(solution)/shard_map/ppermute | solution.py:371
  38.6 15.5 %collective-permute-start.18 = (bf16[2,2,128,256]{3,2,1,0:T(8,128)(2,1)S(1)}, bf16[2,2,128,256]{3,2,1,0:T(8,128)(2,1)S(1)}, u32[]{:S(2)}, u32[]{:S(2)}) collective-permute-start(bf16[2,2,128,256]{3,2,1,0:T(8,128)(2,1)S(1)} %get-tuple-element.108), channel_id=1, source_target_pairs={{0,2},{1,3},{2,0},{3,1},{4,6},{5,7},{6,4},{7,5},{8,10},{9,11},{10,... | collective-permute-start | bytes 786440 | tf_op jit(solution)/shard_map/ppermute | solution.py:371
  40.1 16.2 %collective-permute-start.19 = (bf16[2,2,128,256]{3,2,1,0:T(8,128)(2,1)S(1)}, bf16[2,2,128,256]{3,2,1,0:T(8,128)(2,1)S(1)}, u32[]{:S(2)}, u32[]{:S(2)}) collective-permute-start(bf16[2,2,128,256]{3,2,1,0:T(8,128)(2,1)S(1)} %get-tuple-element.109), channel_id=1, source_target_pairs={{0,4},{1,5},{2,6},{3,7},{4,0},{5,1},{6,2},{7,3},{8,12},{9,13},{10,... | collective-permute-start | bytes 786440 | tf_op jit(solution)/shard_map/ppermute | solution.py:371
  41.5 15.2 %collective-permute-start.20 = (bf16[2,2,128,256]{3,2,1,0:T(8,128)(2,1)S(1)}, bf16[2,2,128,256]{3,2,1,0:T(8,128)(2,1)S(1)}, u32[]{:S(2)}, u32[]{:S(2)}) collective-permute-start(bf16[2,2,128,256]{3,2,1,0:T(8,128)(2,1)S(1)} %get-tuple-element.110), channel_id=1, source_target_pairs={{0,6},{1,7},{2,4},{3,5},{4,2},{5,3},{6,0},{7,1},{8,14},{9,15},{10,... | collective-permute-start | bytes 786440 | tf_op jit(solution)/shard_map/ppermute | solution.py:371
  51.5 8.6 %collective-permute-start.21 = (bf16[2,2,128,256]{3,2,1,0:T(8,128)(2,1)S(1)}, bf16[2,2,128,256]{3,2,1,0:T(8,128)(2,1)S(1)}, u32[]{:S(2)}, u32[]{:S(2)}) collective-permute-start(bf16[2,2,128,256]{3,2,1,0:T(8,128)(2,1)S(1)} %get-tuple-element.111), channel_id=1, source_target_pairs={{0,3},{1,2},{2,1},{3,0},{4,7},{5,6},{6,5},{7,4},{8,11},{9,10},{10,... | collective-permute-start | bytes 786440 | tf_op jit(solution)/shard_map/ppermute | solution.py:371
  51.7 15.5 %collective-permute-start.22 = (bf16[1,256,512]{2,1,0:T(8,128)(2,1)S(1)}, bf16[1,256,512]{2,1,0:T(8,128)(2,1)S(1)}, u32[]{:S(2)}, u32[]{:S(2)}) collective-permute-start(bf16[1,256,512]{2,1,0:T(8,128)(2,1)S(1)} %get-tuple-element.120), channel_id=1, source_target_pairs={{0,16},{8,24},{16,0},{24,8},{1,17},{9,25},{17,1},{25,9},{2,18},{10... | collective-permute-start | bytes 786440 | tf_op jit(solution)/shard_map/ppermute | solution.py:337
  54.1 14.2 %collective-permute-start.14 = (bf16[2,2,128,256]{3,2,1,0:T(8,128)(2,1)S(1)}, bf16[2,2,128,256]{3,2,1,0:T(8,128)(2,1)S(1)}, u32[]{:S(2)}, u32[]{:S(2)}) collective-permute-start(bf16[2,2,128,256]{3,2,1,0:T(8,128)(2,1)S(1)} %get-tuple-element.101), channel_id=1, source_target_pairs={{0,5},{1,4},{2,7},{3,6},{4,1},{5,0},{6,3},{7,2},{8,13},{9,12},{10,... | collective-permute-start | bytes 786440 | tf_op jit(solution)/shard_map/ppermute | solution.py:371
  56.3 12.0 %collective-permute-start.16 = (bf16[2,2,128,256]{3,2,1,0:T(8,128)(2,1)S(1)}, bf16[2,2,128,256]{3,2,1,0:T(8,128)(2,1)S(1)}, u32[]{:S(2)}, u32[]{:S(2)}) collective-permute-start(bf16[2,2,128,256]{3,2,1,0:T(8,128)(2,1)S(1)} %after.5), channel_id=1, source_target_pairs={{0,7},{1,6},{2,5},{3,4},{4,3},{5,2},{6,1},{7,0},{8,15},{9,14},{10,... | collective-permute-start | bytes 786440 | tf_op jit(solution)/shard_map/ppermute | solution.py:371

commit v13 on v12

--- a/solution.py
+++ b/solution.py
@@ -192,7 +192,6 @@
     groups = lane_groups(width)
     step_rows = m2 // CLASSES
     part_rows = rows // CLASSES
-    chans = slice(half * width, (half + 1) * width)
 
     for a in range(2):
         for g, lanes in enumerate(groups):
@@ -235,9 +234,9 @@
         for c in range(CLASSES):
             part = grad[c, pl.ds(at, per)]
             if j % 2:
-                send[j // 2, c * per : (c + 1) * per, chans] = part.astype(BF16)
+                send[j // 2, c * per : (c + 1) * per] = part.astype(BF16)
             else:
-                keep[j // 2, c * per : (c + 1) * per, chans] = part
+                keep[j // 2, c * per : (c + 1) * per] = part
 
 
 def conv(n, d, half, me, got, filt, fwd, back, before):
@@ -249,7 +248,7 @@
         in_specs=[SMEM] + [VMEM] * (n + 3 + len(before)),
         out_specs=[VMEM] * (n + 2),
         out_shape=[pltpu.VMEM((HALVES, 2, rows, width), BF16)] * n
-        + [pltpu.VMEM((d // 2, length // d, HALVES * width), dtype) for dtype in (F32, BF16)],
+        + [pltpu.VMEM((d // 2, length // d, width), dtype) for dtype in (F32, BF16)],
         scratch_shapes=[
             pltpu.VMEM((2, width // 128, length, 128), F32),
             pltpu.VMEM((2, CLASSES, m2, width), BF16),
@@ -273,7 +272,8 @@
 
 
 def gate_kernel(js, me, query, grad, value, key, gain, *refs):
-    got, outs, (sent, sems, nat) = refs[: len(js)], refs[-7:-3], refs[-3:]
+    got, outs, token, (sent, sems, nat) = refs[: len(js)], refs[-8:-4], refs[-4], refs[-3:]
+    token[...] = jnp.zeros_like(token)
     _, _, rows, width = got[0].shape
     copies = []
     for i, j in enumerate(js):
@@ -308,8 +308,8 @@
     return pl.pallas_call(
         functools.partial(gate_kernel, js),
         in_specs=[SMEM] + [VMEM] * (5 + len(got)) + [HBM] * len(outs),
-        out_specs=[HBM] * 4,
-        out_shape=[jax.ShapeDtypeStruct(query.shape, BF16)] * 4,
+        out_specs=[HBM] * 4 + [VMEM],
+        out_shape=[jax.ShapeDtypeStruct(query.shape, BF16)] * 4 + [pltpu.VMEM((8, 128), F32)],
         scratch_shapes=[
             pltpu.VMEM((4, len(js), rows, HALVES * width), BF16),
             pltpu.SemaphoreType.DMA((4, len(js))),
@@ -321,10 +321,15 @@
     )(me, query, grad, value, key, gain, *got, *outs)
 
 
-def add_kernel(keep, got, new_keep, new_send):
-    for i in range(new_keep.shape[0]):
-        new_keep[i] = keep[2 * i] + got[2 * i].astype(F32)
-        new_send[i] = (keep[2 * i + 1] + got[2 * i + 1].astype(F32)).astype(BF16)
+def add_kernel(*refs):
+    parts, (new_keep, new_send) = refs[:-2], refs[-2:]
+    width = parts[0].shape[2]
+    for h in range(len(parts) // 2):
+        keep, got = parts[2 * h : 2 * h + 2]
+        chans = slice(h * width, (h + 1) * width)
+        for i in range(new_keep.shape[0]):
+            new_keep[i, :, chans] = keep[2 * i] + got[2 * i].astype(F32)
+            new_send[i, :, chans] = (keep[2 * i + 1] + got[2 * i + 1].astype(F32)).astype(BF16)
 
 
 def turn_kernel(keep, got, out, nat):
@@ -337,16 +342,17 @@
     return resident(lax.ppermute(send, "dp", [(i, i ^ bit) for i in range(d)]))
 
 
-def add_grads(keep, got):
-    shape = (keep.shape[0] // 2, *keep.shape[1:])
+def add_grads(*parts):
+    count, per, width = parts[0].shape
+    shape = (count // 2, per, width * len(parts) // 2)
     return pl.pallas_call(
         add_kernel,
-        in_specs=[VMEM] * 2,
+        in_specs=[VMEM] * len(parts),
         out_specs=[VMEM] * 2,
         out_shape=[pltpu.VMEM(shape, F32), pltpu.VMEM(shape, BF16)],
         compiler_params=PARAMS,
         name="add_grads",
-    )(keep, got)
+    )(*parts)
 
 
 def turn_grads(keep, got):
@@ -363,7 +369,7 @@
 
 
 def peers(n):
-    return [0, 1, *range(2, n, 2), *range(3, n, 2)]
+    return [0, n - 2, 1, *range(2, n - 2, 2), *range(3, n, 2)]
 
 
 def exchange(n, js, blocks):
@@ -405,22 +411,23 @@
     second = exchange(n, js[:cut], after([spec], got[1][:cut]))
     spec_other = filter_spectrum(1, filters, fwd, [spec])
     second += exchange(n, js[cut:], after([spec_other], got[1][cut:]))
-    results = conv(n, d, 0, me, first, spec, fwd, back, [])
-    *mixed, keep, send = conv(n, d, 1, me, second, spec_other, fwd, back, results)
+    *mixed, keep, send = conv(n, d, 0, me, first, spec, fwd, back, [])
+    traded = trade(d, 1, send)
+    *mixed, keep_other, send = conv(n, d, 1, me, second, spec_other, fwd, back, mixed)
 
     bits = [1 << b for b in range(d.bit_length() - 1)]
-    traded = trade(d, 1, send)
+    parts_ = keep, traded, keep_other, trade(d, 1, send)
     early = exchange(n, js[:-1], mixed[:-1])
     for bit in bits[1:]:
-        keep, send = add_grads(keep, traded)
-        traded = trade(d, bit, send)
-    grad_filter = turn_grads(keep, traded)
+        keep, send = add_grads(*parts_)
+        parts_ = keep, trade(d, bit, send)
     mixed = early + exchange(n, js[-1:], after([keep], mixed[-1:]))
 
     outs = []
     early = n - 2
     for at in (slice(early), slice(early, n)):
-        outs = gate(peers(n)[at], me, query, grad, value, key, gain, mixed[at], outs)
+        *outs, gated = gate(peers(n)[at], me, query, grad, value, key, gain, mixed[at], outs)
+    grad_filter = turn_grads(*parts_)
     return *(x[None] for x in outs), grad_filter
 
 

time: 70.8 us -> 69.7 us (0.984)
  waiting for transfers between devices: 20 us -> 13.6 us
  starting transfers between devices: 26.2 us -> 30.3 us
  Pallas kernels: 23.5 us -> 24.6 us
    ppermute x2 -> x3, waiting for transfers between devices: 12.6 us -> 3.33 us  [trade(): return resident(lax.ppermute(send, 'dp', [(i, i ^ bit) for i in range(d)]))]
    ppermute x21, waiting for transfers between devices: 7.39 us -> 10.3 us  [exchange(): lax.ppermute(block, 'ctx', [(i, i ^ j) for i in range(n)])]
    ppermute x2 -> x3, starting transfers between devices: 3.65 us -> 5.87 us  [trade(): return resident(lax.ppermute(send, 'dp', [(i, i ^ bit) for i in range(d)]))]
    ppermute x21, starting transfers between devices: 22.5 us -> 24.4 us  [exchange(): lax.ppermute(block, 'ctx', [(i, i ^ j) for i in range(n)])]
    pallas_call x2, Pallas kernels: 5.93 us -> 7.17 us  [gate(): pl.pallas_call(functools.partial(gate_kernel, js), in_specs=[SMEM] + [VME...]
  transfers between devices with their start and end apart: 23 -> 24, of which waited for: 8 -> 8; matrix products, arithmetic and copies ran while one was open for 0% -> 0% of each run, Pallas kernels for 19% -> 27%
where the time goes in v13:
time: 69.7 us; the launch traced here: 69.6 us
  starting transfers between devices  30.3 us (43%)
  Pallas kernels  24.6 us (35%)
  waiting for transfers between devices  13.6 us (20%)
  between operations  0.94 us (1%)
    ppermute x21, starting transfers between devices, exchange(): lax.ppermute(block, 'ctx', [(i, i ^ j) for i in range(n)])  24.4 us
    ppermute x21, waiting for transfers between devices, exchange(): lax.ppermute(block, 'ctx', [(i, i ^ j) for i in range(n)])  10.3 us
    pallas_call x2, Pallas kernels, conv(): pl.pallas_call(functools.partial(conv_kernel, n, d, half), in_specs=[SMEM...  9.56 us
    pallas_call x2, Pallas kernels, gate(): pl.pallas_call(functools.partial(gate_kernel, js), in_specs=[SMEM] + [VME...  7.17 us
    ppermute x3, starting transfers between devices, trade(): return resident(lax.ppermute(send, 'dp', [(i, i ^ bit) for i in range(d)]))  5.87 us
    pallas_call x2, Pallas kernels, filter_spectrum(): pl.pallas_call(functools.partial(filter_kernel, half), in_specs=[VMEM] *...  3.6 us
    ppermute x3, waiting for transfers between devices, trade(): return resident(lax.ppermute(send, 'dp', [(i, i ^ bit) for i in range(d)]))  3.33 us
    pallas_call x1, Pallas kernels, products(): pl.pallas_call(functools.partial(product_kernel, n), in_specs=[SMEM] + [H...  3.14 us
  transfers between devices with their start and end apart: 24, of which 8 were waited for; matrix products, arithmetic and copies ran while one was open for 0% of the time, Pallas kernels for 27%

profile of v13, /device:TPU:0, one launch (start us, length us, event | category | flops | bytes accessed | tf_op | source)
XLA Modules:
  0.0 69.6 jit_solution(2182875206126049060)
XLA Ops:
  0.7 3.1 %products.1 = (bf16[128,4096]{1,0:T(8,128)(2,1)S(1)}, bf16[128,4096]{1,0:T(8,128)(2,1)S(1)}, bf16[128,4096]{1,0:T(8,128)(2,1)S(1)}, bf16[128,4096]{1,0:T(8,128)(...) custom-call(s32[2]{0:T(128)S(1)} %pad_add_fusion.me, ...), custom_call_target="tpu_custom_call" | custom-call | tf_op jit(solution)/shard_map/products/pallas_call | solution.py:126
  3.9 4.0 %collective-permute-start = (bf16[2,128,256]{2,1,0:T(8,128)(2,1)S(1)}, bf16[2,128,256]{2,1,0:T(8,128)(2,1)S(1)}, u32[]{:S(2)}, u32[]{:S(2)}) collective-permute-start(bf16[2,128,256]{2,1,0:T(8,128)(2,1)S(1)} %get-tuple-element.67), channel_id=1, source_target_pairs={{0,6},{1,7},{2,4},{3,5},{4,2},{5,3},{6,0},{7,1},{8,14},{9,15},{10,... | collective-permute-start | bytes 393224 | tf_op jit(solution)/shard_map/ppermute | solution.py:377
  7.8 0.5 collective-permute-start.9
  8.4 0.2 collective-permute-start.10
  8.5 1.4 %collective-permute-start.11 = (bf16[2,128,256]{2,1,0:T(8,128)(2,1)S(1)}, bf16[2,128,256]{2,1,0:T(8,128)(2,1)S(1)}, u32[]{:S(2)}, u32[]{:S(2)}) collective-permute-start(bf16[2,128,256]{2,1,0:T(8,128)(2,1)S(1)} %get-tuple-element.88), channel_id=1, source_target_pairs={{0,3},{1,2},{2,1},{3,0},{4,7},{5,6},{6,5},{7,4},{8,11},{9,10},{10,... | collective-permute-start | bytes 393224 | tf_op jit(solution)/shard_map/ppermute | solution.py:377
  9.9 1.8 %collective-permute-done.refs_0_.refs_1_ = bf16[2,128,256]{2,1,0:T(8,128)(2,1)S(1)} collective-permute-done((bf16[2,128,256]{2,1,0:T(8,128)(2,1)S(1)}, bf16[2,128,256]{2,1,0:T(8,128)(2,1)S(1)}, u32[]{:S(2)}, u32[]{:S(2)}) %collective-permute-start) | collective-permute-done | bytes 131104 | tf_op jit(solution)/shard_map/ppermute | solution.py:377
  11.7 3.6 %collective-permute-start.13 = (bf16[2,128,256]{2,1,0:T(8,128)(2,1)S(1)}, bf16[2,128,256]{2,1,0:T(8,128)(2,1)S(1)}, u32[]{:S(2)}, u32[]{:S(2)}) collective-permute-start(bf16[2,128,256]{2,1,0:T(8,128)(2,1)S(1)} %get-tuple-element.90), channel_id=1, source_target_pairs={{0,7},{1,6},{2,5},{3,4},{4,3},{5,2},{6,1},{7,0},{8,15},{9,14},{10,... | collective-permute-start | bytes 393224 | tf_op jit(solution)/shard_map/ppermute | solution.py:377
  15.3 1.9 %filter_spectrum.2.refs_0_.refs_8_ = f32[8,256,256]{2,1,0:T(8,128)S(1)} custom-call(f32[512,1024]{1,0:T(8,128)S(1)} %copy-done.1, bf16[8,256,256]{2,1,0:T(8,128)(2,1)S(1)} %copy-done, bf16[2,128,256]{2,1,0:T(8,128)(2,1)S(1)} %collective-permute-done.refs_0_.refs_1_, bf16[2,128,256]{2,1,0:T(8,128)(2,1)S(1)} %collective-permute-done.1.refs_1_.refs_2_), custom_call_target="tpu_custom_call" | custom-call | tf_op jit(solution)/shard_map/filter_spectrum/pallas_call | solution.py:171
  17.3 1.0 %collective-permute-start.2 = (bf16[2,128,256]{2,1,0:T(8,128)(2,1)S(1)}, bf16[2,128,256]{2,1,0:T(8,128)(2,1)S(1)}, u32[]{:S(2)}, u32[]{:S(2)}) collective-permute-start(bf16[2,128,256]{2,1,0:T(8,128)(2,1)S(1)} %get-tuple-element.74), channel_id=1, source_target_pairs={{0,6},{1,7},{2,4},{3,5},{4,2},{5,3},{6,0},{7,1},{8,14},{9,15},{10,... | collective-permute-start | bytes 393224 | tf_op jit(solution)/shard_map/ppermute | solution.py:377
  18.3 1.7 %filter_spectrum.3.refs_0_.refs_8_ = f32[8,256,256]{2,1,0:T(8,128)S(1)} custom-call(f32[512,1024]{1,0:T(8,128)S(1)} %copy-done.1, bf16[8,256,256]{2,1,0:T(8,128)(2,1)S(1)} %copy-done, f32[8,256,256]{2,1,0:T(8,128)S(1)} %filter_spectrum.2.refs_0_.refs_8_), custom_call_target="tpu_custom_call" | custom-call | tf_op jit(solution)/shard_map/filter_spectrum/pallas_call | solution.py:171
  20.1 2.1 %collective-permute-start.4 = (bf16[2,128,256]{2,1,0:T(8,128)(2,1)S(1)}, bf16[2,128,256]{2,1,0:T(8,128)(2,1)S(1)}, u32[]{:S(2)}, u32[]{:S(2)}) collective-permute-start(bf16[2,128,256]{2,1,0:T(8,128)(2,1)S(1)} %get-tuple-element.76), channel_id=1, source_target_pairs={{0,2},{1,3},{2,0},{3,1},{4,6},{5,7},{6,4},{7,5},{8,10},{9,11},{10,... | collective-permute-start | bytes 393224 | tf_op jit(solution)/shard_map/ppermute | solution.py:377
  22.1 0.5 collective-permute-start.5
  22.7 2.6 %collective-permute-start.6 = (bf16[2,128,256]{2,1,0:T(8,128)(2,1)S(1)}, bf16[2,128,256]{2,1,0:T(8,128)(2,1)S(1)}, u32[]{:S(2)}, u32[]{:S(2)}) collective-permute-start(bf16[2,128,256]{2,1,0:T(8,128)(2,1)S(1)} %get-tuple-element.82), channel_id=1, source_target_pairs={{0,3},{1,2},{2,1},{3,0},{4,7},{5,6},{6,5},{7,4},{8,11},{9,10},{10,... | collective-permute-start | bytes 393224 | tf_op jit(solution)/shard_map/ppermute | solution.py:377
  25.2 2.0 %collective-permute-start.7 = (bf16[2,128,256]{2,1,0:T(8,128)(2,1)S(1)}, bf16[2,128,256]{2,1,0:T(8,128)(2,1)S(1)}, u32[]{:S(2)}, u32[]{:S(2)}) collective-permute-start(bf16[2,128,256]{2,1,0:T(8,128)(2,1)S(1)} %get-tuple-element.83), channel_id=1, source_target_pairs={{0,5},{1,4},{2,7},{3,6},{4,1},{5,0},{6,3},{7,2},{8,13},{9,12},{10,... | collective-permute-start | bytes 393224 | tf_op jit(solution)/shard_map/ppermute | solution.py:377
  27.4 4.8 %conv.2 = (bf16[2,2,128,256]{3,2,1,0:T(8,128)(2,1)S(1)}, bf16[2,2,128,256]{3,2,1,0:T(8,128)(2,1)S(1)}, bf16[2,2,128,256]{3,2,1,0:T(8,128)(2,1)S(1)}, bf16[2,2,12...) custom-call(s32[2]{0:T(128)S(1)} %pad_add_fusion.me, ...), custom_call_target="tpu_custom_call" | custom-call | tf_op jit(solution)/shard_map/conv/pallas_call | solution.py:246
  32.2 1.6 %collective-permute-start.15 = (bf16[2,256,256]{2,1,0:T(8,128)(2,1)S(1)}, bf16[2,256,256]{2,1,0:T(8,128)(2,1)S(1)}, u32[]{:S(2)}, u32[]{:S(2)}) collective-permute-start(bf16[2,256,256]{2,1,0:T(8,128)(2,1)S(1)} %get-tuple-element.101), channel_id=1, source_target_pairs={{0,8},{8,0},{16,24},{24,16},{1,9},{9,1},{17,25},{25,17},{2,10},{10... | collective-permute-start | bytes 786440 | tf_op jit(solution)/shard_map/ppermute | solution.py:342
  34.0 4.8 %conv.3 = (bf16[2,2,128,256]{3,2,1,0:T(8,128)(2,1)S(1)}, bf16[2,2,128,256]{3,2,1,0:T(8,128)(2,1)S(1)}, bf16[2,2,128,256]{3,2,1,0:T(8,128)(2,1)S(1)}, bf16[2,2,12...) custom-call(s32[2]{0:T(128)S(1)} %pad_add_fusion.me, ...), custom_call_target="tpu_custom_call", output_to_operand_aliasing={{0}: (12, {}), {1}: (13, {}), {2}: (14, {}), {3}: (15, {}),... | custom-call | tf_op jit(solution)/shard_map/conv/pallas_call | solution.py:246
  38.8 1.6 %collective-permute-start.16 = (bf16[2,256,256]{2,1,0:T(8,128)(2,1)S(1)}, bf16[2,256,256]{2,1,0:T(8,128)(2,1)S(1)}, u32[]{:S(2)}, u32[]{:S(2)}) collective-permute-start(bf16[2,256,256]{2,1,0:T(8,128)(2,1)S(1)} %get-tuple-element.103), channel_id=1, source_target_pairs={{0,8},{8,0},{16,24},{24,16},{1,9},{9,1},{17,25},{25,17},{2,10},{10... | collective-permute-start | bytes 786440 | tf_op jit(solution)/shard_map/ppermute | solution.py:342
  40.5 1.6 %collective-permute-start.18 = (bf16[2,2,128,256]{3,2,1,0:T(8,128)(2,1)S(1)}, bf16[2,2,128,256]{3,2,1,0:T(8,128)(2,1)S(1)}, u32[]{:S(2)}, u32[]{:S(2)}) collective-permute-start(bf16[2,2,128,256]{3,2,1,0:T(8,128)(2,1)S(1)} %get-tuple-element.107), channel_id=1, source_target_pairs={{0,6},{1,7},{2,4},{3,5},{4,2},{5,3},{6,0},{7,1},{8,14},{9,15},{10,... | collective-permute-start | bytes 786440 | tf_op jit(solution)/shard_map/ppermute | solution.py:377
  42.1 0.7 collective-permute-start.20
  42.8 1.2 %collective-permute-start.21 = (bf16[2,2,128,256]{3,2,1,0:T(8,128)(2,1)S(1)}, bf16[2,2,128,256]{3,2,1,0:T(8,128)(2,1)S(1)}, u32[]{:S(2)}, u32[]{:S(2)}) collective-permute-start(bf16[2,2,128,256]{3,2,1,0:T(8,128)(2,1)S(1)} %get-tuple-element.110), channel_id=1, source_target_pairs={{0,4},{1,5},{2,6},{3,7},{4,0},{5,1},{6,2},{7,3},{8,12},{9,13},{10,... | collective-permute-start | bytes 786440 | tf_op jit(solution)/shard_map/ppermute | solution.py:377
  44.0 3.2 %collective-permute-done.16.refs_3_ = bf16[2,256,256]{2,1,0:T(8,128)(2,1)S(1)} collective-permute-done((bf16[2,256,256]{2,1,0:T(8,128)(2,1)S(1)}, bf16[2,256,256]{2,1,0:T(8,128)(2,1)S(1)}, u32[]{:S(2)}, u32[]{:S(2)}) %collective-permute-start.16) | collective-permute-done | bytes 262176 | tf_op jit(solution)/shard_map/ppermute | solution.py:342
  47.2 1.8 %collective-permute-start.22 = (bf16[2,2,128,256]{3,2,1,0:T(8,128)(2,1)S(1)}, bf16[2,2,128,256]{3,2,1,0:T(8,128)(2,1)S(1)}, u32[]{:S(2)}, u32[]{:S(2)}) collective-permute-start(bf16[2,2,128,256]{3,2,1,0:T(8,128)(2,1)S(1)} %get-tuple-element.111), channel_id=1, source_target_pairs={{0,3},{1,2},{2,1},{3,0},{4,7},{5,6},{6,5},{7,4},{8,11},{9,10},{10,... | collective-permute-start | bytes 786440 | tf_op jit(solution)/shard_map/ppermute | solution.py:377
  49.0 1.6 %collective-permute-done.18.refs_1_ = bf16[2,2,128,256]{3,2,1,0:T(8,128)(2,1)S(1)} collective-permute-done((bf16[2,2,128,256]{3,2,1,0:T(8,128)(2,1)S(1)}, bf16[2,2,128,256]{3,2,1,0:T(8,128)(2,1)S(1)}, u32[]{:S(2)}, u32[]{:S(2)}) %collective-permute-start.18) | collective-permute-done | bytes 262176 | tf_op jit(solution)/shard_map/ppermute | solution.py:377
  50.6 2.6 %collective-permute-start.23 = (bf16[1,256,512]{2,1,0:T(8,128)(2,1)S(1)}, bf16[1,256,512]{2,1,0:T(8,128)(2,1)S(1)}, u32[]{:S(2)}, u32[]{:S(2)}) collective-permute-start(bf16[1,256,512]{2,1,0:T(8,128)(2,1)S(1)} %get-tuple-element.120), channel_id=1, source_target_pairs={{0,16},{8,24},{16,0},{24,8},{1,17},{9,25},{17,1},{25,9},{2,18},{10... | collective-permute-start | bytes 786440 | tf_op jit(solution)/shard_map/ppermute | solution.py:342
  53.2 2.2 %collective-permute-done.20.refs_3_ = bf16[2,2,128,256]{3,2,1,0:T(8,128)(2,1)S(1)} collective-permute-done((bf16[2,2,128,256]{3,2,1,0:T(8,128)(2,1)S(1)}, bf16[2,2,128,256]{3,2,1,0:T(8,128)(2,1)S(1)}, u32[]{:S(2)}, u32[]{:S(2)}) %collective-permute-start.20) | collective-permute-done | bytes 262176 | tf_op jit(solution)/shard_map/ppermute | solution.py:377
  55.4 1.1 %collective-permute-start.17 = (bf16[2,2,128,256]{3,2,1,0:T(8,128)(2,1)S(1)}, bf16[2,2,128,256]{3,2,1,0:T(8,128)(2,1)S(1)}, u32[]{:S(2)}, u32[]{:S(2)}) collective-permute-start(bf16[2,2,128,256]{3,2,1,0:T(8,128)(2,1)S(1)} %after.5), channel_id=1, source_target_pairs={{0,7},{1,6},{2,5},{3,4},{4,3},{5,2},{6,1},{7,0},{8,15},{9,14},{10,... | collective-permute-start | bytes 786440 | tf_op jit(solution)/shard_map/ppermute | solution.py:377
  56.6 3.4 %collective-permute-done.22.refs_5_ = bf16[2,2,128,256]{3,2,1,0:T(8,128)(2,1)S(1)} collective-permute-done((bf16[2,2,128,256]{3,2,1,0:T(8,128)(2,1)S(1)}, bf16[2,2,128,256]{3,2,1,0:T(8,128)(2,1)S(1)}, u32[]{:S(2)}, u32[]{:S(2)}) %collective-permute-start.22) | collective-permute-done | bytes 262176 | tf_op jit(solution)/shard_map/ppermute | solution.py:377
  60.0 4.4 %gate.2 = (bf16[128,4096]{1,0:T(8,128)(2,1)}, bf16[128,4096]{1,0:T(8,128)(2,1)}, bf16[128,4096]{1,0:T(8,128)(2,1)}, bf16[128,4096]{1,0:T(8,128)(2,1)}, f32[8,128]{1,0:T(8,128)}) custom-call(s32[2]{0:T(128)S(1)} %pad_add_fusion.me, bf16[128,4096]{1,0:T(8,128)(2,1)S(1)} %get-tuple-element.63.query, bf16[128,4096]{1,0:T(8,128)(2,1)S(1)} %get-tuple-element.64.grad, ...), custom_call_target="tpu_custom_call" | custom-call | tf_op jit(solution)/shard_map/gate/pallas_call | solution.py:308
  64.6 1.1 %turn_grads.1 = f32[512,256]{1,0:T(8,128)} custom-call(f32[1,256,512]{2,1,0:T(8,128)S(1)} %get-tuple-element.104.refs_0_.keep, bf16[1,256,512]{2,1,0:T(8,128)(2,1)S(1)} %collective-permute-done.23.got), custom_call_target="tpu_custom_call" | custom-call | tf_op jit(solution)/shard_map/turn_grads/pallas_call | solution.py:360
  65.6 1.0 %collective-permute-done.14.refs_0_ = bf16[2,2,128,256]{3,2,1,0:T(8,128)(2,1)S(1)} collective-permute-done((bf16[2,2,128,256]{3,2,1,0:T(8,128)(2,1)S(1)}, bf16[2,2,128,256]{3,2,1,0:T(8,128)(2,1)S(1)}, u32[]{:S(2)}, u32[]{:S(2)}) %collective-permute-start.14) | collective-permute-done | bytes 262176 | tf_op jit(solution)/shard_map/ppermute | solution.py:377
  66.7 2.8 %gate.3 = (bf16[128,4096]{1,0:T(8,128)(2,1)}, bf16[128,4096]{1,0:T(8,128)(2,1)}, bf16[128,4096]{1,0:T(8,128)(2,1)}, bf16[128,4096]{1,0:T(8,128)(2,1)}, f32[8,128]{1,0:T(8,128)}) custom-call(s32[2]{0:T(128)S(1)} %pad_add_fusion.me, ...), custom_call_target="tpu_custom_call", output_to_operand_aliasing={{0}: (8, {}), {1}: (9, {}), {2}: (10, {}), {3}: (11, {})} | custom-call | tf_op jit(solution)/shard_map/gate/pallas_call | solution.py:308
  (37 shorter events, 0.7 us)
Async XLA Ops:
  0.7 14.6 %copy-start = (bf16[8,256,256]{2,1,0:T(8,128)(2,1)S(1)}, bf16[8,256,256]{2,1,0:T(8,128)(2,1)}, u32[]{:S(2)}) copy-start(bf16[8,256,256]{2,1,0:T(8,128)(2,1)} %constant.12.clone.fwd.refs_9_) | copy-start | bytes 3145732
  0.7 14.6 %copy-start.1 = (f32[512,1024]{1,0:T(8,128)S(1)}, f32[512,1024]{1,0:T(8,128)}, u32[]{:S(2)}) copy-start(f32[512,1024]{1,0:T(8,128)} %filt.3) | copy-start | bytes 6291460
  3.9 7.9 %collective-permute-start = (bf16[2,128,256]{2,1,0:T(8,128)(2,1)S(1)}, bf16[2,128,256]{2,1,0:T(8,128)(2,1)S(1)}, u32[]{:S(2)}, u32[]{:S(2)}) collective-permute-start(bf16[2,128,256]{2,1,0:T(8,128)(2,1)S(1)} %get-tuple-element.67), channel_id=1, source_target_pairs={{0,6},{1,7},{2,4},{3,5},{4,2},{5,3},{6,0},{7,1},{8,14},{9,15},{10,... | collective-permute-start | bytes 393224 | tf_op jit(solution)/shard_map/ppermute | solution.py:377
  7.8 3.9 %collective-permute-start.1 = (bf16[2,128,256]{2,1,0:T(8,128)(2,1)S(1)}, bf16[2,128,256]{2,1,0:T(8,128)(2,1)S(1)}, u32[]{:S(2)}, u32[]{:S(2)}) collective-permute-start(bf16[2,128,256]{2,1,0:T(8,128)(2,1)S(1)} %get-tuple-element.68), channel_id=1, source_target_pairs={{0,1},{1,0},{2,3},{3,2},{4,5},{5,4},{6,7},{7,6},{8,9},{9,8},{10,11... | collective-permute-start | bytes 393224 | tf_op jit(solution)/shard_map/ppermute | solution.py:377
  7.8 9.4 %collective-permute-start.9 = (bf16[2,128,256]{2,1,0:T(8,128)(2,1)S(1)}, bf16[2,128,256]{2,1,0:T(8,128)(2,1)S(1)}, u32[]{:S(2)}, u32[]{:S(2)}) collective-permute-start(bf16[2,128,256]{2,1,0:T(8,128)(2,1)S(1)} %get-tuple-element.86), channel_id=1, source_target_pairs={{0,2},{1,3},{2,0},{3,1},{4,6},{5,7},{6,4},{7,5},{8,10},{9,11},{10,... | collective-permute-start | bytes 393224 | tf_op jit(solution)/shard_map/ppermute | solution.py:377
  8.4 10.0 %collective-permute-start.10 = (bf16[2,128,256]{2,1,0:T(8,128)(2,1)S(1)}, bf16[2,128,256]{2,1,0:T(8,128)(2,1)S(1)}, u32[]{:S(2)}, u32[]{:S(2)}) collective-permute-start(bf16[2,128,256]{2,1,0:T(8,128)(2,1)S(1)} %get-tuple-element.87), channel_id=1, source_target_pairs={{0,4},{1,5},{2,6},{3,7},{4,0},{5,1},{6,2},{7,3},{8,12},{9,13},{10,... | collective-permute-start | bytes 393224 | tf_op jit(solution)/shard_map/ppermute | solution.py:377
  8.5 11.5 %collective-permute-start.11 = (bf16[2,128,256]{2,1,0:T(8,128)(2,1)S(1)}, bf16[2,128,256]{2,1,0:T(8,128)(2,1)S(1)}, u32[]{:S(2)}, u32[]{:S(2)}) collective-permute-start(bf16[2,128,256]{2,1,0:T(8,128)(2,1)S(1)} %get-tuple-element.88), channel_id=1, source_target_pairs={{0,3},{1,2},{2,1},{3,0},{4,7},{5,6},{6,5},{7,4},{8,11},{9,10},{10,... | collective-permute-start | bytes 393224 | tf_op jit(solution)/shard_map/ppermute | solution.py:377
  11.7 10.4 %collective-permute-start.12 = (bf16[2,128,256]{2,1,0:T(8,128)(2,1)S(1)}, bf16[2,128,256]{2,1,0:T(8,128)(2,1)S(1)}, u32[]{:S(2)}, u32[]{:S(2)}) collective-permute-start(bf16[2,128,256]{2,1,0:T(8,128)(2,1)S(1)} %get-tuple-element.89), channel_id=1, source_target_pairs={{0,5},{1,4},{2,7},{3,6},{4,1},{5,0},{6,3},{7,2},{8,13},{9,12},{10,... | collective-permute-start | bytes 393224 | tf_op jit(solution)/shard_map/ppermute | solution.py:377
  11.7 10.9 %collective-permute-start.13 = (bf16[2,128,256]{2,1,0:T(8,128)(2,1)S(1)}, bf16[2,128,256]{2,1,0:T(8,128)(2,1)S(1)}, u32[]{:S(2)}, u32[]{:S(2)}) collective-permute-start(bf16[2,128,256]{2,1,0:T(8,128)(2,1)S(1)} %get-tuple-element.90), channel_id=1, source_target_pairs={{0,7},{1,6},{2,5},{3,4},{4,3},{5,2},{6,1},{7,0},{8,15},{9,14},{10,... | collective-permute-start | bytes 393224 | tf_op jit(solution)/shard_map/ppermute | solution.py:377
  17.3 8.0 %collective-permute-start.2 = (bf16[2,128,256]{2,1,0:T(8,128)(2,1)S(1)}, bf16[2,128,256]{2,1,0:T(8,128)(2,1)S(1)}, u32[]{:S(2)}, u32[]{:S(2)}) collective-permute-start(bf16[2,128,256]{2,1,0:T(8,128)(2,1)S(1)} %get-tuple-element.74), channel_id=1, source_target_pairs={{0,6},{1,7},{2,4},{3,5},{4,2},{5,3},{6,0},{7,1},{8,14},{9,15},{10,... | collective-permute-start | bytes 393224 | tf_op jit(solution)/shard_map/ppermute | solution.py:377
  18.3 8.9 %collective-permute-start.3 = (bf16[2,128,256]{2,1,0:T(8,128)(2,1)S(1)}, bf16[2,128,256]{2,1,0:T(8,128)(2,1)S(1)}, u32[]{:S(2)}, u32[]{:S(2)}) collective-permute-start(bf16[2,128,256]{2,1,0:T(8,128)(2,1)S(1)} %get-tuple-element.75), channel_id=1, source_target_pairs={{0,1},{1,0},{2,3},{3,2},{4,5},{5,4},{6,7},{7,6},{8,9},{9,8},{10,11... | collective-permute-start | bytes 393224 | tf_op jit(solution)/shard_map/ppermute | solution.py:377
  20.0 7.4 %copy-start.2 = (bf16[8,128,256]{2,1,0:T(8,128)(2,1)S(1)}, bf16[8,128,256]{2,1,0:T(8,128)(2,1)}, u32[]{:S(2)}) copy-start(bf16[8,128,256]{2,1,0:T(8,128)(2,1)} %constant.13.clone.refs_10_) | copy-start | bytes 1572868
  20.1 12.1 %collective-permute-start.4 = (bf16[2,128,256]{2,1,0:T(8,128)(2,1)S(1)}, bf16[2,128,256]{2,1,0:T(8,128)(2,1)S(1)}, u32[]{:S(2)}, u32[]{:S(2)}) collective-permute-start(bf16[2,128,256]{2,1,0:T(8,128)(2,1)S(1)} %get-tuple-element.76), channel_id=1, source_target_pairs={{0,2},{1,3},{2,0},{3,1},{4,6},{5,7},{6,4},{7,5},{8,10},{9,11},{10,... | collective-permute-start | bytes 393224 | tf_op jit(solution)/shard_map/ppermute | solution.py:377
  22.1 11.7 %collective-permute-start.5 = (bf16[2,128,256]{2,1,0:T(8,128)(2,1)S(1)}, bf16[2,128,256]{2,1,0:T(8,128)(2,1)S(1)}, u32[]{:S(2)}, u32[]{:S(2)}) collective-permute-start(bf16[2,128,256]{2,1,0:T(8,128)(2,1)S(1)} %get-tuple-element.81), channel_id=1, source_target_pairs={{0,4},{1,5},{2,6},{3,7},{4,0},{5,1},{6,2},{7,3},{8,12},{9,13},{10,... | collective-permute-start | bytes 393224 | tf_op jit(solution)/shard_map/ppermute | solution.py:377
  22.7 11.2 %collective-permute-start.6 = (bf16[2,128,256]{2,1,0:T(8,128)(2,1)S(1)}, bf16[2,128,256]{2,1,0:T(8,128)(2,1)S(1)}, u32[]{:S(2)}, u32[]{:S(2)}) collective-permute-start(bf16[2,128,256]{2,1,0:T(8,128)(2,1)S(1)} %get-tuple-element.82), channel_id=1, source_target_pairs={{0,3},{1,2},{2,1},{3,0},{4,7},{5,6},{6,5},{7,4},{8,11},{9,10},{10,... | collective-permute-start | bytes 393224 | tf_op jit(solution)/shard_map/ppermute | solution.py:377
  25.2 8.6 %collective-permute-start.7 = (bf16[2,128,256]{2,1,0:T(8,128)(2,1)S(1)}, bf16[2,128,256]{2,1,0:T(8,128)(2,1)S(1)}, u32[]{:S(2)}, u32[]{:S(2)}) collective-permute-start(bf16[2,128,256]{2,1,0:T(8,128)(2,1)S(1)} %get-tuple-element.83), channel_id=1, source_target_pairs={{0,5},{1,4},{2,7},{3,6},{4,1},{5,0},{6,3},{7,2},{8,13},{9,12},{10,... | collective-permute-start | bytes 393224 | tf_op jit(solution)/shard_map/ppermute | solution.py:377
  27.3 6.8 %collective-permute-start.8 = (bf16[2,128,256]{2,1,0:T(8,128)(2,1)S(1)}, bf16[2,128,256]{2,1,0:T(8,128)(2,1)S(1)}, u32[]{:S(2)}, u32[]{:S(2)}) collective-permute-start(bf16[2,128,256]{2,1,0:T(8,128)(2,1)S(1)} %get-tuple-element.84), channel_id=1, source_target_pairs={{0,7},{1,6},{2,5},{3,4},{4,3},{5,2},{6,1},{7,0},{8,15},{9,14},{10,... | collective-permute-start | bytes 393224 | tf_op jit(solution)/shard_map/ppermute | solution.py:377
  32.2 10.6 %collective-permute-start.15 = (bf16[2,256,256]{2,1,0:T(8,128)(2,1)S(1)}, bf16[2,256,256]{2,1,0:T(8,128)(2,1)S(1)}, u32[]{:S(2)}, u32[]{:S(2)}) collective-permute-start(bf16[2,256,256]{2,1,0:T(8,128)(2,1)S(1)} %get-tuple-element.101), channel_id=1, source_target_pairs={{0,8},{8,0},{16,24},{24,16},{1,9},{9,1},{17,25},{25,17},{2,10},{10... | collective-permute-start | bytes 786440 | tf_op jit(solution)/shard_map/ppermute | solution.py:342
  38.8 21.2 %copy-start.3 = (f32[4096]{0:T(1024)S(1)}, f32[4096]{0:T(1024)}, u32[]{:S(2)}) copy-start(f32[4096]{0:T(1024)} %param.13) | copy-start | bytes 49156
  38.8 8.3 %collective-permute-start.16 = (bf16[2,256,256]{2,1,0:T(8,128)(2,1)S(1)}, bf16[2,256,256]{2,1,0:T(8,128)(2,1)S(1)}, u32[]{:S(2)}, u32[]{:S(2)}) collective-permute-start(bf16[2,256,256]{2,1,0:T(8,128)(2,1)S(1)} %get-tuple-element.103), channel_id=1, source_target_pairs={{0,8},{8,0},{16,24},{24,16},{1,9},{9,1},{17,25},{25,17},{2,10},{10... | collective-permute-start | bytes 786440 | tf_op jit(solution)/shard_map/ppermute | solution.py:342
  40.5 10.1 %collective-permute-start.18 = (bf16[2,2,128,256]{3,2,1,0:T(8,128)(2,1)S(1)}, bf16[2,2,128,256]{3,2,1,0:T(8,128)(2,1)S(1)}, u32[]{:S(2)}, u32[]{:S(2)}) collective-permute-start(bf16[2,2,128,256]{3,2,1,0:T(8,128)(2,1)S(1)} %get-tuple-element.107), channel_id=1, source_target_pairs={{0,6},{1,7},{2,4},{3,5},{4,2},{5,3},{6,0},{7,1},{8,14},{9,15},{10,... | collective-permute-start | bytes 786440 | tf_op jit(solution)/shard_map/ppermute | solution.py:377
  42.1 11.1 %collective-permute-start.19 = (bf16[2,2,128,256]{3,2,1,0:T(8,128)(2,1)S(1)}, bf16[2,2,128,256]{3,2,1,0:T(8,128)(2,1)S(1)}, u32[]{:S(2)}, u32[]{:S(2)}) collective-permute-start(bf16[2,2,128,256]{3,2,1,0:T(8,128)(2,1)S(1)} %get-tuple-element.108), channel_id=1, source_target_pairs={{0,1},{1,0},{2,3},{3,2},{4,5},{5,4},{6,7},{7,6},{8,9},{9,8},{10,11... | collective-permute-start | bytes 786440 | tf_op jit(solution)/shard_map/ppermute | solution.py:377
  42.1 13.4 %collective-permute-start.20 = (bf16[2,2,128,256]{3,2,1,0:T(8,128)(2,1)S(1)}, bf16[2,2,128,256]{3,2,1,0:T(8,128)(2,1)S(1)}, u32[]{:S(2)}, u32[]{:S(2)}) collective-permute-start(bf16[2,2,128,256]{3,2,1,0:T(8,128)(2,1)S(1)} %get-tuple-element.109), channel_id=1, source_target_pairs={{0,2},{1,3},{2,0},{3,1},{4,6},{5,7},{6,4},{7,5},{8,10},{9,11},{10,... | collective-permute-start | bytes 786440 | tf_op jit(solution)/shard_map/ppermute | solution.py:377
  42.8 13.8 %collective-permute-start.21 = (bf16[2,2,128,256]{3,2,1,0:T(8,128)(2,1)S(1)}, bf16[2,2,128,256]{3,2,1,0:T(8,128)(2,1)S(1)}, u32[]{:S(2)}, u32[]{:S(2)}) collective-permute-start(bf16[2,2,128,256]{3,2,1,0:T(8,128)(2,1)S(1)} %get-tuple-element.110), channel_id=1, source_target_pairs={{0,4},{1,5},{2,6},{3,7},{4,0},{5,1},{6,2},{7,3},{8,12},{9,13},{10,... | collective-permute-start | bytes 786440 | tf_op jit(solution)/shard_map/ppermute | solution.py:377
  47.2 12.8 %collective-permute-start.22 = (bf16[2,2,128,256]{3,2,1,0:T(8,128)(2,1)S(1)}, bf16[2,2,128,256]{3,2,1,0:T(8,128)(2,1)S(1)}, u32[]{:S(2)}, u32[]{:S(2)}) collective-permute-start(bf16[2,2,128,256]{3,2,1,0:T(8,128)(2,1)S(1)} %get-tuple-element.111), channel_id=1, source_target_pairs={{0,3},{1,2},{2,1},{3,0},{4,7},{5,6},{6,5},{7,4},{8,11},{9,10},{10,... | collective-permute-start | bytes 786440 | tf_op jit(solution)/shard_map/ppermute | solution.py:377
  50.6 13.9 %collective-permute-start.23 = (bf16[1,256,512]{2,1,0:T(8,128)(2,1)S(1)}, bf16[1,256,512]{2,1,0:T(8,128)(2,1)S(1)}, u32[]{:S(2)}, u32[]{:S(2)}) collective-permute-start(bf16[1,256,512]{2,1,0:T(8,128)(2,1)S(1)} %get-tuple-element.120), channel_id=1, source_target_pairs={{0,16},{8,24},{16,0},{24,8},{1,17},{9,25},{17,1},{25,9},{2,18},{10... | collective-permute-start | bytes 786440 | tf_op jit(solution)/shard_map/ppermute | solution.py:342
  53.2 13.4 %collective-permute-start.14 = (bf16[2,2,128,256]{3,2,1,0:T(8,128)(2,1)S(1)}, bf16[2,2,128,256]{3,2,1,0:T(8,128)(2,1)S(1)}, u32[]{:S(2)}, u32[]{:S(2)}) collective-permute-start(bf16[2,2,128,256]{3,2,1,0:T(8,128)(2,1)S(1)} %get-tuple-element.99), channel_id=1, source_target_pairs={{0,5},{1,4},{2,7},{3,6},{4,1},{5,0},{6,3},{7,2},{8,13},{9,12},{10,... | collective-permute-start | bytes 786440 | tf_op jit(solution)/shard_map/ppermute | solution.py:377
  55.4 11.2 %collective-permute-start.17 = (bf16[2,2,128,256]{3,2,1,0:T(8,128)(2,1)S(1)}, bf16[2,2,128,256]{3,2,1,0:T(8,128)(2,1)S(1)}, u32[]{:S(2)}, u32[]{:S(2)}) collective-permute-start(bf16[2,2,128,256]{3,2,1,0:T(8,128)(2,1)S(1)} %after.5), channel_id=1, source_target_pairs={{0,7},{1,6},{2,5},{3,4},{4,3},{5,2},{6,1},{7,0},{8,15},{9,14},{10,... | collective-permute-start | bytes 786440 | tf_op jit(solution)/shard_map/ppermute | solution.py:377

commit v14 on v13

--- a/solution.py
+++ b/solution.py
@@ -224,7 +224,7 @@
         grad[c] = dot(back[c], y[2, c])
         for o in range(2):
             turned[o, c] = dot(back[c], y[o, c]).astype(BF16)
-    for i, j in enumerate(peers(n)):
+    for i, j in enumerate(back_peers(n)):
         at = pl.multiple_of((me[0] ^ j) * part_rows, part_rows)
         for o in range(2):
             for c in range(CLASSES):
@@ -369,6 +369,10 @@
 
 
 def peers(n):
+    return [0, 1, *range(2, n, 2), *range(3, n, 2)]
+
+
+def back_peers(n):
     return [0, n - 2, 1, *range(2, n - 2, 2), *range(3, n, 2)]
 
 
@@ -417,16 +421,16 @@
 
     bits = [1 << b for b in range(d.bit_length() - 1)]
     parts_ = keep, traded, keep_other, trade(d, 1, send)
-    early = exchange(n, js[:-1], mixed[:-1])
+    js = back_peers(n)
+    mixed = exchange(n, js, mixed)
     for bit in bits[1:]:
         keep, send = add_grads(*parts_)
         parts_ = keep, trade(d, bit, send)
-    mixed = early + exchange(n, js[-1:], after([keep], mixed[-1:]))
 
     outs = []
     early = n - 2
     for at in (slice(early), slice(early, n)):
-        *outs, gated = gate(peers(n)[at], me, query, grad, value, key, gain, mixed[at], outs)
+        *outs, _ = gate(js[at], me, query, grad, value, key, gain, mixed[at], outs)
     grad_filter = turn_grads(*parts_)
     return *(x[None] for x in outs), grad_filter
 

time: 69.7 us -> 68 us (0.976)
  starting transfers between devices: 30.3 us -> 28.7 us
    ppermute x21, waiting for transfers between devices: 10.3 us -> 13 us  [exchange(): lax.ppermute(block, 'ctx', [(i, i ^ j) for i in range(n)])]
    ppermute x3, waiting for transfers between devices: 3.33 us -> 0.73 us  [trade(): return resident(lax.ppermute(send, 'dp', [(i, i ^ bit) for i in range(d)]))]
    ppermute x21, starting transfers between devices: 24.4 us -> 23.4 us  [exchange(): lax.ppermute(block, 'ctx', [(i, i ^ j) for i in range(n)])]
  transfers between devices with their start and end apart: 24 -> 24, of which waited for: 8 -> 8; matrix products, arithmetic and copies ran while one was open for 0% -> 0% of each run, Pallas kernels for 27% -> 30%
where the time goes in v14:
time: 68 us; the launch traced here: 67.8 us
  starting transfers between devices  28.7 us (42%)
  Pallas kernels  24.6 us (36%)
  waiting for transfers between devices  13.7 us (20%)
  between operations  0.77 us (1%)
    ppermute x21, starting transfers between devices, exchange(): lax.ppermute(block, 'ctx', [(i, i ^ j) for i in range(n)])  23.4 us
    ppermute x21, waiting for transfers between devices, exchange(): lax.ppermute(block, 'ctx', [(i, i ^ j) for i in range(n)])  13 us
    pallas_call x2, Pallas kernels, conv(): pl.pallas_call(functools.partial(conv_kernel, n, d, half), in_specs=[SMEM...  9.56 us
    pallas_call x2, Pallas kernels, gate(): pl.pallas_call(functools.partial(gate_kernel, js), in_specs=[SMEM] + [VME...  7.17 us
    ppermute x3, starting transfers between devices, trade(): return resident(lax.ppermute(send, 'dp', [(i, i ^ bit) for i in range(d)]))  5.27 us
    pallas_call x2, Pallas kernels, filter_spectrum(): pl.pallas_call(functools.partial(filter_kernel, half), in_specs=[VMEM] *...  3.6 us
    pallas_call x1, Pallas kernels, products(): pl.pallas_call(functools.partial(product_kernel, n), in_specs=[SMEM] + [H...  3.14 us
  transfers between devices with their start and end apart: 24, of which 8 were waited for; matrix products, arithmetic and copies ran while one was open for 0% of the time, Pallas kernels for 30%

profile of v14, /device:TPU:0, one launch (start us, length us, event | category | flops | bytes accessed | tf_op | source)
XLA Modules:
  0.0 67.8 jit_solution(18150932898915540808)
XLA Ops:
  0.7 3.1 %products.1 = (bf16[128,4096]{1,0:T(8,128)(2,1)S(1)}, bf16[128,4096]{1,0:T(8,128)(2,1)S(1)}, bf16[128,4096]{1,0:T(8,128)(2,1)S(1)}, bf16[128,4096]{1,0:T(8,128)(...) custom-call(s32[2]{0:T(128)S(1)} %pad_add_fusion.me, ...), custom_call_target="tpu_custom_call" | custom-call | tf_op jit(solution)/shard_map/products/pallas_call | solution.py:126
  4.4 2.6 %collective-permute-start.1 = (bf16[2,128,256]{2,1,0:T(8,128)(2,1)S(1)}, bf16[2,128,256]{2,1,0:T(8,128)(2,1)S(1)}, u32[]{:S(2)}, u32[]{:S(2)}) collective-permute-start(bf16[2,128,256]{2,1,0:T(8,128)(2,1)S(1)} %get-tuple-element.68), channel_id=1, source_target_pairs={{0,2},{1,3},{2,0},{3,1},{4,6},{5,7},{6,4},{7,5},{8,10},{9,11},{10,... | collective-permute-start | bytes 393224 | tf_op jit(solution)/shard_map/ppermute | solution.py:381
  6.9 1.5 %collective-permute-start.9 = (bf16[2,128,256]{2,1,0:T(8,128)(2,1)S(1)}, bf16[2,128,256]{2,1,0:T(8,128)(2,1)S(1)}, u32[]{:S(2)}, u32[]{:S(2)}) collective-permute-start(bf16[2,128,256]{2,1,0:T(8,128)(2,1)S(1)} %get-tuple-element.86), channel_id=1, source_target_pairs={{0,4},{1,5},{2,6},{3,7},{4,0},{5,1},{6,2},{7,3},{8,12},{9,13},{10,... | collective-permute-start | bytes 393224 | tf_op jit(solution)/shard_map/ppermute | solution.py:381
  8.5 1.2 %collective-permute-start.11 = (bf16[2,128,256]{2,1,0:T(8,128)(2,1)S(1)}, bf16[2,128,256]{2,1,0:T(8,128)(2,1)S(1)}, u32[]{:S(2)}, u32[]{:S(2)}) collective-permute-start(bf16[2,128,256]{2,1,0:T(8,128)(2,1)S(1)} %get-tuple-element.88), channel_id=1, source_target_pairs={{0,3},{1,2},{2,1},{3,0},{4,7},{5,6},{6,5},{7,4},{8,11},{9,10},{10,... | collective-permute-start | bytes 393224 | tf_op jit(solution)/shard_map/ppermute | solution.py:381
  9.7 2.0 %collective-permute-start.12 = (bf16[2,128,256]{2,1,0:T(8,128)(2,1)S(1)}, bf16[2,128,256]{2,1,0:T(8,128)(2,1)S(1)}, u32[]{:S(2)}, u32[]{:S(2)}) collective-permute-start(bf16[2,128,256]{2,1,0:T(8,128)(2,1)S(1)} %get-tuple-element.89), channel_id=1, source_target_pairs={{0,5},{1,4},{2,7},{3,6},{4,1},{5,0},{6,3},{7,2},{8,13},{9,12},{10,... | collective-permute-start | bytes 393224 | tf_op jit(solution)/shard_map/ppermute | solution.py:381
  11.7 1.3 %collective-permute-start.13 = (bf16[2,128,256]{2,1,0:T(8,128)(2,1)S(1)}, bf16[2,128,256]{2,1,0:T(8,128)(2,1)S(1)}, u32[]{:S(2)}, u32[]{:S(2)}) collective-permute-start(bf16[2,128,256]{2,1,0:T(8,128)(2,1)S(1)} %get-tuple-element.90), channel_id=1, source_target_pairs={{0,7},{1,6},{2,5},{3,4},{4,3},{5,2},{6,1},{7,0},{8,15},{9,14},{10,... | collective-permute-start | bytes 393224 | tf_op jit(solution)/shard_map/ppermute | solution.py:381
  13.0 1.9 %filter_spectrum.2.refs_0_.refs_8_ = f32[8,256,256]{2,1,0:T(8,128)S(1)} custom-call(f32[512,1024]{1,0:T(8,128)S(1)} %copy-done.1, bf16[8,256,256]{2,1,0:T(8,128)(2,1)S(1)} %copy-done, bf16[2,128,256]{2,1,0:T(8,128)(2,1)S(1)} %collective-permute-done.refs_0_.refs_1_, bf16[2,128,256]{2,1,0:T(8,128)(2,1)S(1)} %collective-permute-done.1.refs_1_.refs_2_), custom_call_target="tpu_custom_call" | custom-call | tf_op jit(solution)/shard_map/filter_spectrum/pallas_call | solution.py:171
  15.0 1.3 %collective-permute-start.2 = (bf16[2,128,256]{2,1,0:T(8,128)(2,1)S(1)}, bf16[2,128,256]{2,1,0:T(8,128)(2,1)S(1)}, u32[]{:S(2)}, u32[]{:S(2)}) collective-permute-start(bf16[2,128,256]{2,1,0:T(8,128)(2,1)S(1)} %get-tuple-element.74), channel_id=1, source_target_pairs={{0,1},{1,0},{2,3},{3,2},{4,5},{5,4},{6,7},{7,6},{8,9},{9,8},{10,11... | collective-permute-start | bytes 393224 | tf_op jit(solution)/shard_map/ppermute | solution.py:381
  16.3 0.7 %collective-permute-start.3 = (bf16[2,128,256]{2,1,0:T(8,128)(2,1)S(1)}, bf16[2,128,256]{2,1,0:T(8,128)(2,1)S(1)}, u32[]{:S(2)}, u32[]{:S(2)}) collective-permute-start(bf16[2,128,256]{2,1,0:T(8,128)(2,1)S(1)} %get-tuple-element.75), channel_id=1, source_target_pairs={{0,2},{1,3},{2,0},{3,1},{4,6},{5,7},{6,4},{7,5},{8,10},{9,11},{10,... | collective-permute-start | bytes 393224 | tf_op jit(solution)/shard_map/ppermute | solution.py:381
  17.1 1.7 %filter_spectrum.3.refs_0_.refs_8_ = f32[8,256,256]{2,1,0:T(8,128)S(1)} custom-call(f32[512,1024]{1,0:T(8,128)S(1)} %copy-done.1, bf16[8,256,256]{2,1,0:T(8,128)(2,1)S(1)} %copy-done, f32[8,256,256]{2,1,0:T(8,128)S(1)} %filter_spectrum.2.refs_0_.refs_8_), custom_call_target="tpu_custom_call" | custom-call | tf_op jit(solution)/shard_map/filter_spectrum/pallas_call | solution.py:171
  18.8 1.0 %collective-permute-start.4 = (bf16[2,128,256]{2,1,0:T(8,128)(2,1)S(1)}, bf16[2,128,256]{2,1,0:T(8,128)(2,1)S(1)}, u32[]{:S(2)}, u32[]{:S(2)}) collective-permute-start(bf16[2,128,256]{2,1,0:T(8,128)(2,1)S(1)} %get-tuple-element.76), channel_id=1, source_target_pairs={{0,4},{1,5},{2,6},{3,7},{4,0},{5,1},{6,2},{7,3},{8,12},{9,13},{10,... | collective-permute-start | bytes 393224 | tf_op jit(solution)/shard_map/ppermute | solution.py:381
  19.8 0.9 %collective-permute-done.12.refs_6_ = bf16[2,128,256]{2,1,0:T(8,128)(2,1)S(1)} collective-permute-done((bf16[2,128,256]{2,1,0:T(8,128)(2,1)S(1)}, bf16[2,128,256]{2,1,0:T(8,128)(2,1)S(1)}, u32[]{:S(2)}, u32[]{:S(2)}) %collective-permute-start.12) | collective-permute-done | bytes 131104 | tf_op jit(solution)/shard_map/ppermute | solution.py:381
  20.8 1.1 %collective-permute-start.5 = (bf16[2,128,256]{2,1,0:T(8,128)(2,1)S(1)}, bf16[2,128,256]{2,1,0:T(8,128)(2,1)S(1)}, u32[]{:S(2)}, u32[]{:S(2)}) collective-permute-start(bf16[2,128,256]{2,1,0:T(8,128)(2,1)S(1)} %get-tuple-element.81), channel_id=1, source_target_pairs={{0,6},{1,7},{2,4},{3,5},{4,2},{5,3},{6,0},{7,1},{8,14},{9,15},{10,... | collective-permute-start | bytes 393224 | tf_op jit(solution)/shard_map/ppermute | solution.py:381
  21.9 1.5 %collective-permute-start.6 = (bf16[2,128,256]{2,1,0:T(8,128)(2,1)S(1)}, bf16[2,128,256]{2,1,0:T(8,128)(2,1)S(1)}, u32[]{:S(2)}, u32[]{:S(2)}) collective-permute-start(bf16[2,128,256]{2,1,0:T(8,128)(2,1)S(1)} %get-tuple-element.82), channel_id=1, source_target_pairs={{0,3},{1,2},{2,1},{3,0},{4,7},{5,6},{6,5},{7,4},{8,11},{9,10},{10,... | collective-permute-start | bytes 393224 | tf_op jit(solution)/shard_map/ppermute | solution.py:381
  24.6 4.8 %conv.2 = (bf16[2,2,128,256]{3,2,1,0:T(8,128)(2,1)S(1)}, bf16[2,2,128,256]{3,2,1,0:T(8,128)(2,1)S(1)}, bf16[2,2,128,256]{3,2,1,0:T(8,128)(2,1)S(1)}, bf16[2,2,12...) custom-call(s32[2]{0:T(128)S(1)} %pad_add_fusion.me, ...), custom_call_target="tpu_custom_call" | custom-call | tf_op jit(solution)/shard_map/conv/pallas_call | solution.py:246
  29.4 1.6 %collective-permute-start.21 = (bf16[2,256,256]{2,1,0:T(8,128)(2,1)S(1)}, bf16[2,256,256]{2,1,0:T(8,128)(2,1)S(1)}, u32[]{:S(2)}, u32[]{:S(2)}) collective-permute-start(bf16[2,256,256]{2,1,0:T(8,128)(2,1)S(1)} %get-tuple-element.116), channel_id=1, source_target_pairs={{0,8},{8,0},{16,24},{24,16},{1,9},{9,1},{17,25},{25,17},{2,10},{10... | collective-permute-start | bytes 786440 | tf_op jit(solution)/shard_map/ppermute | solution.py:342
  31.0 1.3 %collective-permute-done.8.refs_7_ = bf16[2,128,256]{2,1,0:T(8,128)(2,1)S(1)} collective-permute-done((bf16[2,128,256]{2,1,0:T(8,128)(2,1)S(1)}, bf16[2,128,256]{2,1,0:T(8,128)(2,1)S(1)}, u32[]{:S(2)}, u32[]{:S(2)}) %collective-permute-start.8) | collective-permute-done | bytes 131104 | tf_op jit(solution)/shard_map/ppermute | solution.py:381
  32.4 4.8 %conv.3 = (bf16[2,2,128,256]{3,2,1,0:T(8,128)(2,1)S(1)}, bf16[2,2,128,256]{3,2,1,0:T(8,128)(2,1)S(1)}, bf16[2,2,128,256]{3,2,1,0:T(8,128)(2,1)S(1)}, bf16[2,2,12...) custom-call(s32[2]{0:T(128)S(1)} %pad_add_fusion.me, ...), custom_call_target="tpu_custom_call", output_to_operand_aliasing={{0}: (12, {}), {1}: (13, {}), {2}: (14, {}), {3}: (15, {}),... | custom-call | tf_op jit(solution)/shard_map/conv/pallas_call | solution.py:246
  37.1 2.4 %collective-permute-start.16 = (bf16[2,2,128,256]{3,2,1,0:T(8,128)(2,1)S(1)}, bf16[2,2,128,256]{3,2,1,0:T(8,128)(2,1)S(1)}, u32[]{:S(2)}, u32[]{:S(2)}) collective-permute-start(bf16[2,2,128,256]{3,2,1,0:T(8,128)(2,1)S(1)} %get-tuple-element.102), channel_id=1, source_target_pairs={{0,6},{1,7},{2,4},{3,5},{4,2},{5,3},{6,0},{7,1},{8,14},{9,15},{10,... | collective-permute-start | bytes 786440 | tf_op jit(solution)/shard_map/ppermute | solution.py:381
  40.1 1.2 %collective-permute-start.22 = (bf16[2,256,256]{2,1,0:T(8,128)(2,1)S(1)}, bf16[2,256,256]{2,1,0:T(8,128)(2,1)S(1)}, u32[]{:S(2)}, u32[]{:S(2)}) collective-permute-start(bf16[2,256,256]{2,1,0:T(8,128)(2,1)S(1)} %get-tuple-element.118), channel_id=1, source_target_pairs={{0,8},{8,0},{16,24},{24,16},{1,9},{9,1},{17,25},{25,17},{2,10},{10... | collective-permute-start | bytes 786440 | tf_op jit(solution)/shard_map/ppermute | solution.py:342
  41.2 1.0 %collective-permute-start.18 = (bf16[2,2,128,256]{3,2,1,0:T(8,128)(2,1)S(1)}, bf16[2,2,128,256]{3,2,1,0:T(8,128)(2,1)S(1)}, u32[]{:S(2)}, u32[]{:S(2)}) collective-permute-start(bf16[2,2,128,256]{3,2,1,0:T(8,128)(2,1)S(1)} %get-tuple-element.104), channel_id=1, source_target_pairs={{0,2},{1,3},{2,0},{3,1},{4,6},{5,7},{6,4},{7,5},{8,10},{9,11},{10,... | collective-permute-start | bytes 786440 | tf_op jit(solution)/shard_map/ppermute | solution.py:381
  42.2 5.0 %collective-permute-done.16.refs_1_ = bf16[2,2,128,256]{3,2,1,0:T(8,128)(2,1)S(1)} collective-permute-done((bf16[2,2,128,256]{3,2,1,0:T(8,128)(2,1)S(1)}, bf16[2,2,128,256]{3,2,1,0:T(8,128)(2,1)S(1)}, u32[]{:S(2)}, u32[]{:S(2)}) %collective-permute-start.16) | collective-permute-done | bytes 262176 | tf_op jit(solution)/shard_map/ppermute | solution.py:381
  47.2 2.7 %collective-permute-start.14 = (bf16[2,2,128,256]{3,2,1,0:T(8,128)(2,1)S(1)}, bf16[2,2,128,256]{3,2,1,0:T(8,128)(2,1)S(1)}, u32[]{:S(2)}, u32[]{:S(2)}) collective-permute-start(bf16[2,2,128,256]{3,2,1,0:T(8,128)(2,1)S(1)} %get-tuple-element.99), channel_id=1, source_target_pairs={{0,5},{1,4},{2,7},{3,6},{4,1},{5,0},{6,3},{7,2},{8,13},{9,12},{10,... | collective-permute-start | bytes 786440 | tf_op jit(solution)/shard_map/ppermute | solution.py:381
  49.9 0.8 %collective-permute-start.15 = (bf16[2,2,128,256]{3,2,1,0:T(8,128)(2,1)S(1)}, bf16[2,2,128,256]{3,2,1,0:T(8,128)(2,1)S(1)}, u32[]{:S(2)}, u32[]{:S(2)}) collective-permute-start(bf16[2,2,128,256]{3,2,1,0:T(8,128)(2,1)S(1)} %get-tuple-element.100), channel_id=1, source_target_pairs={{0,7},{1,6},{2,5},{3,4},{4,3},{5,2},{6,1},{7,0},{8,15},{9,14},{10,... | collective-permute-start | bytes 786440 | tf_op jit(solution)/shard_map/ppermute | solution.py:381
  50.8 2.8 %collective-permute-done.18.refs_3_ = bf16[2,2,128,256]{3,2,1,0:T(8,128)(2,1)S(1)} collective-permute-done((bf16[2,2,128,256]{3,2,1,0:T(8,128)(2,1)S(1)}, bf16[2,2,128,256]{3,2,1,0:T(8,128)(2,1)S(1)}, u32[]{:S(2)}, u32[]{:S(2)}) %collective-permute-start.18) | collective-permute-done | bytes 262176 | tf_op jit(solution)/shard_map/ppermute | solution.py:381
  53.6 2.5 %collective-permute-start.23 = (bf16[1,256,512]{2,1,0:T(8,128)(2,1)S(1)}, bf16[1,256,512]{2,1,0:T(8,128)(2,1)S(1)}, u32[]{:S(2)}, u32[]{:S(2)}) collective-permute-start(bf16[1,256,512]{2,1,0:T(8,128)(2,1)S(1)} %get-tuple-element.120), channel_id=1, source_target_pairs={{0,16},{8,24},{16,0},{24,8},{1,17},{9,25},{17,1},{25,9},{2,18},{10... | collective-permute-start | bytes 786440 | tf_op jit(solution)/shard_map/ppermute | solution.py:342
  56.1 1.5 %collective-permute-done.20.refs_5_ = bf16[2,2,128,256]{3,2,1,0:T(8,128)(2,1)S(1)} collective-permute-done((bf16[2,2,128,256]{3,2,1,0:T(8,128)(2,1)S(1)}, bf16[2,2,128,256]{3,2,1,0:T(8,128)(2,1)S(1)}, u32[]{:S(2)}, u32[]{:S(2)}) %collective-permute-start.20) | collective-permute-done | bytes 262176 | tf_op jit(solution)/shard_map/ppermute | solution.py:381
  57.5 4.4 %gate.2 = (bf16[128,4096]{1,0:T(8,128)(2,1)}, bf16[128,4096]{1,0:T(8,128)(2,1)}, bf16[128,4096]{1,0:T(8,128)(2,1)}, bf16[128,4096]{1,0:T(8,128)(2,1)}, f32[8,128]{1,0:T(8,128)}) custom-call(s32[2]{0:T(128)S(1)} %pad_add_fusion.me, bf16[128,4096]{1,0:T(8,128)(2,1)S(1)} %get-tuple-element.63.query, bf16[128,4096]{1,0:T(8,128)(2,1)S(1)} %get-tuple-element.64.grad, ...), custom_call_target="tpu_custom_call" | custom-call | tf_op jit(solution)/shard_map/gate/pallas_call | solution.py:308
  62.0 1.3 %collective-permute-done.15.refs_1_ = bf16[2,2,128,256]{3,2,1,0:T(8,128)(2,1)S(1)} collective-permute-done((bf16[2,2,128,256]{3,2,1,0:T(8,128)(2,1)S(1)}, bf16[2,2,128,256]{3,2,1,0:T(8,128)(2,1)S(1)}, u32[]{:S(2)}, u32[]{:S(2)}) %collective-permute-start.15) | collective-permute-done | bytes 262176 | tf_op jit(solution)/shard_map/ppermute | solution.py:381
  63.3 2.7 %gate.3 = (bf16[128,4096]{1,0:T(8,128)(2,1)}, bf16[128,4096]{1,0:T(8,128)(2,1)}, bf16[128,4096]{1,0:T(8,128)(2,1)}, bf16[128,4096]{1,0:T(8,128)(2,1)}, f32[8,128]{1,0:T(8,128)}) custom-call(s32[2]{0:T(128)S(1)} %pad_add_fusion.me, ...), custom_call_target="tpu_custom_call", output_to_operand_aliasing={{0}: (8, {}), {1}: (9, {}), {2}: (10, {}), {3}: (11, {})} | custom-call | tf_op jit(solution)/shard_map/gate/pallas_call | solution.py:308
  66.0 0.7 %collective-permute-done.23.got = bf16[1,256,512]{2,1,0:T(8,128)(2,1)S(1)} collective-permute-done((bf16[1,256,512]{2,1,0:T(8,128)(2,1)S(1)}, bf16[1,256,512]{2,1,0:T(8,128)(2,1)S(1)}, u32[]{:S(2)}, u32[]{:S(2)}) %collective-permute-start.23) | collective-permute-done | bytes 262176 | tf_op jit(solution)/shard_map/ppermute | solution.py:342
  66.8 1.1 %turn_grads.1 = f32[512,256]{1,0:T(8,128)} custom-call(f32[1,256,512]{2,1,0:T(8,128)S(1)} %get-tuple-element.119.keep, bf16[1,256,512]{2,1,0:T(8,128)(2,1)S(1)} %collective-permute-done.23.got), custom_call_target="tpu_custom_call" | custom-call | tf_op jit(solution)/shard_map/turn_grads/pallas_call | solution.py:360
  (36 shorter events, 2.6 us)
Async XLA Ops:
  0.7 12.3 %copy-start = (bf16[8,256,256]{2,1,0:T(8,128)(2,1)S(1)}, bf16[8,256,256]{2,1,0:T(8,128)(2,1)}, u32[]{:S(2)}) copy-start(bf16[8,256,256]{2,1,0:T(8,128)(2,1)} %constant.12.clone.fwd.refs_9_) | copy-start | bytes 3145732
  0.7 12.3 %copy-start.1 = (f32[512,1024]{1,0:T(8,128)S(1)}, f32[512,1024]{1,0:T(8,128)}, u32[]{:S(2)}) copy-start(f32[512,1024]{1,0:T(8,128)} %filt.3) | copy-start | bytes 6291460
  3.9 5.8 %collective-permute-start = (bf16[2,128,256]{2,1,0:T(8,128)(2,1)S(1)}, bf16[2,128,256]{2,1,0:T(8,128)(2,1)S(1)}, u32[]{:S(2)}, u32[]{:S(2)}) collective-permute-start(bf16[2,128,256]{2,1,0:T(8,128)(2,1)S(1)} %get-tuple-element.67), channel_id=1, source_target_pairs={{0,1},{1,0},{2,3},{3,2},{4,5},{5,4},{6,7},{7,6},{8,9},{9,8},{10,11... | collective-permute-start | bytes 393224 | tf_op jit(solution)/shard_map/ppermute | solution.py:381
  4.4 7.3 %collective-permute-start.1 = (bf16[2,128,256]{2,1,0:T(8,128)(2,1)S(1)}, bf16[2,128,256]{2,1,0:T(8,128)(2,1)S(1)}, u32[]{:S(2)}, u32[]{:S(2)}) collective-permute-start(bf16[2,128,256]{2,1,0:T(8,128)(2,1)S(1)} %get-tuple-element.68), channel_id=1, source_target_pairs={{0,2},{1,3},{2,0},{3,1},{4,6},{5,7},{6,4},{7,5},{8,10},{9,11},{10,... | collective-permute-start | bytes 393224 | tf_op jit(solution)/shard_map/ppermute | solution.py:381
  6.9 8.1 %collective-permute-start.9 = (bf16[2,128,256]{2,1,0:T(8,128)(2,1)S(1)}, bf16[2,128,256]{2,1,0:T(8,128)(2,1)S(1)}, u32[]{:S(2)}, u32[]{:S(2)}) collective-permute-start(bf16[2,128,256]{2,1,0:T(8,128)(2,1)S(1)} %get-tuple-element.86), channel_id=1, source_target_pairs={{0,4},{1,5},{2,6},{3,7},{4,0},{5,1},{6,2},{7,3},{8,12},{9,13},{10,... | collective-permute-start | bytes 393224 | tf_op jit(solution)/shard_map/ppermute | solution.py:381
  8.5 7.8 %collective-permute-start.10 = (bf16[2,128,256]{2,1,0:T(8,128)(2,1)S(1)}, bf16[2,128,256]{2,1,0:T(8,128)(2,1)S(1)}, u32[]{:S(2)}, u32[]{:S(2)}) collective-permute-start(bf16[2,128,256]{2,1,0:T(8,128)(2,1)S(1)} %get-tuple-element.87), channel_id=1, source_target_pairs={{0,6},{1,7},{2,4},{3,5},{4,2},{5,3},{6,0},{7,1},{8,14},{9,15},{10,... | collective-permute-start | bytes 393224 | tf_op jit(solution)/shard_map/ppermute | solution.py:381
  8.5 10.3 %collective-permute-start.11 = (bf16[2,128,256]{2,1,0:T(8,128)(2,1)S(1)}, bf16[2,128,256]{2,1,0:T(8,128)(2,1)S(1)}, u32[]{:S(2)}, u32[]{:S(2)}) collective-permute-start(bf16[2,128,256]{2,1,0:T(8,128)(2,1)S(1)} %get-tuple-element.88), channel_id=1, source_target_pairs={{0,3},{1,2},{2,1},{3,0},{4,7},{5,6},{6,5},{7,4},{8,11},{9,10},{10,... | collective-permute-start | bytes 393224 | tf_op jit(solution)/shard_map/ppermute | solution.py:381
  9.7 11.1 %collective-permute-start.12 = (bf16[2,128,256]{2,1,0:T(8,128)(2,1)S(1)}, bf16[2,128,256]{2,1,0:T(8,128)(2,1)S(1)}, u32[]{:S(2)}, u32[]{:S(2)}) collective-permute-start(bf16[2,128,256]{2,1,0:T(8,128)(2,1)S(1)} %get-tuple-element.89), channel_id=1, source_target_pairs={{0,5},{1,4},{2,7},{3,6},{4,1},{5,0},{6,3},{7,2},{8,13},{9,12},{10,... | collective-permute-start | bytes 393224 | tf_op jit(solution)/shard_map/ppermute | solution.py:381
  11.7 10.2 %collective-permute-start.13 = (bf16[2,128,256]{2,1,0:T(8,128)(2,1)S(1)}, bf16[2,128,256]{2,1,0:T(8,128)(2,1)S(1)}, u32[]{:S(2)}, u32[]{:S(2)}) collective-permute-start(bf16[2,128,256]{2,1,0:T(8,128)(2,1)S(1)} %get-tuple-element.90), channel_id=1, source_target_pairs={{0,7},{1,6},{2,5},{3,4},{4,3},{5,2},{6,1},{7,0},{8,15},{9,14},{10,... | collective-permute-start | bytes 393224 | tf_op jit(solution)/shard_map/ppermute | solution.py:381
  15.0 8.3 %collective-permute-start.2 = (bf16[2,128,256]{2,1,0:T(8,128)(2,1)S(1)}, bf16[2,128,256]{2,1,0:T(8,128)(2,1)S(1)}, u32[]{:S(2)}, u32[]{:S(2)}) collective-permute-start(bf16[2,128,256]{2,1,0:T(8,128)(2,1)S(1)} %get-tuple-element.74), channel_id=1, source_target_pairs={{0,1},{1,0},{2,3},{3,2},{4,5},{5,4},{6,7},{7,6},{8,9},{9,8},{10,11... | collective-permute-start | bytes 393224 | tf_op jit(solution)/shard_map/ppermute | solution.py:381
  16.3 7.7 %collective-permute-start.3 = (bf16[2,128,256]{2,1,0:T(8,128)(2,1)S(1)}, bf16[2,128,256]{2,1,0:T(8,128)(2,1)S(1)}, u32[]{:S(2)}, u32[]{:S(2)}) collective-permute-start(bf16[2,128,256]{2,1,0:T(8,128)(2,1)S(1)} %get-tuple-element.75), channel_id=1, source_target_pairs={{0,2},{1,3},{2,0},{3,1},{4,6},{5,7},{6,4},{7,5},{8,10},{9,11},{10,... | collective-permute-start | bytes 393224 | tf_op jit(solution)/shard_map/ppermute | solution.py:381
  18.8 5.8 %copy-start.2 = (bf16[8,128,256]{2,1,0:T(8,128)(2,1)S(1)}, bf16[8,128,256]{2,1,0:T(8,128)(2,1)}, u32[]{:S(2)}) copy-start(bf16[8,128,256]{2,1,0:T(8,128)(2,1)} %constant.13.clone.refs_10_) | copy-start | bytes 1572868
  18.8 10.6 %collective-permute-start.4 = (bf16[2,128,256]{2,1,0:T(8,128)(2,1)S(1)}, bf16[2,128,256]{2,1,0:T(8,128)(2,1)S(1)}, u32[]{:S(2)}, u32[]{:S(2)}) collective-permute-start(bf16[2,128,256]{2,1,0:T(8,128)(2,1)S(1)} %get-tuple-element.76), channel_id=1, source_target_pairs={{0,4},{1,5},{2,6},{3,7},{4,0},{5,1},{6,2},{7,3},{8,12},{9,13},{10,... | collective-permute-start | bytes 393224 | tf_op jit(solution)/shard_map/ppermute | solution.py:381
  20.8 10.2 %collective-permute-start.5 = (bf16[2,128,256]{2,1,0:T(8,128)(2,1)S(1)}, bf16[2,128,256]{2,1,0:T(8,128)(2,1)S(1)}, u32[]{:S(2)}, u32[]{:S(2)}) collective-permute-start(bf16[2,128,256]{2,1,0:T(8,128)(2,1)S(1)} %get-tuple-element.81), channel_id=1, source_target_pairs={{0,6},{1,7},{2,4},{3,5},{4,2},{5,3},{6,0},{7,1},{8,14},{9,15},{10,... | collective-permute-start | bytes 393224 | tf_op jit(solution)/shard_map/ppermute | solution.py:381
  21.9 9.1 %collective-permute-start.6 = (bf16[2,128,256]{2,1,0:T(8,128)(2,1)S(1)}, bf16[2,128,256]{2,1,0:T(8,128)(2,1)S(1)}, u32[]{:S(2)}, u32[]{:S(2)}) collective-permute-start(bf16[2,128,256]{2,1,0:T(8,128)(2,1)S(1)} %get-tuple-element.82), channel_id=1, source_target_pairs={{0,3},{1,2},{2,1},{3,0},{4,7},{5,6},{6,5},{7,4},{8,11},{9,10},{10,... | collective-permute-start | bytes 393224 | tf_op jit(solution)/shard_map/ppermute | solution.py:381
  23.4 7.6 %collective-permute-start.7 = (bf16[2,128,256]{2,1,0:T(8,128)(2,1)S(1)}, bf16[2,128,256]{2,1,0:T(8,128)(2,1)S(1)}, u32[]{:S(2)}, u32[]{:S(2)}) collective-permute-start(bf16[2,128,256]{2,1,0:T(8,128)(2,1)S(1)} %get-tuple-element.83), channel_id=1, source_target_pairs={{0,5},{1,4},{2,7},{3,6},{4,1},{5,0},{6,3},{7,2},{8,13},{9,12},{10,... | collective-permute-start | bytes 393224 | tf_op jit(solution)/shard_map/ppermute | solution.py:381
  24.0 8.4 %collective-permute-start.8 = (bf16[2,128,256]{2,1,0:T(8,128)(2,1)S(1)}, bf16[2,128,256]{2,1,0:T(8,128)(2,1)S(1)}, u32[]{:S(2)}, u32[]{:S(2)}) collective-permute-start(bf16[2,128,256]{2,1,0:T(8,128)(2,1)S(1)} %get-tuple-element.84), channel_id=1, source_target_pairs={{0,7},{1,6},{2,5},{3,4},{4,3},{5,2},{6,1},{7,0},{8,15},{9,14},{10,... | collective-permute-start | bytes 393224 | tf_op jit(solution)/shard_map/ppermute | solution.py:381
  29.4 12.9 %collective-permute-start.21 = (bf16[2,256,256]{2,1,0:T(8,128)(2,1)S(1)}, bf16[2,256,256]{2,1,0:T(8,128)(2,1)S(1)}, u32[]{:S(2)}, u32[]{:S(2)}) collective-permute-start(bf16[2,256,256]{2,1,0:T(8,128)(2,1)S(1)} %get-tuple-element.116), channel_id=1, source_target_pairs={{0,8},{8,0},{16,24},{24,16},{1,9},{9,1},{17,25},{25,17},{2,10},{10... | collective-permute-start | bytes 786440 | tf_op jit(solution)/shard_map/ppermute | solution.py:342
  32.4 25.2 %copy-start.3 = (f32[4096]{0:T(1024)S(1)}, f32[4096]{0:T(1024)}, u32[]{:S(2)}) copy-start(f32[4096]{0:T(1024)} %param.13) | copy-start | bytes 49156
  37.1 10.1 %collective-permute-start.16 = (bf16[2,2,128,256]{3,2,1,0:T(8,128)(2,1)S(1)}, bf16[2,2,128,256]{3,2,1,0:T(8,128)(2,1)S(1)}, u32[]{:S(2)}, u32[]{:S(2)}) collective-permute-start(bf16[2,2,128,256]{3,2,1,0:T(8,128)(2,1)S(1)} %get-tuple-element.102), channel_id=1, source_target_pairs={{0,6},{1,7},{2,4},{3,5},{4,2},{5,3},{6,0},{7,1},{8,14},{9,15},{10,... | collective-permute-start | bytes 786440 | tf_op jit(solution)/shard_map/ppermute | solution.py:381
  39.5 7.7 %collective-permute-start.17 = (bf16[2,2,128,256]{3,2,1,0:T(8,128)(2,1)S(1)}, bf16[2,2,128,256]{3,2,1,0:T(8,128)(2,1)S(1)}, u32[]{:S(2)}, u32[]{:S(2)}) collective-permute-start(bf16[2,2,128,256]{3,2,1,0:T(8,128)(2,1)S(1)} %get-tuple-element.103), channel_id=1, source_target_pairs={{0,1},{1,0},{2,3},{3,2},{4,5},{5,4},{6,7},{7,6},{8,9},{9,8},{10,11... | collective-permute-start | bytes 786440 | tf_op jit(solution)/shard_map/ppermute | solution.py:381
  40.1 9.9 %collective-permute-start.22 = (bf16[2,256,256]{2,1,0:T(8,128)(2,1)S(1)}, bf16[2,256,256]{2,1,0:T(8,128)(2,1)S(1)}, u32[]{:S(2)}, u32[]{:S(2)}) collective-permute-start(bf16[2,256,256]{2,1,0:T(8,128)(2,1)S(1)} %get-tuple-element.118), channel_id=1, source_target_pairs={{0,8},{8,0},{16,24},{24,16},{1,9},{9,1},{17,25},{25,17},{2,10},{10... | collective-permute-start | bytes 786440 | tf_op jit(solution)/shard_map/ppermute | solution.py:342
  41.2 12.3 %collective-permute-start.18 = (bf16[2,2,128,256]{3,2,1,0:T(8,128)(2,1)S(1)}, bf16[2,2,128,256]{3,2,1,0:T(8,128)(2,1)S(1)}, u32[]{:S(2)}, u32[]{:S(2)}) collective-permute-start(bf16[2,2,128,256]{3,2,1,0:T(8,128)(2,1)S(1)} %get-tuple-element.104), channel_id=1, source_target_pairs={{0,2},{1,3},{2,0},{3,1},{4,6},{5,7},{6,4},{7,5},{8,10},{9,11},{10,... | collective-permute-start | bytes 786440 | tf_op jit(solution)/shard_map/ppermute | solution.py:381
  42.2 13.8 %collective-permute-start.19 = (bf16[2,2,128,256]{3,2,1,0:T(8,128)(2,1)S(1)}, bf16[2,2,128,256]{3,2,1,0:T(8,128)(2,1)S(1)}, u32[]{:S(2)}, u32[]{:S(2)}) collective-permute-start(bf16[2,2,128,256]{3,2,1,0:T(8,128)(2,1)S(1)} %get-tuple-element.105), channel_id=1, source_target_pairs={{0,4},{1,5},{2,6},{3,7},{4,0},{5,1},{6,2},{7,3},{8,12},{9,13},{10,... | collective-permute-start | bytes 786440 | tf_op jit(solution)/shard_map/ppermute | solution.py:381
  47.2 10.3 %collective-permute-start.20 = (bf16[2,2,128,256]{3,2,1,0:T(8,128)(2,1)S(1)}, bf16[2,2,128,256]{3,2,1,0:T(8,128)(2,1)S(1)}, u32[]{:S(2)}, u32[]{:S(2)}) collective-permute-start(bf16[2,2,128,256]{3,2,1,0:T(8,128)(2,1)S(1)} %get-tuple-element.106), channel_id=1, source_target_pairs={{0,3},{1,2},{2,1},{3,0},{4,7},{5,6},{6,5},{7,4},{8,11},{9,10},{10,... | collective-permute-start | bytes 786440 | tf_op jit(solution)/shard_map/ppermute | solution.py:381
  47.2 14.7 %collective-permute-start.14 = (bf16[2,2,128,256]{3,2,1,0:T(8,128)(2,1)S(1)}, bf16[2,2,128,256]{3,2,1,0:T(8,128)(2,1)S(1)}, u32[]{:S(2)}, u32[]{:S(2)}) collective-permute-start(bf16[2,2,128,256]{3,2,1,0:T(8,128)(2,1)S(1)} %get-tuple-element.99), channel_id=1, source_target_pairs={{0,5},{1,4},{2,7},{3,6},{4,1},{5,0},{6,3},{7,2},{8,13},{9,12},{10,... | collective-permute-start | bytes 786440 | tf_op jit(solution)/shard_map/ppermute | solution.py:381
  49.9 13.4 %collective-permute-start.15 = (bf16[2,2,128,256]{3,2,1,0:T(8,128)(2,1)S(1)}, bf16[2,2,128,256]{3,2,1,0:T(8,128)(2,1)S(1)}, u32[]{:S(2)}, u32[]{:S(2)}) collective-permute-start(bf16[2,2,128,256]{3,2,1,0:T(8,128)(2,1)S(1)} %get-tuple-element.100), channel_id=1, source_target_pairs={{0,7},{1,6},{2,5},{3,4},{4,3},{5,2},{6,1},{7,0},{8,15},{9,14},{10,... | collective-permute-start | bytes 786440 | tf_op jit(solution)/shard_map/ppermute | solution.py:381
  53.6 13.2 %collective-permute-start.23 = (bf16[1,256,512]{2,1,0:T(8,128)(2,1)S(1)}, bf16[1,256,512]{2,1,0:T(8,128)(2,1)S(1)}, u32[]{:S(2)}, u32[]{:S(2)}) collective-permute-start(bf16[1,256,512]{2,1,0:T(8,128)(2,1)S(1)} %get-tuple-element.120), channel_id=1, source_target_pairs={{0,16},{8,24},{16,0},{24,8},{1,17},{9,25},{17,1},{25,9},{2,18},{10... | collective-permute-start | bytes 786440 | tf_op jit(solution)/shard_map/ppermute | solution.py:342

commit v15 on v14

--- a/solution.py
+++ b/solution.py
@@ -14,7 +14,6 @@
 BF16 = jnp.bfloat16
 CLASSES = 8
 HALVES = 2
-STEPS = 4
 PARAMS = pltpu.CompilerParams(vmem_limit_bytes=16 * 1024 * 1024)
 CONV_PARAMS = pltpu.CompilerParams(vmem_limit_bytes=34 * 1024 * 1024)
 SMEM = pl.BlockSpec(memory_space=pltpu.SMEM)
@@ -92,48 +91,54 @@
     return pl.ds(pl.multiple_of((me[0] ^ j) * width, 128), width)
 
 
-def product_kernel(n, me, key, value, query, grad, *refs):
-    bufs, outs, sems = refs[:4], refs[4:-1], refs[-1]
-    _, rows, width = outs[0].shape
-    width *= HALVES
-    step = rows // STEPS
+def half_columns(me, j, half, width):
+    return pl.ds(pl.multiple_of((HALVES * (me[0] ^ j) + half) * width, 128), width)
+
+
+def first_kernel(n, me, key, value, query, grad, *refs):
+    outs, (bufs, sems) = refs[:n], refs[n:]
+    width = outs[0].shape[2]
     copies = []
-    for i in range(STEPS):
-        at = pl.ds(i * step, step)
+    for i, j in enumerate(peers(n)):
+        cols = half_columns(me, j, 0, width)
         copies.append(
             [
-                pltpu.make_async_copy(src.at[at], dst.at[at], sems.at[a, i])
-                for a, (src, dst) in enumerate(zip((key, value, query, grad), bufs))
+                pltpu.make_async_copy(src.at[:, cols], bufs.at[a, i], sems.at[a, i])
+                for a, src in enumerate((key, value, query, grad))
             ]
         )
         for copy in copies[i]:
             copy.start()
-    for s in range(STEPS):
-        at = pl.ds(s * step, step)
-        for a, (left, right) in enumerate((bufs[:2], bufs[2:])):
-            copies[s][2 * a].wait()
-            copies[s][2 * a + 1].wait()
-            for i, j in enumerate(peers(n)):
-                cols = peer_columns(me, j, width)
-                value = (left[at, cols].astype(F32) * right[at, cols].astype(F32)).astype(BF16)
-                for half in range(HALVES):
-                    outs[half * n + i][a, at] = value[:, half * width // HALVES :][:, : width // HALVES]
-
-
-def products(n, me, key, value, query, grad):
-    rows, total = key.shape
+    for i, out in enumerate(outs):
+        for copy in copies[i]:
+            copy.wait()
+        for a in range(2):
+            left, right = bufs[2 * a, i].astype(F32), bufs[2 * a + 1, i].astype(F32)
+            out[a] = (left * right).astype(BF16)
+
+
+def second_kernel(n, me, key, value, query, grad, *refs):
+    outs = refs[-n:]
+    width = outs[0].shape[2]
+    for out, j in zip(outs, peers(n)):
+        cols = half_columns(me, j, 1, width)
+        for a, (left, right) in enumerate(((key, value), (query, grad))):
+            out[a] = (left[:, cols].astype(F32) * right[:, cols].astype(F32)).astype(BF16)
+
+
+def products(half, n, me, arrays, arrived):
+    rows, total = arrays[0].shape
     width = total // n // HALVES
-    out = pl.pallas_call(
-        functools.partial(product_kernel, n),
-        in_specs=[SMEM] + [HBM] * 4,
-        out_specs=[VMEM] * (4 + HALVES * n),
-        out_shape=[pltpu.VMEM(key.shape, BF16)] * 4
-        + [pltpu.VMEM((2, rows, width), BF16)] * (HALVES * n),
-        scratch_shapes=[pltpu.SemaphoreType.DMA((4, STEPS))],
+    scratch = [pltpu.VMEM((4, n, rows, width), BF16), pltpu.SemaphoreType.DMA((4, n))]
+    return pl.pallas_call(
+        functools.partial(second_kernel if half else first_kernel, n),
+        in_specs=[SMEM] + [VMEM if half else HBM] * 4 + [VMEM] * len(arrived),
+        out_specs=[VMEM] * n,
+        out_shape=[pltpu.VMEM((2, rows, width), BF16)] * n,
+        scratch_shapes=[] if half else scratch,
         compiler_params=PARAMS,
         name="products",
-    )(me, key, value, query, grad)
-    return out[:4], [out[4 + h * n : 4 + (h + 1) * n] for h in range(HALVES)]
+    )(me, *arrays, *arrived)
 
 
 def lane_groups(width):
@@ -406,15 +411,17 @@
     gain = skip_gain[None, :]
     me = jnp.stack([lax.axis_index("ctx"), lax.axis_index("dp")]).astype(jnp.int32)
 
-    arrays = [in_hbm(x[0]) for x in (key_in, value_in, query_in, grad_out)]
-    (key, value, query, grad), got = products(n, me, *arrays)
+    arrays = [x[0] for x in (key_in, value_in, query_in, grad_out)]
     js = peers(n)
     cut = n // 2
-    first = exchange(n, js, got[0])
+    first = products(0, n, me, [in_hbm(x) for x in arrays], [])
+    first = exchange(n, js, first)
+    key, value, query, grad = arrays = [resident(x) for x in arrays]
+    other = products(1, n, me, arrays, first[1:2])
     spec = filter_spectrum(0, filters, fwd, first[1:3])
-    second = exchange(n, js[:cut], after([spec], got[1][:cut]))
+    second = exchange(n, js[:cut], after([spec], other[:cut]))
     spec_other = filter_spectrum(1, filters, fwd, [spec])
-    second += exchange(n, js[cut:], after([spec_other], got[1][cut:]))
+    second += exchange(n, js[cut:], after([spec_other], other[cut:]))
     *mixed, keep, send = conv(n, d, 0, me, first, spec, fwd, back, [])
     traded = trade(d, 1, send)
     *mixed, keep_other, send = conv(n, d, 1, me, second, spec_other, fwd, back, mixed)

time: 68 us -> 67.5 us (level)
  starting transfers between devices: 28.7 us -> 28 us
    ppermute x21, starting transfers between devices: 23.4 us -> 22.7 us  [exchange(): lax.ppermute(block, 'ctx', [(i, i ^ j) for i in range(n)])]
    pallas_call x1 -> x2, Pallas kernels: 3.14 us -> 3.53 us  [products(): pl.pallas_call(functools.partial(second_kernel if half else first_kernel,...]
  transfers between devices with their start and end apart: 24 -> 24, of which waited for: 8 -> 8; matrix products, arithmetic and copies ran while one was open for 0% -> 0% of each run, Pallas kernels for 30% -> 32%
where the time goes in v15:
time: 67.5 us; the launch traced here: 67.4 us
  starting transfers between devices  28 us (41%)
  Pallas kernels  25 us (37%)
  waiting for transfers between devices  13.5 us (20%)
  between operations  0.8 us (1%)
    ppermute x21, starting transfers between devices, exchange(): lax.ppermute(block, 'ctx', [(i, i ^ j) for i in range(n)])  22.7 us
    ppermute x21, waiting for transfers between devices, exchange(): lax.ppermute(block, 'ctx', [(i, i ^ j) for i in range(n)])  12.8 us
    pallas_call x2, Pallas kernels, conv(): pl.pallas_call(functools.partial(conv_kernel, n, d, half), in_specs=[SMEM...  9.56 us
    pallas_call x2, Pallas kernels, gate(): pl.pallas_call(functools.partial(gate_kernel, js), in_specs=[SMEM] + [VME...  7.17 us
    ppermute x3, starting transfers between devices, trade(): return resident(lax.ppermute(send, 'dp', [(i, i ^ bit) for i in range(d)]))  5.27 us
    pallas_call x2, Pallas kernels, filter_spectrum(): pl.pallas_call(functools.partial(filter_kernel, half), in_specs=[VMEM] *...  3.6 us
    pallas_call x2, Pallas kernels, products(): pl.pallas_call(functools.partial(second_kernel if half else first_kernel,...  3.53 us
  transfers between devices with their start and end apart: 24, of which 8 were waited for; matrix products, arithmetic and copies ran while one was open for 0% of the time, Pallas kernels for 32%

profile of v15, /device:TPU:0, one launch (start us, length us, event | category | flops | bytes accessed | tf_op | source)
XLA Modules:
  0.0 67.4 jit_solution(10522229379006063443)
XLA Ops:
  0.7 2.7 %products.2 = (bf16[2,128,256]{2,1,0:T(8,128)(2,1)S(1)}, bf16[2,128,256]{2,1,0:T(8,128)(2,1)S(1)}, bf16[2,128,256]{2,1,0:T(8,128)(2,1)S(1)}, bf16[2,128,256]{2,1...) custom-call(s32[2]{0:T(128)S(1)} %pad_add_fusion.me, ...), custom_call_target="tpu_custom_call" | custom-call | tf_op jit(solution)/shard_map/products/pallas_call | solution.py:133
  4.0 2.6 %collective-permute-start.1 = (bf16[2,128,256]{2,1,0:T(8,128)(2,1)S(1)}, bf16[2,128,256]{2,1,0:T(8,128)(2,1)S(1)}, u32[]{:S(2)}, u32[]{:S(2)}) collective-permute-start(bf16[2,128,256]{2,1,0:T(8,128)(2,1)S(1)} %get-tuple-element.60), channel_id=1, source_target_pairs={{0,2},{1,3},{2,0},{3,1},{4,6},{5,7},{6,4},{7,5},{8,10},{9,11},{10,... | collective-permute-start | bytes 393224 | tf_op jit(solution)/shard_map/ppermute | solution.py:386
  6.5 1.5 %collective-permute-start.9 = (bf16[2,128,256]{2,1,0:T(8,128)(2,1)S(1)}, bf16[2,128,256]{2,1,0:T(8,128)(2,1)S(1)}, u32[]{:S(2)}, u32[]{:S(2)}) collective-permute-start(bf16[2,128,256]{2,1,0:T(8,128)(2,1)S(1)} %get-tuple-element.78), channel_id=1, source_target_pairs={{0,4},{1,5},{2,6},{3,7},{4,0},{5,1},{6,2},{7,3},{8,12},{9,13},{10,... | collective-permute-start | bytes 393224 | tf_op jit(solution)/shard_map/ppermute | solution.py:386
  8.1 1.2 %collective-permute-start.11 = (bf16[2,128,256]{2,1,0:T(8,128)(2,1)S(1)}, bf16[2,128,256]{2,1,0:T(8,128)(2,1)S(1)}, u32[]{:S(2)}, u32[]{:S(2)}) collective-permute-start(bf16[2,128,256]{2,1,0:T(8,128)(2,1)S(1)} %get-tuple-element.80), channel_id=1, source_target_pairs={{0,3},{1,2},{2,1},{3,0},{4,7},{5,6},{6,5},{7,4},{8,11},{9,10},{10,... | collective-permute-start | bytes 393224 | tf_op jit(solution)/shard_map/ppermute | solution.py:386
  9.2 2.0 %collective-permute-start.12 = (bf16[2,128,256]{2,1,0:T(8,128)(2,1)S(1)}, bf16[2,128,256]{2,1,0:T(8,128)(2,1)S(1)}, u32[]{:S(2)}, u32[]{:S(2)}) collective-permute-start(bf16[2,128,256]{2,1,0:T(8,128)(2,1)S(1)} %get-tuple-element.81), channel_id=1, source_target_pairs={{0,5},{1,4},{2,7},{3,6},{4,1},{5,0},{6,3},{7,2},{8,13},{9,12},{10,... | collective-permute-start | bytes 393224 | tf_op jit(solution)/shard_map/ppermute | solution.py:386
  11.3 0.8 %products.3 = (bf16[2,128,256]{2,1,0:T(8,128)(2,1)S(1)}, bf16[2,128,256]{2,1,0:T(8,128)(2,1)S(1)}, bf16[2,128,256]{2,1,0:T(8,128)(2,1)S(1)}, bf16[2,128,256]{2,1...) custom-call(s32[2]{0:T(128)S(1)} %pad_add_fusion.me, ...), custom_call_target="tpu_custom_call" | custom-call | tf_op jit(solution)/shard_map/products/pallas_call | solution.py:133
  12.6 1.9 %filter_spectrum.2.refs_0_.refs_8_ = f32[8,256,256]{2,1,0:T(8,128)S(1)} custom-call(f32[512,1024]{1,0:T(8,128)S(1)} %copy-done.5, bf16[8,256,256]{2,1,0:T(8,128)(2,1)S(1)} %copy-done.4, bf16[2,128,256]{2,1,0:T(8,128)(2,1)S(1)} %collective-permute-done.refs_0_.refs_1_, bf16[2,128,256]{2,1,0:T(8,128)(2,1)S(1)} %collective-permute-done.1.refs_1_.refs_2_), custom_call_target="tpu_custom_call" | custom-call | tf_op jit(solution)/shard_map/filter_spectrum/pallas_call | solution.py:176
  14.6 1.3 %collective-permute-start.2 = (bf16[2,128,256]{2,1,0:T(8,128)(2,1)S(1)}, bf16[2,128,256]{2,1,0:T(8,128)(2,1)S(1)}, u32[]{:S(2)}, u32[]{:S(2)}) collective-permute-start(bf16[2,128,256]{2,1,0:T(8,128)(2,1)S(1)} %get-tuple-element.66), channel_id=1, source_target_pairs={{0,1},{1,0},{2,3},{3,2},{4,5},{5,4},{6,7},{7,6},{8,9},{9,8},{10,11... | collective-permute-start | bytes 393224 | tf_op jit(solution)/shard_map/ppermute | solution.py:386
  15.9 0.7 %collective-permute-start.3 = (bf16[2,128,256]{2,1,0:T(8,128)(2,1)S(1)}, bf16[2,128,256]{2,1,0:T(8,128)(2,1)S(1)}, u32[]{:S(2)}, u32[]{:S(2)}) collective-permute-start(bf16[2,128,256]{2,1,0:T(8,128)(2,1)S(1)} %get-tuple-element.67), channel_id=1, source_target_pairs={{0,2},{1,3},{2,0},{3,1},{4,6},{5,7},{6,4},{7,5},{8,10},{9,11},{10,... | collective-permute-start | bytes 393224 | tf_op jit(solution)/shard_map/ppermute | solution.py:386
  16.6 1.7 %filter_spectrum.3.refs_0_.refs_8_ = f32[8,256,256]{2,1,0:T(8,128)S(1)} custom-call(f32[512,1024]{1,0:T(8,128)S(1)} %copy-done.5, bf16[8,256,256]{2,1,0:T(8,128)(2,1)S(1)} %copy-done.4, f32[8,256,256]{2,1,0:T(8,128)S(1)} %filter_spectrum.2.refs_0_.refs_8_), custom_call_target="tpu_custom_call" | custom-call | tf_op jit(solution)/shard_map/filter_spectrum/pallas_call | solution.py:176
  18.4 1.2 %collective-permute-start.4 = (bf16[2,128,256]{2,1,0:T(8,128)(2,1)S(1)}, bf16[2,128,256]{2,1,0:T(8,128)(2,1)S(1)}, u32[]{:S(2)}, u32[]{:S(2)}) collective-permute-start(bf16[2,128,256]{2,1,0:T(8,128)(2,1)S(1)} %get-tuple-element.68), channel_id=1, source_target_pairs={{0,4},{1,5},{2,6},{3,7},{4,0},{5,1},{6,2},{7,3},{8,12},{9,13},{10,... | collective-permute-start | bytes 393224 | tf_op jit(solution)/shard_map/ppermute | solution.py:386
  19.6 0.7 %collective-permute-done.12.refs_6_ = bf16[2,128,256]{2,1,0:T(8,128)(2,1)S(1)} collective-permute-done((bf16[2,128,256]{2,1,0:T(8,128)(2,1)S(1)}, bf16[2,128,256]{2,1,0:T(8,128)(2,1)S(1)}, u32[]{:S(2)}, u32[]{:S(2)}) %collective-permute-start.12) | collective-permute-done | bytes 131104 | tf_op jit(solution)/shard_map/ppermute | solution.py:386
  20.3 1.1 %collective-permute-start.5 = (bf16[2,128,256]{2,1,0:T(8,128)(2,1)S(1)}, bf16[2,128,256]{2,1,0:T(8,128)(2,1)S(1)}, u32[]{:S(2)}, u32[]{:S(2)}) collective-permute-start(bf16[2,128,256]{2,1,0:T(8,128)(2,1)S(1)} %get-tuple-element.73), channel_id=1, source_target_pairs={{0,6},{1,7},{2,4},{3,5},{4,2},{5,3},{6,0},{7,1},{8,14},{9,15},{10,... | collective-permute-start | bytes 393224 | tf_op jit(solution)/shard_map/ppermute | solution.py:386
  21.5 1.5 %collective-permute-start.6 = (bf16[2,128,256]{2,1,0:T(8,128)(2,1)S(1)}, bf16[2,128,256]{2,1,0:T(8,128)(2,1)S(1)}, u32[]{:S(2)}, u32[]{:S(2)}) collective-permute-start(bf16[2,128,256]{2,1,0:T(8,128)(2,1)S(1)} %get-tuple-element.74), channel_id=1, source_target_pairs={{0,3},{1,2},{2,1},{3,0},{4,7},{5,6},{6,5},{7,4},{8,11},{9,10},{10,... | collective-permute-start | bytes 393224 | tf_op jit(solution)/shard_map/ppermute | solution.py:386
  24.2 4.8 %conv.2 = (bf16[2,2,128,256]{3,2,1,0:T(8,128)(2,1)S(1)}, bf16[2,2,128,256]{3,2,1,0:T(8,128)(2,1)S(1)}, bf16[2,2,128,256]{3,2,1,0:T(8,128)(2,1)S(1)}, bf16[2,2,12...) custom-call(s32[2]{0:T(128)S(1)} %pad_add_fusion.me, ...), custom_call_target="tpu_custom_call" | custom-call | tf_op jit(solution)/shard_map/conv/pallas_call | solution.py:251
  29.0 1.6 %collective-permute-start.21 = (bf16[2,256,256]{2,1,0:T(8,128)(2,1)S(1)}, bf16[2,256,256]{2,1,0:T(8,128)(2,1)S(1)}, u32[]{:S(2)}, u32[]{:S(2)}) collective-permute-start(bf16[2,256,256]{2,1,0:T(8,128)(2,1)S(1)} %get-tuple-element.108), channel_id=1, source_target_pairs={{0,8},{8,0},{16,24},{24,16},{1,9},{9,1},{17,25},{25,17},{2,10},{10... | collective-permute-start | bytes 786440 | tf_op jit(solution)/shard_map/ppermute | solution.py:347
  30.6 1.3 %collective-permute-done.8.refs_7_ = bf16[2,128,256]{2,1,0:T(8,128)(2,1)S(1)} collective-permute-done((bf16[2,128,256]{2,1,0:T(8,128)(2,1)S(1)}, bf16[2,128,256]{2,1,0:T(8,128)(2,1)S(1)}, u32[]{:S(2)}, u32[]{:S(2)}) %collective-permute-start.8) | collective-permute-done | bytes 131104 | tf_op jit(solution)/shard_map/ppermute | solution.py:386
  31.9 4.8 %conv.3 = (bf16[2,2,128,256]{3,2,1,0:T(8,128)(2,1)S(1)}, bf16[2,2,128,256]{3,2,1,0:T(8,128)(2,1)S(1)}, bf16[2,2,128,256]{3,2,1,0:T(8,128)(2,1)S(1)}, bf16[2,2,12...) custom-call(s32[2]{0:T(128)S(1)} %pad_add_fusion.me, ...), custom_call_target="tpu_custom_call", output_to_operand_aliasing={{0}: (12, {}), {1}: (13, {}), {2}: (14, {}), {3}: (15, {}),... | custom-call | tf_op jit(solution)/shard_map/conv/pallas_call | solution.py:251
  36.7 2.4 %collective-permute-start.16 = (bf16[2,2,128,256]{3,2,1,0:T(8,128)(2,1)S(1)}, bf16[2,2,128,256]{3,2,1,0:T(8,128)(2,1)S(1)}, u32[]{:S(2)}, u32[]{:S(2)}) collective-permute-start(bf16[2,2,128,256]{3,2,1,0:T(8,128)(2,1)S(1)} %get-tuple-element.94), channel_id=1, source_target_pairs={{0,6},{1,7},{2,4},{3,5},{4,2},{5,3},{6,0},{7,1},{8,14},{9,15},{10,... | collective-permute-start | bytes 786440 | tf_op jit(solution)/shard_map/ppermute | solution.py:386
  39.6 1.2 %collective-permute-start.22 = (bf16[2,256,256]{2,1,0:T(8,128)(2,1)S(1)}, bf16[2,256,256]{2,1,0:T(8,128)(2,1)S(1)}, u32[]{:S(2)}, u32[]{:S(2)}) collective-permute-start(bf16[2,256,256]{2,1,0:T(8,128)(2,1)S(1)} %get-tuple-element.110), channel_id=1, source_target_pairs={{0,8},{8,0},{16,24},{24,16},{1,9},{9,1},{17,25},{25,17},{2,10},{10... | collective-permute-start | bytes 786440 | tf_op jit(solution)/shard_map/ppermute | solution.py:347
  40.8 1.0 %collective-permute-start.18 = (bf16[2,2,128,256]{3,2,1,0:T(8,128)(2,1)S(1)}, bf16[2,2,128,256]{3,2,1,0:T(8,128)(2,1)S(1)}, u32[]{:S(2)}, u32[]{:S(2)}) collective-permute-start(bf16[2,2,128,256]{3,2,1,0:T(8,128)(2,1)S(1)} %get-tuple-element.96), channel_id=1, source_target_pairs={{0,2},{1,3},{2,0},{3,1},{4,6},{5,7},{6,4},{7,5},{8,10},{9,11},{10,... | collective-permute-start | bytes 786440 | tf_op jit(solution)/shard_map/ppermute | solution.py:386
  41.8 5.0 %collective-permute-done.16.refs_1_ = bf16[2,2,128,256]{3,2,1,0:T(8,128)(2,1)S(1)} collective-permute-done((bf16[2,2,128,256]{3,2,1,0:T(8,128)(2,1)S(1)}, bf16[2,2,128,256]{3,2,1,0:T(8,128)(2,1)S(1)}, u32[]{:S(2)}, u32[]{:S(2)}) %collective-permute-start.16) | collective-permute-done | bytes 262176 | tf_op jit(solution)/shard_map/ppermute | solution.py:386
  46.8 2.7 %collective-permute-start.14 = (bf16[2,2,128,256]{3,2,1,0:T(8,128)(2,1)S(1)}, bf16[2,2,128,256]{3,2,1,0:T(8,128)(2,1)S(1)}, u32[]{:S(2)}, u32[]{:S(2)}) collective-permute-start(bf16[2,2,128,256]{3,2,1,0:T(8,128)(2,1)S(1)} %get-tuple-element.91), channel_id=1, source_target_pairs={{0,5},{1,4},{2,7},{3,6},{4,1},{5,0},{6,3},{7,2},{8,13},{9,12},{10,... | collective-permute-start | bytes 786440 | tf_op jit(solution)/shard_map/ppermute | solution.py:386
  49.5 0.8 %collective-permute-start.15 = (bf16[2,2,128,256]{3,2,1,0:T(8,128)(2,1)S(1)}, bf16[2,2,128,256]{3,2,1,0:T(8,128)(2,1)S(1)}, u32[]{:S(2)}, u32[]{:S(2)}) collective-permute-start(bf16[2,2,128,256]{3,2,1,0:T(8,128)(2,1)S(1)} %get-tuple-element.92), channel_id=1, source_target_pairs={{0,7},{1,6},{2,5},{3,4},{4,3},{5,2},{6,1},{7,0},{8,15},{9,14},{10,... | collective-permute-start | bytes 786440 | tf_op jit(solution)/shard_map/ppermute | solution.py:386
  50.3 2.8 %collective-permute-done.18.refs_3_ = bf16[2,2,128,256]{3,2,1,0:T(8,128)(2,1)S(1)} collective-permute-done((bf16[2,2,128,256]{3,2,1,0:T(8,128)(2,1)S(1)}, bf16[2,2,128,256]{3,2,1,0:T(8,128)(2,1)S(1)}, u32[]{:S(2)}, u32[]{:S(2)}) %collective-permute-start.18) | collective-permute-done | bytes 262176 | tf_op jit(solution)/shard_map/ppermute | solution.py:386
  53.1 2.5 %collective-permute-start.23 = (bf16[1,256,512]{2,1,0:T(8,128)(2,1)S(1)}, bf16[1,256,512]{2,1,0:T(8,128)(2,1)S(1)}, u32[]{:S(2)}, u32[]{:S(2)}) collective-permute-start(bf16[1,256,512]{2,1,0:T(8,128)(2,1)S(1)} %get-tuple-element.112), channel_id=1, source_target_pairs={{0,16},{8,24},{16,0},{24,8},{1,17},{9,25},{17,1},{25,9},{2,18},{10... | collective-permute-start | bytes 786440 | tf_op jit(solution)/shard_map/ppermute | solution.py:347
  55.6 1.5 %collective-permute-done.20.refs_5_ = bf16[2,2,128,256]{3,2,1,0:T(8,128)(2,1)S(1)} collective-permute-done((bf16[2,2,128,256]{3,2,1,0:T(8,128)(2,1)S(1)}, bf16[2,2,128,256]{3,2,1,0:T(8,128)(2,1)S(1)}, u32[]{:S(2)}, u32[]{:S(2)}) %collective-permute-start.20) | collective-permute-done | bytes 262176 | tf_op jit(solution)/shard_map/ppermute | solution.py:386
  57.1 4.4 %gate.2 = (bf16[128,4096]{1,0:T(8,128)(2,1)}, bf16[128,4096]{1,0:T(8,128)(2,1)}, bf16[128,4096]{1,0:T(8,128)(2,1)}, bf16[128,4096]{1,0:T(8,128)(2,1)}, f32[8,128]{1,0:T(8,128)}) custom-call(s32[2]{0:T(128)S(1)} %pad_add_fusion.me, bf16[128,4096]{1,0:T(8,128)(2,1)S(1)} %bitcast.13, bf16[128,4096]{1,0:T(8,128)(2,1)S(1)} %bitcast.17, ...), custom_call_target="tpu_custom_call" | custom-call | tf_op jit(solution)/shard_map/gate/pallas_call | solution.py:313
  61.5 1.3 %collective-permute-done.15.refs_1_ = bf16[2,2,128,256]{3,2,1,0:T(8,128)(2,1)S(1)} collective-permute-done((bf16[2,2,128,256]{3,2,1,0:T(8,128)(2,1)S(1)}, bf16[2,2,128,256]{3,2,1,0:T(8,128)(2,1)S(1)}, u32[]{:S(2)}, u32[]{:S(2)}) %collective-permute-start.15) | collective-permute-done | bytes 262176 | tf_op jit(solution)/shard_map/ppermute | solution.py:386
  62.8 2.7 %gate.3 = (bf16[128,4096]{1,0:T(8,128)(2,1)}, bf16[128,4096]{1,0:T(8,128)(2,1)}, bf16[128,4096]{1,0:T(8,128)(2,1)}, bf16[128,4096]{1,0:T(8,128)(2,1)}, f32[8,128]{1,0:T(8,128)}) custom-call(s32[2]{0:T(128)S(1)} %pad_add_fusion.me, bf16[128,4096]{1,0:T(8,128)(2,1)S(1)} %bitcast.14, ...), custom_call_target="tpu_custom_call", output_to_operand_aliasing={{0}: (8, {}), {1}: (9, {}), {2}: (10, {}), {3}: (11, {})} | custom-call | tf_op jit(solution)/shard_map/gate/pallas_call | solution.py:313
  65.6 0.7 %collective-permute-done.23.got = bf16[1,256,512]{2,1,0:T(8,128)(2,1)S(1)} collective-permute-done((bf16[1,256,512]{2,1,0:T(8,128)(2,1)S(1)}, bf16[1,256,512]{2,1,0:T(8,128)(2,1)S(1)}, u32[]{:S(2)}, u32[]{:S(2)}) %collective-permute-start.23) | collective-permute-done | bytes 262176 | tf_op jit(solution)/shard_map/ppermute | solution.py:347
  66.3 1.1 %turn_grads.1 = f32[512,256]{1,0:T(8,128)} custom-call(f32[1,256,512]{2,1,0:T(8,128)S(1)} %get-tuple-element.111.keep, bf16[1,256,512]{2,1,0:T(8,128)(2,1)S(1)} %collective-permute-done.23.got), custom_call_target="tpu_custom_call" | custom-call | tf_op jit(solution)/shard_map/turn_grads/pallas_call | solution.py:365
  (45 shorter events, 3.1 us)
Async XLA Ops:
  0.7 10.5 %copy-start = (bf16[1,128,4096]{2,1,0:T(8,128)(2,1)S(1)}, bf16[1,128,4096]{2,1,0:T(8,128)(2,1)}, u32[]{:S(2)}) copy-start(bf16[1,128,4096]{2,1,0:T(8,128)(2,1)} %param.8) | copy-start | bytes 3145732
  0.7 10.5 %copy-start.1 = (bf16[1,128,4096]{2,1,0:T(8,128)(2,1)S(1)}, bf16[1,128,4096]{2,1,0:T(8,128)(2,1)}, u32[]{:S(2)}) copy-start(bf16[1,128,4096]{2,1,0:T(8,128)(2,1)} %param.11) | copy-start | bytes 3145732
  0.7 10.5 %copy-start.2 = (bf16[1,128,4096]{2,1,0:T(8,128)(2,1)S(1)}, bf16[1,128,4096]{2,1,0:T(8,128)(2,1)}, u32[]{:S(2)}) copy-start(bf16[1,128,4096]{2,1,0:T(8,128)(2,1)} %param.10) | copy-start | bytes 3145732
  0.7 10.5 %copy-start.3 = (bf16[1,128,4096]{2,1,0:T(8,128)(2,1)S(1)}, bf16[1,128,4096]{2,1,0:T(8,128)(2,1)}, u32[]{:S(2)}) copy-start(bf16[1,128,4096]{2,1,0:T(8,128)(2,1)} %param.9) | copy-start | bytes 3145732
  3.4 5.8 %collective-permute-start = (bf16[2,128,256]{2,1,0:T(8,128)(2,1)S(1)}, bf16[2,128,256]{2,1,0:T(8,128)(2,1)S(1)}, u32[]{:S(2)}, u32[]{:S(2)}) collective-permute-start(bf16[2,128,256]{2,1,0:T(8,128)(2,1)S(1)} %get-tuple-element.59), channel_id=1, source_target_pairs={{0,1},{1,0},{2,3},{3,2},{4,5},{5,4},{6,7},{7,6},{8,9},{9,8},{10,11... | collective-permute-start | bytes 393224 | tf_op jit(solution)/shard_map/ppermute | solution.py:386
  4.0 8.2 %collective-permute-start.1 = (bf16[2,128,256]{2,1,0:T(8,128)(2,1)S(1)}, bf16[2,128,256]{2,1,0:T(8,128)(2,1)S(1)}, u32[]{:S(2)}, u32[]{:S(2)}) collective-permute-start(bf16[2,128,256]{2,1,0:T(8,128)(2,1)S(1)} %get-tuple-element.60), channel_id=1, source_target_pairs={{0,2},{1,3},{2,0},{3,1},{4,6},{5,7},{6,4},{7,5},{8,10},{9,11},{10,... | collective-permute-start | bytes 393224 | tf_op jit(solution)/shard_map/ppermute | solution.py:386
  6.5 8.1 %collective-permute-start.9 = (bf16[2,128,256]{2,1,0:T(8,128)(2,1)S(1)}, bf16[2,128,256]{2,1,0:T(8,128)(2,1)S(1)}, u32[]{:S(2)}, u32[]{:S(2)}) collective-permute-start(bf16[2,128,256]{2,1,0:T(8,128)(2,1)S(1)} %get-tuple-element.78), channel_id=1, source_target_pairs={{0,4},{1,5},{2,6},{3,7},{4,0},{5,1},{6,2},{7,3},{8,12},{9,13},{10,... | collective-permute-start | bytes 393224 | tf_op jit(solution)/shard_map/ppermute | solution.py:386
  8.0 7.8 %collective-permute-start.10 = (bf16[2,128,256]{2,1,0:T(8,128)(2,1)S(1)}, bf16[2,128,256]{2,1,0:T(8,128)(2,1)S(1)}, u32[]{:S(2)}, u32[]{:S(2)}) collective-permute-start(bf16[2,128,256]{2,1,0:T(8,128)(2,1)S(1)} %get-tuple-element.79), channel_id=1, source_target_pairs={{0,6},{1,7},{2,4},{3,5},{4,2},{5,3},{6,0},{7,1},{8,14},{9,15},{10,... | collective-permute-start | bytes 393224 | tf_op jit(solution)/shard_map/ppermute | solution.py:386
  8.1 10.3 %collective-permute-start.11 = (bf16[2,128,256]{2,1,0:T(8,128)(2,1)S(1)}, bf16[2,128,256]{2,1,0:T(8,128)(2,1)S(1)}, u32[]{:S(2)}, u32[]{:S(2)}) collective-permute-start(bf16[2,128,256]{2,1,0:T(8,128)(2,1)S(1)} %get-tuple-element.80), channel_id=1, source_target_pairs={{0,3},{1,2},{2,1},{3,0},{4,7},{5,6},{6,5},{7,4},{8,11},{9,10},{10,... | collective-permute-start | bytes 393224 | tf_op jit(solution)/shard_map/ppermute | solution.py:386
  9.2 3.4 %copy-start.4 = (bf16[8,256,256]{2,1,0:T(8,128)(2,1)S(1)}, bf16[8,256,256]{2,1,0:T(8,128)(2,1)}, u32[]{:S(2)}) copy-start(bf16[8,256,256]{2,1,0:T(8,128)(2,1)} %constant.12.clone.fwd.refs_9_) | copy-start | bytes 3145732
  9.2 3.4 %copy-start.5 = (f32[512,1024]{1,0:T(8,128)S(1)}, f32[512,1024]{1,0:T(8,128)}, u32[]{:S(2)}) copy-start(f32[512,1024]{1,0:T(8,128)} %filt.3) | copy-start | bytes 6291460
  9.2 11.1 %collective-permute-start.12 = (bf16[2,128,256]{2,1,0:T(8,128)(2,1)S(1)}, bf16[2,128,256]{2,1,0:T(8,128)(2,1)S(1)}, u32[]{:S(2)}, u32[]{:S(2)}) collective-permute-start(bf16[2,128,256]{2,1,0:T(8,128)(2,1)S(1)} %get-tuple-element.81), channel_id=1, source_target_pairs={{0,5},{1,4},{2,7},{3,6},{4,1},{5,0},{6,3},{7,2},{8,13},{9,12},{10,... | collective-permute-start | bytes 393224 | tf_op jit(solution)/shard_map/ppermute | solution.py:386
  12.1 9.4 %collective-permute-start.13 = (bf16[2,128,256]{2,1,0:T(8,128)(2,1)S(1)}, bf16[2,128,256]{2,1,0:T(8,128)(2,1)S(1)}, u32[]{:S(2)}, u32[]{:S(2)}) collective-permute-start(bf16[2,128,256]{2,1,0:T(8,128)(2,1)S(1)} %get-tuple-element.82), channel_id=1, source_target_pairs={{0,7},{1,6},{2,5},{3,4},{4,3},{5,2},{6,1},{7,0},{8,15},{9,14},{10,... | collective-permute-start | bytes 393224 | tf_op jit(solution)/shard_map/ppermute | solution.py:386
  14.6 8.3 %collective-permute-start.2 = (bf16[2,128,256]{2,1,0:T(8,128)(2,1)S(1)}, bf16[2,128,256]{2,1,0:T(8,128)(2,1)S(1)}, u32[]{:S(2)}, u32[]{:S(2)}) collective-permute-start(bf16[2,128,256]{2,1,0:T(8,128)(2,1)S(1)} %get-tuple-element.66), channel_id=1, source_target_pairs={{0,1},{1,0},{2,3},{3,2},{4,5},{5,4},{6,7},{7,6},{8,9},{9,8},{10,11... | collective-permute-start | bytes 393224 | tf_op jit(solution)/shard_map/ppermute | solution.py:386
  15.9 7.7 %collective-permute-start.3 = (bf16[2,128,256]{2,1,0:T(8,128)(2,1)S(1)}, bf16[2,128,256]{2,1,0:T(8,128)(2,1)S(1)}, u32[]{:S(2)}, u32[]{:S(2)}) collective-permute-start(bf16[2,128,256]{2,1,0:T(8,128)(2,1)S(1)} %get-tuple-element.67), channel_id=1, source_target_pairs={{0,2},{1,3},{2,0},{3,1},{4,6},{5,7},{6,4},{7,5},{8,10},{9,11},{10,... | collective-permute-start | bytes 393224 | tf_op jit(solution)/shard_map/ppermute | solution.py:386
  18.3 5.8 %copy-start.6 = (bf16[8,128,256]{2,1,0:T(8,128)(2,1)S(1)}, bf16[8,128,256]{2,1,0:T(8,128)(2,1)}, u32[]{:S(2)}) copy-start(bf16[8,128,256]{2,1,0:T(8,128)(2,1)} %constant.13.clone.refs_10_) | copy-start | bytes 1572868
  18.4 10.6 %collective-permute-start.4 = (bf16[2,128,256]{2,1,0:T(8,128)(2,1)S(1)}, bf16[2,128,256]{2,1,0:T(8,128)(2,1)S(1)}, u32[]{:S(2)}, u32[]{:S(2)}) collective-permute-start(bf16[2,128,256]{2,1,0:T(8,128)(2,1)S(1)} %get-tuple-element.68), channel_id=1, source_target_pairs={{0,4},{1,5},{2,6},{3,7},{4,0},{5,1},{6,2},{7,3},{8,12},{9,13},{10,... | collective-permute-start | bytes 393224 | tf_op jit(solution)/shard_map/ppermute | solution.py:386
  20.3 10.2 %collective-permute-start.5 = (bf16[2,128,256]{2,1,0:T(8,128)(2,1)S(1)}, bf16[2,128,256]{2,1,0:T(8,128)(2,1)S(1)}, u32[]{:S(2)}, u32[]{:S(2)}) collective-permute-start(bf16[2,128,256]{2,1,0:T(8,128)(2,1)S(1)} %get-tuple-element.73), channel_id=1, source_target_pairs={{0,6},{1,7},{2,4},{3,5},{4,2},{5,3},{6,0},{7,1},{8,14},{9,15},{10,... | collective-permute-start | bytes 393224 | tf_op jit(solution)/shard_map/ppermute | solution.py:386
  21.5 9.1 %collective-permute-start.6 = (bf16[2,128,256]{2,1,0:T(8,128)(2,1)S(1)}, bf16[2,128,256]{2,1,0:T(8,128)(2,1)S(1)}, u32[]{:S(2)}, u32[]{:S(2)}) collective-permute-start(bf16[2,128,256]{2,1,0:T(8,128)(2,1)S(1)} %get-tuple-element.74), channel_id=1, source_target_pairs={{0,3},{1,2},{2,1},{3,0},{4,7},{5,6},{6,5},{7,4},{8,11},{9,10},{10,... | collective-permute-start | bytes 393224 | tf_op jit(solution)/shard_map/ppermute | solution.py:386
  22.9 7.6 %collective-permute-start.7 = (bf16[2,128,256]{2,1,0:T(8,128)(2,1)S(1)}, bf16[2,128,256]{2,1,0:T(8,128)(2,1)S(1)}, u32[]{:S(2)}, u32[]{:S(2)}) collective-permute-start(bf16[2,128,256]{2,1,0:T(8,128)(2,1)S(1)} %get-tuple-element.75), channel_id=1, source_target_pairs={{0,5},{1,4},{2,7},{3,6},{4,1},{5,0},{6,3},{7,2},{8,13},{9,12},{10,... | collective-permute-start | bytes 393224 | tf_op jit(solution)/shard_map/ppermute | solution.py:386
  23.6 8.4 %collective-permute-start.8 = (bf16[2,128,256]{2,1,0:T(8,128)(2,1)S(1)}, bf16[2,128,256]{2,1,0:T(8,128)(2,1)S(1)}, u32[]{:S(2)}, u32[]{:S(2)}) collective-permute-start(bf16[2,128,256]{2,1,0:T(8,128)(2,1)S(1)} %get-tuple-element.76), channel_id=1, source_target_pairs={{0,7},{1,6},{2,5},{3,4},{4,3},{5,2},{6,1},{7,0},{8,15},{9,14},{10,... | collective-permute-start | bytes 393224 | tf_op jit(solution)/shard_map/ppermute | solution.py:386
  29.0 12.8 %collective-permute-start.21 = (bf16[2,256,256]{2,1,0:T(8,128)(2,1)S(1)}, bf16[2,256,256]{2,1,0:T(8,128)(2,1)S(1)}, u32[]{:S(2)}, u32[]{:S(2)}) collective-permute-start(bf16[2,256,256]{2,1,0:T(8,128)(2,1)S(1)} %get-tuple-element.108), channel_id=1, source_target_pairs={{0,8},{8,0},{16,24},{24,16},{1,9},{9,1},{17,25},{25,17},{2,10},{10... | collective-permute-start | bytes 786440 | tf_op jit(solution)/shard_map/ppermute | solution.py:347
  31.9 25.2 %copy-start.7 = (f32[4096]{0:T(1024)S(1)}, f32[4096]{0:T(1024)}, u32[]{:S(2)}) copy-start(f32[4096]{0:T(1024)} %param.13) | copy-start | bytes 49156
  36.7 10.1 %collective-permute-start.16 = (bf16[2,2,128,256]{3,2,1,0:T(8,128)(2,1)S(1)}, bf16[2,2,128,256]{3,2,1,0:T(8,128)(2,1)S(1)}, u32[]{:S(2)}, u32[]{:S(2)}) collective-permute-start(bf16[2,2,128,256]{3,2,1,0:T(8,128)(2,1)S(1)} %get-tuple-element.94), channel_id=1, source_target_pairs={{0,6},{1,7},{2,4},{3,5},{4,2},{5,3},{6,0},{7,1},{8,14},{9,15},{10,... | collective-permute-start | bytes 786440 | tf_op jit(solution)/shard_map/ppermute | solution.py:386
  39.1 7.7 %collective-permute-start.17 = (bf16[2,2,128,256]{3,2,1,0:T(8,128)(2,1)S(1)}, bf16[2,2,128,256]{3,2,1,0:T(8,128)(2,1)S(1)}, u32[]{:S(2)}, u32[]{:S(2)}) collective-permute-start(bf16[2,2,128,256]{3,2,1,0:T(8,128)(2,1)S(1)} %get-tuple-element.95), channel_id=1, source_target_pairs={{0,1},{1,0},{2,3},{3,2},{4,5},{5,4},{6,7},{7,6},{8,9},{9,8},{10,11... | collective-permute-start | bytes 786440 | tf_op jit(solution)/shard_map/ppermute | solution.py:386
  39.6 9.9 %collective-permute-start.22 = (bf16[2,256,256]{2,1,0:T(8,128)(2,1)S(1)}, bf16[2,256,256]{2,1,0:T(8,128)(2,1)S(1)}, u32[]{:S(2)}, u32[]{:S(2)}) collective-permute-start(bf16[2,256,256]{2,1,0:T(8,128)(2,1)S(1)} %get-tuple-element.110), channel_id=1, source_target_pairs={{0,8},{8,0},{16,24},{24,16},{1,9},{9,1},{17,25},{25,17},{2,10},{10... | collective-permute-start | bytes 786440 | tf_op jit(solution)/shard_map/ppermute | solution.py:347
  40.8 12.3 %collective-permute-start.18 = (bf16[2,2,128,256]{3,2,1,0:T(8,128)(2,1)S(1)}, bf16[2,2,128,256]{3,2,1,0:T(8,128)(2,1)S(1)}, u32[]{:S(2)}, u32[]{:S(2)}) collective-permute-start(bf16[2,2,128,256]{3,2,1,0:T(8,128)(2,1)S(1)} %get-tuple-element.96), channel_id=1, source_target_pairs={{0,2},{1,3},{2,0},{3,1},{4,6},{5,7},{6,4},{7,5},{8,10},{9,11},{10,... | collective-permute-start | bytes 786440 | tf_op jit(solution)/shard_map/ppermute | solution.py:386
  41.8 13.8 %collective-permute-start.19 = (bf16[2,2,128,256]{3,2,1,0:T(8,128)(2,1)S(1)}, bf16[2,2,128,256]{3,2,1,0:T(8,128)(2,1)S(1)}, u32[]{:S(2)}, u32[]{:S(2)}) collective-permute-start(bf16[2,2,128,256]{3,2,1,0:T(8,128)(2,1)S(1)} %get-tuple-element.97), channel_id=1, source_target_pairs={{0,4},{1,5},{2,6},{3,7},{4,0},{5,1},{6,2},{7,3},{8,12},{9,13},{10,... | collective-permute-start | bytes 786440 | tf_op jit(solution)/shard_map/ppermute | solution.py:386
  46.8 10.3 %collective-permute-start.20 = (bf16[2,2,128,256]{3,2,1,0:T(8,128)(2,1)S(1)}, bf16[2,2,128,256]{3,2,1,0:T(8,128)(2,1)S(1)}, u32[]{:S(2)}, u32[]{:S(2)}) collective-permute-start(bf16[2,2,128,256]{3,2,1,0:T(8,128)(2,1)S(1)} %get-tuple-element.98), channel_id=1, source_target_pairs={{0,3},{1,2},{2,1},{3,0},{4,7},{5,6},{6,5},{7,4},{8,11},{9,10},{10,... | collective-permute-start | bytes 786440 | tf_op jit(solution)/shard_map/ppermute | solution.py:386
  46.8 14.7 %collective-permute-start.14 = (bf16[2,2,128,256]{3,2,1,0:T(8,128)(2,1)S(1)}, bf16[2,2,128,256]{3,2,1,0:T(8,128)(2,1)S(1)}, u32[]{:S(2)}, u32[]{:S(2)}) collective-permute-start(bf16[2,2,128,256]{3,2,1,0:T(8,128)(2,1)S(1)} %get-tuple-element.91), channel_id=1, source_target_pairs={{0,5},{1,4},{2,7},{3,6},{4,1},{5,0},{6,3},{7,2},{8,13},{9,12},{10,... | collective-permute-start | bytes 786440 | tf_op jit(solution)/shard_map/ppermute | solution.py:386
  49.5 13.3 %collective-permute-start.15 = (bf16[2,2,128,256]{3,2,1,0:T(8,128)(2,1)S(1)}, bf16[2,2,128,256]{3,2,1,0:T(8,128)(2,1)S(1)}, u32[]{:S(2)}, u32[]{:S(2)}) collective-permute-start(bf16[2,2,128,256]{3,2,1,0:T(8,128)(2,1)S(1)} %get-tuple-element.92), channel_id=1, source_target_pairs={{0,7},{1,6},{2,5},{3,4},{4,3},{5,2},{6,1},{7,0},{8,15},{9,14},{10,... | collective-permute-start | bytes 786440 | tf_op jit(solution)/shard_map/ppermute | solution.py:386
  53.1 13.2 %collective-permute-start.23 = (bf16[1,256,512]{2,1,0:T(8,128)(2,1)S(1)}, bf16[1,256,512]{2,1,0:T(8,128)(2,1)S(1)}, u32[]{:S(2)}, u32[]{:S(2)}) collective-permute-start(bf16[1,256,512]{2,1,0:T(8,128)(2,1)S(1)} %get-tuple-element.112), channel_id=1, source_target_pairs={{0,16},{8,24},{16,0},{24,8},{1,17},{9,25},{17,1},{25,9},{2,18},{10... | collective-permute-start | bytes 786440 | tf_op jit(solution)/shard_map/ppermute | solution.py:347

commit v16 on v15

--- a/solution.py
+++ b/solution.py
@@ -223,7 +223,7 @@
                     y[o, c, im, lanes] = z[c][1].astype(BF16)
         return carry
 
-    lax.fori_loop(0, CLASSES, middle, 0)
+    lax.fori_loop(0, CLASSES, middle, 0, unroll=2)
 
     for c in range(CLASSES):
         grad[c] = dot(back[c], y[2, c])

time: 67.5 us -> 67.5 us (level)
  transfers between devices with their start and end apart: 24 -> 24, of which waited for: 8 -> 8; matrix products, arithmetic and copies ran while one was open for 0% -> 0% of each run, Pallas kernels for 32% -> 31%
where the time goes in v16:
time: 67.5 us; the launch traced here: 67.3 us
  starting transfers between devices  28 us (41%)
  Pallas kernels  24.9 us (37%)
  waiting for transfers between devices  13.6 us (20%)
  between operations  0.8 us (1%)
    ppermute x21, starting transfers between devices, exchange(): lax.ppermute(block, 'ctx', [(i, i ^ j) for i in range(n)])  22.7 us
    ppermute x21, waiting for transfers between devices, exchange(): lax.ppermute(block, 'ctx', [(i, i ^ j) for i in range(n)])  12.8 us
    pallas_call x2, Pallas kernels, conv(): pl.pallas_call(functools.partial(conv_kernel, n, d, half), in_specs=[SMEM...  9.42 us
    pallas_call x2, Pallas kernels, gate(): pl.pallas_call(functools.partial(gate_kernel, js), in_specs=[SMEM] + [VME...  7.17 us
    ppermute x3, starting transfers between devices, trade(): return resident(lax.ppermute(send, 'dp', [(i, i ^ bit) for i in range(d)]))  5.27 us
    pallas_call x2, Pallas kernels, filter_spectrum(): pl.pallas_call(functools.partial(filter_kernel, half), in_specs=[VMEM] *...  3.6 us
    pallas_call x2, Pallas kernels, products(): pl.pallas_call(functools.partial(second_kernel if half else first_kernel,...  3.53 us
  transfers between devices with their start and end apart: 24, of which 8 were waited for; matrix products, arithmetic and copies ran while one was open for 0% of the time, Pallas kernels for 31%

profile of v16, /device:TPU:0, one launch (start us, length us, event | category | flops | bytes accessed | tf_op | source)
XLA Modules:
  0.0 67.3 jit_solution(6937454690979777825)
XLA Ops:
  0.7 2.7 %products.2 = (bf16[2,128,256]{2,1,0:T(8,128)(2,1)S(1)}, bf16[2,128,256]{2,1,0:T(8,128)(2,1)S(1)}, bf16[2,128,256]{2,1,0:T(8,128)(2,1)S(1)}, bf16[2,128,256]{2,1...) custom-call(s32[2]{0:T(128)S(1)} %pad_add_fusion.me, ...), custom_call_target="tpu_custom_call" | custom-call | tf_op jit(solution)/shard_map/products/pallas_call | solution.py:133
  4.0 2.6 %collective-permute-start.1 = (bf16[2,128,256]{2,1,0:T(8,128)(2,1)S(1)}, bf16[2,128,256]{2,1,0:T(8,128)(2,1)S(1)}, u32[]{:S(2)}, u32[]{:S(2)}) collective-permute-start(bf16[2,128,256]{2,1,0:T(8,128)(2,1)S(1)} %get-tuple-element.60), channel_id=1, source_target_pairs={{0,2},{1,3},{2,0},{3,1},{4,6},{5,7},{6,4},{7,5},{8,10},{9,11},{10,... | collective-permute-start | bytes 393224 | tf_op jit(solution)/shard_map/ppermute | solution.py:386
  6.5 1.5 %collective-permute-start.9 = (bf16[2,128,256]{2,1,0:T(8,128)(2,1)S(1)}, bf16[2,128,256]{2,1,0:T(8,128)(2,1)S(1)}, u32[]{:S(2)}, u32[]{:S(2)}) collective-permute-start(bf16[2,128,256]{2,1,0:T(8,128)(2,1)S(1)} %get-tuple-element.78), channel_id=1, source_target_pairs={{0,4},{1,5},{2,6},{3,7},{4,0},{5,1},{6,2},{7,3},{8,12},{9,13},{10,... | collective-permute-start | bytes 393224 | tf_op jit(solution)/shard_map/ppermute | solution.py:386
  8.1 1.2 %collective-permute-start.11 = (bf16[2,128,256]{2,1,0:T(8,128)(2,1)S(1)}, bf16[2,128,256]{2,1,0:T(8,128)(2,1)S(1)}, u32[]{:S(2)}, u32[]{:S(2)}) collective-permute-start(bf16[2,128,256]{2,1,0:T(8,128)(2,1)S(1)} %get-tuple-element.80), channel_id=1, source_target_pairs={{0,3},{1,2},{2,1},{3,0},{4,7},{5,6},{6,5},{7,4},{8,11},{9,10},{10,... | collective-permute-start | bytes 393224 | tf_op jit(solution)/shard_map/ppermute | solution.py:386
  9.2 2.0 %collective-permute-start.12 = (bf16[2,128,256]{2,1,0:T(8,128)(2,1)S(1)}, bf16[2,128,256]{2,1,0:T(8,128)(2,1)S(1)}, u32[]{:S(2)}, u32[]{:S(2)}) collective-permute-start(bf16[2,128,256]{2,1,0:T(8,128)(2,1)S(1)} %get-tuple-element.81), channel_id=1, source_target_pairs={{0,5},{1,4},{2,7},{3,6},{4,1},{5,0},{6,3},{7,2},{8,13},{9,12},{10,... | collective-permute-start | bytes 393224 | tf_op jit(solution)/shard_map/ppermute | solution.py:386
  11.3 0.8 %products.3 = (bf16[2,128,256]{2,1,0:T(8,128)(2,1)S(1)}, bf16[2,128,256]{2,1,0:T(8,128)(2,1)S(1)}, bf16[2,128,256]{2,1,0:T(8,128)(2,1)S(1)}, bf16[2,128,256]{2,1...) custom-call(s32[2]{0:T(128)S(1)} %pad_add_fusion.me, ...), custom_call_target="tpu_custom_call" | custom-call | tf_op jit(solution)/shard_map/products/pallas_call | solution.py:133
  12.6 1.9 %filter_spectrum.2.refs_0_.refs_8_ = f32[8,256,256]{2,1,0:T(8,128)S(1)} custom-call(f32[512,1024]{1,0:T(8,128)S(1)} %copy-done.5, bf16[8,256,256]{2,1,0:T(8,128)(2,1)S(1)} %copy-done.4, bf16[2,128,256]{2,1,0:T(8,128)(2,1)S(1)} %collective-permute-done.refs_0_.refs_1_, bf16[2,128,256]{2,1,0:T(8,128)(2,1)S(1)} %collective-permute-done.1.refs_1_.refs_2_), custom_call_target="tpu_custom_call" | custom-call | tf_op jit(solution)/shard_map/filter_spectrum/pallas_call | solution.py:176
  14.6 1.3 %collective-permute-start.2 = (bf16[2,128,256]{2,1,0:T(8,128)(2,1)S(1)}, bf16[2,128,256]{2,1,0:T(8,128)(2,1)S(1)}, u32[]{:S(2)}, u32[]{:S(2)}) collective-permute-start(bf16[2,128,256]{2,1,0:T(8,128)(2,1)S(1)} %get-tuple-element.66), channel_id=1, source_target_pairs={{0,1},{1,0},{2,3},{3,2},{4,5},{5,4},{6,7},{7,6},{8,9},{9,8},{10,11... | collective-permute-start | bytes 393224 | tf_op jit(solution)/shard_map/ppermute | solution.py:386
  15.9 0.7 %collective-permute-start.3 = (bf16[2,128,256]{2,1,0:T(8,128)(2,1)S(1)}, bf16[2,128,256]{2,1,0:T(8,128)(2,1)S(1)}, u32[]{:S(2)}, u32[]{:S(2)}) collective-permute-start(bf16[2,128,256]{2,1,0:T(8,128)(2,1)S(1)} %get-tuple-element.67), channel_id=1, source_target_pairs={{0,2},{1,3},{2,0},{3,1},{4,6},{5,7},{6,4},{7,5},{8,10},{9,11},{10,... | collective-permute-start | bytes 393224 | tf_op jit(solution)/shard_map/ppermute | solution.py:386
  16.6 1.7 %filter_spectrum.3.refs_0_.refs_8_ = f32[8,256,256]{2,1,0:T(8,128)S(1)} custom-call(f32[512,1024]{1,0:T(8,128)S(1)} %copy-done.5, bf16[8,256,256]{2,1,0:T(8,128)(2,1)S(1)} %copy-done.4, f32[8,256,256]{2,1,0:T(8,128)S(1)} %filter_spectrum.2.refs_0_.refs_8_), custom_call_target="tpu_custom_call" | custom-call | tf_op jit(solution)/shard_map/filter_spectrum/pallas_call | solution.py:176
  18.4 1.2 %collective-permute-start.4 = (bf16[2,128,256]{2,1,0:T(8,128)(2,1)S(1)}, bf16[2,128,256]{2,1,0:T(8,128)(2,1)S(1)}, u32[]{:S(2)}, u32[]{:S(2)}) collective-permute-start(bf16[2,128,256]{2,1,0:T(8,128)(2,1)S(1)} %get-tuple-element.68), channel_id=1, source_target_pairs={{0,4},{1,5},{2,6},{3,7},{4,0},{5,1},{6,2},{7,3},{8,12},{9,13},{10,... | collective-permute-start | bytes 393224 | tf_op jit(solution)/shard_map/ppermute | solution.py:386
  19.6 0.7 %collective-permute-done.12.refs_6_ = bf16[2,128,256]{2,1,0:T(8,128)(2,1)S(1)} collective-permute-done((bf16[2,128,256]{2,1,0:T(8,128)(2,1)S(1)}, bf16[2,128,256]{2,1,0:T(8,128)(2,1)S(1)}, u32[]{:S(2)}, u32[]{:S(2)}) %collective-permute-start.12) | collective-permute-done | bytes 131104 | tf_op jit(solution)/shard_map/ppermute | solution.py:386
  20.3 1.1 %collective-permute-start.5 = (bf16[2,128,256]{2,1,0:T(8,128)(2,1)S(1)}, bf16[2,128,256]{2,1,0:T(8,128)(2,1)S(1)}, u32[]{:S(2)}, u32[]{:S(2)}) collective-permute-start(bf16[2,128,256]{2,1,0:T(8,128)(2,1)S(1)} %get-tuple-element.73), channel_id=1, source_target_pairs={{0,6},{1,7},{2,4},{3,5},{4,2},{5,3},{6,0},{7,1},{8,14},{9,15},{10,... | collective-permute-start | bytes 393224 | tf_op jit(solution)/shard_map/ppermute | solution.py:386
  21.5 1.5 %collective-permute-start.6 = (bf16[2,128,256]{2,1,0:T(8,128)(2,1)S(1)}, bf16[2,128,256]{2,1,0:T(8,128)(2,1)S(1)}, u32[]{:S(2)}, u32[]{:S(2)}) collective-permute-start(bf16[2,128,256]{2,1,0:T(8,128)(2,1)S(1)} %get-tuple-element.74), channel_id=1, source_target_pairs={{0,3},{1,2},{2,1},{3,0},{4,7},{5,6},{6,5},{7,4},{8,11},{9,10},{10,... | collective-permute-start | bytes 393224 | tf_op jit(solution)/shard_map/ppermute | solution.py:386
  24.2 4.7 %conv.2 = (bf16[2,2,128,256]{3,2,1,0:T(8,128)(2,1)S(1)}, bf16[2,2,128,256]{3,2,1,0:T(8,128)(2,1)S(1)}, bf16[2,2,128,256]{3,2,1,0:T(8,128)(2,1)S(1)}, bf16[2,2,12...) custom-call(s32[2]{0:T(128)S(1)} %pad_add_fusion.me, ...), custom_call_target="tpu_custom_call" | custom-call | tf_op jit(solution)/shard_map/conv/pallas_call | solution.py:251
  28.9 1.6 %collective-permute-start.21 = (bf16[2,256,256]{2,1,0:T(8,128)(2,1)S(1)}, bf16[2,256,256]{2,1,0:T(8,128)(2,1)S(1)}, u32[]{:S(2)}, u32[]{:S(2)}) collective-permute-start(bf16[2,256,256]{2,1,0:T(8,128)(2,1)S(1)} %get-tuple-element.108), channel_id=1, source_target_pairs={{0,8},{8,0},{16,24},{24,16},{1,9},{9,1},{17,25},{25,17},{2,10},{10... | collective-permute-start | bytes 786440 | tf_op jit(solution)/shard_map/ppermute | solution.py:347
  30.5 1.4 %collective-permute-done.8.refs_7_ = bf16[2,128,256]{2,1,0:T(8,128)(2,1)S(1)} collective-permute-done((bf16[2,128,256]{2,1,0:T(8,128)(2,1)S(1)}, bf16[2,128,256]{2,1,0:T(8,128)(2,1)S(1)}, u32[]{:S(2)}, u32[]{:S(2)}) %collective-permute-start.8) | collective-permute-done | bytes 131104 | tf_op jit(solution)/shard_map/ppermute | solution.py:386
  31.9 4.7 %conv.3 = (bf16[2,2,128,256]{3,2,1,0:T(8,128)(2,1)S(1)}, bf16[2,2,128,256]{3,2,1,0:T(8,128)(2,1)S(1)}, bf16[2,2,128,256]{3,2,1,0:T(8,128)(2,1)S(1)}, bf16[2,2,12...) custom-call(s32[2]{0:T(128)S(1)} %pad_add_fusion.me, ...), custom_call_target="tpu_custom_call", output_to_operand_aliasing={{0}: (12, {}), {1}: (13, {}), {2}: (14, {}), {3}: (15, {}),... | custom-call | tf_op jit(solution)/shard_map/conv/pallas_call | solution.py:251
  36.6 2.4 %collective-permute-start.16 = (bf16[2,2,128,256]{3,2,1,0:T(8,128)(2,1)S(1)}, bf16[2,2,128,256]{3,2,1,0:T(8,128)(2,1)S(1)}, u32[]{:S(2)}, u32[]{:S(2)}) collective-permute-start(bf16[2,2,128,256]{3,2,1,0:T(8,128)(2,1)S(1)} %get-tuple-element.94), channel_id=1, source_target_pairs={{0,6},{1,7},{2,4},{3,5},{4,2},{5,3},{6,0},{7,1},{8,14},{9,15},{10,... | collective-permute-start | bytes 786440 | tf_op jit(solution)/shard_map/ppermute | solution.py:386
  39.6 1.2 %collective-permute-start.22 = (bf16[2,256,256]{2,1,0:T(8,128)(2,1)S(1)}, bf16[2,256,256]{2,1,0:T(8,128)(2,1)S(1)}, u32[]{:S(2)}, u32[]{:S(2)}) collective-permute-start(bf16[2,256,256]{2,1,0:T(8,128)(2,1)S(1)} %get-tuple-element.110), channel_id=1, source_target_pairs={{0,8},{8,0},{16,24},{24,16},{1,9},{9,1},{17,25},{25,17},{2,10},{10... | collective-permute-start | bytes 786440 | tf_op jit(solution)/shard_map/ppermute | solution.py:347
  40.7 1.0 %collective-permute-start.18 = (bf16[2,2,128,256]{3,2,1,0:T(8,128)(2,1)S(1)}, bf16[2,2,128,256]{3,2,1,0:T(8,128)(2,1)S(1)}, u32[]{:S(2)}, u32[]{:S(2)}) collective-permute-start(bf16[2,2,128,256]{3,2,1,0:T(8,128)(2,1)S(1)} %get-tuple-element.96), channel_id=1, source_target_pairs={{0,2},{1,3},{2,0},{3,1},{4,6},{5,7},{6,4},{7,5},{8,10},{9,11},{10,... | collective-permute-start | bytes 786440 | tf_op jit(solution)/shard_map/ppermute | solution.py:386
  41.7 5.0 %collective-permute-done.16.refs_1_ = bf16[2,2,128,256]{3,2,1,0:T(8,128)(2,1)S(1)} collective-permute-done((bf16[2,2,128,256]{3,2,1,0:T(8,128)(2,1)S(1)}, bf16[2,2,128,256]{3,2,1,0:T(8,128)(2,1)S(1)}, u32[]{:S(2)}, u32[]{:S(2)}) %collective-permute-start.16) | collective-permute-done | bytes 262176 | tf_op jit(solution)/shard_map/ppermute | solution.py:386
  46.7 2.7 %collective-permute-start.14 = (bf16[2,2,128,256]{3,2,1,0:T(8,128)(2,1)S(1)}, bf16[2,2,128,256]{3,2,1,0:T(8,128)(2,1)S(1)}, u32[]{:S(2)}, u32[]{:S(2)}) collective-permute-start(bf16[2,2,128,256]{3,2,1,0:T(8,128)(2,1)S(1)} %get-tuple-element.91), channel_id=1, source_target_pairs={{0,5},{1,4},{2,7},{3,6},{4,1},{5,0},{6,3},{7,2},{8,13},{9,12},{10,... | collective-permute-start | bytes 786440 | tf_op jit(solution)/shard_map/ppermute | solution.py:386
  49.4 0.8 %collective-permute-start.15 = (bf16[2,2,128,256]{3,2,1,0:T(8,128)(2,1)S(1)}, bf16[2,2,128,256]{3,2,1,0:T(8,128)(2,1)S(1)}, u32[]{:S(2)}, u32[]{:S(2)}) collective-permute-start(bf16[2,2,128,256]{3,2,1,0:T(8,128)(2,1)S(1)} %get-tuple-element.92), channel_id=1, source_target_pairs={{0,7},{1,6},{2,5},{3,4},{4,3},{5,2},{6,1},{7,0},{8,15},{9,14},{10,... | collective-permute-start | bytes 786440 | tf_op jit(solution)/shard_map/ppermute | solution.py:386
  50.3 2.8 %collective-permute-done.18.refs_3_ = bf16[2,2,128,256]{3,2,1,0:T(8,128)(2,1)S(1)} collective-permute-done((bf16[2,2,128,256]{3,2,1,0:T(8,128)(2,1)S(1)}, bf16[2,2,128,256]{3,2,1,0:T(8,128)(2,1)S(1)}, u32[]{:S(2)}, u32[]{:S(2)}) %collective-permute-start.18) | collective-permute-done | bytes 262176 | tf_op jit(solution)/shard_map/ppermute | solution.py:386
  53.1 2.5 %collective-permute-start.23 = (bf16[1,256,512]{2,1,0:T(8,128)(2,1)S(1)}, bf16[1,256,512]{2,1,0:T(8,128)(2,1)S(1)}, u32[]{:S(2)}, u32[]{:S(2)}) collective-permute-start(bf16[1,256,512]{2,1,0:T(8,128)(2,1)S(1)} %get-tuple-element.112), channel_id=1, source_target_pairs={{0,16},{8,24},{16,0},{24,8},{1,17},{9,25},{17,1},{25,9},{2,18},{10... | collective-permute-start | bytes 786440 | tf_op jit(solution)/shard_map/ppermute | solution.py:347
  55.6 1.5 %collective-permute-done.20.refs_5_ = bf16[2,2,128,256]{3,2,1,0:T(8,128)(2,1)S(1)} collective-permute-done((bf16[2,2,128,256]{3,2,1,0:T(8,128)(2,1)S(1)}, bf16[2,2,128,256]{3,2,1,0:T(8,128)(2,1)S(1)}, u32[]{:S(2)}, u32[]{:S(2)}) %collective-permute-start.20) | collective-permute-done | bytes 262176 | tf_op jit(solution)/shard_map/ppermute | solution.py:386
  57.0 4.4 %gate.2 = (bf16[128,4096]{1,0:T(8,128)(2,1)}, bf16[128,4096]{1,0:T(8,128)(2,1)}, bf16[128,4096]{1,0:T(8,128)(2,1)}, bf16[128,4096]{1,0:T(8,128)(2,1)}, f32[8,128]{1,0:T(8,128)}) custom-call(s32[2]{0:T(128)S(1)} %pad_add_fusion.me, bf16[128,4096]{1,0:T(8,128)(2,1)S(1)} %bitcast.13, bf16[128,4096]{1,0:T(8,128)(2,1)S(1)} %bitcast.17, ...), custom_call_target="tpu_custom_call" | custom-call | tf_op jit(solution)/shard_map/gate/pallas_call | solution.py:313
  61.5 1.3 %collective-permute-done.15.refs_1_ = bf16[2,2,128,256]{3,2,1,0:T(8,128)(2,1)S(1)} collective-permute-done((bf16[2,2,128,256]{3,2,1,0:T(8,128)(2,1)S(1)}, bf16[2,2,128,256]{3,2,1,0:T(8,128)(2,1)S(1)}, u32[]{:S(2)}, u32[]{:S(2)}) %collective-permute-start.15) | collective-permute-done | bytes 262176 | tf_op jit(solution)/shard_map/ppermute | solution.py:386
  62.8 2.7 %gate.3 = (bf16[128,4096]{1,0:T(8,128)(2,1)}, bf16[128,4096]{1,0:T(8,128)(2,1)}, bf16[128,4096]{1,0:T(8,128)(2,1)}, bf16[128,4096]{1,0:T(8,128)(2,1)}, f32[8,128]{1,0:T(8,128)}) custom-call(s32[2]{0:T(128)S(1)} %pad_add_fusion.me, bf16[128,4096]{1,0:T(8,128)(2,1)S(1)} %bitcast.14, ...), custom_call_target="tpu_custom_call", output_to_operand_aliasing={{0}: (8, {}), {1}: (9, {}), {2}: (10, {}), {3}: (11, {})} | custom-call | tf_op jit(solution)/shard_map/gate/pallas_call | solution.py:313
  65.5 0.7 %collective-permute-done.23.got = bf16[1,256,512]{2,1,0:T(8,128)(2,1)S(1)} collective-permute-done((bf16[1,256,512]{2,1,0:T(8,128)(2,1)S(1)}, bf16[1,256,512]{2,1,0:T(8,128)(2,1)S(1)}, u32[]{:S(2)}, u32[]{:S(2)}) %collective-permute-start.23) | collective-permute-done | bytes 262176 | tf_op jit(solution)/shard_map/ppermute | solution.py:347
  66.3 1.1 %turn_grads.1 = f32[512,256]{1,0:T(8,128)} custom-call(f32[1,256,512]{2,1,0:T(8,128)S(1)} %get-tuple-element.111.keep, bf16[1,256,512]{2,1,0:T(8,128)(2,1)S(1)} %collective-permute-done.23.got), custom_call_target="tpu_custom_call" | custom-call | tf_op jit(solution)/shard_map/turn_grads/pallas_call | solution.py:365
  (45 shorter events, 3.1 us)
Async XLA Ops:
  0.7 10.5 %copy-start = (bf16[1,128,4096]{2,1,0:T(8,128)(2,1)S(1)}, bf16[1,128,4096]{2,1,0:T(8,128)(2,1)}, u32[]{:S(2)}) copy-start(bf16[1,128,4096]{2,1,0:T(8,128)(2,1)} %param.8) | copy-start | bytes 3145732
  0.7 10.5 %copy-start.1 = (bf16[1,128,4096]{2,1,0:T(8,128)(2,1)S(1)}, bf16[1,128,4096]{2,1,0:T(8,128)(2,1)}, u32[]{:S(2)}) copy-start(bf16[1,128,4096]{2,1,0:T(8,128)(2,1)} %param.11) | copy-start | bytes 3145732
  0.7 10.5 %copy-start.2 = (bf16[1,128,4096]{2,1,0:T(8,128)(2,1)S(1)}, bf16[1,128,4096]{2,1,0:T(8,128)(2,1)}, u32[]{:S(2)}) copy-start(bf16[1,128,4096]{2,1,0:T(8,128)(2,1)} %param.10) | copy-start | bytes 3145732
  0.7 10.5 %copy-start.3 = (bf16[1,128,4096]{2,1,0:T(8,128)(2,1)S(1)}, bf16[1,128,4096]{2,1,0:T(8,128)(2,1)}, u32[]{:S(2)}) copy-start(bf16[1,128,4096]{2,1,0:T(8,128)(2,1)} %param.9) | copy-start | bytes 3145732
  3.4 5.8 %collective-permute-start = (bf16[2,128,256]{2,1,0:T(8,128)(2,1)S(1)}, bf16[2,128,256]{2,1,0:T(8,128)(2,1)S(1)}, u32[]{:S(2)}, u32[]{:S(2)}) collective-permute-start(bf16[2,128,256]{2,1,0:T(8,128)(2,1)S(1)} %get-tuple-element.59), channel_id=1, source_target_pairs={{0,1},{1,0},{2,3},{3,2},{4,5},{5,4},{6,7},{7,6},{8,9},{9,8},{10,11... | collective-permute-start | bytes 393224 | tf_op jit(solution)/shard_map/ppermute | solution.py:386
  4.0 8.2 %collective-permute-start.1 = (bf16[2,128,256]{2,1,0:T(8,128)(2,1)S(1)}, bf16[2,128,256]{2,1,0:T(8,128)(2,1)S(1)}, u32[]{:S(2)}, u32[]{:S(2)}) collective-permute-start(bf16[2,128,256]{2,1,0:T(8,128)(2,1)S(1)} %get-tuple-element.60), channel_id=1, source_target_pairs={{0,2},{1,3},{2,0},{3,1},{4,6},{5,7},{6,4},{7,5},{8,10},{9,11},{10,... | collective-permute-start | bytes 393224 | tf_op jit(solution)/shard_map/ppermute | solution.py:386
  6.5 8.1 %collective-permute-start.9 = (bf16[2,128,256]{2,1,0:T(8,128)(2,1)S(1)}, bf16[2,128,256]{2,1,0:T(8,128)(2,1)S(1)}, u32[]{:S(2)}, u32[]{:S(2)}) collective-permute-start(bf16[2,128,256]{2,1,0:T(8,128)(2,1)S(1)} %get-tuple-element.78), channel_id=1, source_target_pairs={{0,4},{1,5},{2,6},{3,7},{4,0},{5,1},{6,2},{7,3},{8,12},{9,13},{10,... | collective-permute-start | bytes 393224 | tf_op jit(solution)/shard_map/ppermute | solution.py:386
  8.0 7.8 %collective-permute-start.10 = (bf16[2,128,256]{2,1,0:T(8,128)(2,1)S(1)}, bf16[2,128,256]{2,1,0:T(8,128)(2,1)S(1)}, u32[]{:S(2)}, u32[]{:S(2)}) collective-permute-start(bf16[2,128,256]{2,1,0:T(8,128)(2,1)S(1)} %get-tuple-element.79), channel_id=1, source_target_pairs={{0,6},{1,7},{2,4},{3,5},{4,2},{5,3},{6,0},{7,1},{8,14},{9,15},{10,... | collective-permute-start | bytes 393224 | tf_op jit(solution)/shard_map/ppermute | solution.py:386
  8.1 10.3 %collective-permute-start.11 = (bf16[2,128,256]{2,1,0:T(8,128)(2,1)S(1)}, bf16[2,128,256]{2,1,0:T(8,128)(2,1)S(1)}, u32[]{:S(2)}, u32[]{:S(2)}) collective-permute-start(bf16[2,128,256]{2,1,0:T(8,128)(2,1)S(1)} %get-tuple-element.80), channel_id=1, source_target_pairs={{0,3},{1,2},{2,1},{3,0},{4,7},{5,6},{6,5},{7,4},{8,11},{9,10},{10,... | collective-permute-start | bytes 393224 | tf_op jit(solution)/shard_map/ppermute | solution.py:386
  9.2 3.4 %copy-start.4 = (bf16[8,256,256]{2,1,0:T(8,128)(2,1)S(1)}, bf16[8,256,256]{2,1,0:T(8,128)(2,1)}, u32[]{:S(2)}) copy-start(bf16[8,256,256]{2,1,0:T(8,128)(2,1)} %constant.12.clone.fwd.refs_9_) | copy-start | bytes 3145732
  9.2 3.4 %copy-start.5 = (f32[512,1024]{1,0:T(8,128)S(1)}, f32[512,1024]{1,0:T(8,128)}, u32[]{:S(2)}) copy-start(f32[512,1024]{1,0:T(8,128)} %filt.3) | copy-start | bytes 6291460
  9.2 11.1 %collective-permute-start.12 = (bf16[2,128,256]{2,1,0:T(8,128)(2,1)S(1)}, bf16[2,128,256]{2,1,0:T(8,128)(2,1)S(1)}, u32[]{:S(2)}, u32[]{:S(2)}) collective-permute-start(bf16[2,128,256]{2,1,0:T(8,128)(2,1)S(1)} %get-tuple-element.81), channel_id=1, source_target_pairs={{0,5},{1,4},{2,7},{3,6},{4,1},{5,0},{6,3},{7,2},{8,13},{9,12},{10,... | collective-permute-start | bytes 393224 | tf_op jit(solution)/shard_map/ppermute | solution.py:386
  12.1 9.4 %collective-permute-start.13 = (bf16[2,128,256]{2,1,0:T(8,128)(2,1)S(1)}, bf16[2,128,256]{2,1,0:T(8,128)(2,1)S(1)}, u32[]{:S(2)}, u32[]{:S(2)}) collective-permute-start(bf16[2,128,256]{2,1,0:T(8,128)(2,1)S(1)} %get-tuple-element.82), channel_id=1, source_target_pairs={{0,7},{1,6},{2,5},{3,4},{4,3},{5,2},{6,1},{7,0},{8,15},{9,14},{10,... | collective-permute-start | bytes 393224 | tf_op jit(solution)/shard_map/ppermute | solution.py:386
  14.6 8.3 %collective-permute-start.2 = (bf16[2,128,256]{2,1,0:T(8,128)(2,1)S(1)}, bf16[2,128,256]{2,1,0:T(8,128)(2,1)S(1)}, u32[]{:S(2)}, u32[]{:S(2)}) collective-permute-start(bf16[2,128,256]{2,1,0:T(8,128)(2,1)S(1)} %get-tuple-element.66), channel_id=1, source_target_pairs={{0,1},{1,0},{2,3},{3,2},{4,5},{5,4},{6,7},{7,6},{8,9},{9,8},{10,11... | collective-permute-start | bytes 393224 | tf_op jit(solution)/shard_map/ppermute | solution.py:386
  15.9 7.7 %collective-permute-start.3 = (bf16[2,128,256]{2,1,0:T(8,128)(2,1)S(1)}, bf16[2,128,256]{2,1,0:T(8,128)(2,1)S(1)}, u32[]{:S(2)}, u32[]{:S(2)}) collective-permute-start(bf16[2,128,256]{2,1,0:T(8,128)(2,1)S(1)} %get-tuple-element.67), channel_id=1, source_target_pairs={{0,2},{1,3},{2,0},{3,1},{4,6},{5,7},{6,4},{7,5},{8,10},{9,11},{10,... | collective-permute-start | bytes 393224 | tf_op jit(solution)/shard_map/ppermute | solution.py:386
  18.3 5.8 %copy-start.6 = (bf16[8,128,256]{2,1,0:T(8,128)(2,1)S(1)}, bf16[8,128,256]{2,1,0:T(8,128)(2,1)}, u32[]{:S(2)}) copy-start(bf16[8,128,256]{2,1,0:T(8,128)(2,1)} %constant.13.clone.refs_10_) | copy-start | bytes 1572868
  18.4 10.5 %collective-permute-start.4 = (bf16[2,128,256]{2,1,0:T(8,128)(2,1)S(1)}, bf16[2,128,256]{2,1,0:T(8,128)(2,1)S(1)}, u32[]{:S(2)}, u32[]{:S(2)}) collective-permute-start(bf16[2,128,256]{2,1,0:T(8,128)(2,1)S(1)} %get-tuple-element.68), channel_id=1, source_target_pairs={{0,4},{1,5},{2,6},{3,7},{4,0},{5,1},{6,2},{7,3},{8,12},{9,13},{10,... | collective-permute-start | bytes 393224 | tf_op jit(solution)/shard_map/ppermute | solution.py:386
  20.3 10.2 %collective-permute-start.5 = (bf16[2,128,256]{2,1,0:T(8,128)(2,1)S(1)}, bf16[2,128,256]{2,1,0:T(8,128)(2,1)S(1)}, u32[]{:S(2)}, u32[]{:S(2)}) collective-permute-start(bf16[2,128,256]{2,1,0:T(8,128)(2,1)S(1)} %get-tuple-element.73), channel_id=1, source_target_pairs={{0,6},{1,7},{2,4},{3,5},{4,2},{5,3},{6,0},{7,1},{8,14},{9,15},{10,... | collective-permute-start | bytes 393224 | tf_op jit(solution)/shard_map/ppermute | solution.py:386
  21.5 9.0 %collective-permute-start.6 = (bf16[2,128,256]{2,1,0:T(8,128)(2,1)S(1)}, bf16[2,128,256]{2,1,0:T(8,128)(2,1)S(1)}, u32[]{:S(2)}, u32[]{:S(2)}) collective-permute-start(bf16[2,128,256]{2,1,0:T(8,128)(2,1)S(1)} %get-tuple-element.74), channel_id=1, source_target_pairs={{0,3},{1,2},{2,1},{3,0},{4,7},{5,6},{6,5},{7,4},{8,11},{9,10},{10,... | collective-permute-start | bytes 393224 | tf_op jit(solution)/shard_map/ppermute | solution.py:386
  22.9 7.6 %collective-permute-start.7 = (bf16[2,128,256]{2,1,0:T(8,128)(2,1)S(1)}, bf16[2,128,256]{2,1,0:T(8,128)(2,1)S(1)}, u32[]{:S(2)}, u32[]{:S(2)}) collective-permute-start(bf16[2,128,256]{2,1,0:T(8,128)(2,1)S(1)} %get-tuple-element.75), channel_id=1, source_target_pairs={{0,5},{1,4},{2,7},{3,6},{4,1},{5,0},{6,3},{7,2},{8,13},{9,12},{10,... | collective-permute-start | bytes 393224 | tf_op jit(solution)/shard_map/ppermute | solution.py:386
  23.6 8.4 %collective-permute-start.8 = (bf16[2,128,256]{2,1,0:T(8,128)(2,1)S(1)}, bf16[2,128,256]{2,1,0:T(8,128)(2,1)S(1)}, u32[]{:S(2)}, u32[]{:S(2)}) collective-permute-start(bf16[2,128,256]{2,1,0:T(8,128)(2,1)S(1)} %get-tuple-element.76), channel_id=1, source_target_pairs={{0,7},{1,6},{2,5},{3,4},{4,3},{5,2},{6,1},{7,0},{8,15},{9,14},{10,... | collective-permute-start | bytes 393224 | tf_op jit(solution)/shard_map/ppermute | solution.py:386
  28.9 12.8 %collective-permute-start.21 = (bf16[2,256,256]{2,1,0:T(8,128)(2,1)S(1)}, bf16[2,256,256]{2,1,0:T(8,128)(2,1)S(1)}, u32[]{:S(2)}, u32[]{:S(2)}) collective-permute-start(bf16[2,256,256]{2,1,0:T(8,128)(2,1)S(1)} %get-tuple-element.108), channel_id=1, source_target_pairs={{0,8},{8,0},{16,24},{24,16},{1,9},{9,1},{17,25},{25,17},{2,10},{10... | collective-permute-start | bytes 786440 | tf_op jit(solution)/shard_map/ppermute | solution.py:347
  31.9 25.1 %copy-start.7 = (f32[4096]{0:T(1024)S(1)}, f32[4096]{0:T(1024)}, u32[]{:S(2)}) copy-start(f32[4096]{0:T(1024)} %param.13) | copy-start | bytes 49156
  36.6 10.1 %collective-permute-start.16 = (bf16[2,2,128,256]{3,2,1,0:T(8,128)(2,1)S(1)}, bf16[2,2,128,256]{3,2,1,0:T(8,128)(2,1)S(1)}, u32[]{:S(2)}, u32[]{:S(2)}) collective-permute-start(bf16[2,2,128,256]{3,2,1,0:T(8,128)(2,1)S(1)} %get-tuple-element.94), channel_id=1, source_target_pairs={{0,6},{1,7},{2,4},{3,5},{4,2},{5,3},{6,0},{7,1},{8,14},{9,15},{10,... | collective-permute-start | bytes 786440 | tf_op jit(solution)/shard_map/ppermute | solution.py:386
  39.0 7.7 %collective-permute-start.17 = (bf16[2,2,128,256]{3,2,1,0:T(8,128)(2,1)S(1)}, bf16[2,2,128,256]{3,2,1,0:T(8,128)(2,1)S(1)}, u32[]{:S(2)}, u32[]{:S(2)}) collective-permute-start(bf16[2,2,128,256]{3,2,1,0:T(8,128)(2,1)S(1)} %get-tuple-element.95), channel_id=1, source_target_pairs={{0,1},{1,0},{2,3},{3,2},{4,5},{5,4},{6,7},{7,6},{8,9},{9,8},{10,11... | collective-permute-start | bytes 786440 | tf_op jit(solution)/shard_map/ppermute | solution.py:386
  39.6 9.9 %collective-permute-start.22 = (bf16[2,256,256]{2,1,0:T(8,128)(2,1)S(1)}, bf16[2,256,256]{2,1,0:T(8,128)(2,1)S(1)}, u32[]{:S(2)}, u32[]{:S(2)}) collective-permute-start(bf16[2,256,256]{2,1,0:T(8,128)(2,1)S(1)} %get-tuple-element.110), channel_id=1, source_target_pairs={{0,8},{8,0},{16,24},{24,16},{1,9},{9,1},{17,25},{25,17},{2,10},{10... | collective-permute-start | bytes 786440 | tf_op jit(solution)/shard_map/ppermute | solution.py:347
  40.7 12.3 %collective-permute-start.18 = (bf16[2,2,128,256]{3,2,1,0:T(8,128)(2,1)S(1)}, bf16[2,2,128,256]{3,2,1,0:T(8,128)(2,1)S(1)}, u32[]{:S(2)}, u32[]{:S(2)}) collective-permute-start(bf16[2,2,128,256]{3,2,1,0:T(8,128)(2,1)S(1)} %get-tuple-element.96), channel_id=1, source_target_pairs={{0,2},{1,3},{2,0},{3,1},{4,6},{5,7},{6,4},{7,5},{8,10},{9,11},{10,... | collective-permute-start | bytes 786440 | tf_op jit(solution)/shard_map/ppermute | solution.py:386
  41.7 13.8 %collective-permute-start.19 = (bf16[2,2,128,256]{3,2,1,0:T(8,128)(2,1)S(1)}, bf16[2,2,128,256]{3,2,1,0:T(8,128)(2,1)S(1)}, u32[]{:S(2)}, u32[]{:S(2)}) collective-permute-start(bf16[2,2,128,256]{3,2,1,0:T(8,128)(2,1)S(1)} %get-tuple-element.97), channel_id=1, source_target_pairs={{0,4},{1,5},{2,6},{3,7},{4,0},{5,1},{6,2},{7,3},{8,12},{9,13},{10,... | collective-permute-start | bytes 786440 | tf_op jit(solution)/shard_map/ppermute | solution.py:386
  46.7 10.3 %collective-permute-start.20 = (bf16[2,2,128,256]{3,2,1,0:T(8,128)(2,1)S(1)}, bf16[2,2,128,256]{3,2,1,0:T(8,128)(2,1)S(1)}, u32[]{:S(2)}, u32[]{:S(2)}) collective-permute-start(bf16[2,2,128,256]{3,2,1,0:T(8,128)(2,1)S(1)} %get-tuple-element.98), channel_id=1, source_target_pairs={{0,3},{1,2},{2,1},{3,0},{4,7},{5,6},{6,5},{7,4},{8,11},{9,10},{10,... | collective-permute-start | bytes 786440 | tf_op jit(solution)/shard_map/ppermute | solution.py:386
  46.7 14.7 %collective-permute-start.14 = (bf16[2,2,128,256]{3,2,1,0:T(8,128)(2,1)S(1)}, bf16[2,2,128,256]{3,2,1,0:T(8,128)(2,1)S(1)}, u32[]{:S(2)}, u32[]{:S(2)}) collective-permute-start(bf16[2,2,128,256]{3,2,1,0:T(8,128)(2,1)S(1)} %get-tuple-element.91), channel_id=1, source_target_pairs={{0,5},{1,4},{2,7},{3,6},{4,1},{5,0},{6,3},{7,2},{8,13},{9,12},{10,... | collective-permute-start | bytes 786440 | tf_op jit(solution)/shard_map/ppermute | solution.py:386
  49.4 13.3 %collective-permute-start.15 = (bf16[2,2,128,256]{3,2,1,0:T(8,128)(2,1)S(1)}, bf16[2,2,128,256]{3,2,1,0:T(8,128)(2,1)S(1)}, u32[]{:S(2)}, u32[]{:S(2)}) collective-permute-start(bf16[2,2,128,256]{3,2,1,0:T(8,128)(2,1)S(1)} %get-tuple-element.92), channel_id=1, source_target_pairs={{0,7},{1,6},{2,5},{3,4},{4,3},{5,2},{6,1},{7,0},{8,15},{9,14},{10,... | collective-permute-start | bytes 786440 | tf_op jit(solution)/shard_map/ppermute | solution.py:386
  53.1 13.2 %collective-permute-start.23 = (bf16[1,256,512]{2,1,0:T(8,128)(2,1)S(1)}, bf16[1,256,512]{2,1,0:T(8,128)(2,1)S(1)}, u32[]{:S(2)}, u32[]{:S(2)}) collective-permute-start(bf16[1,256,512]{2,1,0:T(8,128)(2,1)S(1)} %get-tuple-element.112), channel_id=1, source_target_pairs={{0,16},{8,24},{16,0},{24,8},{1,17},{9,25},{17,1},{25,9},{2,18},{10... | collective-permute-start | bytes 786440 | tf_op jit(solution)/shard_map/ppermute | solution.py:347

commit v17 on v16

--- a/solution.py
+++ b/solution.py
@@ -378,7 +378,7 @@
 
 
 def back_peers(n):
-    return [0, n - 2, 1, *range(2, n - 2, 2), *range(3, n, 2)]
+    return [0, n - 2, 1, *range(2, n - 2, 2), n - 1, *range(3, n - 2, 2)]
 
 
 def exchange(n, js, blocks):

time: 67.5 us -> 67.5 us (level)
    ppermute x21, waiting for transfers between devices: 12.8 us -> 13.8 us  [exchange(): lax.ppermute(block, 'ctx', [(i, i ^ j) for i in range(n)])]
  transfers between devices with their start and end apart: 24 -> 24, of which waited for: 8 -> 9; matrix products, arithmetic and copies ran while one was open for 0% -> 0% of each run, Pallas kernels for 31% -> 31%
where the time goes in v17:
time: 67.5 us; the launch traced here: 67.3 us
  starting transfers between devices  27.4 us (41%)
  Pallas kernels  24.9 us (37%)
  waiting for transfers between devices  14.1 us (21%)
  between operations  0.79 us (1%)
    ppermute x21, starting transfers between devices, exchange(): lax.ppermute(block, 'ctx', [(i, i ^ j) for i in range(n)])  22.6 us
    ppermute x21, waiting for transfers between devices, exchange(): lax.ppermute(block, 'ctx', [(i, i ^ j) for i in range(n)])  13.8 us
    pallas_call x2, Pallas kernels, conv(): pl.pallas_call(functools.partial(conv_kernel, n, d, half), in_specs=[SMEM...  9.42 us
    pallas_call x2, Pallas kernels, gate(): pl.pallas_call(functools.partial(gate_kernel, js), in_specs=[SMEM] + [VME...  7.17 us
    ppermute x3, starting transfers between devices, trade(): return resident(lax.ppermute(send, 'dp', [(i, i ^ bit) for i in range(d)]))  4.78 us
    pallas_call x2, Pallas kernels, filter_spectrum(): pl.pallas_call(functools.partial(filter_kernel, half), in_specs=[VMEM] *...  3.6 us
    pallas_call x2, Pallas kernels, products(): pl.pallas_call(functools.partial(second_kernel if half else first_kernel,...  3.53 us
  transfers between devices with their start and end apart: 24, of which 9 were waited for; matrix products, arithmetic and copies ran while one was open for 0% of the time, Pallas kernels for 31%

profile of v17, /device:TPU:0, one launch (start us, length us, event | category | flops | bytes accessed | tf_op | source)
XLA Modules:
  0.0 67.3 jit_solution(3675688179193964362)
XLA Ops:
  0.7 2.7 %products.2 = (bf16[2,128,256]{2,1,0:T(8,128)(2,1)S(1)}, bf16[2,128,256]{2,1,0:T(8,128)(2,1)S(1)}, bf16[2,128,256]{2,1,0:T(8,128)(2,1)S(1)}, bf16[2,128,256]{2,1...) custom-call(s32[2]{0:T(128)S(1)} %pad_add_fusion.me, ...), custom_call_target="tpu_custom_call" | custom-call | tf_op jit(solution)/shard_map/products/pallas_call | solution.py:133
  4.0 2.6 %collective-permute-start.1 = (bf16[2,128,256]{2,1,0:T(8,128)(2,1)S(1)}, bf16[2,128,256]{2,1,0:T(8,128)(2,1)S(1)}, u32[]{:S(2)}, u32[]{:S(2)}) collective-permute-start(bf16[2,128,256]{2,1,0:T(8,128)(2,1)S(1)} %get-tuple-element.60), channel_id=1, source_target_pairs={{0,2},{1,3},{2,0},{3,1},{4,6},{5,7},{6,4},{7,5},{8,10},{9,11},{10,... | collective-permute-start | bytes 393224 | tf_op jit(solution)/shard_map/ppermute | solution.py:386
  6.5 1.5 %collective-permute-start.9 = (bf16[2,128,256]{2,1,0:T(8,128)(2,1)S(1)}, bf16[2,128,256]{2,1,0:T(8,128)(2,1)S(1)}, u32[]{:S(2)}, u32[]{:S(2)}) collective-permute-start(bf16[2,128,256]{2,1,0:T(8,128)(2,1)S(1)} %get-tuple-element.78), channel_id=1, source_target_pairs={{0,4},{1,5},{2,6},{3,7},{4,0},{5,1},{6,2},{7,3},{8,12},{9,13},{10,... | collective-permute-start | bytes 393224 | tf_op jit(solution)/shard_map/ppermute | solution.py:386
  8.1 1.2 %collective-permute-start.11 = (bf16[2,128,256]{2,1,0:T(8,128)(2,1)S(1)}, bf16[2,128,256]{2,1,0:T(8,128)(2,1)S(1)}, u32[]{:S(2)}, u32[]{:S(2)}) collective-permute-start(bf16[2,128,256]{2,1,0:T(8,128)(2,1)S(1)} %get-tuple-element.80), channel_id=1, source_target_pairs={{0,3},{1,2},{2,1},{3,0},{4,7},{5,6},{6,5},{7,4},{8,11},{9,10},{10,... | collective-permute-start | bytes 393224 | tf_op jit(solution)/shard_map/ppermute | solution.py:386
  9.2 2.0 %collective-permute-start.12 = (bf16[2,128,256]{2,1,0:T(8,128)(2,1)S(1)}, bf16[2,128,256]{2,1,0:T(8,128)(2,1)S(1)}, u32[]{:S(2)}, u32[]{:S(2)}) collective-permute-start(bf16[2,128,256]{2,1,0:T(8,128)(2,1)S(1)} %get-tuple-element.81), channel_id=1, source_target_pairs={{0,5},{1,4},{2,7},{3,6},{4,1},{5,0},{6,3},{7,2},{8,13},{9,12},{10,... | collective-permute-start | bytes 393224 | tf_op jit(solution)/shard_map/ppermute | solution.py:386
  11.3 0.8 %products.3 = (bf16[2,128,256]{2,1,0:T(8,128)(2,1)S(1)}, bf16[2,128,256]{2,1,0:T(8,128)(2,1)S(1)}, bf16[2,128,256]{2,1,0:T(8,128)(2,1)S(1)}, bf16[2,128,256]{2,1...) custom-call(s32[2]{0:T(128)S(1)} %pad_add_fusion.me, ...), custom_call_target="tpu_custom_call" | custom-call | tf_op jit(solution)/shard_map/products/pallas_call | solution.py:133
  12.6 1.9 %filter_spectrum.2.refs_0_.refs_8_ = f32[8,256,256]{2,1,0:T(8,128)S(1)} custom-call(f32[512,1024]{1,0:T(8,128)S(1)} %copy-done.5, bf16[8,256,256]{2,1,0:T(8,128)(2,1)S(1)} %copy-done.4, bf16[2,128,256]{2,1,0:T(8,128)(2,1)S(1)} %collective-permute-done.refs_0_.refs_1_, bf16[2,128,256]{2,1,0:T(8,128)(2,1)S(1)} %collective-permute-done.1.refs_1_.refs_2_), custom_call_target="tpu_custom_call" | custom-call | tf_op jit(solution)/shard_map/filter_spectrum/pallas_call | solution.py:176
  14.6 1.3 %collective-permute-start.2 = (bf16[2,128,256]{2,1,0:T(8,128)(2,1)S(1)}, bf16[2,128,256]{2,1,0:T(8,128)(2,1)S(1)}, u32[]{:S(2)}, u32[]{:S(2)}) collective-permute-start(bf16[2,128,256]{2,1,0:T(8,128)(2,1)S(1)} %get-tuple-element.66), channel_id=1, source_target_pairs={{0,1},{1,0},{2,3},{3,2},{4,5},{5,4},{6,7},{7,6},{8,9},{9,8},{10,11... | collective-permute-start | bytes 393224 | tf_op jit(solution)/shard_map/ppermute | solution.py:386
  15.9 0.7 %collective-permute-start.3 = (bf16[2,128,256]{2,1,0:T(8,128)(2,1)S(1)}, bf16[2,128,256]{2,1,0:T(8,128)(2,1)S(1)}, u32[]{:S(2)}, u32[]{:S(2)}) collective-permute-start(bf16[2,128,256]{2,1,0:T(8,128)(2,1)S(1)} %get-tuple-element.67), channel_id=1, source_target_pairs={{0,2},{1,3},{2,0},{3,1},{4,6},{5,7},{6,4},{7,5},{8,10},{9,11},{10,... | collective-permute-start | bytes 393224 | tf_op jit(solution)/shard_map/ppermute | solution.py:386
  16.6 1.7 %filter_spectrum.3.refs_0_.refs_8_ = f32[8,256,256]{2,1,0:T(8,128)S(1)} custom-call(f32[512,1024]{1,0:T(8,128)S(1)} %copy-done.5, bf16[8,256,256]{2,1,0:T(8,128)(2,1)S(1)} %copy-done.4, f32[8,256,256]{2,1,0:T(8,128)S(1)} %filter_spectrum.2.refs_0_.refs_8_), custom_call_target="tpu_custom_call" | custom-call | tf_op jit(solution)/shard_map/filter_spectrum/pallas_call | solution.py:176
  18.4 1.2 %collective-permute-start.4 = (bf16[2,128,256]{2,1,0:T(8,128)(2,1)S(1)}, bf16[2,128,256]{2,1,0:T(8,128)(2,1)S(1)}, u32[]{:S(2)}, u32[]{:S(2)}) collective-permute-start(bf16[2,128,256]{2,1,0:T(8,128)(2,1)S(1)} %get-tuple-element.68), channel_id=1, source_target_pairs={{0,4},{1,5},{2,6},{3,7},{4,0},{5,1},{6,2},{7,3},{8,12},{9,13},{10,... | collective-permute-start | bytes 393224 | tf_op jit(solution)/shard_map/ppermute | solution.py:386
  19.6 0.7 %collective-permute-done.12.refs_6_ = bf16[2,128,256]{2,1,0:T(8,128)(2,1)S(1)} collective-permute-done((bf16[2,128,256]{2,1,0:T(8,128)(2,1)S(1)}, bf16[2,128,256]{2,1,0:T(8,128)(2,1)S(1)}, u32[]{:S(2)}, u32[]{:S(2)}) %collective-permute-start.12) | collective-permute-done | bytes 131104 | tf_op jit(solution)/shard_map/ppermute | solution.py:386
  20.3 1.1 %collective-permute-start.5 = (bf16[2,128,256]{2,1,0:T(8,128)(2,1)S(1)}, bf16[2,128,256]{2,1,0:T(8,128)(2,1)S(1)}, u32[]{:S(2)}, u32[]{:S(2)}) collective-permute-start(bf16[2,128,256]{2,1,0:T(8,128)(2,1)S(1)} %get-tuple-element.73), channel_id=1, source_target_pairs={{0,6},{1,7},{2,4},{3,5},{4,2},{5,3},{6,0},{7,1},{8,14},{9,15},{10,... | collective-permute-start | bytes 393224 | tf_op jit(solution)/shard_map/ppermute | solution.py:386
  21.5 1.5 %collective-permute-start.6 = (bf16[2,128,256]{2,1,0:T(8,128)(2,1)S(1)}, bf16[2,128,256]{2,1,0:T(8,128)(2,1)S(1)}, u32[]{:S(2)}, u32[]{:S(2)}) collective-permute-start(bf16[2,128,256]{2,1,0:T(8,128)(2,1)S(1)} %get-tuple-element.74), channel_id=1, source_target_pairs={{0,3},{1,2},{2,1},{3,0},{4,7},{5,6},{6,5},{7,4},{8,11},{9,10},{10,... | collective-permute-start | bytes 393224 | tf_op jit(solution)/shard_map/ppermute | solution.py:386
  23.6 0.6 collective-permute-start.8
  24.2 4.7 %conv.2 = (bf16[2,2,128,256]{3,2,1,0:T(8,128)(2,1)S(1)}, bf16[2,2,128,256]{3,2,1,0:T(8,128)(2,1)S(1)}, bf16[2,2,128,256]{3,2,1,0:T(8,128)(2,1)S(1)}, bf16[2,2,12...) custom-call(s32[2]{0:T(128)S(1)} %pad_add_fusion.me, ...), custom_call_target="tpu_custom_call" | custom-call | tf_op jit(solution)/shard_map/conv/pallas_call | solution.py:251
  28.9 1.6 %collective-permute-start.21 = (bf16[2,256,256]{2,1,0:T(8,128)(2,1)S(1)}, bf16[2,256,256]{2,1,0:T(8,128)(2,1)S(1)}, u32[]{:S(2)}, u32[]{:S(2)}) collective-permute-start(bf16[2,256,256]{2,1,0:T(8,128)(2,1)S(1)} %get-tuple-element.108), channel_id=1, source_target_pairs={{0,8},{8,0},{16,24},{24,16},{1,9},{9,1},{17,25},{25,17},{2,10},{10... | collective-permute-start | bytes 786440 | tf_op jit(solution)/shard_map/ppermute | solution.py:347
  30.5 1.4 %collective-permute-done.8.refs_7_ = bf16[2,128,256]{2,1,0:T(8,128)(2,1)S(1)} collective-permute-done((bf16[2,128,256]{2,1,0:T(8,128)(2,1)S(1)}, bf16[2,128,256]{2,1,0:T(8,128)(2,1)S(1)}, u32[]{:S(2)}, u32[]{:S(2)}) %collective-permute-start.8) | collective-permute-done | bytes 131104 | tf_op jit(solution)/shard_map/ppermute | solution.py:386
  31.9 4.7 %conv.3 = (bf16[2,2,128,256]{3,2,1,0:T(8,128)(2,1)S(1)}, bf16[2,2,128,256]{3,2,1,0:T(8,128)(2,1)S(1)}, bf16[2,2,128,256]{3,2,1,0:T(8,128)(2,1)S(1)}, bf16[2,2,12...) custom-call(s32[2]{0:T(128)S(1)} %pad_add_fusion.me, ...), custom_call_target="tpu_custom_call", output_to_operand_aliasing={{0}: (12, {}), {1}: (13, {}), {2}: (14, {}), {3}: (15, {}),... | custom-call | tf_op jit(solution)/shard_map/conv/pallas_call | solution.py:251
  36.6 2.4 %collective-permute-start.16 = (bf16[2,2,128,256]{3,2,1,0:T(8,128)(2,1)S(1)}, bf16[2,2,128,256]{3,2,1,0:T(8,128)(2,1)S(1)}, u32[]{:S(2)}, u32[]{:S(2)}) collective-permute-start(bf16[2,2,128,256]{3,2,1,0:T(8,128)(2,1)S(1)} %get-tuple-element.94), channel_id=1, source_target_pairs={{0,6},{1,7},{2,4},{3,5},{4,2},{5,3},{6,0},{7,1},{8,14},{9,15},{10,... | collective-permute-start | bytes 786440 | tf_op jit(solution)/shard_map/ppermute | solution.py:386
  39.6 1.2 %collective-permute-start.22 = (bf16[2,256,256]{2,1,0:T(8,128)(2,1)S(1)}, bf16[2,256,256]{2,1,0:T(8,128)(2,1)S(1)}, u32[]{:S(2)}, u32[]{:S(2)}) collective-permute-start(bf16[2,256,256]{2,1,0:T(8,128)(2,1)S(1)} %get-tuple-element.110), channel_id=1, source_target_pairs={{0,8},{8,0},{16,24},{24,16},{1,9},{9,1},{17,25},{25,17},{2,10},{10... | collective-permute-start | bytes 786440 | tf_op jit(solution)/shard_map/ppermute | solution.py:347
  40.7 1.0 %collective-permute-start.18 = (bf16[2,2,128,256]{3,2,1,0:T(8,128)(2,1)S(1)}, bf16[2,2,128,256]{3,2,1,0:T(8,128)(2,1)S(1)}, u32[]{:S(2)}, u32[]{:S(2)}) collective-permute-start(bf16[2,2,128,256]{3,2,1,0:T(8,128)(2,1)S(1)} %get-tuple-element.96), channel_id=1, source_target_pairs={{0,2},{1,3},{2,0},{3,1},{4,6},{5,7},{6,4},{7,5},{8,10},{9,11},{10,... | collective-permute-start | bytes 786440 | tf_op jit(solution)/shard_map/ppermute | solution.py:386
  41.7 5.0 %collective-permute-done.16.refs_1_ = bf16[2,2,128,256]{3,2,1,0:T(8,128)(2,1)S(1)} collective-permute-done((bf16[2,2,128,256]{3,2,1,0:T(8,128)(2,1)S(1)}, bf16[2,2,128,256]{3,2,1,0:T(8,128)(2,1)S(1)}, u32[]{:S(2)}, u32[]{:S(2)}) %collective-permute-start.16) | collective-permute-done | bytes 262176 | tf_op jit(solution)/shard_map/ppermute | solution.py:386
  46.7 1.8 %collective-permute-start.20 = (bf16[2,2,128,256]{3,2,1,0:T(8,128)(2,1)S(1)}, bf16[2,2,128,256]{3,2,1,0:T(8,128)(2,1)S(1)}, u32[]{:S(2)}, u32[]{:S(2)}) collective-permute-start(bf16[2,2,128,256]{3,2,1,0:T(8,128)(2,1)S(1)} %get-tuple-element.98), channel_id=1, source_target_pairs={{0,7},{1,6},{2,5},{3,4},{4,3},{5,2},{6,1},{7,0},{8,15},{9,14},{10,... | collective-permute-start | bytes 786440 | tf_op jit(solution)/shard_map/ppermute | solution.py:386
  48.6 1.5 %collective-permute-start.14 = (bf16[2,2,128,256]{3,2,1,0:T(8,128)(2,1)S(1)}, bf16[2,2,128,256]{3,2,1,0:T(8,128)(2,1)S(1)}, u32[]{:S(2)}, u32[]{:S(2)}) collective-permute-start(bf16[2,2,128,256]{3,2,1,0:T(8,128)(2,1)S(1)} %get-tuple-element.91), channel_id=1, source_target_pairs={{0,3},{1,2},{2,1},{3,0},{4,7},{5,6},{6,5},{7,4},{8,11},{9,10},{10,... | collective-permute-start | bytes 786440 | tf_op jit(solution)/shard_map/ppermute | solution.py:386
  50.2 2.9 %collective-permute-done.18.refs_3_ = bf16[2,2,128,256]{3,2,1,0:T(8,128)(2,1)S(1)} collective-permute-done((bf16[2,2,128,256]{3,2,1,0:T(8,128)(2,1)S(1)}, bf16[2,2,128,256]{3,2,1,0:T(8,128)(2,1)S(1)}, u32[]{:S(2)}, u32[]{:S(2)}) %collective-permute-start.18) | collective-permute-done | bytes 262176 | tf_op jit(solution)/shard_map/ppermute | solution.py:386
  53.1 2.0 %collective-permute-start.23 = (bf16[1,256,512]{2,1,0:T(8,128)(2,1)S(1)}, bf16[1,256,512]{2,1,0:T(8,128)(2,1)S(1)}, u32[]{:S(2)}, u32[]{:S(2)}) collective-permute-start(bf16[1,256,512]{2,1,0:T(8,128)(2,1)S(1)} %get-tuple-element.112), channel_id=1, source_target_pairs={{0,16},{8,24},{16,0},{24,8},{1,17},{9,25},{17,1},{25,9},{2,18},{10... | collective-permute-start | bytes 786440 | tf_op jit(solution)/shard_map/ppermute | solution.py:347
  55.1 2.2 %collective-permute-done.20.refs_5_ = bf16[2,2,128,256]{3,2,1,0:T(8,128)(2,1)S(1)} collective-permute-done((bf16[2,2,128,256]{3,2,1,0:T(8,128)(2,1)S(1)}, bf16[2,2,128,256]{3,2,1,0:T(8,128)(2,1)S(1)}, u32[]{:S(2)}, u32[]{:S(2)}) %collective-permute-start.20) | collective-permute-done | bytes 262176 | tf_op jit(solution)/shard_map/ppermute | solution.py:386
  57.3 4.4 %gate.2 = (bf16[128,4096]{1,0:T(8,128)(2,1)}, bf16[128,4096]{1,0:T(8,128)(2,1)}, bf16[128,4096]{1,0:T(8,128)(2,1)}, bf16[128,4096]{1,0:T(8,128)(2,1)}, f32[8,128]{1,0:T(8,128)}) custom-call(s32[2]{0:T(128)S(1)} %pad_add_fusion.me, bf16[128,4096]{1,0:T(8,128)(2,1)S(1)} %bitcast.13, bf16[128,4096]{1,0:T(8,128)(2,1)S(1)} %bitcast.17, ...), custom_call_target="tpu_custom_call" | custom-call | tf_op jit(solution)/shard_map/gate/pallas_call | solution.py:313
  61.7 1.0 %collective-permute-done.14.refs_0_ = bf16[2,2,128,256]{3,2,1,0:T(8,128)(2,1)S(1)} collective-permute-done((bf16[2,2,128,256]{3,2,1,0:T(8,128)(2,1)S(1)}, bf16[2,2,128,256]{3,2,1,0:T(8,128)(2,1)S(1)}, u32[]{:S(2)}, u32[]{:S(2)}) %collective-permute-start.14) | collective-permute-done | bytes 262176 | tf_op jit(solution)/shard_map/ppermute | solution.py:386
  63.2 2.8 %gate.3 = (bf16[128,4096]{1,0:T(8,128)(2,1)}, bf16[128,4096]{1,0:T(8,128)(2,1)}, bf16[128,4096]{1,0:T(8,128)(2,1)}, bf16[128,4096]{1,0:T(8,128)(2,1)}, f32[8,128]{1,0:T(8,128)}) custom-call(s32[2]{0:T(128)S(1)} %pad_add_fusion.me, bf16[128,4096]{1,0:T(8,128)(2,1)S(1)} %bitcast.14, ...), custom_call_target="tpu_custom_call", output_to_operand_aliasing={{0}: (8, {}), {1}: (9, {}), {2}: (10, {}), {3}: (11, {})} | custom-call | tf_op jit(solution)/shard_map/gate/pallas_call | solution.py:313
  66.3 1.1 %turn_grads.1 = f32[512,256]{1,0:T(8,128)} custom-call(f32[1,256,512]{2,1,0:T(8,128)S(1)} %get-tuple-element.111.keep, bf16[1,256,512]{2,1,0:T(8,128)(2,1)S(1)} %collective-permute-done.23.got), custom_call_target="tpu_custom_call" | custom-call | tf_op jit(solution)/shard_map/turn_grads/pallas_call | solution.py:365
  (45 shorter events, 3.3 us)
Async XLA Ops:
  0.7 10.5 %copy-start = (bf16[1,128,4096]{2,1,0:T(8,128)(2,1)S(1)}, bf16[1,128,4096]{2,1,0:T(8,128)(2,1)}, u32[]{:S(2)}) copy-start(bf16[1,128,4096]{2,1,0:T(8,128)(2,1)} %param.8) | copy-start | bytes 3145732
  0.7 10.5 %copy-start.1 = (bf16[1,128,4096]{2,1,0:T(8,128)(2,1)S(1)}, bf16[1,128,4096]{2,1,0:T(8,128)(2,1)}, u32[]{:S(2)}) copy-start(bf16[1,128,4096]{2,1,0:T(8,128)(2,1)} %param.11) | copy-start | bytes 3145732
  0.7 10.5 %copy-start.2 = (bf16[1,128,4096]{2,1,0:T(8,128)(2,1)S(1)}, bf16[1,128,4096]{2,1,0:T(8,128)(2,1)}, u32[]{:S(2)}) copy-start(bf16[1,128,4096]{2,1,0:T(8,128)(2,1)} %param.10) | copy-start | bytes 3145732
  0.7 10.5 %copy-start.3 = (bf16[1,128,4096]{2,1,0:T(8,128)(2,1)S(1)}, bf16[1,128,4096]{2,1,0:T(8,128)(2,1)}, u32[]{:S(2)}) copy-start(bf16[1,128,4096]{2,1,0:T(8,128)(2,1)} %param.9) | copy-start | bytes 3145732
  3.4 5.8 %collective-permute-start = (bf16[2,128,256]{2,1,0:T(8,128)(2,1)S(1)}, bf16[2,128,256]{2,1,0:T(8,128)(2,1)S(1)}, u32[]{:S(2)}, u32[]{:S(2)}) collective-permute-start(bf16[2,128,256]{2,1,0:T(8,128)(2,1)S(1)} %get-tuple-element.59), channel_id=1, source_target_pairs={{0,1},{1,0},{2,3},{3,2},{4,5},{5,4},{6,7},{7,6},{8,9},{9,8},{10,11... | collective-permute-start | bytes 393224 | tf_op jit(solution)/shard_map/ppermute | solution.py:386
  4.0 8.2 %collective-permute-start.1 = (bf16[2,128,256]{2,1,0:T(8,128)(2,1)S(1)}, bf16[2,128,256]{2,1,0:T(8,128)(2,1)S(1)}, u32[]{:S(2)}, u32[]{:S(2)}) collective-permute-start(bf16[2,128,256]{2,1,0:T(8,128)(2,1)S(1)} %get-tuple-element.60), channel_id=1, source_target_pairs={{0,2},{1,3},{2,0},{3,1},{4,6},{5,7},{6,4},{7,5},{8,10},{9,11},{10,... | collective-permute-start | bytes 393224 | tf_op jit(solution)/shard_map/ppermute | solution.py:386
  6.5 8.1 %collective-permute-start.9 = (bf16[2,128,256]{2,1,0:T(8,128)(2,1)S(1)}, bf16[2,128,256]{2,1,0:T(8,128)(2,1)S(1)}, u32[]{:S(2)}, u32[]{:S(2)}) collective-permute-start(bf16[2,128,256]{2,1,0:T(8,128)(2,1)S(1)} %get-tuple-element.78), channel_id=1, source_target_pairs={{0,4},{1,5},{2,6},{3,7},{4,0},{5,1},{6,2},{7,3},{8,12},{9,13},{10,... | collective-permute-start | bytes 393224 | tf_op jit(solution)/shard_map/ppermute | solution.py:386
  8.0 7.8 %collective-permute-start.10 = (bf16[2,128,256]{2,1,0:T(8,128)(2,1)S(1)}, bf16[2,128,256]{2,1,0:T(8,128)(2,1)S(1)}, u32[]{:S(2)}, u32[]{:S(2)}) collective-permute-start(bf16[2,128,256]{2,1,0:T(8,128)(2,1)S(1)} %get-tuple-element.79), channel_id=1, source_target_pairs={{0,6},{1,7},{2,4},{3,5},{4,2},{5,3},{6,0},{7,1},{8,14},{9,15},{10,... | collective-permute-start | bytes 393224 | tf_op jit(solution)/shard_map/ppermute | solution.py:386
  8.1 10.3 %collective-permute-start.11 = (bf16[2,128,256]{2,1,0:T(8,128)(2,1)S(1)}, bf16[2,128,256]{2,1,0:T(8,128)(2,1)S(1)}, u32[]{:S(2)}, u32[]{:S(2)}) collective-permute-start(bf16[2,128,256]{2,1,0:T(8,128)(2,1)S(1)} %get-tuple-element.80), channel_id=1, source_target_pairs={{0,3},{1,2},{2,1},{3,0},{4,7},{5,6},{6,5},{7,4},{8,11},{9,10},{10,... | collective-permute-start | bytes 393224 | tf_op jit(solution)/shard_map/ppermute | solution.py:386
  9.2 3.4 %copy-start.4 = (bf16[8,256,256]{2,1,0:T(8,128)(2,1)S(1)}, bf16[8,256,256]{2,1,0:T(8,128)(2,1)}, u32[]{:S(2)}) copy-start(bf16[8,256,256]{2,1,0:T(8,128)(2,1)} %constant.12.clone.fwd.refs_9_) | copy-start | bytes 3145732
  9.2 3.4 %copy-start.5 = (f32[512,1024]{1,0:T(8,128)S(1)}, f32[512,1024]{1,0:T(8,128)}, u32[]{:S(2)}) copy-start(f32[512,1024]{1,0:T(8,128)} %filt.3) | copy-start | bytes 6291460
  9.2 11.1 %collective-permute-start.12 = (bf16[2,128,256]{2,1,0:T(8,128)(2,1)S(1)}, bf16[2,128,256]{2,1,0:T(8,128)(2,1)S(1)}, u32[]{:S(2)}, u32[]{:S(2)}) collective-permute-start(bf16[2,128,256]{2,1,0:T(8,128)(2,1)S(1)} %get-tuple-element.81), channel_id=1, source_target_pairs={{0,5},{1,4},{2,7},{3,6},{4,1},{5,0},{6,3},{7,2},{8,13},{9,12},{10,... | collective-permute-start | bytes 393224 | tf_op jit(solution)/shard_map/ppermute | solution.py:386
  12.1 9.4 %collective-permute-start.13 = (bf16[2,128,256]{2,1,0:T(8,128)(2,1)S(1)}, bf16[2,128,256]{2,1,0:T(8,128)(2,1)S(1)}, u32[]{:S(2)}, u32[]{:S(2)}) collective-permute-start(bf16[2,128,256]{2,1,0:T(8,128)(2,1)S(1)} %get-tuple-element.82), channel_id=1, source_target_pairs={{0,7},{1,6},{2,5},{3,4},{4,3},{5,2},{6,1},{7,0},{8,15},{9,14},{10,... | collective-permute-start | bytes 393224 | tf_op jit(solution)/shard_map/ppermute | solution.py:386
  14.6 8.3 %collective-permute-start.2 = (bf16[2,128,256]{2,1,0:T(8,128)(2,1)S(1)}, bf16[2,128,256]{2,1,0:T(8,128)(2,1)S(1)}, u32[]{:S(2)}, u32[]{:S(2)}) collective-permute-start(bf16[2,128,256]{2,1,0:T(8,128)(2,1)S(1)} %get-tuple-element.66), channel_id=1, source_target_pairs={{0,1},{1,0},{2,3},{3,2},{4,5},{5,4},{6,7},{7,6},{8,9},{9,8},{10,11... | collective-permute-start | bytes 393224 | tf_op jit(solution)/shard_map/ppermute | solution.py:386
  15.9 7.7 %collective-permute-start.3 = (bf16[2,128,256]{2,1,0:T(8,128)(2,1)S(1)}, bf16[2,128,256]{2,1,0:T(8,128)(2,1)S(1)}, u32[]{:S(2)}, u32[]{:S(2)}) collective-permute-start(bf16[2,128,256]{2,1,0:T(8,128)(2,1)S(1)} %get-tuple-element.67), channel_id=1, source_target_pairs={{0,2},{1,3},{2,0},{3,1},{4,6},{5,7},{6,4},{7,5},{8,10},{9,11},{10,... | collective-permute-start | bytes 393224 | tf_op jit(solution)/shard_map/ppermute | solution.py:386
  18.3 5.8 %copy-start.6 = (bf16[8,128,256]{2,1,0:T(8,128)(2,1)S(1)}, bf16[8,128,256]{2,1,0:T(8,128)(2,1)}, u32[]{:S(2)}) copy-start(bf16[8,128,256]{2,1,0:T(8,128)(2,1)} %constant.13.clone.refs_10_) | copy-start | bytes 1572868
  18.4 10.5 %collective-permute-start.4 = (bf16[2,128,256]{2,1,0:T(8,128)(2,1)S(1)}, bf16[2,128,256]{2,1,0:T(8,128)(2,1)S(1)}, u32[]{:S(2)}, u32[]{:S(2)}) collective-permute-start(bf16[2,128,256]{2,1,0:T(8,128)(2,1)S(1)} %get-tuple-element.68), channel_id=1, source_target_pairs={{0,4},{1,5},{2,6},{3,7},{4,0},{5,1},{6,2},{7,3},{8,12},{9,13},{10,... | collective-permute-start | bytes 393224 | tf_op jit(solution)/shard_map/ppermute | solution.py:386
  20.3 10.2 %collective-permute-start.5 = (bf16[2,128,256]{2,1,0:T(8,128)(2,1)S(1)}, bf16[2,128,256]{2,1,0:T(8,128)(2,1)S(1)}, u32[]{:S(2)}, u32[]{:S(2)}) collective-permute-start(bf16[2,128,256]{2,1,0:T(8,128)(2,1)S(1)} %get-tuple-element.73), channel_id=1, source_target_pairs={{0,6},{1,7},{2,4},{3,5},{4,2},{5,3},{6,0},{7,1},{8,14},{9,15},{10,... | collective-permute-start | bytes 393224 | tf_op jit(solution)/shard_map/ppermute | solution.py:386
  21.5 9.0 %collective-permute-start.6 = (bf16[2,128,256]{2,1,0:T(8,128)(2,1)S(1)}, bf16[2,128,256]{2,1,0:T(8,128)(2,1)S(1)}, u32[]{:S(2)}, u32[]{:S(2)}) collective-permute-start(bf16[2,128,256]{2,1,0:T(8,128)(2,1)S(1)} %get-tuple-element.74), channel_id=1, source_target_pairs={{0,3},{1,2},{2,1},{3,0},{4,7},{5,6},{6,5},{7,4},{8,11},{9,10},{10,... | collective-permute-start | bytes 393224 | tf_op jit(solution)/shard_map/ppermute | solution.py:386
  22.9 7.6 %collective-permute-start.7 = (bf16[2,128,256]{2,1,0:T(8,128)(2,1)S(1)}, bf16[2,128,256]{2,1,0:T(8,128)(2,1)S(1)}, u32[]{:S(2)}, u32[]{:S(2)}) collective-permute-start(bf16[2,128,256]{2,1,0:T(8,128)(2,1)S(1)} %get-tuple-element.75), channel_id=1, source_target_pairs={{0,5},{1,4},{2,7},{3,6},{4,1},{5,0},{6,3},{7,2},{8,13},{9,12},{10,... | collective-permute-start | bytes 393224 | tf_op jit(solution)/shard_map/ppermute | solution.py:386
  23.6 8.4 %collective-permute-start.8 = (bf16[2,128,256]{2,1,0:T(8,128)(2,1)S(1)}, bf16[2,128,256]{2,1,0:T(8,128)(2,1)S(1)}, u32[]{:S(2)}, u32[]{:S(2)}) collective-permute-start(bf16[2,128,256]{2,1,0:T(8,128)(2,1)S(1)} %get-tuple-element.76), channel_id=1, source_target_pairs={{0,7},{1,6},{2,5},{3,4},{4,3},{5,2},{6,1},{7,0},{8,15},{9,14},{10,... | collective-permute-start | bytes 393224 | tf_op jit(solution)/shard_map/ppermute | solution.py:386
  28.9 12.8 %collective-permute-start.21 = (bf16[2,256,256]{2,1,0:T(8,128)(2,1)S(1)}, bf16[2,256,256]{2,1,0:T(8,128)(2,1)S(1)}, u32[]{:S(2)}, u32[]{:S(2)}) collective-permute-start(bf16[2,256,256]{2,1,0:T(8,128)(2,1)S(1)} %get-tuple-element.108), channel_id=1, source_target_pairs={{0,8},{8,0},{16,24},{24,16},{1,9},{9,1},{17,25},{25,17},{2,10},{10... | collective-permute-start | bytes 786440 | tf_op jit(solution)/shard_map/ppermute | solution.py:347
  31.9 25.3 %copy-start.7 = (f32[4096]{0:T(1024)S(1)}, f32[4096]{0:T(1024)}, u32[]{:S(2)}) copy-start(f32[4096]{0:T(1024)} %param.13) | copy-start | bytes 49156
  36.6 10.1 %collective-permute-start.16 = (bf16[2,2,128,256]{3,2,1,0:T(8,128)(2,1)S(1)}, bf16[2,2,128,256]{3,2,1,0:T(8,128)(2,1)S(1)}, u32[]{:S(2)}, u32[]{:S(2)}) collective-permute-start(bf16[2,2,128,256]{3,2,1,0:T(8,128)(2,1)S(1)} %get-tuple-element.94), channel_id=1, source_target_pairs={{0,6},{1,7},{2,4},{3,5},{4,2},{5,3},{6,0},{7,1},{8,14},{9,15},{10,... | collective-permute-start | bytes 786440 | tf_op jit(solution)/shard_map/ppermute | solution.py:386
  39.0 9.6 %collective-permute-start.17 = (bf16[2,2,128,256]{3,2,1,0:T(8,128)(2,1)S(1)}, bf16[2,2,128,256]{3,2,1,0:T(8,128)(2,1)S(1)}, u32[]{:S(2)}, u32[]{:S(2)}) collective-permute-start(bf16[2,2,128,256]{3,2,1,0:T(8,128)(2,1)S(1)} %get-tuple-element.95), channel_id=1, source_target_pairs={{0,1},{1,0},{2,3},{3,2},{4,5},{5,4},{6,7},{7,6},{8,9},{9,8},{10,11... | collective-permute-start | bytes 786440 | tf_op jit(solution)/shard_map/ppermute | solution.py:386
  39.6 10.6 %collective-permute-start.22 = (bf16[2,256,256]{2,1,0:T(8,128)(2,1)S(1)}, bf16[2,256,256]{2,1,0:T(8,128)(2,1)S(1)}, u32[]{:S(2)}, u32[]{:S(2)}) collective-permute-start(bf16[2,256,256]{2,1,0:T(8,128)(2,1)S(1)} %get-tuple-element.110), channel_id=1, source_target_pairs={{0,8},{8,0},{16,24},{24,16},{1,9},{9,1},{17,25},{25,17},{2,10},{10... | collective-permute-start | bytes 786440 | tf_op jit(solution)/shard_map/ppermute | solution.py:347
  40.7 12.3 %collective-permute-start.18 = (bf16[2,2,128,256]{3,2,1,0:T(8,128)(2,1)S(1)}, bf16[2,2,128,256]{3,2,1,0:T(8,128)(2,1)S(1)}, u32[]{:S(2)}, u32[]{:S(2)}) collective-permute-start(bf16[2,2,128,256]{3,2,1,0:T(8,128)(2,1)S(1)} %get-tuple-element.96), channel_id=1, source_target_pairs={{0,2},{1,3},{2,0},{3,1},{4,6},{5,7},{6,4},{7,5},{8,10},{9,11},{10,... | collective-permute-start | bytes 786440 | tf_op jit(solution)/shard_map/ppermute | solution.py:386
  41.7 13.3 %collective-permute-start.19 = (bf16[2,2,128,256]{3,2,1,0:T(8,128)(2,1)S(1)}, bf16[2,2,128,256]{3,2,1,0:T(8,128)(2,1)S(1)}, u32[]{:S(2)}, u32[]{:S(2)}) collective-permute-start(bf16[2,2,128,256]{3,2,1,0:T(8,128)(2,1)S(1)} %get-tuple-element.97), channel_id=1, source_target_pairs={{0,4},{1,5},{2,6},{3,7},{4,0},{5,1},{6,2},{7,3},{8,12},{9,13},{10,... | collective-permute-start | bytes 786440 | tf_op jit(solution)/shard_map/ppermute | solution.py:386
  46.7 10.5 %collective-permute-start.20 = (bf16[2,2,128,256]{3,2,1,0:T(8,128)(2,1)S(1)}, bf16[2,2,128,256]{3,2,1,0:T(8,128)(2,1)S(1)}, u32[]{:S(2)}, u32[]{:S(2)}) collective-permute-start(bf16[2,2,128,256]{3,2,1,0:T(8,128)(2,1)S(1)} %get-tuple-element.98), channel_id=1, source_target_pairs={{0,7},{1,6},{2,5},{3,4},{4,3},{5,2},{6,1},{7,0},{8,15},{9,14},{10,... | collective-permute-start | bytes 786440 | tf_op jit(solution)/shard_map/ppermute | solution.py:386
  48.6 14.1 %collective-permute-start.14 = (bf16[2,2,128,256]{3,2,1,0:T(8,128)(2,1)S(1)}, bf16[2,2,128,256]{3,2,1,0:T(8,128)(2,1)S(1)}, u32[]{:S(2)}, u32[]{:S(2)}) collective-permute-start(bf16[2,2,128,256]{3,2,1,0:T(8,128)(2,1)S(1)} %get-tuple-element.91), channel_id=1, source_target_pairs={{0,3},{1,2},{2,1},{3,0},{4,7},{5,6},{6,5},{7,4},{8,11},{9,10},{10,... | collective-permute-start | bytes 786440 | tf_op jit(solution)/shard_map/ppermute | solution.py:386
  50.1 13.1 %collective-permute-start.15 = (bf16[2,2,128,256]{3,2,1,0:T(8,128)(2,1)S(1)}, bf16[2,2,128,256]{3,2,1,0:T(8,128)(2,1)S(1)}, u32[]{:S(2)}, u32[]{:S(2)}) collective-permute-start(bf16[2,2,128,256]{3,2,1,0:T(8,128)(2,1)S(1)} %get-tuple-element.92), channel_id=1, source_target_pairs={{0,5},{1,4},{2,7},{3,6},{4,1},{5,0},{6,3},{7,2},{8,13},{9,12},{10,... | collective-permute-start | bytes 786440 | tf_op jit(solution)/shard_map/ppermute | solution.py:386
  53.1 13.2 %collective-permute-start.23 = (bf16[1,256,512]{2,1,0:T(8,128)(2,1)S(1)}, bf16[1,256,512]{2,1,0:T(8,128)(2,1)S(1)}, u32[]{:S(2)}, u32[]{:S(2)}) collective-permute-start(bf16[1,256,512]{2,1,0:T(8,128)(2,1)S(1)} %get-tuple-element.112), channel_id=1, source_target_pairs={{0,16},{8,24},{16,0},{24,8},{1,17},{9,25},{17,1},{25,9},{2,18},{10... | collective-permute-start | bytes 786440 | tf_op jit(solution)/shard_map/ppermute | solution.py:347

commit v18 on v16

--- a/solution.py
+++ b/solution.py
@@ -223,7 +223,7 @@
                     y[o, c, im, lanes] = z[c][1].astype(BF16)
         return carry
 
-    lax.fori_loop(0, CLASSES, middle, 0, unroll=2)
+    lax.fori_loop(0, CLASSES, middle, 0, unroll=4)
 
     for c in range(CLASSES):
         grad[c] = dot(back[c], y[2, c])

time: 67.5 us -> 67.6 us (level)
  no operation moved by 1% of the time
where the time goes in v18:
time: 67.6 us; the launch traced here: 67.5 us
  starting transfers between devices  27.8 us (41%)
  Pallas kernels  24.8 us (37%)
  waiting for transfers between devices  14 us (21%)
  between operations  0.8 us (1%)
    ppermute x21, starting transfers between devices, exchange(): lax.ppermute(block, 'ctx', [(i, i ^ j) for i in range(n)])  22.5 us
    ppermute x21, waiting for transfers between devices, exchange(): lax.ppermute(block, 'ctx', [(i, i ^ j) for i in range(n)])  13.2 us
    pallas_call x2, Pallas kernels, conv(): pl.pallas_call(functools.partial(conv_kernel, n, d, half), in_specs=[SMEM...  9.54 us
    pallas_call x2, Pallas kernels, gate(): pl.pallas_call(functools.partial(gate_kernel, js), in_specs=[SMEM] + [VME...  7.17 us
    ppermute x3, starting transfers between devices, trade(): return resident(lax.ppermute(send, 'dp', [(i, i ^ bit) for i in range(d)]))  5.26 us
    pallas_call x2, Pallas kernels, products(): pl.pallas_call(functools.partial(second_kernel if half else first_kernel,...  3.53 us
    pallas_call x2, Pallas kernels, filter_spectrum(): pl.pallas_call(functools.partial(filter_kernel, half), in_specs=[VMEM] *...  3.42 us
  transfers between devices with their start and end apart: 24, of which 8 were waited for; matrix products, arithmetic and copies ran while one was open for 0% of the time, Pallas kernels for 31%

profile of v18, /device:TPU:0, one launch (start us, length us, event | category | flops | bytes accessed | tf_op | source)
XLA Modules:
  0.0 67.5 jit_solution(5535537048637672841)
XLA Ops:
  0.7 2.7 %products.2 = (bf16[2,128,256]{2,1,0:T(8,128)(2,1)S(1)}, bf16[2,128,256]{2,1,0:T(8,128)(2,1)S(1)}, bf16[2,128,256]{2,1,0:T(8,128)(2,1)S(1)}, bf16[2,128,256]{2,1...) custom-call(s32[2]{0:T(128)S(1)} %pad_add_fusion.me, ...), custom_call_target="tpu_custom_call" | custom-call | tf_op jit(solution)/shard_map/products/pallas_call | solution.py:133
  4.0 2.6 %collective-permute-start.1 = (bf16[2,128,256]{2,1,0:T(8,128)(2,1)S(1)}, bf16[2,128,256]{2,1,0:T(8,128)(2,1)S(1)}, u32[]{:S(2)}, u32[]{:S(2)}) collective-permute-start(bf16[2,128,256]{2,1,0:T(8,128)(2,1)S(1)} %get-tuple-element.60), channel_id=1, source_target_pairs={{0,2},{1,3},{2,0},{3,1},{4,6},{5,7},{6,4},{7,5},{8,10},{9,11},{10,... | collective-permute-start | bytes 393224 | tf_op jit(solution)/shard_map/ppermute | solution.py:386
  6.5 1.5 %collective-permute-start.9 = (bf16[2,128,256]{2,1,0:T(8,128)(2,1)S(1)}, bf16[2,128,256]{2,1,0:T(8,128)(2,1)S(1)}, u32[]{:S(2)}, u32[]{:S(2)}) collective-permute-start(bf16[2,128,256]{2,1,0:T(8,128)(2,1)S(1)} %get-tuple-element.78), channel_id=1, source_target_pairs={{0,4},{1,5},{2,6},{3,7},{4,0},{5,1},{6,2},{7,3},{8,12},{9,13},{10,... | collective-permute-start | bytes 393224 | tf_op jit(solution)/shard_map/ppermute | solution.py:386
  8.1 1.2 %collective-permute-start.11 = (bf16[2,128,256]{2,1,0:T(8,128)(2,1)S(1)}, bf16[2,128,256]{2,1,0:T(8,128)(2,1)S(1)}, u32[]{:S(2)}, u32[]{:S(2)}) collective-permute-start(bf16[2,128,256]{2,1,0:T(8,128)(2,1)S(1)} %get-tuple-element.80), channel_id=1, source_target_pairs={{0,3},{1,2},{2,1},{3,0},{4,7},{5,6},{6,5},{7,4},{8,11},{9,10},{10,... | collective-permute-start | bytes 393224 | tf_op jit(solution)/shard_map/ppermute | solution.py:386
  9.2 2.0 %collective-permute-start.12 = (bf16[2,128,256]{2,1,0:T(8,128)(2,1)S(1)}, bf16[2,128,256]{2,1,0:T(8,128)(2,1)S(1)}, u32[]{:S(2)}, u32[]{:S(2)}) collective-permute-start(bf16[2,128,256]{2,1,0:T(8,128)(2,1)S(1)} %get-tuple-element.81), channel_id=1, source_target_pairs={{0,5},{1,4},{2,7},{3,6},{4,1},{5,0},{6,3},{7,2},{8,13},{9,12},{10,... | collective-permute-start | bytes 393224 | tf_op jit(solution)/shard_map/ppermute | solution.py:386
  11.3 0.8 %products.3 = (bf16[2,128,256]{2,1,0:T(8,128)(2,1)S(1)}, bf16[2,128,256]{2,1,0:T(8,128)(2,1)S(1)}, bf16[2,128,256]{2,1,0:T(8,128)(2,1)S(1)}, bf16[2,128,256]{2,1...) custom-call(s32[2]{0:T(128)S(1)} %pad_add_fusion.me, ...), custom_call_target="tpu_custom_call" | custom-call | tf_op jit(solution)/shard_map/products/pallas_call | solution.py:133
  12.6 1.7 %filter_spectrum.2.refs_0_.refs_8_ = f32[8,256,256]{2,1,0:T(8,128)S(1)} custom-call(f32[512,1024]{1,0:T(8,128)S(1)} %copy-done.5, bf16[8,256,256]{2,1,0:T(8,128)(2,1)S(1)} %copy-done.4, bf16[2,128,256]{2,1,0:T(8,128)(2,1)S(1)} %collective-permute-done.refs_0_.refs_1_, bf16[2,128,256]{2,1,0:T(8,128)(2,1)S(1)} %collective-permute-done.1.refs_1_.refs_2_), custom_call_target="tpu_custom_call" | custom-call | tf_op jit(solution)/shard_map/filter_spectrum/pallas_call | solution.py:176
  14.6 1.1 %collective-permute-start.2 = (bf16[2,128,256]{2,1,0:T(8,128)(2,1)S(1)}, bf16[2,128,256]{2,1,0:T(8,128)(2,1)S(1)}, u32[]{:S(2)}, u32[]{:S(2)}) collective-permute-start(bf16[2,128,256]{2,1,0:T(8,128)(2,1)S(1)} %get-tuple-element.66), channel_id=1, source_target_pairs={{0,1},{1,0},{2,3},{3,2},{4,5},{5,4},{6,7},{7,6},{8,9},{9,8},{10,11... | collective-permute-start | bytes 393224 | tf_op jit(solution)/shard_map/ppermute | solution.py:386
  15.7 0.9 %collective-permute-start.3 = (bf16[2,128,256]{2,1,0:T(8,128)(2,1)S(1)}, bf16[2,128,256]{2,1,0:T(8,128)(2,1)S(1)}, u32[]{:S(2)}, u32[]{:S(2)}) collective-permute-start(bf16[2,128,256]{2,1,0:T(8,128)(2,1)S(1)} %get-tuple-element.67), channel_id=1, source_target_pairs={{0,2},{1,3},{2,0},{3,1},{4,6},{5,7},{6,4},{7,5},{8,10},{9,11},{10,... | collective-permute-start | bytes 393224 | tf_op jit(solution)/shard_map/ppermute | solution.py:386
  16.6 1.7 %filter_spectrum.3.refs_0_.refs_8_ = f32[8,256,256]{2,1,0:T(8,128)S(1)} custom-call(f32[512,1024]{1,0:T(8,128)S(1)} %copy-done.5, bf16[8,256,256]{2,1,0:T(8,128)(2,1)S(1)} %copy-done.4, f32[8,256,256]{2,1,0:T(8,128)S(1)} %filter_spectrum.2.refs_0_.refs_8_), custom_call_target="tpu_custom_call" | custom-call | tf_op jit(solution)/shard_map/filter_spectrum/pallas_call | solution.py:176
  18.4 1.0 %collective-permute-start.4 = (bf16[2,128,256]{2,1,0:T(8,128)(2,1)S(1)}, bf16[2,128,256]{2,1,0:T(8,128)(2,1)S(1)}, u32[]{:S(2)}, u32[]{:S(2)}) collective-permute-start(bf16[2,128,256]{2,1,0:T(8,128)(2,1)S(1)} %get-tuple-element.68), channel_id=1, source_target_pairs={{0,4},{1,5},{2,6},{3,7},{4,0},{5,1},{6,2},{7,3},{8,12},{9,13},{10,... | collective-permute-start | bytes 393224 | tf_op jit(solution)/shard_map/ppermute | solution.py:386
  19.4 0.9 %collective-permute-done.12.refs_6_ = bf16[2,128,256]{2,1,0:T(8,128)(2,1)S(1)} collective-permute-done((bf16[2,128,256]{2,1,0:T(8,128)(2,1)S(1)}, bf16[2,128,256]{2,1,0:T(8,128)(2,1)S(1)}, u32[]{:S(2)}, u32[]{:S(2)}) %collective-permute-start.12) | collective-permute-done | bytes 131104 | tf_op jit(solution)/shard_map/ppermute | solution.py:386
  20.3 1.1 %collective-permute-start.5 = (bf16[2,128,256]{2,1,0:T(8,128)(2,1)S(1)}, bf16[2,128,256]{2,1,0:T(8,128)(2,1)S(1)}, u32[]{:S(2)}, u32[]{:S(2)}) collective-permute-start(bf16[2,128,256]{2,1,0:T(8,128)(2,1)S(1)} %get-tuple-element.73), channel_id=1, source_target_pairs={{0,6},{1,7},{2,4},{3,5},{4,2},{5,3},{6,0},{7,1},{8,14},{9,15},{10,... | collective-permute-start | bytes 393224 | tf_op jit(solution)/shard_map/ppermute | solution.py:386
  21.5 1.5 %collective-permute-start.6 = (bf16[2,128,256]{2,1,0:T(8,128)(2,1)S(1)}, bf16[2,128,256]{2,1,0:T(8,128)(2,1)S(1)}, u32[]{:S(2)}, u32[]{:S(2)}) collective-permute-start(bf16[2,128,256]{2,1,0:T(8,128)(2,1)S(1)} %get-tuple-element.74), channel_id=1, source_target_pairs={{0,3},{1,2},{2,1},{3,0},{4,7},{5,6},{6,5},{7,4},{8,11},{9,10},{10,... | collective-permute-start | bytes 393224 | tf_op jit(solution)/shard_map/ppermute | solution.py:386
  24.2 4.7 %conv.2 = (bf16[2,2,128,256]{3,2,1,0:T(8,128)(2,1)S(1)}, bf16[2,2,128,256]{3,2,1,0:T(8,128)(2,1)S(1)}, bf16[2,2,128,256]{3,2,1,0:T(8,128)(2,1)S(1)}, bf16[2,2,12...) custom-call(s32[2]{0:T(128)S(1)} %pad_add_fusion.me, ...), custom_call_target="tpu_custom_call" | custom-call | tf_op jit(solution)/shard_map/conv/pallas_call | solution.py:251
  28.9 1.6 %collective-permute-start.21 = (bf16[2,256,256]{2,1,0:T(8,128)(2,1)S(1)}, bf16[2,256,256]{2,1,0:T(8,128)(2,1)S(1)}, u32[]{:S(2)}, u32[]{:S(2)}) collective-permute-start(bf16[2,256,256]{2,1,0:T(8,128)(2,1)S(1)} %get-tuple-element.108), channel_id=1, source_target_pairs={{0,8},{8,0},{16,24},{24,16},{1,9},{9,1},{17,25},{25,17},{2,10},{10... | collective-permute-start | bytes 786440 | tf_op jit(solution)/shard_map/ppermute | solution.py:347
  30.5 1.4 %collective-permute-done.8.refs_7_ = bf16[2,128,256]{2,1,0:T(8,128)(2,1)S(1)} collective-permute-done((bf16[2,128,256]{2,1,0:T(8,128)(2,1)S(1)}, bf16[2,128,256]{2,1,0:T(8,128)(2,1)S(1)}, u32[]{:S(2)}, u32[]{:S(2)}) %collective-permute-start.8) | collective-permute-done | bytes 131104 | tf_op jit(solution)/shard_map/ppermute | solution.py:386
  31.9 4.9 %conv.3 = (bf16[2,2,128,256]{3,2,1,0:T(8,128)(2,1)S(1)}, bf16[2,2,128,256]{3,2,1,0:T(8,128)(2,1)S(1)}, bf16[2,2,128,256]{3,2,1,0:T(8,128)(2,1)S(1)}, bf16[2,2,12...) custom-call(s32[2]{0:T(128)S(1)} %pad_add_fusion.me, ...), custom_call_target="tpu_custom_call", output_to_operand_aliasing={{0}: (12, {}), {1}: (13, {}), {2}: (14, {}), {3}: (15, {}),... | custom-call | tf_op jit(solution)/shard_map/conv/pallas_call | solution.py:251
  36.8 2.4 %collective-permute-start.16 = (bf16[2,2,128,256]{3,2,1,0:T(8,128)(2,1)S(1)}, bf16[2,2,128,256]{3,2,1,0:T(8,128)(2,1)S(1)}, u32[]{:S(2)}, u32[]{:S(2)}) collective-permute-start(bf16[2,2,128,256]{3,2,1,0:T(8,128)(2,1)S(1)} %get-tuple-element.94), channel_id=1, source_target_pairs={{0,6},{1,7},{2,4},{3,5},{4,2},{5,3},{6,0},{7,1},{8,14},{9,15},{10,... | collective-permute-start | bytes 786440 | tf_op jit(solution)/shard_map/ppermute | solution.py:386
  39.7 1.2 %collective-permute-start.22 = (bf16[2,256,256]{2,1,0:T(8,128)(2,1)S(1)}, bf16[2,256,256]{2,1,0:T(8,128)(2,1)S(1)}, u32[]{:S(2)}, u32[]{:S(2)}) collective-permute-start(bf16[2,256,256]{2,1,0:T(8,128)(2,1)S(1)} %get-tuple-element.110), channel_id=1, source_target_pairs={{0,8},{8,0},{16,24},{24,16},{1,9},{9,1},{17,25},{25,17},{2,10},{10... | collective-permute-start | bytes 786440 | tf_op jit(solution)/shard_map/ppermute | solution.py:347
  40.9 1.0 %collective-permute-start.18 = (bf16[2,2,128,256]{3,2,1,0:T(8,128)(2,1)S(1)}, bf16[2,2,128,256]{3,2,1,0:T(8,128)(2,1)S(1)}, u32[]{:S(2)}, u32[]{:S(2)}) collective-permute-start(bf16[2,2,128,256]{3,2,1,0:T(8,128)(2,1)S(1)} %get-tuple-element.96), channel_id=1, source_target_pairs={{0,2},{1,3},{2,0},{3,1},{4,6},{5,7},{6,4},{7,5},{8,10},{9,11},{10,... | collective-permute-start | bytes 786440 | tf_op jit(solution)/shard_map/ppermute | solution.py:386
  41.9 5.0 %collective-permute-done.16.refs_1_ = bf16[2,2,128,256]{3,2,1,0:T(8,128)(2,1)S(1)} collective-permute-done((bf16[2,2,128,256]{3,2,1,0:T(8,128)(2,1)S(1)}, bf16[2,2,128,256]{3,2,1,0:T(8,128)(2,1)S(1)}, u32[]{:S(2)}, u32[]{:S(2)}) %collective-permute-start.16) | collective-permute-done | bytes 262176 | tf_op jit(solution)/shard_map/ppermute | solution.py:386
  46.9 2.7 %collective-permute-start.14 = (bf16[2,2,128,256]{3,2,1,0:T(8,128)(2,1)S(1)}, bf16[2,2,128,256]{3,2,1,0:T(8,128)(2,1)S(1)}, u32[]{:S(2)}, u32[]{:S(2)}) collective-permute-start(bf16[2,2,128,256]{3,2,1,0:T(8,128)(2,1)S(1)} %get-tuple-element.91), channel_id=1, source_target_pairs={{0,5},{1,4},{2,7},{3,6},{4,1},{5,0},{6,3},{7,2},{8,13},{9,12},{10,... | collective-permute-start | bytes 786440 | tf_op jit(solution)/shard_map/ppermute | solution.py:386
  49.6 0.8 %collective-permute-start.15 = (bf16[2,2,128,256]{3,2,1,0:T(8,128)(2,1)S(1)}, bf16[2,2,128,256]{3,2,1,0:T(8,128)(2,1)S(1)}, u32[]{:S(2)}, u32[]{:S(2)}) collective-permute-start(bf16[2,2,128,256]{3,2,1,0:T(8,128)(2,1)S(1)} %get-tuple-element.92), channel_id=1, source_target_pairs={{0,7},{1,6},{2,5},{3,4},{4,3},{5,2},{6,1},{7,0},{8,15},{9,14},{10,... | collective-permute-start | bytes 786440 | tf_op jit(solution)/shard_map/ppermute | solution.py:386
  50.4 2.8 %collective-permute-done.18.refs_3_ = bf16[2,2,128,256]{3,2,1,0:T(8,128)(2,1)S(1)} collective-permute-done((bf16[2,2,128,256]{3,2,1,0:T(8,128)(2,1)S(1)}, bf16[2,2,128,256]{3,2,1,0:T(8,128)(2,1)S(1)}, u32[]{:S(2)}, u32[]{:S(2)}) %collective-permute-start.18) | collective-permute-done | bytes 262176 | tf_op jit(solution)/shard_map/ppermute | solution.py:386
  53.2 2.5 %collective-permute-start.23 = (bf16[1,256,512]{2,1,0:T(8,128)(2,1)S(1)}, bf16[1,256,512]{2,1,0:T(8,128)(2,1)S(1)}, u32[]{:S(2)}, u32[]{:S(2)}) collective-permute-start(bf16[1,256,512]{2,1,0:T(8,128)(2,1)S(1)} %get-tuple-element.112), channel_id=1, source_target_pairs={{0,16},{8,24},{16,0},{24,8},{1,17},{9,25},{17,1},{25,9},{2,18},{10... | collective-permute-start | bytes 786440 | tf_op jit(solution)/shard_map/ppermute | solution.py:347
  55.7 1.5 %collective-permute-done.20.refs_5_ = bf16[2,2,128,256]{3,2,1,0:T(8,128)(2,1)S(1)} collective-permute-done((bf16[2,2,128,256]{3,2,1,0:T(8,128)(2,1)S(1)}, bf16[2,2,128,256]{3,2,1,0:T(8,128)(2,1)S(1)}, u32[]{:S(2)}, u32[]{:S(2)}) %collective-permute-start.20) | collective-permute-done | bytes 262176 | tf_op jit(solution)/shard_map/ppermute | solution.py:386
  57.2 4.4 %gate.2 = (bf16[128,4096]{1,0:T(8,128)(2,1)}, bf16[128,4096]{1,0:T(8,128)(2,1)}, bf16[128,4096]{1,0:T(8,128)(2,1)}, bf16[128,4096]{1,0:T(8,128)(2,1)}, f32[8,128]{1,0:T(8,128)}) custom-call(s32[2]{0:T(128)S(1)} %pad_add_fusion.me, bf16[128,4096]{1,0:T(8,128)(2,1)S(1)} %bitcast.13, bf16[128,4096]{1,0:T(8,128)(2,1)S(1)} %bitcast.17, ...), custom_call_target="tpu_custom_call" | custom-call | tf_op jit(solution)/shard_map/gate/pallas_call | solution.py:313
  61.6 1.3 %collective-permute-done.15.refs_1_ = bf16[2,2,128,256]{3,2,1,0:T(8,128)(2,1)S(1)} collective-permute-done((bf16[2,2,128,256]{3,2,1,0:T(8,128)(2,1)S(1)}, bf16[2,2,128,256]{3,2,1,0:T(8,128)(2,1)S(1)}, u32[]{:S(2)}, u32[]{:S(2)}) %collective-permute-start.15) | collective-permute-done | bytes 262176 | tf_op jit(solution)/shard_map/ppermute | solution.py:386
  62.9 2.7 %gate.3 = (bf16[128,4096]{1,0:T(8,128)(2,1)}, bf16[128,4096]{1,0:T(8,128)(2,1)}, bf16[128,4096]{1,0:T(8,128)(2,1)}, bf16[128,4096]{1,0:T(8,128)(2,1)}, f32[8,128]{1,0:T(8,128)}) custom-call(s32[2]{0:T(128)S(1)} %pad_add_fusion.me, bf16[128,4096]{1,0:T(8,128)(2,1)S(1)} %bitcast.14, ...), custom_call_target="tpu_custom_call", output_to_operand_aliasing={{0}: (8, {}), {1}: (9, {}), {2}: (10, {}), {3}: (11, {})} | custom-call | tf_op jit(solution)/shard_map/gate/pallas_call | solution.py:313
  65.7 0.7 %collective-permute-done.23.got = bf16[1,256,512]{2,1,0:T(8,128)(2,1)S(1)} collective-permute-done((bf16[1,256,512]{2,1,0:T(8,128)(2,1)S(1)}, bf16[1,256,512]{2,1,0:T(8,128)(2,1)S(1)}, u32[]{:S(2)}, u32[]{:S(2)}) %collective-permute-start.23) | collective-permute-done | bytes 262176 | tf_op jit(solution)/shard_map/ppermute | solution.py:347
  66.4 1.1 %turn_grads.1 = f32[512,256]{1,0:T(8,128)} custom-call(f32[1,256,512]{2,1,0:T(8,128)S(1)} %get-tuple-element.111.keep, bf16[1,256,512]{2,1,0:T(8,128)(2,1)S(1)} %collective-permute-done.23.got), custom_call_target="tpu_custom_call" | custom-call | tf_op jit(solution)/shard_map/turn_grads/pallas_call | solution.py:365
  (45 shorter events, 3.3 us)
Async XLA Ops:
  0.7 10.5 %copy-start = (bf16[1,128,4096]{2,1,0:T(8,128)(2,1)S(1)}, bf16[1,128,4096]{2,1,0:T(8,128)(2,1)}, u32[]{:S(2)}) copy-start(bf16[1,128,4096]{2,1,0:T(8,128)(2,1)} %param.8) | copy-start | bytes 3145732
  0.7 10.5 %copy-start.1 = (bf16[1,128,4096]{2,1,0:T(8,128)(2,1)S(1)}, bf16[1,128,4096]{2,1,0:T(8,128)(2,1)}, u32[]{:S(2)}) copy-start(bf16[1,128,4096]{2,1,0:T(8,128)(2,1)} %param.11) | copy-start | bytes 3145732
  0.7 10.5 %copy-start.2 = (bf16[1,128,4096]{2,1,0:T(8,128)(2,1)S(1)}, bf16[1,128,4096]{2,1,0:T(8,128)(2,1)}, u32[]{:S(2)}) copy-start(bf16[1,128,4096]{2,1,0:T(8,128)(2,1)} %param.10) | copy-start | bytes 3145732
  0.7 10.5 %copy-start.3 = (bf16[1,128,4096]{2,1,0:T(8,128)(2,1)S(1)}, bf16[1,128,4096]{2,1,0:T(8,128)(2,1)}, u32[]{:S(2)}) copy-start(bf16[1,128,4096]{2,1,0:T(8,128)(2,1)} %param.9) | copy-start | bytes 3145732
  3.4 5.8 %collective-permute-start = (bf16[2,128,256]{2,1,0:T(8,128)(2,1)S(1)}, bf16[2,128,256]{2,1,0:T(8,128)(2,1)S(1)}, u32[]{:S(2)}, u32[]{:S(2)}) collective-permute-start(bf16[2,128,256]{2,1,0:T(8,128)(2,1)S(1)} %get-tuple-element.59), channel_id=1, source_target_pairs={{0,1},{1,0},{2,3},{3,2},{4,5},{5,4},{6,7},{7,6},{8,9},{9,8},{10,11... | collective-permute-start | bytes 393224 | tf_op jit(solution)/shard_map/ppermute | solution.py:386
  4.0 8.2 %collective-permute-start.1 = (bf16[2,128,256]{2,1,0:T(8,128)(2,1)S(1)}, bf16[2,128,256]{2,1,0:T(8,128)(2,1)S(1)}, u32[]{:S(2)}, u32[]{:S(2)}) collective-permute-start(bf16[2,128,256]{2,1,0:T(8,128)(2,1)S(1)} %get-tuple-element.60), channel_id=1, source_target_pairs={{0,2},{1,3},{2,0},{3,1},{4,6},{5,7},{6,4},{7,5},{8,10},{9,11},{10,... | collective-permute-start | bytes 393224 | tf_op jit(solution)/shard_map/ppermute | solution.py:386
  6.5 8.1 %collective-permute-start.9 = (bf16[2,128,256]{2,1,0:T(8,128)(2,1)S(1)}, bf16[2,128,256]{2,1,0:T(8,128)(2,1)S(1)}, u32[]{:S(2)}, u32[]{:S(2)}) collective-permute-start(bf16[2,128,256]{2,1,0:T(8,128)(2,1)S(1)} %get-tuple-element.78), channel_id=1, source_target_pairs={{0,4},{1,5},{2,6},{3,7},{4,0},{5,1},{6,2},{7,3},{8,12},{9,13},{10,... | collective-permute-start | bytes 393224 | tf_op jit(solution)/shard_map/ppermute | solution.py:386
  8.0 7.7 %collective-permute-start.10 = (bf16[2,128,256]{2,1,0:T(8,128)(2,1)S(1)}, bf16[2,128,256]{2,1,0:T(8,128)(2,1)S(1)}, u32[]{:S(2)}, u32[]{:S(2)}) collective-permute-start(bf16[2,128,256]{2,1,0:T(8,128)(2,1)S(1)} %get-tuple-element.79), channel_id=1, source_target_pairs={{0,6},{1,7},{2,4},{3,5},{4,2},{5,3},{6,0},{7,1},{8,14},{9,15},{10,... | collective-permute-start | bytes 393224 | tf_op jit(solution)/shard_map/ppermute | solution.py:386
  8.1 10.3 %collective-permute-start.11 = (bf16[2,128,256]{2,1,0:T(8,128)(2,1)S(1)}, bf16[2,128,256]{2,1,0:T(8,128)(2,1)S(1)}, u32[]{:S(2)}, u32[]{:S(2)}) collective-permute-start(bf16[2,128,256]{2,1,0:T(8,128)(2,1)S(1)} %get-tuple-element.80), channel_id=1, source_target_pairs={{0,3},{1,2},{2,1},{3,0},{4,7},{5,6},{6,5},{7,4},{8,11},{9,10},{10,... | collective-permute-start | bytes 393224 | tf_op jit(solution)/shard_map/ppermute | solution.py:386
  9.2 3.4 %copy-start.4 = (bf16[8,256,256]{2,1,0:T(8,128)(2,1)S(1)}, bf16[8,256,256]{2,1,0:T(8,128)(2,1)}, u32[]{:S(2)}) copy-start(bf16[8,256,256]{2,1,0:T(8,128)(2,1)} %constant.12.clone.fwd.refs_9_) | copy-start | bytes 3145732
  9.2 3.4 %copy-start.5 = (f32[512,1024]{1,0:T(8,128)S(1)}, f32[512,1024]{1,0:T(8,128)}, u32[]{:S(2)}) copy-start(f32[512,1024]{1,0:T(8,128)} %filt.3) | copy-start | bytes 6291460
  9.2 11.1 %collective-permute-start.12 = (bf16[2,128,256]{2,1,0:T(8,128)(2,1)S(1)}, bf16[2,128,256]{2,1,0:T(8,128)(2,1)S(1)}, u32[]{:S(2)}, u32[]{:S(2)}) collective-permute-start(bf16[2,128,256]{2,1,0:T(8,128)(2,1)S(1)} %get-tuple-element.81), channel_id=1, source_target_pairs={{0,5},{1,4},{2,7},{3,6},{4,1},{5,0},{6,3},{7,2},{8,13},{9,12},{10,... | collective-permute-start | bytes 393224 | tf_op jit(solution)/shard_map/ppermute | solution.py:386
  12.1 9.4 %collective-permute-start.13 = (bf16[2,128,256]{2,1,0:T(8,128)(2,1)S(1)}, bf16[2,128,256]{2,1,0:T(8,128)(2,1)S(1)}, u32[]{:S(2)}, u32[]{:S(2)}) collective-permute-start(bf16[2,128,256]{2,1,0:T(8,128)(2,1)S(1)} %get-tuple-element.82), channel_id=1, source_target_pairs={{0,7},{1,6},{2,5},{3,4},{4,3},{5,2},{6,1},{7,0},{8,15},{9,14},{10,... | collective-permute-start | bytes 393224 | tf_op jit(solution)/shard_map/ppermute | solution.py:386
  14.6 8.3 %collective-permute-start.2 = (bf16[2,128,256]{2,1,0:T(8,128)(2,1)S(1)}, bf16[2,128,256]{2,1,0:T(8,128)(2,1)S(1)}, u32[]{:S(2)}, u32[]{:S(2)}) collective-permute-start(bf16[2,128,256]{2,1,0:T(8,128)(2,1)S(1)} %get-tuple-element.66), channel_id=1, source_target_pairs={{0,1},{1,0},{2,3},{3,2},{4,5},{5,4},{6,7},{7,6},{8,9},{9,8},{10,11... | collective-permute-start | bytes 393224 | tf_op jit(solution)/shard_map/ppermute | solution.py:386
  15.7 7.8 %collective-permute-start.3 = (bf16[2,128,256]{2,1,0:T(8,128)(2,1)S(1)}, bf16[2,128,256]{2,1,0:T(8,128)(2,1)S(1)}, u32[]{:S(2)}, u32[]{:S(2)}) collective-permute-start(bf16[2,128,256]{2,1,0:T(8,128)(2,1)S(1)} %get-tuple-element.67), channel_id=1, source_target_pairs={{0,2},{1,3},{2,0},{3,1},{4,6},{5,7},{6,4},{7,5},{8,10},{9,11},{10,... | collective-permute-start | bytes 393224 | tf_op jit(solution)/shard_map/ppermute | solution.py:386
  18.3 5.8 %copy-start.6 = (bf16[8,128,256]{2,1,0:T(8,128)(2,1)S(1)}, bf16[8,128,256]{2,1,0:T(8,128)(2,1)}, u32[]{:S(2)}) copy-start(bf16[8,128,256]{2,1,0:T(8,128)(2,1)} %constant.13.clone.refs_10_) | copy-start | bytes 1572868
  18.4 10.5 %collective-permute-start.4 = (bf16[2,128,256]{2,1,0:T(8,128)(2,1)S(1)}, bf16[2,128,256]{2,1,0:T(8,128)(2,1)S(1)}, u32[]{:S(2)}, u32[]{:S(2)}) collective-permute-start(bf16[2,128,256]{2,1,0:T(8,128)(2,1)S(1)} %get-tuple-element.68), channel_id=1, source_target_pairs={{0,4},{1,5},{2,6},{3,7},{4,0},{5,1},{6,2},{7,3},{8,12},{9,13},{10,... | collective-permute-start | bytes 393224 | tf_op jit(solution)/shard_map/ppermute | solution.py:386
  20.3 10.2 %collective-permute-start.5 = (bf16[2,128,256]{2,1,0:T(8,128)(2,1)S(1)}, bf16[2,128,256]{2,1,0:T(8,128)(2,1)S(1)}, u32[]{:S(2)}, u32[]{:S(2)}) collective-permute-start(bf16[2,128,256]{2,1,0:T(8,128)(2,1)S(1)} %get-tuple-element.73), channel_id=1, source_target_pairs={{0,6},{1,7},{2,4},{3,5},{4,2},{5,3},{6,0},{7,1},{8,14},{9,15},{10,... | collective-permute-start | bytes 393224 | tf_op jit(solution)/shard_map/ppermute | solution.py:386
  21.5 9.0 %collective-permute-start.6 = (bf16[2,128,256]{2,1,0:T(8,128)(2,1)S(1)}, bf16[2,128,256]{2,1,0:T(8,128)(2,1)S(1)}, u32[]{:S(2)}, u32[]{:S(2)}) collective-permute-start(bf16[2,128,256]{2,1,0:T(8,128)(2,1)S(1)} %get-tuple-element.74), channel_id=1, source_target_pairs={{0,3},{1,2},{2,1},{3,0},{4,7},{5,6},{6,5},{7,4},{8,11},{9,10},{10,... | collective-permute-start | bytes 393224 | tf_op jit(solution)/shard_map/ppermute | solution.py:386
  22.9 7.5 %collective-permute-start.7 = (bf16[2,128,256]{2,1,0:T(8,128)(2,1)S(1)}, bf16[2,128,256]{2,1,0:T(8,128)(2,1)S(1)}, u32[]{:S(2)}, u32[]{:S(2)}) collective-permute-start(bf16[2,128,256]{2,1,0:T(8,128)(2,1)S(1)} %get-tuple-element.75), channel_id=1, source_target_pairs={{0,5},{1,4},{2,7},{3,6},{4,1},{5,0},{6,3},{7,2},{8,13},{9,12},{10,... | collective-permute-start | bytes 393224 | tf_op jit(solution)/shard_map/ppermute | solution.py:386
  23.6 8.4 %collective-permute-start.8 = (bf16[2,128,256]{2,1,0:T(8,128)(2,1)S(1)}, bf16[2,128,256]{2,1,0:T(8,128)(2,1)S(1)}, u32[]{:S(2)}, u32[]{:S(2)}) collective-permute-start(bf16[2,128,256]{2,1,0:T(8,128)(2,1)S(1)} %get-tuple-element.76), channel_id=1, source_target_pairs={{0,7},{1,6},{2,5},{3,4},{4,3},{5,2},{6,1},{7,0},{8,15},{9,14},{10,... | collective-permute-start | bytes 393224 | tf_op jit(solution)/shard_map/ppermute | solution.py:386
  28.9 13.0 %collective-permute-start.21 = (bf16[2,256,256]{2,1,0:T(8,128)(2,1)S(1)}, bf16[2,256,256]{2,1,0:T(8,128)(2,1)S(1)}, u32[]{:S(2)}, u32[]{:S(2)}) collective-permute-start(bf16[2,256,256]{2,1,0:T(8,128)(2,1)S(1)} %get-tuple-element.108), channel_id=1, source_target_pairs={{0,8},{8,0},{16,24},{24,16},{1,9},{9,1},{17,25},{25,17},{2,10},{10... | collective-permute-start | bytes 786440 | tf_op jit(solution)/shard_map/ppermute | solution.py:347
  31.9 25.3 %copy-start.7 = (f32[4096]{0:T(1024)S(1)}, f32[4096]{0:T(1024)}, u32[]{:S(2)}) copy-start(f32[4096]{0:T(1024)} %param.13) | copy-start | bytes 49156
  36.8 10.1 %collective-permute-start.16 = (bf16[2,2,128,256]{3,2,1,0:T(8,128)(2,1)S(1)}, bf16[2,2,128,256]{3,2,1,0:T(8,128)(2,1)S(1)}, u32[]{:S(2)}, u32[]{:S(2)}) collective-permute-start(bf16[2,2,128,256]{3,2,1,0:T(8,128)(2,1)S(1)} %get-tuple-element.94), channel_id=1, source_target_pairs={{0,6},{1,7},{2,4},{3,5},{4,2},{5,3},{6,0},{7,1},{8,14},{9,15},{10,... | collective-permute-start | bytes 786440 | tf_op jit(solution)/shard_map/ppermute | solution.py:386
  39.2 7.7 %collective-permute-start.17 = (bf16[2,2,128,256]{3,2,1,0:T(8,128)(2,1)S(1)}, bf16[2,2,128,256]{3,2,1,0:T(8,128)(2,1)S(1)}, u32[]{:S(2)}, u32[]{:S(2)}) collective-permute-start(bf16[2,2,128,256]{3,2,1,0:T(8,128)(2,1)S(1)} %get-tuple-element.95), channel_id=1, source_target_pairs={{0,1},{1,0},{2,3},{3,2},{4,5},{5,4},{6,7},{7,6},{8,9},{9,8},{10,11... | collective-permute-start | bytes 786440 | tf_op jit(solution)/shard_map/ppermute | solution.py:386
  39.7 9.9 %collective-permute-start.22 = (bf16[2,256,256]{2,1,0:T(8,128)(2,1)S(1)}, bf16[2,256,256]{2,1,0:T(8,128)(2,1)S(1)}, u32[]{:S(2)}, u32[]{:S(2)}) collective-permute-start(bf16[2,256,256]{2,1,0:T(8,128)(2,1)S(1)} %get-tuple-element.110), channel_id=1, source_target_pairs={{0,8},{8,0},{16,24},{24,16},{1,9},{9,1},{17,25},{25,17},{2,10},{10... | collective-permute-start | bytes 786440 | tf_op jit(solution)/shard_map/ppermute | solution.py:347
  40.9 12.4 %collective-permute-start.18 = (bf16[2,2,128,256]{3,2,1,0:T(8,128)(2,1)S(1)}, bf16[2,2,128,256]{3,2,1,0:T(8,128)(2,1)S(1)}, u32[]{:S(2)}, u32[]{:S(2)}) collective-permute-start(bf16[2,2,128,256]{3,2,1,0:T(8,128)(2,1)S(1)} %get-tuple-element.96), channel_id=1, source_target_pairs={{0,2},{1,3},{2,0},{3,1},{4,6},{5,7},{6,4},{7,5},{8,10},{9,11},{10,... | collective-permute-start | bytes 786440 | tf_op jit(solution)/shard_map/ppermute | solution.py:386
  41.9 13.8 %collective-permute-start.19 = (bf16[2,2,128,256]{3,2,1,0:T(8,128)(2,1)S(1)}, bf16[2,2,128,256]{3,2,1,0:T(8,128)(2,1)S(1)}, u32[]{:S(2)}, u32[]{:S(2)}) collective-permute-start(bf16[2,2,128,256]{3,2,1,0:T(8,128)(2,1)S(1)} %get-tuple-element.97), channel_id=1, source_target_pairs={{0,4},{1,5},{2,6},{3,7},{4,0},{5,1},{6,2},{7,3},{8,12},{9,13},{10,... | collective-permute-start | bytes 786440 | tf_op jit(solution)/shard_map/ppermute | solution.py:386
  46.9 10.3 %collective-permute-start.20 = (bf16[2,2,128,256]{3,2,1,0:T(8,128)(2,1)S(1)}, bf16[2,2,128,256]{3,2,1,0:T(8,128)(2,1)S(1)}, u32[]{:S(2)}, u32[]{:S(2)}) collective-permute-start(bf16[2,2,128,256]{3,2,1,0:T(8,128)(2,1)S(1)} %get-tuple-element.98), channel_id=1, source_target_pairs={{0,3},{1,2},{2,1},{3,0},{4,7},{5,6},{6,5},{7,4},{8,11},{9,10},{10,... | collective-permute-start | bytes 786440 | tf_op jit(solution)/shard_map/ppermute | solution.py:386
  46.9 14.8 %collective-permute-start.14 = (bf16[2,2,128,256]{3,2,1,0:T(8,128)(2,1)S(1)}, bf16[2,2,128,256]{3,2,1,0:T(8,128)(2,1)S(1)}, u32[]{:S(2)}, u32[]{:S(2)}) collective-permute-start(bf16[2,2,128,256]{3,2,1,0:T(8,128)(2,1)S(1)} %get-tuple-element.91), channel_id=1, source_target_pairs={{0,5},{1,4},{2,7},{3,6},{4,1},{5,0},{6,3},{7,2},{8,13},{9,12},{10,... | collective-permute-start | bytes 786440 | tf_op jit(solution)/shard_map/ppermute | solution.py:386
  49.6 13.3 %collective-permute-start.15 = (bf16[2,2,128,256]{3,2,1,0:T(8,128)(2,1)S(1)}, bf16[2,2,128,256]{3,2,1,0:T(8,128)(2,1)S(1)}, u32[]{:S(2)}, u32[]{:S(2)}) collective-permute-start(bf16[2,2,128,256]{3,2,1,0:T(8,128)(2,1)S(1)} %get-tuple-element.92), channel_id=1, source_target_pairs={{0,7},{1,6},{2,5},{3,4},{4,3},{5,2},{6,1},{7,0},{8,15},{9,14},{10,... | collective-permute-start | bytes 786440 | tf_op jit(solution)/shard_map/ppermute | solution.py:386
  53.2 13.2 %collective-permute-start.23 = (bf16[1,256,512]{2,1,0:T(8,128)(2,1)S(1)}, bf16[1,256,512]{2,1,0:T(8,128)(2,1)S(1)}, u32[]{:S(2)}, u32[]{:S(2)}) collective-permute-start(bf16[1,256,512]{2,1,0:T(8,128)(2,1)S(1)} %get-tuple-element.112), channel_id=1, source_target_pairs={{0,16},{8,24},{16,0},{24,8},{1,17},{9,25},{17,1},{25,9},{2,18},{10... | collective-permute-start | bytes 786440 | tf_op jit(solution)/shard_map/ppermute | solution.py:347
